TPU v7x, 32 devices: a whole 2x2x4 slice. The times are simulated.
32 devices in a mesh: groups: 2 (over y), expert: 4 (over z), dp: 2 (over x), pipe: 2 (over core).
Axes of the slice: x: 2, y: 2, z: 4, core: 2. Of those that a mesh axis runs over, the one named last changes fastest.
Arguments:
- tokens: bfloat16 [256, 4096], P(('groups', 'expert'), ('dp', 'pipe')), parts along dimension 0, may hold values from -6 to 6
- routes: int32 [256, 4], P('groups'), parts along dimension 0, may hold values from 0 to 15, all different within a row; in each aligned block of 32 rows (0 to 31, 32 to 63, ...) at most 16 rows name the same one
- gate_weights: float32 [256, 4], P('groups'), parts along dimension 0, may hold values from 0.1 to 0.6
- teacher_gate: bfloat16 [4096, 14336], P(('dp', 'pipe'), 'expert'), may hold values from -0.09375 to 0.09375
- teacher_up: bfloat16 [4096, 14336], P(('dp', 'pipe'), 'expert'), may hold values from -0.09375 to 0.09375
- teacher_down: bfloat16 [14336, 4096], P('expert', ('dp', 'pipe')), may hold values from -0.046875 to 0.046875
- expert_gate: bfloat16 [4096, 14336], P(('dp', 'pipe'), 'expert'), may hold values from -0.09375 to 0.09375
- expert_up: bfloat16 [4096, 14336], P(('dp', 'pipe'), 'expert'), may hold values from -0.09375 to 0.09375
- expert_down: bfloat16 [14336, 4096], P('expert', ('dp', 'pipe')), may hold values from -0.1875 to 0.1875
Outputs:
- student_out: bfloat16 [256, 4096], P(('groups', 'expert'), ('dp', 'pipe')), parts along dimension 0
- grad_gate: bfloat16 [8192, 14336], P(('groups', 'dp', 'pipe'), 'expert'), parts along dimension 0
- grad_up: bfloat16 [8192, 14336], P(('groups', 'dp', 'pipe'), 'expert'), parts along dimension 0
- grad_down: bfloat16 [28672, 4096], P(('groups', 'expert'), ('dp', 'pipe')), parts along dimension 0
There are 2 independent parts, one for each index of `groups`. A program takes and returns all parts, laid end to end along the dimension named above; an argument that names none is the same for every part. Nothing has to cross between parts.
Inputs may be any that keep to these rules, and one draw needn't show every extreme that they name: `routes`: the 4 experts of a row differ. In each aligned block of 32 rows (the tokens of one index of expert) no expert is named by more than 16 rows, a bound that some block reaches.
All inputs are finite; a program needn't handle non-finite values.
Results may differ from a plain program's by a relative error of at most 0.028.
Values may be sent and summed in bfloat16 or wider, within the bound.
No kernel may reach another device: no remote copies, remote signals or barrier semaphores. Data moves between devices by JAX's collectives and lax.ppermute only.
A program may use at most 192 MiB of HBM per device.

v0:
```python
import jax
import jax.numpy as jnp
from jax import lax
from jax.sharding import PartitionSpec as P

H = 896


def slot_tables(routes, gate_weights, expert_ids, rank_count, capacity):
    token_count = routes.shape[0]
    matched = routes[None, :, :] == expert_ids[:, None, None]
    routed = jnp.any(matched, axis=2).astype(jnp.int32)
    weight = jnp.sum(jnp.where(matched, gate_weights[None, :, :], 0.0), axis=2)
    blocks = routed.reshape(expert_ids.shape[0], rank_count, token_count // rank_count)
    within = jnp.cumsum(blocks, axis=2) - blocks
    offsets = capacity * jnp.arange(rank_count, dtype=jnp.int32)[None, :, None]
    slot_index = (within + offsets).reshape(expert_ids.shape[0], token_count)
    slot_index = jnp.where(routed > 0, slot_index, -1)
    slot_ids = jnp.arange(rank_count * capacity, dtype=jnp.int32)
    picker = slot_index[:, None, :] == slot_ids[None, :, None]
    return (picker, weight)


def body(
    tokens,
    routes,
    gate_weights,
    teacher_gate,
    teacher_up,
    teacher_down,
    expert_gate,
    expert_up,
    expert_down,
):
    rank_count = lax.axis_size("expert")
    rank_here = lax.axis_index("expert")
    tok_block = tokens.shape[0]
    feature_block = tokens.shape[1]
    capacity = tok_block // 2
    experts_here = expert_gate.shape[1] // H
    gathered = lax.all_gather(tokens, "expert", axis=0, tiled=True)
    local_ids = rank_here * experts_here + jnp.arange(experts_here, dtype=jnp.int32)
    picker, weight = slot_tables(routes, gate_weights, local_ids, rank_count, capacity)
    slot_gate = jnp.sum(jnp.where(picker, weight[:, None, :], 0.0), axis=2)
    token_slots = jnp.einsum(
        "ert,td->erd", picker.astype(jnp.bfloat16), gathered, preferred_element_type=jnp.float32
    ).astype(jnp.bfloat16)
    gate_local = expert_gate.reshape(feature_block, experts_here, H)
    up_local = expert_up.reshape(feature_block, experts_here, H)
    down_local = expert_down.reshape(experts_here, H, feature_block)
    part_gate = jnp.einsum(
        "erd,deh->erh", token_slots, gate_local, preferred_element_type=jnp.float32
    )
    part_up = jnp.einsum("erd,deh->erh", token_slots, up_local, preferred_element_type=jnp.float32)
    teacher_pg = jnp.dot(gathered, teacher_gate, preferred_element_type=jnp.float32)
    teacher_pu = jnp.dot(gathered, teacher_up, preferred_element_type=jnp.float32)
    teacher_g, teacher_u, slot_pre_gate, slot_pre_up = (
        lax.psum(teacher_pg.astype(jnp.bfloat16), ("dp", "pipe")).astype(jnp.float32),
        lax.psum(teacher_pu.astype(jnp.bfloat16), ("dp", "pipe")).astype(jnp.float32),
        lax.psum(part_gate.astype(jnp.bfloat16), ("dp", "pipe")).astype(jnp.float32),
        lax.psum(part_up.astype(jnp.bfloat16), ("dp", "pipe")).astype(jnp.float32),
    )
    teacher_hidden = (jax.nn.silu(teacher_g) * teacher_u).astype(jnp.bfloat16)
    hidden_slots = (jax.nn.silu(slot_pre_gate) * slot_pre_up).astype(jnp.bfloat16)
    expert_out = jnp.einsum(
        "erh,ehd->erd", hidden_slots, down_local, preferred_element_type=jnp.float32
    )
    combine = jnp.where(jnp.swapaxes(picker, 1, 2), weight[:, :, None], 0.0)
    student_rows = jnp.einsum("etr,erd->td", combine, expert_out, precision=lax.Precision.HIGHEST)
    both_outputs = lax.psum_scatter(
        jnp.concatenate(
            [
                jnp.dot(teacher_hidden, teacher_down, preferred_element_type=jnp.float32),
                student_rows,
            ],
            axis=1,
        ).astype(jnp.bfloat16),
        "expert",
        scatter_dimension=0,
        tiled=True,
    ).astype(jnp.float32)
    target = both_outputs[:, :feature_block]
    student_sum = both_outputs[:, feature_block:]
    student_out = student_sum.astype(jnp.bfloat16)
    residual = (student_sum - target).astype(jnp.bfloat16)
    residual_all = lax.all_gather(residual, "expert", axis=0, tiled=True)
    picked = jnp.einsum(
        "ert,td->erd", picker.astype(jnp.bfloat16), residual_all, preferred_element_type=jnp.float32
    )
    output_grad = (slot_gate[:, :, None] * picked).astype(jnp.bfloat16)
    hidden_part = jnp.einsum(
        "erd,ehd->erh", output_grad, down_local, preferred_element_type=jnp.float32
    )
    hidden_grad = lax.psum(hidden_part.astype(jnp.bfloat16), ("dp", "pipe")).astype(jnp.float32)
    sigmoid_gate = jax.nn.sigmoid(slot_pre_gate)
    gate_grad = (
        hidden_grad * slot_pre_up * sigmoid_gate * (1.0 + slot_pre_gate * (1.0 - sigmoid_gate))
    ).astype(jnp.bfloat16)
    up_grad = (hidden_grad * slot_pre_gate * sigmoid_gate).astype(jnp.bfloat16)
    down_grad = jnp.einsum(
        "erh,erd->ehd", hidden_slots, output_grad, preferred_element_type=jnp.float32
    ).astype(jnp.bfloat16)
    gate_grad_w = jnp.einsum(
        "erd,erh->deh", token_slots, gate_grad, preferred_element_type=jnp.float32
    ).astype(jnp.bfloat16)
    up_grad_w = jnp.einsum(
        "erd,erh->deh", token_slots, up_grad, preferred_element_type=jnp.float32
    ).astype(jnp.bfloat16)
    grad_gate = gate_grad_w.reshape(feature_block, experts_here * H)
    grad_up = up_grad_w.reshape(feature_block, experts_here * H)
    grad_down = down_grad.reshape(experts_here * H, feature_block)
    return (student_out, grad_gate, grad_up, grad_down)


def solution(mesh):
    placed = (
        P(("groups", "expert"), ("dp", "pipe")),
        P("groups", None),
        P("groups", None),
        P(("dp", "pipe"), "expert"),
        P(("dp", "pipe"), "expert"),
        P("expert", ("dp", "pipe")),
        P(("dp", "pipe"), "expert"),
        P(("dp", "pipe"), "expert"),
        P("expert", ("dp", "pipe")),
    )
    return jax.shard_map(
        body,
        mesh=mesh,
        in_specs=placed,
        out_specs=(
            P(("groups", "expert"), ("dp", "pipe")),
            P(("groups", "dp", "pipe"), "expert"),
            P(("groups", "dp", "pipe"), "expert"),
            P(("groups", "expert"), ("dp", "pipe")),
        ),
        check_vma=False,
    )
```

profile of v0, /device:TPU:0, one launch (start us, length us, event | category | flops | bytes accessed | tf_op | source)
XLA Modules:
  0.0 225.1 jit_solution(16088021885582305294)
XLA Ops:
  7.2 0.0 all-reduce.6.cloned.1.call-start
  7.2 15.8 %all_gather.6 = bf16[128,1024]{1,0:T(8,128)(2,1)S(1)} all-gather(bf16[32,1024]{1,0:T(8,128)(2,1)} %param.9), channel_id=1, replica_groups=mesh['groups'=2,'expert'=4,'dp'=2,'pipe'=2] {'expert'}, dimensions={0}, use_global_device_ids=true | all-gather | bytes 327680 | tf_op jit(solution)/shard_map/all_gather | solution.py:41
  23.1 0.8 compare_reduce_fusion
  23.8 0.1 reshape.77
  23.9 0.8 reduce_window_sum.13
  24.7 0.1 reduce_window_sum.14
  24.8 0.1 add.54
  24.9 0.1 add.55
  25.0 0.0 copy-start.6
  25.0 0.3 convolution_convert_fusion.5
  25.3 0.0 slice-start
  25.3 5.3 %fusion.15 = bf16[4,64,896]{2,1,0:T(8,128)(2,1)} fusion(bf16[4,64,1024]{2,1,0:T(8,128)(2,1)S(1)} %convolution_convert_fusion.5, bf16[128,4,8,896]{3,2,1,0:T(8,128)(2,1)} %bitcast.53), kind=kOutput, calls=%fused_computation.26 | convolution fusion | flops 469991424 | bytes 8323072 | tf_op jit(solution)/shard_map/erd,deh->erh/dot_general | solution.py:54
  30.6 0.0 slice-start.1
  30.6 0.0 copy-done.6
  30.6 0.0 slice-start.2
  30.6 2.1 fusion.12
  32.7 0.0 slice-done
  32.7 0.1 slice-done.1
  32.7 0.0 slice-start.3
  32.7 2.1 convolution_convert_fusion.3
  34.8 0.0 slice-done.2
  34.8 0.1 slice-done.3
  35.0 0.0 copy-start.4
  35.0 0.0 copy-start.5
  35.0 2.1 convolution_convert_fusion.4
  37.0 0.0 all-reduce.6.cloned.1.call-update
  37.1 0.0 reduce-scatter.2.cloned.1.call-start
  37.1 0.0 copy-done.4
  37.1 0.0 copy-done.5
  37.1 0.1 fusion.44
  37.2 64.1 %all-reduce.6.cloned.1.call-done = (bf16[4,64,896]{2,1,0:T(8,128)(2,1)}, bf16[4,64,896]{2,1,0:T(8,128)(2,1)}, bf16[128,3584]{1,0:T(8,128)(2,1)}, bf16[128,3584]{1,0:T(8,128)(2,1)}) async-done(((bf16[4,64,896]{2,1,0:T(8,128)(2,1)}, bf16[4,64,896]{2,1,0:T(8,128)(2,1)}, bf16[128,3584]{1,0:T(8,128)(2,1)}, bf16[128,3584]{1,0:T(8,128)(2,1)}), (bf16[4,64,896]{2,1,0:T(8,128)(2,1)}, bf16[4,64,896]{2,1,0:T(8,128)(2,1)}, ...) | async-done | bytes 2752528 | tf_op jit(solution)/shard_map/psum | solution.py:61
  101.4 0.0 copy-start.7
  101.4 0.0 copy-start.8
  101.4 4.9 %fusion.50 = f32[4,64,1024]{2,1,0:T(8,128)S(1)} fusion(bf16[4,896,1024]{2,1,0:T(8,128)(2,1)} %bitcast.50, bf16[4,64,896]{2,1,0:T(8,128)(2,1)} %get-tuple-element.12, bf16[4,64,896]{2,1,0:T(8,128)(2,1)} %get-tuple-element.13), kind=kOutput, calls=%fused_computation.71 | convolution fusion | flops 471597056 | bytes 9306112 | tf_op jit(solution)/shard_map/erh,ehd->erd/dot_general | solution.py:65
  106.2 0.7 fusion.18
  107.0 0.0 copy-done.7
  107.0 0.0 copy-done.8
  107.0 4.5 %convolution_convert_fusion.7 = bf16[128,1024]{1,0:T(8,128)(2,1)S(1)} fusion(bf16[3584,1024]{1,0:T(8,128)(2,1)} %param.14, bf16[128,3584]{1,0:T(8,128)(2,1)S(1)} %copy-done.7, bf16[128,3584]{1,0:T(8,128)(2,1)S(1)} %copy-done.8), kind=kOutput, calls=%fused_computation.30 | convolution fusion | flops 943325184 | bytes 9437184 | tf_op jit(solution)/shard_map/dot_general | solution.py:73
  111.5 0.0 copy-start
  111.5 0.0 copy-start.1
  111.5 0.8 pad_maximum_fusion
  112.3 0.0 reduce-scatter.2.cloned.1.call-update
  112.3 0.0 all-reduce.4.cloned.1.call-start
  112.4 0.1 select_reduce_fusion
  112.5 21.7 %reduce-scatter.2.cloned.1.call-done = bf16[32,2048]{1,0:T(8,128)(2,1)} async-done(((bf16[128,2048]{1,0:T(8,128)(2,1)}), bf16[32,2048]{1,0:T(8,128)(2,1)}) %reduce-scatter.2.cloned.1.call-update) | async-done | bytes 131088 | tf_op jit(solution)/shard_map/reduce_scatter | solution.py:70
  134.2 0.0 copy-start.3
  134.2 1.0 convert_element_type.104
  135.2 14.3 %all_gather.7 = bf16[128,1024]{1,0:T(8,128)(2,1)S(1)} all-gather(bf16[32,1024]{1,0:T(8,128)(2,1)S(1)} %fusion.37), channel_id=1, replica_groups=mesh['groups'=2,'expert'=4,'dp'=2,'pipe'=2] {'expert'}, dimensions={0}, use_global_device_ids=true | all-gather | bytes 327680 | tf_op jit(solution)/shard_map/all_gather | solution.py:86
  149.5 0.3 fusion.11
  149.8 6.2 %convolution_convert_fusion.6 = bf16[4,64,896]{2,1,0:T(8,128)(2,1)} fusion(bf16[4,64,1024]{2,1,0:T(8,128)(2,1)S(1)} %fusion.11, bf16[4,896,1024]{2,1,0:T(8,128)(2,1)} %bitcast.51), kind=kOutput, calls=%fused_computation.27 | convolution fusion | flops 469991424 | bytes 8323072 | tf_op jit(solution)/shard_map/erd,ehd->erh/dot_general | solution.py:91
  156.0 0.0 all-reduce.4.cloned.1.call-update
  156.0 0.0 copy-done.3
  156.0 0.6 slice.15
  156.7 0.0 copy-done
  156.7 0.0 copy-done.1
  156.7 5.2 %convolution_convert_fusion = bf16[4,896,1024]{2,1,0:T(8,128)(2,1)} fusion(bf16[4,64,1024]{2,1,0:T(8,128)(2,1)S(1)} %fusion.11, bf16[4,64,896]{2,1,0:T(8,128)(2,1)S(1)} %copy-done.1, bf16[4,64,896]{2,1,0:T(8,128)(2,1)S(1)} %copy-done), kind=kOutput, calls=%fused_computation.6 | convolution fusion | flops 475267072 | bytes 8781824 | tf_op jit(solution)/shard_map/erh,erd->ehd/dot_general | solution.py:100
  161.9 25.5 %all-reduce.4.cloned.1.call-done = bf16[4,64,896]{2,1,0:T(8,128)(2,1)} async-done(((bf16[4,64,896]{2,1,0:T(8,128)(2,1)}), bf16[4,64,896]{2,1,0:T(8,128)(2,1)}) %all-reduce.4.cloned.1.call-update) | async-done | bytes 458768 | tf_op jit(solution)/shard_map/psum | solution.py:94
  187.4 6.2 %convolution_convert_fusion.2 = bf16[4,896,1024]{2,1,0:T(8,128)(2,1)} fusion(bf16[4,64,1024]{2,1,0:T(8,128)(2,1)S(1)} %convolution_convert_fusion.5, bf16[4,64,896]{2,1,0:T(8,128)(2,1)S(1)} %copy-done.1, bf16[4,64,896]{2,1,0:T(8,128)(2,1)} %all-reduce.4.cloned.1.call-done, bf16[4,64,896]{2,1,0:T(8,128)(2,1)S(1)} %copy-done), kind=kOutput, calls=%fused_computation.8 | convolution fusion | flops 476413952 | bytes 9240576 | tf_op jit(solution)/shard_map/erd,erh->deh/dot_general | solution.py:103
  193.6 0.0 copy-start.2
  193.6 10.0 %copy.21 = bf16[1024,3584]{1,0:T(8,128)(2,1)} copy(bf16[1024,3584]{0,1:T(8,128)(2,1)} %bitcast.44) | data formatting | bytes 14680064
  203.6 0.0 copy-done.2
  203.6 5.1 %convolution_convert_fusion.1 = bf16[4,896,1024]{2,1,0:T(8,128)(2,1)} fusion(bf16[4,64,1024]{2,1,0:T(8,128)(2,1)S(1)} %convolution_convert_fusion.5, bf16[4,64,896]{2,1,0:T(8,128)(2,1)S(1)} %copy-done, bf16[4,64,896]{2,1,0:T(8,128)(2,1)S(1)} %copy-done.2), kind=kOutput, calls=%fused_computation.7 | convolution fusion | flops 475267072 | bytes 8781824 | tf_op jit(solution)/shard_map/erd,erh->deh/dot_general | solution.py:106
  208.7 9.9 %copy.22 = bf16[1024,3584]{1,0:T(8,128)(2,1)} copy(bf16[1024,3584]{0,1:T(8,128)(2,1)} %bitcast.45) | data formatting | bytes 14680064
  (7 shorter events, 0.0 us)
Async XLA Ops:
  7.2 94.2 %all-reduce.6.cloned.1.call-start = ((), (), s32[]{:S(2)}) async-start(), calls=%async_computation.3 | async-start | bytes 5505024 | tf_op jit(solution)/shard_map/psum | solution.py:61
  25.0 5.6 %copy-start.6 = (bf16[1024,3584]{1,0:T(8,128)(2,1)S(1)}, bf16[1024,3584]{1,0:T(8,128)(2,1)}, u32[]{:S(2)}) copy-start(bf16[1024,3584]{1,0:T(8,128)(2,1)} %param.15) | copy-start | bytes 22020100
  25.3 7.4 %slice-start = ((s8[7340032]{0:T(1024)(128)(4,1)}), s8[4194304]{0:T(1024)(128)(4,1)S(1)}, s32[]{:S(2)}) async-start(s8[7340032]{0:T(1024)(128)(4,1)} %bitcast.46), calls=%async_computation.4 | async-start | bytes 8388608
  30.6 2.1 slice-start.1
  30.6 4.2 %slice-start.2 = ((s8[7340032]{0:T(1024)(128)(4,1)}), s8[4194304]{0:T(1024)(128)(4,1)S(1)}, s32[]{:S(2)}) async-start(s8[7340032]{0:T(1024)(128)(4,1)} %bitcast.48), calls=%async_computation.6 | async-start | bytes 8388608
  32.7 2.2 slice-start.3
  35.0 2.1 copy-start.4
  35.0 2.2 copy-start.5
  37.1 97.1 %reduce-scatter.2.cloned.1.call-start = ((), (), s32[]{:S(2)}) async-start(), calls=%async_computation.1 | async-start | bytes 655360 | tf_op jit(solution)/shard_map/reduce_scatter | solution.py:70
  101.4 5.6 %copy-start.7 = (bf16[128,3584]{1,0:T(8,128)(2,1)S(1)}, bf16[128,3584]{1,0:T(8,128)(2,1)}, u32[]{:S(2)}) copy-start(bf16[128,3584]{1,0:T(8,128)(2,1)} %get-tuple-element.14) | copy-start | bytes 2752516
  101.4 5.6 %copy-start.8 = (bf16[128,3584]{1,0:T(8,128)(2,1)S(1)}, bf16[128,3584]{1,0:T(8,128)(2,1)}, u32[]{:S(2)}) copy-start(bf16[128,3584]{1,0:T(8,128)(2,1)} %get-tuple-element.15) | copy-start | bytes 2752516
  111.5 45.2 %copy-start = (bf16[4,64,896]{2,1,0:T(8,128)(2,1)S(1)}, bf16[4,64,896]{2,1,0:T(8,128)(2,1)}, u32[]{:S(2)}) copy-start(bf16[4,64,896]{2,1,0:T(8,128)(2,1)} %get-tuple-element.13) | copy-start | bytes 1376260
  111.5 45.2 %copy-start.1 = (bf16[4,64,896]{2,1,0:T(8,128)(2,1)S(1)}, bf16[4,64,896]{2,1,0:T(8,128)(2,1)}, u32[]{:S(2)}) copy-start(bf16[4,64,896]{2,1,0:T(8,128)(2,1)} %get-tuple-element.12) | copy-start | bytes 1376260
  112.3 75.1 %all-reduce.4.cloned.1.call-start = ((), (), s32[]{:S(2)}) async-start(), calls=%async_computation.2 | async-start | bytes 917504 | tf_op jit(solution)/shard_map/psum | solution.py:94
  134.2 21.8 %copy-start.3 = (bf16[32,2048]{1,0:T(8,128)(2,1)S(1)}, bf16[32,2048]{1,0:T(8,128)(2,1)}, u32[]{:S(2)}) copy-start(bf16[32,2048]{1,0:T(8,128)(2,1)} %reduce-scatter.2.cloned.1.call-done) | copy-start | bytes 393220
  193.6 10.0 %copy-start.2 = (bf16[4,64,896]{2,1,0:T(8,128)(2,1)S(1)}, bf16[4,64,896]{2,1,0:T(8,128)(2,1)}, u32[]{:S(2)}) copy-start(bf16[4,64,896]{2,1,0:T(8,128)(2,1)} %all-reduce.4.cloned.1.call-done) | copy-start | bytes 1376260
Sparse Core Ops, SparseCore 0:
  37.2 64.1 all-reduce.5
  112.5 21.6 reduce-scatter.1
  156.2 31.1 all-reduce.3
where the time goes:
time: 226 us; the launch traced here: 225 us
  waiting for transfers between devices  111 us (49%)
  matrix products  44.8 us (20%)
  blocking collectives  30.1 us (13%)
  local copies, waits for them, and re-layouts  21.1 us (9%)
  between operations  13.9 us (6%)
  other arithmetic  3.64 us (2%)
    psum x1, waiting for transfers between devices, body(): lax.psum(part_up.astype(jnp.bfloat16), ('dp', 'pipe')).astype(jnp.float32)  64.1 us
    psum x1, waiting for transfers between devices, body(): lax.psum(hidden_part.astype(jnp.bfloat16), ('dp', 'pipe'))  25.5 us
    reduce_scatter x1, waiting for transfers between devices, body(): lax.psum_scatter(jnp.concatenate([jnp.dot(teacher_hidden, teacher_down, p...  21.7 us
    unnamed x28, local copies, waits for them, and re-layouts  20.2 us
    all_gather x1, blocking collectives, body(): gathered = lax.all_gather(tokens, 'expert', axis=0, tiled=True)  15.8 us
    all_gather x1, blocking collectives, body(): residual_all = lax.all_gather(residual, 'expert', axis=0, tiled=True)  14.3 us
    dot_general x1, matrix products, body(): jnp.einsum('erd,ehd->erh', output_grad, down_local, preferred_element_typ...  6.2 us
    dot_general x1, matrix products, body(): jnp.einsum('erd,erh->deh', token_slots, gate_grad, preferred_element_type...  6.19 us
  transfers between devices with their start and end apart: 3, of which 3 were waited for; matrix products, arithmetic and copies ran while one was open for 3% of the time, Pallas kernels for 0%

commit v1 on v0

v1 whole, which is shorter than its diff:
```python
import functools

import jax
import jax.numpy as jnp
from jax import lax
from jax.experimental import pallas as pl
from jax.experimental.pallas import tpu as pltpu
from jax.sharding import PartitionSpec as P

H = 896
BF = jnp.bfloat16
F32 = jnp.float32
VMEM_BYTES = 48 * 1024 * 1024


def shift(value, axis, count, by):
    return lax.ppermute(value, axis, [(i, (i + by) % count) for i in range(count)])


def call(kernel, grid, in_specs, out_specs, out_shape, flops, moved):
    return pl.pallas_call(
        kernel,
        grid=grid,
        in_specs=in_specs,
        out_specs=out_specs,
        out_shape=out_shape,
        compiler_params=pltpu.CompilerParams(vmem_limit_bytes=VMEM_BYTES),
        cost_estimate=pl.CostEstimate(flops=flops, bytes_accessed=moved, transcendentals=0),
    )


def dot(a, b, contract_a=1, contract_b=0):
    return lax.dot_general(
        a, b, (((contract_a,), (contract_b,)), ((), ())), preferred_element_type=F32
    )


def expert_pre_kernel(picker, tokens, gate, up, keep, send):
    half = keep.shape[2]
    rows = dot(picker[0], tokens[...]).astype(BF)
    for which, weight in enumerate((gate, up)):
        product = dot(rows, weight[...]).astype(BF)
        keep[0, which] = product[:half]
        send[0, which] = product[half:]


def expert_pre(picker, tokens, gate, up, first, count):
    slots, token_count = picker.shape[1:]
    width = tokens.shape[1]
    halves = jax.ShapeDtypeStruct((count, 2, slots // 2, H), BF)
    half_spec = pl.BlockSpec((1, 2, slots // 2, H), lambda i: (i, 0, 0, 0))
    weight_spec = pl.BlockSpec((width, H), lambda i: (0, first + i))
    return call(
        expert_pre_kernel,
        (count,),
        [
            pl.BlockSpec((1, slots, token_count), lambda i: (first + i, 0, 0)),
            pl.BlockSpec((token_count, width), lambda i: (0, 0)),
            weight_spec,
            weight_spec,
        ],
        (half_spec, half_spec),
        (halves, halves),
        count * 4 * slots * width * H,
        count * 4 * width * H,
    )(picker, tokens, gate, up)


def student_kernel(picker, hidden, weight, out, total):
    step = pl.program_id(0)
    dense = dot(picker[0], hidden[0], 0, 0).astype(BF)
    product = dot(dense, weight[...])

    @pl.when(step == 0)
    def _():
        total[...] = product

    @pl.when(step > 0)
    def _():
        total[...] += product

    @pl.when(step == pl.num_programs(0) - 1)
    def _():
        out[...] = total[...].astype(BF)


def student_product(picker, hidden, down):
    count, slots, token_count = picker.shape
    width = down.shape[1]
    return pl.pallas_call(
        student_kernel,
        grid=(count,),
        in_specs=[
            pl.BlockSpec((1, slots, token_count), lambda i: (i, 0, 0)),
            pl.BlockSpec((1, slots, H), lambda i: (i, 0, 0)),
            pl.BlockSpec((H, width), lambda i: (i, 0)),
        ],
        out_specs=pl.BlockSpec((token_count, width), lambda i: (0, 0)),
        out_shape=jax.ShapeDtypeStruct((token_count, width), BF),
        scratch_shapes=[pltpu.VMEM((token_count, width), F32)],
        compiler_params=pltpu.CompilerParams(vmem_limit_bytes=VMEM_BYTES),
        cost_estimate=pl.CostEstimate(
            flops=count * 2 * token_count * width * H,
            bytes_accessed=count * 2 * width * H,
            transcendentals=0,
        ),
    )(picker, hidden, down)


def hidden_grad_kernel(picker, residual, weight, keep, send):
    half = keep.shape[1]
    rows = dot(picker[0], residual[...]).astype(BF)
    product = dot(rows, weight[...], 1, 1).astype(BF)
    keep[0] = product[:half]
    send[0] = product[half:]


def hidden_grad_parts(picker, residual, down):
    count, slots, token_count = picker.shape
    width = down.shape[1]
    halves = jax.ShapeDtypeStruct((count, slots // 2, H), BF)
    half_spec = pl.BlockSpec((1, slots // 2, H), lambda i: (i, 0, 0))
    return call(
        hidden_grad_kernel,
        (count,),
        [
            pl.BlockSpec((1, slots, token_count), lambda i: (i, 0, 0)),
            pl.BlockSpec((token_count, width), lambda i: (0, 0)),
            pl.BlockSpec((H, width), lambda i: (i, 0)),
        ],
        (half_spec, half_spec),
        (halves, halves),
        count * 2 * slots * width * H,
        count * 2 * width * H,
    )(picker, residual, down)


def down_grad_kernel(picker, residual, hidden, out):
    rows = dot(picker[0], residual[...]).astype(BF)
    out[...] = dot(hidden[0], rows, 0, 0).astype(BF)


def down_grad(picker, residual, hidden):
    count, slots, token_count = picker.shape
    width = residual.shape[1]
    return call(
        down_grad_kernel,
        (count,),
        [
            pl.BlockSpec((1, slots, token_count), lambda i: (i, 0, 0)),
            pl.BlockSpec((token_count, width), lambda i: (0, 0)),
            pl.BlockSpec((1, slots, H), lambda i: (i, 0, 0)),
        ],
        pl.BlockSpec((H, width), lambda i: (i, 0)),
        jax.ShapeDtypeStruct((count * H, width), BF),
        count * 2 * slots * width * H,
        count * 2 * width * H,
    )(picker, residual, hidden)


def input_grad_kernel(picker, tokens, gate_grad, up_grad, out_gate, out_up):
    rows = dot(picker[0], tokens[...]).astype(BF)
    out_gate[...] = dot(rows, gate_grad[0], 0, 0).astype(BF)
    out_up[...] = dot(rows, up_grad[0], 0, 0).astype(BF)


def input_grads(picker, tokens, gate_grad, up_grad):
    count, slots, token_count = picker.shape
    width = tokens.shape[1]
    grad_spec = pl.BlockSpec((1, slots, H), lambda i: (i, 0, 0))
    out_spec = pl.BlockSpec((width, H), lambda i: (0, i))
    out = jax.ShapeDtypeStruct((width, count * H), BF)
    return call(
        input_grad_kernel,
        (count,),
        [
            pl.BlockSpec((1, slots, token_count), lambda i: (i, 0, 0)),
            pl.BlockSpec((token_count, width), lambda i: (0, 0)),
            grad_spec,
            grad_spec,
        ],
        (out_spec, out_spec),
        (out, out),
        count * 4 * slots * width * H,
        count * 4 * width * H,
    )(picker, tokens, gate_grad, up_grad)


def add(a, b):
    return (a.astype(F32) + b.astype(F32)).astype(BF)


def split_rows(value, count):
    rows = value.shape[-2] // count
    return [value[..., i * rows : (i + 1) * rows, :] for i in range(count)]


def scatter_dp(value, count):
    pieces = split_rows(value, count)
    total = pieces[0].astype(F32)
    for s in range(1, count):
        total = total + shift(pieces[s], "dp", count, s).astype(F32)
    return total


def gather_dp(value, count):
    return jnp.concatenate(
        [value] + [shift(value, "dp", count, -s) for s in range(1, count)], axis=-2
    )


def reduce_dp(value, count):
    if count == 2:
        other = shift(value, "dp", count, 1)
        first, second = split_rows(other, 2)
        return value.astype(F32) + jnp.concatenate([second, first], axis=-2).astype(F32)
    return gather_dp(scatter_dp(value, count).astype(BF), count).astype(F32)


def body(
    tokens,
    routes,
    gate_weights,
    teacher_gate,
    teacher_up,
    teacher_down,
    expert_gate,
    expert_up,
    expert_down,
):
    ranks = lax.axis_size("expert")
    dps = lax.axis_size("dp")
    pipes = lax.axis_size("pipe")
    rank = lax.axis_index("expert")
    dp = lax.axis_index("dp")
    pipe = lax.axis_index("pipe")
    block, width = tokens.shape
    token_count = block * ranks
    capacity = block // 2
    slots = capacity * ranks
    experts = expert_gate.shape[1] // H
    per_piece = ranks // (pipes * dps)

    base = jnp.concatenate(
        [tokens] + [shift(tokens, "expert", ranks, -s) for s in range(1, ranks)], axis=0
    )

    def own_order(table):
        twice = jnp.concatenate([table, table], axis=0)
        return lax.dynamic_slice_in_dim(twice, rank * block, token_count, axis=0)

    names = own_order(routes).T
    shares = own_order(gate_weights).T
    ids = rank * experts + jnp.arange(experts, dtype=jnp.int32)
    matched = names[None, :, :] == ids[:, None, None]
    routed = jnp.any(matched, axis=1)
    weight = jnp.sum(jnp.where(matched, shares[None, :, :], 0.0), axis=1)
    at = jnp.arange(token_count, dtype=jnp.int32)
    earlier = ((at[:, None] // block == at[None, :] // block) & (at[:, None] < at[None, :])).astype(BF)
    within = jnp.dot(routed.astype(BF), earlier, preferred_element_type=F32).astype(jnp.int32)
    at_block = at // block
    at_pipe = at_block // (dps * per_piece)
    at_dp = at_block // per_piece % dps
    place = ((at_pipe + pipes - pipe) % pipes * dps + (at_dp + dps - dp) % dps) * per_piece
    place = (place + at_block % per_piece) * capacity
    slot_of = jnp.where(routed, within + place[None, :], -1)
    picked = slot_of[:, None, :] == jnp.arange(slots, dtype=jnp.int32)[None, :, None]
    picker = picked.astype(BF)
    slot_weight = jnp.sum(jnp.where(picked, weight[:, None, :], 0.0), axis=2)[:, :, None]

    pieces = base.reshape(pipes, dps, per_piece * block, width)
    pieces = jnp.concatenate([pieces, pieces], axis=0)
    pieces = lax.dynamic_slice_in_dim(pieces, pipe, pipes, axis=0)
    pieces = jnp.concatenate([pieces, pieces], axis=1)
    ordered = lax.dynamic_slice_in_dim(pieces, dp, dps, axis=1).reshape(token_count, width)

    def teacher_part(first, size):
        sums = []
        for table in (teacher_gate, teacher_up):
            product = jnp.dot(
                ordered, table[:, first : first + size], preferred_element_type=F32
            ).astype(BF)
            keep, send = split_rows(product, 2)
            half = add(keep, shift(send, "pipe", pipes, 1))
            sums.append(scatter_dp(half, dps))
        hidden = (jax.nn.silu(sums[0]) * sums[1]).astype(BF)
        hidden = gather_dp(hidden, dps)
        other = shift(hidden, "pipe", pipes, 1)
        return jnp.concatenate([hidden, other], axis=0)

    chunks = 2 if teacher_gate.shape[1] % 256 == 0 else 1
    size = teacher_gate.shape[1] // chunks
    hidden = jnp.concatenate([teacher_part(i * size, size) for i in range(chunks)], axis=1)
    hidden = hidden.reshape(pipes, dps, per_piece * block, hidden.shape[1])
    hidden = jnp.concatenate([hidden, hidden], axis=1)
    hidden = lax.dynamic_slice_in_dim(hidden, (dps - dp) % dps, dps, axis=1)
    hidden = jnp.concatenate([hidden, hidden], axis=0)
    hidden = lax.dynamic_slice_in_dim(hidden, (pipes - pipe) % pipes, pipes, axis=0)
    hidden = hidden.reshape(token_count, -1)

    def to_owners(product):
        blocks = split_rows(product, ranks)
        total = blocks[0].astype(F32)
        for s in range(1, ranks):
            total = total + shift(blocks[s], "expert", ranks, s).astype(F32)
        return total

    target = to_owners(jnp.dot(hidden, teacher_down, preferred_element_type=F32).astype(BF))

    group = 2 if experts % 2 == 0 else 1
    pre_gate, pre_up, weighted = [], [], []
    for first in range(0, experts, group):
        keep, send = expert_pre(picker, base, expert_gate, expert_up, first, group)
        half = add(keep, shift(send, "pipe", pipes, 1))
        total = reduce_dp(half, dps)
        mine = slot_weight[first : first + group, : slots // 2]
        part = (jax.nn.silu(total[:, 0]) * total[:, 1] * mine).astype(BF)
        pre_gate.append(total[:, 0])
        pre_up.append(total[:, 1])
        weighted.append(jnp.concatenate([part, shift(part, "pipe", pipes, 1)], axis=1))
    pre_gate = jnp.concatenate(pre_gate, axis=0)
    pre_up = jnp.concatenate(pre_up, axis=0)
    weighted = jnp.concatenate(weighted, axis=0)

    student_sum = to_owners(student_product(picker, weighted, expert_down))
    residual = (student_sum - target).astype(BF)
    residuals = jnp.concatenate(
        [residual] + [shift(residual, "expert", ranks, -s) for s in range(1, ranks)], axis=0
    )

    keep, send = hidden_grad_parts(picker, residuals, expert_down)
    half = add(keep, shift(send, "pipe", pipes, 1))
    hidden_grad = reduce_dp(half, dps) * slot_weight[:, : slots // 2]
    sig = jax.nn.sigmoid(pre_gate)
    gate_grad = (hidden_grad * pre_up * sig * (1.0 + pre_gate * (1.0 - sig))).astype(BF)
    up_grad = (hidden_grad * pre_gate * sig).astype(BF)
    gate_grad = jnp.concatenate([gate_grad, shift(gate_grad, "pipe", pipes, 1)], axis=1)
    up_grad = jnp.concatenate([up_grad, shift(up_grad, "pipe", pipes, 1)], axis=1)

    grad_down = down_grad(picker, residuals, weighted)
    grad_gate, grad_up = input_grads(picker, base, gate_grad, up_grad)
    return (student_sum.astype(BF), grad_gate, grad_up, grad_down)


def solution(mesh):
    placed = (
        P(("groups", "expert"), ("dp", "pipe")),
        P("groups", None),
        P("groups", None),
        P(("dp", "pipe"), "expert"),
        P(("dp", "pipe"), "expert"),
        P("expert", ("dp", "pipe")),
        P(("dp", "pipe"), "expert"),
        P(("dp", "pipe"), "expert"),
        P("expert", ("dp", "pipe")),
    )
    return jax.shard_map(
        body,
        mesh=mesh,
        in_specs=placed,
        out_specs=(
            P(("groups", "expert"), ("dp", "pipe")),
            P(("groups", "dp", "pipe"), "expert"),
            P(("groups", "dp", "pipe"), "expert"),
            P(("groups", "expert"), ("dp", "pipe")),
        ),
        check_vma=False,
    )
```

time: 226 us -> 116 us (0.51)
  waiting for transfers between devices: 111 us -> 35.3 us
  matrix products: 44.8 us -> 8.5 us
  starting transfers between devices: 0.12 us -> 33.2 us
  Pallas kernels: 0 us -> 31 us
  blocking collectives: 30.1 us -> 0 us
  local copies, waits for them, and re-layouts: 21.1 us -> 1.18 us
  between operations: 13.9 us -> 1.18 us
    psum x2 -> x0, waiting for transfers between devices: 89.7 us -> none  [the longest x1 64.1 us: body(): lax.psum(part_up.astype(jnp.bfloat16), ('dp', 'pipe')).astype(jnp.float32)]
    dot_general x13 -> x6, matrix products: 44.8 us -> 8.5 us  [the longest x4 7.17 us: teacher_part(): jnp.dot(ordered, table[:, first:first + size], preferred_element_type=F32)]
    ppermute x0 -> x34, waiting for transfers between devices: none -> 35.3 us  [shift(): lax.ppermute(value, axis, [(i, (i + by) % count) for i in range(count)])]
    ppermute x0 -> x34, starting transfers between devices: none -> 33.2 us  [shift(): lax.ppermute(value, axis, [(i, (i + by) % count) for i in range(count)])]
    pallas_call x0 -> x6, Pallas kernels: none -> 31 us  [the longest x2 8.07 us: expert_pre(): call(expert_pre_kernel, (count,), [pl.BlockSpec((1, slots, token_count),...]
    all_gather x2 -> x0, blocking collectives: 30.1 us -> none  [the longest x1 15.8 us: body(): gathered = lax.all_gather(tokens, 'expert', axis=0, tiled=True)]
    reduce_scatter x1 -> x0, waiting for transfers between devices: 21.7 us -> none  [body(): lax.psum_scatter(jnp.concatenate([jnp.dot(teacher_hidden, teacher_down, p...]
    unnamed x28 -> x9, local copies, waits for them, and re-layouts: 20.2 us -> 0.88 us
  transfers between devices with their start and end apart: 3 -> 34, of which waited for: 3 -> 16; matrix products, arithmetic and copies ran while one was open for 3% -> 6% of each run, Pallas kernels for 0% -> 16%
where the time goes in v1:
time: 116 us; the launch traced here: 115 us
  waiting for transfers between devices  35.3 us (30%)
  starting transfers between devices  33.2 us (29%)
  Pallas kernels  31 us (27%)
  matrix products  8.5 us (7%)
  other arithmetic  5.06 us (4%)
  local copies, waits for them, and re-layouts  1.18 us (1%)
  between operations  1.18 us (1%)
    ppermute x34, waiting for transfers between devices, shift(): lax.ppermute(value, axis, [(i, (i + by) % count) for i in range(count)])  35.3 us
    ppermute x34, starting transfers between devices, shift(): lax.ppermute(value, axis, [(i, (i + by) % count) for i in range(count)])  33.2 us
    pallas_call x2, Pallas kernels, expert_pre(): call(expert_pre_kernel, (count,), [pl.BlockSpec((1, slots, token_count),...  8.07 us
    dot_general x4, matrix products, teacher_part(): jnp.dot(ordered, table[:, first:first + size], preferred_element_type=F32)  7.17 us
    pallas_call x1, Pallas kernels, input_grads(): call(input_grad_kernel, (count,), [pl.BlockSpec((1, slots, token_count),...  6.75 us
    pallas_call x1, Pallas kernels, student_product(): pl.pallas_call(student_kernel, grid=(count,), in_specs=[pl.BlockSpec((1,...  6.05 us
    pallas_call x1, Pallas kernels, hidden_grad_parts(): call(hidden_grad_kernel, (count,), [pl.BlockSpec((1, slots, token_count),...  5.41 us
    pallas_call x1, Pallas kernels, down_grad(): call(down_grad_kernel, (count,), [pl.BlockSpec((1, slots, token_count), l...  4.76 us
  transfers between devices with their start and end apart: 34, of which 16 were waited for; matrix products, arithmetic and copies ran while one was open for 6% of the time, Pallas kernels for 16%

profile of v1, /device:TPU:0, one launch (start us, length us, event | category | flops | bytes accessed | tf_op | source)
XLA Modules:
  0.0 115.4 jit_solution(4061453781238261547)
XLA Ops:
  0.6 5.1 %collective-permute-start = (bf16[32,1024]{1,0:T(8,128)(2,1)}, bf16[32,1024]{1,0:T(8,128)(2,1)S(1)}, u32[]{:S(2)}, u32[]{:S(2)}) collective-permute-start(bf16[32,1024]{1,0:T(8,128)(2,1)} %param.9), channel_id=1, source_target_pairs={{0,12},{4,0},{8,4},{12,8},{1,13},{5,1},{9,5},{13,9},{2,14},{6,2},{... | collective-permute-start | bytes 196616 | tf_op jit(solution)/shard_map/ppermute | solution.py:17
  5.7 1.0 collective-permute-start.2
  6.8 0.8 fusion.40
  7.7 0.2 fusion.21
  7.9 0.8 fusion.38
  8.9 0.1 select_reduce_fusion
  9.0 0.8 constant_dynamic-update-slice_fusion.3
  9.9 2.5 %collective-permute-done.1 = bf16[32,1024]{1,0:T(8,128)(2,1)S(1)} collective-permute-done((bf16[32,1024]{1,0:T(8,128)(2,1)}, bf16[32,1024]{1,0:T(8,128)(2,1)S(1)}, u32[]{:S(2)}, u32[]{:S(2)}) %collective-permute-start.1) | collective-permute-done | bytes 65568 | tf_op jit(solution)/shard_map/ppermute | solution.py:17
  12.4 0.1 fusion.28
  12.6 0.1 fusion.27
  12.7 2.8 %fusion.17 = bf16[128,1792]{1,0:T(8,128)(2,1)S(1)} fusion(bf16[128,1024]{1,0:T(8,128)(2,1)S(1)} %bitcast.43, bf16[1024,3584]{1,0:T(8,128)(2,1)} %param.13), kind=kOutput, calls=%fused_computation.11 | convolution fusion | flops 469991424 | bytes 4390912 | tf_op jit(solution)/shard_map/dot_general | solution.py:280
  15.5 3.0 %fusion.11 = bf16[128,1792]{1,0:T(8,128)(2,1)S(1)} fusion(bf16[128,1024]{1,0:T(8,128)(2,1)S(1)} %bitcast.44, bf16[1024,3584]{1,0:T(8,128)(2,1)} %param.13), kind=kOutput, calls=%fused_computation.9 | convolution fusion | flops 469991424 | bytes 4390912 | tf_op jit(solution)/shard_map/dot_general | solution.py:280
  18.7 0.7 fusion.14
  19.3 0.7 fusion.8
  20.0 0.6 collective-permute-start.18
  20.7 0.6 collective-permute-start.12
  21.3 4.0 %shard_map.121 = (bf16[2,2,32,896]{3,2,1,0:T(8,128)(2,1)S(1)}, bf16[2,2,32,896]{3,2,1,0:T(8,128)(2,1)S(1)}) custom-call(bf16[4,64,128]{2,1,0:T(8,128)(2,1)S(1)} %fusion.29.picker, bf16[128,1024]{1,0:T(8,128)(2,1)S(1)} %constant_dynamic-update-slice_fusion.tokens, bf16[1024,3584]{1,0:T(8,128)(2,1)} %gate.3, bf16[1024,3584]{1,0:T(8,128)(2,1)} %up.3), custom_call_target="tpu_custom_call" | custom-call | flops 469762048 | bytes 7340032 | tf_op jit(solution)/shard_map/pallas_call | solution.py:53
  25.4 4.0 %shard_map.120 = (bf16[2,2,32,896]{3,2,1,0:T(8,128)(2,1)S(1)}, bf16[2,2,32,896]{3,2,1,0:T(8,128)(2,1)S(1)}) custom-call(bf16[4,64,128]{2,1,0:T(8,128)(2,1)S(1)} %fusion.29.picker, bf16[128,1024]{1,0:T(8,128)(2,1)S(1)} %constant_dynamic-update-slice_fusion.tokens, bf16[1024,3584]{1,0:T(8,128)(2,1)} %gate.3, bf16[1024,3584]{1,0:T(8,128)(2,1)} %up.3), custom_call_target="tpu_custom_call" | custom-call | flops 469762048 | bytes 7340032 | tf_op jit(solution)/shard_map/pallas_call | solution.py:53
  29.5 0.5 collective-permute-start.3
  30.2 1.6 %collective-permute-start.21 = (bf16[32,1792]{1,0:T(8,128)(2,1)S(1)}, bf16[32,1792]{1,0:T(8,128)(2,1)S(1)}, u32[]{:S(2)}, u32[]{:S(2)}) collective-permute-start(bf16[32,1792]{1,0:T(8,128)(2,1)S(1)} %slice.195), channel_id=1, source_target_pairs={{0,2},{2,0},{1,3},{3,1},{4,6},{6,4},{5,7},{7,5},{8,10},{10,8},{9,1... | collective-permute-start | bytes 344072 | tf_op jit(solution)/shard_map/ppermute | solution.py:17
  31.8 0.6 collective-permute-start.19
  32.5 1.6 %collective-permute-start.15 = (bf16[32,1792]{1,0:T(8,128)(2,1)S(1)}, bf16[32,1792]{1,0:T(8,128)(2,1)S(1)}, u32[]{:S(2)}, u32[]{:S(2)}) collective-permute-start(bf16[32,1792]{1,0:T(8,128)(2,1)S(1)} %slice.187), channel_id=1, source_target_pairs={{0,2},{2,0},{1,3},{3,1},{4,6},{6,4},{5,7},{7,5},{8,10},{10,8},{9,1... | collective-permute-start | bytes 344072 | tf_op jit(solution)/shard_map/ppermute | solution.py:17
  34.1 0.6 collective-permute-start.13
  34.8 1.6 %collective-permute-start.7 = (bf16[2,2,32,896]{3,2,0,1:T(8,128)(2,1)S(1)}, bf16[2,2,32,896]{3,2,0,1:T(8,128)(2,1)S(1)}, u32[]{:S(2)}, u32[]{:S(2)}) collective-permute-start(bf16[2,2,32,896]{3,2,0,1:T(8,128)(2,1)S(1)} %add_convert_fusion.5), channel_id=1, source_target_pairs={{0,2},{2,0},{1,3},{3,1},{4,6},{6,4},{5,7},{7,5},{8,10},{10,8},{9,1... | collective-permute-start | bytes 688136 | tf_op jit(solution)/shard_map/ppermute | solution.py:17
  36.4 1.3 %collective-permute-start.4 = (bf16[2,2,32,896]{3,2,0,1:T(8,128)(2,1)S(1)}, bf16[2,2,32,896]{3,2,0,1:T(8,128)(2,1)S(1)}, u32[]{:S(2)}, u32[]{:S(2)}) collective-permute-start(bf16[2,2,32,896]{3,2,0,1:T(8,128)(2,1)S(1)} %add_convert_fusion.6), channel_id=1, source_target_pairs={{0,2},{2,0},{1,3},{3,1},{4,6},{6,4},{5,7},{7,5},{8,10},{10,8},{9,1... | collective-permute-start | bytes 688136 | tf_op jit(solution)/shard_map/ppermute | solution.py:17
  37.7 1.0 collective-permute-done.19
  38.7 0.1 multiply_convert_fusion.1
  38.8 1.6 %collective-permute-start.22 = (bf16[32,1792]{1,0:T(8,128)(2,1)S(1)}, bf16[32,1792]{1,0:T(8,128)(2,1)S(1)}, u32[]{:S(2)}, u32[]{:S(2)}) collective-permute-start(bf16[32,1792]{1,0:T(8,128)(2,1)S(1)} %multiply_convert_fusion.1), channel_id=1, source_target_pairs={{0,2},{2,0},{1,3},{3,1},{4,6},{6,4},{5,7},{7,5},{8,10},{10,8},{9,1... | collective-permute-start | bytes 344072 | tf_op jit(solution)/shard_map/ppermute | solution.py:17
  40.3 0.8 collective-permute-done.15
  41.1 2.5 %collective-permute-done.13 = bf16[32,1792]{1,0:T(8,128)(2,1)S(1)} collective-permute-done((bf16[32,1792]{1,0:T(8,128)(2,1)S(1)}, bf16[32,1792]{1,0:T(8,128)(2,1)S(1)}, u32[]{:S(2)}, u32[]{:S(2)}) %collective-permute-start.13) | collective-permute-done | bytes 114720 | tf_op jit(solution)/shard_map/ppermute | solution.py:17
  43.6 0.1 multiply_convert_fusion.2
  43.7 1.6 %collective-permute-start.16 = (bf16[32,1792]{1,0:T(8,128)(2,1)S(1)}, bf16[32,1792]{1,0:T(8,128)(2,1)S(1)}, u32[]{:S(2)}, u32[]{:S(2)}) collective-permute-start(bf16[32,1792]{1,0:T(8,128)(2,1)S(1)} %multiply_convert_fusion.2), channel_id=1, source_target_pairs={{0,2},{2,0},{1,3},{3,1},{4,6},{6,4},{5,7},{7,5},{8,10},{10,8},{9,1... | collective-permute-start | bytes 344072 | tf_op jit(solution)/shard_map/ppermute | solution.py:17
  45.3 10.6 %collective-permute-done.22 = bf16[32,1792]{1,0:T(8,128)(2,1)S(1)} collective-permute-done((bf16[32,1792]{1,0:T(8,128)(2,1)S(1)}, bf16[32,1792]{1,0:T(8,128)(2,1)S(1)}, u32[]{:S(2)}, u32[]{:S(2)}) %collective-permute-start.22) | collective-permute-done | bytes 114720 | tf_op jit(solution)/shard_map/ppermute | solution.py:17
  56.2 0.5 collective-permute-start.8
  57.0 0.4 collective-permute-done.16
  57.4 0.1 collective-permute-start.17
  57.6 0.1 collective-permute-done.8
  57.7 0.6 collective-permute-done.5
  58.4 6.0 %shard_map.122 = bf16[128,1024]{1,0:T(8,128)(2,1)S(1)} custom-call(bf16[4,64,128]{2,1,0:T(8,128)(2,1)S(1)} %fusion.29.picker, bf16[4,64,896]{2,1,0:T(8,128)(2,1)S(1)} %maximum_maximum_fusion.1.hidden, bf16[3584,1024]{1,0:T(8,128)(2,1)} %weight.3), custom_call_target="tpu_custom_call" | custom-call | flops 939524096 | bytes 7340032 | tf_op jit(solution)/shard_map/pallas_call | solution.py:90
  64.4 1.9 %collective-permute-start.11 = (bf16[32,1024]{1,0:T(8,128)(2,1)S(1)}, bf16[32,1024]{1,0:T(8,128)(2,1)S(1)}, u32[]{:S(2)}, u32[]{:S(2)}) collective-permute-start(bf16[32,1024]{1,0:T(8,128)(2,1)S(1)} %get-tuple-element.32), channel_id=1, source_target_pairs={{0,12},{4,0},{8,4},{12,8},{1,13},{5,1},{9,5},{13,9},{2,14},{6,2},{... | collective-permute-start | bytes 196616 | tf_op jit(solution)/shard_map/ppermute | solution.py:17
  66.4 1.9 %collective-permute-start.9 = (bf16[32,1024]{1,0:T(8,128)(2,1)S(1)}, bf16[32,1024]{1,0:T(8,128)(2,1)S(1)}, u32[]{:S(2)}, u32[]{:S(2)}) collective-permute-start(bf16[32,1024]{1,0:T(8,128)(2,1)S(1)} %get-tuple-element.31), channel_id=1, source_target_pairs={{0,4},{4,8},{8,12},{12,0},{1,5},{5,9},{9,13},{13,1},{2,6},{6,10},{... | collective-permute-start | bytes 196616 | tf_op jit(solution)/shard_map/ppermute | solution.py:17
  68.3 0.3 fusion.23
  68.7 0.3 fusion.22
  69.1 1.1 convolution_convert_fusion
  70.2 2.0 %collective-permute-start.26 = (bf16[32,1024]{1,0:T(8,128)(2,1)S(1)}, bf16[32,1024]{1,0:T(8,128)(2,1)S(1)}, u32[]{:S(2)}, u32[]{:S(2)}) collective-permute-start(bf16[32,1024]{1,0:T(8,128)(2,1)S(1)} %get-tuple-element.29), channel_id=1, source_target_pairs={{0,12},{4,0},{8,4},{12,8},{1,13},{5,1},{9,5},{13,9},{2,14},{6,2},{... | collective-permute-start | bytes 196616 | tf_op jit(solution)/shard_map/ppermute | solution.py:17
  72.2 1.1 collective-permute-start.25
  73.4 0.1 collective-permute-start.24
  73.5 0.8 collective-permute-done.10
  74.3 0.9 collective-permute-done.26
  75.2 3.5 %collective-permute-done.25 = bf16[32,1024]{1,0:T(8,128)(2,1)S(1)} collective-permute-done((bf16[32,1024]{1,0:T(8,128)(2,1)S(1)}, bf16[32,1024]{1,0:T(8,128)(2,1)S(1)}, u32[]{:S(2)}, u32[]{:S(2)}) %collective-permute-start.25) | collective-permute-done | bytes 65568 | tf_op jit(solution)/shard_map/ppermute | solution.py:17
  78.7 0.7 collective-permute-done.24
  79.4 0.7 subtract_convert_fusion
  80.1 2.0 %collective-permute-start.28 = (bf16[32,1024]{1,0:T(8,128)(2,1)S(1)}, bf16[32,1024]{1,0:T(8,128)(2,1)S(1)}, u32[]{:S(2)}, u32[]{:S(2)}) collective-permute-start(bf16[32,1024]{1,0:T(8,128)(2,1)S(1)} %get-tuple-element.26), channel_id=1, source_target_pairs={{0,8},{4,12},{8,0},{12,4},{1,9},{5,13},{9,1},{13,5},{2,10},{6,14},... | collective-permute-start | bytes 196616 | tf_op jit(solution)/shard_map/ppermute | solution.py:17
  82.1 2.8 %collective-permute-start.27 = (bf16[32,1024]{1,0:T(8,128)(2,1)S(1)}, bf16[32,1024]{1,0:T(8,128)(2,1)S(1)}, u32[]{:S(2)}, u32[]{:S(2)}) collective-permute-start(bf16[32,1024]{1,0:T(8,128)(2,1)S(1)} %get-tuple-element.26), channel_id=1, source_target_pairs={{0,12},{4,0},{8,4},{12,8},{1,13},{5,1},{9,5},{13,9},{2,14},{6,2},{... | collective-permute-start | bytes 196616 | tf_op jit(solution)/shard_map/ppermute | solution.py:17
  84.9 2.0 %collective-permute-done.29 = bf16[32,1024]{1,0:T(8,128)(2,1)S(1)} collective-permute-done((bf16[32,1024]{1,0:T(8,128)(2,1)S(1)}, bf16[32,1024]{1,0:T(8,128)(2,1)S(1)}, u32[]{:S(2)}, u32[]{:S(2)}) %collective-permute-start.29) | collective-permute-done | bytes 65568 | tf_op jit(solution)/shard_map/ppermute | solution.py:17
  86.9 1.2 %collective-permute-done.28 = bf16[32,1024]{1,0:T(8,128)(2,1)S(1)} collective-permute-done((bf16[32,1024]{1,0:T(8,128)(2,1)S(1)}, bf16[32,1024]{1,0:T(8,128)(2,1)S(1)}, u32[]{:S(2)}, u32[]{:S(2)}) %collective-permute-start.28) | collective-permute-done | bytes 65568 | tf_op jit(solution)/shard_map/ppermute | solution.py:17
  88.1 5.4 %shard_map.123 = (bf16[4,32,896]{2,1,0:T(8,128)(2,1)S(1)}, bf16[4,32,896]{2,1,0:T(8,128)(2,1)S(1)}) custom-call(bf16[4,64,128]{2,1,0:T(8,128)(2,1)S(1)} %fusion.29.picker, bf16[128,1024]{1,0:T(8,128)(2,1)S(1)} %pad_maximum_fusion.3.residual, bf16[3584,1024]{1,0:T(8,128)(2,1)} %weight.3), custom_call_target="tpu_custom_call" | custom-call | flops 469762048 | bytes 7340032 | tf_op jit(solution)/shard_map/pallas_call | solution.py:123
  93.7 1.4 %collective-permute-done.30 = bf16[4,32,896]{2,1,0:T(8,128)(2,1)S(1)} collective-permute-done((bf16[4,32,896]{2,1,0:T(8,128)(2,1)S(1)}, bf16[4,32,896]{2,1,0:T(8,128)(2,1)S(1)}, u32[]{:S(2)}, u32[]{:S(2)}) %collective-permute-start.30) | collective-permute-done | bytes 229408 | tf_op jit(solution)/shard_map/ppermute | solution.py:17
  95.2 1.6 %collective-permute-start.31 = (bf16[4,32,896]{2,1,0:T(8,128)(2,1)S(1)}, bf16[4,32,896]{2,1,0:T(8,128)(2,1)S(1)}, u32[]{:S(2)}, u32[]{:S(2)}) collective-permute-start(bf16[4,32,896]{2,1,0:T(8,128)(2,1)S(1)} %add_convert_fusion), channel_id=1, source_target_pairs={{0,2},{2,0},{1,3},{3,1},{4,6},{6,4},{5,7},{7,5},{8,10},{10,8},{9,1... | collective-permute-start | bytes 688136 | tf_op jit(solution)/shard_map/ppermute | solution.py:17
  96.8 6.1 %collective-permute-done.31 = bf16[4,32,896]{2,1,0:T(8,128)(2,1)S(1)} collective-permute-done((bf16[4,32,896]{2,1,0:T(8,128)(2,1)S(1)}, bf16[4,32,896]{2,1,0:T(8,128)(2,1)S(1)}, u32[]{:S(2)}, u32[]{:S(2)}) %collective-permute-start.31) | collective-permute-done | bytes 229408 | tf_op jit(solution)/shard_map/ppermute | solution.py:17
  102.9 0.3 multiply_convert_fusion
  103.3 0.5 collective-permute-start.33
  103.8 4.8 %shard_map.125 = bf16[3584,1024]{1,0:T(8,128)(2,1)} custom-call(bf16[4,64,128]{2,1,0:T(8,128)(2,1)S(1)} %fusion.29.picker, bf16[128,1024]{1,0:T(8,128)(2,1)S(1)} %pad_maximum_fusion.3.residual, bf16[4,64,896]{2,1,0:T(8,128)(2,1)S(1)} %maximum_maximum_fusion.1.hidden), custom_call_target="tpu_custom_call" | custom-call | flops 469762048 | bytes 7340032 | tf_op jit(solution)/shard_map/pallas_call | solution.py:146
  108.7 6.7 %shard_map.124 = (bf16[1024,3584]{1,0:T(8,128)(2,1)}, bf16[1024,3584]{1,0:T(8,128)(2,1)}) custom-call(bf16[4,64,128]{2,1,0:T(8,128)(2,1)S(1)} %fusion.29.picker, bf16[128,1024]{1,0:T(8,128)(2,1)S(1)} %constant_dynamic-update-slice_fusion.tokens, bf16[4,64,896]{2,1,0:T(8,128)(2,1)S(1)} %pad_maximum_fusion.1.gate_grad, ...), custom_call_target="tpu_custom_call" | custom-call | flops 939524096 | bytes 14680064 | tf_op jit(solution)/shard_map/pallas_call | solution.py:173
  (80 shorter events, 2.1 us)
Async XLA Ops:
  0.6 9.2 %collective-permute-start = (bf16[32,1024]{1,0:T(8,128)(2,1)}, bf16[32,1024]{1,0:T(8,128)(2,1)S(1)}, u32[]{:S(2)}, u32[]{:S(2)}) collective-permute-start(bf16[32,1024]{1,0:T(8,128)(2,1)} %param.9), channel_id=1, source_target_pairs={{0,12},{4,0},{8,4},{12,8},{1,13},{5,1},{9,5},{13,9},{2,14},{6,2},{... | collective-permute-start | bytes 196616 | tf_op jit(solution)/shard_map/ppermute | solution.py:17
  5.7 6.7 %collective-permute-start.1 = (bf16[32,1024]{1,0:T(8,128)(2,1)}, bf16[32,1024]{1,0:T(8,128)(2,1)S(1)}, u32[]{:S(2)}, u32[]{:S(2)}) collective-permute-start(bf16[32,1024]{1,0:T(8,128)(2,1)} %param.9), channel_id=1, source_target_pairs={{0,8},{4,12},{8,0},{12,4},{1,9},{5,13},{9,1},{13,5},{2,10},{6,14},... | collective-permute-start | bytes 196616 | tf_op jit(solution)/shard_map/ppermute | solution.py:17
  5.7 6.7 %collective-permute-start.2 = (bf16[32,1024]{1,0:T(8,128)(2,1)}, bf16[32,1024]{1,0:T(8,128)(2,1)S(1)}, u32[]{:S(2)}, u32[]{:S(2)}) collective-permute-start(bf16[32,1024]{1,0:T(8,128)(2,1)} %param.9), channel_id=1, source_target_pairs={{0,4},{4,8},{8,12},{12,0},{1,5},{5,9},{9,13},{13,1},{2,6},{6,10},{... | collective-permute-start | bytes 196616 | tf_op jit(solution)/shard_map/ppermute | solution.py:17
  12.7 6.0 %copy-start = (bf16[1024,3584]{1,0:T(8,128)(2,1)S(1)}, bf16[1024,3584]{1,0:T(8,128)(2,1)}, u32[]{:S(2)}) copy-start(bf16[1024,3584]{1,0:T(8,128)(2,1)} %param.12) | copy-start | bytes 22020100
  18.6 10.9 %collective-permute-start.20 = (bf16[64,1792]{1,0:T(8,128)(2,1)S(1)}, bf16[64,1792]{1,0:T(8,128)(2,1)S(1)}, u32[]{:S(2)}, u32[]{:S(2)}) collective-permute-start(bf16[64,1792]{1,0:T(8,128)(2,1)S(1)} %slice.193), channel_id=1, source_target_pairs={{0,1},{1,0},{2,3},{3,2},{4,5},{5,4},{6,7},{7,6},{8,9},{9,8},{10,11... | collective-permute-start | bytes 688136 | tf_op jit(solution)/shard_map/ppermute | solution.py:17
  20.0 10.1 %collective-permute-start.18 = (bf16[64,1792]{1,0:T(8,128)(2,1)S(1)}, bf16[64,1792]{1,0:T(8,128)(2,1)S(1)}, u32[]{:S(2)}, u32[]{:S(2)}) collective-permute-start(bf16[64,1792]{1,0:T(8,128)(2,1)S(1)} %slice.189), channel_id=1, source_target_pairs={{0,1},{1,0},{2,3},{3,2},{4,5},{5,4},{6,7},{7,6},{8,9},{9,8},{10,11... | collective-permute-start | bytes 688136 | tf_op jit(solution)/shard_map/ppermute | solution.py:17
  20.6 11.2 %collective-permute-start.14 = (bf16[64,1792]{1,0:T(8,128)(2,1)S(1)}, bf16[64,1792]{1,0:T(8,128)(2,1)S(1)}, u32[]{:S(2)}, u32[]{:S(2)}) collective-permute-start(bf16[64,1792]{1,0:T(8,128)(2,1)S(1)} %slice.185), channel_id=1, source_target_pairs={{0,1},{1,0},{2,3},{3,2},{4,5},{5,4},{6,7},{7,6},{8,9},{9,8},{10,11... | collective-permute-start | bytes 688136 | tf_op jit(solution)/shard_map/ppermute | solution.py:17
  20.7 11.8 %collective-permute-start.12 = (bf16[64,1792]{1,0:T(8,128)(2,1)S(1)}, bf16[64,1792]{1,0:T(8,128)(2,1)S(1)}, u32[]{:S(2)}, u32[]{:S(2)}) collective-permute-start(bf16[64,1792]{1,0:T(8,128)(2,1)S(1)} %slice.181), channel_id=1, source_target_pairs={{0,1},{1,0},{2,3},{3,2},{4,5},{5,4},{6,7},{7,6},{8,9},{9,8},{10,11... | collective-permute-start | bytes 688136 | tf_op jit(solution)/shard_map/ppermute | solution.py:17
  25.3 8.8 %collective-permute-start.6 = (bf16[2,2,32,896]{3,2,0,1:T(8,128)(2,1)S(1)}, bf16[2,2,32,896]{3,2,0,1:T(8,128)(2,1)S(1)}, u32[]{:S(2)}, u32[]{:S(2)}) collective-permute-start(bf16[2,2,32,896]{3,2,0,1:T(8,128)(2,1)S(1)} %copy.20), channel_id=1, source_target_pairs={{0,1},{1,0},{2,3},{3,2},{4,5},{5,4},{6,7},{7,6},{8,9},{9,8},{10,11... | collective-permute-start | bytes 688136 | tf_op jit(solution)/shard_map/ppermute | solution.py:17
  29.5 5.3 %collective-permute-start.3 = (bf16[2,2,32,896]{3,2,0,1:T(8,128)(2,1)S(1)}, bf16[2,2,32,896]{3,2,0,1:T(8,128)(2,1)S(1)}, u32[]{:S(2)}, u32[]{:S(2)}) collective-permute-start(bf16[2,2,32,896]{3,2,0,1:T(8,128)(2,1)S(1)} %copy.18), channel_id=1, source_target_pairs={{0,1},{1,0},{2,3},{3,2},{4,5},{5,4},{6,7},{7,6},{8,9},{9,8},{10,11... | collective-permute-start | bytes 688136 | tf_op jit(solution)/shard_map/ppermute | solution.py:17
  30.2 6.3 %collective-permute-start.21 = (bf16[32,1792]{1,0:T(8,128)(2,1)S(1)}, bf16[32,1792]{1,0:T(8,128)(2,1)S(1)}, u32[]{:S(2)}, u32[]{:S(2)}) collective-permute-start(bf16[32,1792]{1,0:T(8,128)(2,1)S(1)} %slice.195), channel_id=1, source_target_pairs={{0,2},{2,0},{1,3},{3,1},{4,6},{6,4},{5,7},{7,5},{8,10},{10,8},{9,1... | collective-permute-start | bytes 344072 | tf_op jit(solution)/shard_map/ppermute | solution.py:17
  31.8 6.9 %collective-permute-start.19 = (bf16[32,1792]{1,0:T(8,128)(2,1)S(1)}, bf16[32,1792]{1,0:T(8,128)(2,1)S(1)}, u32[]{:S(2)}, u32[]{:S(2)}) collective-permute-start(bf16[32,1792]{1,0:T(8,128)(2,1)S(1)} %slice.191), channel_id=1, source_target_pairs={{0,2},{2,0},{1,3},{3,1},{4,6},{6,4},{5,7},{7,5},{8,10},{10,8},{9,1... | collective-permute-start | bytes 344072 | tf_op jit(solution)/shard_map/ppermute | solution.py:17
  32.5 8.7 %collective-permute-start.15 = (bf16[32,1792]{1,0:T(8,128)(2,1)S(1)}, bf16[32,1792]{1,0:T(8,128)(2,1)S(1)}, u32[]{:S(2)}, u32[]{:S(2)}) collective-permute-start(bf16[32,1792]{1,0:T(8,128)(2,1)S(1)} %slice.187), channel_id=1, source_target_pairs={{0,2},{2,0},{1,3},{3,1},{4,6},{6,4},{5,7},{7,5},{8,10},{10,8},{9,1... | collective-permute-start | bytes 344072 | tf_op jit(solution)/shard_map/ppermute | solution.py:17
  34.1 9.5 %collective-permute-start.13 = (bf16[32,1792]{1,0:T(8,128)(2,1)S(1)}, bf16[32,1792]{1,0:T(8,128)(2,1)S(1)}, u32[]{:S(2)}, u32[]{:S(2)}) collective-permute-start(bf16[32,1792]{1,0:T(8,128)(2,1)S(1)} %slice.183), channel_id=1, source_target_pairs={{0,2},{2,0},{1,3},{3,1},{4,6},{6,4},{5,7},{7,5},{8,10},{10,8},{9,1... | collective-permute-start | bytes 344072 | tf_op jit(solution)/shard_map/ppermute | solution.py:17
  34.8 21.2 %collective-permute-start.7 = (bf16[2,2,32,896]{3,2,0,1:T(8,128)(2,1)S(1)}, bf16[2,2,32,896]{3,2,0,1:T(8,128)(2,1)S(1)}, u32[]{:S(2)}, u32[]{:S(2)}) collective-permute-start(bf16[2,2,32,896]{3,2,0,1:T(8,128)(2,1)S(1)} %add_convert_fusion.5), channel_id=1, source_target_pairs={{0,2},{2,0},{1,3},{3,1},{4,6},{6,4},{5,7},{7,5},{8,10},{10,8},{9,1... | collective-permute-start | bytes 688136 | tf_op jit(solution)/shard_map/ppermute | solution.py:17
  36.4 20.3 %collective-permute-start.4 = (bf16[2,2,32,896]{3,2,0,1:T(8,128)(2,1)S(1)}, bf16[2,2,32,896]{3,2,0,1:T(8,128)(2,1)S(1)}, u32[]{:S(2)}, u32[]{:S(2)}) collective-permute-start(bf16[2,2,32,896]{3,2,0,1:T(8,128)(2,1)S(1)} %add_convert_fusion.6), channel_id=1, source_target_pairs={{0,2},{2,0},{1,3},{3,1},{4,6},{6,4},{5,7},{7,5},{8,10},{10,8},{9,1... | collective-permute-start | bytes 688136 | tf_op jit(solution)/shard_map/ppermute | solution.py:17
  38.8 17.1 %collective-permute-start.22 = (bf16[32,1792]{1,0:T(8,128)(2,1)S(1)}, bf16[32,1792]{1,0:T(8,128)(2,1)S(1)}, u32[]{:S(2)}, u32[]{:S(2)}) collective-permute-start(bf16[32,1792]{1,0:T(8,128)(2,1)S(1)} %multiply_convert_fusion.1), channel_id=1, source_target_pairs={{0,2},{2,0},{1,3},{3,1},{4,6},{6,4},{5,7},{7,5},{8,10},{10,8},{9,1... | collective-permute-start | bytes 344072 | tf_op jit(solution)/shard_map/ppermute | solution.py:17
  43.7 13.7 %collective-permute-start.16 = (bf16[32,1792]{1,0:T(8,128)(2,1)S(1)}, bf16[32,1792]{1,0:T(8,128)(2,1)S(1)}, u32[]{:S(2)}, u32[]{:S(2)}) collective-permute-start(bf16[32,1792]{1,0:T(8,128)(2,1)S(1)} %multiply_convert_fusion.2), channel_id=1, source_target_pairs={{0,2},{2,0},{1,3},{3,1},{4,6},{6,4},{5,7},{7,5},{8,10},{10,8},{9,1... | collective-permute-start | bytes 344072 | tf_op jit(solution)/shard_map/ppermute | solution.py:17
  55.9 12.4 %collective-permute-start.23 = (bf16[64,1792]{1,0:T(8,128)(2,1)S(1)}, bf16[64,1792]{1,0:T(8,128)(2,1)S(1)}, u32[]{:S(2)}, u32[]{:S(2)}) collective-permute-start(bf16[64,1792]{1,0:T(8,128)(2,1)S(1)} %pad_maximum_fusion.5), channel_id=1, source_target_pairs={{0,1},{1,0},{2,3},{3,2},{4,5},{5,4},{6,7},{7,6},{8,9},{9,8},{10,11... | collective-permute-start | bytes 688136 | tf_op jit(solution)/shard_map/ppermute | solution.py:17
  56.2 1.5 %collective-permute-start.8 = (bf16[2,32,896]{2,1,0:T(8,128)(2,1)S(1)}, bf16[2,32,896]{2,1,0:T(8,128)(2,1)S(1)}, u32[]{:S(2)}, u32[]{:S(2)}) collective-permute-start(bf16[2,32,896]{2,1,0:T(8,128)(2,1)S(1)} %multiply_convert_fusion.3), channel_id=1, source_target_pairs={{0,1},{1,0},{2,3},{3,2},{4,5},{5,4},{6,7},{7,6},{8,9},{9,8},{10,11... | collective-permute-start | bytes 344072 | tf_op jit(solution)/shard_map/ppermute | solution.py:17
  56.9 1.4 %collective-permute-start.5 = (bf16[2,32,896]{2,1,0:T(8,128)(2,1)S(1)}, bf16[2,32,896]{2,1,0:T(8,128)(2,1)S(1)}, u32[]{:S(2)}, u32[]{:S(2)}) collective-permute-start(bf16[2,32,896]{2,1,0:T(8,128)(2,1)S(1)} %multiply_convert_fusion.4), channel_id=1, source_target_pairs={{0,1},{1,0},{2,3},{3,2},{4,5},{5,4},{6,7},{7,6},{8,9},{9,8},{10,11... | collective-permute-start | bytes 344072 | tf_op jit(solution)/shard_map/ppermute | solution.py:17
  57.4 10.8 %collective-permute-start.17 = (bf16[64,1792]{1,0:T(8,128)(2,1)S(1)}, bf16[64,1792]{1,0:T(8,128)(2,1)S(1)}, u32[]{:S(2)}, u32[]{:S(2)}) collective-permute-start(bf16[64,1792]{1,0:T(8,128)(2,1)S(1)} %pad_maximum_fusion.4), channel_id=1, source_target_pairs={{0,1},{1,0},{2,3},{3,2},{4,5},{5,4},{6,7},{7,6},{8,9},{9,8},{10,11... | collective-permute-start | bytes 688136 | tf_op jit(solution)/shard_map/ppermute | solution.py:17
  58.3 10.7 %slice-start = ((s8[7340032]{0:T(1024)(128)(4,1)}), s8[4194304]{0:T(1024)(128)(4,1)S(1)}, s32[]{:S(2)}) async-start(s8[7340032]{0:T(1024)(128)(4,1)} %bitcast.39), calls=%async_computation | async-start | bytes 8388608
  58.3 10.7 %slice-start.1 = ((s8[7340032]{0:T(1024)(128)(4,1)}), s8[3145728]{0:T(1024)(128)(4,1)S(1)}, s32[]{:S(2)}) async-start(s8[7340032]{0:T(1024)(128)(4,1)} %bitcast.39), calls=%async_computation.1 | async-start | bytes 6291456
  64.4 8.9 %collective-permute-start.11 = (bf16[32,1024]{1,0:T(8,128)(2,1)S(1)}, bf16[32,1024]{1,0:T(8,128)(2,1)S(1)}, u32[]{:S(2)}, u32[]{:S(2)}) collective-permute-start(bf16[32,1024]{1,0:T(8,128)(2,1)S(1)} %get-tuple-element.32), channel_id=1, source_target_pairs={{0,12},{4,0},{8,4},{12,8},{1,13},{5,1},{9,5},{13,9},{2,14},{6,2},{... | collective-permute-start | bytes 196616 | tf_op jit(solution)/shard_map/ppermute | solution.py:17
  66.4 7.9 %collective-permute-start.10 = (bf16[32,1024]{1,0:T(8,128)(2,1)S(1)}, bf16[32,1024]{1,0:T(8,128)(2,1)S(1)}, u32[]{:S(2)}, u32[]{:S(2)}) collective-permute-start(bf16[32,1024]{1,0:T(8,128)(2,1)S(1)} %get-tuple-element.33), channel_id=1, source_target_pairs={{0,8},{4,12},{8,0},{12,4},{1,9},{5,13},{9,1},{13,5},{2,10},{6,14},... | collective-permute-start | bytes 196616 | tf_op jit(solution)/shard_map/ppermute | solution.py:17
  66.4 7.9 %collective-permute-start.9 = (bf16[32,1024]{1,0:T(8,128)(2,1)S(1)}, bf16[32,1024]{1,0:T(8,128)(2,1)S(1)}, u32[]{:S(2)}, u32[]{:S(2)}) collective-permute-start(bf16[32,1024]{1,0:T(8,128)(2,1)S(1)} %get-tuple-element.31), channel_id=1, source_target_pairs={{0,4},{4,8},{8,12},{12,0},{1,5},{5,9},{9,13},{13,1},{2,6},{6,10},{... | collective-permute-start | bytes 196616 | tf_op jit(solution)/shard_map/ppermute | solution.py:17
  70.2 5.0 %collective-permute-start.26 = (bf16[32,1024]{1,0:T(8,128)(2,1)S(1)}, bf16[32,1024]{1,0:T(8,128)(2,1)S(1)}, u32[]{:S(2)}, u32[]{:S(2)}) collective-permute-start(bf16[32,1024]{1,0:T(8,128)(2,1)S(1)} %get-tuple-element.29), channel_id=1, source_target_pairs={{0,12},{4,0},{8,4},{12,8},{1,13},{5,1},{9,5},{13,9},{2,14},{6,2},{... | collective-permute-start | bytes 196616 | tf_op jit(solution)/shard_map/ppermute | solution.py:17
  72.2 6.5 %collective-permute-start.25 = (bf16[32,1024]{1,0:T(8,128)(2,1)S(1)}, bf16[32,1024]{1,0:T(8,128)(2,1)S(1)}, u32[]{:S(2)}, u32[]{:S(2)}) collective-permute-start(bf16[32,1024]{1,0:T(8,128)(2,1)S(1)} %get-tuple-element.30), channel_id=1, source_target_pairs={{0,8},{4,12},{8,0},{12,4},{1,9},{5,13},{9,1},{13,5},{2,10},{6,14},... | collective-permute-start | bytes 196616 | tf_op jit(solution)/shard_map/ppermute | solution.py:17
  73.4 6.1 %collective-permute-start.24 = (bf16[32,1024]{1,0:T(8,128)(2,1)S(1)}, bf16[32,1024]{1,0:T(8,128)(2,1)S(1)}, u32[]{:S(2)}, u32[]{:S(2)}) collective-permute-start(bf16[32,1024]{1,0:T(8,128)(2,1)S(1)} %get-tuple-element.28), channel_id=1, source_target_pairs={{0,4},{4,8},{8,12},{12,0},{1,5},{5,9},{9,13},{13,1},{2,6},{6,10},{... | collective-permute-start | bytes 196616 | tf_op jit(solution)/shard_map/ppermute | solution.py:17
  80.1 6.8 %collective-permute-start.29 = (bf16[32,1024]{1,0:T(8,128)(2,1)S(1)}, bf16[32,1024]{1,0:T(8,128)(2,1)S(1)}, u32[]{:S(2)}, u32[]{:S(2)}) collective-permute-start(bf16[32,1024]{1,0:T(8,128)(2,1)S(1)} %get-tuple-element.26), channel_id=1, source_target_pairs={{0,4},{4,8},{8,12},{12,0},{1,5},{5,9},{9,13},{13,1},{2,6},{6,10},{... | collective-permute-start | bytes 196616 | tf_op jit(solution)/shard_map/ppermute | solution.py:17
  80.1 8.0 %collective-permute-start.28 = (bf16[32,1024]{1,0:T(8,128)(2,1)S(1)}, bf16[32,1024]{1,0:T(8,128)(2,1)S(1)}, u32[]{:S(2)}, u32[]{:S(2)}) collective-permute-start(bf16[32,1024]{1,0:T(8,128)(2,1)S(1)} %get-tuple-element.26), channel_id=1, source_target_pairs={{0,8},{4,12},{8,0},{12,4},{1,9},{5,13},{9,1},{13,5},{2,10},{6,14},... | collective-permute-start | bytes 196616 | tf_op jit(solution)/shard_map/ppermute | solution.py:17
  82.1 6.0 %collective-permute-start.27 = (bf16[32,1024]{1,0:T(8,128)(2,1)S(1)}, bf16[32,1024]{1,0:T(8,128)(2,1)S(1)}, u32[]{:S(2)}, u32[]{:S(2)}) collective-permute-start(bf16[32,1024]{1,0:T(8,128)(2,1)S(1)} %get-tuple-element.26), channel_id=1, source_target_pairs={{0,12},{4,0},{8,4},{12,8},{1,13},{5,1},{9,5},{13,9},{2,14},{6,2},{... | collective-permute-start | bytes 196616 | tf_op jit(solution)/shard_map/ppermute | solution.py:17
  93.6 1.6 %collective-permute-start.30 = (bf16[4,32,896]{2,1,0:T(8,128)(2,1)S(1)}, bf16[4,32,896]{2,1,0:T(8,128)(2,1)S(1)}, u32[]{:S(2)}, u32[]{:S(2)}) collective-permute-start(bf16[4,32,896]{2,1,0:T(8,128)(2,1)S(1)} %get-tuple-element.17), channel_id=1, source_target_pairs={{0,1},{1,0},{2,3},{3,2},{4,5},{5,4},{6,7},{7,6},{8,9},{9,8},{10,11... | collective-permute-start | bytes 688136 | tf_op jit(solution)/shard_map/ppermute | solution.py:17
  95.2 7.7 %collective-permute-start.31 = (bf16[4,32,896]{2,1,0:T(8,128)(2,1)S(1)}, bf16[4,32,896]{2,1,0:T(8,128)(2,1)S(1)}, u32[]{:S(2)}, u32[]{:S(2)}) collective-permute-start(bf16[4,32,896]{2,1,0:T(8,128)(2,1)S(1)} %add_convert_fusion), channel_id=1, source_target_pairs={{0,2},{2,0},{1,3},{3,1},{4,6},{6,4},{5,7},{7,5},{8,10},{10,8},{9,1... | collective-permute-start | bytes 688136 | tf_op jit(solution)/shard_map/ppermute | solution.py:17
  103.2 5.3 %collective-permute-start.32 = (bf16[4,32,896]{2,1,0:T(8,128)(2,1)S(1)}, bf16[4,32,896]{2,1,0:T(8,128)(2,1)S(1)}, u32[]{:S(2)}, u32[]{:S(2)}) collective-permute-start(bf16[4,32,896]{2,1,0:T(8,128)(2,1)S(1)} %get-tuple-element.21), channel_id=1, source_target_pairs={{0,1},{1,0},{2,3},{3,2},{4,5},{5,4},{6,7},{7,6},{8,9},{9,8},{10,11... | collective-permute-start | bytes 688136 | tf_op jit(solution)/shard_map/ppermute | solution.py:17
  103.3 5.3 %collective-permute-start.33 = (bf16[4,32,896]{2,1,0:T(8,128)(2,1)S(1)}, bf16[4,32,896]{2,1,0:T(8,128)(2,1)S(1)}, u32[]{:S(2)}, u32[]{:S(2)}) collective-permute-start(bf16[4,32,896]{2,1,0:T(8,128)(2,1)S(1)} %get-tuple-element.20), channel_id=1, source_target_pairs={{0,1},{1,0},{2,3},{3,2},{4,5},{5,4},{6,7},{7,6},{8,9},{9,8},{10,11... | collective-permute-start | bytes 688136 | tf_op jit(solution)/shard_map/ppermute | solution.py:17

commit v2 on v0

v2 whole, which is shorter than its diff:
```python
import functools

import jax
import jax.numpy as jnp
from jax import lax
from jax.experimental import pallas as pl
from jax.experimental.pallas import tpu as pltpu
from jax.sharding import PartitionSpec as P

H = 896
BF = jnp.bfloat16
F32 = jnp.float32


def shift(value, axis, count, by):
    return lax.ppermute(value, axis, [(i, (i + by) % count) for i in range(count)])


def dot(a, b, contract_a=1, contract_b=0):
    return lax.dot_general(
        a, b, (((contract_a,), (contract_b,)), ((), ())), preferred_element_type=F32
    )


def whole():
    return pl.BlockSpec(memory_space=pltpu.VMEM)


def in_hbm():
    return pl.BlockSpec(memory_space=pltpu.HBM)


def anywhere():
    return pl.BlockSpec(memory_space=pl.ANY)


def scalars():
    return pl.BlockSpec(memory_space=pltpu.SMEM)


def prepare_kernel(
    ranks, capacity, dps, pipes, place, routes, shares, gate, up, picker, weights, gate_out, up_out, sems
):
    pieces = 8
    rows = gate.shape[0] // pieces
    copies = []
    for which, (source, target) in enumerate(((gate, gate_out), (up, up_out))):
        for i in range(pieces):
            part = pl.ds(i * rows, rows)
            copies.append(
                pltpu.make_async_copy(source.at[part], target.at[part], sems.at[which, i])
            )
    for copy in copies:
        copy.start()
    rank, dp, pipe = place[0], place[1], place[2]
    experts, slots, token_count = picker.shape
    block = token_count // ranks
    per_piece = ranks // (dps * pipes)
    lane = lax.broadcasted_iota(jnp.int32, (token_count, 128), 1)
    names = lane + rank * experts
    weight = jnp.zeros((token_count, 128), F32)
    routed = jnp.zeros((token_count, 128), F32)
    for k in range(routes.shape[1]):
        hit = (routes[:, k : k + 1] == names) & (lane < experts)
        weight = weight + jnp.where(hit, shares[:, k : k + 1], 0.0)
        routed = routed + jnp.where(hit, 1.0, 0.0)
    weight = weight.T
    t_from = lax.broadcasted_iota(jnp.int32, (token_count, token_count), 0)
    t_to = lax.broadcasted_iota(jnp.int32, (token_count, token_count), 1)
    earlier = jnp.where((t_from // block == t_to // block) & (t_from < t_to), 1.0, 0.0)
    routed = routed.T
    within = dot(routed.astype(BF), earlier.astype(BF)).astype(jnp.int32)
    at_block = lax.broadcasted_iota(jnp.int32, (1, token_count), 1) // block
    at_pipe = lax.rem(at_block // (dps * per_piece) + pipes - pipe, pipes)
    at_dp = lax.rem(lax.rem(at_block // per_piece, dps) + dps - dp, dps)
    first = ((at_pipe * dps + at_dp) * per_piece + lax.rem(at_block, per_piece)) * capacity
    slot = jnp.where(routed > 0.0, within + first, -1)
    ids = lax.broadcasted_iota(jnp.int32, (slots, token_count), 0)
    for e in range(experts):
        hit = slot[e : e + 1] == ids
        picker[e] = jnp.where(hit, 1.0, 0.0).astype(BF)
        weights[e] = jnp.sum(jnp.where(hit, weight[e : e + 1], 0.0), axis=1, keepdims=True)
    for copy in copies:
        copy.wait()


def prepare(place, routes, shares, gate, up, ranks, dps, pipes, block, experts):
    capacity = block // 2
    token_count = block * ranks
    slots = capacity * ranks
    return pl.pallas_call(
        functools.partial(prepare_kernel, ranks, capacity, dps, pipes),
        in_specs=[scalars(), whole(), whole(), in_hbm(), in_hbm()],
        out_specs=(whole(), whole(), whole(), whole()),
        out_shape=(
            jax.ShapeDtypeStruct((experts, slots, token_count), BF),
            jax.ShapeDtypeStruct((experts, slots, 1), F32),
            pltpu.VMEM(gate.shape, BF),
            pltpu.VMEM(up.shape, BF),
        ),
        scratch_shapes=[pltpu.SemaphoreType.DMA((2, 8))],
        compiler_params=pltpu.CompilerParams(vmem_limit_bytes=8 * 1024 * 1024),
        cost_estimate=pl.CostEstimate(
            flops=0, bytes_accessed=4 * gate.size, transcendentals=0
        ),
    )(place, routes, shares, gate, up)


def tile_of(size):
    return 256 if size % 256 == 0 else 128


def teacher_kernel(first, size, dps, pipes, place, tokens, gate, up, keep, send):
    dp, pipe = place[1], place[2]
    rows = tokens.shape[0] // (dps * pipes)
    half = dps * rows
    parts = []
    for j1 in range(pipes):
        for j0 in range(dps):
            piece = lax.rem(pipe + j1, pipes) * dps + lax.rem(dp + j0, dps)
            parts.append(tokens[pl.ds(pl.multiple_of(piece * rows, rows), rows), :])
    ordered = jnp.concatenate(parts, axis=0)
    tile = tile_of(size)
    for which, weight in enumerate((gate, up)):
        for i in range(size // tile):
            product = dot(ordered, weight[:, first + i * tile : first + (i + 1) * tile]).astype(BF)
            keep[which, :, i * tile : (i + 1) * tile] = product[:half]
            send[which, :, i * tile : (i + 1) * tile] = product[half:]


def teacher_pre(place, tokens, gate, up, first, size, dps, pipes):
    token_count, width = tokens.shape
    half = jax.ShapeDtypeStruct((2, token_count // pipes, size), BF)
    return pl.pallas_call(
        functools.partial(teacher_kernel, first, size, dps, pipes),
        in_specs=[scalars(), whole(), whole(), whole()],
        out_specs=(whole(), whole()),
        out_shape=(half, half),
        compiler_params=pltpu.CompilerParams(vmem_limit_bytes=8 * 1024 * 1024),
        cost_estimate=pl.CostEstimate(
            flops=4 * token_count * width * size, bytes_accessed=4 * width * size, transcendentals=0
        ),
    )(place, tokens, gate, up)


def expert_kernel(first, picker, tokens, gate, up, before, keep, send):
    half = keep.shape[2]
    for i in range(keep.shape[0]):
        e = first + i
        rows = dot(picker[e], tokens[...]).astype(BF)
        for which, weight in enumerate((gate, up)):
            product = dot(rows, weight[:, e * H : (e + 1) * H]).astype(BF)
            keep[i, which] = product[:half]
            send[i, which] = product[half:]


def expert_pre(picker, tokens, gate, up, before, first, count):
    slots = picker.shape[1]
    width = tokens.shape[1]
    halves = jax.ShapeDtypeStruct((count, 2, slots // 2, H), BF)
    return pl.pallas_call(
        functools.partial(expert_kernel, first),
        in_specs=[whole(), whole(), whole(), whole(), anywhere()],
        out_specs=(whole(), whole()),
        out_shape=(halves, halves),
        compiler_params=pltpu.CompilerParams(vmem_limit_bytes=8 * 1024 * 1024),
        cost_estimate=pl.CostEstimate(
            flops=count * 4 * slots * width * H,
            bytes_accessed=count * 4 * width * H,
            transcendentals=0,
        ),
    )(picker, tokens, gate, up, before)


def spread_kernel(picker, hidden, out):
    for e in range(picker.shape[0]):
        out[:, e * H : (e + 1) * H] = dot(picker[e], hidden[e], 0, 0).astype(BF)


def spread(picker, hidden):
    count, slots, token_count = picker.shape
    return pl.pallas_call(
        spread_kernel,
        in_specs=[whole(), whole()],
        out_specs=whole(),
        out_shape=jax.ShapeDtypeStruct((token_count, count * H), BF),
        compiler_params=pltpu.CompilerParams(vmem_limit_bytes=8 * 1024 * 1024),
    )(picker, hidden)


def pick_kernel(first, picker, dense, keep, send):
    half = keep.shape[1]
    for i in range(keep.shape[0]):
        e = first + i
        rows = dot(picker[e], dense[:, e * H : (e + 1) * H]).astype(BF)
        keep[i] = rows[:half]
        send[i] = rows[half:]


def pick(picker, dense, first, count):
    slots = picker.shape[1]
    halves = jax.ShapeDtypeStruct((count, slots // 2, H), BF)
    return pl.pallas_call(
        functools.partial(pick_kernel, first),
        in_specs=[whole(), whole()],
        out_specs=(whole(), whole()),
        out_shape=(halves, halves),
        compiler_params=pltpu.CompilerParams(vmem_limit_bytes=8 * 1024 * 1024),
    )(picker, dense)


def hidden_grad_act_kernel(first, swap, mine, other, pre, weight, before, out):
    count, rows = mine.shape[:2]
    for i in range(count):
        total = mine[i].astype(F32)
        if swap:
            flipped = jnp.concatenate([other[i, rows // 2 :], other[i, : rows // 2]], axis=0)
            total = total + flipped.astype(F32)
        total = total * weight[first + i, :rows]
        pre_gate, pre_up = pre[i, 0], pre[i, 1]
        sig = jax.nn.sigmoid(pre_gate)
        gate_grad = total * pre_up * sig * (1.0 + pre_gate * (1.0 - sig))
        up_grad = total * pre_gate * sig
        out[i, 0] = gate_grad.astype(BF)
        out[i, 1] = up_grad.astype(BF)


def hidden_grad_act(mine, other, swap, pre, weight, before, first):
    count, rows, width = mine.shape
    return pl.pallas_call(
        functools.partial(hidden_grad_act_kernel, first, swap),
        in_specs=[whole(), whole(), whole(), whole(), anywhere()],
        out_specs=whole(),
        out_shape=jax.ShapeDtypeStruct((count, 2, rows, width), BF),
        compiler_params=pltpu.CompilerParams(vmem_limit_bytes=8 * 1024 * 1024),
    )(mine, other, pre, weight, before)


def down_grad_kernel(picker, residual, hidden, before, out):
    rows = dot(picker[0], residual[...]).astype(BF)
    out[...] = dot(hidden[0], rows, 0, 0).astype(BF)


def down_grad(picker, residual, hidden, before):
    count, slots, token_count = picker.shape
    width = residual.shape[1]
    split = 2 if width % 256 == 0 else 1
    part = width // split
    return pl.pallas_call(
        down_grad_kernel,
        grid=(count, split),
        in_specs=[
            pl.BlockSpec((1, slots, token_count), lambda i, j: (i, 0, 0)),
            pl.BlockSpec((token_count, part), lambda i, j: (0, j)),
            pl.BlockSpec((1, slots, H), lambda i, j: (i, 0, 0)),
            anywhere(),
        ],
        out_specs=pl.BlockSpec((H, part), lambda i, j: (i, j)),
        out_shape=jax.ShapeDtypeStruct((count * H, width), BF),
        compiler_params=pltpu.CompilerParams(vmem_limit_bytes=16 * 1024 * 1024),
        cost_estimate=pl.CostEstimate(
            flops=count * 2 * slots * width * H,
            bytes_accessed=count * 2 * width * H,
            transcendentals=0,
        ),
    )(picker, residual, hidden, before)


def input_grad_kernel(picker, tokens, mine, theirs, *rest):
    out_gate, out_up = rest[-2:]
    rows = dot(picker[0], tokens[...]).astype(BF)
    for which, out in enumerate((out_gate, out_up)):
        grad = jnp.concatenate([mine[0, which], theirs[0, which]], axis=0)
        out[...] = dot(rows, grad, 0, 0).astype(BF)


def input_grads(picker, tokens, mine, theirs, first, so_far):
    experts, slots, token_count = picker.shape
    width = tokens.shape[1]
    count = mine.shape[0]
    split = 2 if width % 256 == 0 else 1
    part = width // split
    grad_spec = pl.BlockSpec((1, 2, slots // 2, H), lambda i, j: (i, 0, 0, 0))
    out_spec = pl.BlockSpec((part, H), lambda i, j: (j, first + i))
    out = jax.ShapeDtypeStruct((width, experts * H), BF)
    extra = () if so_far is None else so_far
    return pl.pallas_call(
        input_grad_kernel,
        grid=(count, split),
        in_specs=[
            pl.BlockSpec((1, slots, token_count), lambda i, j: (first + i, 0, 0)),
            pl.BlockSpec((token_count, part), lambda i, j: (0, j)),
            grad_spec,
            grad_spec,
        ]
        + [in_hbm()] * len(extra),
        out_specs=(out_spec, out_spec),
        out_shape=(out, out),
        input_output_aliases={4 + i: i for i in range(len(extra))},
        compiler_params=pltpu.CompilerParams(vmem_limit_bytes=16 * 1024 * 1024),
        cost_estimate=pl.CostEstimate(
            flops=count * 4 * slots * width * H,
            bytes_accessed=count * 4 * width * H,
            transcendentals=0,
        ),
    )(picker, tokens, mine, theirs, *extra)


def add(a, b):
    return (a.astype(F32) + b.astype(F32)).astype(BF)


def split_rows(value, count):
    rows = value.shape[-2] // count
    return [value[..., i * rows : (i + 1) * rows, :] for i in range(count)]


def scatter_dp(value, count):
    pieces = split_rows(value, count)
    total = pieces[0].astype(F32)
    for s in range(1, count):
        total = total + shift(pieces[s], "dp", count, s).astype(F32)
    return total


def gather_dp(value, count):
    return jnp.concatenate(
        [value] + [shift(value, "dp", count, -s) for s in range(1, count)], axis=-2
    )


def reduce_dp(value, count):
    if count == 2:
        first, second = split_rows(shift(value, "dp", count, 1), 2)
        return value.astype(F32) + jnp.concatenate([second, first], axis=-2).astype(F32)
    return gather_dp(scatter_dp(value, count).astype(BF), count).astype(F32)


def body(
    tokens,
    routes,
    gate_weights,
    teacher_gate,
    teacher_up,
    teacher_down,
    expert_gate,
    expert_up,
    expert_down,
):
    ranks = lax.axis_size("expert")
    dps = lax.axis_size("dp")
    pipes = lax.axis_size("pipe")
    rank = lax.axis_index("expert")
    dp = lax.axis_index("dp")
    pipe = lax.axis_index("pipe")
    block, width = tokens.shape
    token_count = block * ranks
    experts = expert_gate.shape[1] // H
    slots = block // 2 * ranks
    place = jnp.stack([rank, dp, pipe]).astype(jnp.int32)

    def gather_tokens(mine):
        whole_rows = jnp.zeros((token_count, mine.shape[1]), BF)
        whole_rows = lax.dynamic_update_slice(whole_rows, mine, (rank * block, 0))
        for s in range(1, ranks):
            theirs = shift(mine, "expert", ranks, -s)
            at = (rank + s) % ranks * block
            whole_rows = lax.dynamic_update_slice(whole_rows, theirs, (at, 0))
        return whole_rows

    def to_owners(product):
        def block_of(s):
            return lax.dynamic_slice_in_dim(product, (rank + s) % ranks * block, block, axis=0)

        total = block_of(0).astype(F32)
        for s in range(1, ranks):
            total = total + shift(block_of(s), "expert", ranks, s).astype(F32)
        return total

    base = gather_tokens(tokens)
    picker, slot_weight, gate_near, up_near = prepare(
        place, routes, gate_weights, teacher_gate, teacher_up, ranks, dps, pipes, block, experts
    )

    chunks = 2 if teacher_gate.shape[1] % 512 == 0 else 1
    size = teacher_gate.shape[1] // chunks
    halves = []
    for i in range(chunks):
        keep, send = teacher_pre(place, base, gate_near, up_near, i * size, size, dps, pipes)
        halves.append(add(keep, shift(send, "pipe", pipes, 1)))

    group = 2 if experts % 2 == 0 else 1
    firsts = range(0, experts, group)
    expert_halves = []
    for first in firsts:
        keep, send = expert_pre(picker, base, expert_gate, expert_up, halves[0], first, group)
        expert_halves.append(add(keep, shift(send, "pipe", pipes, 1)))

    hiddens = []
    for half in halves:
        total = scatter_dp(half, dps)
        hidden = gather_dp((jax.nn.silu(total[0]) * total[1]).astype(BF), dps)
        hiddens.append(jnp.concatenate([hidden, shift(hidden, "pipe", pipes, 1)], axis=0))
    hidden = jnp.concatenate(hiddens, axis=1)
    hidden = hidden.reshape(pipes, dps, token_count // (pipes * dps), hidden.shape[1])
    hidden = jnp.concatenate([hidden, hidden], axis=1)
    hidden = lax.dynamic_slice_in_dim(hidden, (dps - dp) % dps, dps, axis=1)
    hidden = jnp.concatenate([hidden, hidden], axis=0)
    hidden = lax.dynamic_slice_in_dim(hidden, (pipes - pipe) % pipes, pipes, axis=0)
    hidden = hidden.reshape(token_count, -1)
    target = to_owners(jnp.dot(hidden, teacher_down, preferred_element_type=F32).astype(BF))

    pre, weighted = [], []
    for first, half in zip(firsts, expert_halves):
        total = reduce_dp(half, dps)
        mine = slot_weight[first : first + group, : slots // 2]
        part = (jax.nn.silu(total[:, 0]) * total[:, 1] * mine).astype(BF)
        pre.append(total)
        weighted.append(jnp.concatenate([part, shift(part, "pipe", pipes, 1)], axis=1))
    weighted = jnp.concatenate(weighted, axis=0)

    dense = spread(picker, weighted)
    student_sum = to_owners(jnp.dot(dense, expert_down, preferred_element_type=F32).astype(BF))
    residual = gather_tokens((student_sum - target).astype(BF))

    dense_grad = lax.dot_general(
        residual, expert_down, (((1,), (1,)), ((), ())), preferred_element_type=F32
    ).astype(BF)
    sums = []
    for first in firsts:
        keep, send = pick(picker, dense_grad, first, group)
        sums.append(add(keep, shift(send, "pipe", pipes, 1)))
    others = []
    if dps == 2:
        others = [shift(value, "dp", dps, 1) for value in sums]
    else:
        sums = [gather_dp(scatter_dp(value, dps).astype(BF), dps) for value in sums]
        others = sums
    grad_down = down_grad(picker, residual, weighted, sums[0])
    grads = None
    for i, first in enumerate(firsts):
        mine = hidden_grad_act(
            sums[i], others[i], dps == 2, pre[i], slot_weight, grad_down, first
        )
        grads = input_grads(picker, base, mine, shift(mine, "pipe", pipes, 1), first, grads)
    return (student_sum.astype(BF), grads[0], grads[1], grad_down)


def solution(mesh):
    placed = (
        P(("groups", "expert"), ("dp", "pipe")),
        P("groups", None),
        P("groups", None),
        P(("dp", "pipe"), "expert"),
        P(("dp", "pipe"), "expert"),
        P("expert", ("dp", "pipe")),
        P(("dp", "pipe"), "expert"),
        P(("dp", "pipe"), "expert"),
        P("expert", ("dp", "pipe")),
    )
    return jax.shard_map(
        body,
        mesh=mesh,
        in_specs=placed,
        out_specs=(
            P(("groups", "expert"), ("dp", "pipe")),
            P(("groups", "dp", "pipe"), "expert"),
            P(("groups", "dp", "pipe"), "expert"),
            P(("groups", "expert"), ("dp", "pipe")),
        ),
        check_vma=False,
    )
```

time: 226 us -> 128 us (0.57)
  waiting for transfers between devices: 111 us -> 25.4 us
  matrix products: 44.8 us -> 7.84 us
  blocking collectives: 30.1 us -> 0 us
  starting transfers between devices: 0.12 us -> 28.7 us
  Pallas kernels: 0 us -> 28.5 us
  between operations: 13.9 us -> 1.22 us
  local copies, waits for them, and re-layouts: 21.1 us -> 32 us
    psum x2 -> x0, waiting for transfers between devices: 89.7 us -> none  [the longest x1 64.1 us: body(): lax.psum(part_up.astype(jnp.bfloat16), ('dp', 'pipe')).astype(jnp.float32)]
    dot_general x13 -> x3, matrix products: 44.8 us -> 7.84 us  [the longest x1 5.6 us: body(): lax.dot_general(residual, expert_down, (((1,), (1,)), ((), ())), preferre...]
    all_gather x2 -> x0, blocking collectives: 30.1 us -> none  [the longest x1 15.8 us: body(): gathered = lax.all_gather(tokens, 'expert', axis=0, tiled=True)]
    ppermute x0 -> x32, starting transfers between devices: none -> 28.7 us  [shift(): lax.ppermute(value, axis, [(i, (i + by) % count) for i in range(count)])]
    pallas_call x0 -> x13, Pallas kernels: none -> 28.5 us  [the longest x2 8.97 us: input_grads(): pl.pallas_call(input_grad_kernel, grid=(count, split), in_specs=[pl.Block...]
    ppermute x0 -> x32, waiting for transfers between devices: none -> 25.4 us  [shift(): lax.ppermute(value, axis, [(i, (i + by) % count) for i in range(count)])]
    reduce_scatter x1 -> x0, waiting for transfers between devices: 21.7 us -> none  [body(): lax.psum_scatter(jnp.concatenate([jnp.dot(teacher_hidden, teacher_down, p...]
    unnamed x28 -> x44, local copies, waits for them, and re-layouts: 20.2 us -> 30.8 us
  transfers between devices with their start and end apart: 3 -> 32, of which waited for: 3 -> 11; matrix products, arithmetic and copies ran while one was open for 3% -> 7% of each run, Pallas kernels for 0% -> 17%
where the time goes in v2:
time: 128 us; the launch traced here: 127 us
  local copies, waits for them, and re-layouts  32 us (25%)
  starting transfers between devices  28.7 us (22%)
  Pallas kernels  28.5 us (22%)
  waiting for transfers between devices  25.4 us (20%)
  matrix products  7.84 us (6%)
  other arithmetic  3.65 us (3%)
    unnamed x44, local copies, waits for them, and re-layouts  30.8 us
    ppermute x32, starting transfers between devices, shift(): lax.ppermute(value, axis, [(i, (i + by) % count) for i in range(count)])  28.7 us
    ppermute x32, waiting for transfers between devices, shift(): lax.ppermute(value, axis, [(i, (i + by) % count) for i in range(count)])  25.4 us
    pallas_call x2, Pallas kernels, input_grads(): pl.pallas_call(input_grad_kernel, grid=(count, split), in_specs=[pl.Block...  8.97 us
    pallas_call x1, Pallas kernels, down_grad(): pl.pallas_call(down_grad_kernel, grid=(count, split), in_specs=[pl.BlockS...  6.42 us
    dot_general x1, matrix products, body(): lax.dot_general(residual, expert_down, (((1,), (1,)), ((), ())), preferre...  5.6 us
    pallas_call x1, Pallas kernels, prepare(): pl.pallas_call(functools.partial(prepare_kernel, ranks, capacity, dps, pi...  4.74 us
    pallas_call x2, Pallas kernels, teacher_pre(): pl.pallas_call(functools.partial(teacher_kernel, first, size, dps, pipes)...  4.11 us
  transfers between devices with their start and end apart: 32, of which 11 were waited for; matrix products, arithmetic and copies ran while one was open for 7% of the time, Pallas kernels for 17%

profile of v2, /device:TPU:0, one launch (start us, length us, event | category | flops | bytes accessed | tf_op | source)
XLA Modules:
  0.0 127.3 jit_solution(15430565252191733701)
XLA Ops:
  0.6 5.1 %collective-permute-start = (bf16[32,1024]{1,0:T(8,128)(2,1)}, bf16[32,1024]{1,0:T(8,128)(2,1)S(1)}, u32[]{:S(2)}, u32[]{:S(2)}) collective-permute-start(bf16[32,1024]{1,0:T(8,128)(2,1)} %param.9), channel_id=1, source_target_pairs={{0,12},{4,0},{8,4},{12,8},{1,13},{5,1},{9,5},{13,9},{2,14},{6,2},{... | collective-permute-start | bytes 196616 | tf_op jit(solution)/shard_map/ppermute | solution.py:16
  5.7 1.0 collective-permute-start.1
  6.7 0.8 copy.21.routes
  7.5 0.8 copy.22.shares
  8.4 3.1 %copy-done.8 = bf16[1024,3584]{1,0:T(8,128)(2,1)S(1)} copy-done((bf16[1024,3584]{1,0:T(8,128)(2,1)S(1)}, bf16[1024,3584]{1,0:T(8,128)(2,1)}, u32[]{:S(2)}) %copy-start.8) | copy-done | bytes 7340056
  11.5 3.1 %copy-done.9 = bf16[1024,3584]{1,0:T(8,128)(2,1)S(1)} copy-done((bf16[1024,3584]{1,0:T(8,128)(2,1)S(1)}, bf16[1024,3584]{1,0:T(8,128)(2,1)}, u32[]{:S(2)}) %copy-start.9) | copy-done | bytes 7340056
  14.6 4.7 %shard_map.120 = (bf16[4,64,128]{2,1,0:T(8,128)(2,1)S(1)}, f32[4,64,1]{2,1,0:T(8,128)S(1)}, bf16[1024,3584]{1,0:T(8,128)(2,1)S(1)}, bf16[1024,3584]{1,0:T(8,128)(2,1)S(1)}) custom-call(s32[3]{0:T(128)S(1)} %pad_add_fusion.place, s32[128,4]{1,0:T(8,128)S(1)} %copy.21.routes, f32[128,4]{1,0:T(8,128)S(1)} %copy.22.shares, bf16[1024,3584]{1,0:T(8,128)(2,1)S(1)} %copy-done.8, ...), custom_call_target="tpu_custom_call" | custom-call | bytes 14680064 | tf_op jit(solution)/shard_map/pallas_call | solution.py:91
  19.3 0.7 copy-done.10
  20.2 2.4 %shard_map.125 = (bf16[2,64,1792]{2,1,0:T(8,128)(2,1)S(1)}, bf16[2,64,1792]{2,1,0:T(8,128)(2,1)}) custom-call(s32[3]{0:T(128)S(1)} %pad_add_fusion.place, bf16[128,1024]{1,0:T(8,128)(2,1)S(1)} %constant_dynamic-update-slice_fusion.4.tokens, bf16[1024,3584]{1,0:T(8,128)(2,1)S(1)} %get-tuple-element.25.gate, bf16[1024,3584]{1,0:T(8,128)(2,1)S(1)} %get-tuple-element.26.up), custom_call_target="tpu_custom_call" | custom-call | flops 939524096 | bytes 7340032 | tf_op jit(solution)/shard_map/pallas_call | solution.py:134
  22.6 1.1 copy-done.2
  23.7 2.2 %copy-done.4 = bf16[1024,3584]{1,0:T(8,128)(2,1)} copy-done((bf16[1024,3584]{1,0:T(8,128)(2,1)}, bf16[1024,3584]{1,0:T(8,128)(2,1)S(1)}, u32[]{:S(2)}) %copy-start.4) | copy-done | bytes 7340056
  25.9 0.8 copy-done.12
  26.7 0.9 slice_reduce_fusion.1
  27.6 3.1 %copy-done.3 = bf16[1024,3584]{1,0:T(8,128)(2,1)S(1)} copy-done((bf16[1024,3584]{1,0:T(8,128)(2,1)S(1)}, bf16[1024,3584]{1,0:T(8,128)(2,1)}, u32[]{:S(2)}) %copy-start.3) | copy-done | bytes 7340056
  30.7 3.1 %copy-done.5 = bf16[1024,3584]{1,0:T(8,128)(2,1)S(1)} copy-done((bf16[1024,3584]{1,0:T(8,128)(2,1)S(1)}, bf16[1024,3584]{1,0:T(8,128)(2,1)}, u32[]{:S(2)}) %copy-start.5) | copy-done | bytes 7340056
  33.8 1.7 %shard_map.121 = (bf16[2,64,1792]{2,1,0:T(8,128)(2,1)S(1)}, bf16[2,64,1792]{2,1,0:T(8,128)(2,1)S(1)}) custom-call(s32[3]{0:T(128)S(1)} %pad_add_fusion.place, bf16[128,1024]{1,0:T(8,128)(2,1)S(1)} %constant_dynamic-update-slice_fusion.4.tokens, bf16[1024,3584]{1,0:T(8,128)(2,1)S(1)} %copy-done.3, bf16[1024,3584]{1,0:T(8,128)(2,1)S(1)} %copy-done.5), custom_call_target="tpu_custom_call" | custom-call | flops 939524096 | bytes 7340032 | tf_op jit(solution)/shard_map/pallas_call | solution.py:134
  35.4 0.6 collective-permute-start.3
  36.0 1.2 add_convert_fusion
  37.2 1.6 %collective-permute-start.17 = (bf16[2,32,1792]{2,1,0:T(8,128)(2,1)S(1)}, bf16[2,32,1792]{2,1,0:T(8,128)(2,1)S(1)}, u32[]{:S(2)}, u32[]{:S(2)}) collective-permute-start(bf16[2,32,1792]{2,1,0:T(8,128)(2,1)S(1)} %slice.85), channel_id=1, source_target_pairs={{0,2},{2,0},{1,3},{3,1},{4,6},{6,4},{5,7},{7,5},{8,10},{10,8},{9,1... | collective-permute-start | bytes 688136 | tf_op jit(solution)/shard_map/ppermute | solution.py:16
  38.9 0.6 collective-permute-start.13
  39.5 3.1 %copy-done.6 = bf16[1024,3584]{1,0:T(8,128)(2,1)S(1)} copy-done((bf16[1024,3584]{1,0:T(8,128)(2,1)S(1)}, bf16[1024,3584]{1,0:T(8,128)(2,1)}, u32[]{:S(2)}) %copy-start.6) | copy-done | bytes 7340056
  42.6 1.6 %shard_map.123 = (bf16[2,2,32,896]{3,2,1,0:T(8,128)(2,1)S(1)}, bf16[2,2,32,896]{3,2,1,0:T(8,128)(2,1)S(1)}) custom-call(bf16[4,64,128]{2,1,0:T(8,128)(2,1)S(1)} %get-tuple-element.24.picker, bf16[128,1024]{1,0:T(8,128)(2,1)S(1)} %constant_dynamic-update-slice_fusion.4.tokens, bf16[1024,3584]{1,0:T(8,128)(2,1)S(1)} %bitcast.58, ...), custom_call_target="tpu_custom_call" | custom-call | flops 469762048 | bytes 7340032 | tf_op jit(solution)/shard_map/pallas_call | solution.py:161
  44.3 3.1 %copy-done.7 = bf16[1024,3584]{1,0:T(8,128)(2,1)S(1)} copy-done((bf16[1024,3584]{1,0:T(8,128)(2,1)S(1)}, bf16[1024,3584]{1,0:T(8,128)(2,1)}, u32[]{:S(2)}) %copy-start.7) | copy-done | bytes 7340056
  47.4 1.6 %shard_map.122 = (bf16[2,2,32,896]{3,2,1,0:T(8,128)(2,1)S(1)}, bf16[2,2,32,896]{3,2,1,0:T(8,128)(2,1)S(1)}) custom-call(bf16[4,64,128]{2,1,0:T(8,128)(2,1)S(1)} %get-tuple-element.24.picker, bf16[128,1024]{1,0:T(8,128)(2,1)S(1)} %constant_dynamic-update-slice_fusion.4.tokens, bf16[1024,3584]{1,0:T(8,128)(2,1)S(1)} %bitcast.58, ...), custom_call_target="tpu_custom_call" | custom-call | flops 469762048 | bytes 7340032 | tf_op jit(solution)/shard_map/pallas_call | solution.py:161
  48.9 0.6 collective-permute-start.4
  49.6 1.6 %collective-permute-start.18 = (bf16[32,1792]{1,0:T(8,128)(2,1)S(1)}, bf16[32,1792]{1,0:T(8,128)(2,1)S(1)}, u32[]{:S(2)}, u32[]{:S(2)}) collective-permute-start(bf16[32,1792]{1,0:T(8,128)(2,1)S(1)} %fusion.3), channel_id=1, source_target_pairs={{0,2},{2,0},{1,3},{3,1},{4,6},{6,4},{5,7},{7,5},{8,10},{10,8},{9,1... | collective-permute-start | bytes 344072 | tf_op jit(solution)/shard_map/ppermute | solution.py:16
  51.3 0.6 collective-permute-start.14
  52.0 1.6 %collective-permute-start.8 = (bf16[2,2,32,896]{3,2,0,1:T(8,128)(2,1)S(1)}, bf16[2,2,32,896]{3,2,0,1:T(8,128)(2,1)S(1)}, u32[]{:S(2)}, u32[]{:S(2)}) collective-permute-start(bf16[2,2,32,896]{3,2,0,1:T(8,128)(2,1)S(1)} %add_convert_fusion.2), channel_id=1, source_target_pairs={{0,2},{2,0},{1,3},{3,1},{4,6},{6,4},{5,7},{7,5},{8,10},{10,8},{9,1... | collective-permute-start | bytes 688136 | tf_op jit(solution)/shard_map/ppermute | solution.py:16
  53.6 0.6 collective-permute-start.5
  54.2 1.5 %collective-permute-done.18 = bf16[32,1792]{1,0:T(8,128)(2,1)S(1)} collective-permute-done((bf16[32,1792]{1,0:T(8,128)(2,1)S(1)}, bf16[32,1792]{1,0:T(8,128)(2,1)S(1)}, u32[]{:S(2)}, u32[]{:S(2)}) %collective-permute-start.18) | collective-permute-done | bytes 114720 | tf_op jit(solution)/shard_map/ppermute | solution.py:16
  55.8 2.4 %collective-permute-done.14 = bf16[32,1792]{1,0:T(8,128)(2,1)S(1)} collective-permute-done((bf16[32,1792]{1,0:T(8,128)(2,1)S(1)}, bf16[32,1792]{1,0:T(8,128)(2,1)S(1)}, u32[]{:S(2)}, u32[]{:S(2)}) %collective-permute-start.14) | collective-permute-done | bytes 114720 | tf_op jit(solution)/shard_map/ppermute | solution.py:16
  58.2 4.8 %collective-permute-done.8 = bf16[2,2,32,896]{3,2,0,1:T(8,128)(2,1)S(1)} collective-permute-done((bf16[2,2,32,896]{3,2,0,1:T(8,128)(2,1)S(1)}, bf16[2,2,32,896]{3,2,0,1:T(8,128)(2,1)S(1)}, u32[]{:S(2)}, u32[]{:S(2)}) %collective-permute-start.8) | collective-permute-done | bytes 229408 | tf_op jit(solution)/shard_map/ppermute | solution.py:16
  63.3 3.7 %collective-permute-done.5 = bf16[2,2,32,896]{3,2,1,0:T(8,128)(2,1)S(1)} collective-permute-done((bf16[2,2,32,896]{3,2,1,0:T(8,128)(2,1)S(1)}, bf16[2,2,32,896]{3,2,1,0:T(8,128)(2,1)S(1)}, u32[]{:S(2)}, u32[]{:S(2)}) %collective-permute-start.5) | collective-permute-done | bytes 229408 | tf_op jit(solution)/shard_map/ppermute | solution.py:16
  67.4 0.3 fusion.1
  67.8 0.3 fusion
  68.1 1.1 convolution_convert_fusion.1
  69.3 3.4 %collective-permute-start.20 = (bf16[32,1024]{1,0:T(8,128)(2,1)S(1)}, bf16[32,1024]{1,0:T(8,128)(2,1)S(1)}, u32[]{:S(2)}, u32[]{:S(2)}) collective-permute-start(bf16[32,1024]{1,0:T(8,128)(2,1)S(1)} %get-tuple-element.48), channel_id=1, source_target_pairs={{0,4},{4,8},{8,12},{12,0},{1,5},{5,9},{9,13},{13,1},{2,6},{6,10},{... | collective-permute-start | bytes 196616 | tf_op jit(solution)/shard_map/ppermute | solution.py:16
  72.7 0.4 collective-permute-start.22
  73.2 1.1 collective-permute-start.21
  74.3 0.4 shard_map.124
  74.8 1.1 convolution_convert_fusion.2
  75.9 0.6 collective-permute-start.10
  76.5 3.3 %collective-permute-start.12 = (bf16[32,1024]{1,0:T(8,128)(2,1)S(1)}, bf16[32,1024]{1,0:T(8,128)(2,1)S(1)}, u32[]{:S(2)}, u32[]{:S(2)}) collective-permute-start(bf16[32,1024]{1,0:T(8,128)(2,1)S(1)} %get-tuple-element.52), channel_id=1, source_target_pairs={{0,12},{4,0},{8,4},{12,8},{1,13},{5,1},{9,5},{13,9},{2,14},{6,2},{... | collective-permute-start | bytes 196616 | tf_op jit(solution)/shard_map/ppermute | solution.py:16
  80.0 2.9 %collective-permute-done.10 = bf16[32,1024]{1,0:T(8,128)(2,1)S(1)} collective-permute-done((bf16[32,1024]{1,0:T(8,128)(2,1)S(1)}, bf16[32,1024]{1,0:T(8,128)(2,1)S(1)}, u32[]{:S(2)}, u32[]{:S(2)}) %collective-permute-start.10) | collective-permute-done | bytes 65568 | tf_op jit(solution)/shard_map/ppermute | solution.py:16
  82.8 2.8 %collective-permute-done.11 = bf16[32,1024]{1,0:T(8,128)(2,1)S(1)} collective-permute-done((bf16[32,1024]{1,0:T(8,128)(2,1)S(1)}, bf16[32,1024]{1,0:T(8,128)(2,1)S(1)}, u32[]{:S(2)}, u32[]{:S(2)}) %collective-permute-start.11) | collective-permute-done | bytes 65568 | tf_op jit(solution)/shard_map/ppermute | solution.py:16
  85.7 2.2 %collective-permute-start.23 = (bf16[32,1024]{1,0:T(8,128)(2,1)S(1)}, bf16[32,1024]{1,0:T(8,128)(2,1)S(1)}, u32[]{:S(2)}, u32[]{:S(2)}) collective-permute-start(bf16[32,1024]{1,0:T(8,128)(2,1)S(1)} %get-tuple-element.47), channel_id=1, source_target_pairs={{0,12},{4,0},{8,4},{12,8},{1,13},{5,1},{9,5},{13,9},{2,14},{6,2},{... | collective-permute-start | bytes 196616 | tf_op jit(solution)/shard_map/ppermute | solution.py:16
  87.9 0.6 collective-permute-start.25
  88.6 1.9 %collective-permute-done.23 = bf16[32,1024]{1,0:T(8,128)(2,1)S(1)} collective-permute-done((bf16[32,1024]{1,0:T(8,128)(2,1)S(1)}, bf16[32,1024]{1,0:T(8,128)(2,1)S(1)}, u32[]{:S(2)}, u32[]{:S(2)}) %collective-permute-start.23) | collective-permute-done | bytes 65568 | tf_op jit(solution)/shard_map/ppermute | solution.py:16
  90.5 4.0 %collective-permute-done.24 = bf16[32,1024]{1,0:T(8,128)(2,1)S(1)} collective-permute-done((bf16[32,1024]{1,0:T(8,128)(2,1)S(1)}, bf16[32,1024]{1,0:T(8,128)(2,1)S(1)}, u32[]{:S(2)}, u32[]{:S(2)}) %collective-permute-start.24) | collective-permute-done | bytes 65568 | tf_op jit(solution)/shard_map/ppermute | solution.py:16
  94.5 5.6 %convolution_convert_fusion.dense = bf16[128,3584]{1,0:T(8,128)(2,1)S(1)} fusion(bf16[128,1024]{1,0:T(8,128)(2,1)S(1)} %constant_dynamic-update-slice_fusion.residual, bf16[3584,1024]{1,0:T(8,128)(2,1)} %param.17), kind=kOutput, calls=%fused_computation | convolution fusion | flops 939982848 | bytes 8519680 | tf_op jit(solution)/shard_map/dot_general | solution.py:426
  100.2 0.2 shard_map.126
  100.5 0.2 shard_map.127
  100.7 0.6 collective-permute-start.28
  101.2 0.5 collective-permute-done.26
  101.8 1.6 %collective-permute-start.27 = (bf16[2,32,896]{2,1,0:T(8,128)(2,1)S(1)}, bf16[2,32,896]{2,1,0:T(8,128)(2,1)S(1)}, u32[]{:S(2)}, u32[]{:S(2)}) collective-permute-start(bf16[2,32,896]{2,1,0:T(8,128)(2,1)S(1)} %add_convert_fusion.5.mine), channel_id=1, source_target_pairs={{0,2},{2,0},{1,3},{3,1},{4,6},{6,4},{5,7},{7,5},{8,10},{10,8},{9,1... | collective-permute-start | bytes 344072 | tf_op jit(solution)/shard_map/ppermute | solution.py:16
  103.4 0.6 collective-permute-start.30
  104.0 6.4 %shard_map.128.before = bf16[3584,1024]{1,0:T(8,128)(2,1)} custom-call(bf16[4,64,128]{2,1,0:T(8,128)(2,1)S(1)} %get-tuple-element.24.picker, bf16[128,1024]{1,0:T(8,128)(2,1)S(1)} %constant_dynamic-update-slice_fusion.residual, bf16[4,64,896]{2,1,0:T(8,128)(2,1)S(1)} %maximum_maximum_fusion.1.hidden, bf16[2,32,896]{2,1,0:T(8,128)(2,1)S(1)} %add_convert_fusion.4.before.mine), custom_call_target="tpu_custom_call" | custom-call | flops 469762048 | bytes 7340032 | tf_op jit(solution)/shard_map/pallas_call | solution.py:249
  110.5 3.1 %copy-done = bf16[3584,1024]{1,0:T(8,128)(2,1)S(1)} copy-done((bf16[3584,1024]{1,0:T(8,128)(2,1)S(1)}, bf16[3584,1024]{1,0:T(8,128)(2,1)}, u32[]{:S(2)}) %copy-start) | copy-done | bytes 7340056
  113.5 0.1 shard_map.129.mine
  113.8 2.8 %copy-done.1 = bf16[3584,1024]{1,0:T(8,128)(2,1)S(1)} copy-done((bf16[3584,1024]{1,0:T(8,128)(2,1)S(1)}, bf16[3584,1024]{1,0:T(8,128)(2,1)}, u32[]{:S(2)}) %copy-start.1) | copy-done | bytes 7340056
  116.8 0.7 fusion.12
  117.5 0.8 collective-permute-done.31.theirs
  118.3 4.5 %shard_map.131 = (bf16[1024,3584]{1,0:T(8,128)(2,1)}, bf16[1024,3584]{1,0:T(8,128)(2,1)}) custom-call(bf16[4,64,128]{2,1,0:T(8,128)(2,1)S(1)} %get-tuple-element.24.picker, bf16[128,1024]{1,0:T(8,128)(2,1)S(1)} %constant_dynamic-update-slice_fusion.4.tokens, bf16[2,2,32,896]{3,2,1,0:T(8,128)(2,1)S(1)} %shard_map.130.mine, ...), custom_call_target="tpu_custom_call" | custom-call | flops 469762048 | bytes 7340032 | tf_op jit(solution)/shard_map/pallas_call | solution.py:287
  122.8 4.5 %shard_map.132 = (bf16[1024,3584]{1,0:T(8,128)(2,1)}, bf16[1024,3584]{1,0:T(8,128)(2,1)}) custom-call(bf16[4,64,128]{2,1,0:T(8,128)(2,1)S(1)} %get-tuple-element.24.picker, bf16[128,1024]{1,0:T(8,128)(2,1)S(1)} %constant_dynamic-update-slice_fusion.4.tokens, ...), custom_call_target="tpu_custom_call", output_to_operand_aliasing={{0}: (4, {}), {1}: (5, {})} | custom-call | flops 469762048 | bytes 7340032 | tf_op jit(solution)/shard_map/pallas_call | solution.py:287
  (104 shorter events, 2.4 us)
Async XLA Ops:
  0.6 19.4 %collective-permute-start = (bf16[32,1024]{1,0:T(8,128)(2,1)}, bf16[32,1024]{1,0:T(8,128)(2,1)S(1)}, u32[]{:S(2)}, u32[]{:S(2)}) collective-permute-start(bf16[32,1024]{1,0:T(8,128)(2,1)} %param.9), channel_id=1, source_target_pairs={{0,12},{4,0},{8,4},{12,8},{1,13},{5,1},{9,5},{13,9},{2,14},{6,2},{... | collective-permute-start | bytes 196616 | tf_op jit(solution)/shard_map/ppermute | solution.py:16
  5.7 14.4 %collective-permute-start.2 = (bf16[32,1024]{1,0:T(8,128)(2,1)}, bf16[32,1024]{1,0:T(8,128)(2,1)S(1)}, u32[]{:S(2)}, u32[]{:S(2)}) collective-permute-start(bf16[32,1024]{1,0:T(8,128)(2,1)} %param.9), channel_id=1, source_target_pairs={{0,4},{4,8},{8,12},{12,0},{1,5},{5,9},{9,13},{13,1},{2,6},{6,10},{... | collective-permute-start | bytes 196616 | tf_op jit(solution)/shard_map/ppermute | solution.py:16
  5.7 14.4 %collective-permute-start.1 = (bf16[32,1024]{1,0:T(8,128)(2,1)}, bf16[32,1024]{1,0:T(8,128)(2,1)S(1)}, u32[]{:S(2)}, u32[]{:S(2)}) collective-permute-start(bf16[32,1024]{1,0:T(8,128)(2,1)} %param.9), channel_id=1, source_target_pairs={{0,8},{4,12},{8,0},{12,4},{1,9},{5,13},{9,1},{13,5},{2,10},{6,14},... | collective-permute-start | bytes 196616 | tf_op jit(solution)/shard_map/ppermute | solution.py:16
  8.4 3.1 %copy-start.8 = (bf16[1024,3584]{1,0:T(8,128)(2,1)S(1)}, bf16[1024,3584]{1,0:T(8,128)(2,1)}, u32[]{:S(2)}) copy-start(bf16[1024,3584]{1,0:T(8,128)(2,1)} %gate.3) | copy-start | bytes 22020100
  11.5 3.1 %copy-start.9 = (bf16[1024,3584]{1,0:T(8,128)(2,1)S(1)}, bf16[1024,3584]{1,0:T(8,128)(2,1)}, u32[]{:S(2)}) copy-start(bf16[1024,3584]{1,0:T(8,128)(2,1)} %up.3) | copy-start | bytes 22020100
  14.6 5.4 %copy-start.14 = (bf16[32,1024]{1,0:T(8,128)(2,1)S(1)}, bf16[32,1024]{1,0:T(8,128)(2,1)}, u32[]{:S(2)}) copy-start(bf16[32,1024]{1,0:T(8,128)(2,1)} %param.9) | copy-start | bytes 196612
  19.3 0.7 copy-start.10
  20.0 3.7 %copy-start.2 = (bf16[1024,3584]{1,0:T(8,128)(2,1)}, bf16[1024,3584]{1,0:T(8,128)(2,1)S(1)}, u32[]{:S(2)}) copy-start(bf16[1024,3584]{1,0:T(8,128)(2,1)S(1)} %get-tuple-element.25.gate) | copy-start | bytes 22020100
  20.0 5.9 %copy-start.4 = (bf16[1024,3584]{1,0:T(8,128)(2,1)}, bf16[1024,3584]{1,0:T(8,128)(2,1)S(1)}, u32[]{:S(2)}) copy-start(bf16[1024,3584]{1,0:T(8,128)(2,1)S(1)} %get-tuple-element.26.up) | copy-start | bytes 22020100
  20.1 19.4 %slice-start = ((s8[7340032]{0:T(1024)(128)(4,1)}), s8[3145728]{0:T(1024)(128)(4,1)S(1)}, s32[]{:S(2)}) async-start(s8[7340032]{0:T(1024)(128)(4,1)} %bitcast.57), calls=%async_computation | async-start | bytes 6291456
  25.9 0.8 copy-start.12
  26.7 9.3 %collective-permute-start.16 = (bf16[2,64,1792]{2,1,0:T(8,128)(2,1)}, bf16[2,64,1792]{2,1,0:T(8,128)(2,1)}, u32[]{:S(2)}, u32[]{:S(2)}) collective-permute-start(bf16[2,64,1792]{2,1,0:T(8,128)(2,1)} %get-tuple-element.35), channel_id=1, source_target_pairs={{0,1},{1,0},{2,3},{3,2},{4,5},{5,4},{6,7},{7,6},{8,9},{9,8},{10,11... | collective-permute-start | bytes 1376264 | tf_op jit(solution)/shard_map/ppermute | solution.py:16
  27.6 3.1 %copy-start.3 = (bf16[1024,3584]{1,0:T(8,128)(2,1)S(1)}, bf16[1024,3584]{1,0:T(8,128)(2,1)}, u32[]{:S(2)}) copy-start(bf16[1024,3584]{1,0:T(8,128)(2,1)} %copy-done.2) | copy-start | bytes 22020100
  30.7 3.1 %copy-start.5 = (bf16[1024,3584]{1,0:T(8,128)(2,1)S(1)}, bf16[1024,3584]{1,0:T(8,128)(2,1)}, u32[]{:S(2)}) copy-start(bf16[1024,3584]{1,0:T(8,128)(2,1)} %copy-done.4) | copy-start | bytes 22020100
  33.8 2.3 %copy-start.13 = (bf16[2,64,1792]{2,1,0:T(8,128)(2,1)S(1)}, bf16[2,64,1792]{2,1,0:T(8,128)(2,1)}, u32[]{:S(2)}) copy-start(bf16[2,64,1792]{2,1,0:T(8,128)(2,1)} %copy-done.12) | copy-start | bytes 1376260
  33.8 5.7 %slice-start.1 = ((s8[7340032]{0:T(1024)(128)(4,1)}), s8[4194304]{0:T(1024)(128)(4,1)S(1)}, s32[]{:S(2)}) async-start(s8[7340032]{0:T(1024)(128)(4,1)} %bitcast.57), calls=%async_computation.1 | async-start | bytes 8388608
  33.8 34.3 %slice-start.4 = ((s8[7340032]{0:T(1024)(128)(4,1)}), s8[3145728]{0:T(1024)(128)(4,1)S(1)}, s32[]{:S(2)}) async-start(s8[7340032]{0:T(1024)(128)(4,1)} %bitcast.61), calls=%async_computation.4 | async-start | bytes 6291456
  35.4 3.3 %collective-permute-start.3 = (bf16[2,64,1792]{2,1,0:T(8,128)(2,1)S(1)}, bf16[2,64,1792]{2,1,0:T(8,128)(2,1)S(1)}, u32[]{:S(2)}, u32[]{:S(2)}) collective-permute-start(bf16[2,64,1792]{2,1,0:T(8,128)(2,1)S(1)} %get-tuple-element.28), channel_id=1, source_target_pairs={{0,1},{1,0},{2,3},{3,2},{4,5},{5,4},{6,7},{7,6},{8,9},{9,8},{10,11... | collective-permute-start | bytes 1376264 | tf_op jit(solution)/shard_map/ppermute | solution.py:16
  37.2 12.3 %collective-permute-start.17 = (bf16[2,32,1792]{2,1,0:T(8,128)(2,1)S(1)}, bf16[2,32,1792]{2,1,0:T(8,128)(2,1)S(1)}, u32[]{:S(2)}, u32[]{:S(2)}) collective-permute-start(bf16[2,32,1792]{2,1,0:T(8,128)(2,1)S(1)} %slice.85), channel_id=1, source_target_pairs={{0,2},{2,0},{1,3},{3,1},{4,6},{6,4},{5,7},{7,5},{8,10},{10,8},{9,1... | collective-permute-start | bytes 688136 | tf_op jit(solution)/shard_map/ppermute | solution.py:16
  38.9 12.3 %collective-permute-start.13 = (bf16[2,32,1792]{2,1,0:T(8,128)(2,1)S(1)}, bf16[2,32,1792]{2,1,0:T(8,128)(2,1)S(1)}, u32[]{:S(2)}, u32[]{:S(2)}) collective-permute-start(bf16[2,32,1792]{2,1,0:T(8,128)(2,1)S(1)} %slice.81), channel_id=1, source_target_pairs={{0,2},{2,0},{1,3},{3,1},{4,6},{6,4},{5,7},{7,5},{8,10},{10,8},{9,1... | collective-permute-start | bytes 688136 | tf_op jit(solution)/shard_map/ppermute | solution.py:16
  39.5 3.1 %copy-start.6 = (bf16[1024,3584]{1,0:T(8,128)(2,1)S(1)}, bf16[1024,3584]{1,0:T(8,128)(2,1)}, u32[]{:S(2)}) copy-start(bf16[1024,3584]{1,0:T(8,128)(2,1)} %up.5) | copy-start | bytes 22020100
  42.6 25.5 %slice-start.5 = ((s8[7340032]{0:T(1024)(128)(4,1)}), s8[4194304]{0:T(1024)(128)(4,1)S(1)}, s32[]{:S(2)}) async-start(s8[7340032]{0:T(1024)(128)(4,1)} %bitcast.61), calls=%async_computation.5 | async-start | bytes 8388608
  44.2 7.7 %collective-permute-start.7 = (bf16[2,2,32,896]{3,2,0,1:T(8,128)(2,1)S(1)}, bf16[2,2,32,896]{3,2,0,1:T(8,128)(2,1)S(1)}, u32[]{:S(2)}, u32[]{:S(2)}) collective-permute-start(bf16[2,2,32,896]{3,2,0,1:T(8,128)(2,1)S(1)} %copy.25), channel_id=1, source_target_pairs={{0,1},{1,0},{2,3},{3,2},{4,5},{5,4},{6,7},{7,6},{8,9},{9,8},{10,11... | collective-permute-start | bytes 688136 | tf_op jit(solution)/shard_map/ppermute | solution.py:16
  44.3 3.1 %copy-start.7 = (bf16[1024,3584]{1,0:T(8,128)(2,1)S(1)}, bf16[1024,3584]{1,0:T(8,128)(2,1)}, u32[]{:S(2)}) copy-start(bf16[1024,3584]{1,0:T(8,128)(2,1)} %up.5) | copy-start | bytes 22020100
  48.9 4.6 %collective-permute-start.4 = (bf16[2,2,32,896]{3,2,1,0:T(8,128)(2,1)S(1)}, bf16[2,2,32,896]{3,2,1,0:T(8,128)(2,1)S(1)}, u32[]{:S(2)}, u32[]{:S(2)}) collective-permute-start(bf16[2,2,32,896]{3,2,1,0:T(8,128)(2,1)S(1)} %get-tuple-element.30), channel_id=1, source_target_pairs={{0,1},{1,0},{2,3},{3,2},{4,5},{5,4},{6,7},{7,6},{8,9},{9,8},{10,11... | collective-permute-start | bytes 688136 | tf_op jit(solution)/shard_map/ppermute | solution.py:16
  49.6 6.1 %collective-permute-start.18 = (bf16[32,1792]{1,0:T(8,128)(2,1)S(1)}, bf16[32,1792]{1,0:T(8,128)(2,1)S(1)}, u32[]{:S(2)}, u32[]{:S(2)}) collective-permute-start(bf16[32,1792]{1,0:T(8,128)(2,1)S(1)} %fusion.3), channel_id=1, source_target_pairs={{0,2},{2,0},{1,3},{3,1},{4,6},{6,4},{5,7},{7,5},{8,10},{10,8},{9,1... | collective-permute-start | bytes 344072 | tf_op jit(solution)/shard_map/ppermute | solution.py:16
  51.3 6.8 %collective-permute-start.14 = (bf16[32,1792]{1,0:T(8,128)(2,1)S(1)}, bf16[32,1792]{1,0:T(8,128)(2,1)S(1)}, u32[]{:S(2)}, u32[]{:S(2)}) collective-permute-start(bf16[32,1792]{1,0:T(8,128)(2,1)S(1)} %fusion.5), channel_id=1, source_target_pairs={{0,2},{2,0},{1,3},{3,1},{4,6},{6,4},{5,7},{7,5},{8,10},{10,8},{9,1... | collective-permute-start | bytes 344072 | tf_op jit(solution)/shard_map/ppermute | solution.py:16
  52.0 11.1 %collective-permute-start.8 = (bf16[2,2,32,896]{3,2,0,1:T(8,128)(2,1)S(1)}, bf16[2,2,32,896]{3,2,0,1:T(8,128)(2,1)S(1)}, u32[]{:S(2)}, u32[]{:S(2)}) collective-permute-start(bf16[2,2,32,896]{3,2,0,1:T(8,128)(2,1)S(1)} %add_convert_fusion.2), channel_id=1, source_target_pairs={{0,2},{2,0},{1,3},{3,1},{4,6},{6,4},{5,7},{7,5},{8,10},{10,8},{9,1... | collective-permute-start | bytes 688136 | tf_op jit(solution)/shard_map/ppermute | solution.py:16
  53.6 13.4 %collective-permute-start.5 = (bf16[2,2,32,896]{3,2,1,0:T(8,128)(2,1)S(1)}, bf16[2,2,32,896]{3,2,1,0:T(8,128)(2,1)S(1)}, u32[]{:S(2)}, u32[]{:S(2)}) collective-permute-start(bf16[2,2,32,896]{3,2,1,0:T(8,128)(2,1)S(1)} %add_convert_fusion.3), channel_id=1, source_target_pairs={{0,2},{2,0},{1,3},{3,1},{4,6},{6,4},{5,7},{7,5},{8,10},{10,8},{9,1... | collective-permute-start | bytes 688136 | tf_op jit(solution)/shard_map/ppermute | solution.py:16
  55.7 11.6 %collective-permute-start.19 = (bf16[64,1792]{1,0:T(8,128)(2,1)S(1)}, bf16[64,1792]{1,0:T(8,128)(2,1)S(1)}, u32[]{:S(2)}, u32[]{:S(2)}) collective-permute-start(bf16[64,1792]{1,0:T(8,128)(2,1)S(1)} %pad_maximum_fusion.1), channel_id=1, source_target_pairs={{0,1},{1,0},{2,3},{3,2},{4,5},{5,4},{6,7},{7,6},{8,9},{9,8},{10,11... | collective-permute-start | bytes 688136 | tf_op jit(solution)/shard_map/ppermute | solution.py:16
  58.2 9.1 %collective-permute-start.15 = (bf16[64,1792]{1,0:T(8,128)(2,1)S(1)}, bf16[64,1792]{1,0:T(8,128)(2,1)S(1)}, u32[]{:S(2)}, u32[]{:S(2)}) collective-permute-start(bf16[64,1792]{1,0:T(8,128)(2,1)S(1)} %pad_maximum_fusion), channel_id=1, source_target_pairs={{0,1},{1,0},{2,3},{3,2},{4,5},{5,4},{6,7},{7,6},{8,9},{9,8},{10,11... | collective-permute-start | bytes 688136 | tf_op jit(solution)/shard_map/ppermute | solution.py:16
  63.2 11.0 %collective-permute-start.9 = (bf16[2,32,896]{2,1,0:T(8,128)(2,1)S(1)}, bf16[2,32,896]{2,1,0:T(8,128)(2,1)S(1)}, u32[]{:S(2)}, u32[]{:S(2)}) collective-permute-start(bf16[2,32,896]{2,1,0:T(8,128)(2,1)S(1)} %fusion.8), channel_id=1, source_target_pairs={{0,1},{1,0},{2,3},{3,2},{4,5},{5,4},{6,7},{7,6},{8,9},{9,8},{10,11... | collective-permute-start | bytes 344072 | tf_op jit(solution)/shard_map/ppermute | solution.py:16
  67.2 7.1 %collective-permute-start.6 = (bf16[2,32,896]{2,1,0:T(8,128)(2,1)S(1)}, bf16[2,32,896]{2,1,0:T(8,128)(2,1)S(1)}, u32[]{:S(2)}, u32[]{:S(2)}) collective-permute-start(bf16[2,32,896]{2,1,0:T(8,128)(2,1)S(1)} %fusion.11), channel_id=1, source_target_pairs={{0,1},{1,0},{2,3},{3,2},{4,5},{5,4},{6,7},{7,6},{8,9},{9,8},{10,11... | collective-permute-start | bytes 344072 | tf_op jit(solution)/shard_map/ppermute | solution.py:16
  67.7 7.0 %slice-start.2 = ((s8[7340032]{0:T(1024)(128)(4,1)}), s8[4194304]{0:T(1024)(128)(4,1)S(1)}, s32[]{:S(2)}) async-start(s8[7340032]{0:T(1024)(128)(4,1)} %bitcast.59), calls=%async_computation.2 | async-start | bytes 8388608
  68.1 6.6 %slice-start.3 = ((s8[7340032]{0:T(1024)(128)(4,1)}), s8[3145728]{0:T(1024)(128)(4,1)S(1)}, s32[]{:S(2)}) async-start(s8[7340032]{0:T(1024)(128)(4,1)} %bitcast.59), calls=%async_computation.3 | async-start | bytes 6291456
  69.3 10.5 %collective-permute-start.20 = (bf16[32,1024]{1,0:T(8,128)(2,1)S(1)}, bf16[32,1024]{1,0:T(8,128)(2,1)S(1)}, u32[]{:S(2)}, u32[]{:S(2)}) collective-permute-start(bf16[32,1024]{1,0:T(8,128)(2,1)S(1)} %get-tuple-element.48), channel_id=1, source_target_pairs={{0,4},{4,8},{8,12},{12,0},{1,5},{5,9},{9,13},{13,1},{2,6},{6,10},{... | collective-permute-start | bytes 196616 | tf_op jit(solution)/shard_map/ppermute | solution.py:16
  72.7 7.1 %collective-permute-start.22 = (bf16[32,1024]{1,0:T(8,128)(2,1)S(1)}, bf16[32,1024]{1,0:T(8,128)(2,1)S(1)}, u32[]{:S(2)}, u32[]{:S(2)}) collective-permute-start(bf16[32,1024]{1,0:T(8,128)(2,1)S(1)} %get-tuple-element.49), channel_id=1, source_target_pairs={{0,12},{4,0},{8,4},{12,8},{1,13},{5,1},{9,5},{13,9},{2,14},{6,2},{... | collective-permute-start | bytes 196616 | tf_op jit(solution)/shard_map/ppermute | solution.py:16
  73.2 6.8 %collective-permute-start.21 = (bf16[32,1024]{1,0:T(8,128)(2,1)S(1)}, bf16[32,1024]{1,0:T(8,128)(2,1)S(1)}, u32[]{:S(2)}, u32[]{:S(2)}) collective-permute-start(bf16[32,1024]{1,0:T(8,128)(2,1)S(1)} %get-tuple-element.50), channel_id=1, source_target_pairs={{0,8},{4,12},{8,0},{12,4},{1,9},{5,13},{9,1},{13,5},{2,10},{6,14},... | collective-permute-start | bytes 196616 | tf_op jit(solution)/shard_map/ppermute | solution.py:16
  75.9 6.9 %collective-permute-start.10 = (bf16[32,1024]{1,0:T(8,128)(2,1)S(1)}, bf16[32,1024]{1,0:T(8,128)(2,1)S(1)}, u32[]{:S(2)}, u32[]{:S(2)}) collective-permute-start(bf16[32,1024]{1,0:T(8,128)(2,1)S(1)} %get-tuple-element.51), channel_id=1, source_target_pairs={{0,4},{4,8},{8,12},{12,0},{1,5},{5,9},{9,13},{13,1},{2,6},{6,10},{... | collective-permute-start | bytes 196616 | tf_op jit(solution)/shard_map/ppermute | solution.py:16
  76.5 6.3 %collective-permute-start.12 = (bf16[32,1024]{1,0:T(8,128)(2,1)S(1)}, bf16[32,1024]{1,0:T(8,128)(2,1)S(1)}, u32[]{:S(2)}, u32[]{:S(2)}) collective-permute-start(bf16[32,1024]{1,0:T(8,128)(2,1)S(1)} %get-tuple-element.52), channel_id=1, source_target_pairs={{0,12},{4,0},{8,4},{12,8},{1,13},{5,1},{9,5},{13,9},{2,14},{6,2},{... | collective-permute-start | bytes 196616 | tf_op jit(solution)/shard_map/ppermute | solution.py:16
  79.8 5.8 %collective-permute-start.11 = (bf16[32,1024]{1,0:T(8,128)(2,1)S(1)}, bf16[32,1024]{1,0:T(8,128)(2,1)S(1)}, u32[]{:S(2)}, u32[]{:S(2)}) collective-permute-start(bf16[32,1024]{1,0:T(8,128)(2,1)S(1)} %get-tuple-element.53), channel_id=1, source_target_pairs={{0,8},{4,12},{8,0},{12,4},{1,9},{5,13},{9,1},{13,5},{2,10},{6,14},... | collective-permute-start | bytes 196616 | tf_op jit(solution)/shard_map/ppermute | solution.py:16
  85.7 4.7 %collective-permute-start.23 = (bf16[32,1024]{1,0:T(8,128)(2,1)S(1)}, bf16[32,1024]{1,0:T(8,128)(2,1)S(1)}, u32[]{:S(2)}, u32[]{:S(2)}) collective-permute-start(bf16[32,1024]{1,0:T(8,128)(2,1)S(1)} %get-tuple-element.47), channel_id=1, source_target_pairs={{0,12},{4,0},{8,4},{12,8},{1,13},{5,1},{9,5},{13,9},{2,14},{6,2},{... | collective-permute-start | bytes 196616 | tf_op jit(solution)/shard_map/ppermute | solution.py:16
  87.9 6.6 %collective-permute-start.24 = (bf16[32,1024]{1,0:T(8,128)(2,1)S(1)}, bf16[32,1024]{1,0:T(8,128)(2,1)S(1)}, u32[]{:S(2)}, u32[]{:S(2)}) collective-permute-start(bf16[32,1024]{1,0:T(8,128)(2,1)S(1)} %get-tuple-element.47), channel_id=1, source_target_pairs={{0,8},{4,12},{8,0},{12,4},{1,9},{5,13},{9,1},{13,5},{2,10},{6,14},... | collective-permute-start | bytes 196616 | tf_op jit(solution)/shard_map/ppermute | solution.py:16
  87.9 6.6 %collective-permute-start.25 = (bf16[32,1024]{1,0:T(8,128)(2,1)S(1)}, bf16[32,1024]{1,0:T(8,128)(2,1)S(1)}, u32[]{:S(2)}, u32[]{:S(2)}) collective-permute-start(bf16[32,1024]{1,0:T(8,128)(2,1)S(1)} %get-tuple-element.47), channel_id=1, source_target_pairs={{0,4},{4,8},{8,12},{12,0},{1,5},{5,9},{9,13},{13,1},{2,6},{6,10},{... | collective-permute-start | bytes 196616 | tf_op jit(solution)/shard_map/ppermute | solution.py:16
  100.1 10.3 %copy-start.11 = (f32[4,64,1]{2,1,0:T(8,128)S(1)}, f32[4,64,1]{2,1,0:T(8,128)}, u32[]{:S(2)}) copy-start(f32[4,64,1]{2,1,0:T(8,128)} %copy-done.10) | copy-start | bytes 3076
  100.4 1.4 %collective-permute-start.26 = (bf16[2,32,896]{2,1,0:T(8,128)(2,1)S(1)}, bf16[2,32,896]{2,1,0:T(8,128)(2,1)S(1)}, u32[]{:S(2)}, u32[]{:S(2)}) collective-permute-start(bf16[2,32,896]{2,1,0:T(8,128)(2,1)S(1)} %get-tuple-element.37), channel_id=1, source_target_pairs={{0,1},{1,0},{2,3},{3,2},{4,5},{5,4},{6,7},{7,6},{8,9},{9,8},{10,11... | collective-permute-start | bytes 344072 | tf_op jit(solution)/shard_map/ppermute | solution.py:16
  100.7 2.7 %collective-permute-start.28 = (bf16[2,32,896]{2,1,0:T(8,128)(2,1)S(1)}, bf16[2,32,896]{2,1,0:T(8,128)(2,1)S(1)}, u32[]{:S(2)}, u32[]{:S(2)}) collective-permute-start(bf16[2,32,896]{2,1,0:T(8,128)(2,1)S(1)} %get-tuple-element.39), channel_id=1, source_target_pairs={{0,1},{1,0},{2,3},{3,2},{4,5},{5,4},{6,7},{7,6},{8,9},{9,8},{10,11... | collective-permute-start | bytes 344072 | tf_op jit(solution)/shard_map/ppermute | solution.py:16
  101.8 8.7 %collective-permute-start.27 = (bf16[2,32,896]{2,1,0:T(8,128)(2,1)S(1)}, bf16[2,32,896]{2,1,0:T(8,128)(2,1)S(1)}, u32[]{:S(2)}, u32[]{:S(2)}) collective-permute-start(bf16[2,32,896]{2,1,0:T(8,128)(2,1)S(1)} %add_convert_fusion.5.mine), channel_id=1, source_target_pairs={{0,2},{2,0},{1,3},{3,1},{4,6},{6,4},{5,7},{7,5},{8,10},{10,8},{9,1... | collective-permute-start | bytes 344072 | tf_op jit(solution)/shard_map/ppermute | solution.py:16
  103.4 10.4 %collective-permute-start.30 = (bf16[2,32,896]{2,1,0:T(8,128)(2,1)S(1)}, bf16[2,32,896]{2,1,0:T(8,128)(2,1)S(1)}, u32[]{:S(2)}, u32[]{:S(2)}) collective-permute-start(bf16[2,32,896]{2,1,0:T(8,128)(2,1)S(1)} %add_convert_fusion.4.before.mine), channel_id=1, source_target_pairs={{0,2},{2,0},{1,3},{3,1},{4,6},{6,4},{5,7},{7,5},{8,10},{10,8},{9,1... | collective-permute-start | bytes 344072 | tf_op jit(solution)/shard_map/ppermute | solution.py:16
  110.5 3.1 %copy-start = (bf16[3584,1024]{1,0:T(8,128)(2,1)S(1)}, bf16[3584,1024]{1,0:T(8,128)(2,1)}, u32[]{:S(2)}) copy-start(bf16[3584,1024]{1,0:T(8,128)(2,1)} %shard_map.128.before) | copy-start | bytes 22020100
  113.5 3.1 %copy-start.1 = (bf16[3584,1024]{1,0:T(8,128)(2,1)S(1)}, bf16[3584,1024]{1,0:T(8,128)(2,1)}, u32[]{:S(2)}) copy-start(bf16[3584,1024]{1,0:T(8,128)(2,1)} %shard_map.128.before) | copy-start | bytes 22020100
  113.7 9.1 %collective-permute-start.29 = (bf16[2,2,32,896]{3,2,1,0:T(8,128)(2,1)S(1)}, bf16[2,2,32,896]{3,2,1,0:T(8,128)(2,1)S(1)}, u32[]{:S(2)}, u32[]{:S(2)}) collective-permute-start(bf16[2,2,32,896]{3,2,1,0:T(8,128)(2,1)S(1)} %shard_map.129.mine), channel_id=1, source_target_pairs={{0,1},{1,0},{2,3},{3,2},{4,5},{5,4},{6,7},{7,6},{8,9},{9,8},{10,11... | collective-permute-start | bytes 688136 | tf_op jit(solution)/shard_map/ppermute | solution.py:16
  116.8 1.6 %collective-permute-start.31 = (bf16[2,2,32,896]{3,2,1,0:T(8,128)(2,1)S(1)}, bf16[2,2,32,896]{3,2,1,0:T(8,128)(2,1)S(1)}, u32[]{:S(2)}, u32[]{:S(2)}) collective-permute-start(bf16[2,2,32,896]{3,2,1,0:T(8,128)(2,1)S(1)} %shard_map.130.mine), channel_id=1, source_target_pairs={{0,1},{1,0},{2,3},{3,2},{4,5},{5,4},{6,7},{7,6},{8,9},{9,8},{10,11... | collective-permute-start | bytes 688136 | tf_op jit(solution)/shard_map/ppermute | solution.py:16

commit v3 on v2

--- a/solution.py
+++ b/solution.py
@@ -38,13 +38,10 @@
     return pl.BlockSpec(memory_space=pltpu.SMEM)
 
 
-def prepare_kernel(
-    ranks, capacity, dps, pipes, place, routes, shares, gate, up, picker, weights, gate_out, up_out, sems
-):
-    pieces = 8
-    rows = gate.shape[0] // pieces
+def load_start(pairs, sems, pieces):
     copies = []
-    for which, (source, target) in enumerate(((gate, gate_out), (up, up_out))):
+    for which, (source, target) in enumerate(pairs):
+        rows = source.shape[0] // pieces
         for i in range(pieces):
             part = pl.ds(i * rows, rows)
             copies.append(
@@ -52,23 +49,32 @@
             )
     for copy in copies:
         copy.start()
+    return copies
+
+
+def far(value):
+    return pltpu.with_memory_space_constraint(value, pltpu.HBM)
+
+
+def prepare_kernel(
+    ranks, capacity, dps, pipes, place, routes, shares, gate, up, picker, weights, gate_out, up_out, sems
+):
+    copies = load_start(((gate, gate_out), (up, up_out)), sems, 8)
     rank, dp, pipe = place[0], place[1], place[2]
     experts, slots, token_count = picker.shape
     block = token_count // ranks
     per_piece = ranks // (dps * pipes)
-    lane = lax.broadcasted_iota(jnp.int32, (token_count, 128), 1)
-    names = lane + rank * experts
-    weight = jnp.zeros((token_count, 128), F32)
-    routed = jnp.zeros((token_count, 128), F32)
-    for k in range(routes.shape[1]):
-        hit = (routes[:, k : k + 1] == names) & (lane < experts)
-        weight = weight + jnp.where(hit, shares[:, k : k + 1], 0.0)
+    row = lax.broadcasted_iota(jnp.int32, (8, token_count), 0)
+    names = row + rank * experts
+    weight = jnp.zeros((8, token_count), F32)
+    routed = jnp.zeros((8, token_count), F32)
+    for k in range(routes.shape[0]):
+        hit = (routes[k : k + 1, :] == names) & (row < experts)
+        weight = weight + jnp.where(hit, shares[k : k + 1, :], 0.0)
         routed = routed + jnp.where(hit, 1.0, 0.0)
-    weight = weight.T
     t_from = lax.broadcasted_iota(jnp.int32, (token_count, token_count), 0)
     t_to = lax.broadcasted_iota(jnp.int32, (token_count, token_count), 1)
     earlier = jnp.where((t_from // block == t_to // block) & (t_from < t_to), 1.0, 0.0)
-    routed = routed.T
     within = dot(routed.astype(BF), earlier.astype(BF)).astype(jnp.int32)
     at_block = lax.broadcasted_iota(jnp.int32, (1, token_count), 1) // block
     at_pipe = lax.rem(at_block // (dps * per_piece) + pipes - pipe, pipes)
@@ -85,6 +91,7 @@
 
 
 def prepare(place, routes, shares, gate, up, ranks, dps, pipes, block, experts):
+    assert experts <= 8
     capacity = block // 2
     token_count = block * ranks
     slots = capacity * ranks
@@ -103,7 +110,40 @@
         cost_estimate=pl.CostEstimate(
             flops=0, bytes_accessed=4 * gate.size, transcendentals=0
         ),
-    )(place, routes, shares, gate, up)
+    )(place, routes, shares, far(gate), far(up))
+
+
+def load_kernel(source, before, out, sems):
+    for copy in load_start(((source, out),), sems, 8):
+        copy.wait()
+
+
+def load(source, before):
+    return pl.pallas_call(
+        load_kernel,
+        in_specs=[in_hbm(), anywhere()],
+        out_specs=whole(),
+        out_shape=pltpu.VMEM(source.shape, source.dtype),
+        scratch_shapes=[pltpu.SemaphoreType.DMA((1, 8))],
+        compiler_params=pltpu.CompilerParams(vmem_limit_bytes=4 * 1024 * 1024),
+        cost_estimate=pl.CostEstimate(
+            flops=0, bytes_accessed=2 * source.size, transcendentals=0
+        ),
+    )(far(source), before)
+
+
+def add_kernel(a, b, before, out):
+    out[...] = (a[...].astype(F32) + b[...].astype(F32)).astype(BF)
+
+
+def add_after(a, b, before):
+    return pl.pallas_call(
+        add_kernel,
+        in_specs=[whole(), whole(), anywhere()],
+        out_specs=whole(),
+        out_shape=jax.ShapeDtypeStruct(a.shape, BF),
+        compiler_params=pltpu.CompilerParams(vmem_limit_bytes=4 * 1024 * 1024),
+    )(a, b, before)
 
 
 def tile_of(size):
@@ -143,13 +183,27 @@
     )(place, tokens, gate, up)
 
 
-def expert_kernel(first, picker, tokens, gate, up, before, keep, send):
+def expert_kernel(first, picker, tokens, gate, up, before, keep, send, held, sems):
     half = keep.shape[2]
-    for i in range(keep.shape[0]):
-        e = first + i
-        rows = dot(picker[e], tokens[...]).astype(BF)
+    count = keep.shape[0]
+    pieces = sems.shape[2]
+    rows_each = gate.shape[0] // pieces
+    copies = {}
+    for i in range(count):
         for which, weight in enumerate((gate, up)):
-            product = dot(rows, weight[:, e * H : (e + 1) * H]).astype(BF)
+            for p in range(pieces):
+                part = pl.ds(p * rows_each, rows_each)
+                columns = pl.ds((first + i) * H, H)
+                copies[i, which, p] = pltpu.make_async_copy(
+                    weight.at[part, columns], held.at[i, which, part], sems.at[i, which, p]
+                )
+                copies[i, which, p].start()
+    for i in range(count):
+        rows = dot(picker[first + i], tokens[...]).astype(BF)
+        for which in range(2):
+            for p in range(pieces):
+                copies[i, which, p].wait()
+            product = dot(rows, held[i, which]).astype(BF)
             keep[i, which] = product[:half]
             send[i, which] = product[half:]
 
@@ -160,16 +214,78 @@
     halves = jax.ShapeDtypeStruct((count, 2, slots // 2, H), BF)
     return pl.pallas_call(
         functools.partial(expert_kernel, first),
-        in_specs=[whole(), whole(), whole(), whole(), anywhere()],
+        in_specs=[whole(), whole(), in_hbm(), in_hbm(), anywhere()],
         out_specs=(whole(), whole()),
         out_shape=(halves, halves),
-        compiler_params=pltpu.CompilerParams(vmem_limit_bytes=8 * 1024 * 1024),
+        scratch_shapes=[
+            pltpu.VMEM((count, 2, width, H), BF),
+            pltpu.SemaphoreType.DMA((count, 2, 4)),
+        ],
+        compiler_params=pltpu.CompilerParams(vmem_limit_bytes=16 * 1024 * 1024),
         cost_estimate=pl.CostEstimate(
             flops=count * 4 * slots * width * H,
             bytes_accessed=count * 4 * width * H,
             transcendentals=0,
         ),
-    )(picker, tokens, gate, up, before)
+    )(picker, tokens, far(gate), far(up), before)
+
+
+def hidden_act_kernel(first, swap, mine, other, weight, pre, out):
+    count, _, rows = mine.shape[:3]
+    for i in range(count):
+        totals = []
+        for which in range(2):
+            total = mine[i, which].astype(F32)
+            if swap:
+                theirs = other[i, which].astype(F32)
+                total = total + jnp.concatenate([theirs[rows // 2 :], theirs[: rows // 2]], axis=0)
+            pre[i, which] = total
+            totals.append(total)
+        gate, up = totals
+        out[i] = (gate * jax.nn.sigmoid(gate) * up * weight[first + i, :rows]).astype(BF)
+
+
+def hidden_act(mine, other, swap, weight, first):
+    count, _, rows, width = mine.shape
+    return pl.pallas_call(
+        functools.partial(hidden_act_kernel, first, swap),
+        in_specs=[whole(), whole(), whole()],
+        out_specs=(whole(), whole()),
+        out_shape=(
+            jax.ShapeDtypeStruct(mine.shape, F32),
+            jax.ShapeDtypeStruct((count, rows, width), BF),
+        ),
+        compiler_params=pltpu.CompilerParams(vmem_limit_bytes=8 * 1024 * 1024),
+    )(mine, other, weight)
+
+
+def join_kernel(dps, pipes, place, *refs):
+    out = refs[-1]
+    dp, pipe = place[1], place[2]
+    rows = out.shape[0] // (dps * pipes)
+    at = 0
+    for i in range((len(refs) - 1) // 2):
+        size = refs[2 * i].shape[1]
+        for j1 in range(pipes):
+            for j0 in range(dps):
+                piece = lax.rem(pipe + j1, pipes) * dps + lax.rem(dp + j0, dps)
+                target = pl.ds(pl.multiple_of(piece * rows, rows), rows)
+                out[target, at : at + size] = refs[2 * i + j1][j0 * rows : (j0 + 1) * rows, :]
+        at += size
+
+
+def join(place, parts, dps, pipes):
+    assert pipes == 2
+    flat = [value for pair in parts for value in pair]
+    rows = flat[0].shape[0] * pipes
+    width = sum(pair[0].shape[1] for pair in parts)
+    return pl.pallas_call(
+        functools.partial(join_kernel, dps, pipes),
+        in_specs=[scalars()] + [whole()] * len(flat),
+        out_specs=whole(),
+        out_shape=jax.ShapeDtypeStruct((rows, width), BF),
+        compiler_params=pltpu.CompilerParams(vmem_limit_bytes=8 * 1024 * 1024),
+    )(place, *flat)
 
 
 def spread_kernel(picker, hidden, out):
@@ -188,25 +304,44 @@
     )(picker, hidden)
 
 
-def pick_kernel(first, picker, dense, keep, send):
+def flip_kernel(dense, tokens, before, dense_out, tokens_out):
+    dense_out[...] = dense[...].astype(F32).T.astype(BF)
+    tokens_out[...] = tokens[...].astype(F32).T.astype(BF)
+
+
+def flip(dense, tokens, before):
+    return pl.pallas_call(
+        flip_kernel,
+        in_specs=[whole(), whole(), anywhere()],
+        out_specs=(whole(), whole()),
+        out_shape=(
+            jax.ShapeDtypeStruct(dense.shape[::-1], BF),
+            jax.ShapeDtypeStruct(tokens.shape[::-1], BF),
+        ),
+        compiler_params=pltpu.CompilerParams(vmem_limit_bytes=16 * 1024 * 1024),
+    )(dense, tokens, before)
+
+
+def hidden_grad_kernel(first, picker, residual, down, keep, send):
     half = keep.shape[1]
     for i in range(keep.shape[0]):
         e = first + i
-        rows = dot(picker[e], dense[:, e * H : (e + 1) * H]).astype(BF)
-        keep[i] = rows[:half]
-        send[i] = rows[half:]
-
-
-def pick(picker, dense, first, count):
+        rows = dot(picker[e], residual[...]).astype(BF)
+        product = dot(down[e * H : (e + 1) * H, :], rows, 1, 1).T.astype(BF)
+        keep[i] = product[:half]
+        send[i] = product[half:]
+
+
+def hidden_grad_parts(picker, residual, down, first, count):
     slots = picker.shape[1]
     halves = jax.ShapeDtypeStruct((count, slots // 2, H), BF)
     return pl.pallas_call(
-        functools.partial(pick_kernel, first),
-        in_specs=[whole(), whole()],
+        functools.partial(hidden_grad_kernel, first),
+        in_specs=[whole(), whole(), whole()],
         out_specs=(whole(), whole()),
         out_shape=(halves, halves),
         compiler_params=pltpu.CompilerParams(vmem_limit_bytes=8 * 1024 * 1024),
-    )(picker, dense)
+    )(picker, residual, down)
 
 
 def hidden_grad_act_kernel(first, swap, mine, other, pre, weight, before, out):
@@ -236,47 +371,50 @@
     )(mine, other, pre, weight, before)
 
 
-def down_grad_kernel(picker, residual, hidden, before, out):
-    rows = dot(picker[0], residual[...]).astype(BF)
-    out[...] = dot(hidden[0], rows, 0, 0).astype(BF)
-
-
-def down_grad(picker, residual, hidden, before):
-    count, slots, token_count = picker.shape
+def down_grad_kernel(hidden, residual, before, out, done):
+    out[...] = dot(hidden[...], residual[...]).astype(BF)
+    done[...] = jnp.zeros_like(done)
+
+
+def down_grad(hidden, residual, before):
+    rows, token_count = hidden.shape
     width = residual.shape[1]
-    split = 2 if width % 256 == 0 else 1
-    part = width // split
     return pl.pallas_call(
         down_grad_kernel,
-        grid=(count, split),
+        grid=(rows // H,),
         in_specs=[
-            pl.BlockSpec((1, slots, token_count), lambda i, j: (i, 0, 0)),
-            pl.BlockSpec((token_count, part), lambda i, j: (0, j)),
-            pl.BlockSpec((1, slots, H), lambda i, j: (i, 0, 0)),
+            pl.BlockSpec((H, token_count), lambda i: (i, 0)),
+            pl.BlockSpec((token_count, width), lambda i: (0, 0)),
             anywhere(),
         ],
-        out_specs=pl.BlockSpec((H, part), lambda i, j: (i, j)),
-        out_shape=jax.ShapeDtypeStruct((count * H, width), BF),
+        out_specs=(
+            pl.BlockSpec((H, width), lambda i: (i, 0)),
+            pl.BlockSpec((8, 128), lambda i: (0, 0)),
+        ),
+        out_shape=(
+            jax.ShapeDtypeStruct((rows, width), BF),
+            jax.ShapeDtypeStruct((8, 128), F32),
+        ),
         compiler_params=pltpu.CompilerParams(vmem_limit_bytes=16 * 1024 * 1024),
         cost_estimate=pl.CostEstimate(
-            flops=count * 2 * slots * width * H,
-            bytes_accessed=count * 2 * width * H,
+            flops=2 * rows * width * token_count,
+            bytes_accessed=2 * rows * width,
             transcendentals=0,
         ),
-    )(picker, residual, hidden, before)
+    )(hidden, residual, before)
 
 
 def input_grad_kernel(picker, tokens, mine, theirs, *rest):
     out_gate, out_up = rest[-2:]
-    rows = dot(picker[0], tokens[...]).astype(BF)
     for which, out in enumerate((out_gate, out_up)):
         grad = jnp.concatenate([mine[0, which], theirs[0, which]], axis=0)
-        out[...] = dot(rows, grad, 0, 0).astype(BF)
+        dense = dot(picker[0], grad, 0, 0).astype(BF)
+        out[...] = dot(tokens[...], dense).astype(BF)
 
 
 def input_grads(picker, tokens, mine, theirs, first, so_far):
     experts, slots, token_count = picker.shape
-    width = tokens.shape[1]
+    width = tokens.shape[0]
     count = mine.shape[0]
     split = 2 if width % 256 == 0 else 1
     part = width // split
@@ -289,7 +427,7 @@
         grid=(count, split),
         in_specs=[
             pl.BlockSpec((1, slots, token_count), lambda i, j: (first + i, 0, 0)),
-            pl.BlockSpec((token_count, part), lambda i, j: (0, j)),
+            pl.BlockSpec((part, token_count), lambda i, j: (j, 0)),
             grad_spec,
             grad_spec,
         ]
@@ -299,11 +437,11 @@
         input_output_aliases={4 + i: i for i in range(len(extra))},
         compiler_params=pltpu.CompilerParams(vmem_limit_bytes=16 * 1024 * 1024),
         cost_estimate=pl.CostEstimate(
-            flops=count * 4 * slots * width * H,
+            flops=count * 4 * token_count * width * H,
             bytes_accessed=count * 4 * width * H,
             transcendentals=0,
         ),
-    )(picker, tokens, mine, theirs, *extra)
+    )(picker, tokens, mine, theirs, *[far(value) for value in extra])
 
 
 def add(a, b):
@@ -329,11 +467,11 @@
     )
 
 
-def reduce_dp(value, count):
+def exchange_dp(value, count):
     if count == 2:
-        first, second = split_rows(shift(value, "dp", count, 1), 2)
-        return value.astype(F32) + jnp.concatenate([second, first], axis=-2).astype(F32)
-    return gather_dp(scatter_dp(value, count).astype(BF), count).astype(F32)
+        return value, shift(value, "dp", count, 1)
+    total = gather_dp(scatter_dp(value, count).astype(BF), count)
+    return total, total
 
 
 def body(
@@ -379,7 +517,7 @@
 
     base = gather_tokens(tokens)
     picker, slot_weight, gate_near, up_near = prepare(
-        place, routes, gate_weights, teacher_gate, teacher_up, ranks, dps, pipes, block, experts
+        place, routes.T, gate_weights.T, teacher_gate, teacher_up, ranks, dps, pipes, block, experts
     )
 
     chunks = 2 if teacher_gate.shape[1] % 512 == 0 else 1
@@ -391,58 +529,48 @@
 
     group = 2 if experts % 2 == 0 else 1
     firsts = range(0, experts, group)
-    expert_halves = []
+    parts = []
+    last = halves[-1]
     for first in firsts:
-        keep, send = expert_pre(picker, base, expert_gate, expert_up, halves[0], first, group)
-        expert_halves.append(add(keep, shift(send, "pipe", pipes, 1)))
+        keep, send = expert_pre(picker, base, expert_gate, expert_up, last, first, group)
+        last = keep
+        parts.append((keep, shift(send, "pipe", pipes, 1)))
+    teacher_down = load(teacher_down, last)
+    expert_down = load(expert_down, teacher_down)
 
     hiddens = []
     for half in halves:
         total = scatter_dp(half, dps)
         hidden = gather_dp((jax.nn.silu(total[0]) * total[1]).astype(BF), dps)
-        hiddens.append(jnp.concatenate([hidden, shift(hidden, "pipe", pipes, 1)], axis=0))
-    hidden = jnp.concatenate(hiddens, axis=1)
-    hidden = hidden.reshape(pipes, dps, token_count // (pipes * dps), hidden.shape[1])
-    hidden = jnp.concatenate([hidden, hidden], axis=1)
-    hidden = lax.dynamic_slice_in_dim(hidden, (dps - dp) % dps, dps, axis=1)
-    hidden = jnp.concatenate([hidden, hidden], axis=0)
-    hidden = lax.dynamic_slice_in_dim(hidden, (pipes - pipe) % pipes, pipes, axis=0)
-    hidden = hidden.reshape(token_count, -1)
+        hiddens.append((hidden, shift(hidden, "pipe", pipes, 1)))
+    hidden = join(place, hiddens, dps, pipes)
     target = to_owners(jnp.dot(hidden, teacher_down, preferred_element_type=F32).astype(BF))
 
     pre, weighted = [], []
-    for first, half in zip(firsts, expert_halves):
-        total = reduce_dp(half, dps)
-        mine = slot_weight[first : first + group, : slots // 2]
-        part = (jax.nn.silu(total[:, 0]) * total[:, 1] * mine).astype(BF)
+    for first, (keep, theirs) in zip(firsts, parts):
+        mine, other = exchange_dp(add(keep, theirs), dps)
+        total, part = hidden_act(mine, other, dps == 2, slot_weight, first)
         pre.append(total)
         weighted.append(jnp.concatenate([part, shift(part, "pipe", pipes, 1)], axis=1))
     weighted = jnp.concatenate(weighted, axis=0)
 
     dense = spread(picker, weighted)
-    student_sum = to_owners(jnp.dot(dense, expert_down, preferred_element_type=F32).astype(BF))
+    product = jnp.dot(dense, expert_down, preferred_element_type=F32).astype(BF)
+    student_sum = to_owners(product)
+    dense_flipped, base_flipped = flip(dense, base, product)
     residual = gather_tokens((student_sum - target).astype(BF))
 
-    dense_grad = lax.dot_general(
-        residual, expert_down, (((1,), (1,)), ((), ())), preferred_element_type=F32
-    ).astype(BF)
     sums = []
     for first in firsts:
-        keep, send = pick(picker, dense_grad, first, group)
+        keep, send = hidden_grad_parts(picker, residual, expert_down, first, group)
         sums.append(add(keep, shift(send, "pipe", pipes, 1)))
-    others = []
-    if dps == 2:
-        others = [shift(value, "dp", dps, 1) for value in sums]
-    else:
-        sums = [gather_dp(scatter_dp(value, dps).astype(BF), dps) for value in sums]
-        others = sums
-    grad_down = down_grad(picker, residual, weighted, sums[0])
+    pairs = [exchange_dp(value, dps) for value in sums]
+    grad_down, done = down_grad(dense_flipped, residual, sums[-1])
     grads = None
     for i, first in enumerate(firsts):
-        mine = hidden_grad_act(
-            sums[i], others[i], dps == 2, pre[i], slot_weight, grad_down, first
-        )
-        grads = input_grads(picker, base, mine, shift(mine, "pipe", pipes, 1), first, grads)
+        mine = hidden_grad_act(*pairs[i], dps == 2, pre[i], slot_weight, done, first)
+        theirs = shift(mine, "pipe", pipes, 1)
+        grads = input_grads(picker, base_flipped, mine, theirs, first, grads)
     return (student_sum.astype(BF), grads[0], grads[1], grad_down)
 
 

time: 128 us -> 101 us (0.79)
  local copies, waits for them, and re-layouts: 32 us -> 4.65 us
  Pallas kernels: 28.5 us -> 42.4 us
  waiting for transfers between devices: 25.4 us -> 18.4 us
  matrix products: 7.84 us -> 2.24 us
  other arithmetic: 3.65 us -> 1.53 us
  starting transfers between devices: 28.7 us -> 30.2 us
    unnamed x44 -> x10, local copies, waits for them, and re-layouts: 30.8 us -> 4.45 us
    pallas_call x3 -> x9, Pallas kernels: 6.85 us -> 14.6 us  [the longest x2 6.34 us: load(): pl.pallas_call(load_kernel, in_specs=[in_hbm(), anywhere()], out_specs=wh...]
    ppermute x32, waiting for transfers between devices: 25.4 us -> 18.4 us  [shift(): lax.ppermute(value, axis, [(i, (i + by) % count) for i in range(count)])]
    dot_general x2 -> x1, matrix products: 6.72 us -> 1.12 us  [body(): product = jnp.dot(dense, expert_down, preferred_element_type=F32).astype(BF)]
    pallas_call x2, Pallas kernels: 3.11 us -> 7.44 us  [expert_pre(): pl.pallas_call(functools.partial(expert_kernel, first), in_specs=[whole()...]
    pallas_call x2, Pallas kernels: 8.97 us -> 10.4 us  [input_grads(): pl.pallas_call(input_grad_kernel, grid=(count, split), in_specs=[pl.Block...]
    ppermute x32, starting transfers between devices: 28.7 us -> 30.2 us  [shift(): lax.ppermute(value, axis, [(i, (i + by) % count) for i in range(count)])]
  transfers between devices with their start and end apart: 32 -> 32, of which waited for: 11 -> 12; matrix products, arithmetic and copies ran while one was open for 7% -> 4% of each run, Pallas kernels for 17% -> 34%
where the time goes in v3:
time: 101 us
  Pallas kernels  42.4 us (42%)
  starting transfers between devices  30.2 us (30%)
  waiting for transfers between devices  18.4 us (18%)
  local copies, waits for them, and re-layouts  4.65 us (5%)
  matrix products  2.24 us (2%)
  other arithmetic  1.53 us (2%)
  between operations  1.08 us (1%)
    ppermute x32, starting transfers between devices, shift(): lax.ppermute(value, axis, [(i, (i + by) % count) for i in range(count)])  30.2 us
    ppermute x32, waiting for transfers between devices, shift(): lax.ppermute(value, axis, [(i, (i + by) % count) for i in range(count)])  18.4 us
    pallas_call x2, Pallas kernels, input_grads(): pl.pallas_call(input_grad_kernel, grid=(count, split), in_specs=[pl.Block...  10.4 us
    pallas_call x2, Pallas kernels, expert_pre(): pl.pallas_call(functools.partial(expert_kernel, first), in_specs=[whole()...  7.44 us
    pallas_call x2, Pallas kernels, load(): pl.pallas_call(load_kernel, in_specs=[in_hbm(), anywhere()], out_specs=wh...  6.34 us
    pallas_call x1, Pallas kernels, prepare(): pl.pallas_call(functools.partial(prepare_kernel, ranks, capacity, dps, pi...  5.9 us
    unnamed x10, local copies, waits for them, and re-layouts  4.45 us
    pallas_call x1, Pallas kernels, down_grad(): pl.pallas_call(down_grad_kernel, grid=(rows // H,), in_specs=[pl.BlockSpe...  4.37 us
  transfers between devices with their start and end apart: 32, of which 12 were waited for; matrix products, arithmetic and copies ran while one was open for 4% of the time, Pallas kernels for 34%

profile of v3, /device:TPU:0, one launch (start us, length us, event | category | flops | bytes accessed | tf_op | source)
XLA Modules:
  0.0 100.5 jit_solution(11400719445636853360)
XLA Ops:
  0.6 5.1 %collective-permute-start = (bf16[32,1024]{1,0:T(8,128)(2,1)}, bf16[32,1024]{1,0:T(8,128)(2,1)S(1)}, u32[]{:S(2)}, u32[]{:S(2)}) collective-permute-start(bf16[32,1024]{1,0:T(8,128)(2,1)} %param.9), channel_id=1, source_target_pairs={{0,12},{4,0},{8,4},{12,8},{1,13},{5,1},{9,5},{13,9},{2,14},{6,2},{... | collective-permute-start | bytes 196616 | tf_op jit(solution)/shard_map/ppermute | solution.py:16
  5.7 1.0 %collective-permute-start.1 = (bf16[32,1024]{1,0:T(8,128)(2,1)}, bf16[32,1024]{1,0:T(8,128)(2,1)S(1)}, u32[]{:S(2)}, u32[]{:S(2)}) collective-permute-start(bf16[32,1024]{1,0:T(8,128)(2,1)} %param.9), channel_id=1, source_target_pairs={{0,8},{4,12},{8,0},{12,4},{1,9},{5,13},{9,1},{13,5},{2,10},{6,14},... | collective-permute-start | bytes 196616 | tf_op jit(solution)/shard_map/ppermute | solution.py:16
  6.7 0.1 pad_add_fusion.place
  6.8 0.7 copy-done.2
  7.5 0.7 copy-done.3
  8.2 5.9 %shard_map.120 = (bf16[4,64,128]{2,1,0:T(8,128)(2,1)S(1)}, f32[4,64,1]{2,1,0:T(8,128)S(1)}, bf16[1024,3584]{1,0:T(8,128)(2,1)S(1)}, bf16[1024,3584]{1,0:T(8,128)(2,1)S(1)}) custom-call(s32[3]{0:T(128)S(1)} %pad_add_fusion.place, s32[4,128]{1,0:T(4,128)S(1)} %bitcast.29, f32[4,128]{1,0:T(4,128)S(1)} %bitcast.30, bf16[1024,3584]{1,0:T(8,128)(2,1)} %gate.3, ...), custom_call_target="tpu_custom_call" | custom-call | bytes 14680064 | tf_op jit(solution)/shard_map/pallas_call | solution.py:98
  14.3 1.7 %shard_map.130 = (bf16[2,64,1792]{2,1,0:T(8,128)(2,1)S(1)}, bf16[2,64,1792]{2,1,0:T(8,128)(2,1)S(1)}) custom-call(s32[3]{0:T(128)S(1)} %pad_add_fusion.place, bf16[128,1024]{1,0:T(8,128)(2,1)S(1)} %constant_dynamic-update-slice_fusion.4.tokens, bf16[1024,3584]{1,0:T(8,128)(2,1)S(1)} %get-tuple-element.33.gate, bf16[1024,3584]{1,0:T(8,128)(2,1)S(1)} %get-tuple-element.34.up), custom_call_target="tpu_custom_call" | custom-call | flops 939524096 | bytes 7340032 | tf_op jit(solution)/shard_map/pallas_call | solution.py:174
  16.0 1.7 %shard_map.121 = (bf16[2,64,1792]{2,1,0:T(8,128)(2,1)S(1)}, bf16[2,64,1792]{2,1,0:T(8,128)(2,1)S(1)}) custom-call(s32[3]{0:T(128)S(1)} %pad_add_fusion.place, bf16[128,1024]{1,0:T(8,128)(2,1)S(1)} %constant_dynamic-update-slice_fusion.4.tokens, bf16[1024,3584]{1,0:T(8,128)(2,1)S(1)} %get-tuple-element.33.gate, bf16[1024,3584]{1,0:T(8,128)(2,1)S(1)} %get-tuple-element.34.up), custom_call_target="tpu_custom_call" | custom-call | flops 939524096 | bytes 7340032 | tf_op jit(solution)/shard_map/pallas_call | solution.py:174
  17.7 0.6 collective-permute-start.3
  18.3 0.1 add_convert_fusion
  18.4 1.5 %collective-permute-start.14 = (bf16[2,32,1792]{2,1,0:T(8,128)(2,1)S(1)}, bf16[2,32,1792]{2,1,0:T(8,128)(2,1)S(1)}, u32[]{:S(2)}, u32[]{:S(2)}) collective-permute-start(bf16[2,32,1792]{2,1,0:T(8,128)(2,1)S(1)} %slice.33), channel_id=1, source_target_pairs={{0,2},{2,0},{1,3},{3,1},{4,6},{6,4},{5,7},{7,5},{8,10},{10,8},{9,1... | collective-permute-start | bytes 688136 | tf_op jit(solution)/shard_map/ppermute | solution.py:16
  19.9 0.1 add_convert_fusion.1.before
  20.1 1.3 %collective-permute-start.17 = (bf16[2,32,1792]{2,1,0:T(8,128)(2,1)S(1)}, bf16[2,32,1792]{2,1,0:T(8,128)(2,1)S(1)}, u32[]{:S(2)}, u32[]{:S(2)}) collective-permute-start(bf16[2,32,1792]{2,1,0:T(8,128)(2,1)S(1)} %slice.37), channel_id=1, source_target_pairs={{0,2},{2,0},{1,3},{3,1},{4,6},{6,4},{5,7},{7,5},{8,10},{10,8},{9,1... | collective-permute-start | bytes 688136 | tf_op jit(solution)/shard_map/ppermute | solution.py:16
  21.4 3.7 %shard_map.122 = (bf16[2,2,32,896]{3,2,1,0:T(8,128)(2,1)S(1)}, bf16[2,2,32,896]{3,2,1,0:T(8,128)(2,1)S(1)}) custom-call(bf16[4,64,128]{2,1,0:T(8,128)(2,1)S(1)} %get-tuple-element.32.picker, bf16[128,1024]{1,0:T(8,128)(2,1)S(1)} %constant_dynamic-update-slice_fusion.4.tokens, bf16[1024,3584]{1,0:T(8,128)(2,1)} %gate.5, bf16[1024,3584]{1,0:T(8,128)(2,1)} %up.5, ...), custom_call_target="tpu_custom_call" | custom-call | flops 469762048 | bytes 7340032 | tf_op jit(solution)/shard_map/pallas_call | solution.py:215
  25.1 0.1 collective-permute-start.4
  25.3 3.7 %shard_map.124 = (bf16[2,2,32,896]{3,2,1,0:T(8,128)(2,1)S(1)}, bf16[2,2,32,896]{3,2,1,0:T(8,128)(2,1)S(1)}) custom-call(bf16[4,64,128]{2,1,0:T(8,128)(2,1)S(1)} %get-tuple-element.32.picker, bf16[128,1024]{1,0:T(8,128)(2,1)S(1)} %constant_dynamic-update-slice_fusion.4.tokens, bf16[1024,3584]{1,0:T(8,128)(2,1)} %gate.5, bf16[1024,3584]{1,0:T(8,128)(2,1)} %up.5, ...), custom_call_target="tpu_custom_call" | custom-call | flops 469762048 | bytes 7340032 | tf_op jit(solution)/shard_map/pallas_call | solution.py:215
  29.0 0.5 collective-permute-start.7
  29.6 0.8 collective-permute-start.15
  30.5 0.4 collective-permute-done.17
  31.0 1.5 %collective-permute-start.18 = (bf16[32,1792]{1,0:T(8,128)(2,1)S(1)}, bf16[32,1792]{1,0:T(8,128)(2,1)S(1)}, u32[]{:S(2)}, u32[]{:S(2)}) collective-permute-start(bf16[32,1792]{1,0:T(8,128)(2,1)S(1)} %fusion.1), channel_id=1, source_target_pairs={{0,2},{2,0},{1,3},{3,1},{4,6},{6,4},{5,7},{7,5},{8,10},{10,8},{9,1... | collective-permute-start | bytes 344072 | tf_op jit(solution)/shard_map/ppermute | solution.py:16
  32.7 0.6 collective-permute-start.8
  33.3 1.5 %collective-permute-start.5 = (bf16[2,2,32,896]{3,2,1,0:T(8,128)(2,1)S(1)}, bf16[2,2,32,896]{3,2,1,0:T(8,128)(2,1)S(1)}, u32[]{:S(2)}, u32[]{:S(2)}) collective-permute-start(bf16[2,2,32,896]{3,2,1,0:T(8,128)(2,1)S(1)} %add_convert_fusion.3.mine), channel_id=1, source_target_pairs={{0,2},{2,0},{1,3},{3,1},{4,6},{6,4},{5,7},{7,5},{8,10},{10,8},{9,1... | collective-permute-start | bytes 688136 | tf_op jit(solution)/shard_map/ppermute | solution.py:16
  34.9 0.8 collective-permute-done.15
  35.8 2.4 %collective-permute-done.18 = bf16[32,1792]{1,0:T(8,128)(2,1)S(1)} collective-permute-done((bf16[32,1792]{1,0:T(8,128)(2,1)S(1)}, bf16[32,1792]{1,0:T(8,128)(2,1)S(1)}, u32[]{:S(2)}, u32[]{:S(2)}) %collective-permute-start.18) | collective-permute-done | bytes 114720 | tf_op jit(solution)/shard_map/ppermute | solution.py:16
  38.3 3.2 %shard_map.127.before = bf16[3584,1024]{1,0:T(8,128)(2,1)S(1)} custom-call(bf16[3584,1024]{1,0:T(8,128)(2,1)} %source.2, bf16[2,2,32,896]{3,2,1,0:T(8,128)(2,1)S(1)} %get-tuple-element.41.before), custom_call_target="tpu_custom_call" | custom-call | bytes 7340032 | tf_op jit(solution)/shard_map/pallas_call | solution.py:122
  41.4 3.2 %shard_map.128.down = bf16[3584,1024]{1,0:T(8,128)(2,1)S(1)} custom-call(bf16[3584,1024]{1,0:T(8,128)(2,1)} %source.3, bf16[3584,1024]{1,0:T(8,128)(2,1)S(1)} %shard_map.127.before), custom_call_target="tpu_custom_call" | custom-call | bytes 7340032 | tf_op jit(solution)/shard_map/pallas_call | solution.py:122
  44.6 0.1 shard_map.125
  44.7 0.6 collective-permute-start.9
  45.3 1.8 %collective-permute-done.5.other = bf16[2,2,32,896]{3,2,1,0:T(8,128)(2,1)S(1)} collective-permute-done((bf16[2,2,32,896]{3,2,1,0:T(8,128)(2,1)S(1)}, bf16[2,2,32,896]{3,2,1,0:T(8,128)(2,1)S(1)}, u32[]{:S(2)}, u32[]{:S(2)}) %collective-permute-start.5) | collective-permute-done | bytes 229408 | tf_op jit(solution)/shard_map/ppermute | solution.py:16
  47.1 0.1 shard_map.123
  47.3 0.6 shard_map.131
  47.9 1.1 %convolution_convert_fusion = bf16[128,1024]{1,0:T(8,128)(2,1)S(1)} fusion(bf16[128,3584]{1,0:T(8,128)(2,1)S(1)} %shard_map.131, bf16[3584,1024]{1,0:T(8,128)(2,1)S(1)} %shard_map.127.before), kind=kOutput, calls=%fused_computation | convolution fusion | flops 939655168 | bytes 8519680 | tf_op jit(solution)/shard_map/dot_general | solution.py:547
  49.1 3.4 %collective-permute-start.20 = (bf16[32,1024]{1,0:T(8,128)(2,1)S(1)}, bf16[32,1024]{1,0:T(8,128)(2,1)S(1)}, u32[]{:S(2)}, u32[]{:S(2)}) collective-permute-start(bf16[32,1024]{1,0:T(8,128)(2,1)S(1)} %get-tuple-element.62), channel_id=1, source_target_pairs={{0,4},{4,8},{8,12},{12,0},{1,5},{5,9},{9,13},{13,1},{2,6},{6,10},{... | collective-permute-start | bytes 196616 | tf_op jit(solution)/shard_map/ppermute | solution.py:16
  52.5 0.4 collective-permute-start.22
  53.0 1.1 %collective-permute-start.21 = (bf16[32,1024]{1,0:T(8,128)(2,1)S(1)}, bf16[32,1024]{1,0:T(8,128)(2,1)S(1)}, u32[]{:S(2)}, u32[]{:S(2)}) collective-permute-start(bf16[32,1024]{1,0:T(8,128)(2,1)S(1)} %get-tuple-element.64), channel_id=1, source_target_pairs={{0,8},{4,12},{8,0},{12,4},{1,9},{5,13},{9,1},{13,5},{2,10},{6,14},... | collective-permute-start | bytes 196616 | tf_op jit(solution)/shard_map/ppermute | solution.py:16
  54.1 0.4 shard_map.126.dense
  54.5 1.1 %convolution_convert_fusion.1.before = bf16[128,1024]{1,0:T(8,128)(2,1)S(1)} fusion(bf16[128,3584]{1,0:T(8,128)(2,1)S(1)} %shard_map.126.dense, bf16[3584,1024]{1,0:T(8,128)(2,1)S(1)} %shard_map.128.down), kind=kOutput, calls=%fused_computation.1 | convolution fusion | flops 939655168 | bytes 8519680 | tf_op jit(solution)/shard_map/dot_general | solution.py:558
  55.7 0.6 collective-permute-start.10
  56.3 3.3 %collective-permute-start.12 = (bf16[32,1024]{1,0:T(8,128)(2,1)S(1)}, bf16[32,1024]{1,0:T(8,128)(2,1)S(1)}, u32[]{:S(2)}, u32[]{:S(2)}) collective-permute-start(bf16[32,1024]{1,0:T(8,128)(2,1)S(1)} %get-tuple-element.66), channel_id=1, source_target_pairs={{0,12},{4,0},{8,4},{12,8},{1,13},{5,1},{9,5},{13,9},{2,14},{6,2},{... | collective-permute-start | bytes 196616 | tf_op jit(solution)/shard_map/ppermute | solution.py:16
  59.6 0.1 collective-permute-done.21
  59.8 2.8 %collective-permute-done.10 = bf16[32,1024]{1,0:T(8,128)(2,1)S(1)} collective-permute-done((bf16[32,1024]{1,0:T(8,128)(2,1)S(1)}, bf16[32,1024]{1,0:T(8,128)(2,1)S(1)}, u32[]{:S(2)}, u32[]{:S(2)}) %collective-permute-start.10) | collective-permute-done | bytes 65568 | tf_op jit(solution)/shard_map/ppermute | solution.py:16
  62.6 2.8 %collective-permute-done.11 = bf16[32,1024]{1,0:T(8,128)(2,1)S(1)} collective-permute-done((bf16[32,1024]{1,0:T(8,128)(2,1)S(1)}, bf16[32,1024]{1,0:T(8,128)(2,1)S(1)}, u32[]{:S(2)}, u32[]{:S(2)}) %collective-permute-start.11) | collective-permute-done | bytes 65568 | tf_op jit(solution)/shard_map/ppermute | solution.py:16
  65.4 0.1 constant_dynamic-update-slice_fusion.3
  65.5 2.2 %collective-permute-start.23 = (bf16[32,1024]{1,0:T(8,128)(2,1)S(1)}, bf16[32,1024]{1,0:T(8,128)(2,1)S(1)}, u32[]{:S(2)}, u32[]{:S(2)}) collective-permute-start(bf16[32,1024]{1,0:T(8,128)(2,1)S(1)} %get-tuple-element.61), channel_id=1, source_target_pairs={{0,12},{4,0},{8,4},{12,8},{1,13},{5,1},{9,5},{13,9},{2,14},{6,2},{... | collective-permute-start | bytes 196616 | tf_op jit(solution)/shard_map/ppermute | solution.py:16
  67.7 0.6 collective-permute-start.25
  68.4 1.9 %collective-permute-done.23 = bf16[32,1024]{1,0:T(8,128)(2,1)S(1)} collective-permute-done((bf16[32,1024]{1,0:T(8,128)(2,1)S(1)}, bf16[32,1024]{1,0:T(8,128)(2,1)S(1)}, u32[]{:S(2)}, u32[]{:S(2)}) %collective-permute-start.23) | collective-permute-done | bytes 65568 | tf_op jit(solution)/shard_map/ppermute | solution.py:16
  70.2 4.0 %collective-permute-done.24 = bf16[32,1024]{1,0:T(8,128)(2,1)S(1)} collective-permute-done((bf16[32,1024]{1,0:T(8,128)(2,1)S(1)}, bf16[32,1024]{1,0:T(8,128)(2,1)S(1)}, u32[]{:S(2)}, u32[]{:S(2)}) %collective-permute-start.24) | collective-permute-done | bytes 65568 | tf_op jit(solution)/shard_map/ppermute | solution.py:16
  74.3 3.1 %copy-done.1 = bf16[3584,1024]{1,0:T(8,128)(2,1)S(1)} copy-done((bf16[3584,1024]{1,0:T(8,128)(2,1)S(1)}, bf16[3584,1024]{1,0:T(8,128)(2,1)}, u32[]{:S(2)}) %copy-start.1) | copy-done | bytes 7340056
  77.4 1.4 %shard_map.132 = (bf16[2,32,896]{2,1,0:T(8,128)(2,1)S(1)}, bf16[2,32,896]{2,1,0:T(8,128)(2,1)S(1)}) custom-call(bf16[4,64,128]{2,1,0:T(8,128)(2,1)S(1)} %get-tuple-element.32.picker, bf16[128,1024]{1,0:T(8,128)(2,1)S(1)} %constant_dynamic-update-slice_fusion.residual, bf16[3584,1024]{1,0:T(8,128)(2,1)S(1)} %copy-done.1), custom_call_target="tpu_custom_call" | custom-call | tf_op jit(solution)/shard_map/pallas_call | solution.py:338
  78.8 1.3 %shard_map.135 = (bf16[2,32,896]{2,1,0:T(8,128)(2,1)S(1)}, bf16[2,32,896]{2,1,0:T(8,128)(2,1)S(1)}) custom-call(bf16[4,64,128]{2,1,0:T(8,128)(2,1)S(1)} %get-tuple-element.32.picker, bf16[128,1024]{1,0:T(8,128)(2,1)S(1)} %constant_dynamic-update-slice_fusion.residual, bf16[3584,1024]{1,0:T(8,128)(2,1)S(1)} %copy-done.1), custom_call_target="tpu_custom_call" | custom-call | tf_op jit(solution)/shard_map/pallas_call | solution.py:338
  80.2 0.6 collective-permute-start.29
  80.8 0.8 collective-permute-start.27
  81.6 0.1 collective-permute-done.29
  81.7 1.2 %collective-permute-start.30 = (bf16[2,32,896]{2,1,0:T(8,128)(2,1)S(1)}, bf16[2,32,896]{2,1,0:T(8,128)(2,1)S(1)}, u32[]{:S(2)}, u32[]{:S(2)}) collective-permute-start(bf16[2,32,896]{2,1,0:T(8,128)(2,1)S(1)} %add_convert_fusion.4.mine), channel_id=1, source_target_pairs={{0,2},{2,0},{1,3},{3,1},{4,6},{6,4},{5,7},{7,5},{8,10},{10,8},{9,1... | collective-permute-start | bytes 344072 | tf_op jit(solution)/shard_map/ppermute | solution.py:16
  83.0 0.4 shard_map.129
  83.4 4.4 %shard_map.133 = (bf16[3584,1024]{1,0:T(8,128)(2,1)}, f32[8,128]{1,0:T(8,128)S(1)}) custom-call(bf16[3584,128]{1,0:T(8,128)(2,1)S(1)} %get-tuple-element.50.hidden, bf16[128,1024]{1,0:T(8,128)(2,1)S(1)} %constant_dynamic-update-slice_fusion.residual, bf16[2,32,896]{2,1,0:T(8,128)(2,1)S(1)} %add_convert_fusion.5.before.mine), custom_call_target="tpu_custom_call" | custom-call | flops 939524096 | bytes 7340032 | tf_op jit(solution)/shard_map/pallas_call | solution.py:382
  87.7 0.1 shard_map.134.mine
  88.0 0.4 collective-permute-done.30.other
  88.4 0.1 shard_map.136.mine
  88.5 0.1 collective-permute-start.31
  88.7 0.7 fusion.4
  89.3 0.8 collective-permute-done.31.theirs
  90.1 5.2 %shard_map.137 = (bf16[1024,3584]{1,0:T(8,128)(2,1)}, bf16[1024,3584]{1,0:T(8,128)(2,1)}) custom-call(bf16[4,64,128]{2,1,0:T(8,128)(2,1)S(1)} %get-tuple-element.32.picker, bf16[1024,128]{1,0:T(8,128)(2,1)S(1)} %get-tuple-element.44.tokens, bf16[2,2,32,896]{3,2,1,0:T(8,128)(2,1)S(1)} %shard_map.136.mine, ...), custom_call_target="tpu_custom_call" | custom-call | flops 939524096 | bytes 7340032 | tf_op jit(solution)/shard_map/pallas_call | solution.py:425
  95.3 5.2 %shard_map.138 = (bf16[1024,3584]{1,0:T(8,128)(2,1)}, bf16[1024,3584]{1,0:T(8,128)(2,1)}) custom-call(bf16[4,64,128]{2,1,0:T(8,128)(2,1)S(1)} %get-tuple-element.32.picker, bf16[1024,128]{1,0:T(8,128)(2,1)S(1)} %get-tuple-element.44.tokens, bf16[2,2,32,896]{3,2,1,0:T(8,128)(2,1)S(1)} %shard_map.134.mine, ...), custom_call_target="tpu_custom_call", output_to_operand_aliasing={{0}: (4, {}), {1}: (5, {})} | custom-call | flops 939524096 | bytes 7340032 | tf_op jit(solution)/shard_map/pallas_call | solution.py:425
  (60 shorter events, 1.2 us)
Async XLA Ops:
  0.6 13.5 %collective-permute-start = (bf16[32,1024]{1,0:T(8,128)(2,1)}, bf16[32,1024]{1,0:T(8,128)(2,1)S(1)}, u32[]{:S(2)}, u32[]{:S(2)}) collective-permute-start(bf16[32,1024]{1,0:T(8,128)(2,1)} %param.9), channel_id=1, source_target_pairs={{0,12},{4,0},{8,4},{12,8},{1,13},{5,1},{9,5},{13,9},{2,14},{6,2},{... | collective-permute-start | bytes 196616 | tf_op jit(solution)/shard_map/ppermute | solution.py:16
  5.7 8.5 %collective-permute-start.2 = (bf16[32,1024]{1,0:T(8,128)(2,1)}, bf16[32,1024]{1,0:T(8,128)(2,1)S(1)}, u32[]{:S(2)}, u32[]{:S(2)}) collective-permute-start(bf16[32,1024]{1,0:T(8,128)(2,1)} %param.9), channel_id=1, source_target_pairs={{0,4},{4,8},{8,12},{12,0},{1,5},{5,9},{9,13},{13,1},{2,6},{6,10},{... | collective-permute-start | bytes 196616 | tf_op jit(solution)/shard_map/ppermute | solution.py:16
  5.7 8.5 %collective-permute-start.1 = (bf16[32,1024]{1,0:T(8,128)(2,1)}, bf16[32,1024]{1,0:T(8,128)(2,1)S(1)}, u32[]{:S(2)}, u32[]{:S(2)}) collective-permute-start(bf16[32,1024]{1,0:T(8,128)(2,1)} %param.9), channel_id=1, source_target_pairs={{0,8},{4,12},{8,0},{12,4},{1,9},{5,13},{9,1},{13,5},{2,10},{6,14},... | collective-permute-start | bytes 196616 | tf_op jit(solution)/shard_map/ppermute | solution.py:16
  6.8 0.7 copy-start.2
  7.5 0.7 copy-start.3
  8.2 5.9 %copy-start.4 = (bf16[32,1024]{1,0:T(8,128)(2,1)S(1)}, bf16[32,1024]{1,0:T(8,128)(2,1)}, u32[]{:S(2)}) copy-start(bf16[32,1024]{1,0:T(8,128)(2,1)} %param.9) | copy-start | bytes 196612
  15.9 2.3 %collective-permute-start.13 = (bf16[2,64,1792]{2,1,0:T(8,128)(2,1)S(1)}, bf16[2,64,1792]{2,1,0:T(8,128)(2,1)S(1)}, u32[]{:S(2)}, u32[]{:S(2)}) collective-permute-start(bf16[2,64,1792]{2,1,0:T(8,128)(2,1)S(1)} %get-tuple-element.46), channel_id=1, source_target_pairs={{0,1},{1,0},{2,3},{3,2},{4,5},{5,4},{6,7},{7,6},{8,9},{9,8},{10,11... | collective-permute-start | bytes 1376264 | tf_op jit(solution)/shard_map/ppermute | solution.py:16
  17.7 2.2 %collective-permute-start.3 = (bf16[2,64,1792]{2,1,0:T(8,128)(2,1)S(1)}, bf16[2,64,1792]{2,1,0:T(8,128)(2,1)S(1)}, u32[]{:S(2)}, u32[]{:S(2)}) collective-permute-start(bf16[2,64,1792]{2,1,0:T(8,128)(2,1)S(1)} %get-tuple-element.36), channel_id=1, source_target_pairs={{0,1},{1,0},{2,3},{3,2},{4,5},{5,4},{6,7},{7,6},{8,9},{9,8},{10,11... | collective-permute-start | bytes 1376264 | tf_op jit(solution)/shard_map/ppermute | solution.py:16
  18.4 11.1 %collective-permute-start.14 = (bf16[2,32,1792]{2,1,0:T(8,128)(2,1)S(1)}, bf16[2,32,1792]{2,1,0:T(8,128)(2,1)S(1)}, u32[]{:S(2)}, u32[]{:S(2)}) collective-permute-start(bf16[2,32,1792]{2,1,0:T(8,128)(2,1)S(1)} %slice.33), channel_id=1, source_target_pairs={{0,2},{2,0},{1,3},{3,1},{4,6},{6,4},{5,7},{7,5},{8,10},{10,8},{9,1... | collective-permute-start | bytes 688136 | tf_op jit(solution)/shard_map/ppermute | solution.py:16
  20.1 10.8 %collective-permute-start.17 = (bf16[2,32,1792]{2,1,0:T(8,128)(2,1)S(1)}, bf16[2,32,1792]{2,1,0:T(8,128)(2,1)S(1)}, u32[]{:S(2)}, u32[]{:S(2)}) collective-permute-start(bf16[2,32,1792]{2,1,0:T(8,128)(2,1)S(1)} %slice.37), channel_id=1, source_target_pairs={{0,2},{2,0},{1,3},{3,1},{4,6},{6,4},{5,7},{7,5},{8,10},{10,8},{9,1... | collective-permute-start | bytes 688136 | tf_op jit(solution)/shard_map/ppermute | solution.py:16
  25.1 8.1 %collective-permute-start.4 = (bf16[2,2,32,896]{3,2,1,0:T(8,128)(2,1)S(1)}, bf16[2,2,32,896]{3,2,1,0:T(8,128)(2,1)S(1)}, u32[]{:S(2)}, u32[]{:S(2)}) collective-permute-start(bf16[2,2,32,896]{3,2,1,0:T(8,128)(2,1)S(1)} %get-tuple-element.38), channel_id=1, source_target_pairs={{0,1},{1,0},{2,3},{3,2},{4,5},{5,4},{6,7},{7,6},{8,9},{9,8},{10,11... | collective-permute-start | bytes 688136 | tf_op jit(solution)/shard_map/ppermute | solution.py:16
  29.0 3.6 %collective-permute-start.7 = (bf16[2,2,32,896]{3,2,1,0:T(8,128)(2,1)S(1)}, bf16[2,2,32,896]{3,2,1,0:T(8,128)(2,1)S(1)}, u32[]{:S(2)}, u32[]{:S(2)}) collective-permute-start(bf16[2,2,32,896]{3,2,1,0:T(8,128)(2,1)S(1)} %get-tuple-element.42), channel_id=1, source_target_pairs={{0,1},{1,0},{2,3},{3,2},{4,5},{5,4},{6,7},{7,6},{8,9},{9,8},{10,11... | collective-permute-start | bytes 688136 | tf_op jit(solution)/shard_map/ppermute | solution.py:16
  29.6 6.1 %collective-permute-start.15 = (bf16[32,1792]{1,0:T(8,128)(2,1)S(1)}, bf16[32,1792]{1,0:T(8,128)(2,1)S(1)}, u32[]{:S(2)}, u32[]{:S(2)}) collective-permute-start(bf16[32,1792]{1,0:T(8,128)(2,1)S(1)} %fusion.3), channel_id=1, source_target_pairs={{0,2},{2,0},{1,3},{3,1},{4,6},{6,4},{5,7},{7,5},{8,10},{10,8},{9,1... | collective-permute-start | bytes 344072 | tf_op jit(solution)/shard_map/ppermute | solution.py:16
  31.0 7.1 %collective-permute-start.18 = (bf16[32,1792]{1,0:T(8,128)(2,1)S(1)}, bf16[32,1792]{1,0:T(8,128)(2,1)S(1)}, u32[]{:S(2)}, u32[]{:S(2)}) collective-permute-start(bf16[32,1792]{1,0:T(8,128)(2,1)S(1)} %fusion.1), channel_id=1, source_target_pairs={{0,2},{2,0},{1,3},{3,1},{4,6},{6,4},{5,7},{7,5},{8,10},{10,8},{9,1... | collective-permute-start | bytes 344072 | tf_op jit(solution)/shard_map/ppermute | solution.py:16
  32.7 12.0 %collective-permute-start.8 = (bf16[2,2,32,896]{3,2,1,0:T(8,128)(2,1)S(1)}, bf16[2,2,32,896]{3,2,1,0:T(8,128)(2,1)S(1)}, u32[]{:S(2)}, u32[]{:S(2)}) collective-permute-start(bf16[2,2,32,896]{3,2,1,0:T(8,128)(2,1)S(1)} %add_convert_fusion.2.mine), channel_id=1, source_target_pairs={{0,2},{2,0},{1,3},{3,1},{4,6},{6,4},{5,7},{7,5},{8,10},{10,8},{9,1... | collective-permute-start | bytes 688136 | tf_op jit(solution)/shard_map/ppermute | solution.py:16
  33.3 13.8 %collective-permute-start.5 = (bf16[2,2,32,896]{3,2,1,0:T(8,128)(2,1)S(1)}, bf16[2,2,32,896]{3,2,1,0:T(8,128)(2,1)S(1)}, u32[]{:S(2)}, u32[]{:S(2)}) collective-permute-start(bf16[2,2,32,896]{3,2,1,0:T(8,128)(2,1)S(1)} %add_convert_fusion.3.mine), channel_id=1, source_target_pairs={{0,2},{2,0},{1,3},{3,1},{4,6},{6,4},{5,7},{7,5},{8,10},{10,8},{9,1... | collective-permute-start | bytes 688136 | tf_op jit(solution)/shard_map/ppermute | solution.py:16
  35.7 11.6 %collective-permute-start.16 = (bf16[64,1792]{1,0:T(8,128)(2,1)S(1)}, bf16[64,1792]{1,0:T(8,128)(2,1)S(1)}, u32[]{:S(2)}, u32[]{:S(2)}) collective-permute-start(bf16[64,1792]{1,0:T(8,128)(2,1)S(1)} %pad_maximum_fusion.refs_0_), channel_id=1, source_target_pairs={{0,1},{1,0},{2,3},{3,2},{4,5},{5,4},{6,7},{7,6},{8,9},{9,8},{10,11... | collective-permute-start | bytes 688136 | tf_op jit(solution)/shard_map/ppermute | solution.py:16
  38.2 9.1 %collective-permute-start.19 = (bf16[64,1792]{1,0:T(8,128)(2,1)S(1)}, bf16[64,1792]{1,0:T(8,128)(2,1)S(1)}, u32[]{:S(2)}, u32[]{:S(2)}) collective-permute-start(bf16[64,1792]{1,0:T(8,128)(2,1)S(1)} %pad_maximum_fusion.1.refs_2_), channel_id=1, source_target_pairs={{0,1},{1,0},{2,3},{3,2},{4,5},{5,4},{6,7},{7,6},{8,9},{9,8},{10,11... | collective-permute-start | bytes 688136 | tf_op jit(solution)/shard_map/ppermute | solution.py:16
  44.6 9.9 %copy-start = (bf16[3584,1024]{1,0:T(8,128)(2,1)}, bf16[3584,1024]{1,0:T(8,128)(2,1)S(1)}, u32[]{:S(2)}) copy-start(bf16[3584,1024]{1,0:T(8,128)(2,1)S(1)} %shard_map.128.down) | copy-start | bytes 22020100
  44.7 9.3 %collective-permute-start.9 = (bf16[2,32,896]{2,1,0:T(8,128)(2,1)S(1)}, bf16[2,32,896]{2,1,0:T(8,128)(2,1)S(1)}, u32[]{:S(2)}, u32[]{:S(2)}) collective-permute-start(bf16[2,32,896]{2,1,0:T(8,128)(2,1)S(1)} %get-tuple-element.43), channel_id=1, source_target_pairs={{0,1},{1,0},{2,3},{3,2},{4,5},{5,4},{6,7},{7,6},{8,9},{9,8},{10,11... | collective-permute-start | bytes 344072 | tf_op jit(solution)/shard_map/ppermute | solution.py:16
  47.2 6.8 %collective-permute-start.6 = (bf16[2,32,896]{2,1,0:T(8,128)(2,1)S(1)}, bf16[2,32,896]{2,1,0:T(8,128)(2,1)S(1)}, u32[]{:S(2)}, u32[]{:S(2)}) collective-permute-start(bf16[2,32,896]{2,1,0:T(8,128)(2,1)S(1)} %get-tuple-element.40), channel_id=1, source_target_pairs={{0,1},{1,0},{2,3},{3,2},{4,5},{5,4},{6,7},{7,6},{8,9},{9,8},{10,11... | collective-permute-start | bytes 344072 | tf_op jit(solution)/shard_map/ppermute | solution.py:16
  49.1 10.5 %collective-permute-start.20 = (bf16[32,1024]{1,0:T(8,128)(2,1)S(1)}, bf16[32,1024]{1,0:T(8,128)(2,1)S(1)}, u32[]{:S(2)}, u32[]{:S(2)}) collective-permute-start(bf16[32,1024]{1,0:T(8,128)(2,1)S(1)} %get-tuple-element.62), channel_id=1, source_target_pairs={{0,4},{4,8},{8,12},{12,0},{1,5},{5,9},{9,13},{13,1},{2,6},{6,10},{... | collective-permute-start | bytes 196616 | tf_op jit(solution)/shard_map/ppermute | solution.py:16
  52.5 7.1 %collective-permute-start.22 = (bf16[32,1024]{1,0:T(8,128)(2,1)S(1)}, bf16[32,1024]{1,0:T(8,128)(2,1)S(1)}, u32[]{:S(2)}, u32[]{:S(2)}) collective-permute-start(bf16[32,1024]{1,0:T(8,128)(2,1)S(1)} %get-tuple-element.63), channel_id=1, source_target_pairs={{0,12},{4,0},{8,4},{12,8},{1,13},{5,1},{9,5},{13,9},{2,14},{6,2},{... | collective-permute-start | bytes 196616 | tf_op jit(solution)/shard_map/ppermute | solution.py:16
  53.0 6.8 %collective-permute-start.21 = (bf16[32,1024]{1,0:T(8,128)(2,1)S(1)}, bf16[32,1024]{1,0:T(8,128)(2,1)S(1)}, u32[]{:S(2)}, u32[]{:S(2)}) collective-permute-start(bf16[32,1024]{1,0:T(8,128)(2,1)S(1)} %get-tuple-element.64), channel_id=1, source_target_pairs={{0,8},{4,12},{8,0},{12,4},{1,9},{5,13},{9,1},{13,5},{2,10},{6,14},... | collective-permute-start | bytes 196616 | tf_op jit(solution)/shard_map/ppermute | solution.py:16
  55.7 6.9 %collective-permute-start.10 = (bf16[32,1024]{1,0:T(8,128)(2,1)S(1)}, bf16[32,1024]{1,0:T(8,128)(2,1)S(1)}, u32[]{:S(2)}, u32[]{:S(2)}) collective-permute-start(bf16[32,1024]{1,0:T(8,128)(2,1)S(1)} %get-tuple-element.65), channel_id=1, source_target_pairs={{0,4},{4,8},{8,12},{12,0},{1,5},{5,9},{9,13},{13,1},{2,6},{6,10},{... | collective-permute-start | bytes 196616 | tf_op jit(solution)/shard_map/ppermute | solution.py:16
  56.3 6.3 %collective-permute-start.12 = (bf16[32,1024]{1,0:T(8,128)(2,1)S(1)}, bf16[32,1024]{1,0:T(8,128)(2,1)S(1)}, u32[]{:S(2)}, u32[]{:S(2)}) collective-permute-start(bf16[32,1024]{1,0:T(8,128)(2,1)S(1)} %get-tuple-element.66), channel_id=1, source_target_pairs={{0,12},{4,0},{8,4},{12,8},{1,13},{5,1},{9,5},{13,9},{2,14},{6,2},{... | collective-permute-start | bytes 196616 | tf_op jit(solution)/shard_map/ppermute | solution.py:16
  59.6 5.8 %collective-permute-start.11 = (bf16[32,1024]{1,0:T(8,128)(2,1)S(1)}, bf16[32,1024]{1,0:T(8,128)(2,1)S(1)}, u32[]{:S(2)}, u32[]{:S(2)}) collective-permute-start(bf16[32,1024]{1,0:T(8,128)(2,1)S(1)} %get-tuple-element.67), channel_id=1, source_target_pairs={{0,8},{4,12},{8,0},{12,4},{1,9},{5,13},{9,1},{13,5},{2,10},{6,14},... | collective-permute-start | bytes 196616 | tf_op jit(solution)/shard_map/ppermute | solution.py:16
  65.5 4.8 %collective-permute-start.23 = (bf16[32,1024]{1,0:T(8,128)(2,1)S(1)}, bf16[32,1024]{1,0:T(8,128)(2,1)S(1)}, u32[]{:S(2)}, u32[]{:S(2)}) collective-permute-start(bf16[32,1024]{1,0:T(8,128)(2,1)S(1)} %get-tuple-element.61), channel_id=1, source_target_pairs={{0,12},{4,0},{8,4},{12,8},{1,13},{5,1},{9,5},{13,9},{2,14},{6,2},{... | collective-permute-start | bytes 196616 | tf_op jit(solution)/shard_map/ppermute | solution.py:16
  67.7 6.5 %collective-permute-start.24 = (bf16[32,1024]{1,0:T(8,128)(2,1)S(1)}, bf16[32,1024]{1,0:T(8,128)(2,1)S(1)}, u32[]{:S(2)}, u32[]{:S(2)}) collective-permute-start(bf16[32,1024]{1,0:T(8,128)(2,1)S(1)} %get-tuple-element.61), channel_id=1, source_target_pairs={{0,8},{4,12},{8,0},{12,4},{1,9},{5,13},{9,1},{13,5},{2,10},{6,14},... | collective-permute-start | bytes 196616 | tf_op jit(solution)/shard_map/ppermute | solution.py:16
  67.7 6.6 %collective-permute-start.25 = (bf16[32,1024]{1,0:T(8,128)(2,1)S(1)}, bf16[32,1024]{1,0:T(8,128)(2,1)S(1)}, u32[]{:S(2)}, u32[]{:S(2)}) collective-permute-start(bf16[32,1024]{1,0:T(8,128)(2,1)S(1)} %get-tuple-element.61), channel_id=1, source_target_pairs={{0,4},{4,8},{8,12},{12,0},{1,5},{5,9},{9,13},{13,1},{2,6},{6,10},{... | collective-permute-start | bytes 196616 | tf_op jit(solution)/shard_map/ppermute | solution.py:16
  74.3 3.1 %copy-start.1 = (bf16[3584,1024]{1,0:T(8,128)(2,1)S(1)}, bf16[3584,1024]{1,0:T(8,128)(2,1)}, u32[]{:S(2)}) copy-start(bf16[3584,1024]{1,0:T(8,128)(2,1)} %copy-done) | copy-start | bytes 22020100
  78.7 2.0 %collective-permute-start.26 = (bf16[2,32,896]{2,1,0:T(8,128)(2,1)S(1)}, bf16[2,32,896]{2,1,0:T(8,128)(2,1)S(1)}, u32[]{:S(2)}, u32[]{:S(2)}) collective-permute-start(bf16[2,32,896]{2,1,0:T(8,128)(2,1)S(1)} %get-tuple-element.48), channel_id=1, source_target_pairs={{0,1},{1,0},{2,3},{3,2},{4,5},{5,4},{6,7},{7,6},{8,9},{9,8},{10,11... | collective-permute-start | bytes 344072 | tf_op jit(solution)/shard_map/ppermute | solution.py:16
  80.2 1.5 %collective-permute-start.29 = (bf16[2,32,896]{2,1,0:T(8,128)(2,1)S(1)}, bf16[2,32,896]{2,1,0:T(8,128)(2,1)S(1)}, u32[]{:S(2)}, u32[]{:S(2)}) collective-permute-start(bf16[2,32,896]{2,1,0:T(8,128)(2,1)S(1)} %get-tuple-element.53), channel_id=1, source_target_pairs={{0,1},{1,0},{2,3},{3,2},{4,5},{5,4},{6,7},{7,6},{8,9},{9,8},{10,11... | collective-permute-start | bytes 344072 | tf_op jit(solution)/shard_map/ppermute | solution.py:16
  80.8 6.9 %collective-permute-start.27 = (bf16[2,32,896]{2,1,0:T(8,128)(2,1)S(1)}, bf16[2,32,896]{2,1,0:T(8,128)(2,1)S(1)}, u32[]{:S(2)}, u32[]{:S(2)}) collective-permute-start(bf16[2,32,896]{2,1,0:T(8,128)(2,1)S(1)} %add_convert_fusion.5.before.mine), channel_id=1, source_target_pairs={{0,2},{2,0},{1,3},{3,1},{4,6},{6,4},{5,7},{7,5},{8,10},{10,8},{9,1... | collective-permute-start | bytes 344072 | tf_op jit(solution)/shard_map/ppermute | solution.py:16
  81.7 6.6 %collective-permute-start.30 = (bf16[2,32,896]{2,1,0:T(8,128)(2,1)S(1)}, bf16[2,32,896]{2,1,0:T(8,128)(2,1)S(1)}, u32[]{:S(2)}, u32[]{:S(2)}) collective-permute-start(bf16[2,32,896]{2,1,0:T(8,128)(2,1)S(1)} %add_convert_fusion.4.mine), channel_id=1, source_target_pairs={{0,2},{2,0},{1,3},{3,1},{4,6},{6,4},{5,7},{7,5},{8,10},{10,8},{9,1... | collective-permute-start | bytes 344072 | tf_op jit(solution)/shard_map/ppermute | solution.py:16
  87.9 7.4 %collective-permute-start.28 = (bf16[2,2,32,896]{3,2,1,0:T(8,128)(2,1)S(1)}, bf16[2,2,32,896]{3,2,1,0:T(8,128)(2,1)S(1)}, u32[]{:S(2)}, u32[]{:S(2)}) collective-permute-start(bf16[2,2,32,896]{3,2,1,0:T(8,128)(2,1)S(1)} %shard_map.134.mine), channel_id=1, source_target_pairs={{0,1},{1,0},{2,3},{3,2},{4,5},{5,4},{6,7},{7,6},{8,9},{9,8},{10,11... | collective-permute-start | bytes 688136 | tf_op jit(solution)/shard_map/ppermute | solution.py:16
  88.5 1.6 %collective-permute-start.31 = (bf16[2,2,32,896]{3,2,1,0:T(8,128)(2,1)S(1)}, bf16[2,2,32,896]{3,2,1,0:T(8,128)(2,1)S(1)}, u32[]{:S(2)}, u32[]{:S(2)}) collective-permute-start(bf16[2,2,32,896]{3,2,1,0:T(8,128)(2,1)S(1)} %shard_map.136.mine), channel_id=1, source_target_pairs={{0,1},{1,0},{2,3},{3,2},{4,5},{5,4},{6,7},{7,6},{8,9},{9,8},{10,11... | collective-permute-start | bytes 688136 | tf_op jit(solution)/shard_map/ppermute | solution.py:16

commit v4 on v3

--- a/solution.py
+++ b/solution.py
@@ -57,9 +57,33 @@
 
 
 def prepare_kernel(
-    ranks, capacity, dps, pipes, place, routes, shares, gate, up, picker, weights, gate_out, up_out, sems
+    ranks,
+    capacity,
+    dps,
+    pipes,
+    place,
+    far_routes,
+    far_shares,
+    gate,
+    up,
+    picker,
+    weights,
+    gate_out,
+    up_out,
+    routes,
+    shares,
+    sems,
+    table_sems,
 ):
+    tables = [
+        pltpu.make_async_copy(far_routes, routes, table_sems.at[0]),
+        pltpu.make_async_copy(far_shares, shares, table_sems.at[1]),
+    ]
+    for copy in tables:
+        copy.start()
     copies = load_start(((gate, gate_out), (up, up_out)), sems, 8)
+    for copy in tables:
+        copy.wait()
     rank, dp, pipe = place[0], place[1], place[2]
     experts, slots, token_count = picker.shape
     block = token_count // ranks
@@ -97,7 +121,7 @@
     slots = capacity * ranks
     return pl.pallas_call(
         functools.partial(prepare_kernel, ranks, capacity, dps, pipes),
-        in_specs=[scalars(), whole(), whole(), in_hbm(), in_hbm()],
+        in_specs=[scalars(), in_hbm(), in_hbm(), in_hbm(), in_hbm()],
         out_specs=(whole(), whole(), whole(), whole()),
         out_shape=(
             jax.ShapeDtypeStruct((experts, slots, token_count), BF),
@@ -105,12 +129,17 @@
             pltpu.VMEM(gate.shape, BF),
             pltpu.VMEM(up.shape, BF),
         ),
-        scratch_shapes=[pltpu.SemaphoreType.DMA((2, 8))],
+        scratch_shapes=[
+            pltpu.VMEM(routes.shape, routes.dtype),
+            pltpu.VMEM(shares.shape, shares.dtype),
+            pltpu.SemaphoreType.DMA((2, 8)),
+            pltpu.SemaphoreType.DMA((2,)),
+        ],
         compiler_params=pltpu.CompilerParams(vmem_limit_bytes=8 * 1024 * 1024),
         cost_estimate=pl.CostEstimate(
             flops=0, bytes_accessed=4 * gate.size, transcendentals=0
         ),
-    )(place, routes, shares, far(gate), far(up))
+    )(place, far(routes), far(shares), far(gate), far(up))
 
 
 def load_kernel(source, before, out, sems):
@@ -132,18 +161,44 @@
     )(far(source), before)
 
 
-def add_kernel(a, b, before, out):
-    out[...] = (a[...].astype(F32) + b[...].astype(F32)).astype(BF)
-
-
-def add_after(a, b, before):
-    return pl.pallas_call(
-        add_kernel,
-        in_specs=[whole(), whole(), anywhere()],
+def pair_kernel(*refs):
+    out = refs[-1]
+    rows = out.shape[0] // (len(refs) - 2)
+    for i, value in enumerate(refs[:-2]):
+        out[i * rows : (i + 1) * rows, :] = value[...]
+
+
+def pair(values, before):
+    rows, width = values[0].shape
+    return pl.pallas_call(
+        pair_kernel,
+        in_specs=[whole()] * len(values) + [anywhere()],
         out_specs=whole(),
-        out_shape=jax.ShapeDtypeStruct(a.shape, BF),
+        out_shape=jax.ShapeDtypeStruct((rows * len(values), width), BF),
         compiler_params=pltpu.CompilerParams(vmem_limit_bytes=4 * 1024 * 1024),
-    )(a, b, before)
+    )(*values, before)
+
+
+def residual_kernel(ranks, *refs):
+    student = refs[0][...].astype(F32)
+    target = refs[ranks][...].astype(F32)
+    for i in range(1, ranks):
+        student = student + refs[i][...].astype(F32)
+        target = target + refs[ranks + i][...].astype(F32)
+    refs[-2][...] = student.astype(BF)
+    refs[-1][...] = (student - target).astype(BF)
+
+
+def residual_of(student, target, before):
+    ranks = len(student)
+    block = jax.ShapeDtypeStruct(student[0].shape, BF)
+    return pl.pallas_call(
+        functools.partial(residual_kernel, ranks),
+        in_specs=[whole()] * (2 * ranks) + [anywhere()] * len(before),
+        out_specs=(whole(), whole()),
+        out_shape=(block, block),
+        compiler_params=pltpu.CompilerParams(vmem_limit_bytes=4 * 1024 * 1024),
+    )(*student, *target, *before)
 
 
 def tile_of(size):
@@ -264,7 +319,7 @@
     dp, pipe = place[1], place[2]
     rows = out.shape[0] // (dps * pipes)
     at = 0
-    for i in range((len(refs) - 1) // 2):
+    for i in range((len(refs) - 2) // 2):
         size = refs[2 * i].shape[1]
         for j1 in range(pipes):
             for j0 in range(dps):
@@ -274,18 +329,18 @@
         at += size
 
 
-def join(place, parts, dps, pipes):
+def join(place, parts, before, dps, pipes):
     assert pipes == 2
     flat = [value for pair in parts for value in pair]
     rows = flat[0].shape[0] * pipes
     width = sum(pair[0].shape[1] for pair in parts)
     return pl.pallas_call(
         functools.partial(join_kernel, dps, pipes),
-        in_specs=[scalars()] + [whole()] * len(flat),
+        in_specs=[scalars()] + [whole()] * len(flat) + [anywhere()],
         out_specs=whole(),
         out_shape=jax.ShapeDtypeStruct((rows, width), BF),
         compiler_params=pltpu.CompilerParams(vmem_limit_bytes=8 * 1024 * 1024),
-    )(place, *flat)
+    )(place, *flat, before)
 
 
 def spread_kernel(picker, hidden, out):
@@ -322,7 +377,7 @@
     )(dense, tokens, before)
 
 
-def hidden_grad_kernel(first, picker, residual, down, keep, send):
+def hidden_grad_kernel(first, picker, residual, down, before, keep, send):
     half = keep.shape[1]
     for i in range(keep.shape[0]):
         e = first + i
@@ -332,16 +387,16 @@
         send[i] = product[half:]
 
 
-def hidden_grad_parts(picker, residual, down, first, count):
+def hidden_grad_parts(picker, residual, down, before, first, count):
     slots = picker.shape[1]
     halves = jax.ShapeDtypeStruct((count, slots // 2, H), BF)
     return pl.pallas_call(
         functools.partial(hidden_grad_kernel, first),
-        in_specs=[whole(), whole(), whole()],
+        in_specs=[whole(), whole(), whole(), anywhere()],
         out_specs=(whole(), whole()),
         out_shape=(halves, halves),
         compiler_params=pltpu.CompilerParams(vmem_limit_bytes=8 * 1024 * 1024),
-    )(picker, residual, down)
+    )(picker, residual, down, before)
 
 
 def hidden_grad_act_kernel(first, swap, mine, other, pre, weight, before, out):
@@ -371,9 +426,18 @@
     )(mine, other, pre, weight, before)
 
 
-def down_grad_kernel(hidden, residual, before, out, done):
-    out[...] = dot(hidden[...], residual[...]).astype(BF)
+def down_grad_kernel(hidden, residual, before, out, done, held, sems):
+    tiles = sems.shape[0]
+    rows = hidden.shape[0] // tiles
+    copies = []
+    for i in range(tiles):
+        part = pl.ds(i * rows, rows)
+        held[part, :] = dot(hidden[part, :], residual[...]).astype(BF)
+        copies.append(pltpu.make_async_copy(held.at[part], out.at[part], sems.at[i]))
+        copies[-1].start()
     done[...] = jnp.zeros_like(done)
+    for copy in copies:
+        copy.wait()
 
 
 def down_grad(hidden, residual, before):
@@ -381,20 +445,16 @@
     width = residual.shape[1]
     return pl.pallas_call(
         down_grad_kernel,
-        grid=(rows // H,),
-        in_specs=[
-            pl.BlockSpec((H, token_count), lambda i: (i, 0)),
-            pl.BlockSpec((token_count, width), lambda i: (0, 0)),
-            anywhere(),
-        ],
-        out_specs=(
-            pl.BlockSpec((H, width), lambda i: (i, 0)),
-            pl.BlockSpec((8, 128), lambda i: (0, 0)),
-        ),
+        in_specs=[whole(), whole(), anywhere()],
+        out_specs=(in_hbm(), whole()),
         out_shape=(
             jax.ShapeDtypeStruct((rows, width), BF),
             jax.ShapeDtypeStruct((8, 128), F32),
         ),
+        scratch_shapes=[
+            pltpu.VMEM((rows, width), BF),
+            pltpu.SemaphoreType.DMA((rows // (H // 2),)),
+        ],
         compiler_params=pltpu.CompilerParams(vmem_limit_bytes=16 * 1024 * 1024),
         cost_estimate=pl.CostEstimate(
             flops=2 * rows * width * token_count,
@@ -404,36 +464,45 @@
     )(hidden, residual, before)
 
 
-def input_grad_kernel(picker, tokens, mine, theirs, *rest):
-    out_gate, out_up = rest[-2:]
-    for which, out in enumerate((out_gate, out_up)):
-        grad = jnp.concatenate([mine[0, which], theirs[0, which]], axis=0)
-        dense = dot(picker[0], grad, 0, 0).astype(BF)
-        out[...] = dot(tokens[...], dense).astype(BF)
+def input_grad_kernel(first, picker, tokens, mine, theirs, *rest):
+    outs, held, sems = rest[-4:-2], rest[-2], rest[-1]
+    count = mine.shape[0]
+    splits = sems.shape[2]
+    rows = tokens.shape[0] // splits
+    copies = []
+    for i in range(count):
+        for which in range(2):
+            grad = jnp.concatenate([mine[i, which], theirs[i, which]], axis=0)
+            dense = dot(picker[first + i], grad, 0, 0).astype(BF)
+            for r in range(splits):
+                part = pl.ds(r * rows, rows)
+                columns = pl.ds((first + i) * H, H)
+                held[i, which, part] = dot(tokens[part, :], dense).astype(BF)
+                copies.append(
+                    pltpu.make_async_copy(
+                        held.at[i, which, part], outs[which].at[part, columns], sems.at[i, which, r]
+                    )
+                )
+                copies[-1].start()
+    for copy in copies:
+        copy.wait()
 
 
 def input_grads(picker, tokens, mine, theirs, first, so_far):
     experts, slots, token_count = picker.shape
     width = tokens.shape[0]
     count = mine.shape[0]
-    split = 2 if width % 256 == 0 else 1
-    part = width // split
-    grad_spec = pl.BlockSpec((1, 2, slots // 2, H), lambda i, j: (i, 0, 0, 0))
-    out_spec = pl.BlockSpec((part, H), lambda i, j: (j, first + i))
     out = jax.ShapeDtypeStruct((width, experts * H), BF)
     extra = () if so_far is None else so_far
     return pl.pallas_call(
-        input_grad_kernel,
-        grid=(count, split),
-        in_specs=[
-            pl.BlockSpec((1, slots, token_count), lambda i, j: (first + i, 0, 0)),
-            pl.BlockSpec((part, token_count), lambda i, j: (j, 0)),
-            grad_spec,
-            grad_spec,
-        ]
-        + [in_hbm()] * len(extra),
-        out_specs=(out_spec, out_spec),
+        functools.partial(input_grad_kernel, first),
+        in_specs=[whole()] * 4 + [in_hbm()] * len(extra),
+        out_specs=(in_hbm(), in_hbm()),
         out_shape=(out, out),
+        scratch_shapes=[
+            pltpu.VMEM((count, 2, width, H), BF),
+            pltpu.SemaphoreType.DMA((count, 2, 2)),
+        ],
         input_output_aliases={4 + i: i for i in range(len(extra))},
         compiler_params=pltpu.CompilerParams(vmem_limit_bytes=16 * 1024 * 1024),
         cost_estimate=pl.CostEstimate(
@@ -461,10 +530,12 @@
     return total
 
 
+def gather_dp_parts(value, count):
+    return [value] + [shift(value, "dp", count, -s) for s in range(1, count)]
+
+
 def gather_dp(value, count):
-    return jnp.concatenate(
-        [value] + [shift(value, "dp", count, -s) for s in range(1, count)], axis=-2
-    )
+    return jnp.concatenate(gather_dp_parts(value, count), axis=-2)
 
 
 def exchange_dp(value, count):
@@ -497,23 +568,32 @@
     slots = block // 2 * ranks
     place = jnp.stack([rank, dp, pipe]).astype(jnp.int32)
 
+    paired = ranks & (ranks - 1) == 0
+
+    def to_partner(value, s):
+        if paired:
+            return lax.ppermute(value, "expert", [(i, i ^ s) for i in range(ranks)])
+        return shift(value, "expert", ranks, s)
+
+    def target_of(s):
+        return rank ^ s if paired else (rank + s) % ranks
+
+    def source_of(s):
+        return rank ^ s if paired else (rank + ranks - s) % ranks
+
     def gather_tokens(mine):
         whole_rows = jnp.zeros((token_count, mine.shape[1]), BF)
         whole_rows = lax.dynamic_update_slice(whole_rows, mine, (rank * block, 0))
         for s in range(1, ranks):
-            theirs = shift(mine, "expert", ranks, -s)
-            at = (rank + s) % ranks * block
-            whole_rows = lax.dynamic_update_slice(whole_rows, theirs, (at, 0))
+            theirs = to_partner(mine, s)
+            whole_rows = lax.dynamic_update_slice(whole_rows, theirs, (source_of(s) * block, 0))
         return whole_rows
 
     def to_owners(product):
-        def block_of(s):
-            return lax.dynamic_slice_in_dim(product, (rank + s) % ranks * block, block, axis=0)
-
-        total = block_of(0).astype(F32)
-        for s in range(1, ranks):
-            total = total + shift(block_of(s), "expert", ranks, s).astype(F32)
-        return total
+        def block_of(r):
+            return lax.dynamic_slice_in_dim(product, r * block, block, axis=0)
+
+        return [block_of(rank)] + [to_partner(block_of(target_of(s)), s) for s in range(1, ranks)]
 
     base = gather_tokens(tokens)
     picker, slot_weight, gate_near, up_near = prepare(
@@ -535,16 +615,17 @@
         keep, send = expert_pre(picker, base, expert_gate, expert_up, last, first, group)
         last = keep
         parts.append((keep, shift(send, "pipe", pipes, 1)))
-    teacher_down = load(teacher_down, last)
-    expert_down = load(expert_down, teacher_down)
+    teacher_near = load(teacher_down, last)
 
     hiddens = []
     for half in halves:
         total = scatter_dp(half, dps)
-        hidden = gather_dp((jax.nn.silu(total[0]) * total[1]).astype(BF), dps)
+        hidden = (jax.nn.silu(total[0]) * total[1]).astype(BF)
+        hidden = pair(gather_dp_parts(hidden, dps), teacher_near)
         hiddens.append((hidden, shift(hidden, "pipe", pipes, 1)))
-    hidden = join(place, hiddens, dps, pipes)
-    target = to_owners(jnp.dot(hidden, teacher_down, preferred_element_type=F32).astype(BF))
+    expert_near = load(expert_down, hiddens[-1][0])
+    hidden = join(place, hiddens, expert_near, dps, pipes)
+    target = to_owners(jnp.dot(hidden, teacher_near, preferred_element_type=F32).astype(BF))
 
     pre, weighted = [], []
     for first, (keep, theirs) in zip(firsts, parts):
@@ -555,14 +636,18 @@
     weighted = jnp.concatenate(weighted, axis=0)
 
     dense = spread(picker, weighted)
-    product = jnp.dot(dense, expert_down, preferred_element_type=F32).astype(BF)
-    student_sum = to_owners(product)
+    product = jnp.dot(dense, expert_near, preferred_element_type=F32).astype(BF)
+    student = to_owners(product)
     dense_flipped, base_flipped = flip(dense, base, product)
-    residual = gather_tokens((student_sum - target).astype(BF))
+    expert_near = load(expert_down, base_flipped)
+    student_out, residual = residual_of(student, target, (expert_near,))
+    residual = gather_tokens(residual)
 
     sums = []
+    last = residual
     for first in firsts:
-        keep, send = hidden_grad_parts(picker, residual, expert_down, first, group)
+        keep, send = hidden_grad_parts(picker, residual, expert_near, last, first, group)
+        last = keep
         sums.append(add(keep, shift(send, "pipe", pipes, 1)))
     pairs = [exchange_dp(value, dps) for value in sums]
     grad_down, done = down_grad(dense_flipped, residual, sums[-1])
@@ -571,7 +656,7 @@
         mine = hidden_grad_act(*pairs[i], dps == 2, pre[i], slot_weight, done, first)
         theirs = shift(mine, "pipe", pipes, 1)
         grads = input_grads(picker, base_flipped, mine, theirs, first, grads)
-    return (student_sum.astype(BF), grads[0], grads[1], grad_down)
+    return (student_out, grads[0], grads[1], grad_down)
 
 
 def solution(mesh):

time: 101 us -> 94.8 us (0.939)
  local copies, waits for them, and re-layouts: 4.65 us -> 0.23 us
  waiting for transfers between devices: 18.4 us -> 16.8 us
    ppermute x0 -> x12, starting transfers between devices: none -> 19 us  [to_partner(): return lax.ppermute(value, 'expert', [(i, i ^ s) for i in range(ranks)])]
    ppermute x32 -> x20, starting transfers between devices: 30.2 us -> 11.5 us  [shift(): lax.ppermute(value, axis, [(i, (i + by) % count) for i in range(count)])]
    ppermute x32 -> x20, waiting for transfers between devices: 18.4 us -> 11.2 us  [shift(): lax.ppermute(value, axis, [(i, (i + by) % count) for i in range(count)])]
    ppermute x0 -> x12, waiting for transfers between devices: none -> 5.56 us  [to_partner(): return lax.ppermute(value, 'expert', [(i, i ^ s) for i in range(ranks)])]
    unnamed x10 -> x2, local copies, waits for them, and re-layouts: 4.45 us -> 0.01 us
    pallas_call x2 -> x3, Pallas kernels: 6.34 us -> 9.51 us  [load(): pl.pallas_call(load_kernel, in_specs=[in_hbm(), anywhere()], out_specs=wh...]
    pallas_call x3 -> x6, Pallas kernels: 14.8 us -> 11.8 us  [the longest x2 7.69 us: input_grads(): pl.pallas_call(functools.partial(input_grad_kernel, first), in_specs=[who...]
  transfers between devices with their start and end apart: 32 -> 32, of which waited for: 12 -> 11; matrix products, arithmetic and copies ran while one was open for 4% -> 3% of each run, Pallas kernels for 34% -> 37%
where the time goes in v4:
time: 94.8 us; the launch traced here: 94.6 us
  Pallas kernels  42.8 us (45%)
  starting transfers between devices  30.5 us (32%)
  waiting for transfers between devices  16.8 us (18%)
  matrix products  2.24 us (2%)
  between operations  1.28 us (1%)
    ppermute x12, starting transfers between devices, to_partner(): return lax.ppermute(value, 'expert', [(i, i ^ s) for i in range(ranks)])  19 us
    ppermute x20, starting transfers between devices, shift(): lax.ppermute(value, axis, [(i, (i + by) % count) for i in range(count)])  11.5 us
    ppermute x20, waiting for transfers between devices, shift(): lax.ppermute(value, axis, [(i, (i + by) % count) for i in range(count)])  11.2 us
    pallas_call x3, Pallas kernels, load(): pl.pallas_call(load_kernel, in_specs=[in_hbm(), anywhere()], out_specs=wh...  9.51 us
    pallas_call x2, Pallas kernels, input_grads(): pl.pallas_call(functools.partial(input_grad_kernel, first), in_specs=[who...  7.69 us
    pallas_call x2, Pallas kernels, expert_pre(): pl.pallas_call(functools.partial(expert_kernel, first), in_specs=[whole()...  7.44 us
    pallas_call x1, Pallas kernels, prepare(): pl.pallas_call(functools.partial(prepare_kernel, ranks, capacity, dps, pi...  5.89 us
    ppermute x12, waiting for transfers between devices, to_partner(): return lax.ppermute(value, 'expert', [(i, i ^ s) for i in range(ranks)])  5.56 us
  transfers between devices with their start and end apart: 32, of which 11 were waited for; matrix products, arithmetic and copies ran while one was open for 3% of the time, Pallas kernels for 37%

profile of v4, /device:TPU:0, one launch (start us, length us, event | category | flops | bytes accessed | tf_op | source)
XLA Modules:
  0.0 94.6 jit_solution(10642299800406281141)
XLA Ops:
  0.6 3.1 %collective-permute-start = (bf16[32,1024]{1,0:T(8,128)(2,1)}, bf16[32,1024]{1,0:T(8,128)(2,1)S(1)}, u32[]{:S(2)}, u32[]{:S(2)}) collective-permute-start(bf16[32,1024]{1,0:T(8,128)(2,1)} %param.9), channel_id=1, source_target_pairs={{0,4},{4,0},{8,12},{12,8},{1,5},{5,1},{9,13},{13,9},{2,6},{6,2},{1... | collective-permute-start | bytes 196616 | tf_op jit(solution)/shard_map/ppermute | solution.py:575
  3.7 2.5 %collective-permute-start.2 = (bf16[32,1024]{1,0:T(8,128)(2,1)}, bf16[32,1024]{1,0:T(8,128)(2,1)S(1)}, u32[]{:S(2)}, u32[]{:S(2)}) collective-permute-start(bf16[32,1024]{1,0:T(8,128)(2,1)} %param.9), channel_id=1, source_target_pairs={{0,12},{4,8},{8,4},{12,0},{1,13},{5,9},{9,5},{13,1},{2,14},{6,10},... | collective-permute-start | bytes 196616 | tf_op jit(solution)/shard_map/ppermute | solution.py:575
  6.2 0.1 collective-permute-start.1
  6.3 0.1 pad_add_fusion.place
  6.4 5.9 %shard_map.120 = (bf16[4,64,128]{2,1,0:T(8,128)(2,1)S(1)}, f32[4,64,1]{2,1,0:T(8,128)S(1)}, bf16[1024,3584]{1,0:T(8,128)(2,1)S(1)}, bf16[1024,3584]{1,0:T(8,128)(2,1)S(1)}) custom-call(s32[3]{0:T(128)S(1)} %pad_add_fusion.place, s32[4,128]{1,0:T(4,128)} %bitcast.29, f32[4,128]{1,0:T(4,128)} %bitcast.30, bf16[1024,3584]{1,0:T(8,128)(2,1)} %gate.3, ...), custom_call_target="tpu_custom_call" | custom-call | bytes 14680064 | tf_op jit(solution)/shard_map/pallas_call | solution.py:122
  12.4 0.5 collective-permute-done.1
  12.9 1.7 %shard_map.130 = (bf16[2,64,1792]{2,1,0:T(8,128)(2,1)S(1)}, bf16[2,64,1792]{2,1,0:T(8,128)(2,1)S(1)}) custom-call(s32[3]{0:T(128)S(1)} %pad_add_fusion.place, bf16[128,1024]{1,0:T(8,128)(2,1)S(1)} %constant_dynamic-update-slice_fusion.4.tokens, bf16[1024,3584]{1,0:T(8,128)(2,1)S(1)} %get-tuple-element.35.gate, bf16[1024,3584]{1,0:T(8,128)(2,1)S(1)} %get-tuple-element.36.up), custom_call_target="tpu_custom_call" | custom-call | flops 939524096 | bytes 7340032 | tf_op jit(solution)/shard_map/pallas_call | solution.py:229
  14.6 0.1 collective-permute-start.15
  14.7 1.7 %shard_map.121 = (bf16[2,64,1792]{2,1,0:T(8,128)(2,1)S(1)}, bf16[2,64,1792]{2,1,0:T(8,128)(2,1)S(1)}) custom-call(s32[3]{0:T(128)S(1)} %pad_add_fusion.place, bf16[128,1024]{1,0:T(8,128)(2,1)S(1)} %constant_dynamic-update-slice_fusion.4.tokens, bf16[1024,3584]{1,0:T(8,128)(2,1)S(1)} %get-tuple-element.35.gate, bf16[1024,3584]{1,0:T(8,128)(2,1)S(1)} %get-tuple-element.36.up), custom_call_target="tpu_custom_call" | custom-call | flops 939524096 | bytes 7340032 | tf_op jit(solution)/shard_map/pallas_call | solution.py:229
  16.3 0.6 collective-permute-start.3
  16.9 0.1 add_convert_fusion
  17.0 1.6 %collective-permute-start.16 = (bf16[2,32,1792]{2,1,0:T(8,128)(2,1)S(1)}, bf16[2,32,1792]{2,1,0:T(8,128)(2,1)S(1)}, u32[]{:S(2)}, u32[]{:S(2)}) collective-permute-start(bf16[2,32,1792]{2,1,0:T(8,128)(2,1)S(1)} %slice.37), channel_id=1, source_target_pairs={{0,2},{2,0},{1,3},{3,1},{4,6},{6,4},{5,7},{7,5},{8,10},{10,8},{9,1... | collective-permute-start | bytes 688136 | tf_op jit(solution)/shard_map/ppermute | solution.py:16
  18.6 0.1 add_convert_fusion.1.before
  18.7 1.3 %collective-permute-start.10 = (bf16[2,32,1792]{2,1,0:T(8,128)(2,1)S(1)}, bf16[2,32,1792]{2,1,0:T(8,128)(2,1)S(1)}, u32[]{:S(2)}, u32[]{:S(2)}) collective-permute-start(bf16[2,32,1792]{2,1,0:T(8,128)(2,1)S(1)} %slice.33), channel_id=1, source_target_pairs={{0,2},{2,0},{1,3},{3,1},{4,6},{6,4},{5,7},{7,5},{8,10},{10,8},{9,1... | collective-permute-start | bytes 688136 | tf_op jit(solution)/shard_map/ppermute | solution.py:16
  20.1 3.7 %shard_map.122 = (bf16[2,2,32,896]{3,2,1,0:T(8,128)(2,1)S(1)}, bf16[2,2,32,896]{3,2,1,0:T(8,128)(2,1)S(1)}) custom-call(bf16[4,64,128]{2,1,0:T(8,128)(2,1)S(1)} %get-tuple-element.34.picker, bf16[128,1024]{1,0:T(8,128)(2,1)S(1)} %constant_dynamic-update-slice_fusion.4.tokens, bf16[1024,3584]{1,0:T(8,128)(2,1)} %gate.5, bf16[1024,3584]{1,0:T(8,128)(2,1)} %up.5, ...), custom_call_target="tpu_custom_call" | custom-call | flops 469762048 | bytes 7340032 | tf_op jit(solution)/shard_map/pallas_call | solution.py:270
  23.8 0.1 collective-permute-start.4
  23.9 3.7 %shard_map.124 = (bf16[2,2,32,896]{3,2,1,0:T(8,128)(2,1)S(1)}, bf16[2,2,32,896]{3,2,1,0:T(8,128)(2,1)S(1)}) custom-call(bf16[4,64,128]{2,1,0:T(8,128)(2,1)S(1)} %get-tuple-element.34.picker, bf16[128,1024]{1,0:T(8,128)(2,1)S(1)} %constant_dynamic-update-slice_fusion.4.tokens, bf16[1024,3584]{1,0:T(8,128)(2,1)} %gate.5, bf16[1024,3584]{1,0:T(8,128)(2,1)} %up.5, ...), custom_call_target="tpu_custom_call" | custom-call | flops 469762048 | bytes 7340032 | tf_op jit(solution)/shard_map/pallas_call | solution.py:270
  27.7 0.5 collective-permute-start.7
  28.2 3.2 %shard_map.127.refs_2_ = bf16[3584,1024]{1,0:T(8,128)(2,1)S(1)} custom-call(bf16[3584,1024]{1,0:T(8,128)(2,1)} %source.3, bf16[2,2,32,896]{3,2,1,0:T(8,128)(2,1)S(1)} %get-tuple-element.43.before), custom_call_target="tpu_custom_call" | custom-call | bytes 7340032 | tf_op jit(solution)/shard_map/pallas_call | solution.py:151
  31.4 0.1 fusion.1.refs_0_
  31.5 0.8 collective-permute-start.17
  32.4 0.1 fusion.3.refs_0_
  32.5 1.3 %collective-permute-start.11 = (bf16[32,1792]{1,0:T(8,128)(2,1)S(1)}, bf16[32,1792]{1,0:T(8,128)(2,1)S(1)}, u32[]{:S(2)}, u32[]{:S(2)}) collective-permute-start(bf16[32,1792]{1,0:T(8,128)(2,1)S(1)} %fusion.3.refs_0_), channel_id=1, source_target_pairs={{0,2},{2,0},{1,3},{3,1},{4,6},{6,4},{5,7},{7,5},{8,10},{10,8},{9,1... | collective-permute-start | bytes 344072 | tf_op jit(solution)/shard_map/ppermute | solution.py:16
  33.9 0.8 collective-permute-start.8
  34.8 1.3 %collective-permute-start.5 = (bf16[2,2,32,896]{3,2,1,0:T(8,128)(2,1)S(1)}, bf16[2,2,32,896]{3,2,1,0:T(8,128)(2,1)S(1)}, u32[]{:S(2)}, u32[]{:S(2)}) collective-permute-start(bf16[2,2,32,896]{3,2,1,0:T(8,128)(2,1)S(1)} %add_convert_fusion.3.mine), channel_id=1, source_target_pairs={{0,2},{2,0},{1,3},{3,1},{4,6},{6,4},{5,7},{7,5},{8,10},{10,8},{9,1... | collective-permute-start | bytes 688136 | tf_op jit(solution)/shard_map/ppermute | solution.py:16
  36.1 1.5 %collective-permute-done.17.refs_1_ = bf16[32,1792]{1,0:T(8,128)(2,1)S(1)} collective-permute-done((bf16[32,1792]{1,0:T(8,128)(2,1)S(1)}, bf16[32,1792]{1,0:T(8,128)(2,1)S(1)}, u32[]{:S(2)}, u32[]{:S(2)}) %collective-permute-start.17) | collective-permute-done | bytes 114720 | tf_op jit(solution)/shard_map/ppermute | solution.py:16
  37.6 0.1 collective-permute-start.18
  37.6 2.4 %collective-permute-done.11.refs_1_ = bf16[32,1792]{1,0:T(8,128)(2,1)S(1)} collective-permute-done((bf16[32,1792]{1,0:T(8,128)(2,1)S(1)}, bf16[32,1792]{1,0:T(8,128)(2,1)S(1)}, u32[]{:S(2)}, u32[]{:S(2)}) %collective-permute-start.11) | collective-permute-done | bytes 114720 | tf_op jit(solution)/shard_map/ppermute | solution.py:16
  40.1 3.2 %shard_map.129.refs_4_ = bf16[3584,1024]{1,0:T(8,128)(2,1)S(1)} custom-call(bf16[3584,1024]{1,0:T(8,128)(2,1)} %source.5, bf16[64,1792]{1,0:T(8,128)(2,1)S(1)} %shard_map.128.before.refs_2_), custom_call_target="tpu_custom_call" | custom-call | bytes 7340032 | tf_op jit(solution)/shard_map/pallas_call | solution.py:151
  43.3 1.6 %collective-permute-done.8.other = bf16[2,2,32,896]{3,2,1,0:T(8,128)(2,1)S(1)} collective-permute-done((bf16[2,2,32,896]{3,2,1,0:T(8,128)(2,1)S(1)}, bf16[2,2,32,896]{3,2,1,0:T(8,128)(2,1)S(1)}, u32[]{:S(2)}, u32[]{:S(2)}) %collective-permute-start.8) | collective-permute-done | bytes 229408 | tf_op jit(solution)/shard_map/ppermute | solution.py:16
  44.9 0.1 shard_map.125
  45.1 3.9 %collective-permute-done.5.other = bf16[2,2,32,896]{3,2,1,0:T(8,128)(2,1)S(1)} collective-permute-done((bf16[2,2,32,896]{3,2,1,0:T(8,128)(2,1)S(1)}, bf16[2,2,32,896]{3,2,1,0:T(8,128)(2,1)S(1)}, u32[]{:S(2)}, u32[]{:S(2)}) %collective-permute-start.5) | collective-permute-done | bytes 229408 | tf_op jit(solution)/shard_map/ppermute | solution.py:16
  49.0 0.1 shard_map.123
  49.2 0.6 shard_map.132
  49.8 1.1 %convolution_convert_fusion = bf16[128,1024]{1,0:T(8,128)(2,1)S(1)} fusion(bf16[128,3584]{1,0:T(8,128)(2,1)S(1)} %shard_map.132, bf16[3584,1024]{1,0:T(8,128)(2,1)S(1)} %shard_map.127.refs_2_), kind=kOutput, calls=%fused_computation | convolution fusion | flops 939655168 | bytes 8519680 | tf_op jit(solution)/shard_map/dot_general | solution.py:628
  51.0 2.5 %collective-permute-start.22 = (bf16[32,1024]{1,0:T(8,128)(2,1)S(1)}, bf16[32,1024]{1,0:T(8,128)(2,1)S(1)}, u32[]{:S(2)}, u32[]{:S(2)}) collective-permute-start(bf16[32,1024]{1,0:T(8,128)(2,1)S(1)} %get-tuple-element.64), channel_id=1, source_target_pairs={{0,12},{4,8},{8,4},{12,0},{1,13},{5,9},{9,5},{13,1},{2,14},{6,10},... | collective-permute-start | bytes 196616 | tf_op jit(solution)/shard_map/ppermute | solution.py:575
  53.5 0.3 collective-permute-start.21
  53.8 1.6 %collective-permute-start.20 = (bf16[32,1024]{1,0:T(8,128)(2,1)S(1)}, bf16[32,1024]{1,0:T(8,128)(2,1)S(1)}, u32[]{:S(2)}, u32[]{:S(2)}) collective-permute-start(bf16[32,1024]{1,0:T(8,128)(2,1)S(1)} %get-tuple-element.66), channel_id=1, source_target_pairs={{0,4},{4,0},{8,12},{12,8},{1,5},{5,1},{9,13},{13,9},{2,6},{6,2},{1... | collective-permute-start | bytes 196616 | tf_op jit(solution)/shard_map/ppermute | solution.py:575
  55.5 0.4 shard_map.126.dense
  55.9 1.1 %convolution_convert_fusion.1.before = bf16[128,1024]{1,0:T(8,128)(2,1)S(1)} fusion(bf16[128,3584]{1,0:T(8,128)(2,1)S(1)} %shard_map.126.dense, bf16[3584,1024]{1,0:T(8,128)(2,1)S(1)} %shard_map.129.refs_4_), kind=kOutput, calls=%fused_computation.1 | convolution fusion | flops 939655168 | bytes 8519680 | tf_op jit(solution)/shard_map/dot_general | solution.py:639
  57.1 2.5 %collective-permute-start.14 = (bf16[32,1024]{1,0:T(8,128)(2,1)S(1)}, bf16[32,1024]{1,0:T(8,128)(2,1)S(1)}, u32[]{:S(2)}, u32[]{:S(2)}) collective-permute-start(bf16[32,1024]{1,0:T(8,128)(2,1)S(1)} %get-tuple-element.68), channel_id=1, source_target_pairs={{0,12},{4,8},{8,4},{12,0},{1,13},{5,9},{9,5},{13,1},{2,14},{6,10},... | collective-permute-start | bytes 196616 | tf_op jit(solution)/shard_map/ppermute | solution.py:575
  59.6 1.9 %collective-permute-start.12 = (bf16[32,1024]{1,0:T(8,128)(2,1)S(1)}, bf16[32,1024]{1,0:T(8,128)(2,1)S(1)}, u32[]{:S(2)}, u32[]{:S(2)}) collective-permute-start(bf16[32,1024]{1,0:T(8,128)(2,1)S(1)} %get-tuple-element.70), channel_id=1, source_target_pairs={{0,4},{4,0},{8,12},{12,8},{1,5},{5,1},{9,13},{13,9},{2,6},{6,2},{1... | collective-permute-start | bytes 196616 | tf_op jit(solution)/shard_map/ppermute | solution.py:575
  61.5 0.4 shard_map.133
  61.9 3.2 %shard_map.134.refs_8_.down = bf16[3584,1024]{1,0:T(8,128)(2,1)S(1)} custom-call(bf16[3584,1024]{1,0:T(8,128)(2,1)} %source.5, bf16[1024,128]{1,0:T(8,128)(2,1)S(1)} %get-tuple-element.48.before.tokens), custom_call_target="tpu_custom_call" | custom-call | bytes 7340032 | tf_op jit(solution)/shard_map/pallas_call | solution.py:151
  65.1 1.0 %collective-permute-done.13.refs_2_ = bf16[32,1024]{1,0:T(8,128)(2,1)S(1)} collective-permute-done((bf16[32,1024]{1,0:T(8,128)(2,1)S(1)}, bf16[32,1024]{1,0:T(8,128)(2,1)S(1)}, u32[]{:S(2)}, u32[]{:S(2)}) %collective-permute-start.13) | collective-permute-done | bytes 65568 | tf_op jit(solution)/shard_map/ppermute | solution.py:575
  66.1 0.7 shard_map.135
  66.8 2.5 %collective-permute-start.25 = (bf16[32,1024]{1,0:T(8,128)(2,1)S(1)}, bf16[32,1024]{1,0:T(8,128)(2,1)S(1)}, u32[]{:S(2)}, u32[]{:S(2)}) collective-permute-start(bf16[32,1024]{1,0:T(8,128)(2,1)S(1)} %get-tuple-element.50), channel_id=1, source_target_pairs={{0,12},{4,8},{8,4},{12,0},{1,13},{5,9},{9,5},{13,1},{2,14},{6,10},... | collective-permute-start | bytes 196616 | tf_op jit(solution)/shard_map/ppermute | solution.py:575
  69.3 1.9 %collective-permute-start.23 = (bf16[32,1024]{1,0:T(8,128)(2,1)S(1)}, bf16[32,1024]{1,0:T(8,128)(2,1)S(1)}, u32[]{:S(2)}, u32[]{:S(2)}) collective-permute-start(bf16[32,1024]{1,0:T(8,128)(2,1)S(1)} %get-tuple-element.50), channel_id=1, source_target_pairs={{0,4},{4,0},{8,12},{12,8},{1,5},{5,1},{9,13},{13,9},{2,6},{6,2},{1... | collective-permute-start | bytes 196616 | tf_op jit(solution)/shard_map/ppermute | solution.py:575
  71.2 3.1 %collective-permute-done.23 = bf16[32,1024]{1,0:T(8,128)(2,1)S(1)} collective-permute-done((bf16[32,1024]{1,0:T(8,128)(2,1)S(1)}, bf16[32,1024]{1,0:T(8,128)(2,1)S(1)}, u32[]{:S(2)}, u32[]{:S(2)}) %collective-permute-start.23) | collective-permute-done | bytes 65568 | tf_op jit(solution)/shard_map/ppermute | solution.py:575
  74.3 1.0 %collective-permute-done.24 = bf16[32,1024]{1,0:T(8,128)(2,1)S(1)} collective-permute-done((bf16[32,1024]{1,0:T(8,128)(2,1)S(1)}, bf16[32,1024]{1,0:T(8,128)(2,1)S(1)}, u32[]{:S(2)}, u32[]{:S(2)}) %collective-permute-start.24) | collective-permute-done | bytes 65568 | tf_op jit(solution)/shard_map/ppermute | solution.py:575
  75.3 1.4 %shard_map.136 = (bf16[2,32,896]{2,1,0:T(8,128)(2,1)S(1)}, bf16[2,32,896]{2,1,0:T(8,128)(2,1)S(1)}) custom-call(bf16[4,64,128]{2,1,0:T(8,128)(2,1)S(1)} %get-tuple-element.34.picker, bf16[128,1024]{1,0:T(8,128)(2,1)S(1)} %constant_dynamic-update-slice_fusion.residual.before, bf16[3584,1024]{1,0:T(8,128)(2,1)S(1)} %shard_map.134.refs_8_.down, ...), custom_call_target="tpu_custom_call" | custom-call | tf_op jit(solution)/shard_map/pallas_call | solution.py:393
  76.7 0.1 collective-permute-start.29
  76.8 1.5 %shard_map.137 = (bf16[2,32,896]{2,1,0:T(8,128)(2,1)S(1)}, bf16[2,32,896]{2,1,0:T(8,128)(2,1)S(1)}) custom-call(bf16[4,64,128]{2,1,0:T(8,128)(2,1)S(1)} %get-tuple-element.34.picker, bf16[128,1024]{1,0:T(8,128)(2,1)S(1)} %constant_dynamic-update-slice_fusion.residual.before, bf16[3584,1024]{1,0:T(8,128)(2,1)S(1)} %shard_map.134.refs_8_.down, ...), custom_call_target="tpu_custom_call" | custom-call | tf_op jit(solution)/shard_map/pallas_call | solution.py:393
  78.3 0.6 collective-permute-start.26
  78.9 0.8 collective-permute-start.30
  79.7 0.1 collective-permute-done.26
  79.9 1.2 %collective-permute-start.27 = (bf16[2,32,896]{2,1,0:T(8,128)(2,1)S(1)}, bf16[2,32,896]{2,1,0:T(8,128)(2,1)S(1)}, u32[]{:S(2)}, u32[]{:S(2)}) collective-permute-start(bf16[2,32,896]{2,1,0:T(8,128)(2,1)S(1)} %add_convert_fusion.5.before.mine), channel_id=1, source_target_pairs={{0,2},{2,0},{1,3},{3,1},{4,6},{6,4},{5,7},{7,5},{8,10},{10,8},{9,1... | collective-permute-start | bytes 344072 | tf_op jit(solution)/shard_map/ppermute | solution.py:16
  81.1 3.4 %shard_map.138 = (bf16[3584,1024]{1,0:T(8,128)(2,1)}, f32[8,128]{1,0:T(8,128)S(1)}) custom-call(bf16[3584,128]{1,0:T(8,128)(2,1)S(1)} %get-tuple-element.55.hidden, bf16[128,1024]{1,0:T(8,128)(2,1)S(1)} %constant_dynamic-update-slice_fusion.residual.before, bf16[2,32,896]{2,1,0:T(8,128)(2,1)S(1)} %add_convert_fusion.5.before.mine), custom_call_target="tpu_custom_call" | custom-call | flops 939524096 | bytes 7340032 | tf_op jit(solution)/shard_map/pallas_call | solution.py:446
  84.5 0.4 collective-permute-done.30.other
  85.0 0.2 shard_map.140.mine
  85.2 1.3 %collective-permute-done.27.other = bf16[2,32,896]{2,1,0:T(8,128)(2,1)S(1)} collective-permute-done((bf16[2,32,896]{2,1,0:T(8,128)(2,1)S(1)}, bf16[2,32,896]{2,1,0:T(8,128)(2,1)S(1)}, u32[]{:S(2)}, u32[]{:S(2)}) %collective-permute-start.27) | collective-permute-done | bytes 114720 | tf_op jit(solution)/shard_map/ppermute | solution.py:16
  86.5 0.2 shard_map.139.mine
  86.8 3.8 %shard_map.141 = (bf16[1024,3584]{1,0:T(8,128)(2,1)}, bf16[1024,3584]{1,0:T(8,128)(2,1)}) custom-call(bf16[4,64,128]{2,1,0:T(8,128)(2,1)S(1)} %get-tuple-element.34.picker, bf16[1024,128]{1,0:T(8,128)(2,1)S(1)} %get-tuple-element.48.before.tokens, bf16[2,2,32,896]{3,2,1,0:T(8,128)(2,1)S(1)} %shard_map.140.mine, ...), custom_call_target="tpu_custom_call" | custom-call | flops 939524096 | bytes 7340032 | tf_op jit(solution)/shard_map/pallas_call | solution.py:497
  90.6 3.8 %shard_map.142 = (bf16[1024,3584]{1,0:T(8,128)(2,1)}, bf16[1024,3584]{1,0:T(8,128)(2,1)}) custom-call(bf16[4,64,128]{2,1,0:T(8,128)(2,1)S(1)} %get-tuple-element.34.picker, bf16[1024,128]{1,0:T(8,128)(2,1)S(1)} %get-tuple-element.48.before.tokens, bf16[2,2,32,896]{3,2,1,0:T(8,128)(2,1)S(1)} %shard_map.139.mine, ...), custom_call_target="tpu_custom_call", output_to_operand_aliasing={{0}: (4, {}), {1}: (5, {})} | custom-call | flops 939524096 | bytes 7340032 | tf_op jit(solution)/shard_map/pallas_call | solution.py:497
  (53 shorter events, 1.0 us)
Async XLA Ops:
  0.6 11.7 %collective-permute-start = (bf16[32,1024]{1,0:T(8,128)(2,1)}, bf16[32,1024]{1,0:T(8,128)(2,1)S(1)}, u32[]{:S(2)}, u32[]{:S(2)}) collective-permute-start(bf16[32,1024]{1,0:T(8,128)(2,1)} %param.9), channel_id=1, source_target_pairs={{0,4},{4,0},{8,12},{12,8},{1,5},{5,1},{9,13},{13,9},{2,6},{6,2},{1... | collective-permute-start | bytes 196616 | tf_op jit(solution)/shard_map/ppermute | solution.py:575
  3.7 9.2 %collective-permute-start.2 = (bf16[32,1024]{1,0:T(8,128)(2,1)}, bf16[32,1024]{1,0:T(8,128)(2,1)S(1)}, u32[]{:S(2)}, u32[]{:S(2)}) collective-permute-start(bf16[32,1024]{1,0:T(8,128)(2,1)} %param.9), channel_id=1, source_target_pairs={{0,12},{4,8},{8,4},{12,0},{1,13},{5,9},{9,5},{13,1},{2,14},{6,10},... | collective-permute-start | bytes 196616 | tf_op jit(solution)/shard_map/ppermute | solution.py:575
  6.2 6.7 %collective-permute-start.1 = (bf16[32,1024]{1,0:T(8,128)(2,1)}, bf16[32,1024]{1,0:T(8,128)(2,1)S(1)}, u32[]{:S(2)}, u32[]{:S(2)}) collective-permute-start(bf16[32,1024]{1,0:T(8,128)(2,1)} %param.9), channel_id=1, source_target_pairs={{0,8},{4,12},{8,0},{12,4},{1,9},{5,13},{9,1},{13,5},{2,10},{6,14},... | collective-permute-start | bytes 196616 | tf_op jit(solution)/shard_map/ppermute | solution.py:575
  6.4 5.9 %copy-start = (bf16[32,1024]{1,0:T(8,128)(2,1)S(1)}, bf16[32,1024]{1,0:T(8,128)(2,1)}, u32[]{:S(2)}) copy-start(bf16[32,1024]{1,0:T(8,128)(2,1)} %param.9) | copy-start | bytes 196612
  14.6 2.3 %collective-permute-start.15 = (bf16[2,64,1792]{2,1,0:T(8,128)(2,1)S(1)}, bf16[2,64,1792]{2,1,0:T(8,128)(2,1)S(1)}, u32[]{:S(2)}, u32[]{:S(2)}) collective-permute-start(bf16[2,64,1792]{2,1,0:T(8,128)(2,1)S(1)} %get-tuple-element.47), channel_id=1, source_target_pairs={{0,1},{1,0},{2,3},{3,2},{4,5},{5,4},{6,7},{7,6},{8,9},{9,8},{10,11... | collective-permute-start | bytes 1376264 | tf_op jit(solution)/shard_map/ppermute | solution.py:16
  16.3 2.3 %collective-permute-start.3 = (bf16[2,64,1792]{2,1,0:T(8,128)(2,1)S(1)}, bf16[2,64,1792]{2,1,0:T(8,128)(2,1)S(1)}, u32[]{:S(2)}, u32[]{:S(2)}) collective-permute-start(bf16[2,64,1792]{2,1,0:T(8,128)(2,1)S(1)} %get-tuple-element.38), channel_id=1, source_target_pairs={{0,1},{1,0},{2,3},{3,2},{4,5},{5,4},{6,7},{7,6},{8,9},{9,8},{10,11... | collective-permute-start | bytes 1376264 | tf_op jit(solution)/shard_map/ppermute | solution.py:16
  17.0 14.3 %collective-permute-start.16 = (bf16[2,32,1792]{2,1,0:T(8,128)(2,1)S(1)}, bf16[2,32,1792]{2,1,0:T(8,128)(2,1)S(1)}, u32[]{:S(2)}, u32[]{:S(2)}) collective-permute-start(bf16[2,32,1792]{2,1,0:T(8,128)(2,1)S(1)} %slice.37), channel_id=1, source_target_pairs={{0,2},{2,0},{1,3},{3,1},{4,6},{6,4},{5,7},{7,5},{8,10},{10,8},{9,1... | collective-permute-start | bytes 688136 | tf_op jit(solution)/shard_map/ppermute | solution.py:16
  18.7 13.6 %collective-permute-start.10 = (bf16[2,32,1792]{2,1,0:T(8,128)(2,1)S(1)}, bf16[2,32,1792]{2,1,0:T(8,128)(2,1)S(1)}, u32[]{:S(2)}, u32[]{:S(2)}) collective-permute-start(bf16[2,32,1792]{2,1,0:T(8,128)(2,1)S(1)} %slice.33), channel_id=1, source_target_pairs={{0,2},{2,0},{1,3},{3,1},{4,6},{6,4},{5,7},{7,5},{8,10},{10,8},{9,1... | collective-permute-start | bytes 688136 | tf_op jit(solution)/shard_map/ppermute | solution.py:16
  23.8 10.9 %collective-permute-start.4 = (bf16[2,2,32,896]{3,2,1,0:T(8,128)(2,1)S(1)}, bf16[2,2,32,896]{3,2,1,0:T(8,128)(2,1)S(1)}, u32[]{:S(2)}, u32[]{:S(2)}) collective-permute-start(bf16[2,2,32,896]{3,2,1,0:T(8,128)(2,1)S(1)} %get-tuple-element.40), channel_id=1, source_target_pairs={{0,1},{1,0},{2,3},{3,2},{4,5},{5,4},{6,7},{7,6},{8,9},{9,8},{10,11... | collective-permute-start | bytes 688136 | tf_op jit(solution)/shard_map/ppermute | solution.py:16
  27.7 6.1 %collective-permute-start.7 = (bf16[2,2,32,896]{3,2,1,0:T(8,128)(2,1)S(1)}, bf16[2,2,32,896]{3,2,1,0:T(8,128)(2,1)S(1)}, u32[]{:S(2)}, u32[]{:S(2)}) collective-permute-start(bf16[2,2,32,896]{3,2,1,0:T(8,128)(2,1)S(1)} %get-tuple-element.44), channel_id=1, source_target_pairs={{0,1},{1,0},{2,3},{3,2},{4,5},{5,4},{6,7},{7,6},{8,9},{9,8},{10,11... | collective-permute-start | bytes 688136 | tf_op jit(solution)/shard_map/ppermute | solution.py:16
  31.5 6.1 %collective-permute-start.17 = (bf16[32,1792]{1,0:T(8,128)(2,1)S(1)}, bf16[32,1792]{1,0:T(8,128)(2,1)S(1)}, u32[]{:S(2)}, u32[]{:S(2)}) collective-permute-start(bf16[32,1792]{1,0:T(8,128)(2,1)S(1)} %fusion.1.refs_0_), channel_id=1, source_target_pairs={{0,2},{2,0},{1,3},{3,1},{4,6},{6,4},{5,7},{7,5},{8,10},{10,8},{9,1... | collective-permute-start | bytes 344072 | tf_op jit(solution)/shard_map/ppermute | solution.py:16
  32.5 7.5 %collective-permute-start.11 = (bf16[32,1792]{1,0:T(8,128)(2,1)S(1)}, bf16[32,1792]{1,0:T(8,128)(2,1)S(1)}, u32[]{:S(2)}, u32[]{:S(2)}) collective-permute-start(bf16[32,1792]{1,0:T(8,128)(2,1)S(1)} %fusion.3.refs_0_), channel_id=1, source_target_pairs={{0,2},{2,0},{1,3},{3,1},{4,6},{6,4},{5,7},{7,5},{8,10},{10,8},{9,1... | collective-permute-start | bytes 344072 | tf_op jit(solution)/shard_map/ppermute | solution.py:16
  33.9 11.1 %collective-permute-start.8 = (bf16[2,2,32,896]{3,2,1,0:T(8,128)(2,1)S(1)}, bf16[2,2,32,896]{3,2,1,0:T(8,128)(2,1)S(1)}, u32[]{:S(2)}, u32[]{:S(2)}) collective-permute-start(bf16[2,2,32,896]{3,2,1,0:T(8,128)(2,1)S(1)} %add_convert_fusion.2.mine), channel_id=1, source_target_pairs={{0,2},{2,0},{1,3},{3,1},{4,6},{6,4},{5,7},{7,5},{8,10},{10,8},{9,1... | collective-permute-start | bytes 688136 | tf_op jit(solution)/shard_map/ppermute | solution.py:16
  34.8 14.2 %collective-permute-start.5 = (bf16[2,2,32,896]{3,2,1,0:T(8,128)(2,1)S(1)}, bf16[2,2,32,896]{3,2,1,0:T(8,128)(2,1)S(1)}, u32[]{:S(2)}, u32[]{:S(2)}) collective-permute-start(bf16[2,2,32,896]{3,2,1,0:T(8,128)(2,1)S(1)} %add_convert_fusion.3.mine), channel_id=1, source_target_pairs={{0,2},{2,0},{1,3},{3,1},{4,6},{6,4},{5,7},{7,5},{8,10},{10,8},{9,1... | collective-permute-start | bytes 688136 | tf_op jit(solution)/shard_map/ppermute | solution.py:16
  37.6 11.6 %collective-permute-start.18 = (bf16[64,1792]{1,0:T(8,128)(2,1)S(1)}, bf16[64,1792]{1,0:T(8,128)(2,1)S(1)}, u32[]{:S(2)}, u32[]{:S(2)}) collective-permute-start(bf16[64,1792]{1,0:T(8,128)(2,1)S(1)} %shard_map.131.refs_0_), channel_id=1, source_target_pairs={{0,1},{1,0},{2,3},{3,2},{4,5},{5,4},{6,7},{7,6},{8,9},{9,8},{10,11... | collective-permute-start | bytes 688136 | tf_op jit(solution)/shard_map/ppermute | solution.py:16
  40.0 9.1 %collective-permute-start.19 = (bf16[64,1792]{1,0:T(8,128)(2,1)S(1)}, bf16[64,1792]{1,0:T(8,128)(2,1)S(1)}, u32[]{:S(2)}, u32[]{:S(2)}) collective-permute-start(bf16[64,1792]{1,0:T(8,128)(2,1)S(1)} %shard_map.128.before.refs_2_), channel_id=1, source_target_pairs={{0,1},{1,0},{2,3},{3,2},{4,5},{5,4},{6,7},{7,6},{8,9},{9,8},{10,11... | collective-permute-start | bytes 688136 | tf_op jit(solution)/shard_map/ppermute | solution.py:16
  45.0 10.4 %collective-permute-start.9 = (bf16[2,32,896]{2,1,0:T(8,128)(2,1)S(1)}, bf16[2,32,896]{2,1,0:T(8,128)(2,1)S(1)}, u32[]{:S(2)}, u32[]{:S(2)}) collective-permute-start(bf16[2,32,896]{2,1,0:T(8,128)(2,1)S(1)} %get-tuple-element.45), channel_id=1, source_target_pairs={{0,1},{1,0},{2,3},{3,2},{4,5},{5,4},{6,7},{7,6},{8,9},{9,8},{10,11... | collective-permute-start | bytes 344072 | tf_op jit(solution)/shard_map/ppermute | solution.py:16
  49.1 6.3 %collective-permute-start.6 = (bf16[2,32,896]{2,1,0:T(8,128)(2,1)S(1)}, bf16[2,32,896]{2,1,0:T(8,128)(2,1)S(1)}, u32[]{:S(2)}, u32[]{:S(2)}) collective-permute-start(bf16[2,32,896]{2,1,0:T(8,128)(2,1)S(1)} %get-tuple-element.42), channel_id=1, source_target_pairs={{0,1},{1,0},{2,3},{3,2},{4,5},{5,4},{6,7},{7,6},{8,9},{9,8},{10,11... | collective-permute-start | bytes 344072 | tf_op jit(solution)/shard_map/ppermute | solution.py:16
  51.0 8.6 %collective-permute-start.22 = (bf16[32,1024]{1,0:T(8,128)(2,1)S(1)}, bf16[32,1024]{1,0:T(8,128)(2,1)S(1)}, u32[]{:S(2)}, u32[]{:S(2)}) collective-permute-start(bf16[32,1024]{1,0:T(8,128)(2,1)S(1)} %get-tuple-element.64), channel_id=1, source_target_pairs={{0,12},{4,8},{8,4},{12,0},{1,13},{5,9},{9,5},{13,1},{2,14},{6,10},... | collective-permute-start | bytes 196616 | tf_op jit(solution)/shard_map/ppermute | solution.py:575
  53.5 11.6 %collective-permute-start.21 = (bf16[32,1024]{1,0:T(8,128)(2,1)S(1)}, bf16[32,1024]{1,0:T(8,128)(2,1)S(1)}, u32[]{:S(2)}, u32[]{:S(2)}) collective-permute-start(bf16[32,1024]{1,0:T(8,128)(2,1)S(1)} %get-tuple-element.65), channel_id=1, source_target_pairs={{0,8},{4,12},{8,0},{12,4},{1,9},{5,13},{9,1},{13,5},{2,10},{6,14},... | collective-permute-start | bytes 196616 | tf_op jit(solution)/shard_map/ppermute | solution.py:575
  53.8 11.3 %collective-permute-start.20 = (bf16[32,1024]{1,0:T(8,128)(2,1)S(1)}, bf16[32,1024]{1,0:T(8,128)(2,1)S(1)}, u32[]{:S(2)}, u32[]{:S(2)}) collective-permute-start(bf16[32,1024]{1,0:T(8,128)(2,1)S(1)} %get-tuple-element.66), channel_id=1, source_target_pairs={{0,4},{4,0},{8,12},{12,8},{1,5},{5,1},{9,13},{13,9},{2,6},{6,2},{1... | collective-permute-start | bytes 196616 | tf_op jit(solution)/shard_map/ppermute | solution.py:575
  57.1 8.0 %collective-permute-start.14 = (bf16[32,1024]{1,0:T(8,128)(2,1)S(1)}, bf16[32,1024]{1,0:T(8,128)(2,1)S(1)}, u32[]{:S(2)}, u32[]{:S(2)}) collective-permute-start(bf16[32,1024]{1,0:T(8,128)(2,1)S(1)} %get-tuple-element.68), channel_id=1, source_target_pairs={{0,12},{4,8},{8,4},{12,0},{1,13},{5,9},{9,5},{13,1},{2,14},{6,10},... | collective-permute-start | bytes 196616 | tf_op jit(solution)/shard_map/ppermute | solution.py:575
  59.6 6.5 %collective-permute-start.13 = (bf16[32,1024]{1,0:T(8,128)(2,1)S(1)}, bf16[32,1024]{1,0:T(8,128)(2,1)S(1)}, u32[]{:S(2)}, u32[]{:S(2)}) collective-permute-start(bf16[32,1024]{1,0:T(8,128)(2,1)S(1)} %get-tuple-element.69), channel_id=1, source_target_pairs={{0,8},{4,12},{8,0},{12,4},{1,9},{5,13},{9,1},{13,5},{2,10},{6,14},... | collective-permute-start | bytes 196616 | tf_op jit(solution)/shard_map/ppermute | solution.py:575
  59.6 6.5 %collective-permute-start.12 = (bf16[32,1024]{1,0:T(8,128)(2,1)S(1)}, bf16[32,1024]{1,0:T(8,128)(2,1)S(1)}, u32[]{:S(2)}, u32[]{:S(2)}) collective-permute-start(bf16[32,1024]{1,0:T(8,128)(2,1)S(1)} %get-tuple-element.70), channel_id=1, source_target_pairs={{0,4},{4,0},{8,12},{12,8},{1,5},{5,1},{9,13},{13,9},{2,6},{6,2},{1... | collective-permute-start | bytes 196616 | tf_op jit(solution)/shard_map/ppermute | solution.py:575
  66.8 8.5 %collective-permute-start.25 = (bf16[32,1024]{1,0:T(8,128)(2,1)S(1)}, bf16[32,1024]{1,0:T(8,128)(2,1)S(1)}, u32[]{:S(2)}, u32[]{:S(2)}) collective-permute-start(bf16[32,1024]{1,0:T(8,128)(2,1)S(1)} %get-tuple-element.50), channel_id=1, source_target_pairs={{0,12},{4,8},{8,4},{12,0},{1,13},{5,9},{9,5},{13,1},{2,14},{6,10},... | collective-permute-start | bytes 196616 | tf_op jit(solution)/shard_map/ppermute | solution.py:575
  69.2 6.0 %collective-permute-start.24 = (bf16[32,1024]{1,0:T(8,128)(2,1)S(1)}, bf16[32,1024]{1,0:T(8,128)(2,1)S(1)}, u32[]{:S(2)}, u32[]{:S(2)}) collective-permute-start(bf16[32,1024]{1,0:T(8,128)(2,1)S(1)} %get-tuple-element.50), channel_id=1, source_target_pairs={{0,8},{4,12},{8,0},{12,4},{1,9},{5,13},{9,1},{13,5},{2,10},{6,14},... | collective-permute-start | bytes 196616 | tf_op jit(solution)/shard_map/ppermute | solution.py:575
  69.3 5.0 %collective-permute-start.23 = (bf16[32,1024]{1,0:T(8,128)(2,1)S(1)}, bf16[32,1024]{1,0:T(8,128)(2,1)S(1)}, u32[]{:S(2)}, u32[]{:S(2)}) collective-permute-start(bf16[32,1024]{1,0:T(8,128)(2,1)S(1)} %get-tuple-element.50), channel_id=1, source_target_pairs={{0,4},{4,0},{8,12},{12,8},{1,5},{5,1},{9,13},{13,9},{2,6},{6,2},{1... | collective-permute-start | bytes 196616 | tf_op jit(solution)/shard_map/ppermute | solution.py:575
  76.7 2.2 %collective-permute-start.29 = (bf16[2,32,896]{2,1,0:T(8,128)(2,1)S(1)}, bf16[2,32,896]{2,1,0:T(8,128)(2,1)S(1)}, u32[]{:S(2)}, u32[]{:S(2)}) collective-permute-start(bf16[2,32,896]{2,1,0:T(8,128)(2,1)S(1)} %get-tuple-element.57), channel_id=1, source_target_pairs={{0,1},{1,0},{2,3},{3,2},{4,5},{5,4},{6,7},{7,6},{8,9},{9,8},{10,11... | collective-permute-start | bytes 344072 | tf_op jit(solution)/shard_map/ppermute | solution.py:16
  78.3 1.5 %collective-permute-start.26 = (bf16[2,32,896]{2,1,0:T(8,128)(2,1)S(1)}, bf16[2,32,896]{2,1,0:T(8,128)(2,1)S(1)}, u32[]{:S(2)}, u32[]{:S(2)}) collective-permute-start(bf16[2,32,896]{2,1,0:T(8,128)(2,1)S(1)} %get-tuple-element.53), channel_id=1, source_target_pairs={{0,1},{1,0},{2,3},{3,2},{4,5},{5,4},{6,7},{7,6},{8,9},{9,8},{10,11... | collective-permute-start | bytes 344072 | tf_op jit(solution)/shard_map/ppermute | solution.py:16
  78.9 6.1 %collective-permute-start.30 = (bf16[2,32,896]{2,1,0:T(8,128)(2,1)S(1)}, bf16[2,32,896]{2,1,0:T(8,128)(2,1)S(1)}, u32[]{:S(2)}, u32[]{:S(2)}) collective-permute-start(bf16[2,32,896]{2,1,0:T(8,128)(2,1)S(1)} %add_convert_fusion.4.mine), channel_id=1, source_target_pairs={{0,2},{2,0},{1,3},{3,1},{4,6},{6,4},{5,7},{7,5},{8,10},{10,8},{9,1... | collective-permute-start | bytes 344072 | tf_op jit(solution)/shard_map/ppermute | solution.py:16
  79.9 6.6 %collective-permute-start.27 = (bf16[2,32,896]{2,1,0:T(8,128)(2,1)S(1)}, bf16[2,32,896]{2,1,0:T(8,128)(2,1)S(1)}, u32[]{:S(2)}, u32[]{:S(2)}) collective-permute-start(bf16[2,32,896]{2,1,0:T(8,128)(2,1)S(1)} %add_convert_fusion.5.before.mine), channel_id=1, source_target_pairs={{0,2},{2,0},{1,3},{3,1},{4,6},{6,4},{5,7},{7,5},{8,10},{10,8},{9,1... | collective-permute-start | bytes 344072 | tf_op jit(solution)/shard_map/ppermute | solution.py:16
  85.1 1.6 %collective-permute-start.31 = (bf16[2,2,32,896]{3,2,1,0:T(8,128)(2,1)S(1)}, bf16[2,2,32,896]{3,2,1,0:T(8,128)(2,1)S(1)}, u32[]{:S(2)}, u32[]{:S(2)}) collective-permute-start(bf16[2,2,32,896]{3,2,1,0:T(8,128)(2,1)S(1)} %shard_map.140.mine), channel_id=1, source_target_pairs={{0,1},{1,0},{2,3},{3,2},{4,5},{5,4},{6,7},{7,6},{8,9},{9,8},{10,11... | collective-permute-start | bytes 688136 | tf_op jit(solution)/shard_map/ppermute | solution.py:16
  86.7 3.9 %collective-permute-start.28 = (bf16[2,2,32,896]{3,2,1,0:T(8,128)(2,1)S(1)}, bf16[2,2,32,896]{3,2,1,0:T(8,128)(2,1)S(1)}, u32[]{:S(2)}, u32[]{:S(2)}) collective-permute-start(bf16[2,2,32,896]{3,2,1,0:T(8,128)(2,1)S(1)} %shard_map.139.mine), channel_id=1, source_target_pairs={{0,1},{1,0},{2,3},{3,2},{4,5},{5,4},{6,7},{7,6},{8,9},{9,8},{10,11... | collective-permute-start | bytes 688136 | tf_op jit(solution)/shard_map/ppermute | solution.py:16

commit v5 on v4

--- a/solution.py
+++ b/solution.py
@@ -142,43 +142,6 @@
     )(place, far(routes), far(shares), far(gate), far(up))
 
 
-def load_kernel(source, before, out, sems):
-    for copy in load_start(((source, out),), sems, 8):
-        copy.wait()
-
-
-def load(source, before):
-    return pl.pallas_call(
-        load_kernel,
-        in_specs=[in_hbm(), anywhere()],
-        out_specs=whole(),
-        out_shape=pltpu.VMEM(source.shape, source.dtype),
-        scratch_shapes=[pltpu.SemaphoreType.DMA((1, 8))],
-        compiler_params=pltpu.CompilerParams(vmem_limit_bytes=4 * 1024 * 1024),
-        cost_estimate=pl.CostEstimate(
-            flops=0, bytes_accessed=2 * source.size, transcendentals=0
-        ),
-    )(far(source), before)
-
-
-def pair_kernel(*refs):
-    out = refs[-1]
-    rows = out.shape[0] // (len(refs) - 2)
-    for i, value in enumerate(refs[:-2]):
-        out[i * rows : (i + 1) * rows, :] = value[...]
-
-
-def pair(values, before):
-    rows, width = values[0].shape
-    return pl.pallas_call(
-        pair_kernel,
-        in_specs=[whole()] * len(values) + [anywhere()],
-        out_specs=whole(),
-        out_shape=jax.ShapeDtypeStruct((rows * len(values), width), BF),
-        compiler_params=pltpu.CompilerParams(vmem_limit_bytes=4 * 1024 * 1024),
-    )(*values, before)
-
-
 def residual_kernel(ranks, *refs):
     student = refs[0][...].astype(F32)
     target = refs[ranks][...].astype(F32)
@@ -319,7 +282,7 @@
     dp, pipe = place[1], place[2]
     rows = out.shape[0] // (dps * pipes)
     at = 0
-    for i in range((len(refs) - 2) // 2):
+    for i in range((len(refs) - 1) // 2):
         size = refs[2 * i].shape[1]
         for j1 in range(pipes):
             for j0 in range(dps):
@@ -329,18 +292,18 @@
         at += size
 
 
-def join(place, parts, before, dps, pipes):
+def join(place, parts, dps, pipes):
     assert pipes == 2
     flat = [value for pair in parts for value in pair]
     rows = flat[0].shape[0] * pipes
     width = sum(pair[0].shape[1] for pair in parts)
     return pl.pallas_call(
         functools.partial(join_kernel, dps, pipes),
-        in_specs=[scalars()] + [whole()] * len(flat) + [anywhere()],
+        in_specs=[scalars()] + [whole()] * len(flat),
         out_specs=whole(),
         out_shape=jax.ShapeDtypeStruct((rows, width), BF),
         compiler_params=pltpu.CompilerParams(vmem_limit_bytes=8 * 1024 * 1024),
-    )(place, *flat, before)
+    )(place, *flat)
 
 
 def spread_kernel(picker, hidden, out):
@@ -426,42 +389,46 @@
     )(mine, other, pre, weight, before)
 
 
-def down_grad_kernel(hidden, residual, before, out, done, held, sems):
+def down_grad_kernel(first, hidden, residual, before, *rest):
+    out, done, held, sems = rest[-4:]
     tiles = sems.shape[0]
-    rows = hidden.shape[0] // tiles
+    rows = H // 2
     copies = []
     for i in range(tiles):
-        part = pl.ds(i * rows, rows)
-        held[part, :] = dot(hidden[part, :], residual[...]).astype(BF)
-        copies.append(pltpu.make_async_copy(held.at[part], out.at[part], sems.at[i]))
+        here = pl.ds(i * rows, rows)
+        part = pl.ds(first * H + i * rows, rows)
+        held[here, :] = dot(hidden[part, :], residual[...]).astype(BF)
+        copies.append(pltpu.make_async_copy(held.at[here], out.at[part], sems.at[i]))
         copies[-1].start()
     done[...] = jnp.zeros_like(done)
     for copy in copies:
         copy.wait()
 
 
-def down_grad(hidden, residual, before):
+def down_grad(hidden, residual, before, first, count, so_far):
     rows, token_count = hidden.shape
     width = residual.shape[1]
-    return pl.pallas_call(
-        down_grad_kernel,
-        in_specs=[whole(), whole(), anywhere()],
+    extra = () if so_far is None else (so_far,)
+    return pl.pallas_call(
+        functools.partial(down_grad_kernel, first),
+        in_specs=[whole(), whole(), anywhere()] + [in_hbm()] * len(extra),
         out_specs=(in_hbm(), whole()),
         out_shape=(
             jax.ShapeDtypeStruct((rows, width), BF),
             jax.ShapeDtypeStruct((8, 128), F32),
         ),
         scratch_shapes=[
-            pltpu.VMEM((rows, width), BF),
-            pltpu.SemaphoreType.DMA((rows // (H // 2),)),
+            pltpu.VMEM((count * H, width), BF),
+            pltpu.SemaphoreType.DMA((2 * count,)),
         ],
+        input_output_aliases={3: 0} if extra else {},
         compiler_params=pltpu.CompilerParams(vmem_limit_bytes=16 * 1024 * 1024),
         cost_estimate=pl.CostEstimate(
-            flops=2 * rows * width * token_count,
-            bytes_accessed=2 * rows * width,
+            flops=2 * count * H * width * token_count,
+            bytes_accessed=2 * count * H * width,
             transcendentals=0,
         ),
-    )(hidden, residual, before)
+    )(hidden, residual, before, *[far(value) for value in extra])
 
 
 def input_grad_kernel(first, picker, tokens, mine, theirs, *rest):
@@ -615,17 +582,14 @@
         keep, send = expert_pre(picker, base, expert_gate, expert_up, last, first, group)
         last = keep
         parts.append((keep, shift(send, "pipe", pipes, 1)))
-    teacher_near = load(teacher_down, last)
-
     hiddens = []
     for half in halves:
         total = scatter_dp(half, dps)
         hidden = (jax.nn.silu(total[0]) * total[1]).astype(BF)
-        hidden = pair(gather_dp_parts(hidden, dps), teacher_near)
+        hidden = jnp.concatenate(gather_dp_parts(hidden, dps), axis=0)
         hiddens.append((hidden, shift(hidden, "pipe", pipes, 1)))
-    expert_near = load(expert_down, hiddens[-1][0])
-    hidden = join(place, hiddens, expert_near, dps, pipes)
-    target = to_owners(jnp.dot(hidden, teacher_near, preferred_element_type=F32).astype(BF))
+    hidden = join(place, hiddens, dps, pipes)
+    target = to_owners(jnp.dot(hidden, teacher_down, preferred_element_type=F32).astype(BF))
 
     pre, weighted = [], []
     for first, (keep, theirs) in zip(firsts, parts):
@@ -636,25 +600,28 @@
     weighted = jnp.concatenate(weighted, axis=0)
 
     dense = spread(picker, weighted)
-    product = jnp.dot(dense, expert_near, preferred_element_type=F32).astype(BF)
+    product = jnp.dot(dense, expert_down, preferred_element_type=F32).astype(BF)
     student = to_owners(product)
     dense_flipped, base_flipped = flip(dense, base, product)
-    expert_near = load(expert_down, base_flipped)
-    student_out, residual = residual_of(student, target, (expert_near,))
+    student_out, residual = residual_of(student, target, (base_flipped,))
     residual = gather_tokens(residual)
 
     sums = []
     last = residual
     for first in firsts:
-        keep, send = hidden_grad_parts(picker, residual, expert_near, last, first, group)
+        keep, send = hidden_grad_parts(picker, residual, expert_down, last, first, group)
         last = keep
         sums.append(add(keep, shift(send, "pipe", pipes, 1)))
     pairs = [exchange_dp(value, dps) for value in sums]
-    grad_down, done = down_grad(dense_flipped, residual, sums[-1])
     grads = None
+    grad_down = None
+    last = sums[-1]
+    activations = []
     for i, first in enumerate(firsts):
-        mine = hidden_grad_act(*pairs[i], dps == 2, pre[i], slot_weight, done, first)
-        theirs = shift(mine, "pipe", pipes, 1)
+        grad_down, done = down_grad(dense_flipped, residual, last, first, group, grad_down)
+        last = hidden_grad_act(*pairs[i], dps == 2, pre[i], slot_weight, done, first)
+        activations.append((last, shift(last, "pipe", pipes, 1)))
+    for (mine, theirs), first in zip(activations, firsts):
         grads = input_grads(picker, base_flipped, mine, theirs, first, grads)
     return (student_out, grads[0], grads[1], grad_down)
 

time: 94.8 us -> 93.2 us (0.983)
  Pallas kernels: 42.8 us -> 34.4 us
  waiting for transfers between devices: 16.8 us -> 22.8 us
    pallas_call x6 -> x2, Pallas kernels: 13 us -> 4.5 us  [down_grad(): pl.pallas_call(functools.partial(down_grad_kernel, first), in_specs=[whol...]
    ppermute x12, waiting for transfers between devices: 5.56 us -> 8.71 us  [to_partner(): return lax.ppermute(value, 'expert', [(i, i ^ s) for i in range(ranks)])]
    ppermute x20, waiting for transfers between devices: 11.2 us -> 14.1 us  [shift(): lax.ppermute(value, axis, [(i, (i + by) % count) for i in range(count)])]
  transfers between devices with their start and end apart: 32 -> 32, of which waited for: 11 -> 12; matrix products, arithmetic and copies ran while one was open for 3% -> 3% of each run, Pallas kernels for 37% -> 29%
where the time goes in v5:
time: 93.2 us; the launch traced here: 93.1 us
  Pallas kernels  34.4 us (37%)
  starting transfers between devices  31.3 us (34%)
  waiting for transfers between devices  22.8 us (24%)
  matrix products  2.24 us (2%)
  between operations  1.31 us (1%)
    ppermute x12, starting transfers between devices, to_partner(): return lax.ppermute(value, 'expert', [(i, i ^ s) for i in range(ranks)])  19 us
    ppermute x20, waiting for transfers between devices, shift(): lax.ppermute(value, axis, [(i, (i + by) % count) for i in range(count)])  14.1 us
    ppermute x20, starting transfers between devices, shift(): lax.ppermute(value, axis, [(i, (i + by) % count) for i in range(count)])  12.3 us
    ppermute x12, waiting for transfers between devices, to_partner(): return lax.ppermute(value, 'expert', [(i, i ^ s) for i in range(ranks)])  8.71 us
    pallas_call x2, Pallas kernels, input_grads(): pl.pallas_call(functools.partial(input_grad_kernel, first), in_specs=[who...  7.67 us
    pallas_call x2, Pallas kernels, expert_pre(): pl.pallas_call(functools.partial(expert_kernel, first), in_specs=[whole()...  7.59 us
    pallas_call x1, Pallas kernels, prepare(): pl.pallas_call(functools.partial(prepare_kernel, ranks, capacity, dps, pi...  5.89 us
    pallas_call x2, Pallas kernels, down_grad(): pl.pallas_call(functools.partial(down_grad_kernel, first), in_specs=[whol...  4.5 us
  transfers between devices with their start and end apart: 32, of which 12 were waited for; matrix products, arithmetic and copies ran while one was open for 3% of the time, Pallas kernels for 29%

profile of v5, /device:TPU:0, one launch (start us, length us, event | category | flops | bytes accessed | tf_op | source)
XLA Modules:
  0.0 93.1 jit_solution(7047606502937508477)
XLA Ops:
  0.6 3.1 %collective-permute-start = (bf16[32,1024]{1,0:T(8,128)(2,1)}, bf16[32,1024]{1,0:T(8,128)(2,1)S(1)}, u32[]{:S(2)}, u32[]{:S(2)}) collective-permute-start(bf16[32,1024]{1,0:T(8,128)(2,1)} %param.9), channel_id=1, source_target_pairs={{0,4},{4,0},{8,12},{12,8},{1,5},{5,1},{9,13},{13,9},{2,6},{6,2},{1... | collective-permute-start | bytes 196616 | tf_op jit(solution)/shard_map/ppermute | solution.py:542
  3.7 2.5 %collective-permute-start.2 = (bf16[32,1024]{1,0:T(8,128)(2,1)}, bf16[32,1024]{1,0:T(8,128)(2,1)S(1)}, u32[]{:S(2)}, u32[]{:S(2)}) collective-permute-start(bf16[32,1024]{1,0:T(8,128)(2,1)} %param.9), channel_id=1, source_target_pairs={{0,12},{4,8},{8,4},{12,0},{1,13},{5,9},{9,5},{13,1},{2,14},{6,10},... | collective-permute-start | bytes 196616 | tf_op jit(solution)/shard_map/ppermute | solution.py:542
  6.2 0.1 collective-permute-start.1
  6.3 0.1 pad_add_fusion.place
  6.4 5.9 %shard_map.120 = (bf16[4,64,128]{2,1,0:T(8,128)(2,1)S(1)}, f32[4,64,1]{2,1,0:T(8,128)S(1)}, bf16[1024,3584]{1,0:T(8,128)(2,1)S(1)}, bf16[1024,3584]{1,0:T(8,128)(2,1)S(1)}) custom-call(s32[3]{0:T(128)S(1)} %pad_add_fusion.place, s32[4,128]{1,0:T(4,128)} %bitcast.33, f32[4,128]{1,0:T(4,128)} %bitcast.34, bf16[1024,3584]{1,0:T(8,128)(2,1)} %gate.3, ...), custom_call_target="tpu_custom_call" | custom-call | bytes 14680064 | tf_op jit(solution)/shard_map/pallas_call | solution.py:122
  12.4 0.5 collective-permute-done.1
  12.9 1.7 %shard_map.127 = (bf16[2,64,1792]{2,1,0:T(8,128)(2,1)S(1)}, bf16[2,64,1792]{2,1,0:T(8,128)(2,1)S(1)}) custom-call(s32[3]{0:T(128)S(1)} %pad_add_fusion.place, bf16[128,1024]{1,0:T(8,128)(2,1)S(1)} %constant_dynamic-update-slice_fusion.4.tokens, bf16[1024,3584]{1,0:T(8,128)(2,1)S(1)} %get-tuple-element.37.gate, bf16[1024,3584]{1,0:T(8,128)(2,1)S(1)} %get-tuple-element.38.up), custom_call_target="tpu_custom_call" | custom-call | flops 939524096 | bytes 7340032 | tf_op jit(solution)/shard_map/pallas_call | solution.py:192
  14.6 0.1 collective-permute-start.13
  14.7 1.7 %shard_map.121 = (bf16[2,64,1792]{2,1,0:T(8,128)(2,1)S(1)}, bf16[2,64,1792]{2,1,0:T(8,128)(2,1)S(1)}) custom-call(s32[3]{0:T(128)S(1)} %pad_add_fusion.place, bf16[128,1024]{1,0:T(8,128)(2,1)S(1)} %constant_dynamic-update-slice_fusion.4.tokens, bf16[1024,3584]{1,0:T(8,128)(2,1)S(1)} %get-tuple-element.37.gate, bf16[1024,3584]{1,0:T(8,128)(2,1)S(1)} %get-tuple-element.38.up), custom_call_target="tpu_custom_call" | custom-call | flops 939524096 | bytes 7340032 | tf_op jit(solution)/shard_map/pallas_call | solution.py:192
  16.3 0.6 collective-permute-start.3
  16.9 0.1 add_convert_fusion
  17.0 1.6 %collective-permute-start.14 = (bf16[2,32,1792]{2,1,0:T(8,128)(2,1)S(1)}, bf16[2,32,1792]{2,1,0:T(8,128)(2,1)S(1)}, u32[]{:S(2)}, u32[]{:S(2)}) collective-permute-start(bf16[2,32,1792]{2,1,0:T(8,128)(2,1)S(1)} %slice.33), channel_id=1, source_target_pairs={{0,2},{2,0},{1,3},{3,1},{4,6},{6,4},{5,7},{7,5},{8,10},{10,8},{9,1... | collective-permute-start | bytes 688136 | tf_op jit(solution)/shard_map/ppermute | solution.py:16
  18.6 0.1 add_convert_fusion.1.before
  18.7 1.3 %collective-permute-start.17 = (bf16[2,32,1792]{2,1,0:T(8,128)(2,1)S(1)}, bf16[2,32,1792]{2,1,0:T(8,128)(2,1)S(1)}, u32[]{:S(2)}, u32[]{:S(2)}) collective-permute-start(bf16[2,32,1792]{2,1,0:T(8,128)(2,1)S(1)} %slice.37), channel_id=1, source_target_pairs={{0,2},{2,0},{1,3},{3,1},{4,6},{6,4},{5,7},{7,5},{8,10},{10,8},{9,1... | collective-permute-start | bytes 688136 | tf_op jit(solution)/shard_map/ppermute | solution.py:16
  20.1 3.7 %shard_map.122 = (bf16[2,2,32,896]{3,2,1,0:T(8,128)(2,1)S(1)}, bf16[2,2,32,896]{3,2,1,0:T(8,128)(2,1)S(1)}) custom-call(bf16[4,64,128]{2,1,0:T(8,128)(2,1)S(1)} %get-tuple-element.36.picker, bf16[128,1024]{1,0:T(8,128)(2,1)S(1)} %constant_dynamic-update-slice_fusion.4.tokens, bf16[1024,3584]{1,0:T(8,128)(2,1)} %gate.5, bf16[1024,3584]{1,0:T(8,128)(2,1)} %up.5, ...), custom_call_target="tpu_custom_call" | custom-call | flops 469762048 | bytes 7340032 | tf_op jit(solution)/shard_map/pallas_call | solution.py:233
  23.8 0.1 collective-permute-start.4
  23.9 3.9 %shard_map.124 = (bf16[2,2,32,896]{3,2,1,0:T(8,128)(2,1)S(1)}, bf16[2,2,32,896]{3,2,1,0:T(8,128)(2,1)S(1)}) custom-call(bf16[4,64,128]{2,1,0:T(8,128)(2,1)S(1)} %get-tuple-element.36.picker, bf16[128,1024]{1,0:T(8,128)(2,1)S(1)} %constant_dynamic-update-slice_fusion.4.tokens, bf16[1024,3584]{1,0:T(8,128)(2,1)} %gate.5, bf16[1024,3584]{1,0:T(8,128)(2,1)} %up.5, ...), custom_call_target="tpu_custom_call" | custom-call | flops 469762048 | bytes 7340032 | tf_op jit(solution)/shard_map/pallas_call | solution.py:233
  27.8 0.5 collective-permute-start.7
  28.4 0.1 fusion.3
  28.4 0.8 collective-permute-start.15
  29.3 0.3 collective-permute-done.17
  29.6 0.1 fusion.1
  29.7 1.6 %collective-permute-start.18 = (bf16[32,1792]{1,0:T(8,128)(2,1)S(1)}, bf16[32,1792]{1,0:T(8,128)(2,1)S(1)}, u32[]{:S(2)}, u32[]{:S(2)}) collective-permute-start(bf16[32,1792]{1,0:T(8,128)(2,1)S(1)} %fusion.1), channel_id=1, source_target_pairs={{0,2},{2,0},{1,3},{3,1},{4,6},{6,4},{5,7},{7,5},{8,10},{10,8},{9,1... | collective-permute-start | bytes 344072 | tf_op jit(solution)/shard_map/ppermute | solution.py:16
  31.3 0.6 collective-permute-start.8
  32.0 1.6 %collective-permute-start.5 = (bf16[2,2,32,896]{3,2,1,0:T(8,128)(2,1)S(1)}, bf16[2,2,32,896]{3,2,1,0:T(8,128)(2,1)S(1)}, u32[]{:S(2)}, u32[]{:S(2)}) collective-permute-start(bf16[2,2,32,896]{3,2,1,0:T(8,128)(2,1)S(1)} %add_convert_fusion.3.mine), channel_id=1, source_target_pairs={{0,2},{2,0},{1,3},{3,1},{4,6},{6,4},{5,7},{7,5},{8,10},{10,8},{9,1... | collective-permute-start | bytes 688136 | tf_op jit(solution)/shard_map/ppermute | solution.py:16
  33.6 1.0 %collective-permute-done.15 = bf16[32,1792]{1,0:T(8,128)(2,1)S(1)} collective-permute-done((bf16[32,1792]{1,0:T(8,128)(2,1)S(1)}, bf16[32,1792]{1,0:T(8,128)(2,1)S(1)}, u32[]{:S(2)}, u32[]{:S(2)}) %collective-permute-start.15) | collective-permute-done | bytes 114720 | tf_op jit(solution)/shard_map/ppermute | solution.py:16
  34.6 2.4 %collective-permute-done.18 = bf16[32,1792]{1,0:T(8,128)(2,1)S(1)} collective-permute-done((bf16[32,1792]{1,0:T(8,128)(2,1)S(1)}, bf16[32,1792]{1,0:T(8,128)(2,1)S(1)}, u32[]{:S(2)}, u32[]{:S(2)}) %collective-permute-start.18) | collective-permute-done | bytes 114720 | tf_op jit(solution)/shard_map/ppermute | solution.py:16
  37.0 0.1 collective-permute-start.19
  37.1 4.8 %collective-permute-done.8.other = bf16[2,2,32,896]{3,2,1,0:T(8,128)(2,1)S(1)} collective-permute-done((bf16[2,2,32,896]{3,2,1,0:T(8,128)(2,1)S(1)}, bf16[2,2,32,896]{3,2,1,0:T(8,128)(2,1)S(1)}, u32[]{:S(2)}, u32[]{:S(2)}) %collective-permute-start.8) | collective-permute-done | bytes 229408 | tf_op jit(solution)/shard_map/ppermute | solution.py:16
  41.9 0.1 shard_map.125
  42.1 3.9 %collective-permute-done.5.other = bf16[2,2,32,896]{3,2,1,0:T(8,128)(2,1)S(1)} collective-permute-done((bf16[2,2,32,896]{3,2,1,0:T(8,128)(2,1)S(1)}, bf16[2,2,32,896]{3,2,1,0:T(8,128)(2,1)S(1)}, u32[]{:S(2)}, u32[]{:S(2)}) %collective-permute-start.5) | collective-permute-done | bytes 229408 | tf_op jit(solution)/shard_map/ppermute | solution.py:16
  45.9 0.1 shard_map.123
  46.0 0.1 collective-permute-start.6
  46.1 0.6 shard_map.128
  46.8 1.1 %convolution_convert_fusion = bf16[128,1024]{1,0:T(8,128)(2,1)S(1)} fusion(bf16[128,3584]{1,0:T(8,128)(2,1)S(1)} %shard_map.128, bf16[3584,1024]{1,0:T(8,128)(2,1)S(1)} %bitcast.32), kind=kOutput, calls=%fused_computation | convolution fusion | flops 939655168 | bytes 8519680 | tf_op jit(solution)/shard_map/dot_general | solution.py:592
  48.0 2.5 %collective-permute-start.22 = (bf16[32,1024]{1,0:T(8,128)(2,1)S(1)}, bf16[32,1024]{1,0:T(8,128)(2,1)S(1)}, u32[]{:S(2)}, u32[]{:S(2)}) collective-permute-start(bf16[32,1024]{1,0:T(8,128)(2,1)S(1)} %get-tuple-element.68), channel_id=1, source_target_pairs={{0,12},{4,8},{8,4},{12,0},{1,13},{5,9},{9,5},{13,1},{2,14},{6,10},... | collective-permute-start | bytes 196616 | tf_op jit(solution)/shard_map/ppermute | solution.py:542
  50.5 0.3 collective-permute-start.21
  50.8 1.6 %collective-permute-start.20 = (bf16[32,1024]{1,0:T(8,128)(2,1)S(1)}, bf16[32,1024]{1,0:T(8,128)(2,1)S(1)}, u32[]{:S(2)}, u32[]{:S(2)}) collective-permute-start(bf16[32,1024]{1,0:T(8,128)(2,1)S(1)} %get-tuple-element.70), channel_id=1, source_target_pairs={{0,4},{4,0},{8,12},{12,8},{1,5},{5,1},{9,13},{13,9},{2,6},{6,2},{1... | collective-permute-start | bytes 196616 | tf_op jit(solution)/shard_map/ppermute | solution.py:542
  52.5 0.4 shard_map.126.dense
  52.9 1.1 %convolution_convert_fusion.1.before = bf16[128,1024]{1,0:T(8,128)(2,1)S(1)} fusion(bf16[128,3584]{1,0:T(8,128)(2,1)S(1)} %shard_map.126.dense, bf16[3584,1024]{1,0:T(8,128)(2,1)S(1)} %bitcast.30), kind=kOutput, calls=%fused_computation.1 | convolution fusion | flops 939655168 | bytes 8519680 | tf_op jit(solution)/shard_map/dot_general | solution.py:603
  54.1 2.5 %collective-permute-start.12 = (bf16[32,1024]{1,0:T(8,128)(2,1)S(1)}, bf16[32,1024]{1,0:T(8,128)(2,1)S(1)}, u32[]{:S(2)}, u32[]{:S(2)}) collective-permute-start(bf16[32,1024]{1,0:T(8,128)(2,1)S(1)} %get-tuple-element.72), channel_id=1, source_target_pairs={{0,12},{4,8},{8,4},{12,0},{1,13},{5,9},{9,5},{13,1},{2,14},{6,10},... | collective-permute-start | bytes 196616 | tf_op jit(solution)/shard_map/ppermute | solution.py:542
  56.6 1.9 %collective-permute-start.10 = (bf16[32,1024]{1,0:T(8,128)(2,1)S(1)}, bf16[32,1024]{1,0:T(8,128)(2,1)S(1)}, u32[]{:S(2)}, u32[]{:S(2)}) collective-permute-start(bf16[32,1024]{1,0:T(8,128)(2,1)S(1)} %get-tuple-element.74), channel_id=1, source_target_pairs={{0,4},{4,0},{8,12},{12,8},{1,5},{5,1},{9,13},{13,9},{2,6},{6,2},{1... | collective-permute-start | bytes 196616 | tf_op jit(solution)/shard_map/ppermute | solution.py:542
  58.6 0.4 shard_map.129
  59.0 1.5 %collective-permute-done.12.refs_3_ = bf16[32,1024]{1,0:T(8,128)(2,1)S(1)} collective-permute-done((bf16[32,1024]{1,0:T(8,128)(2,1)S(1)}, bf16[32,1024]{1,0:T(8,128)(2,1)S(1)}, u32[]{:S(2)}, u32[]{:S(2)}) %collective-permute-start.12) | collective-permute-done | bytes 65568 | tf_op jit(solution)/shard_map/ppermute | solution.py:542
  60.4 2.7 %collective-permute-done.11.refs_2_ = bf16[32,1024]{1,0:T(8,128)(2,1)S(1)} collective-permute-done((bf16[32,1024]{1,0:T(8,128)(2,1)S(1)}, bf16[32,1024]{1,0:T(8,128)(2,1)S(1)}, u32[]{:S(2)}, u32[]{:S(2)}) %collective-permute-start.11) | collective-permute-done | bytes 65568 | tf_op jit(solution)/shard_map/ppermute | solution.py:542
  63.1 0.7 shard_map.130
  63.8 2.5 %collective-permute-start.25 = (bf16[32,1024]{1,0:T(8,128)(2,1)S(1)}, bf16[32,1024]{1,0:T(8,128)(2,1)S(1)}, u32[]{:S(2)}, u32[]{:S(2)}) collective-permute-start(bf16[32,1024]{1,0:T(8,128)(2,1)S(1)} %get-tuple-element.52), channel_id=1, source_target_pairs={{0,12},{4,8},{8,4},{12,0},{1,13},{5,9},{9,5},{13,1},{2,14},{6,10},... | collective-permute-start | bytes 196616 | tf_op jit(solution)/shard_map/ppermute | solution.py:542
  66.3 1.9 %collective-permute-start.23 = (bf16[32,1024]{1,0:T(8,128)(2,1)S(1)}, bf16[32,1024]{1,0:T(8,128)(2,1)S(1)}, u32[]{:S(2)}, u32[]{:S(2)}) collective-permute-start(bf16[32,1024]{1,0:T(8,128)(2,1)S(1)} %get-tuple-element.52), channel_id=1, source_target_pairs={{0,4},{4,0},{8,12},{12,8},{1,5},{5,1},{9,13},{13,9},{2,6},{6,2},{1... | collective-permute-start | bytes 196616 | tf_op jit(solution)/shard_map/ppermute | solution.py:542
  68.2 3.1 %collective-permute-done.23 = bf16[32,1024]{1,0:T(8,128)(2,1)S(1)} collective-permute-done((bf16[32,1024]{1,0:T(8,128)(2,1)S(1)}, bf16[32,1024]{1,0:T(8,128)(2,1)S(1)}, u32[]{:S(2)}, u32[]{:S(2)}) %collective-permute-start.23) | collective-permute-done | bytes 65568 | tf_op jit(solution)/shard_map/ppermute | solution.py:542
  71.3 1.0 %collective-permute-done.24 = bf16[32,1024]{1,0:T(8,128)(2,1)S(1)} collective-permute-done((bf16[32,1024]{1,0:T(8,128)(2,1)S(1)}, bf16[32,1024]{1,0:T(8,128)(2,1)S(1)}, u32[]{:S(2)}, u32[]{:S(2)}) %collective-permute-start.24) | collective-permute-done | bytes 65568 | tf_op jit(solution)/shard_map/ppermute | solution.py:542
  72.3 1.4 %shard_map.131 = (bf16[2,32,896]{2,1,0:T(8,128)(2,1)S(1)}, bf16[2,32,896]{2,1,0:T(8,128)(2,1)S(1)}) custom-call(bf16[4,64,128]{2,1,0:T(8,128)(2,1)S(1)} %get-tuple-element.36.picker, bf16[128,1024]{1,0:T(8,128)(2,1)S(1)} %constant_dynamic-update-slice_fusion.residual.before, bf16[3584,1024]{1,0:T(8,128)(2,1)S(1)} %bitcast.30, ...), custom_call_target="tpu_custom_call" | custom-call | tf_op jit(solution)/shard_map/pallas_call | solution.py:356
  73.8 1.5 %shard_map.132 = (bf16[2,32,896]{2,1,0:T(8,128)(2,1)S(1)}, bf16[2,32,896]{2,1,0:T(8,128)(2,1)S(1)}) custom-call(bf16[4,64,128]{2,1,0:T(8,128)(2,1)S(1)} %get-tuple-element.36.picker, bf16[128,1024]{1,0:T(8,128)(2,1)S(1)} %constant_dynamic-update-slice_fusion.residual.before, bf16[3584,1024]{1,0:T(8,128)(2,1)S(1)} %bitcast.30, ...), custom_call_target="tpu_custom_call" | custom-call | tf_op jit(solution)/shard_map/pallas_call | solution.py:356
  75.3 0.6 collective-permute-start.26
  75.9 0.8 collective-permute-start.29
  76.7 0.1 collective-permute-done.26
  76.9 1.2 %collective-permute-start.27 = (bf16[2,32,896]{2,1,0:T(8,128)(2,1)S(1)}, bf16[2,32,896]{2,1,0:T(8,128)(2,1)S(1)}, u32[]{:S(2)}, u32[]{:S(2)}) collective-permute-start(bf16[2,32,896]{2,1,0:T(8,128)(2,1)S(1)} %add_convert_fusion.5.before.mine), channel_id=1, source_target_pairs={{0,2},{2,0},{1,3},{3,1},{4,6},{6,4},{5,7},{7,5},{8,10},{10,8},{9,1... | collective-permute-start | bytes 344072 | tf_op jit(solution)/shard_map/ppermute | solution.py:16
  78.1 2.2 %shard_map.133 = (bf16[3584,1024]{1,0:T(8,128)(2,1)}, f32[8,128]{1,0:T(8,128)S(1)}) custom-call(bf16[3584,128]{1,0:T(8,128)(2,1)S(1)} %get-tuple-element.57.hidden, bf16[128,1024]{1,0:T(8,128)(2,1)S(1)} %constant_dynamic-update-slice_fusion.residual.before, bf16[2,32,896]{2,1,0:T(8,128)(2,1)S(1)} %add_convert_fusion.5.before.mine), custom_call_target="tpu_custom_call" | custom-call | flops 469762048 | bytes 3670016 | tf_op jit(solution)/shard_map/pallas_call | solution.py:412
  80.4 1.6 %collective-permute-done.29.other = bf16[2,32,896]{2,1,0:T(8,128)(2,1)S(1)} collective-permute-done((bf16[2,32,896]{2,1,0:T(8,128)(2,1)S(1)}, bf16[2,32,896]{2,1,0:T(8,128)(2,1)S(1)}, u32[]{:S(2)}, u32[]{:S(2)}) %collective-permute-start.29) | collective-permute-done | bytes 114720 | tf_op jit(solution)/shard_map/ppermute | solution.py:16
  82.0 0.2 shard_map.134.before.mine
  82.2 2.3 %shard_map.135 = (bf16[3584,1024]{1,0:T(8,128)(2,1)}, f32[8,128]{1,0:T(8,128)S(1)}) custom-call(bf16[3584,128]{1,0:T(8,128)(2,1)S(1)} %get-tuple-element.57.hidden, bf16[128,1024]{1,0:T(8,128)(2,1)S(1)} %constant_dynamic-update-slice_fusion.residual.before, bf16[2,2,32,896]{3,2,1,0:T(8,128)(2,1)S(1)} %shard_map.134.before.mine, ...), custom_call_target="tpu_custom_call", output_to_operand_aliasing={{0}: (3, {})} | custom-call | flops 469762048 | bytes 3670016 | tf_op jit(solution)/shard_map/pallas_call | solution.py:412
  84.5 0.2 shard_map.136.mine
  84.7 0.6 collective-permute-start.30
  85.2 3.8 %shard_map.137 = (bf16[1024,3584]{1,0:T(8,128)(2,1)}, bf16[1024,3584]{1,0:T(8,128)(2,1)}) custom-call(bf16[4,64,128]{2,1,0:T(8,128)(2,1)S(1)} %get-tuple-element.36.picker, bf16[1024,128]{1,0:T(8,128)(2,1)S(1)} %get-tuple-element.50.refs_8_.tokens, bf16[2,2,32,896]{3,2,1,0:T(8,128)(2,1)S(1)} %shard_map.134.before.mine, ...), custom_call_target="tpu_custom_call" | custom-call | flops 939524096 | bytes 7340032 | tf_op jit(solution)/shard_map/pallas_call | solution.py:464
  89.1 3.8 %shard_map.138 = (bf16[1024,3584]{1,0:T(8,128)(2,1)}, bf16[1024,3584]{1,0:T(8,128)(2,1)}) custom-call(bf16[4,64,128]{2,1,0:T(8,128)(2,1)S(1)} %get-tuple-element.36.picker, bf16[1024,128]{1,0:T(8,128)(2,1)S(1)} %get-tuple-element.50.refs_8_.tokens, bf16[2,2,32,896]{3,2,1,0:T(8,128)(2,1)S(1)} %shard_map.136.mine, ...), custom_call_target="tpu_custom_call", output_to_operand_aliasing={{0}: (4, {}), {1}: (5, {})} | custom-call | flops 939524096 | bytes 7340032 | tf_op jit(solution)/shard_map/pallas_call | solution.py:464
  (61 shorter events, 0.9 us)
Async XLA Ops:
  0.6 11.7 %collective-permute-start = (bf16[32,1024]{1,0:T(8,128)(2,1)}, bf16[32,1024]{1,0:T(8,128)(2,1)S(1)}, u32[]{:S(2)}, u32[]{:S(2)}) collective-permute-start(bf16[32,1024]{1,0:T(8,128)(2,1)} %param.9), channel_id=1, source_target_pairs={{0,4},{4,0},{8,12},{12,8},{1,5},{5,1},{9,13},{13,9},{2,6},{6,2},{1... | collective-permute-start | bytes 196616 | tf_op jit(solution)/shard_map/ppermute | solution.py:542
  3.7 9.2 %collective-permute-start.2 = (bf16[32,1024]{1,0:T(8,128)(2,1)}, bf16[32,1024]{1,0:T(8,128)(2,1)S(1)}, u32[]{:S(2)}, u32[]{:S(2)}) collective-permute-start(bf16[32,1024]{1,0:T(8,128)(2,1)} %param.9), channel_id=1, source_target_pairs={{0,12},{4,8},{8,4},{12,0},{1,13},{5,9},{9,5},{13,1},{2,14},{6,10},... | collective-permute-start | bytes 196616 | tf_op jit(solution)/shard_map/ppermute | solution.py:542
  6.2 6.7 %collective-permute-start.1 = (bf16[32,1024]{1,0:T(8,128)(2,1)}, bf16[32,1024]{1,0:T(8,128)(2,1)S(1)}, u32[]{:S(2)}, u32[]{:S(2)}) collective-permute-start(bf16[32,1024]{1,0:T(8,128)(2,1)} %param.9), channel_id=1, source_target_pairs={{0,8},{4,12},{8,0},{12,4},{1,9},{5,13},{9,1},{13,5},{2,10},{6,14},... | collective-permute-start | bytes 196616 | tf_op jit(solution)/shard_map/ppermute | solution.py:542
  6.4 5.9 %copy-start = (bf16[32,1024]{1,0:T(8,128)(2,1)S(1)}, bf16[32,1024]{1,0:T(8,128)(2,1)}, u32[]{:S(2)}) copy-start(bf16[32,1024]{1,0:T(8,128)(2,1)} %param.9) | copy-start | bytes 196612
  14.6 2.3 %collective-permute-start.13 = (bf16[2,64,1792]{2,1,0:T(8,128)(2,1)S(1)}, bf16[2,64,1792]{2,1,0:T(8,128)(2,1)S(1)}, u32[]{:S(2)}, u32[]{:S(2)}) collective-permute-start(bf16[2,64,1792]{2,1,0:T(8,128)(2,1)S(1)} %get-tuple-element.49), channel_id=1, source_target_pairs={{0,1},{1,0},{2,3},{3,2},{4,5},{5,4},{6,7},{7,6},{8,9},{9,8},{10,11... | collective-permute-start | bytes 1376264 | tf_op jit(solution)/shard_map/ppermute | solution.py:16
  16.3 2.3 %collective-permute-start.3 = (bf16[2,64,1792]{2,1,0:T(8,128)(2,1)S(1)}, bf16[2,64,1792]{2,1,0:T(8,128)(2,1)S(1)}, u32[]{:S(2)}, u32[]{:S(2)}) collective-permute-start(bf16[2,64,1792]{2,1,0:T(8,128)(2,1)S(1)} %get-tuple-element.40), channel_id=1, source_target_pairs={{0,1},{1,0},{2,3},{3,2},{4,5},{5,4},{6,7},{7,6},{8,9},{9,8},{10,11... | collective-permute-start | bytes 1376264 | tf_op jit(solution)/shard_map/ppermute | solution.py:16
  17.0 11.3 %collective-permute-start.14 = (bf16[2,32,1792]{2,1,0:T(8,128)(2,1)S(1)}, bf16[2,32,1792]{2,1,0:T(8,128)(2,1)S(1)}, u32[]{:S(2)}, u32[]{:S(2)}) collective-permute-start(bf16[2,32,1792]{2,1,0:T(8,128)(2,1)S(1)} %slice.33), channel_id=1, source_target_pairs={{0,2},{2,0},{1,3},{3,1},{4,6},{6,4},{5,7},{7,5},{8,10},{10,8},{9,1... | collective-permute-start | bytes 688136 | tf_op jit(solution)/shard_map/ppermute | solution.py:16
  18.7 10.8 %collective-permute-start.17 = (bf16[2,32,1792]{2,1,0:T(8,128)(2,1)S(1)}, bf16[2,32,1792]{2,1,0:T(8,128)(2,1)S(1)}, u32[]{:S(2)}, u32[]{:S(2)}) collective-permute-start(bf16[2,32,1792]{2,1,0:T(8,128)(2,1)S(1)} %slice.37), channel_id=1, source_target_pairs={{0,2},{2,0},{1,3},{3,1},{4,6},{6,4},{5,7},{7,5},{8,10},{10,8},{9,1... | collective-permute-start | bytes 688136 | tf_op jit(solution)/shard_map/ppermute | solution.py:16
  23.8 8.1 %collective-permute-start.4 = (bf16[2,2,32,896]{3,2,1,0:T(8,128)(2,1)S(1)}, bf16[2,2,32,896]{3,2,1,0:T(8,128)(2,1)S(1)}, u32[]{:S(2)}, u32[]{:S(2)}) collective-permute-start(bf16[2,2,32,896]{3,2,1,0:T(8,128)(2,1)S(1)} %get-tuple-element.42), channel_id=1, source_target_pairs={{0,1},{1,0},{2,3},{3,2},{4,5},{5,4},{6,7},{7,6},{8,9},{9,8},{10,11... | collective-permute-start | bytes 688136 | tf_op jit(solution)/shard_map/ppermute | solution.py:16
  23.9 22.8 %slice-start.2 = ((s8[7340032]{0:T(1024)(128)(4,1)}), s8[4194304]{0:T(1024)(128)(4,1)S(1)}, s32[]{:S(2)}) async-start(s8[7340032]{0:T(1024)(128)(4,1)} %bitcast.31), calls=%async_computation.2 | async-start | bytes 8388608
  23.9 22.8 %slice-start.3 = ((s8[7340032]{0:T(1024)(128)(4,1)}), s8[3145728]{0:T(1024)(128)(4,1)S(1)}, s32[]{:S(2)}) async-start(s8[7340032]{0:T(1024)(128)(4,1)} %bitcast.31), calls=%async_computation.3 | async-start | bytes 6291456
  27.8 3.4 %collective-permute-start.7 = (bf16[2,2,32,896]{3,2,1,0:T(8,128)(2,1)S(1)}, bf16[2,2,32,896]{3,2,1,0:T(8,128)(2,1)S(1)}, u32[]{:S(2)}, u32[]{:S(2)}) collective-permute-start(bf16[2,2,32,896]{3,2,1,0:T(8,128)(2,1)S(1)} %get-tuple-element.46), channel_id=1, source_target_pairs={{0,1},{1,0},{2,3},{3,2},{4,5},{5,4},{6,7},{7,6},{8,9},{9,8},{10,11... | collective-permute-start | bytes 688136 | tf_op jit(solution)/shard_map/ppermute | solution.py:16
  28.4 6.1 %collective-permute-start.15 = (bf16[32,1792]{1,0:T(8,128)(2,1)S(1)}, bf16[32,1792]{1,0:T(8,128)(2,1)S(1)}, u32[]{:S(2)}, u32[]{:S(2)}) collective-permute-start(bf16[32,1792]{1,0:T(8,128)(2,1)S(1)} %fusion.3), channel_id=1, source_target_pairs={{0,2},{2,0},{1,3},{3,1},{4,6},{6,4},{5,7},{7,5},{8,10},{10,8},{9,1... | collective-permute-start | bytes 344072 | tf_op jit(solution)/shard_map/ppermute | solution.py:16
  29.7 7.3 %collective-permute-start.18 = (bf16[32,1792]{1,0:T(8,128)(2,1)S(1)}, bf16[32,1792]{1,0:T(8,128)(2,1)S(1)}, u32[]{:S(2)}, u32[]{:S(2)}) collective-permute-start(bf16[32,1792]{1,0:T(8,128)(2,1)S(1)} %fusion.1), channel_id=1, source_target_pairs={{0,2},{2,0},{1,3},{3,1},{4,6},{6,4},{5,7},{7,5},{8,10},{10,8},{9,1... | collective-permute-start | bytes 344072 | tf_op jit(solution)/shard_map/ppermute | solution.py:16
  31.3 10.6 %collective-permute-start.8 = (bf16[2,2,32,896]{3,2,1,0:T(8,128)(2,1)S(1)}, bf16[2,2,32,896]{3,2,1,0:T(8,128)(2,1)S(1)}, u32[]{:S(2)}, u32[]{:S(2)}) collective-permute-start(bf16[2,2,32,896]{3,2,1,0:T(8,128)(2,1)S(1)} %add_convert_fusion.2.mine), channel_id=1, source_target_pairs={{0,2},{2,0},{1,3},{3,1},{4,6},{6,4},{5,7},{7,5},{8,10},{10,8},{9,1... | collective-permute-start | bytes 688136 | tf_op jit(solution)/shard_map/ppermute | solution.py:16
  32.0 13.9 %collective-permute-start.5 = (bf16[2,2,32,896]{3,2,1,0:T(8,128)(2,1)S(1)}, bf16[2,2,32,896]{3,2,1,0:T(8,128)(2,1)S(1)}, u32[]{:S(2)}, u32[]{:S(2)}) collective-permute-start(bf16[2,2,32,896]{3,2,1,0:T(8,128)(2,1)S(1)} %add_convert_fusion.3.mine), channel_id=1, source_target_pairs={{0,2},{2,0},{1,3},{3,1},{4,6},{6,4},{5,7},{7,5},{8,10},{10,8},{9,1... | collective-permute-start | bytes 688136 | tf_op jit(solution)/shard_map/ppermute | solution.py:16
  34.5 11.6 %collective-permute-start.16 = (bf16[64,1792]{1,0:T(8,128)(2,1)S(1)}, bf16[64,1792]{1,0:T(8,128)(2,1)S(1)}, u32[]{:S(2)}, u32[]{:S(2)}) collective-permute-start(bf16[64,1792]{1,0:T(8,128)(2,1)S(1)} %pad_maximum_fusion.refs_0_), channel_id=1, source_target_pairs={{0,1},{1,0},{2,3},{3,2},{4,5},{5,4},{6,7},{7,6},{8,9},{9,8},{10,11... | collective-permute-start | bytes 688136 | tf_op jit(solution)/shard_map/ppermute | solution.py:16
  37.0 9.1 %collective-permute-start.19 = (bf16[64,1792]{1,0:T(8,128)(2,1)S(1)}, bf16[64,1792]{1,0:T(8,128)(2,1)S(1)}, u32[]{:S(2)}, u32[]{:S(2)}) collective-permute-start(bf16[64,1792]{1,0:T(8,128)(2,1)S(1)} %pad_maximum_fusion.1.refs_2_), channel_id=1, source_target_pairs={{0,1},{1,0},{2,3},{3,2},{4,5},{5,4},{6,7},{7,6},{8,9},{9,8},{10,11... | collective-permute-start | bytes 688136 | tf_op jit(solution)/shard_map/ppermute | solution.py:16
  42.0 10.4 %collective-permute-start.9 = (bf16[2,32,896]{2,1,0:T(8,128)(2,1)S(1)}, bf16[2,32,896]{2,1,0:T(8,128)(2,1)S(1)}, u32[]{:S(2)}, u32[]{:S(2)}) collective-permute-start(bf16[2,32,896]{2,1,0:T(8,128)(2,1)S(1)} %get-tuple-element.47), channel_id=1, source_target_pairs={{0,1},{1,0},{2,3},{3,2},{4,5},{5,4},{6,7},{7,6},{8,9},{9,8},{10,11... | collective-permute-start | bytes 344072 | tf_op jit(solution)/shard_map/ppermute | solution.py:16
  46.0 6.4 %collective-permute-start.6 = (bf16[2,32,896]{2,1,0:T(8,128)(2,1)S(1)}, bf16[2,32,896]{2,1,0:T(8,128)(2,1)S(1)}, u32[]{:S(2)}, u32[]{:S(2)}) collective-permute-start(bf16[2,32,896]{2,1,0:T(8,128)(2,1)S(1)} %get-tuple-element.44), channel_id=1, source_target_pairs={{0,1},{1,0},{2,3},{3,2},{4,5},{5,4},{6,7},{7,6},{8,9},{9,8},{10,11... | collective-permute-start | bytes 344072 | tf_op jit(solution)/shard_map/ppermute | solution.py:16
  46.1 6.8 %slice-start = ((s8[7340032]{0:T(1024)(128)(4,1)}), s8[4194304]{0:T(1024)(128)(4,1)S(1)}, s32[]{:S(2)}) async-start(s8[7340032]{0:T(1024)(128)(4,1)} %bitcast.29), calls=%async_computation | async-start | bytes 8388608
  46.8 6.1 %slice-start.1 = ((s8[7340032]{0:T(1024)(128)(4,1)}), s8[3145728]{0:T(1024)(128)(4,1)S(1)}, s32[]{:S(2)}) async-start(s8[7340032]{0:T(1024)(128)(4,1)} %bitcast.29), calls=%async_computation.1 | async-start | bytes 6291456
  48.0 8.7 %collective-permute-start.22 = (bf16[32,1024]{1,0:T(8,128)(2,1)S(1)}, bf16[32,1024]{1,0:T(8,128)(2,1)S(1)}, u32[]{:S(2)}, u32[]{:S(2)}) collective-permute-start(bf16[32,1024]{1,0:T(8,128)(2,1)S(1)} %get-tuple-element.68), channel_id=1, source_target_pairs={{0,12},{4,8},{8,4},{12,0},{1,13},{5,9},{9,5},{13,1},{2,14},{6,10},... | collective-permute-start | bytes 196616 | tf_op jit(solution)/shard_map/ppermute | solution.py:542
  50.5 8.4 %collective-permute-start.21 = (bf16[32,1024]{1,0:T(8,128)(2,1)S(1)}, bf16[32,1024]{1,0:T(8,128)(2,1)S(1)}, u32[]{:S(2)}, u32[]{:S(2)}) collective-permute-start(bf16[32,1024]{1,0:T(8,128)(2,1)S(1)} %get-tuple-element.69), channel_id=1, source_target_pairs={{0,8},{4,12},{8,0},{12,4},{1,9},{5,13},{9,1},{13,5},{2,10},{6,14},... | collective-permute-start | bytes 196616 | tf_op jit(solution)/shard_map/ppermute | solution.py:542
  50.8 8.1 %collective-permute-start.20 = (bf16[32,1024]{1,0:T(8,128)(2,1)S(1)}, bf16[32,1024]{1,0:T(8,128)(2,1)S(1)}, u32[]{:S(2)}, u32[]{:S(2)}) collective-permute-start(bf16[32,1024]{1,0:T(8,128)(2,1)S(1)} %get-tuple-element.70), channel_id=1, source_target_pairs={{0,4},{4,0},{8,12},{12,8},{1,5},{5,1},{9,13},{13,9},{2,6},{6,2},{1... | collective-permute-start | bytes 196616 | tf_op jit(solution)/shard_map/ppermute | solution.py:542
  54.1 6.3 %collective-permute-start.12 = (bf16[32,1024]{1,0:T(8,128)(2,1)S(1)}, bf16[32,1024]{1,0:T(8,128)(2,1)S(1)}, u32[]{:S(2)}, u32[]{:S(2)}) collective-permute-start(bf16[32,1024]{1,0:T(8,128)(2,1)S(1)} %get-tuple-element.72), channel_id=1, source_target_pairs={{0,12},{4,8},{8,4},{12,0},{1,13},{5,9},{9,5},{13,1},{2,14},{6,10},... | collective-permute-start | bytes 196616 | tf_op jit(solution)/shard_map/ppermute | solution.py:542
  56.6 6.5 %collective-permute-start.11 = (bf16[32,1024]{1,0:T(8,128)(2,1)S(1)}, bf16[32,1024]{1,0:T(8,128)(2,1)S(1)}, u32[]{:S(2)}, u32[]{:S(2)}) collective-permute-start(bf16[32,1024]{1,0:T(8,128)(2,1)S(1)} %get-tuple-element.73), channel_id=1, source_target_pairs={{0,8},{4,12},{8,0},{12,4},{1,9},{5,13},{9,1},{13,5},{2,10},{6,14},... | collective-permute-start | bytes 196616 | tf_op jit(solution)/shard_map/ppermute | solution.py:542
  56.6 6.5 %collective-permute-start.10 = (bf16[32,1024]{1,0:T(8,128)(2,1)S(1)}, bf16[32,1024]{1,0:T(8,128)(2,1)S(1)}, u32[]{:S(2)}, u32[]{:S(2)}) collective-permute-start(bf16[32,1024]{1,0:T(8,128)(2,1)S(1)} %get-tuple-element.74), channel_id=1, source_target_pairs={{0,4},{4,0},{8,12},{12,8},{1,5},{5,1},{9,13},{13,9},{2,6},{6,2},{1... | collective-permute-start | bytes 196616 | tf_op jit(solution)/shard_map/ppermute | solution.py:542
  63.8 8.5 %collective-permute-start.25 = (bf16[32,1024]{1,0:T(8,128)(2,1)S(1)}, bf16[32,1024]{1,0:T(8,128)(2,1)S(1)}, u32[]{:S(2)}, u32[]{:S(2)}) collective-permute-start(bf16[32,1024]{1,0:T(8,128)(2,1)S(1)} %get-tuple-element.52), channel_id=1, source_target_pairs={{0,12},{4,8},{8,4},{12,0},{1,13},{5,9},{9,5},{13,1},{2,14},{6,10},... | collective-permute-start | bytes 196616 | tf_op jit(solution)/shard_map/ppermute | solution.py:542
  66.3 6.0 %collective-permute-start.24 = (bf16[32,1024]{1,0:T(8,128)(2,1)S(1)}, bf16[32,1024]{1,0:T(8,128)(2,1)S(1)}, u32[]{:S(2)}, u32[]{:S(2)}) collective-permute-start(bf16[32,1024]{1,0:T(8,128)(2,1)S(1)} %get-tuple-element.52), channel_id=1, source_target_pairs={{0,8},{4,12},{8,0},{12,4},{1,9},{5,13},{9,1},{13,5},{2,10},{6,14},... | collective-permute-start | bytes 196616 | tf_op jit(solution)/shard_map/ppermute | solution.py:542
  66.3 5.0 %collective-permute-start.23 = (bf16[32,1024]{1,0:T(8,128)(2,1)S(1)}, bf16[32,1024]{1,0:T(8,128)(2,1)S(1)}, u32[]{:S(2)}, u32[]{:S(2)}) collective-permute-start(bf16[32,1024]{1,0:T(8,128)(2,1)S(1)} %get-tuple-element.52), channel_id=1, source_target_pairs={{0,4},{4,0},{8,12},{12,8},{1,5},{5,1},{9,13},{13,9},{2,6},{6,2},{1... | collective-permute-start | bytes 196616 | tf_op jit(solution)/shard_map/ppermute | solution.py:542
  73.7 2.2 %collective-permute-start.28 = (bf16[2,32,896]{2,1,0:T(8,128)(2,1)S(1)}, bf16[2,32,896]{2,1,0:T(8,128)(2,1)S(1)}, u32[]{:S(2)}, u32[]{:S(2)}) collective-permute-start(bf16[2,32,896]{2,1,0:T(8,128)(2,1)S(1)} %get-tuple-element.58), channel_id=1, source_target_pairs={{0,1},{1,0},{2,3},{3,2},{4,5},{5,4},{6,7},{7,6},{8,9},{9,8},{10,11... | collective-permute-start | bytes 344072 | tf_op jit(solution)/shard_map/ppermute | solution.py:16
  75.3 1.5 %collective-permute-start.26 = (bf16[2,32,896]{2,1,0:T(8,128)(2,1)S(1)}, bf16[2,32,896]{2,1,0:T(8,128)(2,1)S(1)}, u32[]{:S(2)}, u32[]{:S(2)}) collective-permute-start(bf16[2,32,896]{2,1,0:T(8,128)(2,1)S(1)} %get-tuple-element.55), channel_id=1, source_target_pairs={{0,1},{1,0},{2,3},{3,2},{4,5},{5,4},{6,7},{7,6},{8,9},{9,8},{10,11... | collective-permute-start | bytes 344072 | tf_op jit(solution)/shard_map/ppermute | solution.py:16
  75.9 6.1 %collective-permute-start.29 = (bf16[2,32,896]{2,1,0:T(8,128)(2,1)S(1)}, bf16[2,32,896]{2,1,0:T(8,128)(2,1)S(1)}, u32[]{:S(2)}, u32[]{:S(2)}) collective-permute-start(bf16[2,32,896]{2,1,0:T(8,128)(2,1)S(1)} %add_convert_fusion.4.mine), channel_id=1, source_target_pairs={{0,2},{2,0},{1,3},{3,1},{4,6},{6,4},{5,7},{7,5},{8,10},{10,8},{9,1... | collective-permute-start | bytes 344072 | tf_op jit(solution)/shard_map/ppermute | solution.py:16
  76.9 7.6 %collective-permute-start.27 = (bf16[2,32,896]{2,1,0:T(8,128)(2,1)S(1)}, bf16[2,32,896]{2,1,0:T(8,128)(2,1)S(1)}, u32[]{:S(2)}, u32[]{:S(2)}) collective-permute-start(bf16[2,32,896]{2,1,0:T(8,128)(2,1)S(1)} %add_convert_fusion.5.before.mine), channel_id=1, source_target_pairs={{0,2},{2,0},{1,3},{3,1},{4,6},{6,4},{5,7},{7,5},{8,10},{10,8},{9,1... | collective-permute-start | bytes 344072 | tf_op jit(solution)/shard_map/ppermute | solution.py:16
  82.1 3.1 %collective-permute-start.31 = (bf16[2,2,32,896]{3,2,1,0:T(8,128)(2,1)S(1)}, bf16[2,2,32,896]{3,2,1,0:T(8,128)(2,1)S(1)}, u32[]{:S(2)}, u32[]{:S(2)}) collective-permute-start(bf16[2,2,32,896]{3,2,1,0:T(8,128)(2,1)S(1)} %shard_map.134.before.mine), channel_id=1, source_target_pairs={{0,1},{1,0},{2,3},{3,2},{4,5},{5,4},{6,7},{7,6},{8,9},{9,8},{10,11... | collective-permute-start | bytes 688136 | tf_op jit(solution)/shard_map/ppermute | solution.py:16
  84.7 4.4 %collective-permute-start.30 = (bf16[2,2,32,896]{3,2,1,0:T(8,128)(2,1)S(1)}, bf16[2,2,32,896]{3,2,1,0:T(8,128)(2,1)S(1)}, u32[]{:S(2)}, u32[]{:S(2)}) collective-permute-start(bf16[2,2,32,896]{3,2,1,0:T(8,128)(2,1)S(1)} %shard_map.136.mine), channel_id=1, source_target_pairs={{0,1},{1,0},{2,3},{3,2},{4,5},{5,4},{6,7},{7,6},{8,9},{9,8},{10,11... | collective-permute-start | bytes 688136 | tf_op jit(solution)/shard_map/ppermute | solution.py:16

commit v6 on v5

--- a/solution.py
+++ b/solution.py
@@ -248,7 +248,8 @@
     )(picker, tokens, far(gate), far(up), before)
 
 
-def hidden_act_kernel(first, swap, mine, other, weight, pre, out):
+def hidden_act_kernel(first, swap, mine, other, weight, *rest):
+    pre, out = rest[-2:]
     count, _, rows = mine.shape[:3]
     for i in range(count):
         totals = []
@@ -263,18 +264,18 @@
         out[i] = (gate * jax.nn.sigmoid(gate) * up * weight[first + i, :rows]).astype(BF)
 
 
-def hidden_act(mine, other, swap, weight, first):
+def hidden_act(mine, other, swap, weight, before, first):
     count, _, rows, width = mine.shape
     return pl.pallas_call(
         functools.partial(hidden_act_kernel, first, swap),
-        in_specs=[whole(), whole(), whole()],
+        in_specs=[whole(), whole(), whole()] + [anywhere()] * len(before),
         out_specs=(whole(), whole()),
         out_shape=(
             jax.ShapeDtypeStruct(mine.shape, F32),
             jax.ShapeDtypeStruct((count, rows, width), BF),
         ),
         compiler_params=pltpu.CompilerParams(vmem_limit_bytes=8 * 1024 * 1024),
-    )(mine, other, weight)
+    )(mine, other, weight, *before)
 
 
 def join_kernel(dps, pipes, place, *refs):
@@ -389,61 +390,58 @@
     )(mine, other, pre, weight, before)
 
 
-def down_grad_kernel(first, hidden, residual, before, *rest):
-    out, done, held, sems = rest[-4:]
+def down_grad_kernel(hidden, residual, before, out, done, held, sems):
     tiles = sems.shape[0]
-    rows = H // 2
+    rows = hidden.shape[0] // tiles
     copies = []
     for i in range(tiles):
-        here = pl.ds(i * rows, rows)
-        part = pl.ds(first * H + i * rows, rows)
-        held[here, :] = dot(hidden[part, :], residual[...]).astype(BF)
-        copies.append(pltpu.make_async_copy(held.at[here], out.at[part], sems.at[i]))
+        part = pl.ds(i * rows, rows)
+        held[part, :] = dot(hidden[part, :], residual[...]).astype(BF)
+        copies.append(pltpu.make_async_copy(held.at[part], out.at[part], sems.at[i]))
         copies[-1].start()
     done[...] = jnp.zeros_like(done)
     for copy in copies:
         copy.wait()
 
 
-def down_grad(hidden, residual, before, first, count, so_far):
+def down_grad(hidden, residual, before):
     rows, token_count = hidden.shape
     width = residual.shape[1]
-    extra = () if so_far is None else (so_far,)
-    return pl.pallas_call(
-        functools.partial(down_grad_kernel, first),
-        in_specs=[whole(), whole(), anywhere()] + [in_hbm()] * len(extra),
+    return pl.pallas_call(
+        down_grad_kernel,
+        in_specs=[whole(), whole(), anywhere()],
         out_specs=(in_hbm(), whole()),
         out_shape=(
             jax.ShapeDtypeStruct((rows, width), BF),
             jax.ShapeDtypeStruct((8, 128), F32),
         ),
         scratch_shapes=[
-            pltpu.VMEM((count * H, width), BF),
-            pltpu.SemaphoreType.DMA((2 * count,)),
+            pltpu.VMEM((rows, width), BF),
+            pltpu.SemaphoreType.DMA((rows // (H // 2),)),
         ],
-        input_output_aliases={3: 0} if extra else {},
         compiler_params=pltpu.CompilerParams(vmem_limit_bytes=16 * 1024 * 1024),
         cost_estimate=pl.CostEstimate(
-            flops=2 * count * H * width * token_count,
-            bytes_accessed=2 * count * H * width,
+            flops=2 * rows * width * token_count,
+            bytes_accessed=2 * rows * width,
             transcendentals=0,
         ),
-    )(hidden, residual, before, *[far(value) for value in extra])
-
-
-def input_grad_kernel(first, picker, tokens, mine, theirs, *rest):
+    )(hidden, residual, before)
+
+
+def input_grad_kernel(group, picker, tokens, *rest):
     outs, held, sems = rest[-4:-2], rest[-2], rest[-1]
-    count = mine.shape[0]
+    count = picker.shape[0]
     splits = sems.shape[2]
     rows = tokens.shape[0] // splits
     copies = []
     for i in range(count):
         for which in range(2):
-            grad = jnp.concatenate([mine[i, which], theirs[i, which]], axis=0)
-            dense = dot(picker[first + i], grad, 0, 0).astype(BF)
+            mine, theirs = rest[i // group * 2], rest[i // group * 2 + 1]
+            grad = jnp.concatenate([mine[i % group, which], theirs[i % group, which]], axis=0)
+            dense = dot(picker[i], grad, 0, 0).astype(BF)
             for r in range(splits):
                 part = pl.ds(r * rows, rows)
-                columns = pl.ds((first + i) * H, H)
+                columns = pl.ds(i * H, H)
                 held[i, which, part] = dot(tokens[part, :], dense).astype(BF)
                 copies.append(
                     pltpu.make_async_copy(
@@ -455,29 +453,26 @@
         copy.wait()
 
 
-def input_grads(picker, tokens, mine, theirs, first, so_far):
-    experts, slots, token_count = picker.shape
+def input_grads(picker, tokens, parts):
+    count, slots, token_count = picker.shape
     width = tokens.shape[0]
-    count = mine.shape[0]
-    out = jax.ShapeDtypeStruct((width, experts * H), BF)
-    extra = () if so_far is None else so_far
-    return pl.pallas_call(
-        functools.partial(input_grad_kernel, first),
-        in_specs=[whole()] * 4 + [in_hbm()] * len(extra),
+    out = jax.ShapeDtypeStruct((width, count * H), BF)
+    return pl.pallas_call(
+        functools.partial(input_grad_kernel, count // len(parts)),
+        in_specs=[whole()] * (2 + 2 * len(parts)),
         out_specs=(in_hbm(), in_hbm()),
         out_shape=(out, out),
         scratch_shapes=[
             pltpu.VMEM((count, 2, width, H), BF),
             pltpu.SemaphoreType.DMA((count, 2, 2)),
         ],
-        input_output_aliases={4 + i: i for i in range(len(extra))},
-        compiler_params=pltpu.CompilerParams(vmem_limit_bytes=16 * 1024 * 1024),
+        compiler_params=pltpu.CompilerParams(vmem_limit_bytes=24 * 1024 * 1024),
         cost_estimate=pl.CostEstimate(
             flops=count * 4 * token_count * width * H,
             bytes_accessed=count * 4 * width * H,
             transcendentals=0,
         ),
-    )(picker, tokens, mine, theirs, *[far(value) for value in extra])
+    )(picker, tokens, *[value for pair in parts for value in pair])
 
 
 def add(a, b):
@@ -594,7 +589,7 @@
     pre, weighted = [], []
     for first, (keep, theirs) in zip(firsts, parts):
         mine, other = exchange_dp(add(keep, theirs), dps)
-        total, part = hidden_act(mine, other, dps == 2, slot_weight, first)
+        total, part = hidden_act(mine, other, dps == 2, slot_weight, target[-2:], first)
         pre.append(total)
         weighted.append(jnp.concatenate([part, shift(part, "pipe", pipes, 1)], axis=1))
     weighted = jnp.concatenate(weighted, axis=0)
@@ -613,16 +608,12 @@
         last = keep
         sums.append(add(keep, shift(send, "pipe", pipes, 1)))
     pairs = [exchange_dp(value, dps) for value in sums]
-    grads = None
-    grad_down = None
-    last = sums[-1]
+    grad_down, done = down_grad(dense_flipped, residual, sums[-1])
     activations = []
     for i, first in enumerate(firsts):
-        grad_down, done = down_grad(dense_flipped, residual, last, first, group, grad_down)
-        last = hidden_grad_act(*pairs[i], dps == 2, pre[i], slot_weight, done, first)
-        activations.append((last, shift(last, "pipe", pipes, 1)))
-    for (mine, theirs), first in zip(activations, firsts):
-        grads = input_grads(picker, base_flipped, mine, theirs, first, grads)
+        mine = hidden_grad_act(*pairs[i], dps == 2, pre[i], slot_weight, done, first)
+        activations.append((mine, shift(mine, "pipe", pipes, 1)))
+    grads = input_grads(picker, base_flipped, activations)
     return (student_out, grads[0], grads[1], grad_down)
 
 

time: 93.2 us -> 91.3 us (0.980)
  waiting for transfers between devices: 22.8 us -> 25.3 us
  starting transfers between devices: 31.3 us -> 29 us
  Pallas kernels: 34.4 us -> 32.2 us
    ppermute x12, waiting for transfers between devices: 8.71 us -> 15.3 us  [to_partner(): return lax.ppermute(value, 'expert', [(i, i ^ s) for i in range(ranks)])]
    ppermute x20, waiting for transfers between devices: 14.1 us -> 10 us  [shift(): lax.ppermute(value, axis, [(i, (i + by) % count) for i in range(count)])]
    pallas_call x4 -> x2, Pallas kernels: 12.2 us -> 9.94 us  [the longest x1 6.5 us: input_grads(): pl.pallas_call(functools.partial(input_grad_kernel, count // len(parts)),...]
    ppermute x12, starting transfers between devices: 19 us -> 17.4 us  [to_partner(): return lax.ppermute(value, 'expert', [(i, i ^ s) for i in range(ranks)])]
  transfers between devices with their start and end apart: 32 -> 32, of which waited for: 12 -> 17; matrix products, arithmetic and copies ran while one was open for 3% -> 4% of each run, Pallas kernels for 29% -> 24%
where the time goes in v6:
time: 91.3 us; the launch traced here: 91.1 us
  Pallas kernels  32.2 us (35%)
  starting transfers between devices  29 us (32%)
  waiting for transfers between devices  25.3 us (28%)
  matrix products  2.24 us (2%)
  between operations  1.26 us (1%)
    ppermute x12, starting transfers between devices, to_partner(): return lax.ppermute(value, 'expert', [(i, i ^ s) for i in range(ranks)])  17.4 us
    ppermute x12, waiting for transfers between devices, to_partner(): return lax.ppermute(value, 'expert', [(i, i ^ s) for i in range(ranks)])  15.3 us
    ppermute x20, starting transfers between devices, shift(): lax.ppermute(value, axis, [(i, (i + by) % count) for i in range(count)])  11.6 us
    ppermute x20, waiting for transfers between devices, shift(): lax.ppermute(value, axis, [(i, (i + by) % count) for i in range(count)])  10 us
    pallas_call x2, Pallas kernels, expert_pre(): pl.pallas_call(functools.partial(expert_kernel, first), in_specs=[whole()...  7.59 us
    pallas_call x1, Pallas kernels, input_grads(): pl.pallas_call(functools.partial(input_grad_kernel, count // len(parts)),...  6.5 us
    pallas_call x1, Pallas kernels, prepare(): pl.pallas_call(functools.partial(prepare_kernel, ranks, capacity, dps, pi...  5.89 us
    pallas_call x1, Pallas kernels, down_grad(): pl.pallas_call(down_grad_kernel, in_specs=[whole(), whole(), anywhere()],...  3.43 us
  transfers between devices with their start and end apart: 32, of which 17 were waited for; matrix products, arithmetic and copies ran while one was open for 4% of the time, Pallas kernels for 24%

profile of v6, /device:TPU:0, one launch (start us, length us, event | category | flops | bytes accessed | tf_op | source)
XLA Modules:
  0.0 91.1 jit_solution(4643352425683481515)
XLA Ops:
  0.6 3.1 %collective-permute-start = (bf16[32,1024]{1,0:T(8,128)(2,1)}, bf16[32,1024]{1,0:T(8,128)(2,1)S(1)}, u32[]{:S(2)}, u32[]{:S(2)}) collective-permute-start(bf16[32,1024]{1,0:T(8,128)(2,1)} %param.9), channel_id=1, source_target_pairs={{0,4},{4,0},{8,12},{12,8},{1,5},{5,1},{9,13},{13,9},{2,6},{6,2},{1... | collective-permute-start | bytes 196616 | tf_op jit(solution)/shard_map/ppermute | solution.py:537
  3.7 2.5 %collective-permute-start.2 = (bf16[32,1024]{1,0:T(8,128)(2,1)}, bf16[32,1024]{1,0:T(8,128)(2,1)S(1)}, u32[]{:S(2)}, u32[]{:S(2)}) collective-permute-start(bf16[32,1024]{1,0:T(8,128)(2,1)} %param.9), channel_id=1, source_target_pairs={{0,12},{4,8},{8,4},{12,0},{1,13},{5,9},{9,5},{13,1},{2,14},{6,10},... | collective-permute-start | bytes 196616 | tf_op jit(solution)/shard_map/ppermute | solution.py:537
  6.2 0.1 collective-permute-start.1
  6.3 0.1 pad_add_fusion.place
  6.4 5.9 %shard_map.120 = (bf16[4,64,128]{2,1,0:T(8,128)(2,1)S(1)}, f32[4,64,1]{2,1,0:T(8,128)S(1)}, bf16[1024,3584]{1,0:T(8,128)(2,1)S(1)}, bf16[1024,3584]{1,0:T(8,128)(2,1)S(1)}) custom-call(s32[3]{0:T(128)S(1)} %pad_add_fusion.place, s32[4,128]{1,0:T(4,128)} %bitcast.33, f32[4,128]{1,0:T(4,128)} %bitcast.34, bf16[1024,3584]{1,0:T(8,128)(2,1)} %gate.3, ...), custom_call_target="tpu_custom_call" | custom-call | bytes 14680064 | tf_op jit(solution)/shard_map/pallas_call | solution.py:122
  12.4 0.5 collective-permute-done.1
  12.9 1.7 %shard_map.123 = (bf16[2,64,1792]{2,1,0:T(8,128)(2,1)S(1)}, bf16[2,64,1792]{2,1,0:T(8,128)(2,1)S(1)}) custom-call(s32[3]{0:T(128)S(1)} %pad_add_fusion.place, bf16[128,1024]{1,0:T(8,128)(2,1)S(1)} %constant_dynamic-update-slice_fusion.4.tokens, bf16[1024,3584]{1,0:T(8,128)(2,1)S(1)} %get-tuple-element.33.gate, bf16[1024,3584]{1,0:T(8,128)(2,1)S(1)} %get-tuple-element.34.up), custom_call_target="tpu_custom_call" | custom-call | flops 939524096 | bytes 7340032 | tf_op jit(solution)/shard_map/pallas_call | solution.py:192
  14.6 0.1 collective-permute-start.6
  14.7 1.7 %shard_map.121 = (bf16[2,64,1792]{2,1,0:T(8,128)(2,1)S(1)}, bf16[2,64,1792]{2,1,0:T(8,128)(2,1)S(1)}) custom-call(s32[3]{0:T(128)S(1)} %pad_add_fusion.place, bf16[128,1024]{1,0:T(8,128)(2,1)S(1)} %constant_dynamic-update-slice_fusion.4.tokens, bf16[1024,3584]{1,0:T(8,128)(2,1)S(1)} %get-tuple-element.33.gate, bf16[1024,3584]{1,0:T(8,128)(2,1)S(1)} %get-tuple-element.34.up), custom_call_target="tpu_custom_call" | custom-call | flops 939524096 | bytes 7340032 | tf_op jit(solution)/shard_map/pallas_call | solution.py:192
  16.3 0.6 collective-permute-start.3
  16.9 0.1 add_convert_fusion
  17.0 1.6 %collective-permute-start.7 = (bf16[2,32,1792]{2,1,0:T(8,128)(2,1)S(1)}, bf16[2,32,1792]{2,1,0:T(8,128)(2,1)S(1)}, u32[]{:S(2)}, u32[]{:S(2)}) collective-permute-start(bf16[2,32,1792]{2,1,0:T(8,128)(2,1)S(1)} %slice.33), channel_id=1, source_target_pairs={{0,2},{2,0},{1,3},{3,1},{4,6},{6,4},{5,7},{7,5},{8,10},{10,8},{9,1... | collective-permute-start | bytes 688136 | tf_op jit(solution)/shard_map/ppermute | solution.py:16
  18.6 0.1 add_convert_fusion.1.before
  18.7 1.3 %collective-permute-start.10 = (bf16[2,32,1792]{2,1,0:T(8,128)(2,1)S(1)}, bf16[2,32,1792]{2,1,0:T(8,128)(2,1)S(1)}, u32[]{:S(2)}, u32[]{:S(2)}) collective-permute-start(bf16[2,32,1792]{2,1,0:T(8,128)(2,1)S(1)} %slice.37), channel_id=1, source_target_pairs={{0,2},{2,0},{1,3},{3,1},{4,6},{6,4},{5,7},{7,5},{8,10},{10,8},{9,1... | collective-permute-start | bytes 688136 | tf_op jit(solution)/shard_map/ppermute | solution.py:16
  20.1 3.7 %shard_map.122 = (bf16[2,2,32,896]{3,2,1,0:T(8,128)(2,1)S(1)}, bf16[2,2,32,896]{3,2,1,0:T(8,128)(2,1)S(1)}) custom-call(bf16[4,64,128]{2,1,0:T(8,128)(2,1)S(1)} %get-tuple-element.32.picker, bf16[128,1024]{1,0:T(8,128)(2,1)S(1)} %constant_dynamic-update-slice_fusion.4.tokens, bf16[1024,3584]{1,0:T(8,128)(2,1)} %gate.5, bf16[1024,3584]{1,0:T(8,128)(2,1)} %up.5, ...), custom_call_target="tpu_custom_call" | custom-call | flops 469762048 | bytes 7340032 | tf_op jit(solution)/shard_map/pallas_call | solution.py:233
  23.8 0.1 collective-permute-start.4
  23.9 3.9 %shard_map.126 = (bf16[2,2,32,896]{3,2,1,0:T(8,128)(2,1)S(1)}, bf16[2,2,32,896]{3,2,1,0:T(8,128)(2,1)S(1)}) custom-call(bf16[4,64,128]{2,1,0:T(8,128)(2,1)S(1)} %get-tuple-element.32.picker, bf16[128,1024]{1,0:T(8,128)(2,1)S(1)} %constant_dynamic-update-slice_fusion.4.tokens, bf16[1024,3584]{1,0:T(8,128)(2,1)} %gate.5, bf16[1024,3584]{1,0:T(8,128)(2,1)} %up.5, ...), custom_call_target="tpu_custom_call" | custom-call | flops 469762048 | bytes 7340032 | tf_op jit(solution)/shard_map/pallas_call | solution.py:233
  27.8 0.5 collective-permute-start.16
  28.4 0.1 fusion.3
  28.4 0.8 collective-permute-start.8
  29.3 0.3 collective-permute-done.10
  29.6 0.1 fusion.1
  29.7 1.6 %collective-permute-start.11 = (bf16[32,1792]{1,0:T(8,128)(2,1)S(1)}, bf16[32,1792]{1,0:T(8,128)(2,1)S(1)}, u32[]{:S(2)}, u32[]{:S(2)}) collective-permute-start(bf16[32,1792]{1,0:T(8,128)(2,1)S(1)} %fusion.1), channel_id=1, source_target_pairs={{0,2},{2,0},{1,3},{3,1},{4,6},{6,4},{5,7},{7,5},{8,10},{10,8},{9,1... | collective-permute-start | bytes 344072 | tf_op jit(solution)/shard_map/ppermute | solution.py:16
  31.3 0.6 collective-permute-start.17
  31.9 2.6 %collective-permute-done.8 = bf16[32,1792]{1,0:T(8,128)(2,1)S(1)} collective-permute-done((bf16[32,1792]{1,0:T(8,128)(2,1)S(1)}, bf16[32,1792]{1,0:T(8,128)(2,1)S(1)}, u32[]{:S(2)}, u32[]{:S(2)}) %collective-permute-start.8) | collective-permute-done | bytes 114720 | tf_op jit(solution)/shard_map/ppermute | solution.py:16
  34.6 2.4 %collective-permute-done.11 = bf16[32,1792]{1,0:T(8,128)(2,1)S(1)} collective-permute-done((bf16[32,1792]{1,0:T(8,128)(2,1)S(1)}, bf16[32,1792]{1,0:T(8,128)(2,1)S(1)}, u32[]{:S(2)}, u32[]{:S(2)}) %collective-permute-start.11) | collective-permute-done | bytes 114720 | tf_op jit(solution)/shard_map/ppermute | solution.py:16
  37.1 0.8 collective-permute-start.5
  38.0 0.5 collective-permute-done.12.refs_3_
  38.5 0.6 shard_map.124
  39.2 1.1 %convolution_convert_fusion.1 = bf16[128,1024]{1,0:T(8,128)(2,1)S(1)} fusion(bf16[128,3584]{1,0:T(8,128)(2,1)S(1)} %shard_map.124, bf16[3584,1024]{1,0:T(8,128)(2,1)S(1)} %bitcast.32), kind=kOutput, calls=%fused_computation.1 | convolution fusion | flops 939655168 | bytes 8519680 | tf_op jit(solution)/shard_map/dot_general | solution.py:587
  40.4 2.5 %collective-permute-start.14 = (bf16[32,1024]{1,0:T(8,128)(2,1)S(1)}, bf16[32,1024]{1,0:T(8,128)(2,1)S(1)}, u32[]{:S(2)}, u32[]{:S(2)}) collective-permute-start(bf16[32,1024]{1,0:T(8,128)(2,1)S(1)} %get-tuple-element.62), channel_id=1, source_target_pairs={{0,12},{4,8},{8,4},{12,0},{1,13},{5,9},{9,5},{13,1},{2,14},{6,10},... | collective-permute-start | bytes 196616 | tf_op jit(solution)/shard_map/ppermute | solution.py:537
  42.9 0.3 collective-permute-start.13
  43.2 3.7 %collective-permute-done.14.rest_1_.refs_7_ = bf16[32,1024]{1,0:T(8,128)(2,1)S(1)} collective-permute-done((bf16[32,1024]{1,0:T(8,128)(2,1)S(1)}, bf16[32,1024]{1,0:T(8,128)(2,1)S(1)}, u32[]{:S(2)}, u32[]{:S(2)}) %collective-permute-start.14) | collective-permute-done | bytes 65568 | tf_op jit(solution)/shard_map/ppermute | solution.py:537
  46.9 2.8 %collective-permute-done.13.rest_0_.refs_6_ = bf16[32,1024]{1,0:T(8,128)(2,1)S(1)} collective-permute-done((bf16[32,1024]{1,0:T(8,128)(2,1)S(1)}, bf16[32,1024]{1,0:T(8,128)(2,1)S(1)}, u32[]{:S(2)}, u32[]{:S(2)}) %collective-permute-start.13) | collective-permute-done | bytes 65568 | tf_op jit(solution)/shard_map/ppermute | solution.py:537
  49.7 0.1 shard_map.127
  49.9 0.1 shard_map.125
  50.0 0.6 collective-permute-start.15
  50.5 0.6 collective-permute-done.18
  51.2 0.3 collective-permute-done.15
  51.5 0.4 shard_map.128.dense
  52.0 1.1 %convolution_convert_fusion.before = bf16[128,1024]{1,0:T(8,128)(2,1)S(1)} fusion(bf16[128,3584]{1,0:T(8,128)(2,1)S(1)} %shard_map.128.dense, bf16[3584,1024]{1,0:T(8,128)(2,1)S(1)} %bitcast.30), kind=kOutput, calls=%fused_computation | convolution fusion | flops 939655168 | bytes 8519680 | tf_op jit(solution)/shard_map/dot_general | solution.py:598
  53.2 2.6 %collective-permute-start.21 = (bf16[32,1024]{1,0:T(8,128)(2,1)S(1)}, bf16[32,1024]{1,0:T(8,128)(2,1)S(1)}, u32[]{:S(2)}, u32[]{:S(2)}) collective-permute-start(bf16[32,1024]{1,0:T(8,128)(2,1)S(1)} %get-tuple-element.64), channel_id=1, source_target_pairs={{0,12},{4,8},{8,4},{12,0},{1,13},{5,9},{9,5},{13,1},{2,14},{6,10},... | collective-permute-start | bytes 196616 | tf_op jit(solution)/shard_map/ppermute | solution.py:537
  55.8 1.9 %collective-permute-start.19 = (bf16[32,1024]{1,0:T(8,128)(2,1)S(1)}, bf16[32,1024]{1,0:T(8,128)(2,1)S(1)}, u32[]{:S(2)}, u32[]{:S(2)}) collective-permute-start(bf16[32,1024]{1,0:T(8,128)(2,1)S(1)} %get-tuple-element.66), channel_id=1, source_target_pairs={{0,4},{4,0},{8,12},{12,8},{1,5},{5,1},{9,13},{13,9},{2,6},{6,2},{1... | collective-permute-start | bytes 196616 | tf_op jit(solution)/shard_map/ppermute | solution.py:537
  57.6 0.4 shard_map.129
  58.0 2.0 %collective-permute-done.21.refs_3_ = bf16[32,1024]{1,0:T(8,128)(2,1)S(1)} collective-permute-done((bf16[32,1024]{1,0:T(8,128)(2,1)S(1)}, bf16[32,1024]{1,0:T(8,128)(2,1)S(1)}, u32[]{:S(2)}, u32[]{:S(2)}) %collective-permute-start.21) | collective-permute-done | bytes 65568 | tf_op jit(solution)/shard_map/ppermute | solution.py:537
  60.0 2.2 %collective-permute-done.20.refs_2_ = bf16[32,1024]{1,0:T(8,128)(2,1)S(1)} collective-permute-done((bf16[32,1024]{1,0:T(8,128)(2,1)S(1)}, bf16[32,1024]{1,0:T(8,128)(2,1)S(1)}, u32[]{:S(2)}, u32[]{:S(2)}) %collective-permute-start.20) | collective-permute-done | bytes 65568 | tf_op jit(solution)/shard_map/ppermute | solution.py:537
  62.2 0.7 shard_map.130
  62.9 2.5 %collective-permute-start.25 = (bf16[32,1024]{1,0:T(8,128)(2,1)S(1)}, bf16[32,1024]{1,0:T(8,128)(2,1)S(1)}, u32[]{:S(2)}, u32[]{:S(2)}) collective-permute-start(bf16[32,1024]{1,0:T(8,128)(2,1)S(1)} %get-tuple-element.48), channel_id=1, source_target_pairs={{0,12},{4,8},{8,4},{12,0},{1,13},{5,9},{9,5},{13,1},{2,14},{6,10},... | collective-permute-start | bytes 196616 | tf_op jit(solution)/shard_map/ppermute | solution.py:537
  65.4 1.9 %collective-permute-start.23 = (bf16[32,1024]{1,0:T(8,128)(2,1)S(1)}, bf16[32,1024]{1,0:T(8,128)(2,1)S(1)}, u32[]{:S(2)}, u32[]{:S(2)}) collective-permute-start(bf16[32,1024]{1,0:T(8,128)(2,1)S(1)} %get-tuple-element.48), channel_id=1, source_target_pairs={{0,4},{4,0},{8,12},{12,8},{1,5},{5,1},{9,13},{13,9},{2,6},{6,2},{1... | collective-permute-start | bytes 196616 | tf_op jit(solution)/shard_map/ppermute | solution.py:537
  67.3 3.0 %collective-permute-done.23 = bf16[32,1024]{1,0:T(8,128)(2,1)S(1)} collective-permute-done((bf16[32,1024]{1,0:T(8,128)(2,1)S(1)}, bf16[32,1024]{1,0:T(8,128)(2,1)S(1)}, u32[]{:S(2)}, u32[]{:S(2)}) %collective-permute-start.23) | collective-permute-done | bytes 65568 | tf_op jit(solution)/shard_map/ppermute | solution.py:537
  70.4 1.1 %collective-permute-done.24 = bf16[32,1024]{1,0:T(8,128)(2,1)S(1)} collective-permute-done((bf16[32,1024]{1,0:T(8,128)(2,1)S(1)}, bf16[32,1024]{1,0:T(8,128)(2,1)S(1)}, u32[]{:S(2)}, u32[]{:S(2)}) %collective-permute-start.24) | collective-permute-done | bytes 65568 | tf_op jit(solution)/shard_map/ppermute | solution.py:537
  71.6 1.3 %shard_map.131 = (bf16[2,32,896]{2,1,0:T(8,128)(2,1)S(1)}, bf16[2,32,896]{2,1,0:T(8,128)(2,1)S(1)}) custom-call(bf16[4,64,128]{2,1,0:T(8,128)(2,1)S(1)} %get-tuple-element.32.picker, bf16[128,1024]{1,0:T(8,128)(2,1)S(1)} %constant_dynamic-update-slice_fusion.residual.before, bf16[3584,1024]{1,0:T(8,128)(2,1)S(1)} %bitcast.30, ...), custom_call_target="tpu_custom_call" | custom-call | tf_op jit(solution)/shard_map/pallas_call | solution.py:357
  72.9 0.1 collective-permute-start.26
  73.0 1.5 %shard_map.132 = (bf16[2,32,896]{2,1,0:T(8,128)(2,1)S(1)}, bf16[2,32,896]{2,1,0:T(8,128)(2,1)S(1)}) custom-call(bf16[4,64,128]{2,1,0:T(8,128)(2,1)S(1)} %get-tuple-element.32.picker, bf16[128,1024]{1,0:T(8,128)(2,1)S(1)} %constant_dynamic-update-slice_fusion.residual.before, bf16[3584,1024]{1,0:T(8,128)(2,1)S(1)} %bitcast.30, ...), custom_call_target="tpu_custom_call" | custom-call | tf_op jit(solution)/shard_map/pallas_call | solution.py:357
  74.5 0.6 collective-permute-start.28
  75.1 0.9 collective-permute-start.27
  76.1 1.2 %collective-permute-start.30 = (bf16[2,32,896]{2,1,0:T(8,128)(2,1)S(1)}, bf16[2,32,896]{2,1,0:T(8,128)(2,1)S(1)}, u32[]{:S(2)}, u32[]{:S(2)}) collective-permute-start(bf16[2,32,896]{2,1,0:T(8,128)(2,1)S(1)} %add_convert_fusion.4.before.mine), channel_id=1, source_target_pairs={{0,2},{2,0},{1,3},{3,1},{4,6},{6,4},{5,7},{7,5},{8,10},{10,8},{9,1... | collective-permute-start | bytes 344072 | tf_op jit(solution)/shard_map/ppermute | solution.py:16
  77.3 3.4 %shard_map.133 = (bf16[3584,1024]{1,0:T(8,128)(2,1)}, f32[8,128]{1,0:T(8,128)S(1)}) custom-call(bf16[3584,128]{1,0:T(8,128)(2,1)S(1)} %get-tuple-element.52.hidden, bf16[128,1024]{1,0:T(8,128)(2,1)S(1)} %constant_dynamic-update-slice_fusion.residual.before, bf16[2,32,896]{2,1,0:T(8,128)(2,1)S(1)} %add_convert_fusion.4.before.mine), custom_call_target="tpu_custom_call" | custom-call | flops 939524096 | bytes 7340032 | tf_op jit(solution)/shard_map/pallas_call | solution.py:410
  80.8 0.4 collective-permute-done.27.other
  81.2 0.2 shard_map.134.rest_0_
  81.4 1.3 %collective-permute-done.30.other = bf16[2,32,896]{2,1,0:T(8,128)(2,1)S(1)} collective-permute-done((bf16[2,32,896]{2,1,0:T(8,128)(2,1)S(1)}, bf16[2,32,896]{2,1,0:T(8,128)(2,1)S(1)}, u32[]{:S(2)}, u32[]{:S(2)}) %collective-permute-start.30) | collective-permute-done | bytes 114720 | tf_op jit(solution)/shard_map/ppermute | solution.py:16
  82.7 0.2 shard_map.135.rest_2_
  83.0 1.5 %collective-permute-done.31.rest_3_ = bf16[2,2,32,896]{3,2,1,0:T(8,128)(2,1)S(1)} collective-permute-done((bf16[2,2,32,896]{3,2,1,0:T(8,128)(2,1)S(1)}, bf16[2,2,32,896]{3,2,1,0:T(8,128)(2,1)S(1)}, u32[]{:S(2)}, u32[]{:S(2)}) %collective-permute-start.31) | collective-permute-done | bytes 229408 | tf_op jit(solution)/shard_map/ppermute | solution.py:16
  84.5 6.5 %shard_map.136 = (bf16[1024,3584]{1,0:T(8,128)(2,1)}, bf16[1024,3584]{1,0:T(8,128)(2,1)}) custom-call(bf16[4,64,128]{2,1,0:T(8,128)(2,1)S(1)} %get-tuple-element.32.picker, bf16[1024,128]{1,0:T(8,128)(2,1)S(1)} %get-tuple-element.46.refs_8_.tokens, bf16[2,2,32,896]{3,2,1,0:T(8,128)(2,1)S(1)} %shard_map.134.rest_0_, ...), custom_call_target="tpu_custom_call" | custom-call | flops 1879048192 | bytes 14680064 | tf_op jit(solution)/shard_map/pallas_call | solution.py:460
  (59 shorter events, 1.1 us)
Async XLA Ops:
  0.6 11.7 %collective-permute-start = (bf16[32,1024]{1,0:T(8,128)(2,1)}, bf16[32,1024]{1,0:T(8,128)(2,1)S(1)}, u32[]{:S(2)}, u32[]{:S(2)}) collective-permute-start(bf16[32,1024]{1,0:T(8,128)(2,1)} %param.9), channel_id=1, source_target_pairs={{0,4},{4,0},{8,12},{12,8},{1,5},{5,1},{9,13},{13,9},{2,6},{6,2},{1... | collective-permute-start | bytes 196616 | tf_op jit(solution)/shard_map/ppermute | solution.py:537
  3.7 9.2 %collective-permute-start.2 = (bf16[32,1024]{1,0:T(8,128)(2,1)}, bf16[32,1024]{1,0:T(8,128)(2,1)S(1)}, u32[]{:S(2)}, u32[]{:S(2)}) collective-permute-start(bf16[32,1024]{1,0:T(8,128)(2,1)} %param.9), channel_id=1, source_target_pairs={{0,12},{4,8},{8,4},{12,0},{1,13},{5,9},{9,5},{13,1},{2,14},{6,10},... | collective-permute-start | bytes 196616 | tf_op jit(solution)/shard_map/ppermute | solution.py:537
  6.2 6.7 %collective-permute-start.1 = (bf16[32,1024]{1,0:T(8,128)(2,1)}, bf16[32,1024]{1,0:T(8,128)(2,1)S(1)}, u32[]{:S(2)}, u32[]{:S(2)}) collective-permute-start(bf16[32,1024]{1,0:T(8,128)(2,1)} %param.9), channel_id=1, source_target_pairs={{0,8},{4,12},{8,0},{12,4},{1,9},{5,13},{9,1},{13,5},{2,10},{6,14},... | collective-permute-start | bytes 196616 | tf_op jit(solution)/shard_map/ppermute | solution.py:537
  6.4 5.9 %copy-start = (bf16[32,1024]{1,0:T(8,128)(2,1)S(1)}, bf16[32,1024]{1,0:T(8,128)(2,1)}, u32[]{:S(2)}) copy-start(bf16[32,1024]{1,0:T(8,128)(2,1)} %param.9) | copy-start | bytes 196612
  14.6 2.3 %collective-permute-start.6 = (bf16[2,64,1792]{2,1,0:T(8,128)(2,1)S(1)}, bf16[2,64,1792]{2,1,0:T(8,128)(2,1)S(1)}, u32[]{:S(2)}, u32[]{:S(2)}) collective-permute-start(bf16[2,64,1792]{2,1,0:T(8,128)(2,1)S(1)} %get-tuple-element.41), channel_id=1, source_target_pairs={{0,1},{1,0},{2,3},{3,2},{4,5},{5,4},{6,7},{7,6},{8,9},{9,8},{10,11... | collective-permute-start | bytes 1376264 | tf_op jit(solution)/shard_map/ppermute | solution.py:16
  16.3 2.3 %collective-permute-start.3 = (bf16[2,64,1792]{2,1,0:T(8,128)(2,1)S(1)}, bf16[2,64,1792]{2,1,0:T(8,128)(2,1)S(1)}, u32[]{:S(2)}, u32[]{:S(2)}) collective-permute-start(bf16[2,64,1792]{2,1,0:T(8,128)(2,1)S(1)} %get-tuple-element.36), channel_id=1, source_target_pairs={{0,1},{1,0},{2,3},{3,2},{4,5},{5,4},{6,7},{7,6},{8,9},{9,8},{10,11... | collective-permute-start | bytes 1376264 | tf_op jit(solution)/shard_map/ppermute | solution.py:16
  17.0 11.3 %collective-permute-start.7 = (bf16[2,32,1792]{2,1,0:T(8,128)(2,1)S(1)}, bf16[2,32,1792]{2,1,0:T(8,128)(2,1)S(1)}, u32[]{:S(2)}, u32[]{:S(2)}) collective-permute-start(bf16[2,32,1792]{2,1,0:T(8,128)(2,1)S(1)} %slice.33), channel_id=1, source_target_pairs={{0,2},{2,0},{1,3},{3,1},{4,6},{6,4},{5,7},{7,5},{8,10},{10,8},{9,1... | collective-permute-start | bytes 688136 | tf_op jit(solution)/shard_map/ppermute | solution.py:16
  18.7 10.8 %collective-permute-start.10 = (bf16[2,32,1792]{2,1,0:T(8,128)(2,1)S(1)}, bf16[2,32,1792]{2,1,0:T(8,128)(2,1)S(1)}, u32[]{:S(2)}, u32[]{:S(2)}) collective-permute-start(bf16[2,32,1792]{2,1,0:T(8,128)(2,1)S(1)} %slice.37), channel_id=1, source_target_pairs={{0,2},{2,0},{1,3},{3,1},{4,6},{6,4},{5,7},{7,5},{8,10},{10,8},{9,1... | collective-permute-start | bytes 688136 | tf_op jit(solution)/shard_map/ppermute | solution.py:16
  23.8 13.3 %collective-permute-start.4 = (bf16[2,2,32,896]{3,2,1,0:T(8,128)(2,1)S(1)}, bf16[2,2,32,896]{3,2,1,0:T(8,128)(2,1)S(1)}, u32[]{:S(2)}, u32[]{:S(2)}) collective-permute-start(bf16[2,2,32,896]{3,2,1,0:T(8,128)(2,1)S(1)} %get-tuple-element.38), channel_id=1, source_target_pairs={{0,1},{1,0},{2,3},{3,2},{4,5},{5,4},{6,7},{7,6},{8,9},{9,8},{10,11... | collective-permute-start | bytes 688136 | tf_op jit(solution)/shard_map/ppermute | solution.py:16
  23.9 15.2 %slice-start.2 = ((s8[7340032]{0:T(1024)(128)(4,1)}), s8[4194304]{0:T(1024)(128)(4,1)S(1)}, s32[]{:S(2)}) async-start(s8[7340032]{0:T(1024)(128)(4,1)} %bitcast.31), calls=%async_computation.2 | async-start | bytes 8388608
  23.9 15.2 %slice-start.3 = ((s8[7340032]{0:T(1024)(128)(4,1)}), s8[3145728]{0:T(1024)(128)(4,1)S(1)}, s32[]{:S(2)}) async-start(s8[7340032]{0:T(1024)(128)(4,1)} %bitcast.31), calls=%async_computation.3 | async-start | bytes 6291456
  27.8 3.4 %collective-permute-start.16 = (bf16[2,2,32,896]{3,2,1,0:T(8,128)(2,1)S(1)}, bf16[2,2,32,896]{3,2,1,0:T(8,128)(2,1)S(1)}, u32[]{:S(2)}, u32[]{:S(2)}) collective-permute-start(bf16[2,2,32,896]{3,2,1,0:T(8,128)(2,1)S(1)} %get-tuple-element.44), channel_id=1, source_target_pairs={{0,1},{1,0},{2,3},{3,2},{4,5},{5,4},{6,7},{7,6},{8,9},{9,8},{10,11... | collective-permute-start | bytes 688136 | tf_op jit(solution)/shard_map/ppermute | solution.py:16
  28.4 6.1 %collective-permute-start.8 = (bf16[32,1792]{1,0:T(8,128)(2,1)S(1)}, bf16[32,1792]{1,0:T(8,128)(2,1)S(1)}, u32[]{:S(2)}, u32[]{:S(2)}) collective-permute-start(bf16[32,1792]{1,0:T(8,128)(2,1)S(1)} %fusion.3), channel_id=1, source_target_pairs={{0,2},{2,0},{1,3},{3,1},{4,6},{6,4},{5,7},{7,5},{8,10},{10,8},{9,1... | collective-permute-start | bytes 344072 | tf_op jit(solution)/shard_map/ppermute | solution.py:16
  29.7 7.3 %collective-permute-start.11 = (bf16[32,1792]{1,0:T(8,128)(2,1)S(1)}, bf16[32,1792]{1,0:T(8,128)(2,1)S(1)}, u32[]{:S(2)}, u32[]{:S(2)}) collective-permute-start(bf16[32,1792]{1,0:T(8,128)(2,1)S(1)} %fusion.1), channel_id=1, source_target_pairs={{0,2},{2,0},{1,3},{3,1},{4,6},{6,4},{5,7},{7,5},{8,10},{10,8},{9,1... | collective-permute-start | bytes 344072 | tf_op jit(solution)/shard_map/ppermute | solution.py:16
  31.3 11.9 %collective-permute-start.17 = (bf16[2,2,32,896]{3,2,1,0:T(8,128)(2,1)S(1)}, bf16[2,2,32,896]{3,2,1,0:T(8,128)(2,1)S(1)}, u32[]{:S(2)}, u32[]{:S(2)}) collective-permute-start(bf16[2,2,32,896]{3,2,1,0:T(8,128)(2,1)S(1)} %add_convert_fusion.2.mine), channel_id=1, source_target_pairs={{0,2},{2,0},{1,3},{3,1},{4,6},{6,4},{5,7},{7,5},{8,10},{10,8},{9,1... | collective-permute-start | bytes 688136 | tf_op jit(solution)/shard_map/ppermute | solution.py:16
  34.5 3.5 %collective-permute-start.9 = (bf16[64,1792]{1,0:T(8,128)(2,1)S(1)}, bf16[64,1792]{1,0:T(8,128)(2,1)S(1)}, u32[]{:S(2)}, u32[]{:S(2)}) collective-permute-start(bf16[64,1792]{1,0:T(8,128)(2,1)S(1)} %pad_maximum_fusion.refs_0_), channel_id=1, source_target_pairs={{0,1},{1,0},{2,3},{3,2},{4,5},{5,4},{6,7},{7,6},{8,9},{9,8},{10,11... | collective-permute-start | bytes 688136 | tf_op jit(solution)/shard_map/ppermute | solution.py:16
  37.0 1.6 %collective-permute-start.12 = (bf16[64,1792]{1,0:T(8,128)(2,1)S(1)}, bf16[64,1792]{1,0:T(8,128)(2,1)S(1)}, u32[]{:S(2)}, u32[]{:S(2)}) collective-permute-start(bf16[64,1792]{1,0:T(8,128)(2,1)S(1)} %pad_maximum_fusion.1.refs_2_), channel_id=1, source_target_pairs={{0,1},{1,0},{2,3},{3,2},{4,5},{5,4},{6,7},{7,6},{8,9},{9,8},{10,11... | collective-permute-start | bytes 688136 | tf_op jit(solution)/shard_map/ppermute | solution.py:16
  37.1 12.7 %collective-permute-start.5 = (bf16[2,2,32,896]{3,2,1,0:T(8,128)(2,1)S(1)}, bf16[2,2,32,896]{3,2,1,0:T(8,128)(2,1)S(1)}, u32[]{:S(2)}, u32[]{:S(2)}) collective-permute-start(bf16[2,2,32,896]{3,2,1,0:T(8,128)(2,1)S(1)} %add_convert_fusion.3.mine), channel_id=1, source_target_pairs={{0,2},{2,0},{1,3},{3,1},{4,6},{6,4},{5,7},{7,5},{8,10},{10,8},{9,1... | collective-permute-start | bytes 688136 | tf_op jit(solution)/shard_map/ppermute | solution.py:16
  38.5 13.4 %slice-start = ((s8[7340032]{0:T(1024)(128)(4,1)}), s8[4194304]{0:T(1024)(128)(4,1)S(1)}, s32[]{:S(2)}) async-start(s8[7340032]{0:T(1024)(128)(4,1)} %bitcast.29), calls=%async_computation | async-start | bytes 8388608
  39.2 12.8 %slice-start.1 = ((s8[7340032]{0:T(1024)(128)(4,1)}), s8[3145728]{0:T(1024)(128)(4,1)S(1)}, s32[]{:S(2)}) async-start(s8[7340032]{0:T(1024)(128)(4,1)} %bitcast.29), calls=%async_computation.1 | async-start | bytes 6291456
  40.4 6.5 %collective-permute-start.14 = (bf16[32,1024]{1,0:T(8,128)(2,1)S(1)}, bf16[32,1024]{1,0:T(8,128)(2,1)S(1)}, u32[]{:S(2)}, u32[]{:S(2)}) collective-permute-start(bf16[32,1024]{1,0:T(8,128)(2,1)S(1)} %get-tuple-element.62), channel_id=1, source_target_pairs={{0,12},{4,8},{8,4},{12,0},{1,13},{5,9},{9,5},{13,1},{2,14},{6,10},... | collective-permute-start | bytes 196616 | tf_op jit(solution)/shard_map/ppermute | solution.py:537
  42.9 6.8 %collective-permute-start.13 = (bf16[32,1024]{1,0:T(8,128)(2,1)S(1)}, bf16[32,1024]{1,0:T(8,128)(2,1)S(1)}, u32[]{:S(2)}, u32[]{:S(2)}) collective-permute-start(bf16[32,1024]{1,0:T(8,128)(2,1)S(1)} %get-tuple-element.63), channel_id=1, source_target_pairs={{0,8},{4,12},{8,0},{12,4},{1,9},{5,13},{9,1},{13,5},{2,10},{6,14},... | collective-permute-start | bytes 196616 | tf_op jit(solution)/shard_map/ppermute | solution.py:537
  49.8 1.4 %collective-permute-start.18 = (bf16[2,32,896]{2,1,0:T(8,128)(2,1)S(1)}, bf16[2,32,896]{2,1,0:T(8,128)(2,1)S(1)}, u32[]{:S(2)}, u32[]{:S(2)}) collective-permute-start(bf16[2,32,896]{2,1,0:T(8,128)(2,1)S(1)} %get-tuple-element.45), channel_id=1, source_target_pairs={{0,1},{1,0},{2,3},{3,2},{4,5},{5,4},{6,7},{7,6},{8,9},{9,8},{10,11... | collective-permute-start | bytes 344072 | tf_op jit(solution)/shard_map/ppermute | solution.py:16
  50.0 1.5 %collective-permute-start.15 = (bf16[2,32,896]{2,1,0:T(8,128)(2,1)S(1)}, bf16[2,32,896]{2,1,0:T(8,128)(2,1)S(1)}, u32[]{:S(2)}, u32[]{:S(2)}) collective-permute-start(bf16[2,32,896]{2,1,0:T(8,128)(2,1)S(1)} %get-tuple-element.42), channel_id=1, source_target_pairs={{0,1},{1,0},{2,3},{3,2},{4,5},{5,4},{6,7},{7,6},{8,9},{9,8},{10,11... | collective-permute-start | bytes 344072 | tf_op jit(solution)/shard_map/ppermute | solution.py:16
  50.5 7.5 %collective-permute-start.22 = (bf16[32,1024]{1,0:T(8,128)(2,1)S(1)}, bf16[32,1024]{1,0:T(8,128)(2,1)S(1)}, u32[]{:S(2)}, u32[]{:S(2)}) collective-permute-start(bf16[32,1024]{1,0:T(8,128)(2,1)S(1)} %get-tuple-element.60), channel_id=1, source_target_pairs={{0,4},{4,0},{8,12},{12,8},{1,5},{5,1},{9,13},{13,9},{2,6},{6,2},{1... | collective-permute-start | bytes 196616 | tf_op jit(solution)/shard_map/ppermute | solution.py:537
  53.2 6.9 %collective-permute-start.21 = (bf16[32,1024]{1,0:T(8,128)(2,1)S(1)}, bf16[32,1024]{1,0:T(8,128)(2,1)S(1)}, u32[]{:S(2)}, u32[]{:S(2)}) collective-permute-start(bf16[32,1024]{1,0:T(8,128)(2,1)S(1)} %get-tuple-element.64), channel_id=1, source_target_pairs={{0,12},{4,8},{8,4},{12,0},{1,13},{5,9},{9,5},{13,1},{2,14},{6,10},... | collective-permute-start | bytes 196616 | tf_op jit(solution)/shard_map/ppermute | solution.py:537
  55.7 6.5 %collective-permute-start.20 = (bf16[32,1024]{1,0:T(8,128)(2,1)S(1)}, bf16[32,1024]{1,0:T(8,128)(2,1)S(1)}, u32[]{:S(2)}, u32[]{:S(2)}) collective-permute-start(bf16[32,1024]{1,0:T(8,128)(2,1)S(1)} %get-tuple-element.65), channel_id=1, source_target_pairs={{0,8},{4,12},{8,0},{12,4},{1,9},{5,13},{9,1},{13,5},{2,10},{6,14},... | collective-permute-start | bytes 196616 | tf_op jit(solution)/shard_map/ppermute | solution.py:537
  55.8 6.5 %collective-permute-start.19 = (bf16[32,1024]{1,0:T(8,128)(2,1)S(1)}, bf16[32,1024]{1,0:T(8,128)(2,1)S(1)}, u32[]{:S(2)}, u32[]{:S(2)}) collective-permute-start(bf16[32,1024]{1,0:T(8,128)(2,1)S(1)} %get-tuple-element.66), channel_id=1, source_target_pairs={{0,4},{4,0},{8,12},{12,8},{1,5},{5,1},{9,13},{13,9},{2,6},{6,2},{1... | collective-permute-start | bytes 196616 | tf_op jit(solution)/shard_map/ppermute | solution.py:537
  62.9 8.6 %collective-permute-start.25 = (bf16[32,1024]{1,0:T(8,128)(2,1)S(1)}, bf16[32,1024]{1,0:T(8,128)(2,1)S(1)}, u32[]{:S(2)}, u32[]{:S(2)}) collective-permute-start(bf16[32,1024]{1,0:T(8,128)(2,1)S(1)} %get-tuple-element.48), channel_id=1, source_target_pairs={{0,12},{4,8},{8,4},{12,0},{1,13},{5,9},{9,5},{13,1},{2,14},{6,10},... | collective-permute-start | bytes 196616 | tf_op jit(solution)/shard_map/ppermute | solution.py:537
  65.4 6.2 %collective-permute-start.24 = (bf16[32,1024]{1,0:T(8,128)(2,1)S(1)}, bf16[32,1024]{1,0:T(8,128)(2,1)S(1)}, u32[]{:S(2)}, u32[]{:S(2)}) collective-permute-start(bf16[32,1024]{1,0:T(8,128)(2,1)S(1)} %get-tuple-element.48), channel_id=1, source_target_pairs={{0,8},{4,12},{8,0},{12,4},{1,9},{5,13},{9,1},{13,5},{2,10},{6,14},... | collective-permute-start | bytes 196616 | tf_op jit(solution)/shard_map/ppermute | solution.py:537
  65.4 5.0 %collective-permute-start.23 = (bf16[32,1024]{1,0:T(8,128)(2,1)S(1)}, bf16[32,1024]{1,0:T(8,128)(2,1)S(1)}, u32[]{:S(2)}, u32[]{:S(2)}) collective-permute-start(bf16[32,1024]{1,0:T(8,128)(2,1)S(1)} %get-tuple-element.48), channel_id=1, source_target_pairs={{0,4},{4,0},{8,12},{12,8},{1,5},{5,1},{9,13},{13,9},{2,6},{6,2},{1... | collective-permute-start | bytes 196616 | tf_op jit(solution)/shard_map/ppermute | solution.py:537
  72.9 2.2 %collective-permute-start.26 = (bf16[2,32,896]{2,1,0:T(8,128)(2,1)S(1)}, bf16[2,32,896]{2,1,0:T(8,128)(2,1)S(1)}, u32[]{:S(2)}, u32[]{:S(2)}) collective-permute-start(bf16[2,32,896]{2,1,0:T(8,128)(2,1)S(1)} %get-tuple-element.50), channel_id=1, source_target_pairs={{0,1},{1,0},{2,3},{3,2},{4,5},{5,4},{6,7},{7,6},{8,9},{9,8},{10,11... | collective-permute-start | bytes 344072 | tf_op jit(solution)/shard_map/ppermute | solution.py:16
  74.5 1.5 %collective-permute-start.28 = (bf16[2,32,896]{2,1,0:T(8,128)(2,1)S(1)}, bf16[2,32,896]{2,1,0:T(8,128)(2,1)S(1)}, u32[]{:S(2)}, u32[]{:S(2)}) collective-permute-start(bf16[2,32,896]{2,1,0:T(8,128)(2,1)S(1)} %get-tuple-element.54), channel_id=1, source_target_pairs={{0,1},{1,0},{2,3},{3,2},{4,5},{5,4},{6,7},{7,6},{8,9},{9,8},{10,11... | collective-permute-start | bytes 344072 | tf_op jit(solution)/shard_map/ppermute | solution.py:16
  75.1 6.1 %collective-permute-start.27 = (bf16[2,32,896]{2,1,0:T(8,128)(2,1)S(1)}, bf16[2,32,896]{2,1,0:T(8,128)(2,1)S(1)}, u32[]{:S(2)}, u32[]{:S(2)}) collective-permute-start(bf16[2,32,896]{2,1,0:T(8,128)(2,1)S(1)} %add_convert_fusion.5.mine), channel_id=1, source_target_pairs={{0,2},{2,0},{1,3},{3,1},{4,6},{6,4},{5,7},{7,5},{8,10},{10,8},{9,1... | collective-permute-start | bytes 344072 | tf_op jit(solution)/shard_map/ppermute | solution.py:16
  76.1 6.6 %collective-permute-start.30 = (bf16[2,32,896]{2,1,0:T(8,128)(2,1)S(1)}, bf16[2,32,896]{2,1,0:T(8,128)(2,1)S(1)}, u32[]{:S(2)}, u32[]{:S(2)}) collective-permute-start(bf16[2,32,896]{2,1,0:T(8,128)(2,1)S(1)} %add_convert_fusion.4.before.mine), channel_id=1, source_target_pairs={{0,2},{2,0},{1,3},{3,1},{4,6},{6,4},{5,7},{7,5},{8,10},{10,8},{9,1... | collective-permute-start | bytes 344072 | tf_op jit(solution)/shard_map/ppermute | solution.py:16
  81.4 1.6 %collective-permute-start.29 = (bf16[2,2,32,896]{3,2,1,0:T(8,128)(2,1)S(1)}, bf16[2,2,32,896]{3,2,1,0:T(8,128)(2,1)S(1)}, u32[]{:S(2)}, u32[]{:S(2)}) collective-permute-start(bf16[2,2,32,896]{3,2,1,0:T(8,128)(2,1)S(1)} %shard_map.134.rest_0_), channel_id=1, source_target_pairs={{0,1},{1,0},{2,3},{3,2},{4,5},{5,4},{6,7},{7,6},{8,9},{9,8},{10,11... | collective-permute-start | bytes 688136 | tf_op jit(solution)/shard_map/ppermute | solution.py:16
  82.9 1.6 %collective-permute-start.31 = (bf16[2,2,32,896]{3,2,1,0:T(8,128)(2,1)S(1)}, bf16[2,2,32,896]{3,2,1,0:T(8,128)(2,1)S(1)}, u32[]{:S(2)}, u32[]{:S(2)}) collective-permute-start(bf16[2,2,32,896]{3,2,1,0:T(8,128)(2,1)S(1)} %shard_map.135.rest_2_), channel_id=1, source_target_pairs={{0,1},{1,0},{2,3},{3,2},{4,5},{5,4},{6,7},{7,6},{8,9},{9,8},{10,11... | collective-permute-start | bytes 688136 | tf_op jit(solution)/shard_map/ppermute | solution.py:16

commit v7 on v6

--- a/solution.py
+++ b/solution.py
@@ -142,26 +142,25 @@
     )(place, far(routes), far(shares), far(gate), far(up))
 
 
-def residual_kernel(ranks, *refs):
-    student = refs[0][...].astype(F32)
-    target = refs[ranks][...].astype(F32)
-    for i in range(1, ranks):
-        student = student + refs[i][...].astype(F32)
-        target = target + refs[ranks + i][...].astype(F32)
-    refs[-2][...] = student.astype(BF)
-    refs[-1][...] = (student - target).astype(BF)
+def residual_kernel(student_parts, target_parts, before, out, residual):
+    student = student_parts[0].astype(F32)
+    target = target_parts[0].astype(F32)
+    for i in range(1, student_parts.shape[0]):
+        student = student + student_parts[i].astype(F32)
+        target = target + target_parts[i].astype(F32)
+    out[...] = student.astype(BF)
+    residual[...] = (student - target).astype(BF)
 
 
 def residual_of(student, target, before):
-    ranks = len(student)
-    block = jax.ShapeDtypeStruct(student[0].shape, BF)
-    return pl.pallas_call(
-        functools.partial(residual_kernel, ranks),
-        in_specs=[whole()] * (2 * ranks) + [anywhere()] * len(before),
+    block = jax.ShapeDtypeStruct(student.shape[1:], BF)
+    return pl.pallas_call(
+        residual_kernel,
+        in_specs=[whole(), whole(), anywhere()],
         out_specs=(whole(), whole()),
         out_shape=(block, block),
         compiler_params=pltpu.CompilerParams(vmem_limit_bytes=4 * 1024 * 1024),
-    )(*student, *target, *before)
+    )(student, target, before)
 
 
 def tile_of(size):
@@ -552,10 +551,8 @@
         return whole_rows
 
     def to_owners(product):
-        def block_of(r):
-            return lax.dynamic_slice_in_dim(product, r * block, block, axis=0)
-
-        return [block_of(rank)] + [to_partner(block_of(target_of(s)), s) for s in range(1, ranks)]
+        blocks = product.reshape(ranks, block, width)
+        return lax.all_to_all(blocks, "expert", split_axis=0, concat_axis=0)
 
     base = gather_tokens(tokens)
     picker, slot_weight, gate_near, up_near = prepare(
@@ -589,7 +586,7 @@
     pre, weighted = [], []
     for first, (keep, theirs) in zip(firsts, parts):
         mine, other = exchange_dp(add(keep, theirs), dps)
-        total, part = hidden_act(mine, other, dps == 2, slot_weight, target[-2:], first)
+        total, part = hidden_act(mine, other, dps == 2, slot_weight, [target], first)
         pre.append(total)
         weighted.append(jnp.concatenate([part, shift(part, "pipe", pipes, 1)], axis=1))
     weighted = jnp.concatenate(weighted, axis=0)
@@ -598,8 +595,10 @@
     product = jnp.dot(dense, expert_down, preferred_element_type=F32).astype(BF)
     student = to_owners(product)
     dense_flipped, base_flipped = flip(dense, base, product)
-    student_out, residual = residual_of(student, target, (base_flipped,))
-    residual = gather_tokens(residual)
+    student_out, residual = residual_of(student, target, base_flipped)
+    residual = jnp.broadcast_to(residual[None], (ranks, block, width))
+    residual = lax.all_to_all(residual, "expert", split_axis=0, concat_axis=0)
+    residual = residual.reshape(token_count, width)
 
     sums = []
     last = residual

time: 91.3 us -> 108 us (1.18)
  blocking collectives: 0 us -> 11.1 us
  matrix products: 2.24 us -> 6.74 us
  starting transfers between devices: 29 us -> 24.6 us
  local copies, waits for them, and re-layouts: 0.24 us -> 4.13 us
  waiting for transfers between devices: 25.3 us -> 27.1 us
    all_to_all x0 -> x2, waiting for transfers between devices: none -> 16.7 us  [to_owners(): return lax.all_to_all(blocks, 'expert', split_axis=0, concat_axis=0)]
    ppermute x12 -> x3, waiting for transfers between devices: 15.3 us -> 0.49 us  [to_partner(): return lax.ppermute(value, 'expert', [(i, i ^ s) for i in range(ranks)])]
    ppermute x12 -> x3, starting transfers between devices: 17.4 us -> 5.68 us  [to_partner(): return lax.ppermute(value, 'expert', [(i, i ^ s) for i in range(ranks)])]
    all_to_all x0 -> x1, blocking collectives: none -> 11.1 us  [body(): residual = lax.all_to_all(residual, 'expert', split_axis=0, concat_axis=0)]
    all_to_all x0 -> x2, starting transfers between devices: none -> 7.14 us  [to_owners(): return lax.all_to_all(blocks, 'expert', split_axis=0, concat_axis=0)]
    unnamed x10 -> x12, local copies, waits for them, and re-layouts: 0.02 us -> 4.02 us
    dot_general x1, matrix products: 1.12 us -> 4.91 us  [body(): product = jnp.dot(dense, expert_down, preferred_element_type=F32).astype(BF)]
  transfers between devices with their start and end apart: 32 -> 25, of which waited for: 17 -> 13; matrix products, arithmetic and copies ran while one was open for 4% -> 2% of each run, Pallas kernels for 24% -> 20%
where the time goes in v7:
time: 108 us
  Pallas kernels  32 us (30%)
  waiting for transfers between devices  27.1 us (25%)
  starting transfers between devices  24.6 us (23%)
  blocking collectives  11.1 us (10%)
  matrix products  6.74 us (6%)
  local copies, waits for them, and re-layouts  4.13 us (4%)
  between operations  1.19 us (1%)
    all_to_all x2, waiting for transfers between devices, to_owners(): return lax.all_to_all(blocks, 'expert', split_axis=0, concat_axis=0)  16.7 us
    ppermute x20, starting transfers between devices, shift(): lax.ppermute(value, axis, [(i, (i + by) % count) for i in range(count)])  11.7 us
    all_to_all x1, blocking collectives, body(): residual = lax.all_to_all(residual, 'expert', split_axis=0, concat_axis=0)  11.1 us
    ppermute x20, waiting for transfers between devices, shift(): lax.ppermute(value, axis, [(i, (i + by) % count) for i in range(count)])  9.89 us
    pallas_call x2, Pallas kernels, expert_pre(): pl.pallas_call(functools.partial(expert_kernel, first), in_specs=[whole()...  7.59 us
    all_to_all x2, starting transfers between devices, to_owners(): return lax.all_to_all(blocks, 'expert', split_axis=0, concat_axis=0)  7.14 us
    pallas_call x1, Pallas kernels, input_grads(): pl.pallas_call(functools.partial(input_grad_kernel, count // len(parts)),...  6.49 us
    pallas_call x1, Pallas kernels, prepare(): pl.pallas_call(functools.partial(prepare_kernel, ranks, capacity, dps, pi...  5.89 us
  transfers between devices with their start and end apart: 25, of which 13 were waited for; matrix products, arithmetic and copies ran while one was open for 2% of the time, Pallas kernels for 20%

profile of v7, /device:TPU:0, one launch (start us, length us, event | category | flops | bytes accessed | tf_op | source)
XLA Modules:
  0.0 107.6 jit_solution(13676006177151150590)
XLA Ops:
  0.6 3.1 %collective-permute-start = (bf16[32,1024]{1,0:T(8,128)(2,1)}, bf16[32,1024]{1,0:T(8,128)(2,1)S(1)}, u32[]{:S(2)}, u32[]{:S(2)}) collective-permute-start(bf16[32,1024]{1,0:T(8,128)(2,1)} %param.9), channel_id=1, source_target_pairs={{0,4},{4,0},{8,12},{12,8},{1,5},{5,1},{9,13},{13,9},{2,6},{6,2},{1... | collective-permute-start | bytes 196616 | tf_op jit(solution)/shard_map/ppermute | solution.py:536
  3.7 2.5 %collective-permute-start.2 = (bf16[32,1024]{1,0:T(8,128)(2,1)}, bf16[32,1024]{1,0:T(8,128)(2,1)S(1)}, u32[]{:S(2)}, u32[]{:S(2)}) collective-permute-start(bf16[32,1024]{1,0:T(8,128)(2,1)} %param.9), channel_id=1, source_target_pairs={{0,12},{4,8},{8,4},{12,0},{1,13},{5,9},{9,5},{13,1},{2,14},{6,10},... | collective-permute-start | bytes 196616 | tf_op jit(solution)/shard_map/ppermute | solution.py:536
  6.2 0.1 collective-permute-start.1
  6.3 0.1 pad_add_fusion.place
  6.4 5.9 %shard_map.120 = (bf16[4,64,128]{2,1,0:T(8,128)(2,1)S(1)}, f32[4,64,1]{2,1,0:T(8,128)S(1)}, bf16[1024,3584]{1,0:T(8,128)(2,1)S(1)}, bf16[1024,3584]{1,0:T(8,128)(2,1)S(1)}) custom-call(s32[3]{0:T(128)S(1)} %pad_add_fusion.place, s32[4,128]{1,0:T(4,128)} %bitcast.38, f32[4,128]{1,0:T(4,128)} %bitcast.39, bf16[1024,3584]{1,0:T(8,128)(2,1)} %gate.3, ...), custom_call_target="tpu_custom_call" | custom-call | bytes 14680064 | tf_op jit(solution)/shard_map/pallas_call | solution.py:122
  12.4 0.5 collective-permute-done.1
  12.9 1.7 %shard_map.123 = (bf16[2,64,1792]{2,1,0:T(8,128)(2,1)S(1)}, bf16[2,64,1792]{2,1,0:T(8,128)(2,1)S(1)}) custom-call(s32[3]{0:T(128)S(1)} %pad_add_fusion.place, bf16[128,1024]{1,0:T(8,128)(2,1)S(1)} %constant_dynamic-update-slice_fusion.tokens, bf16[1024,3584]{1,0:T(8,128)(2,1)S(1)} %get-tuple-element.33.gate, bf16[1024,3584]{1,0:T(8,128)(2,1)S(1)} %get-tuple-element.34.up), custom_call_target="tpu_custom_call" | custom-call | flops 939524096 | bytes 7340032 | tf_op jit(solution)/shard_map/pallas_call | solution.py:191
  14.6 0.1 collective-permute-start.6
  14.7 1.7 %shard_map.121 = (bf16[2,64,1792]{2,1,0:T(8,128)(2,1)S(1)}, bf16[2,64,1792]{2,1,0:T(8,128)(2,1)S(1)}) custom-call(s32[3]{0:T(128)S(1)} %pad_add_fusion.place, bf16[128,1024]{1,0:T(8,128)(2,1)S(1)} %constant_dynamic-update-slice_fusion.tokens, bf16[1024,3584]{1,0:T(8,128)(2,1)S(1)} %get-tuple-element.33.gate, bf16[1024,3584]{1,0:T(8,128)(2,1)S(1)} %get-tuple-element.34.up), custom_call_target="tpu_custom_call" | custom-call | flops 939524096 | bytes 7340032 | tf_op jit(solution)/shard_map/pallas_call | solution.py:191
  16.3 0.6 collective-permute-start.3
  16.9 0.1 add_convert_fusion
  17.0 1.6 %collective-permute-start.7 = (bf16[2,32,1792]{2,1,0:T(8,128)(2,1)S(1)}, bf16[2,32,1792]{2,1,0:T(8,128)(2,1)S(1)}, u32[]{:S(2)}, u32[]{:S(2)}) collective-permute-start(bf16[2,32,1792]{2,1,0:T(8,128)(2,1)S(1)} %slice.33), channel_id=1, source_target_pairs={{0,2},{2,0},{1,3},{3,1},{4,6},{6,4},{5,7},{7,5},{8,10},{10,8},{9,1... | collective-permute-start | bytes 688136 | tf_op jit(solution)/shard_map/ppermute | solution.py:16
  18.6 0.1 add_convert_fusion.1.before
  18.7 1.3 %collective-permute-start.10 = (bf16[2,32,1792]{2,1,0:T(8,128)(2,1)S(1)}, bf16[2,32,1792]{2,1,0:T(8,128)(2,1)S(1)}, u32[]{:S(2)}, u32[]{:S(2)}) collective-permute-start(bf16[2,32,1792]{2,1,0:T(8,128)(2,1)S(1)} %slice.37), channel_id=1, source_target_pairs={{0,2},{2,0},{1,3},{3,1},{4,6},{6,4},{5,7},{7,5},{8,10},{10,8},{9,1... | collective-permute-start | bytes 688136 | tf_op jit(solution)/shard_map/ppermute | solution.py:16
  20.1 3.7 %shard_map.122 = (bf16[2,2,32,896]{3,2,1,0:T(8,128)(2,1)S(1)}, bf16[2,2,32,896]{3,2,1,0:T(8,128)(2,1)S(1)}) custom-call(bf16[4,64,128]{2,1,0:T(8,128)(2,1)S(1)} %get-tuple-element.32.picker, bf16[128,1024]{1,0:T(8,128)(2,1)S(1)} %constant_dynamic-update-slice_fusion.tokens, bf16[1024,3584]{1,0:T(8,128)(2,1)} %gate.5, bf16[1024,3584]{1,0:T(8,128)(2,1)} %up.5, ...), custom_call_target="tpu_custom_call" | custom-call | flops 469762048 | bytes 7340032 | tf_op jit(solution)/shard_map/pallas_call | solution.py:232
  23.8 0.1 collective-permute-start.4
  23.9 3.9 %shard_map.126 = (bf16[2,2,32,896]{3,2,1,0:T(8,128)(2,1)S(1)}, bf16[2,2,32,896]{3,2,1,0:T(8,128)(2,1)S(1)}) custom-call(bf16[4,64,128]{2,1,0:T(8,128)(2,1)S(1)} %get-tuple-element.32.picker, bf16[128,1024]{1,0:T(8,128)(2,1)S(1)} %constant_dynamic-update-slice_fusion.tokens, bf16[1024,3584]{1,0:T(8,128)(2,1)} %gate.5, bf16[1024,3584]{1,0:T(8,128)(2,1)} %up.5, ...), custom_call_target="tpu_custom_call" | custom-call | flops 469762048 | bytes 7340032 | tf_op jit(solution)/shard_map/pallas_call | solution.py:232
  27.8 0.5 collective-permute-start.14
  28.4 0.1 fusion.3
  28.4 0.8 collective-permute-start.8
  29.3 0.3 collective-permute-done.10
  29.6 0.1 fusion.1
  29.7 1.6 %collective-permute-start.11 = (bf16[32,1792]{1,0:T(8,128)(2,1)S(1)}, bf16[32,1792]{1,0:T(8,128)(2,1)S(1)}, u32[]{:S(2)}, u32[]{:S(2)}) collective-permute-start(bf16[32,1792]{1,0:T(8,128)(2,1)S(1)} %fusion.1), channel_id=1, source_target_pairs={{0,2},{2,0},{1,3},{3,1},{4,6},{6,4},{5,7},{7,5},{8,10},{10,8},{9,1... | collective-permute-start | bytes 344072 | tf_op jit(solution)/shard_map/ppermute | solution.py:16
  31.2 3.3 %collective-permute-done.8 = bf16[32,1792]{1,0:T(8,128)(2,1)S(1)} collective-permute-done((bf16[32,1792]{1,0:T(8,128)(2,1)S(1)}, bf16[32,1792]{1,0:T(8,128)(2,1)S(1)}, u32[]{:S(2)}, u32[]{:S(2)}) %collective-permute-start.8) | collective-permute-done | bytes 114720 | tf_op jit(solution)/shard_map/ppermute | solution.py:16
  34.5 0.1 collective-permute-start.9
  34.6 1.5 %collective-permute-done.11 = bf16[32,1792]{1,0:T(8,128)(2,1)S(1)} collective-permute-done((bf16[32,1792]{1,0:T(8,128)(2,1)S(1)}, bf16[32,1792]{1,0:T(8,128)(2,1)S(1)}, u32[]{:S(2)}, u32[]{:S(2)}) %collective-permute-start.11) | collective-permute-done | bytes 114720 | tf_op jit(solution)/shard_map/ppermute | solution.py:16
  36.1 0.1 collective-permute-start.12
  36.3 0.8 collective-permute-start.15
  37.1 0.6 collective-permute-done.12.refs_3_
  37.7 0.6 shard_map.124
  38.3 1.8 %convolution_convert_fusion.1 = bf16[128,1024]{1,0:T(8,128)(2,1)} fusion(bf16[128,3584]{1,0:T(8,128)(2,1)S(1)} %shard_map.124, bf16[3584,1024]{1,0:T(8,128)(2,1)S(1)} %bitcast.37), kind=kOutput, calls=%fused_computation.1 | convolution fusion | flops 939655168 | bytes 8519680 | tf_op jit(solution)/shard_map/dot_general | solution.py:584
  40.1 3.7 %all-to-all-start = ((bf16[4,32,1024]{2,1,0:T(8,128)(2,1)}), bf16[4,32,1024]{2,1,0:T(8,128)(2,1)S(1)}, u32[]{:S(2)}, u32[]{:S(2)}) async-start(bf16[4,32,1024]{2,1,0:T(8,128)(2,1)} %bitcast.9), calls=%async_computation | async-start | bytes 524288 | tf_op jit(solution)/shard_map/all_to_all | solution.py:555
  43.9 0.8 collective-permute-start.5
  44.7 8.4 %all-to-all-done.rest_0_.target_parts = bf16[4,32,1024]{2,1,0:T(8,128)(2,1)S(1)} async-done(((bf16[4,32,1024]{2,1,0:T(8,128)(2,1)}), bf16[4,32,1024]{2,1,0:T(8,128)(2,1)S(1)}, u32[]{:S(2)}, u32[]{:S(2)}) %all-to-all-start) | async-done | bytes 262176 | tf_op jit(solution)/shard_map/all_to_all | solution.py:555
  53.1 0.1 shard_map.127
  53.2 0.1 collective-permute-start.16
  53.3 0.1 shard_map.125
  53.4 0.5 collective-permute-start.13
  53.9 0.6 collective-permute-done.16
  54.6 0.3 collective-permute-done.13
  54.9 0.4 shard_map.128.dense
  55.4 4.9 %convolution_convert_fusion.before = bf16[128,1024]{1,0:T(8,128)(2,1)} fusion(bf16[128,3584]{1,0:T(8,128)(2,1)S(1)} %shard_map.128.dense, bf16[3584,1024]{1,0:T(8,128)(2,1)} %down.3), kind=kOutput, calls=%fused_computation | convolution fusion | flops 939655168 | bytes 8519680 | tf_op jit(solution)/shard_map/dot_general | solution.py:595
  60.3 3.4 %all-to-all-start.1 = ((bf16[4,32,1024]{2,1,0:T(8,128)(2,1)}), bf16[4,32,1024]{2,1,0:T(8,128)(2,1)S(1)}, u32[]{:S(2)}, u32[]{:S(2)}) async-start(bf16[4,32,1024]{2,1,0:T(8,128)(2,1)} %bitcast.10), calls=%async_computation.1 | async-start | bytes 524288 | tf_op jit(solution)/shard_map/all_to_all | solution.py:555
  63.7 0.4 shard_map.129
  64.1 0.9 copy-done.1
  65.0 8.3 %all-to-all-done.1.student_parts = bf16[4,32,1024]{2,1,0:T(8,128)(2,1)S(1)} async-done(((bf16[4,32,1024]{2,1,0:T(8,128)(2,1)}), bf16[4,32,1024]{2,1,0:T(8,128)(2,1)S(1)}, u32[]{:S(2)}, u32[]{:S(2)}) %all-to-all-start.1) | async-done | bytes 262176 | tf_op jit(solution)/shard_map/all_to_all | solution.py:555
  73.3 0.7 shard_map.130
  74.0 11.1 %all_to_all.15 = bf16[4,32,1024]{2,1,0:T(8,128)(2,1)S(1)} all-to-all(bf16[4,32,1024]{2,1,0:T(8,128)(2,1)S(1)} %broadcast_in_dim.10), channel_id=1, replica_groups=mesh['groups'=2,'expert'=4,'dp'=2,'pipe'=2] {'expert'}, dimensions={0} | all-to-all | bytes 524288 | tf_op jit(solution)/shard_map/all_to_all | solution.py:600
  85.1 3.1 %copy-done = bf16[3584,1024]{1,0:T(8,128)(2,1)S(1)} copy-done((bf16[3584,1024]{1,0:T(8,128)(2,1)S(1)}, bf16[3584,1024]{1,0:T(8,128)(2,1)}, u32[]{:S(2)}) %copy-start) | copy-done | bytes 7340056
  88.2 1.3 %shard_map.131 = (bf16[2,32,896]{2,1,0:T(8,128)(2,1)S(1)}, bf16[2,32,896]{2,1,0:T(8,128)(2,1)S(1)}) custom-call(bf16[4,64,128]{2,1,0:T(8,128)(2,1)S(1)} %get-tuple-element.32.picker, bf16[128,1024]{1,0:T(8,128)(2,1)S(1)} %bitcast.32, bf16[3584,1024]{1,0:T(8,128)(2,1)S(1)} %copy-done, bf16[128,1024]{1,0:T(8,128)(2,1)S(1)} %bitcast.33), custom_call_target="tpu_custom_call" | custom-call | tf_op jit(solution)/shard_map/pallas_call | solution.py:356
  89.6 0.1 collective-permute-start.17
  89.7 1.4 %shard_map.132 = (bf16[2,32,896]{2,1,0:T(8,128)(2,1)S(1)}, bf16[2,32,896]{2,1,0:T(8,128)(2,1)S(1)}) custom-call(bf16[4,64,128]{2,1,0:T(8,128)(2,1)S(1)} %get-tuple-element.32.picker, bf16[128,1024]{1,0:T(8,128)(2,1)S(1)} %bitcast.34, bf16[3584,1024]{1,0:T(8,128)(2,1)S(1)} %copy-done, bf16[2,32,896]{2,1,0:T(8,128)(2,1)S(1)} %get-tuple-element.49.before), custom_call_target="tpu_custom_call" | custom-call | tf_op jit(solution)/shard_map/pallas_call | solution.py:356
  91.0 0.6 collective-permute-start.19
  91.6 0.8 collective-permute-start.18
  92.5 0.1 collective-permute-done.19
  92.6 1.2 %collective-permute-start.21 = (bf16[2,32,896]{2,1,0:T(8,128)(2,1)S(1)}, bf16[2,32,896]{2,1,0:T(8,128)(2,1)S(1)}, u32[]{:S(2)}, u32[]{:S(2)}) collective-permute-start(bf16[2,32,896]{2,1,0:T(8,128)(2,1)S(1)} %add_convert_fusion.4.before.mine), channel_id=1, source_target_pairs={{0,2},{2,0},{1,3},{3,1},{4,6},{6,4},{5,7},{7,5},{8,10},{10,8},{9,1... | collective-permute-start | bytes 344072 | tf_op jit(solution)/shard_map/ppermute | solution.py:16
  93.8 3.4 %shard_map.133 = (bf16[3584,1024]{1,0:T(8,128)(2,1)}, f32[8,128]{1,0:T(8,128)S(1)}) custom-call(bf16[3584,128]{1,0:T(8,128)(2,1)S(1)} %copy-done.2, bf16[128,1024]{1,0:T(8,128)(2,1)S(1)} %bitcast.35, bf16[2,32,896]{2,1,0:T(8,128)(2,1)S(1)} %add_convert_fusion.4.before.mine), custom_call_target="tpu_custom_call" | custom-call | flops 939524096 | bytes 7340032 | tf_op jit(solution)/shard_map/pallas_call | solution.py:409
  97.3 0.4 collective-permute-done.18.other
  97.7 0.1 shard_map.134.rest_0_
  97.8 0.1 collective-permute-start.20
  97.9 1.3 %collective-permute-done.21.other = bf16[2,32,896]{2,1,0:T(8,128)(2,1)S(1)} collective-permute-done((bf16[2,32,896]{2,1,0:T(8,128)(2,1)S(1)}, bf16[2,32,896]{2,1,0:T(8,128)(2,1)S(1)}, u32[]{:S(2)}, u32[]{:S(2)}) %collective-permute-start.21) | collective-permute-done | bytes 114720 | tf_op jit(solution)/shard_map/ppermute | solution.py:16
  99.2 0.1 shard_map.135.rest_2_
  99.5 1.5 %collective-permute-done.22.rest_3_ = bf16[2,2,32,896]{3,2,1,0:T(8,128)(2,1)S(1)} collective-permute-done((bf16[2,2,32,896]{3,2,1,0:T(8,128)(2,1)S(1)}, bf16[2,2,32,896]{3,2,1,0:T(8,128)(2,1)S(1)}, u32[]{:S(2)}, u32[]{:S(2)}) %collective-permute-start.22) | collective-permute-done | bytes 229408 | tf_op jit(solution)/shard_map/ppermute | solution.py:16
  100.9 6.5 %shard_map.136 = (bf16[1024,3584]{1,0:T(8,128)(2,1)}, bf16[1024,3584]{1,0:T(8,128)(2,1)}) custom-call(bf16[4,64,128]{2,1,0:T(8,128)(2,1)S(1)} %get-tuple-element.32.picker, bf16[1024,128]{1,0:T(8,128)(2,1)S(1)} %get-tuple-element.46.before.tokens, bf16[2,2,32,896]{3,2,1,0:T(8,128)(2,1)S(1)} %shard_map.134.rest_0_, ...), custom_call_target="tpu_custom_call" | custom-call | flops 1879048192 | bytes 14680064 | tf_op jit(solution)/shard_map/pallas_call | solution.py:459
  (41 shorter events, 0.6 us)
Async XLA Ops:
  0.6 11.7 %collective-permute-start = (bf16[32,1024]{1,0:T(8,128)(2,1)}, bf16[32,1024]{1,0:T(8,128)(2,1)S(1)}, u32[]{:S(2)}, u32[]{:S(2)}) collective-permute-start(bf16[32,1024]{1,0:T(8,128)(2,1)} %param.9), channel_id=1, source_target_pairs={{0,4},{4,0},{8,12},{12,8},{1,5},{5,1},{9,13},{13,9},{2,6},{6,2},{1... | collective-permute-start | bytes 196616 | tf_op jit(solution)/shard_map/ppermute | solution.py:536
  3.7 9.2 %collective-permute-start.2 = (bf16[32,1024]{1,0:T(8,128)(2,1)}, bf16[32,1024]{1,0:T(8,128)(2,1)S(1)}, u32[]{:S(2)}, u32[]{:S(2)}) collective-permute-start(bf16[32,1024]{1,0:T(8,128)(2,1)} %param.9), channel_id=1, source_target_pairs={{0,12},{4,8},{8,4},{12,0},{1,13},{5,9},{9,5},{13,1},{2,14},{6,10},... | collective-permute-start | bytes 196616 | tf_op jit(solution)/shard_map/ppermute | solution.py:536
  6.2 6.7 %collective-permute-start.1 = (bf16[32,1024]{1,0:T(8,128)(2,1)}, bf16[32,1024]{1,0:T(8,128)(2,1)S(1)}, u32[]{:S(2)}, u32[]{:S(2)}) collective-permute-start(bf16[32,1024]{1,0:T(8,128)(2,1)} %param.9), channel_id=1, source_target_pairs={{0,8},{4,12},{8,0},{12,4},{1,9},{5,13},{9,1},{13,5},{2,10},{6,14},... | collective-permute-start | bytes 196616 | tf_op jit(solution)/shard_map/ppermute | solution.py:536
  6.4 5.9 %copy-start.3 = (bf16[32,1024]{1,0:T(8,128)(2,1)S(1)}, bf16[32,1024]{1,0:T(8,128)(2,1)}, u32[]{:S(2)}) copy-start(bf16[32,1024]{1,0:T(8,128)(2,1)} %param.9) | copy-start | bytes 196612
  14.6 2.3 %collective-permute-start.6 = (bf16[2,64,1792]{2,1,0:T(8,128)(2,1)S(1)}, bf16[2,64,1792]{2,1,0:T(8,128)(2,1)S(1)}, u32[]{:S(2)}, u32[]{:S(2)}) collective-permute-start(bf16[2,64,1792]{2,1,0:T(8,128)(2,1)S(1)} %get-tuple-element.41), channel_id=1, source_target_pairs={{0,1},{1,0},{2,3},{3,2},{4,5},{5,4},{6,7},{7,6},{8,9},{9,8},{10,11... | collective-permute-start | bytes 1376264 | tf_op jit(solution)/shard_map/ppermute | solution.py:16
  16.3 2.3 %collective-permute-start.3 = (bf16[2,64,1792]{2,1,0:T(8,128)(2,1)S(1)}, bf16[2,64,1792]{2,1,0:T(8,128)(2,1)S(1)}, u32[]{:S(2)}, u32[]{:S(2)}) collective-permute-start(bf16[2,64,1792]{2,1,0:T(8,128)(2,1)S(1)} %get-tuple-element.36), channel_id=1, source_target_pairs={{0,1},{1,0},{2,3},{3,2},{4,5},{5,4},{6,7},{7,6},{8,9},{9,8},{10,11... | collective-permute-start | bytes 1376264 | tf_op jit(solution)/shard_map/ppermute | solution.py:16
  17.0 11.3 %collective-permute-start.7 = (bf16[2,32,1792]{2,1,0:T(8,128)(2,1)S(1)}, bf16[2,32,1792]{2,1,0:T(8,128)(2,1)S(1)}, u32[]{:S(2)}, u32[]{:S(2)}) collective-permute-start(bf16[2,32,1792]{2,1,0:T(8,128)(2,1)S(1)} %slice.33), channel_id=1, source_target_pairs={{0,2},{2,0},{1,3},{3,1},{4,6},{6,4},{5,7},{7,5},{8,10},{10,8},{9,1... | collective-permute-start | bytes 688136 | tf_op jit(solution)/shard_map/ppermute | solution.py:16
  18.7 10.8 %collective-permute-start.10 = (bf16[2,32,1792]{2,1,0:T(8,128)(2,1)S(1)}, bf16[2,32,1792]{2,1,0:T(8,128)(2,1)S(1)}, u32[]{:S(2)}, u32[]{:S(2)}) collective-permute-start(bf16[2,32,1792]{2,1,0:T(8,128)(2,1)S(1)} %slice.37), channel_id=1, source_target_pairs={{0,2},{2,0},{1,3},{3,1},{4,6},{6,4},{5,7},{7,5},{8,10},{10,8},{9,1... | collective-permute-start | bytes 688136 | tf_op jit(solution)/shard_map/ppermute | solution.py:16
  23.8 20.1 %collective-permute-start.4 = (bf16[2,2,32,896]{3,2,1,0:T(8,128)(2,1)S(1)}, bf16[2,2,32,896]{3,2,1,0:T(8,128)(2,1)S(1)}, u32[]{:S(2)}, u32[]{:S(2)}) collective-permute-start(bf16[2,2,32,896]{3,2,1,0:T(8,128)(2,1)S(1)} %get-tuple-element.38), channel_id=1, source_target_pairs={{0,1},{1,0},{2,3},{3,2},{4,5},{5,4},{6,7},{7,6},{8,9},{9,8},{10,11... | collective-permute-start | bytes 688136 | tf_op jit(solution)/shard_map/ppermute | solution.py:16
  23.9 14.3 %slice-start = ((s8[7340032]{0:T(1024)(128)(4,1)}), s8[4194304]{0:T(1024)(128)(4,1)S(1)}, s32[]{:S(2)}) async-start(s8[7340032]{0:T(1024)(128)(4,1)} %bitcast.36), calls=%async_computation.3 | async-start | bytes 8388608
  23.9 14.4 %slice-start.1 = ((s8[7340032]{0:T(1024)(128)(4,1)}), s8[3145728]{0:T(1024)(128)(4,1)S(1)}, s32[]{:S(2)}) async-start(s8[7340032]{0:T(1024)(128)(4,1)} %bitcast.36), calls=%async_computation.4 | async-start | bytes 6291456
  27.8 8.4 %collective-permute-start.14 = (bf16[2,2,32,896]{3,2,1,0:T(8,128)(2,1)S(1)}, bf16[2,2,32,896]{3,2,1,0:T(8,128)(2,1)S(1)}, u32[]{:S(2)}, u32[]{:S(2)}) collective-permute-start(bf16[2,2,32,896]{3,2,1,0:T(8,128)(2,1)S(1)} %get-tuple-element.44), channel_id=1, source_target_pairs={{0,1},{1,0},{2,3},{3,2},{4,5},{5,4},{6,7},{7,6},{8,9},{9,8},{10,11... | collective-permute-start | bytes 688136 | tf_op jit(solution)/shard_map/ppermute | solution.py:16
  28.4 6.1 %collective-permute-start.8 = (bf16[32,1792]{1,0:T(8,128)(2,1)S(1)}, bf16[32,1792]{1,0:T(8,128)(2,1)S(1)}, u32[]{:S(2)}, u32[]{:S(2)}) collective-permute-start(bf16[32,1792]{1,0:T(8,128)(2,1)S(1)} %fusion.3), channel_id=1, source_target_pairs={{0,2},{2,0},{1,3},{3,1},{4,6},{6,4},{5,7},{7,5},{8,10},{10,8},{9,1... | collective-permute-start | bytes 344072 | tf_op jit(solution)/shard_map/ppermute | solution.py:16
  29.7 6.4 %collective-permute-start.11 = (bf16[32,1792]{1,0:T(8,128)(2,1)S(1)}, bf16[32,1792]{1,0:T(8,128)(2,1)S(1)}, u32[]{:S(2)}, u32[]{:S(2)}) collective-permute-start(bf16[32,1792]{1,0:T(8,128)(2,1)S(1)} %fusion.1), channel_id=1, source_target_pairs={{0,2},{2,0},{1,3},{3,1},{4,6},{6,4},{5,7},{7,5},{8,10},{10,8},{9,1... | collective-permute-start | bytes 344072 | tf_op jit(solution)/shard_map/ppermute | solution.py:16
  34.5 2.5 %collective-permute-start.9 = (bf16[64,1792]{1,0:T(8,128)(2,1)S(1)}, bf16[64,1792]{1,0:T(8,128)(2,1)S(1)}, u32[]{:S(2)}, u32[]{:S(2)}) collective-permute-start(bf16[64,1792]{1,0:T(8,128)(2,1)S(1)} %pad_maximum_fusion.refs_0_), channel_id=1, source_target_pairs={{0,1},{1,0},{2,3},{3,2},{4,5},{5,4},{6,7},{7,6},{8,9},{9,8},{10,11... | collective-permute-start | bytes 688136 | tf_op jit(solution)/shard_map/ppermute | solution.py:16
  36.1 1.6 %collective-permute-start.12 = (bf16[64,1792]{1,0:T(8,128)(2,1)S(1)}, bf16[64,1792]{1,0:T(8,128)(2,1)S(1)}, u32[]{:S(2)}, u32[]{:S(2)}) collective-permute-start(bf16[64,1792]{1,0:T(8,128)(2,1)S(1)} %pad_maximum_fusion.1.refs_2_), channel_id=1, source_target_pairs={{0,1},{1,0},{2,3},{3,2},{4,5},{5,4},{6,7},{7,6},{8,9},{9,8},{10,11... | collective-permute-start | bytes 688136 | tf_op jit(solution)/shard_map/ppermute | solution.py:16
  36.3 8.5 %collective-permute-start.15 = (bf16[2,2,32,896]{3,2,1,0:T(8,128)(2,1)S(1)}, bf16[2,2,32,896]{3,2,1,0:T(8,128)(2,1)S(1)}, u32[]{:S(2)}, u32[]{:S(2)}) collective-permute-start(bf16[2,2,32,896]{3,2,1,0:T(8,128)(2,1)S(1)} %add_convert_fusion.2.mine), channel_id=1, source_target_pairs={{0,2},{2,0},{1,3},{3,1},{4,6},{6,4},{5,7},{7,5},{8,10},{10,8},{9,1... | collective-permute-start | bytes 688136 | tf_op jit(solution)/shard_map/ppermute | solution.py:16
  40.1 12.9 %all-to-all-start = ((bf16[4,32,1024]{2,1,0:T(8,128)(2,1)}), bf16[4,32,1024]{2,1,0:T(8,128)(2,1)S(1)}, u32[]{:S(2)}, u32[]{:S(2)}) async-start(bf16[4,32,1024]{2,1,0:T(8,128)(2,1)} %bitcast.9), calls=%async_computation | async-start | bytes 524288 | tf_op jit(solution)/shard_map/all_to_all | solution.py:555
  43.9 9.3 %collective-permute-start.5 = (bf16[2,2,32,896]{3,2,1,0:T(8,128)(2,1)S(1)}, bf16[2,2,32,896]{3,2,1,0:T(8,128)(2,1)S(1)}, u32[]{:S(2)}, u32[]{:S(2)}) collective-permute-start(bf16[2,2,32,896]{3,2,1,0:T(8,128)(2,1)S(1)} %add_convert_fusion.3.mine), channel_id=1, source_target_pairs={{0,2},{2,0},{1,3},{3,1},{4,6},{6,4},{5,7},{7,5},{8,10},{10,8},{9,1... | collective-permute-start | bytes 688136 | tf_op jit(solution)/shard_map/ppermute | solution.py:16
  53.2 1.4 %collective-permute-start.16 = (bf16[2,32,896]{2,1,0:T(8,128)(2,1)S(1)}, bf16[2,32,896]{2,1,0:T(8,128)(2,1)S(1)}, u32[]{:S(2)}, u32[]{:S(2)}) collective-permute-start(bf16[2,32,896]{2,1,0:T(8,128)(2,1)S(1)} %get-tuple-element.45), channel_id=1, source_target_pairs={{0,1},{1,0},{2,3},{3,2},{4,5},{5,4},{6,7},{7,6},{8,9},{9,8},{10,11... | collective-permute-start | bytes 344072 | tf_op jit(solution)/shard_map/ppermute | solution.py:16
  53.4 1.5 %collective-permute-start.13 = (bf16[2,32,896]{2,1,0:T(8,128)(2,1)S(1)}, bf16[2,32,896]{2,1,0:T(8,128)(2,1)S(1)}, u32[]{:S(2)}, u32[]{:S(2)}) collective-permute-start(bf16[2,32,896]{2,1,0:T(8,128)(2,1)S(1)} %get-tuple-element.42), channel_id=1, source_target_pairs={{0,1},{1,0},{2,3},{3,2},{4,5},{5,4},{6,7},{7,6},{8,9},{9,8},{10,11... | collective-permute-start | bytes 344072 | tf_op jit(solution)/shard_map/ppermute | solution.py:16
  60.3 13.1 %all-to-all-start.1 = ((bf16[4,32,1024]{2,1,0:T(8,128)(2,1)}), bf16[4,32,1024]{2,1,0:T(8,128)(2,1)S(1)}, u32[]{:S(2)}, u32[]{:S(2)}) async-start(bf16[4,32,1024]{2,1,0:T(8,128)(2,1)} %bitcast.10), calls=%async_computation.1 | async-start | bytes 524288 | tf_op jit(solution)/shard_map/all_to_all | solution.py:555
  64.1 0.9 copy-start.1
  85.1 3.1 %copy-start = (bf16[3584,1024]{1,0:T(8,128)(2,1)S(1)}, bf16[3584,1024]{1,0:T(8,128)(2,1)}, u32[]{:S(2)}) copy-start(bf16[3584,1024]{1,0:T(8,128)(2,1)} %down.3) | copy-start | bytes 22020100
  88.2 5.6 %copy-start.2 = (bf16[3584,128]{1,0:T(8,128)(2,1)S(1)}, bf16[3584,128]{1,0:T(8,128)(2,1)}, u32[]{:S(2)}) copy-start(bf16[3584,128]{1,0:T(8,128)(2,1)} %copy-done.1) | copy-start | bytes 2752516
  89.6 2.0 %collective-permute-start.17 = (bf16[2,32,896]{2,1,0:T(8,128)(2,1)S(1)}, bf16[2,32,896]{2,1,0:T(8,128)(2,1)S(1)}, u32[]{:S(2)}, u32[]{:S(2)}) collective-permute-start(bf16[2,32,896]{2,1,0:T(8,128)(2,1)S(1)} %get-tuple-element.50), channel_id=1, source_target_pairs={{0,1},{1,0},{2,3},{3,2},{4,5},{5,4},{6,7},{7,6},{8,9},{9,8},{10,11... | collective-permute-start | bytes 344072 | tf_op jit(solution)/shard_map/ppermute | solution.py:16
  91.0 1.5 %collective-permute-start.19 = (bf16[2,32,896]{2,1,0:T(8,128)(2,1)S(1)}, bf16[2,32,896]{2,1,0:T(8,128)(2,1)S(1)}, u32[]{:S(2)}, u32[]{:S(2)}) collective-permute-start(bf16[2,32,896]{2,1,0:T(8,128)(2,1)S(1)} %get-tuple-element.54), channel_id=1, source_target_pairs={{0,1},{1,0},{2,3},{3,2},{4,5},{5,4},{6,7},{7,6},{8,9},{9,8},{10,11... | collective-permute-start | bytes 344072 | tf_op jit(solution)/shard_map/ppermute | solution.py:16
  91.6 6.1 %collective-permute-start.18 = (bf16[2,32,896]{2,1,0:T(8,128)(2,1)S(1)}, bf16[2,32,896]{2,1,0:T(8,128)(2,1)S(1)}, u32[]{:S(2)}, u32[]{:S(2)}) collective-permute-start(bf16[2,32,896]{2,1,0:T(8,128)(2,1)S(1)} %add_convert_fusion.5.mine), channel_id=1, source_target_pairs={{0,2},{2,0},{1,3},{3,1},{4,6},{6,4},{5,7},{7,5},{8,10},{10,8},{9,1... | collective-permute-start | bytes 344072 | tf_op jit(solution)/shard_map/ppermute | solution.py:16
  92.6 6.6 %collective-permute-start.21 = (bf16[2,32,896]{2,1,0:T(8,128)(2,1)S(1)}, bf16[2,32,896]{2,1,0:T(8,128)(2,1)S(1)}, u32[]{:S(2)}, u32[]{:S(2)}) collective-permute-start(bf16[2,32,896]{2,1,0:T(8,128)(2,1)S(1)} %add_convert_fusion.4.before.mine), channel_id=1, source_target_pairs={{0,2},{2,0},{1,3},{3,1},{4,6},{6,4},{5,7},{7,5},{8,10},{10,8},{9,1... | collective-permute-start | bytes 344072 | tf_op jit(solution)/shard_map/ppermute | solution.py:16
  97.8 1.6 %collective-permute-start.20 = (bf16[2,2,32,896]{3,2,1,0:T(8,128)(2,1)S(1)}, bf16[2,2,32,896]{3,2,1,0:T(8,128)(2,1)S(1)}, u32[]{:S(2)}, u32[]{:S(2)}) collective-permute-start(bf16[2,2,32,896]{3,2,1,0:T(8,128)(2,1)S(1)} %shard_map.134.rest_0_), channel_id=1, source_target_pairs={{0,1},{1,0},{2,3},{3,2},{4,5},{5,4},{6,7},{7,6},{8,9},{9,8},{10,11... | collective-permute-start | bytes 688136 | tf_op jit(solution)/shard_map/ppermute | solution.py:16
  99.4 1.6 %collective-permute-start.22 = (bf16[2,2,32,896]{3,2,1,0:T(8,128)(2,1)S(1)}, bf16[2,2,32,896]{3,2,1,0:T(8,128)(2,1)S(1)}, u32[]{:S(2)}, u32[]{:S(2)}) collective-permute-start(bf16[2,2,32,896]{3,2,1,0:T(8,128)(2,1)S(1)} %shard_map.135.rest_2_), channel_id=1, source_target_pairs={{0,1},{1,0},{2,3},{3,2},{4,5},{5,4},{6,7},{7,6},{8,9},{9,8},{10,11... | collective-permute-start | bytes 688136 | tf_op jit(solution)/shard_map/ppermute | solution.py:16

commit v8 on v6

--- a/solution.py
+++ b/solution.py
@@ -65,11 +65,9 @@
     far_routes,
     far_shares,
     gate,
-    up,
     picker,
     weights,
     gate_out,
-    up_out,
     routes,
     shares,
     sems,
@@ -81,7 +79,7 @@
     ]
     for copy in tables:
         copy.start()
-    copies = load_start(((gate, gate_out), (up, up_out)), sems, 8)
+    copies = load_start(((gate, gate_out),), sems, 8)
     for copy in tables:
         copy.wait()
     rank, dp, pipe = place[0], place[1], place[2]
@@ -114,94 +112,82 @@
         copy.wait()
 
 
-def prepare(place, routes, shares, gate, up, ranks, dps, pipes, block, experts):
+def prepare(place, routes, shares, gate, ranks, dps, pipes, block, experts):
     assert experts <= 8
     capacity = block // 2
     token_count = block * ranks
     slots = capacity * ranks
     return pl.pallas_call(
         functools.partial(prepare_kernel, ranks, capacity, dps, pipes),
-        in_specs=[scalars(), in_hbm(), in_hbm(), in_hbm(), in_hbm()],
-        out_specs=(whole(), whole(), whole(), whole()),
+        in_specs=[scalars(), in_hbm(), in_hbm(), in_hbm()],
+        out_specs=(whole(), whole(), whole()),
         out_shape=(
             jax.ShapeDtypeStruct((experts, slots, token_count), BF),
             jax.ShapeDtypeStruct((experts, slots, 1), F32),
             pltpu.VMEM(gate.shape, BF),
-            pltpu.VMEM(up.shape, BF),
         ),
         scratch_shapes=[
             pltpu.VMEM(routes.shape, routes.dtype),
             pltpu.VMEM(shares.shape, shares.dtype),
-            pltpu.SemaphoreType.DMA((2, 8)),
+            pltpu.SemaphoreType.DMA((1, 8)),
             pltpu.SemaphoreType.DMA((2,)),
         ],
         compiler_params=pltpu.CompilerParams(vmem_limit_bytes=8 * 1024 * 1024),
         cost_estimate=pl.CostEstimate(
-            flops=0, bytes_accessed=4 * gate.size, transcendentals=0
-        ),
-    )(place, far(routes), far(shares), far(gate), far(up))
-
-
-def residual_kernel(ranks, *refs):
-    student = refs[0][...].astype(F32)
-    target = refs[ranks][...].astype(F32)
-    for i in range(1, ranks):
-        student = student + refs[i][...].astype(F32)
-        target = target + refs[ranks + i][...].astype(F32)
+            flops=0, bytes_accessed=8 * gate.size, transcendentals=0
+        ),
+    )(place, far(routes), far(shares), far(gate))
+
+
+def residual_kernel(counts, *refs):
+    sums = []
+    at = 0
+    for count in counts:
+        total = refs[at][...].astype(F32)
+        for i in range(1, count):
+            total = total + refs[at + i][...].astype(F32)
+        sums.append(total)
+        at += count
+    student, target = sums
     refs[-2][...] = student.astype(BF)
     refs[-1][...] = (student - target).astype(BF)
 
 
 def residual_of(student, target, before):
-    ranks = len(student)
     block = jax.ShapeDtypeStruct(student[0].shape, BF)
     return pl.pallas_call(
-        functools.partial(residual_kernel, ranks),
-        in_specs=[whole()] * (2 * ranks) + [anywhere()] * len(before),
+        functools.partial(residual_kernel, (len(student), len(target))),
+        in_specs=[whole()] * (len(student) + len(target)) + [anywhere()] * len(before),
         out_specs=(whole(), whole()),
         out_shape=(block, block),
         compiler_params=pltpu.CompilerParams(vmem_limit_bytes=4 * 1024 * 1024),
     )(*student, *target, *before)
 
 
-def tile_of(size):
-    return 256 if size % 256 == 0 else 128
-
-
-def teacher_kernel(first, size, dps, pipes, place, tokens, gate, up, keep, send):
+def order_kernel(dps, pipes, place, tokens, *rest):
+    out = rest[-1]
     dp, pipe = place[1], place[2]
     rows = tokens.shape[0] // (dps * pipes)
-    half = dps * rows
-    parts = []
+    at = 0
     for j1 in range(pipes):
         for j0 in range(dps):
             piece = lax.rem(pipe + j1, pipes) * dps + lax.rem(dp + j0, dps)
-            parts.append(tokens[pl.ds(pl.multiple_of(piece * rows, rows), rows), :])
-    ordered = jnp.concatenate(parts, axis=0)
-    tile = tile_of(size)
-    for which, weight in enumerate((gate, up)):
-        for i in range(size // tile):
-            product = dot(ordered, weight[:, first + i * tile : first + (i + 1) * tile]).astype(BF)
-            keep[which, :, i * tile : (i + 1) * tile] = product[:half]
-            send[which, :, i * tile : (i + 1) * tile] = product[half:]
-
-
-def teacher_pre(place, tokens, gate, up, first, size, dps, pipes):
-    token_count, width = tokens.shape
-    half = jax.ShapeDtypeStruct((2, token_count // pipes, size), BF)
-    return pl.pallas_call(
-        functools.partial(teacher_kernel, first, size, dps, pipes),
-        in_specs=[scalars(), whole(), whole(), whole()],
-        out_specs=(whole(), whole()),
-        out_shape=(half, half),
-        compiler_params=pltpu.CompilerParams(vmem_limit_bytes=8 * 1024 * 1024),
-        cost_estimate=pl.CostEstimate(
-            flops=4 * token_count * width * size, bytes_accessed=4 * width * size, transcendentals=0
-        ),
-    )(place, tokens, gate, up)
-
-
-def expert_kernel(first, picker, tokens, gate, up, before, keep, send, held, sems):
+            out[at : at + rows, :] = tokens[pl.ds(pl.multiple_of(piece * rows, rows), rows), :]
+            at += rows
+
+
+def order(place, tokens, before, dps, pipes):
+    return pl.pallas_call(
+        functools.partial(order_kernel, dps, pipes),
+        in_specs=[scalars(), whole()] + [anywhere()] * len(before),
+        out_specs=whole(),
+        out_shape=jax.ShapeDtypeStruct(tokens.shape, BF),
+        compiler_params=pltpu.CompilerParams(vmem_limit_bytes=4 * 1024 * 1024),
+    )(place, tokens, *before)
+
+
+def expert_kernel(first, picker, tokens, gate, up, *rest):
+    keep, send, held, sems = rest[-4:]
     half = keep.shape[2]
     count = keep.shape[0]
     pieces = sems.shape[2]
@@ -232,7 +218,7 @@
     halves = jax.ShapeDtypeStruct((count, 2, slots // 2, H), BF)
     return pl.pallas_call(
         functools.partial(expert_kernel, first),
-        in_specs=[whole(), whole(), in_hbm(), in_hbm(), anywhere()],
+        in_specs=[whole(), whole(), in_hbm(), in_hbm()] + [anywhere()] * len(before),
         out_specs=(whole(), whole()),
         out_shape=(halves, halves),
         scratch_shapes=[
@@ -245,7 +231,7 @@
             bytes_accessed=count * 4 * width * H,
             transcendentals=0,
         ),
-    )(picker, tokens, far(gate), far(up), before)
+    )(picker, tokens, far(gate), far(up), *before)
 
 
 def hidden_act_kernel(first, swap, mine, other, weight, *rest):
@@ -278,31 +264,30 @@
     )(mine, other, weight, *before)
 
 
-def join_kernel(dps, pipes, place, *refs):
+def join_kernel(ranks, dps, pipes, place, *refs):
     out = refs[-1]
-    dp, pipe = place[1], place[2]
-    rows = out.shape[0] // (dps * pipes)
-    at = 0
-    for i in range((len(refs) - 1) // 2):
-        size = refs[2 * i].shape[1]
+    rank, dp, pipe = place[0], place[1], place[2]
+    chunks = (len(refs) - 1) // 2
+    chunk_rows = out.shape[0] // chunks
+    rows = chunk_rows // (dps * pipes)
+    for i in range(chunks):
+        chunk = lax.rem(rank // (ranks // chunks) + i, chunks)
         for j1 in range(pipes):
             for j0 in range(dps):
                 piece = lax.rem(pipe + j1, pipes) * dps + lax.rem(dp + j0, dps)
-                target = pl.ds(pl.multiple_of(piece * rows, rows), rows)
-                out[target, at : at + size] = refs[2 * i + j1][j0 * rows : (j0 + 1) * rows, :]
-        at += size
-
-
-def join(place, parts, dps, pipes):
+                at = pl.multiple_of(chunk * chunk_rows + piece * rows, rows)
+                out[pl.ds(at, rows), :] = refs[2 * i + j1][j0 * rows : (j0 + 1) * rows, :]
+
+
+def join(place, parts, ranks, dps, pipes):
     assert pipes == 2
     flat = [value for pair in parts for value in pair]
-    rows = flat[0].shape[0] * pipes
-    width = sum(pair[0].shape[1] for pair in parts)
-    return pl.pallas_call(
-        functools.partial(join_kernel, dps, pipes),
+    rows, width = flat[0].shape
+    return pl.pallas_call(
+        functools.partial(join_kernel, ranks, dps, pipes),
         in_specs=[scalars()] + [whole()] * len(flat),
         out_specs=whole(),
-        out_shape=jax.ShapeDtypeStruct((rows, width), BF),
+        out_shape=jax.ShapeDtypeStruct((rows * len(flat), width), BF),
         compiler_params=pltpu.CompilerParams(vmem_limit_bytes=8 * 1024 * 1024),
     )(place, *flat)
 
@@ -543,13 +528,14 @@
     def source_of(s):
         return rank ^ s if paired else (rank + ranks - s) % ranks
 
-    def gather_tokens(mine):
-        whole_rows = jnp.zeros((token_count, mine.shape[1]), BF)
-        whole_rows = lax.dynamic_update_slice(whole_rows, mine, (rank * block, 0))
-        for s in range(1, ranks):
-            theirs = to_partner(mine, s)
-            whole_rows = lax.dynamic_update_slice(whole_rows, theirs, (source_of(s) * block, 0))
-        return whole_rows
+    def place_rows(blocks):
+        rows = jnp.zeros((token_count, blocks[0].shape[1]), BF)
+        for s, value in enumerate(blocks):
+            rows = lax.dynamic_update_slice(rows, value, (source_of(s) * block, 0))
+        return rows
+
+    def gather_blocks(mine):
+        return [mine] + [to_partner(mine, s) for s in range(1, ranks)]
 
     def to_owners(product):
         def block_of(r):
@@ -557,25 +543,60 @@
 
         return [block_of(rank)] + [to_partner(block_of(target_of(s)), s) for s in range(1, ranks)]
 
-    base = gather_tokens(tokens)
-    picker, slot_weight, gate_near, up_near = prepare(
-        place, routes.T, gate_weights.T, teacher_gate, teacher_up, ranks, dps, pipes, block, experts
+    def to_owners_in_steps(product):
+        blocks = product.reshape(ranks, block, width)
+        mask = 1
+        seen = None
+        while mask < ranks:
+            blocks = blocks.reshape(-1, 2, block, width)
+            bit = rank // mask % 2
+            keep = lax.dynamic_index_in_dim(blocks, bit, 1, keepdims=False)
+            send = lax.dynamic_index_in_dim(blocks, 1 - bit, 1, keepdims=False)
+            received = to_partner(send, mask)
+            seen = received if seen is None else seen
+            last = (keep[0], received[0])
+            blocks = add(keep, received)
+            mask *= 2
+        return list(last), seen
+
+    blocks = gather_blocks(tokens)
+    base = place_rows(blocks)
+    picker, slot_weight, gate_near = prepare(
+        place, routes.T, gate_weights.T, teacher_gate, ranks, dps, pipes, block, experts
     )
 
-    chunks = 2 if teacher_gate.shape[1] % 512 == 0 else 1
-    size = teacher_gate.shape[1] // chunks
+    halved = paired and ranks > 2 and token_count // 2 % (16 * dps * pipes) == 0
+    if halved:
+        near = jnp.zeros((token_count // 2, width), BF)
+        for s in range(ranks // 2):
+            near = lax.dynamic_update_slice(
+                near, blocks[s], (source_of(s) % (ranks // 2) * block, 0)
+            )
+        start = (1 - rank // (ranks // 2)) * (token_count // 2)
+        chunks = [near, lax.dynamic_slice_in_dim(base, start, token_count // 2, axis=0)]
+    else:
+        chunks = [base]
     halves = []
-    for i in range(chunks):
-        keep, send = teacher_pre(place, base, gate_near, up_near, i * size, size, dps, pipes)
+    before = []
+    for chunk in chunks:
+        ordered = order(place, chunk, before, dps, pipes)
+        products = [
+            jnp.dot(ordered, weight, preferred_element_type=F32).astype(BF)
+            for weight in (gate_near, teacher_up)
+        ]
+        cut = chunk.shape[0] // pipes
+        keep = jnp.stack([value[:cut] for value in products])
+        send = jnp.stack([value[cut:] for value in products])
         halves.append(add(keep, shift(send, "pipe", pipes, 1)))
+        before = halves[-1:]
 
     group = 2 if experts % 2 == 0 else 1
     firsts = range(0, experts, group)
     parts = []
-    last = halves[-1]
+    before = halves
     for first in firsts:
-        keep, send = expert_pre(picker, base, expert_gate, expert_up, last, first, group)
-        last = keep
+        keep, send = expert_pre(picker, base, expert_gate, expert_up, before, first, group)
+        before = [keep]
         parts.append((keep, shift(send, "pipe", pipes, 1)))
     hiddens = []
     for half in halves:
@@ -583,13 +604,18 @@
         hidden = (jax.nn.silu(total[0]) * total[1]).astype(BF)
         hidden = jnp.concatenate(gather_dp_parts(hidden, dps), axis=0)
         hiddens.append((hidden, shift(hidden, "pipe", pipes, 1)))
-    hidden = join(place, hiddens, dps, pipes)
-    target = to_owners(jnp.dot(hidden, teacher_down, preferred_element_type=F32).astype(BF))
+    hidden = join(place, hiddens, ranks, dps, pipes)
+    product = jnp.dot(hidden, teacher_down, preferred_element_type=F32).astype(BF)
+    if paired and ranks > 1:
+        target, seen = to_owners_in_steps(product)
+    else:
+        target = to_owners(product)
+        seen = target[-1]
 
     pre, weighted = [], []
     for first, (keep, theirs) in zip(firsts, parts):
         mine, other = exchange_dp(add(keep, theirs), dps)
-        total, part = hidden_act(mine, other, dps == 2, slot_weight, target[-2:], first)
+        total, part = hidden_act(mine, other, dps == 2, slot_weight, [seen], first)
         pre.append(total)
         weighted.append(jnp.concatenate([part, shift(part, "pipe", pipes, 1)], axis=1))
     weighted = jnp.concatenate(weighted, axis=0)
@@ -599,7 +625,7 @@
     student = to_owners(product)
     dense_flipped, base_flipped = flip(dense, base, product)
     student_out, residual = residual_of(student, target, (base_flipped,))
-    residual = gather_tokens(residual)
+    residual = place_rows(gather_blocks(residual))
 
     sums = []
     last = residual

time: 91.3 us -> 111 us (1.22)
  matrix products: 2.24 us -> 14.4 us
  waiting for transfers between devices: 25.3 us -> 32.3 us
  Pallas kernels: 32.2 us -> 28.1 us
  starting transfers between devices: 29 us -> 32.6 us
  local copies, waits for them, and re-layouts: 0.24 us -> 1.39 us
    dot_general x0 -> x4, matrix products: none -> 8.9 us  [body(): jnp.dot(ordered, weight, preferred_element_type=F32).astype(BF)]
    ppermute x20, waiting for transfers between devices: 10 us -> 14.6 us  [shift(): lax.ppermute(value, axis, [(i, (i + by) % count) for i in range(count)])]
    dot_general x1, matrix products: 1.12 us -> 4.42 us  [body(): product = jnp.dot(dense, expert_down, preferred_element_type=F32).astype(BF)]
    ppermute x12 -> x11, starting transfers between devices: 17.4 us -> 19.9 us  [to_partner(): return lax.ppermute(value, 'expert', [(i, i ^ s) for i in range(ranks)])]
    ppermute x12 -> x11, waiting for transfers between devices: 15.3 us -> 17.7 us  [to_partner(): return lax.ppermute(value, 'expert', [(i, i ^ s) for i in range(ranks)])]
    pallas_call x4, Pallas kernels: 4.61 us -> 2.41 us  [the longest x2 1.12 us: order(): pl.pallas_call(functools.partial(order_kernel, dps, pipes), in_specs=[sca...]
    pallas_call x1, Pallas kernels: 5.89 us -> 3.99 us  [prepare(): pl.pallas_call(functools.partial(prepare_kernel, ranks, capacity, dps, pi...]
  transfers between devices with their start and end apart: 32 -> 31, of which waited for: 17 -> 12; matrix products, arithmetic and copies ran while one was open for 4% -> 6% of each run, Pallas kernels for 24% -> 17%
where the time goes in v8:
time: 111 us
  starting transfers between devices  32.6 us (29%)
  waiting for transfers between devices  32.3 us (29%)
  Pallas kernels  28.1 us (25%)
  matrix products  14.4 us (13%)
  between operations  1.43 us (1%)
  local copies, waits for them, and re-layouts  1.39 us (1%)
    ppermute x11, starting transfers between devices, to_partner(): return lax.ppermute(value, 'expert', [(i, i ^ s) for i in range(ranks)])  19.9 us
    ppermute x11, waiting for transfers between devices, to_partner(): return lax.ppermute(value, 'expert', [(i, i ^ s) for i in range(ranks)])  17.7 us
    ppermute x20, waiting for transfers between devices, shift(): lax.ppermute(value, axis, [(i, (i + by) % count) for i in range(count)])  14.6 us
    ppermute x20, starting transfers between devices, shift(): lax.ppermute(value, axis, [(i, (i + by) % count) for i in range(count)])  12.7 us
    dot_general x4, matrix products, body(): jnp.dot(ordered, weight, preferred_element_type=F32).astype(BF)  8.9 us
    pallas_call x2, Pallas kernels, expert_pre(): pl.pallas_call(functools.partial(expert_kernel, first), in_specs=[whole()...  7.72 us
    pallas_call x1, Pallas kernels, input_grads(): pl.pallas_call(functools.partial(input_grad_kernel, count // len(parts)),...  6.5 us
    dot_general x1, matrix products, body(): product = jnp.dot(dense, expert_down, preferred_element_type=F32).astype(BF)  4.42 us
  transfers between devices with their start and end apart: 31, of which 12 were waited for; matrix products, arithmetic and copies ran while one was open for 6% of the time, Pallas kernels for 17%

profile of v8, /device:TPU:0, one launch (start us, length us, event | category | flops | bytes accessed | tf_op | source)
XLA Modules:
  0.0 111.1 jit_solution(2423632742866525751)
XLA Ops:
  0.6 3.1 %collective-permute-start = (bf16[32,1024]{1,0:T(8,128)(2,1)}, bf16[32,1024]{1,0:T(8,128)(2,1)S(1)}, u32[]{:S(2)}, u32[]{:S(2)}) collective-permute-start(bf16[32,1024]{1,0:T(8,128)(2,1)} %param.9), channel_id=1, source_target_pairs={{0,4},{4,0},{8,12},{12,8},{1,5},{5,1},{9,13},{13,9},{2,6},{6,2},{1... | collective-permute-start | bytes 196616 | tf_op jit(solution)/shard_map/ppermute | solution.py:522
  3.7 0.1 pad_add_fusion.place
  3.8 4.0 %shard_map.120 = (bf16[4,64,128]{2,1,0:T(8,128)(2,1)S(1)}, f32[4,64,1]{2,1,0:T(8,128)S(1)}, bf16[1024,3584]{1,0:T(8,128)(2,1)S(1)}) custom-call(s32[3]{0:T(128)S(1)} %pad_add_fusion.place, s32[4,128]{1,0:T(4,128)} %bitcast.73, f32[4,128]{1,0:T(4,128)} %bitcast.74, bf16[1024,3584]{1,0:T(8,128)(2,1)} %gate.3), custom_call_target="tpu_custom_call" | custom-call | bytes 29360128 | tf_op jit(solution)/shard_map/pallas_call | solution.py:120
  7.9 0.6 shard_map.121
  8.5 0.9 copy-done.1
  9.5 1.4 %convolution_convert_fusion.2 = bf16[64,3584]{1,0:T(8,128)(2,1)S(1)} fusion(bf16[64,1024]{1,0:T(8,128)(2,1)S(1)} %shard_map.121, bf16[1024,3584]{1,0:T(8,128)(2,1)S(1)} %copy-done.1), kind=kOutput, calls=%fused_computation.2 | convolution fusion | flops 469991424 | bytes 7929856 | tf_op jit(solution)/shard_map/dot_general | solution.py:584
  10.8 1.4 %convolution_convert_fusion.3 = bf16[64,3584]{1,0:T(8,128)(2,1)S(1)} fusion(bf16[64,1024]{1,0:T(8,128)(2,1)S(1)} %shard_map.121, bf16[1024,3584]{1,0:T(8,128)(2,1)S(1)} %get-tuple-element.28), kind=kOutput, calls=%fused_computation.3 | convolution fusion | flops 469991424 | bytes 7929856 | tf_op jit(solution)/shard_map/dot_general | solution.py:584
  12.4 2.7 %collective-permute-start.1 = (bf16[32,1024]{1,0:T(8,128)(2,1)S(1)}, bf16[32,1024]{1,0:T(8,128)(2,1)S(1)}, u32[]{:S(2)}, u32[]{:S(2)}) collective-permute-start(bf16[32,1024]{1,0:T(8,128)(2,1)S(1)} %copy-done.2), channel_id=1, source_target_pairs={{0,8},{4,12},{8,0},{12,4},{1,9},{5,13},{9,1},{13,5},{2,10},{6,14},... | collective-permute-start | bytes 196616 | tf_op jit(solution)/shard_map/ppermute | solution.py:522
  15.1 4.0 %collective-permute-done.1 = bf16[32,1024]{1,0:T(8,128)(2,1)S(1)} collective-permute-done((bf16[32,1024]{1,0:T(8,128)(2,1)S(1)}, bf16[32,1024]{1,0:T(8,128)(2,1)S(1)}, u32[]{:S(2)}, u32[]{:S(2)}) %collective-permute-start.1) | collective-permute-done | bytes 65568 | tf_op jit(solution)/shard_map/ppermute | solution.py:522
  19.1 2.1 %collective-permute-done.2 = bf16[32,1024]{1,0:T(8,128)(2,1)S(1)} collective-permute-done((bf16[32,1024]{1,0:T(8,128)(2,1)S(1)}, bf16[32,1024]{1,0:T(8,128)(2,1)S(1)}, u32[]{:S(2)}, u32[]{:S(2)}) %collective-permute-start.2) | collective-permute-done | bytes 65568 | tf_op jit(solution)/shard_map/ppermute | solution.py:522
  21.3 0.1 add_convert_fusion.1.rest_0_
  21.4 0.6 shard_map.122
  22.0 4.8 %convolution_convert_fusion.1 = bf16[64,3584]{1,0:T(8,128)(2,1)S(1)} fusion(bf16[64,1024]{1,0:T(8,128)(2,1)S(1)} %shard_map.122, bf16[1024,3584]{1,0:T(8,128)(2,1)} %copy-done), kind=kOutput, calls=%fused_computation.1 | convolution fusion | flops 469991424 | bytes 7929856 | tf_op jit(solution)/shard_map/dot_general | solution.py:584
  26.8 1.4 %convolution_convert_fusion = bf16[64,3584]{1,0:T(8,128)(2,1)S(1)} fusion(bf16[64,1024]{1,0:T(8,128)(2,1)S(1)} %shard_map.122, bf16[1024,3584]{1,0:T(8,128)(2,1)S(1)} %bitcast.68), kind=kOutput, calls=%fused_computation | convolution fusion | flops 469991424 | bytes 7929856 | tf_op jit(solution)/shard_map/dot_general | solution.py:584
  28.2 1.6 %collective-permute-start.7 = (bf16[2,16,3584]{2,1,0:T(8,128)(2,1)S(1)}, bf16[2,16,3584]{2,1,0:T(8,128)(2,1)S(1)}, u32[]{:S(2)}, u32[]{:S(2)}) collective-permute-start(bf16[2,16,3584]{2,1,0:T(8,128)(2,1)S(1)} %slice.73), channel_id=1, source_target_pairs={{0,2},{2,0},{1,3},{3,1},{4,6},{6,4},{5,7},{7,5},{8,10},{10,8},{9,1... | collective-permute-start | bytes 688136 | tf_op jit(solution)/shard_map/ppermute | solution.py:16
  30.0 4.9 %collective-permute-done.7 = bf16[2,16,3584]{2,1,0:T(8,128)(2,1)S(1)} collective-permute-done((bf16[2,16,3584]{2,1,0:T(8,128)(2,1)S(1)}, bf16[2,16,3584]{2,1,0:T(8,128)(2,1)S(1)}, u32[]{:S(2)}, u32[]{:S(2)}) %collective-permute-start.7) | collective-permute-done | bytes 229408 | tf_op jit(solution)/shard_map/ppermute | solution.py:16
  34.9 0.1 fusion.4
  35.0 1.6 %collective-permute-start.8 = (bf16[16,3584]{1,0:T(8,128)(2,1)S(1)}, bf16[16,3584]{1,0:T(8,128)(2,1)S(1)}, u32[]{:S(2)}, u32[]{:S(2)}) collective-permute-start(bf16[16,3584]{1,0:T(8,128)(2,1)S(1)} %fusion.4), channel_id=1, source_target_pairs={{0,2},{2,0},{1,3},{3,1},{4,6},{6,4},{5,7},{7,5},{8,10},{10,8},{9,1... | collective-permute-start | bytes 344072 | tf_op jit(solution)/shard_map/ppermute | solution.py:16
  36.6 0.1 add_convert_fusion.rest_1_
  36.7 0.6 collective-permute-start.10
  37.3 3.6 %collective-permute-done.8 = bf16[16,3584]{1,0:T(8,128)(2,1)S(1)} collective-permute-done((bf16[16,3584]{1,0:T(8,128)(2,1)S(1)}, bf16[16,3584]{1,0:T(8,128)(2,1)S(1)}, u32[]{:S(2)}, u32[]{:S(2)}) %collective-permute-start.8) | collective-permute-done | bytes 114720 | tf_op jit(solution)/shard_map/ppermute | solution.py:16
  41.0 3.9 %shard_map.123 = (bf16[2,2,32,896]{3,2,1,0:T(8,128)(2,1)S(1)}, bf16[2,2,32,896]{3,2,1,0:T(8,128)(2,1)S(1)}) custom-call(bf16[4,64,128]{2,1,0:T(8,128)(2,1)S(1)} %get-tuple-element.27.picker, bf16[128,1024]{1,0:T(8,128)(2,1)S(1)} %constant_dynamic-update-slice_fusion.6.tokens, bf16[1024,3584]{1,0:T(8,128)(2,1)} %gate.5, bf16[1024,3584]{1,0:T(8,128)(2,1)} %up.3, ...), custom_call_target="tpu_custom_call" | custom-call | flops 469762048 | bytes 7340032 | tf_op jit(solution)/shard_map/pallas_call | solution.py:219
  44.9 0.5 collective-permute-start.5
  45.5 3.9 %shard_map.126 = (bf16[2,2,32,896]{3,2,1,0:T(8,128)(2,1)S(1)}, bf16[2,2,32,896]{3,2,1,0:T(8,128)(2,1)S(1)}) custom-call(bf16[4,64,128]{2,1,0:T(8,128)(2,1)S(1)} %get-tuple-element.27.picker, bf16[128,1024]{1,0:T(8,128)(2,1)S(1)} %constant_dynamic-update-slice_fusion.6.tokens, bf16[1024,3584]{1,0:T(8,128)(2,1)} %gate.5, bf16[1024,3584]{1,0:T(8,128)(2,1)} %up.3, ...), custom_call_target="tpu_custom_call" | custom-call | flops 469762048 | bytes 7340032 | tf_op jit(solution)/shard_map/pallas_call | solution.py:219
  49.3 0.1 collective-permute-start.15
  49.5 0.1 fusion.2
  49.6 1.4 %collective-permute-start.11 = (bf16[16,3584]{1,0:T(8,128)(2,1)S(1)}, bf16[16,3584]{1,0:T(8,128)(2,1)S(1)}, u32[]{:S(2)}, u32[]{:S(2)}) collective-permute-start(bf16[16,3584]{1,0:T(8,128)(2,1)S(1)} %fusion.2), channel_id=1, source_target_pairs={{0,2},{2,0},{1,3},{3,1},{4,6},{6,4},{5,7},{7,5},{8,10},{10,8},{9,1... | collective-permute-start | bytes 344072 | tf_op jit(solution)/shard_map/ppermute | solution.py:16
  51.0 1.3 %collective-permute-start.16 = (bf16[2,2,32,896]{3,2,1,0:T(8,128)(2,1)S(1)}, bf16[2,2,32,896]{3,2,1,0:T(8,128)(2,1)S(1)}, u32[]{:S(2)}, u32[]{:S(2)}) collective-permute-start(bf16[2,2,32,896]{3,2,1,0:T(8,128)(2,1)S(1)} %add_convert_fusion.2.mine), channel_id=1, source_target_pairs={{0,2},{2,0},{1,3},{3,1},{4,6},{6,4},{5,7},{7,5},{8,10},{10,8},{9,1... | collective-permute-start | bytes 688136 | tf_op jit(solution)/shard_map/ppermute | solution.py:16
  52.3 3.3 %collective-permute-done.11 = bf16[16,3584]{1,0:T(8,128)(2,1)S(1)} collective-permute-done((bf16[16,3584]{1,0:T(8,128)(2,1)S(1)}, bf16[16,3584]{1,0:T(8,128)(2,1)S(1)}, u32[]{:S(2)}, u32[]{:S(2)}) %collective-permute-start.11) | collective-permute-done | bytes 114720 | tf_op jit(solution)/shard_map/ppermute | solution.py:16
  55.7 1.4 %collective-permute-start.6 = (bf16[2,2,32,896]{3,2,1,0:T(8,128)(2,1)S(1)}, bf16[2,2,32,896]{3,2,1,0:T(8,128)(2,1)S(1)}, u32[]{:S(2)}, u32[]{:S(2)}) collective-permute-start(bf16[2,2,32,896]{3,2,1,0:T(8,128)(2,1)S(1)} %add_convert_fusion.3.mine), channel_id=1, source_target_pairs={{0,2},{2,0},{1,3},{3,1},{4,6},{6,4},{5,7},{7,5},{8,10},{10,8},{9,1... | collective-permute-start | bytes 688136 | tf_op jit(solution)/shard_map/ppermute | solution.py:16
  57.1 0.6 shard_map.124
  57.8 1.1 %convolution_convert_fusion.5 = bf16[128,1024]{1,0:T(8,128)(2,1)S(1)} fusion(bf16[128,3584]{1,0:T(8,128)(2,1)S(1)} %shard_map.124, bf16[3584,1024]{1,0:T(8,128)(2,1)S(1)} %bitcast.70), kind=kOutput, calls=%fused_computation.5 | convolution fusion | flops 939655168 | bytes 8519680 | tf_op jit(solution)/shard_map/dot_general | solution.py:608
  59.0 2.8 %collective-permute-start.13 = (bf16[2,32,1024]{2,1,0:T(8,128)(2,1)S(1)}, bf16[2,32,1024]{2,1,0:T(8,128)(2,1)S(1)}, u32[]{:S(2)}, u32[]{:S(2)}) collective-permute-start(bf16[2,32,1024]{2,1,0:T(8,128)(2,1)S(1)} %dynamic-slice_bitcast_fusion), channel_id=1, source_target_pairs={{0,4},{4,0},{8,12},{12,8},{1,5},{5,1},{9,13},{13,9},{2,6},{6,2},{1... | collective-permute-start | bytes 393224 | tf_op jit(solution)/shard_map/ppermute | solution.py:522
  61.7 3.9 %collective-permute-done.13.rest_0_ = bf16[2,32,1024]{2,1,0:T(8,128)(2,1)S(1)} collective-permute-done((bf16[2,32,1024]{2,1,0:T(8,128)(2,1)S(1)}, bf16[2,32,1024]{2,1,0:T(8,128)(2,1)S(1)}, u32[]{:S(2)}, u32[]{:S(2)}) %collective-permute-start.13) | collective-permute-done | bytes 131104 | tf_op jit(solution)/shard_map/ppermute | solution.py:522
  65.6 0.1 shard_map.127
  65.8 0.1 shard_map.125
  65.9 0.5 collective-permute-start.14
  66.5 2.5 %collective-permute-start.21 = (bf16[1,32,1024]{2,1,0:T(8,128)(2,1)S(1)}, bf16[1,32,1024]{2,1,0:T(8,128)(2,1)S(1)}, u32[]{:S(2)}, u32[]{:S(2)}) collective-permute-start(bf16[1,32,1024]{2,1,0:T(8,128)(2,1)S(1)} %get-tuple-element.62), channel_id=1, source_target_pairs={{0,8},{4,12},{8,0},{12,4},{1,9},{5,13},{9,1},{13,5},{2,10},{6,14},... | collective-permute-start | bytes 196616 | tf_op jit(solution)/shard_map/ppermute | solution.py:522
  69.1 0.4 shard_map.128.dense
  69.5 4.4 %convolution_convert_fusion.4.before = bf16[128,1024]{1,0:T(8,128)(2,1)S(1)} fusion(bf16[128,3584]{1,0:T(8,128)(2,1)S(1)} %shard_map.128.dense, bf16[3584,1024]{1,0:T(8,128)(2,1)} %down.3), kind=kOutput, calls=%fused_computation.4 | convolution fusion | flops 939655168 | bytes 8519680 | tf_op jit(solution)/shard_map/dot_general | solution.py:624
  74.0 1.7 %collective-permute-start.20 = (bf16[32,1024]{1,0:T(8,128)(2,1)S(1)}, bf16[32,1024]{1,0:T(8,128)(2,1)S(1)}, u32[]{:S(2)}, u32[]{:S(2)}) collective-permute-start(bf16[32,1024]{1,0:T(8,128)(2,1)S(1)} %get-tuple-element.58), channel_id=1, source_target_pairs={{0,12},{4,8},{8,4},{12,0},{1,13},{5,9},{9,5},{13,1},{2,14},{6,10},... | collective-permute-start | bytes 196616 | tf_op jit(solution)/shard_map/ppermute | solution.py:522
  75.7 0.1 collective-permute-start.19
  75.8 2.6 %collective-permute-start.18 = (bf16[32,1024]{1,0:T(8,128)(2,1)S(1)}, bf16[32,1024]{1,0:T(8,128)(2,1)S(1)}, u32[]{:S(2)}, u32[]{:S(2)}) collective-permute-start(bf16[32,1024]{1,0:T(8,128)(2,1)S(1)} %get-tuple-element.60), channel_id=1, source_target_pairs={{0,4},{4,0},{8,12},{12,8},{1,5},{5,1},{9,13},{13,9},{2,6},{6,2},{1... | collective-permute-start | bytes 196616 | tf_op jit(solution)/shard_map/ppermute | solution.py:522
  78.5 0.4 shard_map.129
  78.9 2.0 %collective-permute-done.20.refs_3_ = bf16[32,1024]{1,0:T(8,128)(2,1)S(1)} collective-permute-done((bf16[32,1024]{1,0:T(8,128)(2,1)S(1)}, bf16[32,1024]{1,0:T(8,128)(2,1)S(1)}, u32[]{:S(2)}, u32[]{:S(2)}) %collective-permute-start.20) | collective-permute-done | bytes 65568 | tf_op jit(solution)/shard_map/ppermute | solution.py:522
  80.8 1.6 %collective-permute-done.19.refs_2_ = bf16[32,1024]{1,0:T(8,128)(2,1)S(1)} collective-permute-done((bf16[32,1024]{1,0:T(8,128)(2,1)S(1)}, bf16[32,1024]{1,0:T(8,128)(2,1)S(1)}, u32[]{:S(2)}, u32[]{:S(2)}) %collective-permute-start.19) | collective-permute-done | bytes 65568 | tf_op jit(solution)/shard_map/ppermute | solution.py:522
  82.4 0.7 shard_map.130
  83.1 2.0 %collective-permute-start.24 = (bf16[32,1024]{1,0:T(8,128)(2,1)S(1)}, bf16[32,1024]{1,0:T(8,128)(2,1)S(1)}, u32[]{:S(2)}, u32[]{:S(2)}) collective-permute-start(bf16[32,1024]{1,0:T(8,128)(2,1)S(1)} %get-tuple-element.38), channel_id=1, source_target_pairs={{0,12},{4,8},{8,4},{12,0},{1,13},{5,9},{9,5},{13,1},{2,14},{6,10},... | collective-permute-start | bytes 196616 | tf_op jit(solution)/shard_map/ppermute | solution.py:522
  85.1 2.4 %collective-permute-start.22 = (bf16[32,1024]{1,0:T(8,128)(2,1)S(1)}, bf16[32,1024]{1,0:T(8,128)(2,1)S(1)}, u32[]{:S(2)}, u32[]{:S(2)}) collective-permute-start(bf16[32,1024]{1,0:T(8,128)(2,1)S(1)} %get-tuple-element.38), channel_id=1, source_target_pairs={{0,4},{4,0},{8,12},{12,8},{1,5},{5,1},{9,13},{13,9},{2,6},{6,2},{1... | collective-permute-start | bytes 196616 | tf_op jit(solution)/shard_map/ppermute | solution.py:522
  87.5 3.4 %collective-permute-done.22 = bf16[32,1024]{1,0:T(8,128)(2,1)S(1)} collective-permute-done((bf16[32,1024]{1,0:T(8,128)(2,1)S(1)}, bf16[32,1024]{1,0:T(8,128)(2,1)S(1)}, u32[]{:S(2)}, u32[]{:S(2)}) %collective-permute-start.22) | collective-permute-done | bytes 65568 | tf_op jit(solution)/shard_map/ppermute | solution.py:522
  91.0 0.7 collective-permute-done.23
  91.7 1.4 %shard_map.131 = (bf16[2,32,896]{2,1,0:T(8,128)(2,1)S(1)}, bf16[2,32,896]{2,1,0:T(8,128)(2,1)S(1)}) custom-call(bf16[4,64,128]{2,1,0:T(8,128)(2,1)S(1)} %get-tuple-element.27.picker, bf16[128,1024]{1,0:T(8,128)(2,1)S(1)} %constant_dynamic-update-slice_fusion.residual.before, bf16[3584,1024]{1,0:T(8,128)(2,1)S(1)} %bitcast.65, ...), custom_call_target="tpu_custom_call" | custom-call | tf_op jit(solution)/shard_map/pallas_call | solution.py:342
  93.1 0.1 collective-permute-start.25
  93.2 1.3 %shard_map.132 = (bf16[2,32,896]{2,1,0:T(8,128)(2,1)S(1)}, bf16[2,32,896]{2,1,0:T(8,128)(2,1)S(1)}) custom-call(bf16[4,64,128]{2,1,0:T(8,128)(2,1)S(1)} %get-tuple-element.27.picker, bf16[128,1024]{1,0:T(8,128)(2,1)S(1)} %constant_dynamic-update-slice_fusion.residual.before, bf16[3584,1024]{1,0:T(8,128)(2,1)S(1)} %bitcast.65, ...), custom_call_target="tpu_custom_call" | custom-call | tf_op jit(solution)/shard_map/pallas_call | solution.py:342
  94.5 0.6 collective-permute-start.27
  95.1 1.6 %collective-permute-start.26 = (bf16[2,32,896]{2,1,0:T(8,128)(2,1)S(1)}, bf16[2,32,896]{2,1,0:T(8,128)(2,1)S(1)}, u32[]{:S(2)}, u32[]{:S(2)}) collective-permute-start(bf16[2,32,896]{2,1,0:T(8,128)(2,1)S(1)} %add_convert_fusion.5.mine), channel_id=1, source_target_pairs={{0,2},{2,0},{1,3},{3,1},{4,6},{6,4},{5,7},{7,5},{8,10},{10,8},{9,1... | collective-permute-start | bytes 344072 | tf_op jit(solution)/shard_map/ppermute | solution.py:16
  96.8 0.9 collective-permute-start.29
  97.7 3.4 %shard_map.133 = (bf16[3584,1024]{1,0:T(8,128)(2,1)}, f32[8,128]{1,0:T(8,128)S(1)}) custom-call(bf16[3584,128]{1,0:T(8,128)(2,1)S(1)} %get-tuple-element.42.hidden, bf16[128,1024]{1,0:T(8,128)(2,1)S(1)} %constant_dynamic-update-slice_fusion.residual.before, bf16[2,32,896]{2,1,0:T(8,128)(2,1)S(1)} %add_convert_fusion.4.before.mine), custom_call_target="tpu_custom_call" | custom-call | flops 939524096 | bytes 7340032 | tf_op jit(solution)/shard_map/pallas_call | solution.py:395
  101.2 0.2 shard_map.134.rest_0_
  101.4 0.1 collective-permute-start.28
  101.5 1.2 %collective-permute-done.29.other = bf16[2,32,896]{2,1,0:T(8,128)(2,1)S(1)} collective-permute-done((bf16[2,32,896]{2,1,0:T(8,128)(2,1)S(1)}, bf16[2,32,896]{2,1,0:T(8,128)(2,1)S(1)}, u32[]{:S(2)}, u32[]{:S(2)}) %collective-permute-start.29) | collective-permute-done | bytes 114720 | tf_op jit(solution)/shard_map/ppermute | solution.py:16
  102.7 0.2 shard_map.135.rest_2_
  103.0 1.5 %collective-permute-done.30.rest_3_ = bf16[2,2,32,896]{3,2,1,0:T(8,128)(2,1)S(1)} collective-permute-done((bf16[2,2,32,896]{3,2,1,0:T(8,128)(2,1)S(1)}, bf16[2,2,32,896]{3,2,1,0:T(8,128)(2,1)S(1)}, u32[]{:S(2)}, u32[]{:S(2)}) %collective-permute-start.30) | collective-permute-done | bytes 229408 | tf_op jit(solution)/shard_map/ppermute | solution.py:16
  104.4 6.5 %shard_map.136 = (bf16[1024,3584]{1,0:T(8,128)(2,1)}, bf16[1024,3584]{1,0:T(8,128)(2,1)}) custom-call(bf16[4,64,128]{2,1,0:T(8,128)(2,1)S(1)} %get-tuple-element.27.picker, bf16[1024,128]{1,0:T(8,128)(2,1)S(1)} %get-tuple-element.36.refs_6_.tokens, bf16[2,2,32,896]{3,2,1,0:T(8,128)(2,1)S(1)} %shard_map.134.rest_0_, ...), custom_call_target="tpu_custom_call" | custom-call | flops 1879048192 | bytes 14680064 | tf_op jit(solution)/shard_map/pallas_call | solution.py:445
  (79 shorter events, 1.5 us)
Async XLA Ops:
  0.6 7.2 %copy-start.2 = (bf16[32,1024]{1,0:T(8,128)(2,1)S(1)}, bf16[32,1024]{1,0:T(8,128)(2,1)}, u32[]{:S(2)}) copy-start(bf16[32,1024]{1,0:T(8,128)(2,1)} %param.9) | copy-start | bytes 196612
  0.6 7.3 %collective-permute-start = (bf16[32,1024]{1,0:T(8,128)(2,1)}, bf16[32,1024]{1,0:T(8,128)(2,1)S(1)}, u32[]{:S(2)}, u32[]{:S(2)}) collective-permute-start(bf16[32,1024]{1,0:T(8,128)(2,1)} %param.9), channel_id=1, source_target_pairs={{0,4},{4,0},{8,12},{12,8},{1,5},{5,1},{9,13},{13,9},{2,6},{6,2},{1... | collective-permute-start | bytes 196616 | tf_op jit(solution)/shard_map/ppermute | solution.py:522
  3.7 5.7 %copy-start.1 = (bf16[1024,3584]{1,0:T(8,128)(2,1)S(1)}, bf16[1024,3584]{1,0:T(8,128)(2,1)}, u32[]{:S(2)}) copy-start(bf16[1024,3584]{1,0:T(8,128)(2,1)} %param.13) | copy-start | bytes 22020100
  7.8 4.4 %copy-start = (bf16[1024,3584]{1,0:T(8,128)(2,1)}, bf16[1024,3584]{1,0:T(8,128)(2,1)S(1)}, u32[]{:S(2)}) copy-start(bf16[1024,3584]{1,0:T(8,128)(2,1)S(1)} %get-tuple-element.28) | copy-start | bytes 22020100
  12.4 8.9 %collective-permute-start.3 = (bf16[2,32,3584]{2,1,0:T(8,128)(2,1)S(1)}, bf16[2,32,3584]{2,1,0:T(8,128)(2,1)S(1)}, u32[]{:S(2)}, u32[]{:S(2)}) collective-permute-start(bf16[2,32,3584]{2,1,0:T(8,128)(2,1)S(1)} %pad_maximum_fusion), channel_id=1, source_target_pairs={{0,1},{1,0},{2,3},{3,2},{4,5},{5,4},{6,7},{7,6},{8,9},{9,8},{10,11... | collective-permute-start | bytes 1376264 | tf_op jit(solution)/shard_map/ppermute | solution.py:16
  12.4 6.7 %collective-permute-start.1 = (bf16[32,1024]{1,0:T(8,128)(2,1)S(1)}, bf16[32,1024]{1,0:T(8,128)(2,1)S(1)}, u32[]{:S(2)}, u32[]{:S(2)}) collective-permute-start(bf16[32,1024]{1,0:T(8,128)(2,1)S(1)} %copy-done.2), channel_id=1, source_target_pairs={{0,8},{4,12},{8,0},{12,4},{1,9},{5,13},{9,1},{13,5},{2,10},{6,14},... | collective-permute-start | bytes 196616 | tf_op jit(solution)/shard_map/ppermute | solution.py:522
  15.1 6.1 %collective-permute-start.2 = (bf16[32,1024]{1,0:T(8,128)(2,1)S(1)}, bf16[32,1024]{1,0:T(8,128)(2,1)S(1)}, u32[]{:S(2)}, u32[]{:S(2)}) collective-permute-start(bf16[32,1024]{1,0:T(8,128)(2,1)S(1)} %copy-done.2), channel_id=1, source_target_pairs={{0,12},{4,8},{8,4},{12,0},{1,13},{5,9},{9,5},{13,1},{2,14},{6,10},... | collective-permute-start | bytes 196616 | tf_op jit(solution)/shard_map/ppermute | solution.py:522
  21.4 5.4 %slice-start.2 = ((s8[7340032]{0:T(1024)(128)(4,1)}), s8[4194304]{0:T(1024)(128)(4,1)S(1)}, s32[]{:S(2)}) async-start(s8[7340032]{0:T(1024)(128)(4,1)} %bitcast.67), calls=%async_computation.2 | async-start | bytes 8388608
  22.0 4.8 %slice-start.3 = ((s8[7340032]{0:T(1024)(128)(4,1)}), s8[3145728]{0:T(1024)(128)(4,1)S(1)}, s32[]{:S(2)}) async-start(s8[7340032]{0:T(1024)(128)(4,1)} %bitcast.67), calls=%async_computation.3 | async-start | bytes 6291456
  28.2 6.6 %collective-permute-start.7 = (bf16[2,16,3584]{2,1,0:T(8,128)(2,1)S(1)}, bf16[2,16,3584]{2,1,0:T(8,128)(2,1)S(1)}, u32[]{:S(2)}, u32[]{:S(2)}) collective-permute-start(bf16[2,16,3584]{2,1,0:T(8,128)(2,1)S(1)} %slice.73), channel_id=1, source_target_pairs={{0,2},{2,0},{1,3},{3,1},{4,6},{6,4},{5,7},{7,5},{8,10},{10,8},{9,1... | collective-permute-start | bytes 688136 | tf_op jit(solution)/shard_map/ppermute | solution.py:16
  29.9 6.7 %collective-permute-start.4 = (bf16[2,32,3584]{2,1,0:T(8,128)(2,1)S(1)}, bf16[2,32,3584]{2,1,0:T(8,128)(2,1)S(1)}, u32[]{:S(2)}, u32[]{:S(2)}) collective-permute-start(bf16[2,32,3584]{2,1,0:T(8,128)(2,1)S(1)} %pad_maximum_fusion.1), channel_id=1, source_target_pairs={{0,1},{1,0},{2,3},{3,2},{4,5},{5,4},{6,7},{7,6},{8,9},{9,8},{10,11... | collective-permute-start | bytes 1376264 | tf_op jit(solution)/shard_map/ppermute | solution.py:16
  35.0 5.9 %collective-permute-start.8 = (bf16[16,3584]{1,0:T(8,128)(2,1)S(1)}, bf16[16,3584]{1,0:T(8,128)(2,1)S(1)}, u32[]{:S(2)}, u32[]{:S(2)}) collective-permute-start(bf16[16,3584]{1,0:T(8,128)(2,1)S(1)} %fusion.4), channel_id=1, source_target_pairs={{0,2},{2,0},{1,3},{3,1},{4,6},{6,4},{5,7},{7,5},{8,10},{10,8},{9,1... | collective-permute-start | bytes 344072 | tf_op jit(solution)/shard_map/ppermute | solution.py:16
  36.7 12.7 %collective-permute-start.10 = (bf16[2,16,3584]{2,1,0:T(8,128)(2,1)S(1)}, bf16[2,16,3584]{2,1,0:T(8,128)(2,1)S(1)}, u32[]{:S(2)}, u32[]{:S(2)}) collective-permute-start(bf16[2,16,3584]{2,1,0:T(8,128)(2,1)S(1)} %slice.77), channel_id=1, source_target_pairs={{0,2},{2,0},{1,3},{3,1},{4,6},{6,4},{5,7},{7,5},{8,10},{10,8},{9,1... | collective-permute-start | bytes 688136 | tf_op jit(solution)/shard_map/ppermute | solution.py:16
  40.9 16.2 %collective-permute-start.9 = (bf16[32,3584]{1,0:T(8,128)(2,1)S(1)}, bf16[32,3584]{1,0:T(8,128)(2,1)S(1)}, u32[]{:S(2)}, u32[]{:S(2)}) collective-permute-start(bf16[32,3584]{1,0:T(8,128)(2,1)S(1)} %pad_maximum_fusion.2.refs_0_), channel_id=1, source_target_pairs={{0,1},{1,0},{2,3},{3,2},{4,5},{5,4},{6,7},{7,6},{8,9},{9,8},{10,11... | collective-permute-start | bytes 688136 | tf_op jit(solution)/shard_map/ppermute | solution.py:16
  41.0 16.7 %slice-start.4 = ((s8[7340032]{0:T(1024)(128)(4,1)}), s8[4194304]{0:T(1024)(128)(4,1)S(1)}, s32[]{:S(2)}) async-start(s8[7340032]{0:T(1024)(128)(4,1)} %bitcast.69), calls=%async_computation.4 | async-start | bytes 8388608
  44.9 10.8 %collective-permute-start.5 = (bf16[2,2,32,896]{3,2,1,0:T(8,128)(2,1)S(1)}, bf16[2,2,32,896]{3,2,1,0:T(8,128)(2,1)S(1)}, u32[]{:S(2)}, u32[]{:S(2)}) collective-permute-start(bf16[2,2,32,896]{3,2,1,0:T(8,128)(2,1)S(1)} %get-tuple-element.30), channel_id=1, source_target_pairs={{0,1},{1,0},{2,3},{3,2},{4,5},{5,4},{6,7},{7,6},{8,9},{9,8},{10,11... | collective-permute-start | bytes 688136 | tf_op jit(solution)/shard_map/ppermute | solution.py:16
  45.5 12.3 %slice-start.5 = ((s8[7340032]{0:T(1024)(128)(4,1)}), s8[3145728]{0:T(1024)(128)(4,1)S(1)}, s32[]{:S(2)}) async-start(s8[7340032]{0:T(1024)(128)(4,1)} %bitcast.69), calls=%async_computation.5 | async-start | bytes 6291456
  49.3 1.6 %collective-permute-start.15 = (bf16[2,2,32,896]{3,2,1,0:T(8,128)(2,1)S(1)}, bf16[2,2,32,896]{3,2,1,0:T(8,128)(2,1)S(1)}, u32[]{:S(2)}, u32[]{:S(2)}) collective-permute-start(bf16[2,2,32,896]{3,2,1,0:T(8,128)(2,1)S(1)} %get-tuple-element.34), channel_id=1, source_target_pairs={{0,1},{1,0},{2,3},{3,2},{4,5},{5,4},{6,7},{7,6},{8,9},{9,8},{10,11... | collective-permute-start | bytes 688136 | tf_op jit(solution)/shard_map/ppermute | solution.py:16
  49.6 6.0 %collective-permute-start.11 = (bf16[16,3584]{1,0:T(8,128)(2,1)S(1)}, bf16[16,3584]{1,0:T(8,128)(2,1)S(1)}, u32[]{:S(2)}, u32[]{:S(2)}) collective-permute-start(bf16[16,3584]{1,0:T(8,128)(2,1)S(1)} %fusion.2), channel_id=1, source_target_pairs={{0,2},{2,0},{1,3},{3,1},{4,6},{6,4},{5,7},{7,5},{8,10},{10,8},{9,1... | collective-permute-start | bytes 344072 | tf_op jit(solution)/shard_map/ppermute | solution.py:16
  51.0 10.7 %collective-permute-start.16 = (bf16[2,2,32,896]{3,2,1,0:T(8,128)(2,1)S(1)}, bf16[2,2,32,896]{3,2,1,0:T(8,128)(2,1)S(1)}, u32[]{:S(2)}, u32[]{:S(2)}) collective-permute-start(bf16[2,2,32,896]{3,2,1,0:T(8,128)(2,1)S(1)} %add_convert_fusion.2.mine), channel_id=1, source_target_pairs={{0,2},{2,0},{1,3},{3,1},{4,6},{6,4},{5,7},{7,5},{8,10},{10,8},{9,1... | collective-permute-start | bytes 688136 | tf_op jit(solution)/shard_map/ppermute | solution.py:16
  55.6 1.6 %collective-permute-start.12 = (bf16[32,3584]{1,0:T(8,128)(2,1)S(1)}, bf16[32,3584]{1,0:T(8,128)(2,1)S(1)}, u32[]{:S(2)}, u32[]{:S(2)}) collective-permute-start(bf16[32,3584]{1,0:T(8,128)(2,1)S(1)} %pad_maximum_fusion.3.refs_2_), channel_id=1, source_target_pairs={{0,1},{1,0},{2,3},{3,2},{4,5},{5,4},{6,7},{7,6},{8,9},{9,8},{10,11... | collective-permute-start | bytes 688136 | tf_op jit(solution)/shard_map/ppermute | solution.py:16
  55.7 10.0 %collective-permute-start.6 = (bf16[2,2,32,896]{3,2,1,0:T(8,128)(2,1)S(1)}, bf16[2,2,32,896]{3,2,1,0:T(8,128)(2,1)S(1)}, u32[]{:S(2)}, u32[]{:S(2)}) collective-permute-start(bf16[2,2,32,896]{3,2,1,0:T(8,128)(2,1)S(1)} %add_convert_fusion.3.mine), channel_id=1, source_target_pairs={{0,2},{2,0},{1,3},{3,1},{4,6},{6,4},{5,7},{7,5},{8,10},{10,8},{9,1... | collective-permute-start | bytes 688136 | tf_op jit(solution)/shard_map/ppermute | solution.py:16
  59.0 6.6 %collective-permute-start.13 = (bf16[2,32,1024]{2,1,0:T(8,128)(2,1)S(1)}, bf16[2,32,1024]{2,1,0:T(8,128)(2,1)S(1)}, u32[]{:S(2)}, u32[]{:S(2)}) collective-permute-start(bf16[2,32,1024]{2,1,0:T(8,128)(2,1)S(1)} %dynamic-slice_bitcast_fusion), channel_id=1, source_target_pairs={{0,4},{4,0},{8,12},{12,8},{1,5},{5,1},{9,13},{13,9},{2,6},{6,2},{1... | collective-permute-start | bytes 393224 | tf_op jit(solution)/shard_map/ppermute | solution.py:522
  65.7 3.3 %collective-permute-start.17 = (bf16[2,32,896]{2,1,0:T(8,128)(2,1)S(1)}, bf16[2,32,896]{2,1,0:T(8,128)(2,1)S(1)}, u32[]{:S(2)}, u32[]{:S(2)}) collective-permute-start(bf16[2,32,896]{2,1,0:T(8,128)(2,1)S(1)} %get-tuple-element.35), channel_id=1, source_target_pairs={{0,1},{1,0},{2,3},{3,2},{4,5},{5,4},{6,7},{7,6},{8,9},{9,8},{10,11... | collective-permute-start | bytes 344072 | tf_op jit(solution)/shard_map/ppermute | solution.py:16
  65.9 3.1 %collective-permute-start.14 = (bf16[2,32,896]{2,1,0:T(8,128)(2,1)S(1)}, bf16[2,32,896]{2,1,0:T(8,128)(2,1)S(1)}, u32[]{:S(2)}, u32[]{:S(2)}) collective-permute-start(bf16[2,32,896]{2,1,0:T(8,128)(2,1)S(1)} %get-tuple-element.32), channel_id=1, source_target_pairs={{0,1},{1,0},{2,3},{3,2},{4,5},{5,4},{6,7},{7,6},{8,9},{9,8},{10,11... | collective-permute-start | bytes 344072 | tf_op jit(solution)/shard_map/ppermute | solution.py:16
  66.5 12.3 %collective-permute-start.21 = (bf16[1,32,1024]{2,1,0:T(8,128)(2,1)S(1)}, bf16[1,32,1024]{2,1,0:T(8,128)(2,1)S(1)}, u32[]{:S(2)}, u32[]{:S(2)}) collective-permute-start(bf16[1,32,1024]{2,1,0:T(8,128)(2,1)S(1)} %get-tuple-element.62), channel_id=1, source_target_pairs={{0,8},{4,12},{8,0},{12,4},{1,9},{5,13},{9,1},{13,5},{2,10},{6,14},... | collective-permute-start | bytes 196616 | tf_op jit(solution)/shard_map/ppermute | solution.py:522
  69.1 22.6 %slice-start = ((s8[7340032]{0:T(1024)(128)(4,1)}), s8[4194304]{0:T(1024)(128)(4,1)S(1)}, s32[]{:S(2)}) async-start(s8[7340032]{0:T(1024)(128)(4,1)} %bitcast.64), calls=%async_computation | async-start | bytes 8388608
  69.5 22.2 %slice-start.1 = ((s8[7340032]{0:T(1024)(128)(4,1)}), s8[3145728]{0:T(1024)(128)(4,1)S(1)}, s32[]{:S(2)}) async-start(s8[7340032]{0:T(1024)(128)(4,1)} %bitcast.64), calls=%async_computation.1 | async-start | bytes 6291456
  74.0 6.8 %collective-permute-start.20 = (bf16[32,1024]{1,0:T(8,128)(2,1)S(1)}, bf16[32,1024]{1,0:T(8,128)(2,1)S(1)}, u32[]{:S(2)}, u32[]{:S(2)}) collective-permute-start(bf16[32,1024]{1,0:T(8,128)(2,1)S(1)} %get-tuple-element.58), channel_id=1, source_target_pairs={{0,12},{4,8},{8,4},{12,0},{1,13},{5,9},{9,5},{13,1},{2,14},{6,10},... | collective-permute-start | bytes 196616 | tf_op jit(solution)/shard_map/ppermute | solution.py:522
  75.7 6.7 %collective-permute-start.19 = (bf16[32,1024]{1,0:T(8,128)(2,1)S(1)}, bf16[32,1024]{1,0:T(8,128)(2,1)S(1)}, u32[]{:S(2)}, u32[]{:S(2)}) collective-permute-start(bf16[32,1024]{1,0:T(8,128)(2,1)S(1)} %get-tuple-element.59), channel_id=1, source_target_pairs={{0,8},{4,12},{8,0},{12,4},{1,9},{5,13},{9,1},{13,5},{2,10},{6,14},... | collective-permute-start | bytes 196616 | tf_op jit(solution)/shard_map/ppermute | solution.py:522
  75.8 6.6 %collective-permute-start.18 = (bf16[32,1024]{1,0:T(8,128)(2,1)S(1)}, bf16[32,1024]{1,0:T(8,128)(2,1)S(1)}, u32[]{:S(2)}, u32[]{:S(2)}) collective-permute-start(bf16[32,1024]{1,0:T(8,128)(2,1)S(1)} %get-tuple-element.60), channel_id=1, source_target_pairs={{0,4},{4,0},{8,12},{12,8},{1,5},{5,1},{9,13},{13,9},{2,6},{6,2},{1... | collective-permute-start | bytes 196616 | tf_op jit(solution)/shard_map/ppermute | solution.py:522
  83.1 8.6 %collective-permute-start.24 = (bf16[32,1024]{1,0:T(8,128)(2,1)S(1)}, bf16[32,1024]{1,0:T(8,128)(2,1)S(1)}, u32[]{:S(2)}, u32[]{:S(2)}) collective-permute-start(bf16[32,1024]{1,0:T(8,128)(2,1)S(1)} %get-tuple-element.38), channel_id=1, source_target_pairs={{0,12},{4,8},{8,4},{12,0},{1,13},{5,9},{9,5},{13,1},{2,14},{6,10},... | collective-permute-start | bytes 196616 | tf_op jit(solution)/shard_map/ppermute | solution.py:522
  85.1 6.6 %collective-permute-start.23 = (bf16[32,1024]{1,0:T(8,128)(2,1)S(1)}, bf16[32,1024]{1,0:T(8,128)(2,1)S(1)}, u32[]{:S(2)}, u32[]{:S(2)}) collective-permute-start(bf16[32,1024]{1,0:T(8,128)(2,1)S(1)} %get-tuple-element.38), channel_id=1, source_target_pairs={{0,8},{4,12},{8,0},{12,4},{1,9},{5,13},{9,1},{13,5},{2,10},{6,14},... | collective-permute-start | bytes 196616 | tf_op jit(solution)/shard_map/ppermute | solution.py:522
  85.1 5.9 %collective-permute-start.22 = (bf16[32,1024]{1,0:T(8,128)(2,1)S(1)}, bf16[32,1024]{1,0:T(8,128)(2,1)S(1)}, u32[]{:S(2)}, u32[]{:S(2)}) collective-permute-start(bf16[32,1024]{1,0:T(8,128)(2,1)S(1)} %get-tuple-element.38), channel_id=1, source_target_pairs={{0,4},{4,0},{8,12},{12,8},{1,5},{5,1},{9,13},{13,9},{2,6},{6,2},{1... | collective-permute-start | bytes 196616 | tf_op jit(solution)/shard_map/ppermute | solution.py:522
  93.1 2.0 %collective-permute-start.25 = (bf16[2,32,896]{2,1,0:T(8,128)(2,1)S(1)}, bf16[2,32,896]{2,1,0:T(8,128)(2,1)S(1)}, u32[]{:S(2)}, u32[]{:S(2)}) collective-permute-start(bf16[2,32,896]{2,1,0:T(8,128)(2,1)S(1)} %get-tuple-element.40), channel_id=1, source_target_pairs={{0,1},{1,0},{2,3},{3,2},{4,5},{5,4},{6,7},{7,6},{8,9},{9,8},{10,11... | collective-permute-start | bytes 344072 | tf_op jit(solution)/shard_map/ppermute | solution.py:16
  94.5 2.2 %collective-permute-start.27 = (bf16[2,32,896]{2,1,0:T(8,128)(2,1)S(1)}, bf16[2,32,896]{2,1,0:T(8,128)(2,1)S(1)}, u32[]{:S(2)}, u32[]{:S(2)}) collective-permute-start(bf16[2,32,896]{2,1,0:T(8,128)(2,1)S(1)} %get-tuple-element.44), channel_id=1, source_target_pairs={{0,1},{1,0},{2,3},{3,2},{4,5},{5,4},{6,7},{7,6},{8,9},{9,8},{10,11... | collective-permute-start | bytes 344072 | tf_op jit(solution)/shard_map/ppermute | solution.py:16
  95.1 6.1 %collective-permute-start.26 = (bf16[2,32,896]{2,1,0:T(8,128)(2,1)S(1)}, bf16[2,32,896]{2,1,0:T(8,128)(2,1)S(1)}, u32[]{:S(2)}, u32[]{:S(2)}) collective-permute-start(bf16[2,32,896]{2,1,0:T(8,128)(2,1)S(1)} %add_convert_fusion.5.mine), channel_id=1, source_target_pairs={{0,2},{2,0},{1,3},{3,1},{4,6},{6,4},{5,7},{7,5},{8,10},{10,8},{9,1... | collective-permute-start | bytes 344072 | tf_op jit(solution)/shard_map/ppermute | solution.py:16
  96.8 5.9 %collective-permute-start.29 = (bf16[2,32,896]{2,1,0:T(8,128)(2,1)S(1)}, bf16[2,32,896]{2,1,0:T(8,128)(2,1)S(1)}, u32[]{:S(2)}, u32[]{:S(2)}) collective-permute-start(bf16[2,32,896]{2,1,0:T(8,128)(2,1)S(1)} %add_convert_fusion.4.before.mine), channel_id=1, source_target_pairs={{0,2},{2,0},{1,3},{3,1},{4,6},{6,4},{5,7},{7,5},{8,10},{10,8},{9,1... | collective-permute-start | bytes 344072 | tf_op jit(solution)/shard_map/ppermute | solution.py:16
  101.4 1.6 %collective-permute-start.28 = (bf16[2,2,32,896]{3,2,1,0:T(8,128)(2,1)S(1)}, bf16[2,2,32,896]{3,2,1,0:T(8,128)(2,1)S(1)}, u32[]{:S(2)}, u32[]{:S(2)}) collective-permute-start(bf16[2,2,32,896]{3,2,1,0:T(8,128)(2,1)S(1)} %shard_map.134.rest_0_), channel_id=1, source_target_pairs={{0,1},{1,0},{2,3},{3,2},{4,5},{5,4},{6,7},{7,6},{8,9},{9,8},{10,11... | collective-permute-start | bytes 688136 | tf_op jit(solution)/shard_map/ppermute | solution.py:16
  102.9 1.6 %collective-permute-start.30 = (bf16[2,2,32,896]{3,2,1,0:T(8,128)(2,1)S(1)}, bf16[2,2,32,896]{3,2,1,0:T(8,128)(2,1)S(1)}, u32[]{:S(2)}, u32[]{:S(2)}) collective-permute-start(bf16[2,2,32,896]{3,2,1,0:T(8,128)(2,1)S(1)} %shard_map.135.rest_2_), channel_id=1, source_target_pairs={{0,1},{1,0},{2,3},{3,2},{4,5},{5,4},{6,7},{7,6},{8,9},{9,8},{10,11... | collective-permute-start | bytes 688136 | tf_op jit(solution)/shard_map/ppermute | solution.py:16

commit v9 on v6

--- a/solution.py
+++ b/solution.py
@@ -142,26 +142,23 @@
     )(place, far(routes), far(shares), far(gate), far(up))
 
 
-def residual_kernel(ranks, *refs):
+def residual_kernel(count, *refs):
     student = refs[0][...].astype(F32)
-    target = refs[ranks][...].astype(F32)
-    for i in range(1, ranks):
+    for i in range(1, count):
         student = student + refs[i][...].astype(F32)
-        target = target + refs[ranks + i][...].astype(F32)
     refs[-2][...] = student.astype(BF)
-    refs[-1][...] = (student - target).astype(BF)
+    refs[-1][...] = (student - refs[count][...].astype(F32)).astype(BF)
 
 
 def residual_of(student, target, before):
-    ranks = len(student)
-    block = jax.ShapeDtypeStruct(student[0].shape, BF)
-    return pl.pallas_call(
-        functools.partial(residual_kernel, ranks),
-        in_specs=[whole()] * (2 * ranks) + [anywhere()] * len(before),
+    block = jax.ShapeDtypeStruct(target.shape, BF)
+    return pl.pallas_call(
+        functools.partial(residual_kernel, len(student)),
+        in_specs=[whole()] * (len(student) + 1) + [anywhere()] * len(before),
         out_specs=(whole(), whole()),
         out_shape=(block, block),
         compiler_params=pltpu.CompilerParams(vmem_limit_bytes=4 * 1024 * 1024),
-    )(*student, *target, *before)
+    )(*student, target, *before)
 
 
 def tile_of(size):
@@ -584,12 +581,13 @@
         hidden = jnp.concatenate(gather_dp_parts(hidden, dps), axis=0)
         hiddens.append((hidden, shift(hidden, "pipe", pipes, 1)))
     hidden = join(place, hiddens, dps, pipes)
-    target = to_owners(jnp.dot(hidden, teacher_down, preferred_element_type=F32).astype(BF))
+    product = jnp.dot(hidden, teacher_down, preferred_element_type=F32).astype(BF)
+    target = lax.psum_scatter(product, "expert", scatter_dimension=0, tiled=True)
 
     pre, weighted = [], []
     for first, (keep, theirs) in zip(firsts, parts):
         mine, other = exchange_dp(add(keep, theirs), dps)
-        total, part = hidden_act(mine, other, dps == 2, slot_weight, target[-2:], first)
+        total, part = hidden_act(mine, other, dps == 2, slot_weight, [product], first)
         pre.append(total)
         weighted.append(jnp.concatenate([part, shift(part, "pipe", pipes, 1)], axis=1))
     weighted = jnp.concatenate(weighted, axis=0)

time: 91.3 us -> 112 us (1.23)
  between operations: 1.26 us -> 14.5 us
  local copies, waits for them, and re-layouts: 0.24 us -> 4.13 us
  waiting for transfers between devices: 25.3 us -> 28.9 us
  starting transfers between devices: 29 us -> 25.8 us
  matrix products: 2.24 us -> 5.32 us
    ppermute x20, waiting for transfers between devices: 10 us -> 15.6 us  [shift(): lax.ppermute(value, axis, [(i, (i + by) % count) for i in range(count)])]
    ppermute x12 -> x9, waiting for transfers between devices: 15.3 us -> 10.5 us  [to_partner(): return lax.ppermute(value, 'expert', [(i, i ^ s) for i in range(ranks)])]
    unnamed x10 -> x12, local copies, waits for them, and re-layouts: 0.02 us -> 3.94 us
    dot_general x1, matrix products: 1.12 us -> 4.2 us  [body(): product = jnp.dot(dense, expert_down, preferred_element_type=F32).astype(BF)]
    ppermute x12 -> x9, starting transfers between devices: 17.4 us -> 14.5 us  [to_partner(): return lax.ppermute(value, 'expert', [(i, i ^ s) for i in range(ranks)])]
    reduce_scatter x0 -> x1, waiting for transfers between devices: none -> 2.73 us  [body(): lax.psum_scatter(product, 'expert', scatter_dimension=0, tiled=True)]
  transfers between devices with their start and end apart: 32 -> 30, of which waited for: 17 -> 16; matrix products, arithmetic and copies ran while one was open for 4% -> 6% of each run, Pallas kernels for 24% -> 20%
where the time goes in v9:
time: 112 us
  Pallas kernels  32.2 us (29%)
  waiting for transfers between devices  28.9 us (26%)
  starting transfers between devices  25.8 us (23%)
  between operations  14.5 us (13%)
  matrix products  5.32 us (5%)
  local copies, waits for them, and re-layouts  4.13 us (4%)
    ppermute x20, waiting for transfers between devices, shift(): lax.ppermute(value, axis, [(i, (i + by) % count) for i in range(count)])  15.6 us
    ppermute x9, starting transfers between devices, to_partner(): return lax.ppermute(value, 'expert', [(i, i ^ s) for i in range(ranks)])  14.5 us
    ppermute x20, starting transfers between devices, shift(): lax.ppermute(value, axis, [(i, (i + by) % count) for i in range(count)])  11.3 us
    ppermute x9, waiting for transfers between devices, to_partner(): return lax.ppermute(value, 'expert', [(i, i ^ s) for i in range(ranks)])  10.5 us
    pallas_call x2, Pallas kernels, expert_pre(): pl.pallas_call(functools.partial(expert_kernel, first), in_specs=[whole()...  7.59 us
    pallas_call x1, Pallas kernels, input_grads(): pl.pallas_call(functools.partial(input_grad_kernel, count // len(parts)),...  6.48 us
    pallas_call x1, Pallas kernels, prepare(): pl.pallas_call(functools.partial(prepare_kernel, ranks, capacity, dps, pi...  5.89 us
    dot_general x1, matrix products, body(): product = jnp.dot(dense, expert_down, preferred_element_type=F32).astype(BF)  4.2 us
  transfers between devices with their start and end apart: 30, of which 16 were waited for; matrix products, arithmetic and copies ran while one was open for 6% of the time, Pallas kernels for 20%

profile of v9, /device:TPU:0, one launch (start us, length us, event | category | flops | bytes accessed | tf_op | source)
XLA Modules:
  0.0 111.6 jit_solution(154416604760016516)
XLA Ops:
  7.2 3.1 %collective-permute-start = (bf16[32,1024]{1,0:T(8,128)(2,1)}, bf16[32,1024]{1,0:T(8,128)(2,1)S(1)}, u32[]{:S(2)}, u32[]{:S(2)}) collective-permute-start(bf16[32,1024]{1,0:T(8,128)(2,1)} %param.9), channel_id=1, source_target_pairs={{0,4},{4,0},{8,12},{12,8},{1,5},{5,1},{9,13},{13,9},{2,6},{6,2},{1... | collective-permute-start | bytes 196616 | tf_op jit(solution)/shard_map/ppermute | solution.py:534
  10.3 2.5 %collective-permute-start.2 = (bf16[32,1024]{1,0:T(8,128)(2,1)}, bf16[32,1024]{1,0:T(8,128)(2,1)S(1)}, u32[]{:S(2)}, u32[]{:S(2)}) collective-permute-start(bf16[32,1024]{1,0:T(8,128)(2,1)} %param.9), channel_id=1, source_target_pairs={{0,12},{4,8},{8,4},{12,0},{1,13},{5,9},{9,5},{13,1},{2,14},{6,10},... | collective-permute-start | bytes 196616 | tf_op jit(solution)/shard_map/ppermute | solution.py:534
  12.8 0.1 collective-permute-start.1
  12.9 0.1 pad_add_fusion.place
  13.0 5.9 %shard_map.120 = (bf16[4,64,128]{2,1,0:T(8,128)(2,1)S(1)}, f32[4,64,1]{2,1,0:T(8,128)S(1)}, bf16[1024,3584]{1,0:T(8,128)(2,1)S(1)}, bf16[1024,3584]{1,0:T(8,128)(2,1)S(1)}) custom-call(s32[3]{0:T(128)S(1)} %pad_add_fusion.place, s32[4,128]{1,0:T(4,128)} %bitcast.31, f32[4,128]{1,0:T(4,128)} %bitcast.32, bf16[1024,3584]{1,0:T(8,128)(2,1)} %gate.3, ...), custom_call_target="tpu_custom_call" | custom-call | bytes 14680064 | tf_op jit(solution)/shard_map/pallas_call | solution.py:122
  19.0 0.5 collective-permute-done.1
  19.5 1.7 %shard_map.123 = (bf16[2,64,1792]{2,1,0:T(8,128)(2,1)S(1)}, bf16[2,64,1792]{2,1,0:T(8,128)(2,1)S(1)}) custom-call(s32[3]{0:T(128)S(1)} %pad_add_fusion.place, bf16[128,1024]{1,0:T(8,128)(2,1)S(1)} %constant_dynamic-update-slice_fusion.4.tokens, bf16[1024,3584]{1,0:T(8,128)(2,1)S(1)} %get-tuple-element.33.gate, bf16[1024,3584]{1,0:T(8,128)(2,1)S(1)} %get-tuple-element.34.up), custom_call_target="tpu_custom_call" | custom-call | flops 939524096 | bytes 7340032 | tf_op jit(solution)/shard_map/pallas_call | solution.py:189
  21.2 1.7 %shard_map.121 = (bf16[2,64,1792]{2,1,0:T(8,128)(2,1)S(1)}, bf16[2,64,1792]{2,1,0:T(8,128)(2,1)S(1)}) custom-call(s32[3]{0:T(128)S(1)} %pad_add_fusion.place, bf16[128,1024]{1,0:T(8,128)(2,1)S(1)} %constant_dynamic-update-slice_fusion.4.tokens, bf16[1024,3584]{1,0:T(8,128)(2,1)S(1)} %get-tuple-element.33.gate, bf16[1024,3584]{1,0:T(8,128)(2,1)S(1)} %get-tuple-element.34.up), custom_call_target="tpu_custom_call" | custom-call | flops 939524096 | bytes 7340032 | tf_op jit(solution)/shard_map/pallas_call | solution.py:189
  22.9 0.6 collective-permute-start.3
  23.5 0.1 add_convert_fusion
  23.6 1.6 %collective-permute-start.7 = (bf16[2,32,1792]{2,1,0:T(8,128)(2,1)S(1)}, bf16[2,32,1792]{2,1,0:T(8,128)(2,1)S(1)}, u32[]{:S(2)}, u32[]{:S(2)}) collective-permute-start(bf16[2,32,1792]{2,1,0:T(8,128)(2,1)S(1)} %slice.33), channel_id=1, source_target_pairs={{0,2},{2,0},{1,3},{3,1},{4,6},{6,4},{5,7},{7,5},{8,10},{10,8},{9,1... | collective-permute-start | bytes 688136 | tf_op jit(solution)/shard_map/ppermute | solution.py:16
  25.2 0.1 add_convert_fusion.1.before
  25.3 1.3 %collective-permute-start.10 = (bf16[2,32,1792]{2,1,0:T(8,128)(2,1)S(1)}, bf16[2,32,1792]{2,1,0:T(8,128)(2,1)S(1)}, u32[]{:S(2)}, u32[]{:S(2)}) collective-permute-start(bf16[2,32,1792]{2,1,0:T(8,128)(2,1)S(1)} %slice.37), channel_id=1, source_target_pairs={{0,2},{2,0},{1,3},{3,1},{4,6},{6,4},{5,7},{7,5},{8,10},{10,8},{9,1... | collective-permute-start | bytes 688136 | tf_op jit(solution)/shard_map/ppermute | solution.py:16
  26.6 3.7 %shard_map.122 = (bf16[2,2,32,896]{3,2,1,0:T(8,128)(2,1)S(1)}, bf16[2,2,32,896]{3,2,1,0:T(8,128)(2,1)S(1)}) custom-call(bf16[4,64,128]{2,1,0:T(8,128)(2,1)S(1)} %get-tuple-element.32.picker, bf16[128,1024]{1,0:T(8,128)(2,1)S(1)} %constant_dynamic-update-slice_fusion.4.tokens, bf16[1024,3584]{1,0:T(8,128)(2,1)} %gate.5, bf16[1024,3584]{1,0:T(8,128)(2,1)} %up.5, ...), custom_call_target="tpu_custom_call" | custom-call | flops 469762048 | bytes 7340032 | tf_op jit(solution)/shard_map/pallas_call | solution.py:230
  30.4 0.1 collective-permute-start.4
  30.5 3.9 %shard_map.126 = (bf16[2,2,32,896]{3,2,1,0:T(8,128)(2,1)S(1)}, bf16[2,2,32,896]{3,2,1,0:T(8,128)(2,1)S(1)}) custom-call(bf16[4,64,128]{2,1,0:T(8,128)(2,1)S(1)} %get-tuple-element.32.picker, bf16[128,1024]{1,0:T(8,128)(2,1)S(1)} %constant_dynamic-update-slice_fusion.4.tokens, bf16[1024,3584]{1,0:T(8,128)(2,1)} %gate.5, bf16[1024,3584]{1,0:T(8,128)(2,1)} %up.5, ...), custom_call_target="tpu_custom_call" | custom-call | flops 469762048 | bytes 7340032 | tf_op jit(solution)/shard_map/pallas_call | solution.py:230
  34.4 0.5 collective-permute-start.14
  34.9 0.1 fusion.3
  35.0 0.8 collective-permute-start.8
  35.9 0.3 collective-permute-done.10
  36.2 0.1 fusion.1
  36.3 1.6 %collective-permute-start.11 = (bf16[32,1792]{1,0:T(8,128)(2,1)S(1)}, bf16[32,1792]{1,0:T(8,128)(2,1)S(1)}, u32[]{:S(2)}, u32[]{:S(2)}) collective-permute-start(bf16[32,1792]{1,0:T(8,128)(2,1)S(1)} %fusion.1), channel_id=1, source_target_pairs={{0,2},{2,0},{1,3},{3,1},{4,6},{6,4},{5,7},{7,5},{8,10},{10,8},{9,1... | collective-permute-start | bytes 344072 | tf_op jit(solution)/shard_map/ppermute | solution.py:16
  37.9 0.6 collective-permute-start.15
  38.5 2.6 %collective-permute-done.8 = bf16[32,1792]{1,0:T(8,128)(2,1)S(1)} collective-permute-done((bf16[32,1792]{1,0:T(8,128)(2,1)S(1)}, bf16[32,1792]{1,0:T(8,128)(2,1)S(1)}, u32[]{:S(2)}, u32[]{:S(2)}) %collective-permute-start.8) | collective-permute-done | bytes 114720 | tf_op jit(solution)/shard_map/ppermute | solution.py:16
  41.1 0.1 collective-permute-start.9
  41.2 2.4 %collective-permute-done.11 = bf16[32,1792]{1,0:T(8,128)(2,1)S(1)} collective-permute-done((bf16[32,1792]{1,0:T(8,128)(2,1)S(1)}, bf16[32,1792]{1,0:T(8,128)(2,1)S(1)}, u32[]{:S(2)}, u32[]{:S(2)}) %collective-permute-start.11) | collective-permute-done | bytes 114720 | tf_op jit(solution)/shard_map/ppermute | solution.py:16
  43.7 0.8 collective-permute-start.5
  44.6 0.5 collective-permute-done.12.refs_3_
  45.1 0.6 shard_map.124
  45.8 1.1 %convolution_convert_fusion.1.rest_0_ = bf16[128,1024]{1,0:T(8,128)(2,1)S(1)} fusion(bf16[128,3584]{1,0:T(8,128)(2,1)S(1)} %shard_map.124, bf16[3584,1024]{1,0:T(8,128)(2,1)S(1)} %bitcast.30), kind=kOutput, calls=%fused_computation.1 | convolution fusion | flops 939655168 | bytes 8519680 | tf_op jit(solution)/shard_map/dot_general | solution.py:584
  46.9 1.3 %collective-permute-done.15.other = bf16[2,2,32,896]{3,2,1,0:T(8,128)(2,1)S(1)} collective-permute-done((bf16[2,2,32,896]{3,2,1,0:T(8,128)(2,1)S(1)}, bf16[2,2,32,896]{3,2,1,0:T(8,128)(2,1)S(1)}, u32[]{:S(2)}, u32[]{:S(2)}) %collective-permute-start.15) | collective-permute-done | bytes 229408 | tf_op jit(solution)/shard_map/ppermute | solution.py:16
  48.2 0.1 shard_map.127
  48.4 4.1 %collective-permute-done.5.other = bf16[2,2,32,896]{3,2,1,0:T(8,128)(2,1)S(1)} collective-permute-done((bf16[2,2,32,896]{3,2,1,0:T(8,128)(2,1)S(1)}, bf16[2,2,32,896]{3,2,1,0:T(8,128)(2,1)S(1)}, u32[]{:S(2)}, u32[]{:S(2)}) %collective-permute-start.5) | collective-permute-done | bytes 229408 | tf_op jit(solution)/shard_map/ppermute | solution.py:16
  52.5 0.1 shard_map.125
  52.7 1.3 %collective-permute-done.13 = bf16[2,32,896]{2,1,0:T(8,128)(2,1)S(1)} collective-permute-done((bf16[2,32,896]{2,1,0:T(8,128)(2,1)S(1)}, bf16[2,32,896]{2,1,0:T(8,128)(2,1)S(1)}, u32[]{:S(2)}, u32[]{:S(2)}) %collective-permute-start.13) | collective-permute-done | bytes 114720 | tf_op jit(solution)/shard_map/ppermute | solution.py:16
  54.0 0.4 shard_map.128.dense
  54.5 4.2 %convolution_convert_fusion.before = bf16[128,1024]{1,0:T(8,128)(2,1)S(1)} fusion(bf16[128,3584]{1,0:T(8,128)(2,1)S(1)} %shard_map.128.dense, bf16[3584,1024]{1,0:T(8,128)(2,1)} %down.3), kind=kOutput, calls=%fused_computation | convolution fusion | flops 939655168 | bytes 8519680 | tf_op jit(solution)/shard_map/dot_general | solution.py:596
  58.7 2.5 %collective-permute-start.19 = (bf16[32,1024]{1,0:T(8,128)(2,1)S(1)}, bf16[32,1024]{1,0:T(8,128)(2,1)S(1)}, u32[]{:S(2)}, u32[]{:S(2)}) collective-permute-start(bf16[32,1024]{1,0:T(8,128)(2,1)S(1)} %get-tuple-element.60), channel_id=1, source_target_pairs={{0,12},{4,8},{8,4},{12,0},{1,13},{5,9},{9,5},{13,1},{2,14},{6,10},... | collective-permute-start | bytes 196616 | tf_op jit(solution)/shard_map/ppermute | solution.py:534
  61.2 0.3 collective-permute-start.18
  61.6 1.6 %collective-permute-start.17 = (bf16[32,1024]{1,0:T(8,128)(2,1)S(1)}, bf16[32,1024]{1,0:T(8,128)(2,1)S(1)}, u32[]{:S(2)}, u32[]{:S(2)}) collective-permute-start(bf16[32,1024]{1,0:T(8,128)(2,1)S(1)} %get-tuple-element.62), channel_id=1, source_target_pairs={{0,4},{4,0},{8,12},{12,8},{1,5},{5,1},{9,13},{13,9},{2,6},{6,2},{1... | collective-permute-start | bytes 196616 | tf_op jit(solution)/shard_map/ppermute | solution.py:534
  63.2 0.4 shard_map.129
  63.6 2.8 %collective-permute-done.19.refs_3_ = bf16[32,1024]{1,0:T(8,128)(2,1)S(1)} collective-permute-done((bf16[32,1024]{1,0:T(8,128)(2,1)S(1)}, bf16[32,1024]{1,0:T(8,128)(2,1)S(1)}, u32[]{:S(2)}, u32[]{:S(2)}) %collective-permute-start.19) | collective-permute-done | bytes 65568 | tf_op jit(solution)/shard_map/ppermute | solution.py:534
  66.4 4.6 %collective-permute-done.18.refs_2_ = bf16[32,1024]{1,0:T(8,128)(2,1)S(1)} collective-permute-done((bf16[32,1024]{1,0:T(8,128)(2,1)S(1)}, bf16[32,1024]{1,0:T(8,128)(2,1)S(1)}, u32[]{:S(2)}, u32[]{:S(2)}) %collective-permute-start.18) | collective-permute-done | bytes 65568 | tf_op jit(solution)/shard_map/ppermute | solution.py:534
  71.0 2.7 %reduce-scatter.2.cloned.1.call-done.refs_4_ = bf16[32,1024]{1,0:T(8,128)(2,1)} async-done(((bf16[128,1024]{1,0:T(8,128)(2,1)}), bf16[32,1024]{1,0:T(8,128)(2,1)}) %reduce-scatter.2.cloned.1.call-update) | async-done | bytes 65552 | tf_op jit(solution)/shard_map/reduce_scatter | solution.py:585
  73.7 0.8 copy-done.2
  74.6 0.7 shard_map.130
  75.2 0.2 collective-permute-start.22
  75.4 0.4 collective-permute-start.21
  75.9 3.8 %collective-permute-start.20 = (bf16[32,1024]{1,0:T(8,128)(2,1)S(1)}, bf16[32,1024]{1,0:T(8,128)(2,1)S(1)}, u32[]{:S(2)}, u32[]{:S(2)}) collective-permute-start(bf16[32,1024]{1,0:T(8,128)(2,1)S(1)} %get-tuple-element.48), channel_id=1, source_target_pairs={{0,4},{4,0},{8,12},{12,8},{1,5},{5,1},{9,13},{13,9},{2,6},{6,2},{1... | collective-permute-start | bytes 196616 | tf_op jit(solution)/shard_map/ppermute | solution.py:534
  79.7 2.4 %collective-permute-done.20 = bf16[32,1024]{1,0:T(8,128)(2,1)S(1)} collective-permute-done((bf16[32,1024]{1,0:T(8,128)(2,1)S(1)}, bf16[32,1024]{1,0:T(8,128)(2,1)S(1)}, u32[]{:S(2)}, u32[]{:S(2)}) %collective-permute-start.20) | collective-permute-done | bytes 65568 | tf_op jit(solution)/shard_map/ppermute | solution.py:534
  82.1 0.2 collective-permute-done.21
  82.3 3.1 %copy-done = bf16[3584,1024]{1,0:T(8,128)(2,1)S(1)} copy-done((bf16[3584,1024]{1,0:T(8,128)(2,1)S(1)}, bf16[3584,1024]{1,0:T(8,128)(2,1)}, u32[]{:S(2)}) %copy-start) | copy-done | bytes 7340056
  85.4 1.3 %shard_map.131 = (bf16[2,32,896]{2,1,0:T(8,128)(2,1)S(1)}, bf16[2,32,896]{2,1,0:T(8,128)(2,1)S(1)}) custom-call(bf16[4,64,128]{2,1,0:T(8,128)(2,1)S(1)} %get-tuple-element.32.picker, bf16[128,1024]{1,0:T(8,128)(2,1)S(1)} %constant_dynamic-update-slice_fusion.residual.before, bf16[3584,1024]{1,0:T(8,128)(2,1)S(1)} %copy-done, ...), custom_call_target="tpu_custom_call" | custom-call | tf_op jit(solution)/shard_map/pallas_call | solution.py:354
  86.8 1.5 %shard_map.132 = (bf16[2,32,896]{2,1,0:T(8,128)(2,1)S(1)}, bf16[2,32,896]{2,1,0:T(8,128)(2,1)S(1)}) custom-call(bf16[4,64,128]{2,1,0:T(8,128)(2,1)S(1)} %get-tuple-element.32.picker, bf16[128,1024]{1,0:T(8,128)(2,1)S(1)} %constant_dynamic-update-slice_fusion.residual.before, bf16[3584,1024]{1,0:T(8,128)(2,1)S(1)} %copy-done, ...), custom_call_target="tpu_custom_call" | custom-call | tf_op jit(solution)/shard_map/pallas_call | solution.py:354
  88.4 0.6 collective-permute-start.25
  89.0 1.3 %collective-permute-start.24 = (bf16[2,32,896]{2,1,0:T(8,128)(2,1)S(1)}, bf16[2,32,896]{2,1,0:T(8,128)(2,1)S(1)}, u32[]{:S(2)}, u32[]{:S(2)}) collective-permute-start(bf16[2,32,896]{2,1,0:T(8,128)(2,1)S(1)} %add_convert_fusion.5.mine), channel_id=1, source_target_pairs={{0,2},{2,0},{1,3},{3,1},{4,6},{6,4},{5,7},{7,5},{8,10},{10,8},{9,1... | collective-permute-start | bytes 344072 | tf_op jit(solution)/shard_map/ppermute | solution.py:16
  90.3 0.9 collective-permute-start.27
  91.2 3.4 %shard_map.133 = (bf16[3584,1024]{1,0:T(8,128)(2,1)}, f32[8,128]{1,0:T(8,128)S(1)}) custom-call(bf16[3584,128]{1,0:T(8,128)(2,1)S(1)} %get-tuple-element.52.hidden, bf16[128,1024]{1,0:T(8,128)(2,1)S(1)} %constant_dynamic-update-slice_fusion.residual.before, bf16[2,32,896]{2,1,0:T(8,128)(2,1)S(1)} %add_convert_fusion.4.before.mine), custom_call_target="tpu_custom_call" | custom-call | flops 939524096 | bytes 7340032 | tf_op jit(solution)/shard_map/pallas_call | solution.py:407
  94.7 0.4 collective-permute-done.24.other
  95.0 0.1 shard_map.134.rest_0_
  95.3 1.3 %collective-permute-done.27.other = bf16[2,32,896]{2,1,0:T(8,128)(2,1)S(1)} collective-permute-done((bf16[2,32,896]{2,1,0:T(8,128)(2,1)S(1)}, bf16[2,32,896]{2,1,0:T(8,128)(2,1)S(1)}, u32[]{:S(2)}, u32[]{:S(2)}) %collective-permute-start.27) | collective-permute-done | bytes 114720 | tf_op jit(solution)/shard_map/ppermute | solution.py:16
  96.6 0.1 shard_map.135.rest_2_
  96.8 1.5 %collective-permute-done.28.rest_3_ = bf16[2,2,32,896]{3,2,1,0:T(8,128)(2,1)S(1)} collective-permute-done((bf16[2,2,32,896]{3,2,1,0:T(8,128)(2,1)S(1)}, bf16[2,2,32,896]{3,2,1,0:T(8,128)(2,1)S(1)}, u32[]{:S(2)}, u32[]{:S(2)}) %collective-permute-start.28) | collective-permute-done | bytes 229408 | tf_op jit(solution)/shard_map/ppermute | solution.py:16
  98.3 6.5 %shard_map.136 = (bf16[1024,3584]{1,0:T(8,128)(2,1)}, bf16[1024,3584]{1,0:T(8,128)(2,1)}) custom-call(bf16[4,64,128]{2,1,0:T(8,128)(2,1)S(1)} %get-tuple-element.32.picker, bf16[1024,128]{1,0:T(8,128)(2,1)S(1)} %get-tuple-element.46.refs_5_.tokens, bf16[2,2,32,896]{3,2,1,0:T(8,128)(2,1)S(1)} %shard_map.134.rest_0_, ...), custom_call_target="tpu_custom_call" | custom-call | flops 1879048192 | bytes 14680064 | tf_op jit(solution)/shard_map/pallas_call | solution.py:457
  (56 shorter events, 1.1 us)
Async XLA Ops:
  7.2 66.6 %reduce-scatter.2.cloned.1.call-start = ((), (), s32[]{:S(2)}) async-start(), calls=%async_computation.1 | async-start | bytes 327680 | tf_op jit(solution)/shard_map/reduce_scatter | solution.py:585
  7.2 11.7 %collective-permute-start = (bf16[32,1024]{1,0:T(8,128)(2,1)}, bf16[32,1024]{1,0:T(8,128)(2,1)S(1)}, u32[]{:S(2)}, u32[]{:S(2)}) collective-permute-start(bf16[32,1024]{1,0:T(8,128)(2,1)} %param.9), channel_id=1, source_target_pairs={{0,4},{4,0},{8,12},{12,8},{1,5},{5,1},{9,13},{13,9},{2,6},{6,2},{1... | collective-permute-start | bytes 196616 | tf_op jit(solution)/shard_map/ppermute | solution.py:534
  10.3 9.2 %collective-permute-start.2 = (bf16[32,1024]{1,0:T(8,128)(2,1)}, bf16[32,1024]{1,0:T(8,128)(2,1)S(1)}, u32[]{:S(2)}, u32[]{:S(2)}) collective-permute-start(bf16[32,1024]{1,0:T(8,128)(2,1)} %param.9), channel_id=1, source_target_pairs={{0,12},{4,8},{8,4},{12,0},{1,13},{5,9},{9,5},{13,1},{2,14},{6,10},... | collective-permute-start | bytes 196616 | tf_op jit(solution)/shard_map/ppermute | solution.py:534
  12.8 6.7 %collective-permute-start.1 = (bf16[32,1024]{1,0:T(8,128)(2,1)}, bf16[32,1024]{1,0:T(8,128)(2,1)S(1)}, u32[]{:S(2)}, u32[]{:S(2)}) collective-permute-start(bf16[32,1024]{1,0:T(8,128)(2,1)} %param.9), channel_id=1, source_target_pairs={{0,8},{4,12},{8,0},{12,4},{1,9},{5,13},{9,1},{13,5},{2,10},{6,14},... | collective-permute-start | bytes 196616 | tf_op jit(solution)/shard_map/ppermute | solution.py:534
  13.0 5.9 %copy-start.3 = (bf16[32,1024]{1,0:T(8,128)(2,1)S(1)}, bf16[32,1024]{1,0:T(8,128)(2,1)}, u32[]{:S(2)}) copy-start(bf16[32,1024]{1,0:T(8,128)(2,1)} %param.9) | copy-start | bytes 196612
  21.2 2.3 %collective-permute-start.6 = (bf16[2,64,1792]{2,1,0:T(8,128)(2,1)S(1)}, bf16[2,64,1792]{2,1,0:T(8,128)(2,1)S(1)}, u32[]{:S(2)}, u32[]{:S(2)}) collective-permute-start(bf16[2,64,1792]{2,1,0:T(8,128)(2,1)S(1)} %get-tuple-element.41), channel_id=1, source_target_pairs={{0,1},{1,0},{2,3},{3,2},{4,5},{5,4},{6,7},{7,6},{8,9},{9,8},{10,11... | collective-permute-start | bytes 1376264 | tf_op jit(solution)/shard_map/ppermute | solution.py:16
  22.9 2.3 %collective-permute-start.3 = (bf16[2,64,1792]{2,1,0:T(8,128)(2,1)S(1)}, bf16[2,64,1792]{2,1,0:T(8,128)(2,1)S(1)}, u32[]{:S(2)}, u32[]{:S(2)}) collective-permute-start(bf16[2,64,1792]{2,1,0:T(8,128)(2,1)S(1)} %get-tuple-element.36), channel_id=1, source_target_pairs={{0,1},{1,0},{2,3},{3,2},{4,5},{5,4},{6,7},{7,6},{8,9},{9,8},{10,11... | collective-permute-start | bytes 1376264 | tf_op jit(solution)/shard_map/ppermute | solution.py:16
  23.6 11.3 %collective-permute-start.7 = (bf16[2,32,1792]{2,1,0:T(8,128)(2,1)S(1)}, bf16[2,32,1792]{2,1,0:T(8,128)(2,1)S(1)}, u32[]{:S(2)}, u32[]{:S(2)}) collective-permute-start(bf16[2,32,1792]{2,1,0:T(8,128)(2,1)S(1)} %slice.33), channel_id=1, source_target_pairs={{0,2},{2,0},{1,3},{3,1},{4,6},{6,4},{5,7},{7,5},{8,10},{10,8},{9,1... | collective-permute-start | bytes 688136 | tf_op jit(solution)/shard_map/ppermute | solution.py:16
  25.3 10.8 %collective-permute-start.10 = (bf16[2,32,1792]{2,1,0:T(8,128)(2,1)S(1)}, bf16[2,32,1792]{2,1,0:T(8,128)(2,1)S(1)}, u32[]{:S(2)}, u32[]{:S(2)}) collective-permute-start(bf16[2,32,1792]{2,1,0:T(8,128)(2,1)S(1)} %slice.37), channel_id=1, source_target_pairs={{0,2},{2,0},{1,3},{3,1},{4,6},{6,4},{5,7},{7,5},{8,10},{10,8},{9,1... | collective-permute-start | bytes 688136 | tf_op jit(solution)/shard_map/ppermute | solution.py:16
  30.4 13.3 %collective-permute-start.4 = (bf16[2,2,32,896]{3,2,1,0:T(8,128)(2,1)S(1)}, bf16[2,2,32,896]{3,2,1,0:T(8,128)(2,1)S(1)}, u32[]{:S(2)}, u32[]{:S(2)}) collective-permute-start(bf16[2,2,32,896]{3,2,1,0:T(8,128)(2,1)S(1)} %get-tuple-element.38), channel_id=1, source_target_pairs={{0,1},{1,0},{2,3},{3,2},{4,5},{5,4},{6,7},{7,6},{8,9},{9,8},{10,11... | collective-permute-start | bytes 688136 | tf_op jit(solution)/shard_map/ppermute | solution.py:16
  30.5 15.2 %slice-start = ((s8[7340032]{0:T(1024)(128)(4,1)}), s8[4194304]{0:T(1024)(128)(4,1)S(1)}, s32[]{:S(2)}) async-start(s8[7340032]{0:T(1024)(128)(4,1)} %bitcast.29), calls=%async_computation.2 | async-start | bytes 8388608
  30.5 15.2 %slice-start.1 = ((s8[7340032]{0:T(1024)(128)(4,1)}), s8[3145728]{0:T(1024)(128)(4,1)S(1)}, s32[]{:S(2)}) async-start(s8[7340032]{0:T(1024)(128)(4,1)} %bitcast.29), calls=%async_computation.3 | async-start | bytes 6291456
  34.4 3.4 %collective-permute-start.14 = (bf16[2,2,32,896]{3,2,1,0:T(8,128)(2,1)S(1)}, bf16[2,2,32,896]{3,2,1,0:T(8,128)(2,1)S(1)}, u32[]{:S(2)}, u32[]{:S(2)}) collective-permute-start(bf16[2,2,32,896]{3,2,1,0:T(8,128)(2,1)S(1)} %get-tuple-element.44), channel_id=1, source_target_pairs={{0,1},{1,0},{2,3},{3,2},{4,5},{5,4},{6,7},{7,6},{8,9},{9,8},{10,11... | collective-permute-start | bytes 688136 | tf_op jit(solution)/shard_map/ppermute | solution.py:16
  35.0 6.1 %collective-permute-start.8 = (bf16[32,1792]{1,0:T(8,128)(2,1)S(1)}, bf16[32,1792]{1,0:T(8,128)(2,1)S(1)}, u32[]{:S(2)}, u32[]{:S(2)}) collective-permute-start(bf16[32,1792]{1,0:T(8,128)(2,1)S(1)} %fusion.3), channel_id=1, source_target_pairs={{0,2},{2,0},{1,3},{3,1},{4,6},{6,4},{5,7},{7,5},{8,10},{10,8},{9,1... | collective-permute-start | bytes 344072 | tf_op jit(solution)/shard_map/ppermute | solution.py:16
  36.3 7.3 %collective-permute-start.11 = (bf16[32,1792]{1,0:T(8,128)(2,1)S(1)}, bf16[32,1792]{1,0:T(8,128)(2,1)S(1)}, u32[]{:S(2)}, u32[]{:S(2)}) collective-permute-start(bf16[32,1792]{1,0:T(8,128)(2,1)S(1)} %fusion.1), channel_id=1, source_target_pairs={{0,2},{2,0},{1,3},{3,1},{4,6},{6,4},{5,7},{7,5},{8,10},{10,8},{9,1... | collective-permute-start | bytes 344072 | tf_op jit(solution)/shard_map/ppermute | solution.py:16
  37.9 10.4 %collective-permute-start.15 = (bf16[2,2,32,896]{3,2,1,0:T(8,128)(2,1)S(1)}, bf16[2,2,32,896]{3,2,1,0:T(8,128)(2,1)S(1)}, u32[]{:S(2)}, u32[]{:S(2)}) collective-permute-start(bf16[2,2,32,896]{3,2,1,0:T(8,128)(2,1)S(1)} %add_convert_fusion.2.mine), channel_id=1, source_target_pairs={{0,2},{2,0},{1,3},{3,1},{4,6},{6,4},{5,7},{7,5},{8,10},{10,8},{9,1... | collective-permute-start | bytes 688136 | tf_op jit(solution)/shard_map/ppermute | solution.py:16
  41.1 3.5 %collective-permute-start.9 = (bf16[64,1792]{1,0:T(8,128)(2,1)S(1)}, bf16[64,1792]{1,0:T(8,128)(2,1)S(1)}, u32[]{:S(2)}, u32[]{:S(2)}) collective-permute-start(bf16[64,1792]{1,0:T(8,128)(2,1)S(1)} %pad_maximum_fusion.refs_0_), channel_id=1, source_target_pairs={{0,1},{1,0},{2,3},{3,2},{4,5},{5,4},{6,7},{7,6},{8,9},{9,8},{10,11... | collective-permute-start | bytes 688136 | tf_op jit(solution)/shard_map/ppermute | solution.py:16
  43.6 1.6 %collective-permute-start.12 = (bf16[64,1792]{1,0:T(8,128)(2,1)S(1)}, bf16[64,1792]{1,0:T(8,128)(2,1)S(1)}, u32[]{:S(2)}, u32[]{:S(2)}) collective-permute-start(bf16[64,1792]{1,0:T(8,128)(2,1)S(1)} %pad_maximum_fusion.1.refs_2_), channel_id=1, source_target_pairs={{0,1},{1,0},{2,3},{3,2},{4,5},{5,4},{6,7},{7,6},{8,9},{9,8},{10,11... | collective-permute-start | bytes 688136 | tf_op jit(solution)/shard_map/ppermute | solution.py:16
  43.7 8.8 %collective-permute-start.5 = (bf16[2,2,32,896]{3,2,1,0:T(8,128)(2,1)S(1)}, bf16[2,2,32,896]{3,2,1,0:T(8,128)(2,1)S(1)}, u32[]{:S(2)}, u32[]{:S(2)}) collective-permute-start(bf16[2,2,32,896]{3,2,1,0:T(8,128)(2,1)S(1)} %add_convert_fusion.3.mine), channel_id=1, source_target_pairs={{0,2},{2,0},{1,3},{3,1},{4,6},{6,4},{5,7},{7,5},{8,10},{10,8},{9,1... | collective-permute-start | bytes 688136 | tf_op jit(solution)/shard_map/ppermute | solution.py:16
  46.9 5.8 %copy-start.1 = (bf16[128,1024]{1,0:T(8,128)(2,1)}, bf16[128,1024]{1,0:T(8,128)(2,1)S(1)}, u32[]{:S(2)}) copy-start(bf16[128,1024]{1,0:T(8,128)(2,1)S(1)} %convolution_convert_fusion.1.rest_0_) | copy-start | bytes 786436
  48.4 4.4 %collective-permute-start.16 = (bf16[2,32,896]{2,1,0:T(8,128)(2,1)S(1)}, bf16[2,32,896]{2,1,0:T(8,128)(2,1)S(1)}, u32[]{:S(2)}, u32[]{:S(2)}) collective-permute-start(bf16[2,32,896]{2,1,0:T(8,128)(2,1)S(1)} %get-tuple-element.45), channel_id=1, source_target_pairs={{0,1},{1,0},{2,3},{3,2},{4,5},{5,4},{6,7},{7,6},{8,9},{9,8},{10,11... | collective-permute-start | bytes 344072 | tf_op jit(solution)/shard_map/ppermute | solution.py:16
  52.6 1.4 %collective-permute-start.13 = (bf16[2,32,896]{2,1,0:T(8,128)(2,1)S(1)}, bf16[2,32,896]{2,1,0:T(8,128)(2,1)S(1)}, u32[]{:S(2)}, u32[]{:S(2)}) collective-permute-start(bf16[2,32,896]{2,1,0:T(8,128)(2,1)S(1)} %get-tuple-element.42), channel_id=1, source_target_pairs={{0,1},{1,0},{2,3},{3,2},{4,5},{5,4},{6,7},{7,6},{8,9},{9,8},{10,11... | collective-permute-start | bytes 344072 | tf_op jit(solution)/shard_map/ppermute | solution.py:16
  58.7 7.7 %collective-permute-start.19 = (bf16[32,1024]{1,0:T(8,128)(2,1)S(1)}, bf16[32,1024]{1,0:T(8,128)(2,1)S(1)}, u32[]{:S(2)}, u32[]{:S(2)}) collective-permute-start(bf16[32,1024]{1,0:T(8,128)(2,1)S(1)} %get-tuple-element.60), channel_id=1, source_target_pairs={{0,12},{4,8},{8,4},{12,0},{1,13},{5,9},{9,5},{13,1},{2,14},{6,10},... | collective-permute-start | bytes 196616 | tf_op jit(solution)/shard_map/ppermute | solution.py:534
  61.2 9.7 %collective-permute-start.18 = (bf16[32,1024]{1,0:T(8,128)(2,1)S(1)}, bf16[32,1024]{1,0:T(8,128)(2,1)S(1)}, u32[]{:S(2)}, u32[]{:S(2)}) collective-permute-start(bf16[32,1024]{1,0:T(8,128)(2,1)S(1)} %get-tuple-element.61), channel_id=1, source_target_pairs={{0,8},{4,12},{8,0},{12,4},{1,9},{5,13},{9,1},{13,5},{2,10},{6,14},... | collective-permute-start | bytes 196616 | tf_op jit(solution)/shard_map/ppermute | solution.py:534
  61.6 9.4 %collective-permute-start.17 = (bf16[32,1024]{1,0:T(8,128)(2,1)S(1)}, bf16[32,1024]{1,0:T(8,128)(2,1)S(1)}, u32[]{:S(2)}, u32[]{:S(2)}) collective-permute-start(bf16[32,1024]{1,0:T(8,128)(2,1)S(1)} %get-tuple-element.62), channel_id=1, source_target_pairs={{0,4},{4,0},{8,12},{12,8},{1,5},{5,1},{9,13},{13,9},{2,6},{6,2},{1... | collective-permute-start | bytes 196616 | tf_op jit(solution)/shard_map/ppermute | solution.py:534
  73.7 0.8 copy-start.2
  75.2 7.1 %collective-permute-start.22 = (bf16[32,1024]{1,0:T(8,128)(2,1)S(1)}, bf16[32,1024]{1,0:T(8,128)(2,1)S(1)}, u32[]{:S(2)}, u32[]{:S(2)}) collective-permute-start(bf16[32,1024]{1,0:T(8,128)(2,1)S(1)} %get-tuple-element.48), channel_id=1, source_target_pairs={{0,12},{4,8},{8,4},{12,0},{1,13},{5,9},{9,5},{13,1},{2,14},{6,10},... | collective-permute-start | bytes 196616 | tf_op jit(solution)/shard_map/ppermute | solution.py:534
  75.4 6.8 %collective-permute-start.21 = (bf16[32,1024]{1,0:T(8,128)(2,1)S(1)}, bf16[32,1024]{1,0:T(8,128)(2,1)S(1)}, u32[]{:S(2)}, u32[]{:S(2)}) collective-permute-start(bf16[32,1024]{1,0:T(8,128)(2,1)S(1)} %get-tuple-element.48), channel_id=1, source_target_pairs={{0,8},{4,12},{8,0},{12,4},{1,9},{5,13},{9,1},{13,5},{2,10},{6,14},... | collective-permute-start | bytes 196616 | tf_op jit(solution)/shard_map/ppermute | solution.py:534
  75.9 6.2 %collective-permute-start.20 = (bf16[32,1024]{1,0:T(8,128)(2,1)S(1)}, bf16[32,1024]{1,0:T(8,128)(2,1)S(1)}, u32[]{:S(2)}, u32[]{:S(2)}) collective-permute-start(bf16[32,1024]{1,0:T(8,128)(2,1)S(1)} %get-tuple-element.48), channel_id=1, source_target_pairs={{0,4},{4,0},{8,12},{12,8},{1,5},{5,1},{9,13},{13,9},{2,6},{6,2},{1... | collective-permute-start | bytes 196616 | tf_op jit(solution)/shard_map/ppermute | solution.py:534
  82.3 3.1 %copy-start = (bf16[3584,1024]{1,0:T(8,128)(2,1)S(1)}, bf16[3584,1024]{1,0:T(8,128)(2,1)}, u32[]{:S(2)}) copy-start(bf16[3584,1024]{1,0:T(8,128)(2,1)} %down.3) | copy-start | bytes 22020100
  86.8 2.2 %collective-permute-start.23 = (bf16[2,32,896]{2,1,0:T(8,128)(2,1)S(1)}, bf16[2,32,896]{2,1,0:T(8,128)(2,1)S(1)}, u32[]{:S(2)}, u32[]{:S(2)}) collective-permute-start(bf16[2,32,896]{2,1,0:T(8,128)(2,1)S(1)} %get-tuple-element.50), channel_id=1, source_target_pairs={{0,1},{1,0},{2,3},{3,2},{4,5},{5,4},{6,7},{7,6},{8,9},{9,8},{10,11... | collective-permute-start | bytes 344072 | tf_op jit(solution)/shard_map/ppermute | solution.py:16
  88.4 1.9 %collective-permute-start.25 = (bf16[2,32,896]{2,1,0:T(8,128)(2,1)S(1)}, bf16[2,32,896]{2,1,0:T(8,128)(2,1)S(1)}, u32[]{:S(2)}, u32[]{:S(2)}) collective-permute-start(bf16[2,32,896]{2,1,0:T(8,128)(2,1)S(1)} %get-tuple-element.54), channel_id=1, source_target_pairs={{0,1},{1,0},{2,3},{3,2},{4,5},{5,4},{6,7},{7,6},{8,9},{9,8},{10,11... | collective-permute-start | bytes 344072 | tf_op jit(solution)/shard_map/ppermute | solution.py:16
  89.0 6.1 %collective-permute-start.24 = (bf16[2,32,896]{2,1,0:T(8,128)(2,1)S(1)}, bf16[2,32,896]{2,1,0:T(8,128)(2,1)S(1)}, u32[]{:S(2)}, u32[]{:S(2)}) collective-permute-start(bf16[2,32,896]{2,1,0:T(8,128)(2,1)S(1)} %add_convert_fusion.5.mine), channel_id=1, source_target_pairs={{0,2},{2,0},{1,3},{3,1},{4,6},{6,4},{5,7},{7,5},{8,10},{10,8},{9,1... | collective-permute-start | bytes 344072 | tf_op jit(solution)/shard_map/ppermute | solution.py:16
  90.3 6.3 %collective-permute-start.27 = (bf16[2,32,896]{2,1,0:T(8,128)(2,1)S(1)}, bf16[2,32,896]{2,1,0:T(8,128)(2,1)S(1)}, u32[]{:S(2)}, u32[]{:S(2)}) collective-permute-start(bf16[2,32,896]{2,1,0:T(8,128)(2,1)S(1)} %add_convert_fusion.4.before.mine), channel_id=1, source_target_pairs={{0,2},{2,0},{1,3},{3,1},{4,6},{6,4},{5,7},{7,5},{8,10},{10,8},{9,1... | collective-permute-start | bytes 344072 | tf_op jit(solution)/shard_map/ppermute | solution.py:16
  95.2 1.6 %collective-permute-start.26 = (bf16[2,2,32,896]{3,2,1,0:T(8,128)(2,1)S(1)}, bf16[2,2,32,896]{3,2,1,0:T(8,128)(2,1)S(1)}, u32[]{:S(2)}, u32[]{:S(2)}) collective-permute-start(bf16[2,2,32,896]{3,2,1,0:T(8,128)(2,1)S(1)} %shard_map.134.rest_0_), channel_id=1, source_target_pairs={{0,1},{1,0},{2,3},{3,2},{4,5},{5,4},{6,7},{7,6},{8,9},{9,8},{10,11... | collective-permute-start | bytes 688136 | tf_op jit(solution)/shard_map/ppermute | solution.py:16
  96.7 1.6 %collective-permute-start.28 = (bf16[2,2,32,896]{3,2,1,0:T(8,128)(2,1)S(1)}, bf16[2,2,32,896]{3,2,1,0:T(8,128)(2,1)S(1)}, u32[]{:S(2)}, u32[]{:S(2)}) collective-permute-start(bf16[2,2,32,896]{3,2,1,0:T(8,128)(2,1)S(1)} %shard_map.135.rest_2_), channel_id=1, source_target_pairs={{0,1},{1,0},{2,3},{3,2},{4,5},{5,4},{6,7},{7,6},{8,9},{9,8},{10,11... | collective-permute-start | bytes 688136 | tf_op jit(solution)/shard_map/ppermute | solution.py:16
Sparse Core Ops, SparseCore 0:
  52.8 20.8 reduce-scatter.1

commit v10 on v6

--- a/solution.py
+++ b/solution.py
@@ -148,18 +148,18 @@
     for i in range(1, ranks):
         student = student + refs[i][...].astype(F32)
         target = target + refs[ranks + i][...].astype(F32)
-    refs[-2][...] = student.astype(BF)
+    refs[-2][...] = student
     refs[-1][...] = (student - target).astype(BF)
 
 
 def residual_of(student, target, before):
     ranks = len(student)
-    block = jax.ShapeDtypeStruct(student[0].shape, BF)
+    shape = student[0].shape
     return pl.pallas_call(
         functools.partial(residual_kernel, ranks),
         in_specs=[whole()] * (2 * ranks) + [anywhere()] * len(before),
         out_specs=(whole(), whole()),
-        out_shape=(block, block),
+        out_shape=(jax.ShapeDtypeStruct(shape, F32), jax.ShapeDtypeStruct(shape, BF)),
         compiler_params=pltpu.CompilerParams(vmem_limit_bytes=4 * 1024 * 1024),
     )(*student, *target, *before)
 
@@ -543,13 +543,20 @@
     def source_of(s):
         return rank ^ s if paired else (rank + ranks - s) % ranks
 
+    def place_rows(blocks):
+        rows = jnp.zeros((token_count, blocks[0].shape[1]), BF)
+        for s, value in enumerate(blocks):
+            rows = lax.dynamic_update_slice(rows, value, (source_of(s) * block, 0))
+        return rows
+
     def gather_tokens(mine):
-        whole_rows = jnp.zeros((token_count, mine.shape[1]), BF)
-        whole_rows = lax.dynamic_update_slice(whole_rows, mine, (rank * block, 0))
-        for s in range(1, ranks):
-            theirs = to_partner(mine, s)
-            whole_rows = lax.dynamic_update_slice(whole_rows, theirs, (source_of(s) * block, 0))
-        return whole_rows
+        return place_rows([mine] + [to_partner(mine, s) for s in range(1, ranks)])
+
+    def gather_forwarded(mine):
+        if not paired or ranks != 4:
+            return gather_tokens(mine)
+        far = to_partner(mine, 2)
+        return place_rows([mine, to_partner(mine, 1), far, to_partner(far, 1)])
 
     def to_owners(product):
         def block_of(r):
@@ -589,7 +596,7 @@
     pre, weighted = [], []
     for first, (keep, theirs) in zip(firsts, parts):
         mine, other = exchange_dp(add(keep, theirs), dps)
-        total, part = hidden_act(mine, other, dps == 2, slot_weight, target[-2:], first)
+        total, part = hidden_act(mine, other, dps == 2, slot_weight, target[-1:], first)
         pre.append(total)
         weighted.append(jnp.concatenate([part, shift(part, "pipe", pipes, 1)], axis=1))
     weighted = jnp.concatenate(weighted, axis=0)
@@ -598,8 +605,8 @@
     product = jnp.dot(dense, expert_down, preferred_element_type=F32).astype(BF)
     student = to_owners(product)
     dense_flipped, base_flipped = flip(dense, base, product)
-    student_out, residual = residual_of(student, target, (base_flipped,))
-    residual = gather_tokens(residual)
+    student_sum, residual = residual_of(student, target, (base_flipped,))
+    residual = gather_forwarded(residual)
 
     sums = []
     last = residual
@@ -614,7 +621,7 @@
         mine = hidden_grad_act(*pairs[i], dps == 2, pre[i], slot_weight, done, first)
         activations.append((mine, shift(mine, "pipe", pipes, 1)))
     grads = input_grads(picker, base_flipped, activations)
-    return (student_out, grads[0], grads[1], grad_down)
+    return (student_sum.astype(BF), grads[0], grads[1], grad_down)
 
 
 def solution(mesh):

time: 91.3 us -> 90.4 us (level)
  waiting for transfers between devices: 25.3 us -> 24.2 us
    ppermute x20, waiting for transfers between devices: 10 us -> 8.42 us  [shift(): lax.ppermute(value, axis, [(i, (i + by) % count) for i in range(count)])]
  transfers between devices with their start and end apart: 32 -> 32, of which waited for: 17 -> 14; matrix products, arithmetic and copies ran while one was open for 4% -> 4% of each run, Pallas kernels for 24% -> 24%
where the time goes in v10:
time: 90.4 us; the launch traced here: 90.3 us
  Pallas kernels  31.6 us (35%)
  starting transfers between devices  29.3 us (32%)
  waiting for transfers between devices  24.2 us (27%)
  matrix products  2.24 us (2%)
  other arithmetic  1.44 us (2%)
  between operations  1.27 us (1%)
    ppermute x12, starting transfers between devices, to_partner(): return lax.ppermute(value, 'expert', [(i, i ^ s) for i in range(ranks)])  17.6 us
    ppermute x12, waiting for transfers between devices, to_partner(): return lax.ppermute(value, 'expert', [(i, i ^ s) for i in range(ranks)])  15.8 us
    ppermute x20, starting transfers between devices, shift(): lax.ppermute(value, axis, [(i, (i + by) % count) for i in range(count)])  11.6 us
    ppermute x20, waiting for transfers between devices, shift(): lax.ppermute(value, axis, [(i, (i + by) % count) for i in range(count)])  8.42 us
    pallas_call x2, Pallas kernels, expert_pre(): pl.pallas_call(functools.partial(expert_kernel, first), in_specs=[whole()...  7.59 us
    pallas_call x1, Pallas kernels, input_grads(): pl.pallas_call(functools.partial(input_grad_kernel, count // len(parts)),...  6.5 us
    pallas_call x1, Pallas kernels, prepare(): pl.pallas_call(functools.partial(prepare_kernel, ranks, capacity, dps, pi...  5.89 us
    pallas_call x1, Pallas kernels, down_grad(): pl.pallas_call(down_grad_kernel, in_specs=[whole(), whole(), anywhere()],...  3.44 us
  transfers between devices with their start and end apart: 32, of which 14 were waited for; matrix products, arithmetic and copies ran while one was open for 4% of the time, Pallas kernels for 24%

profile of v10, /device:TPU:0, one launch (start us, length us, event | category | flops | bytes accessed | tf_op | source)
XLA Modules:
  0.0 90.3 jit_solution(5500575692918404515)
XLA Ops:
  0.6 3.1 %collective-permute-start = (bf16[32,1024]{1,0:T(8,128)(2,1)}, bf16[32,1024]{1,0:T(8,128)(2,1)S(1)}, u32[]{:S(2)}, u32[]{:S(2)}) collective-permute-start(bf16[32,1024]{1,0:T(8,128)(2,1)} %param.9), channel_id=1, source_target_pairs={{0,4},{4,0},{8,12},{12,8},{1,5},{5,1},{9,13},{13,9},{2,6},{6,2},{1... | collective-permute-start | bytes 196616 | tf_op jit(solution)/shard_map/ppermute | solution.py:537
  3.7 2.5 %collective-permute-start.2 = (bf16[32,1024]{1,0:T(8,128)(2,1)}, bf16[32,1024]{1,0:T(8,128)(2,1)S(1)}, u32[]{:S(2)}, u32[]{:S(2)}) collective-permute-start(bf16[32,1024]{1,0:T(8,128)(2,1)} %param.9), channel_id=1, source_target_pairs={{0,12},{4,8},{8,4},{12,0},{1,13},{5,9},{9,5},{13,1},{2,14},{6,10},... | collective-permute-start | bytes 196616 | tf_op jit(solution)/shard_map/ppermute | solution.py:537
  6.2 0.1 collective-permute-start.1
  6.3 0.1 pad_add_fusion.place
  6.4 5.9 %shard_map.120 = (bf16[4,64,128]{2,1,0:T(8,128)(2,1)S(1)}, f32[4,64,1]{2,1,0:T(8,128)S(1)}, bf16[1024,3584]{1,0:T(8,128)(2,1)S(1)}, bf16[1024,3584]{1,0:T(8,128)(2,1)S(1)}) custom-call(s32[3]{0:T(128)S(1)} %pad_add_fusion.place, s32[4,128]{1,0:T(4,128)} %bitcast.33, f32[4,128]{1,0:T(4,128)} %bitcast.34, bf16[1024,3584]{1,0:T(8,128)(2,1)} %gate.3, ...), custom_call_target="tpu_custom_call" | custom-call | bytes 14680064 | tf_op jit(solution)/shard_map/pallas_call | solution.py:122
  12.4 0.5 collective-permute-done.1
  12.9 1.7 %shard_map.123 = (bf16[2,64,1792]{2,1,0:T(8,128)(2,1)S(1)}, bf16[2,64,1792]{2,1,0:T(8,128)(2,1)S(1)}) custom-call(s32[3]{0:T(128)S(1)} %pad_add_fusion.place, bf16[128,1024]{1,0:T(8,128)(2,1)S(1)} %constant_dynamic-update-slice_fusion.4.tokens, bf16[1024,3584]{1,0:T(8,128)(2,1)S(1)} %get-tuple-element.33.gate, bf16[1024,3584]{1,0:T(8,128)(2,1)S(1)} %get-tuple-element.34.up), custom_call_target="tpu_custom_call" | custom-call | flops 939524096 | bytes 7340032 | tf_op jit(solution)/shard_map/pallas_call | solution.py:192
  14.7 1.7 %shard_map.121 = (bf16[2,64,1792]{2,1,0:T(8,128)(2,1)S(1)}, bf16[2,64,1792]{2,1,0:T(8,128)(2,1)S(1)}) custom-call(s32[3]{0:T(128)S(1)} %pad_add_fusion.place, bf16[128,1024]{1,0:T(8,128)(2,1)S(1)} %constant_dynamic-update-slice_fusion.4.tokens, bf16[1024,3584]{1,0:T(8,128)(2,1)S(1)} %get-tuple-element.33.gate, bf16[1024,3584]{1,0:T(8,128)(2,1)S(1)} %get-tuple-element.34.up), custom_call_target="tpu_custom_call" | custom-call | flops 939524096 | bytes 7340032 | tf_op jit(solution)/shard_map/pallas_call | solution.py:192
  16.3 0.6 collective-permute-start.3
  16.9 0.1 add_convert_fusion
  17.0 1.6 %collective-permute-start.7 = (bf16[2,32,1792]{2,1,0:T(8,128)(2,1)S(1)}, bf16[2,32,1792]{2,1,0:T(8,128)(2,1)S(1)}, u32[]{:S(2)}, u32[]{:S(2)}) collective-permute-start(bf16[2,32,1792]{2,1,0:T(8,128)(2,1)S(1)} %slice.33), channel_id=1, source_target_pairs={{0,2},{2,0},{1,3},{3,1},{4,6},{6,4},{5,7},{7,5},{8,10},{10,8},{9,1... | collective-permute-start | bytes 688136 | tf_op jit(solution)/shard_map/ppermute | solution.py:16
  18.6 0.1 add_convert_fusion.1.before
  18.7 1.3 %collective-permute-start.10 = (bf16[2,32,1792]{2,1,0:T(8,128)(2,1)S(1)}, bf16[2,32,1792]{2,1,0:T(8,128)(2,1)S(1)}, u32[]{:S(2)}, u32[]{:S(2)}) collective-permute-start(bf16[2,32,1792]{2,1,0:T(8,128)(2,1)S(1)} %slice.37), channel_id=1, source_target_pairs={{0,2},{2,0},{1,3},{3,1},{4,6},{6,4},{5,7},{7,5},{8,10},{10,8},{9,1... | collective-permute-start | bytes 688136 | tf_op jit(solution)/shard_map/ppermute | solution.py:16
  20.1 3.7 %shard_map.122 = (bf16[2,2,32,896]{3,2,1,0:T(8,128)(2,1)S(1)}, bf16[2,2,32,896]{3,2,1,0:T(8,128)(2,1)S(1)}) custom-call(bf16[4,64,128]{2,1,0:T(8,128)(2,1)S(1)} %get-tuple-element.32.picker, bf16[128,1024]{1,0:T(8,128)(2,1)S(1)} %constant_dynamic-update-slice_fusion.4.tokens, bf16[1024,3584]{1,0:T(8,128)(2,1)} %gate.5, bf16[1024,3584]{1,0:T(8,128)(2,1)} %up.5, ...), custom_call_target="tpu_custom_call" | custom-call | flops 469762048 | bytes 7340032 | tf_op jit(solution)/shard_map/pallas_call | solution.py:233
  23.8 0.1 collective-permute-start.4
  23.9 3.9 %shard_map.126 = (bf16[2,2,32,896]{3,2,1,0:T(8,128)(2,1)S(1)}, bf16[2,2,32,896]{3,2,1,0:T(8,128)(2,1)S(1)}) custom-call(bf16[4,64,128]{2,1,0:T(8,128)(2,1)S(1)} %get-tuple-element.32.picker, bf16[128,1024]{1,0:T(8,128)(2,1)S(1)} %constant_dynamic-update-slice_fusion.4.tokens, bf16[1024,3584]{1,0:T(8,128)(2,1)} %gate.5, bf16[1024,3584]{1,0:T(8,128)(2,1)} %up.5, ...), custom_call_target="tpu_custom_call" | custom-call | flops 469762048 | bytes 7340032 | tf_op jit(solution)/shard_map/pallas_call | solution.py:233
  27.8 0.5 collective-permute-start.15
  28.4 0.1 fusion.3
  28.4 0.8 collective-permute-start.8
  29.3 0.3 collective-permute-done.10
  29.6 0.1 fusion.1
  29.7 1.6 %collective-permute-start.11 = (bf16[32,1792]{1,0:T(8,128)(2,1)S(1)}, bf16[32,1792]{1,0:T(8,128)(2,1)S(1)}, u32[]{:S(2)}, u32[]{:S(2)}) collective-permute-start(bf16[32,1792]{1,0:T(8,128)(2,1)S(1)} %fusion.1), channel_id=1, source_target_pairs={{0,2},{2,0},{1,3},{3,1},{4,6},{6,4},{5,7},{7,5},{8,10},{10,8},{9,1... | collective-permute-start | bytes 344072 | tf_op jit(solution)/shard_map/ppermute | solution.py:16
  31.3 0.6 collective-permute-start.16
  31.9 2.6 %collective-permute-done.8 = bf16[32,1792]{1,0:T(8,128)(2,1)S(1)} collective-permute-done((bf16[32,1792]{1,0:T(8,128)(2,1)S(1)}, bf16[32,1792]{1,0:T(8,128)(2,1)S(1)}, u32[]{:S(2)}, u32[]{:S(2)}) %collective-permute-start.8) | collective-permute-done | bytes 114720 | tf_op jit(solution)/shard_map/ppermute | solution.py:16
  34.5 0.1 collective-permute-start.9
  34.6 2.4 %collective-permute-done.11 = bf16[32,1792]{1,0:T(8,128)(2,1)S(1)} collective-permute-done((bf16[32,1792]{1,0:T(8,128)(2,1)S(1)}, bf16[32,1792]{1,0:T(8,128)(2,1)S(1)}, u32[]{:S(2)}, u32[]{:S(2)}) %collective-permute-start.11) | collective-permute-done | bytes 114720 | tf_op jit(solution)/shard_map/ppermute | solution.py:16
  37.1 0.8 collective-permute-start.5
  38.0 0.5 collective-permute-done.12.refs_3_
  38.5 0.6 shard_map.124
  39.2 1.1 %convolution_convert_fusion.1 = bf16[128,1024]{1,0:T(8,128)(2,1)S(1)} fusion(bf16[128,3584]{1,0:T(8,128)(2,1)S(1)} %shard_map.124, bf16[3584,1024]{1,0:T(8,128)(2,1)S(1)} %bitcast.32), kind=kOutput, calls=%fused_computation.1 | convolution fusion | flops 939655168 | bytes 8519680 | tf_op jit(solution)/shard_map/dot_general | solution.py:594
  40.4 2.5 %collective-permute-start.13 = (bf16[32,1024]{1,0:T(8,128)(2,1)S(1)}, bf16[32,1024]{1,0:T(8,128)(2,1)S(1)}, u32[]{:S(2)}, u32[]{:S(2)}) collective-permute-start(bf16[32,1024]{1,0:T(8,128)(2,1)S(1)} %get-tuple-element.63), channel_id=1, source_target_pairs={{0,12},{4,8},{8,4},{12,0},{1,13},{5,9},{9,5},{13,1},{2,14},{6,10},... | collective-permute-start | bytes 196616 | tf_op jit(solution)/shard_map/ppermute | solution.py:537
  42.9 3.7 %collective-permute-done.13.rest_0_.refs_7_ = bf16[32,1024]{1,0:T(8,128)(2,1)S(1)} collective-permute-done((bf16[32,1024]{1,0:T(8,128)(2,1)S(1)}, bf16[32,1024]{1,0:T(8,128)(2,1)S(1)}, u32[]{:S(2)}, u32[]{:S(2)}) %collective-permute-start.13) | collective-permute-done | bytes 65568 | tf_op jit(solution)/shard_map/ppermute | solution.py:537
  46.6 0.1 shard_map.127
  46.7 0.1 collective-permute-start.17
  46.7 0.1 shard_map.125
  46.9 0.6 collective-permute-start.14
  47.4 1.9 %collective-permute-start.22 = (bf16[32,1024]{1,0:T(8,128)(2,1)S(1)}, bf16[32,1024]{1,0:T(8,128)(2,1)S(1)}, u32[]{:S(2)}, u32[]{:S(2)}) collective-permute-start(bf16[32,1024]{1,0:T(8,128)(2,1)S(1)} %get-tuple-element.60), channel_id=1, source_target_pairs={{0,8},{4,12},{8,0},{12,4},{1,9},{5,13},{9,1},{13,5},{2,10},{6,14},... | collective-permute-start | bytes 196616 | tf_op jit(solution)/shard_map/ppermute | solution.py:537
  49.3 1.1 %collective-permute-start.21 = (bf16[32,1024]{1,0:T(8,128)(2,1)S(1)}, bf16[32,1024]{1,0:T(8,128)(2,1)S(1)}, u32[]{:S(2)}, u32[]{:S(2)}) collective-permute-start(bf16[32,1024]{1,0:T(8,128)(2,1)S(1)} %get-tuple-element.61), channel_id=1, source_target_pairs={{0,4},{4,0},{8,12},{12,8},{1,5},{5,1},{9,13},{13,9},{2,6},{6,2},{1... | collective-permute-start | bytes 196616 | tf_op jit(solution)/shard_map/ppermute | solution.py:537
  50.5 0.4 shard_map.128.dense
  50.9 1.1 %convolution_convert_fusion.before = bf16[128,1024]{1,0:T(8,128)(2,1)S(1)} fusion(bf16[128,3584]{1,0:T(8,128)(2,1)S(1)} %shard_map.128.dense, bf16[3584,1024]{1,0:T(8,128)(2,1)S(1)} %bitcast.30), kind=kOutput, calls=%fused_computation | convolution fusion | flops 939655168 | bytes 8519680 | tf_op jit(solution)/shard_map/dot_general | solution.py:605
  52.1 1.4 %collective-permute-start.20 = (bf16[32,1024]{1,0:T(8,128)(2,1)S(1)}, bf16[32,1024]{1,0:T(8,128)(2,1)S(1)}, u32[]{:S(2)}, u32[]{:S(2)}) collective-permute-start(bf16[32,1024]{1,0:T(8,128)(2,1)S(1)} %get-tuple-element.64), channel_id=1, source_target_pairs={{0,12},{4,8},{8,4},{12,0},{1,13},{5,9},{9,5},{13,1},{2,14},{6,10},... | collective-permute-start | bytes 196616 | tf_op jit(solution)/shard_map/ppermute | solution.py:537
  53.5 1.0 %collective-permute-start.19 = (bf16[32,1024]{1,0:T(8,128)(2,1)S(1)}, bf16[32,1024]{1,0:T(8,128)(2,1)S(1)}, u32[]{:S(2)}, u32[]{:S(2)}) collective-permute-start(bf16[32,1024]{1,0:T(8,128)(2,1)S(1)} %get-tuple-element.65), channel_id=1, source_target_pairs={{0,8},{4,12},{8,0},{12,4},{1,9},{5,13},{9,1},{13,5},{2,10},{6,14},... | collective-permute-start | bytes 196616 | tf_op jit(solution)/shard_map/ppermute | solution.py:537
  54.5 2.0 %collective-permute-start.18 = (bf16[32,1024]{1,0:T(8,128)(2,1)S(1)}, bf16[32,1024]{1,0:T(8,128)(2,1)S(1)}, u32[]{:S(2)}, u32[]{:S(2)}) collective-permute-start(bf16[32,1024]{1,0:T(8,128)(2,1)S(1)} %get-tuple-element.66), channel_id=1, source_target_pairs={{0,4},{4,0},{8,12},{12,8},{1,5},{5,1},{9,13},{13,9},{2,6},{6,2},{1... | collective-permute-start | bytes 196616 | tf_op jit(solution)/shard_map/ppermute | solution.py:537
  56.6 0.4 shard_map.129
  57.0 2.0 %collective-permute-done.20.refs_3_ = bf16[32,1024]{1,0:T(8,128)(2,1)S(1)} collective-permute-done((bf16[32,1024]{1,0:T(8,128)(2,1)S(1)}, bf16[32,1024]{1,0:T(8,128)(2,1)S(1)}, u32[]{:S(2)}, u32[]{:S(2)}) %collective-permute-start.20) | collective-permute-done | bytes 65568 | tf_op jit(solution)/shard_map/ppermute | solution.py:537
  58.9 2.0 %collective-permute-done.19.refs_2_ = bf16[32,1024]{1,0:T(8,128)(2,1)S(1)} collective-permute-done((bf16[32,1024]{1,0:T(8,128)(2,1)S(1)}, bf16[32,1024]{1,0:T(8,128)(2,1)S(1)}, u32[]{:S(2)}, u32[]{:S(2)}) %collective-permute-start.19) | collective-permute-done | bytes 65568 | tf_op jit(solution)/shard_map/ppermute | solution.py:537
  61.0 0.1 shard_map.130
  61.1 1.9 %collective-permute-start.23 = (bf16[32,1024]{1,0:T(8,128)(2,1)S(1)}, bf16[32,1024]{1,0:T(8,128)(2,1)S(1)}, u32[]{:S(2)}, u32[]{:S(2)}) collective-permute-start(bf16[32,1024]{1,0:T(8,128)(2,1)S(1)} %get-tuple-element.48), channel_id=1, source_target_pairs={{0,4},{4,0},{8,12},{12,8},{1,5},{5,1},{9,13},{13,9},{2,6},{6,2},{1... | collective-permute-start | bytes 196616 | tf_op jit(solution)/shard_map/ppermute | solution.py:537
  63.1 3.4 %collective-permute-done.24 = bf16[32,1024]{1,0:T(8,128)(2,1)S(1)} collective-permute-done((bf16[32,1024]{1,0:T(8,128)(2,1)S(1)}, bf16[32,1024]{1,0:T(8,128)(2,1)S(1)}, u32[]{:S(2)}, u32[]{:S(2)}) %collective-permute-start.24) | collective-permute-done | bytes 65568 | tf_op jit(solution)/shard_map/ppermute | solution.py:537
  66.5 4.2 %collective-permute-done.25 = bf16[32,1024]{1,0:T(8,128)(2,1)S(1)} collective-permute-done((bf16[32,1024]{1,0:T(8,128)(2,1)S(1)}, bf16[32,1024]{1,0:T(8,128)(2,1)S(1)}, u32[]{:S(2)}, u32[]{:S(2)}) %collective-permute-start.25) | collective-permute-done | bytes 65568 | tf_op jit(solution)/shard_map/ppermute | solution.py:537
  70.7 1.4 %shard_map.131 = (bf16[2,32,896]{2,1,0:T(8,128)(2,1)S(1)}, bf16[2,32,896]{2,1,0:T(8,128)(2,1)S(1)}) custom-call(bf16[4,64,128]{2,1,0:T(8,128)(2,1)S(1)} %get-tuple-element.32.picker, bf16[128,1024]{1,0:T(8,128)(2,1)S(1)} %constant_dynamic-update-slice_fusion.residual.before, bf16[3584,1024]{1,0:T(8,128)(2,1)S(1)} %bitcast.30, ...), custom_call_target="tpu_custom_call" | custom-call | tf_op jit(solution)/shard_map/pallas_call | solution.py:357
  72.2 1.5 %shard_map.132 = (bf16[2,32,896]{2,1,0:T(8,128)(2,1)S(1)}, bf16[2,32,896]{2,1,0:T(8,128)(2,1)S(1)}) custom-call(bf16[4,64,128]{2,1,0:T(8,128)(2,1)S(1)} %get-tuple-element.32.picker, bf16[128,1024]{1,0:T(8,128)(2,1)S(1)} %constant_dynamic-update-slice_fusion.residual.before, bf16[3584,1024]{1,0:T(8,128)(2,1)S(1)} %bitcast.30, ...), custom_call_target="tpu_custom_call" | custom-call | tf_op jit(solution)/shard_map/pallas_call | solution.py:357
  73.7 0.6 collective-permute-start.28
  74.3 0.8 collective-permute-start.27
  75.2 0.1 collective-permute-done.28
  75.3 1.2 %collective-permute-start.30 = (bf16[2,32,896]{2,1,0:T(8,128)(2,1)S(1)}, bf16[2,32,896]{2,1,0:T(8,128)(2,1)S(1)}, u32[]{:S(2)}, u32[]{:S(2)}) collective-permute-start(bf16[2,32,896]{2,1,0:T(8,128)(2,1)S(1)} %add_convert_fusion.4.before.mine), channel_id=1, source_target_pairs={{0,2},{2,0},{1,3},{3,1},{4,6},{6,4},{5,7},{7,5},{8,10},{10,8},{9,1... | collective-permute-start | bytes 344072 | tf_op jit(solution)/shard_map/ppermute | solution.py:16
  76.5 3.4 %shard_map.133 = (bf16[3584,1024]{1,0:T(8,128)(2,1)}, f32[8,128]{1,0:T(8,128)S(1)}) custom-call(bf16[3584,128]{1,0:T(8,128)(2,1)S(1)} %get-tuple-element.52.hidden, bf16[128,1024]{1,0:T(8,128)(2,1)S(1)} %constant_dynamic-update-slice_fusion.residual.before, bf16[2,32,896]{2,1,0:T(8,128)(2,1)S(1)} %add_convert_fusion.4.before.mine), custom_call_target="tpu_custom_call" | custom-call | flops 939524096 | bytes 7340032 | tf_op jit(solution)/shard_map/pallas_call | solution.py:410
  79.9 0.4 collective-permute-done.27.other
  80.4 0.2 shard_map.134.rest_0_
  80.6 1.3 %collective-permute-done.30.other = bf16[2,32,896]{2,1,0:T(8,128)(2,1)S(1)} collective-permute-done((bf16[2,32,896]{2,1,0:T(8,128)(2,1)S(1)}, bf16[2,32,896]{2,1,0:T(8,128)(2,1)S(1)}, u32[]{:S(2)}, u32[]{:S(2)}) %collective-permute-start.30) | collective-permute-done | bytes 114720 | tf_op jit(solution)/shard_map/ppermute | solution.py:16
  81.9 0.2 shard_map.135.rest_2_
  82.1 0.6 convert_element_type.101
  82.8 0.8 collective-permute-done.31.rest_3_
  83.6 6.5 %shard_map.136 = (bf16[1024,3584]{1,0:T(8,128)(2,1)}, bf16[1024,3584]{1,0:T(8,128)(2,1)}) custom-call(bf16[4,64,128]{2,1,0:T(8,128)(2,1)S(1)} %get-tuple-element.32.picker, bf16[1024,128]{1,0:T(8,128)(2,1)S(1)} %get-tuple-element.46.refs_8_.tokens, bf16[2,2,32,896]{3,2,1,0:T(8,128)(2,1)S(1)} %shard_map.134.rest_0_, ...), custom_call_target="tpu_custom_call" | custom-call | flops 1879048192 | bytes 14680064 | tf_op jit(solution)/shard_map/pallas_call | solution.py:460
  (60 shorter events, 1.1 us)
Async XLA Ops:
  0.6 11.7 %collective-permute-start = (bf16[32,1024]{1,0:T(8,128)(2,1)}, bf16[32,1024]{1,0:T(8,128)(2,1)S(1)}, u32[]{:S(2)}, u32[]{:S(2)}) collective-permute-start(bf16[32,1024]{1,0:T(8,128)(2,1)} %param.9), channel_id=1, source_target_pairs={{0,4},{4,0},{8,12},{12,8},{1,5},{5,1},{9,13},{13,9},{2,6},{6,2},{1... | collective-permute-start | bytes 196616 | tf_op jit(solution)/shard_map/ppermute | solution.py:537
  3.7 9.2 %collective-permute-start.2 = (bf16[32,1024]{1,0:T(8,128)(2,1)}, bf16[32,1024]{1,0:T(8,128)(2,1)S(1)}, u32[]{:S(2)}, u32[]{:S(2)}) collective-permute-start(bf16[32,1024]{1,0:T(8,128)(2,1)} %param.9), channel_id=1, source_target_pairs={{0,12},{4,8},{8,4},{12,0},{1,13},{5,9},{9,5},{13,1},{2,14},{6,10},... | collective-permute-start | bytes 196616 | tf_op jit(solution)/shard_map/ppermute | solution.py:537
  6.2 6.7 %collective-permute-start.1 = (bf16[32,1024]{1,0:T(8,128)(2,1)}, bf16[32,1024]{1,0:T(8,128)(2,1)S(1)}, u32[]{:S(2)}, u32[]{:S(2)}) collective-permute-start(bf16[32,1024]{1,0:T(8,128)(2,1)} %param.9), channel_id=1, source_target_pairs={{0,8},{4,12},{8,0},{12,4},{1,9},{5,13},{9,1},{13,5},{2,10},{6,14},... | collective-permute-start | bytes 196616 | tf_op jit(solution)/shard_map/ppermute | solution.py:537
  6.4 5.9 %copy-start = (bf16[32,1024]{1,0:T(8,128)(2,1)S(1)}, bf16[32,1024]{1,0:T(8,128)(2,1)}, u32[]{:S(2)}) copy-start(bf16[32,1024]{1,0:T(8,128)(2,1)} %param.9) | copy-start | bytes 196612
  14.6 2.3 %collective-permute-start.6 = (bf16[2,64,1792]{2,1,0:T(8,128)(2,1)S(1)}, bf16[2,64,1792]{2,1,0:T(8,128)(2,1)S(1)}, u32[]{:S(2)}, u32[]{:S(2)}) collective-permute-start(bf16[2,64,1792]{2,1,0:T(8,128)(2,1)S(1)} %get-tuple-element.41), channel_id=1, source_target_pairs={{0,1},{1,0},{2,3},{3,2},{4,5},{5,4},{6,7},{7,6},{8,9},{9,8},{10,11... | collective-permute-start | bytes 1376264 | tf_op jit(solution)/shard_map/ppermute | solution.py:16
  16.3 2.3 %collective-permute-start.3 = (bf16[2,64,1792]{2,1,0:T(8,128)(2,1)S(1)}, bf16[2,64,1792]{2,1,0:T(8,128)(2,1)S(1)}, u32[]{:S(2)}, u32[]{:S(2)}) collective-permute-start(bf16[2,64,1792]{2,1,0:T(8,128)(2,1)S(1)} %get-tuple-element.36), channel_id=1, source_target_pairs={{0,1},{1,0},{2,3},{3,2},{4,5},{5,4},{6,7},{7,6},{8,9},{9,8},{10,11... | collective-permute-start | bytes 1376264 | tf_op jit(solution)/shard_map/ppermute | solution.py:16
  17.0 11.3 %collective-permute-start.7 = (bf16[2,32,1792]{2,1,0:T(8,128)(2,1)S(1)}, bf16[2,32,1792]{2,1,0:T(8,128)(2,1)S(1)}, u32[]{:S(2)}, u32[]{:S(2)}) collective-permute-start(bf16[2,32,1792]{2,1,0:T(8,128)(2,1)S(1)} %slice.33), channel_id=1, source_target_pairs={{0,2},{2,0},{1,3},{3,1},{4,6},{6,4},{5,7},{7,5},{8,10},{10,8},{9,1... | collective-permute-start | bytes 688136 | tf_op jit(solution)/shard_map/ppermute | solution.py:16
  18.7 10.8 %collective-permute-start.10 = (bf16[2,32,1792]{2,1,0:T(8,128)(2,1)S(1)}, bf16[2,32,1792]{2,1,0:T(8,128)(2,1)S(1)}, u32[]{:S(2)}, u32[]{:S(2)}) collective-permute-start(bf16[2,32,1792]{2,1,0:T(8,128)(2,1)S(1)} %slice.37), channel_id=1, source_target_pairs={{0,2},{2,0},{1,3},{3,1},{4,6},{6,4},{5,7},{7,5},{8,10},{10,8},{9,1... | collective-permute-start | bytes 688136 | tf_op jit(solution)/shard_map/ppermute | solution.py:16
  23.8 13.3 %collective-permute-start.4 = (bf16[2,2,32,896]{3,2,1,0:T(8,128)(2,1)S(1)}, bf16[2,2,32,896]{3,2,1,0:T(8,128)(2,1)S(1)}, u32[]{:S(2)}, u32[]{:S(2)}) collective-permute-start(bf16[2,2,32,896]{3,2,1,0:T(8,128)(2,1)S(1)} %get-tuple-element.38), channel_id=1, source_target_pairs={{0,1},{1,0},{2,3},{3,2},{4,5},{5,4},{6,7},{7,6},{8,9},{9,8},{10,11... | collective-permute-start | bytes 688136 | tf_op jit(solution)/shard_map/ppermute | solution.py:16
  23.9 15.2 %slice-start.2 = ((s8[7340032]{0:T(1024)(128)(4,1)}), s8[4194304]{0:T(1024)(128)(4,1)S(1)}, s32[]{:S(2)}) async-start(s8[7340032]{0:T(1024)(128)(4,1)} %bitcast.31), calls=%async_computation.2 | async-start | bytes 8388608
  23.9 15.2 %slice-start.3 = ((s8[7340032]{0:T(1024)(128)(4,1)}), s8[3145728]{0:T(1024)(128)(4,1)S(1)}, s32[]{:S(2)}) async-start(s8[7340032]{0:T(1024)(128)(4,1)} %bitcast.31), calls=%async_computation.3 | async-start | bytes 6291456
  27.8 3.4 %collective-permute-start.15 = (bf16[2,2,32,896]{3,2,1,0:T(8,128)(2,1)S(1)}, bf16[2,2,32,896]{3,2,1,0:T(8,128)(2,1)S(1)}, u32[]{:S(2)}, u32[]{:S(2)}) collective-permute-start(bf16[2,2,32,896]{3,2,1,0:T(8,128)(2,1)S(1)} %get-tuple-element.44), channel_id=1, source_target_pairs={{0,1},{1,0},{2,3},{3,2},{4,5},{5,4},{6,7},{7,6},{8,9},{9,8},{10,11... | collective-permute-start | bytes 688136 | tf_op jit(solution)/shard_map/ppermute | solution.py:16
  28.4 6.1 %collective-permute-start.8 = (bf16[32,1792]{1,0:T(8,128)(2,1)S(1)}, bf16[32,1792]{1,0:T(8,128)(2,1)S(1)}, u32[]{:S(2)}, u32[]{:S(2)}) collective-permute-start(bf16[32,1792]{1,0:T(8,128)(2,1)S(1)} %fusion.3), channel_id=1, source_target_pairs={{0,2},{2,0},{1,3},{3,1},{4,6},{6,4},{5,7},{7,5},{8,10},{10,8},{9,1... | collective-permute-start | bytes 344072 | tf_op jit(solution)/shard_map/ppermute | solution.py:16
  29.7 7.3 %collective-permute-start.11 = (bf16[32,1792]{1,0:T(8,128)(2,1)S(1)}, bf16[32,1792]{1,0:T(8,128)(2,1)S(1)}, u32[]{:S(2)}, u32[]{:S(2)}) collective-permute-start(bf16[32,1792]{1,0:T(8,128)(2,1)S(1)} %fusion.1), channel_id=1, source_target_pairs={{0,2},{2,0},{1,3},{3,1},{4,6},{6,4},{5,7},{7,5},{8,10},{10,8},{9,1... | collective-permute-start | bytes 344072 | tf_op jit(solution)/shard_map/ppermute | solution.py:16
  31.3 11.6 %collective-permute-start.16 = (bf16[2,2,32,896]{3,2,1,0:T(8,128)(2,1)S(1)}, bf16[2,2,32,896]{3,2,1,0:T(8,128)(2,1)S(1)}, u32[]{:S(2)}, u32[]{:S(2)}) collective-permute-start(bf16[2,2,32,896]{3,2,1,0:T(8,128)(2,1)S(1)} %add_convert_fusion.2.mine), channel_id=1, source_target_pairs={{0,2},{2,0},{1,3},{3,1},{4,6},{6,4},{5,7},{7,5},{8,10},{10,8},{9,1... | collective-permute-start | bytes 688136 | tf_op jit(solution)/shard_map/ppermute | solution.py:16
  34.5 3.5 %collective-permute-start.9 = (bf16[64,1792]{1,0:T(8,128)(2,1)S(1)}, bf16[64,1792]{1,0:T(8,128)(2,1)S(1)}, u32[]{:S(2)}, u32[]{:S(2)}) collective-permute-start(bf16[64,1792]{1,0:T(8,128)(2,1)S(1)} %pad_maximum_fusion.refs_0_), channel_id=1, source_target_pairs={{0,1},{1,0},{2,3},{3,2},{4,5},{5,4},{6,7},{7,6},{8,9},{9,8},{10,11... | collective-permute-start | bytes 688136 | tf_op jit(solution)/shard_map/ppermute | solution.py:16
  37.0 1.6 %collective-permute-start.12 = (bf16[64,1792]{1,0:T(8,128)(2,1)S(1)}, bf16[64,1792]{1,0:T(8,128)(2,1)S(1)}, u32[]{:S(2)}, u32[]{:S(2)}) collective-permute-start(bf16[64,1792]{1,0:T(8,128)(2,1)S(1)} %pad_maximum_fusion.1.refs_2_), channel_id=1, source_target_pairs={{0,1},{1,0},{2,3},{3,2},{4,5},{5,4},{6,7},{7,6},{8,9},{9,8},{10,11... | collective-permute-start | bytes 688136 | tf_op jit(solution)/shard_map/ppermute | solution.py:16
  37.1 9.6 %collective-permute-start.5 = (bf16[2,2,32,896]{3,2,1,0:T(8,128)(2,1)S(1)}, bf16[2,2,32,896]{3,2,1,0:T(8,128)(2,1)S(1)}, u32[]{:S(2)}, u32[]{:S(2)}) collective-permute-start(bf16[2,2,32,896]{3,2,1,0:T(8,128)(2,1)S(1)} %add_convert_fusion.3.mine), channel_id=1, source_target_pairs={{0,2},{2,0},{1,3},{3,1},{4,6},{6,4},{5,7},{7,5},{8,10},{10,8},{9,1... | collective-permute-start | bytes 688136 | tf_op jit(solution)/shard_map/ppermute | solution.py:16
  38.5 12.4 %slice-start = ((s8[7340032]{0:T(1024)(128)(4,1)}), s8[4194304]{0:T(1024)(128)(4,1)S(1)}, s32[]{:S(2)}) async-start(s8[7340032]{0:T(1024)(128)(4,1)} %bitcast.29), calls=%async_computation | async-start | bytes 8388608
  39.2 11.7 %slice-start.1 = ((s8[7340032]{0:T(1024)(128)(4,1)}), s8[3145728]{0:T(1024)(128)(4,1)S(1)}, s32[]{:S(2)}) async-start(s8[7340032]{0:T(1024)(128)(4,1)} %bitcast.29), calls=%async_computation.1 | async-start | bytes 6291456
  40.4 6.2 %collective-permute-start.13 = (bf16[32,1024]{1,0:T(8,128)(2,1)S(1)}, bf16[32,1024]{1,0:T(8,128)(2,1)S(1)}, u32[]{:S(2)}, u32[]{:S(2)}) collective-permute-start(bf16[32,1024]{1,0:T(8,128)(2,1)S(1)} %get-tuple-element.63), channel_id=1, source_target_pairs={{0,12},{4,8},{8,4},{12,0},{1,13},{5,9},{9,5},{13,1},{2,14},{6,10},... | collective-permute-start | bytes 196616 | tf_op jit(solution)/shard_map/ppermute | solution.py:537
  46.7 3.8 %collective-permute-start.17 = (bf16[2,32,896]{2,1,0:T(8,128)(2,1)S(1)}, bf16[2,32,896]{2,1,0:T(8,128)(2,1)S(1)}, u32[]{:S(2)}, u32[]{:S(2)}) collective-permute-start(bf16[2,32,896]{2,1,0:T(8,128)(2,1)S(1)} %get-tuple-element.45), channel_id=1, source_target_pairs={{0,1},{1,0},{2,3},{3,2},{4,5},{5,4},{6,7},{7,6},{8,9},{9,8},{10,11... | collective-permute-start | bytes 344072 | tf_op jit(solution)/shard_map/ppermute | solution.py:16
  46.9 3.6 %collective-permute-start.14 = (bf16[2,32,896]{2,1,0:T(8,128)(2,1)S(1)}, bf16[2,32,896]{2,1,0:T(8,128)(2,1)S(1)}, u32[]{:S(2)}, u32[]{:S(2)}) collective-permute-start(bf16[2,32,896]{2,1,0:T(8,128)(2,1)S(1)} %get-tuple-element.42), channel_id=1, source_target_pairs={{0,1},{1,0},{2,3},{3,2},{4,5},{5,4},{6,7},{7,6},{8,9},{9,8},{10,11... | collective-permute-start | bytes 344072 | tf_op jit(solution)/shard_map/ppermute | solution.py:16
  47.4 9.5 %collective-permute-start.22 = (bf16[32,1024]{1,0:T(8,128)(2,1)S(1)}, bf16[32,1024]{1,0:T(8,128)(2,1)S(1)}, u32[]{:S(2)}, u32[]{:S(2)}) collective-permute-start(bf16[32,1024]{1,0:T(8,128)(2,1)S(1)} %get-tuple-element.60), channel_id=1, source_target_pairs={{0,8},{4,12},{8,0},{12,4},{1,9},{5,13},{9,1},{13,5},{2,10},{6,14},... | collective-permute-start | bytes 196616 | tf_op jit(solution)/shard_map/ppermute | solution.py:537
  49.3 7.7 %collective-permute-start.21 = (bf16[32,1024]{1,0:T(8,128)(2,1)S(1)}, bf16[32,1024]{1,0:T(8,128)(2,1)S(1)}, u32[]{:S(2)}, u32[]{:S(2)}) collective-permute-start(bf16[32,1024]{1,0:T(8,128)(2,1)S(1)} %get-tuple-element.61), channel_id=1, source_target_pairs={{0,4},{4,0},{8,12},{12,8},{1,5},{5,1},{9,13},{13,9},{2,6},{6,2},{1... | collective-permute-start | bytes 196616 | tf_op jit(solution)/shard_map/ppermute | solution.py:537
  52.1 6.8 %collective-permute-start.20 = (bf16[32,1024]{1,0:T(8,128)(2,1)S(1)}, bf16[32,1024]{1,0:T(8,128)(2,1)S(1)}, u32[]{:S(2)}, u32[]{:S(2)}) collective-permute-start(bf16[32,1024]{1,0:T(8,128)(2,1)S(1)} %get-tuple-element.64), channel_id=1, source_target_pairs={{0,12},{4,8},{8,4},{12,0},{1,13},{5,9},{9,5},{13,1},{2,14},{6,10},... | collective-permute-start | bytes 196616 | tf_op jit(solution)/shard_map/ppermute | solution.py:537
  53.5 7.4 %collective-permute-start.19 = (bf16[32,1024]{1,0:T(8,128)(2,1)S(1)}, bf16[32,1024]{1,0:T(8,128)(2,1)S(1)}, u32[]{:S(2)}, u32[]{:S(2)}) collective-permute-start(bf16[32,1024]{1,0:T(8,128)(2,1)S(1)} %get-tuple-element.65), channel_id=1, source_target_pairs={{0,8},{4,12},{8,0},{12,4},{1,9},{5,13},{9,1},{13,5},{2,10},{6,14},... | collective-permute-start | bytes 196616 | tf_op jit(solution)/shard_map/ppermute | solution.py:537
  54.5 6.5 %collective-permute-start.18 = (bf16[32,1024]{1,0:T(8,128)(2,1)S(1)}, bf16[32,1024]{1,0:T(8,128)(2,1)S(1)}, u32[]{:S(2)}, u32[]{:S(2)}) collective-permute-start(bf16[32,1024]{1,0:T(8,128)(2,1)S(1)} %get-tuple-element.66), channel_id=1, source_target_pairs={{0,4},{4,0},{8,12},{12,8},{1,5},{5,1},{9,13},{13,9},{2,6},{6,2},{1... | collective-permute-start | bytes 196616 | tf_op jit(solution)/shard_map/ppermute | solution.py:537
  61.1 5.4 %collective-permute-start.24 = (bf16[32,1024]{1,0:T(8,128)(2,1)S(1)}, bf16[32,1024]{1,0:T(8,128)(2,1)S(1)}, u32[]{:S(2)}, u32[]{:S(2)}) collective-permute-start(bf16[32,1024]{1,0:T(8,128)(2,1)S(1)} %get-tuple-element.48), channel_id=1, source_target_pairs={{0,8},{4,12},{8,0},{12,4},{1,9},{5,13},{9,1},{13,5},{2,10},{6,14},... | collective-permute-start | bytes 196616 | tf_op jit(solution)/shard_map/ppermute | solution.py:537
  61.1 5.3 %collective-permute-start.23 = (bf16[32,1024]{1,0:T(8,128)(2,1)S(1)}, bf16[32,1024]{1,0:T(8,128)(2,1)S(1)}, u32[]{:S(2)}, u32[]{:S(2)}) collective-permute-start(bf16[32,1024]{1,0:T(8,128)(2,1)S(1)} %get-tuple-element.48), channel_id=1, source_target_pairs={{0,4},{4,0},{8,12},{12,8},{1,5},{5,1},{9,13},{13,9},{2,6},{6,2},{1... | collective-permute-start | bytes 196616 | tf_op jit(solution)/shard_map/ppermute | solution.py:537
  66.4 4.3 %collective-permute-start.25 = (bf16[32,1024]{1,0:T(8,128)(2,1)S(1)}, bf16[32,1024]{1,0:T(8,128)(2,1)S(1)}, u32[]{:S(2)}, u32[]{:S(2)}) collective-permute-start(bf16[32,1024]{1,0:T(8,128)(2,1)S(1)} %collective-permute-done.24), channel_id=1, source_target_pairs={{0,4},{4,0},{8,12},{12,8},{1,5},{5,1},{9,13},{13,9},{2,6},{6,2},{1... | collective-permute-start | bytes 196616 | tf_op jit(solution)/shard_map/ppermute | solution.py:537
  72.1 2.2 %collective-permute-start.26 = (bf16[2,32,896]{2,1,0:T(8,128)(2,1)S(1)}, bf16[2,32,896]{2,1,0:T(8,128)(2,1)S(1)}, u32[]{:S(2)}, u32[]{:S(2)}) collective-permute-start(bf16[2,32,896]{2,1,0:T(8,128)(2,1)S(1)} %get-tuple-element.50), channel_id=1, source_target_pairs={{0,1},{1,0},{2,3},{3,2},{4,5},{5,4},{6,7},{7,6},{8,9},{9,8},{10,11... | collective-permute-start | bytes 344072 | tf_op jit(solution)/shard_map/ppermute | solution.py:16
  73.7 1.5 %collective-permute-start.28 = (bf16[2,32,896]{2,1,0:T(8,128)(2,1)S(1)}, bf16[2,32,896]{2,1,0:T(8,128)(2,1)S(1)}, u32[]{:S(2)}, u32[]{:S(2)}) collective-permute-start(bf16[2,32,896]{2,1,0:T(8,128)(2,1)S(1)} %get-tuple-element.54), channel_id=1, source_target_pairs={{0,1},{1,0},{2,3},{3,2},{4,5},{5,4},{6,7},{7,6},{8,9},{9,8},{10,11... | collective-permute-start | bytes 344072 | tf_op jit(solution)/shard_map/ppermute | solution.py:16
  74.3 6.1 %collective-permute-start.27 = (bf16[2,32,896]{2,1,0:T(8,128)(2,1)S(1)}, bf16[2,32,896]{2,1,0:T(8,128)(2,1)S(1)}, u32[]{:S(2)}, u32[]{:S(2)}) collective-permute-start(bf16[2,32,896]{2,1,0:T(8,128)(2,1)S(1)} %add_convert_fusion.5.mine), channel_id=1, source_target_pairs={{0,2},{2,0},{1,3},{3,1},{4,6},{6,4},{5,7},{7,5},{8,10},{10,8},{9,1... | collective-permute-start | bytes 344072 | tf_op jit(solution)/shard_map/ppermute | solution.py:16
  75.3 6.6 %collective-permute-start.30 = (bf16[2,32,896]{2,1,0:T(8,128)(2,1)S(1)}, bf16[2,32,896]{2,1,0:T(8,128)(2,1)S(1)}, u32[]{:S(2)}, u32[]{:S(2)}) collective-permute-start(bf16[2,32,896]{2,1,0:T(8,128)(2,1)S(1)} %add_convert_fusion.4.before.mine), channel_id=1, source_target_pairs={{0,2},{2,0},{1,3},{3,1},{4,6},{6,4},{5,7},{7,5},{8,10},{10,8},{9,1... | collective-permute-start | bytes 344072 | tf_op jit(solution)/shard_map/ppermute | solution.py:16
  80.5 2.2 %collective-permute-start.29 = (bf16[2,2,32,896]{3,2,1,0:T(8,128)(2,1)S(1)}, bf16[2,2,32,896]{3,2,1,0:T(8,128)(2,1)S(1)}, u32[]{:S(2)}, u32[]{:S(2)}) collective-permute-start(bf16[2,2,32,896]{3,2,1,0:T(8,128)(2,1)S(1)} %shard_map.134.rest_0_), channel_id=1, source_target_pairs={{0,1},{1,0},{2,3},{3,2},{4,5},{5,4},{6,7},{7,6},{8,9},{9,8},{10,11... | collective-permute-start | bytes 688136 | tf_op jit(solution)/shard_map/ppermute | solution.py:16
  82.1 1.6 %collective-permute-start.31 = (bf16[2,2,32,896]{3,2,1,0:T(8,128)(2,1)S(1)}, bf16[2,2,32,896]{3,2,1,0:T(8,128)(2,1)S(1)}, u32[]{:S(2)}, u32[]{:S(2)}) collective-permute-start(bf16[2,2,32,896]{3,2,1,0:T(8,128)(2,1)S(1)} %shard_map.135.rest_2_), channel_id=1, source_target_pairs={{0,1},{1,0},{2,3},{3,2},{4,5},{5,4},{6,7},{7,6},{8,9},{9,8},{10,11... | collective-permute-start | bytes 688136 | tf_op jit(solution)/shard_map/ppermute | solution.py:16

commit v11 on v10

--- a/solution.py
+++ b/solution.py
@@ -57,6 +57,7 @@
 
 
 def prepare_kernel(
+    near_first,
     ranks,
     capacity,
     dps,
@@ -96,14 +97,22 @@
         hit = (routes[k : k + 1, :] == names) & (row < experts)
         weight = weight + jnp.where(hit, shares[k : k + 1, :], 0.0)
         routed = routed + jnp.where(hit, 1.0, 0.0)
+    if near_first:
+        swapped = rank // 2 == 1
+        weight = jnp.where(swapped, pltpu.roll(weight, token_count // 2, 1), weight)
+        routed = jnp.where(swapped, pltpu.roll(routed, token_count // 2, 1), routed)
     t_from = lax.broadcasted_iota(jnp.int32, (token_count, token_count), 0)
     t_to = lax.broadcasted_iota(jnp.int32, (token_count, token_count), 1)
     earlier = jnp.where((t_from // block == t_to // block) & (t_from < t_to), 1.0, 0.0)
     within = dot(routed.astype(BF), earlier.astype(BF)).astype(jnp.int32)
     at_block = lax.broadcasted_iota(jnp.int32, (1, token_count), 1) // block
-    at_pipe = lax.rem(at_block // (dps * per_piece) + pipes - pipe, pipes)
-    at_dp = lax.rem(lax.rem(at_block // per_piece, dps) + dps - dp, dps)
-    first = ((at_pipe * dps + at_dp) * per_piece + lax.rem(at_block, per_piece)) * capacity
+    if near_first:
+        at_pipe = lax.rem(at_block + pipe, 2)
+        first = (at_pipe * 2 + at_block // 2) * capacity
+    else:
+        at_pipe = lax.rem(at_block // (dps * per_piece) + pipes - pipe, pipes)
+        at_dp = lax.rem(lax.rem(at_block // per_piece, dps) + dps - dp, dps)
+        first = ((at_pipe * dps + at_dp) * per_piece + lax.rem(at_block, per_piece)) * capacity
     slot = jnp.where(routed > 0.0, within + first, -1)
     ids = lax.broadcasted_iota(jnp.int32, (slots, token_count), 0)
     for e in range(experts):
@@ -114,13 +123,13 @@
         copy.wait()
 
 
-def prepare(place, routes, shares, gate, up, ranks, dps, pipes, block, experts):
+def prepare(place, routes, shares, gate, up, near_first, ranks, dps, pipes, block, experts):
     assert experts <= 8
     capacity = block // 2
     token_count = block * ranks
     slots = capacity * ranks
     return pl.pallas_call(
-        functools.partial(prepare_kernel, ranks, capacity, dps, pipes),
+        functools.partial(prepare_kernel, near_first, ranks, capacity, dps, pipes),
         in_specs=[scalars(), in_hbm(), in_hbm(), in_hbm(), in_hbm()],
         out_specs=(whole(), whole(), whole(), whole()),
         out_shape=(
@@ -201,45 +210,48 @@
     )(place, tokens, gate, up)
 
 
-def expert_kernel(first, picker, tokens, gate, up, before, keep, send, held, sems):
-    half = keep.shape[2]
-    count = keep.shape[0]
+def expert_kernel(cuts, picker, tokens, gate, up, before, *rest):
+    outs, held, sems = rest[:-2], rest[-2], rest[-1]
+    count, slots = picker.shape[:2]
     pieces = sems.shape[2]
     rows_each = gate.shape[0] // pieces
     copies = {}
-    for i in range(count):
+    for e in range(count):
         for which, weight in enumerate((gate, up)):
             for p in range(pieces):
                 part = pl.ds(p * rows_each, rows_each)
-                columns = pl.ds((first + i) * H, H)
-                copies[i, which, p] = pltpu.make_async_copy(
-                    weight.at[part, columns], held.at[i, which, part], sems.at[i, which, p]
+                columns = pl.ds(e * H, H)
+                copies[e, which, p] = pltpu.make_async_copy(
+                    weight.at[part, columns], held.at[e, which, part], sems.at[e, which, p]
                 )
-                copies[i, which, p].start()
-    for i in range(count):
-        rows = dot(picker[first + i], tokens[...]).astype(BF)
+                copies[e, which, p].start()
+    for e in range(count):
+        rows = dot(picker[e], tokens[...]).astype(BF)
         for which in range(2):
             for p in range(pieces):
-                copies[i, which, p].wait()
-            product = dot(rows, held[i, which]).astype(BF)
-            keep[i, which] = product[:half]
-            send[i, which] = product[half:]
-
-
-def expert_pre(picker, tokens, gate, up, before, first, count):
-    slots = picker.shape[1]
+                copies[e, which, p].wait()
+            product = dot(rows, held[e, which]).astype(BF)
+            for i, (low, high) in enumerate(cuts):
+                outs[2 * i][e, which] = product[low:high]
+                outs[2 * i + 1][e, which] = product[slots // 2 + low : slots // 2 + high]
+
+
+def expert_pre(picker, tokens, gate, up, before, cuts):
+    count, slots = picker.shape[:2]
     width = tokens.shape[1]
-    halves = jax.ShapeDtypeStruct((count, 2, slots // 2, H), BF)
-    return pl.pallas_call(
-        functools.partial(expert_kernel, first),
+    outs = []
+    for low, high in cuts:
+        outs += [jax.ShapeDtypeStruct((count, 2, high - low, H), BF)] * 2
+    return pl.pallas_call(
+        functools.partial(expert_kernel, cuts),
         in_specs=[whole(), whole(), in_hbm(), in_hbm(), anywhere()],
-        out_specs=(whole(), whole()),
-        out_shape=(halves, halves),
+        out_specs=tuple(whole() for _ in outs),
+        out_shape=tuple(outs),
         scratch_shapes=[
             pltpu.VMEM((count, 2, width, H), BF),
             pltpu.SemaphoreType.DMA((count, 2, 4)),
         ],
-        compiler_params=pltpu.CompilerParams(vmem_limit_bytes=16 * 1024 * 1024),
+        compiler_params=pltpu.CompilerParams(vmem_limit_bytes=24 * 1024 * 1024),
         cost_estimate=pl.CostEstimate(
             flops=count * 4 * slots * width * H,
             bytes_accessed=count * 4 * width * H,
@@ -248,26 +260,46 @@
     )(picker, tokens, far(gate), far(up), before)
 
 
-def hidden_act_kernel(first, swap, mine, other, weight, *rest):
+def add_kernel(a, b, before, out):
+    out[...] = (a[...].astype(F32) + b[...].astype(F32)).astype(BF)
+
+
+def add_after(a, b, before):
+    return pl.pallas_call(
+        add_kernel,
+        in_specs=[whole(), whole(), anywhere()],
+        out_specs=whole(),
+        out_shape=jax.ShapeDtypeStruct(a.shape, BF),
+        compiler_params=pltpu.CompilerParams(vmem_limit_bytes=4 * 1024 * 1024),
+    )(a, b, before)
+
+
+def dp_total(mode, mine, other):
+    total = mine.astype(F32)
+    if mode == "add":
+        total = total + other.astype(F32)
+    if mode == "swap":
+        theirs = other.astype(F32)
+        rows = theirs.shape[0]
+        total = total + jnp.concatenate([theirs[rows // 2 :], theirs[: rows // 2]], axis=0)
+    return total
+
+
+def hidden_act_kernel(mode, low, mine, other, weight, *rest):
     pre, out = rest[-2:]
     count, _, rows = mine.shape[:3]
     for i in range(count):
-        totals = []
-        for which in range(2):
-            total = mine[i, which].astype(F32)
-            if swap:
-                theirs = other[i, which].astype(F32)
-                total = total + jnp.concatenate([theirs[rows // 2 :], theirs[: rows // 2]], axis=0)
-            pre[i, which] = total
-            totals.append(total)
-        gate, up = totals
-        out[i] = (gate * jax.nn.sigmoid(gate) * up * weight[first + i, :rows]).astype(BF)
-
-
-def hidden_act(mine, other, swap, weight, before, first):
+        gate = dp_total(mode, mine[i, 0], other[i, 0])
+        up = dp_total(mode, mine[i, 1], other[i, 1])
+        pre[i, 0] = gate
+        pre[i, 1] = up
+        out[i] = (gate * jax.nn.sigmoid(gate) * up * weight[i, low : low + rows]).astype(BF)
+
+
+def hidden_act(mine, other, mode, weight, before, low):
     count, _, rows, width = mine.shape
     return pl.pallas_call(
-        functools.partial(hidden_act_kernel, first, swap),
+        functools.partial(hidden_act_kernel, mode, low),
         in_specs=[whole(), whole(), whole()] + [anywhere()] * len(before),
         out_specs=(whole(), whole()),
         out_shape=(
@@ -276,6 +308,24 @@
         ),
         compiler_params=pltpu.CompilerParams(vmem_limit_bytes=8 * 1024 * 1024),
     )(mine, other, weight, *before)
+
+
+def pair_kernel(*refs):
+    values, out = refs[:-2], refs[-1]
+    rows = out.shape[0] // len(values)
+    for i, value in enumerate(values):
+        out[i * rows : (i + 1) * rows, :] = value[...]
+
+
+def pair(values, before):
+    rows, width = values[0].shape
+    return pl.pallas_call(
+        pair_kernel,
+        in_specs=[whole()] * len(values) + [anywhere()],
+        out_specs=whole(),
+        out_shape=jax.ShapeDtypeStruct((rows * len(values), width), BF),
+        compiler_params=pltpu.CompilerParams(vmem_limit_bytes=4 * 1024 * 1024),
+    )(*values, before)
 
 
 def join_kernel(dps, pipes, place, *refs):
@@ -307,70 +357,75 @@
     )(place, *flat)
 
 
-def spread_kernel(picker, hidden, out):
+def slot_rows(table, low, high):
+    half = table.shape[0] // 2
+    return jnp.concatenate([table[low:high], table[half + low : half + high]], axis=0)
+
+
+def spread_kernel(cut, tokens, picker, mine, theirs, out):
     for e in range(picker.shape[0]):
-        out[:, e * H : (e + 1) * H] = dot(picker[e], hidden[e], 0, 0).astype(BF)
-
-
-def spread(picker, hidden):
-    count, slots, token_count = picker.shape
-    return pl.pallas_call(
-        spread_kernel,
-        in_specs=[whole(), whole()],
+        hidden = jnp.concatenate([mine[e], theirs[e]], axis=0)
+        dense = dot(slot_rows(picker[e], *cut), hidden, 0, 0)[tokens[0] : tokens[1]]
+        out[:, e * H : (e + 1) * H] = dense.astype(BF)
+
+
+def spread(picker, mine, theirs, cut, tokens):
+    count = picker.shape[0]
+    return pl.pallas_call(
+        functools.partial(spread_kernel, cut, tokens),
+        in_specs=[whole()] * 3,
         out_specs=whole(),
-        out_shape=jax.ShapeDtypeStruct((token_count, count * H), BF),
+        out_shape=jax.ShapeDtypeStruct((tokens[1] - tokens[0], count * H), BF),
         compiler_params=pltpu.CompilerParams(vmem_limit_bytes=8 * 1024 * 1024),
-    )(picker, hidden)
-
-
-def flip_kernel(dense, tokens, before, dense_out, tokens_out):
-    dense_out[...] = dense[...].astype(F32).T.astype(BF)
+    )(picker, mine, theirs)
+
+
+def flip_kernel(*refs):
+    dense_out, tokens_out = refs[-2:]
+    tokens = refs[-4]
+    dense = jnp.concatenate([value[...].astype(F32) for value in refs[:-4]], axis=0)
+    dense_out[...] = dense.T.astype(BF)
     tokens_out[...] = tokens[...].astype(F32).T.astype(BF)
 
 
 def flip(dense, tokens, before):
     return pl.pallas_call(
         flip_kernel,
-        in_specs=[whole(), whole(), anywhere()],
+        in_specs=[whole()] * (len(dense) + 1) + [anywhere()],
         out_specs=(whole(), whole()),
         out_shape=(
-            jax.ShapeDtypeStruct(dense.shape[::-1], BF),
+            jax.ShapeDtypeStruct((dense[0].shape[1], tokens.shape[0]), BF),
             jax.ShapeDtypeStruct(tokens.shape[::-1], BF),
         ),
         compiler_params=pltpu.CompilerParams(vmem_limit_bytes=16 * 1024 * 1024),
-    )(dense, tokens, before)
-
-
-def hidden_grad_kernel(first, picker, residual, down, before, keep, send):
-    half = keep.shape[1]
-    for i in range(keep.shape[0]):
-        e = first + i
-        rows = dot(picker[e], residual[...]).astype(BF)
-        product = dot(down[e * H : (e + 1) * H, :], rows, 1, 1).T.astype(BF)
-        keep[i] = product[:half]
-        send[i] = product[half:]
-
-
-def hidden_grad_parts(picker, residual, down, before, first, count):
-    slots = picker.shape[1]
-    halves = jax.ShapeDtypeStruct((count, slots // 2, H), BF)
-    return pl.pallas_call(
-        functools.partial(hidden_grad_kernel, first),
+    )(*dense, tokens, before)
+
+
+def hidden_grad_kernel(cut, picker, residual, down, before, keep, send):
+    rows = keep.shape[1]
+    for e in range(keep.shape[0]):
+        picked = dot(slot_rows(picker[e], *cut), residual[...]).astype(BF)
+        product = dot(down[e * H : (e + 1) * H, :], picked, 1, 1).T.astype(BF)
+        keep[e] = product[:rows]
+        send[e] = product[rows:]
+
+
+def hidden_grad_parts(picker, residual, down, before, cut):
+    count = picker.shape[0]
+    part = jax.ShapeDtypeStruct((count, cut[1] - cut[0], H), BF)
+    return pl.pallas_call(
+        functools.partial(hidden_grad_kernel, cut),
         in_specs=[whole(), whole(), whole(), anywhere()],
         out_specs=(whole(), whole()),
-        out_shape=(halves, halves),
+        out_shape=(part, part),
         compiler_params=pltpu.CompilerParams(vmem_limit_bytes=8 * 1024 * 1024),
     )(picker, residual, down, before)
 
 
-def hidden_grad_act_kernel(first, swap, mine, other, pre, weight, before, out):
+def hidden_grad_act_kernel(mode, low, mine, other, pre, weight, before, out):
     count, rows = mine.shape[:2]
     for i in range(count):
-        total = mine[i].astype(F32)
-        if swap:
-            flipped = jnp.concatenate([other[i, rows // 2 :], other[i, : rows // 2]], axis=0)
-            total = total + flipped.astype(F32)
-        total = total * weight[first + i, :rows]
+        total = dp_total(mode, mine[i], other[i]) * weight[i, low : low + rows]
         pre_gate, pre_up = pre[i, 0], pre[i, 1]
         sig = jax.nn.sigmoid(pre_gate)
         gate_grad = total * pre_up * sig * (1.0 + pre_gate * (1.0 - sig))
@@ -379,10 +434,10 @@
         out[i, 1] = up_grad.astype(BF)
 
 
-def hidden_grad_act(mine, other, swap, pre, weight, before, first):
+def hidden_grad_act(mine, other, mode, pre, weight, before, low):
     count, rows, width = mine.shape
     return pl.pallas_call(
-        functools.partial(hidden_grad_act_kernel, first, swap),
+        functools.partial(hidden_grad_act_kernel, mode, low),
         in_specs=[whole(), whole(), whole(), whole(), anywhere()],
         out_specs=whole(),
         out_shape=jax.ShapeDtypeStruct((count, 2, rows, width), BF),
@@ -428,16 +483,15 @@
     )(hidden, residual, before)
 
 
-def input_grad_kernel(group, picker, tokens, *rest):
-    outs, held, sems = rest[-4:-2], rest[-2], rest[-1]
+def input_grad_kernel(picker, tokens, *rest):
+    parts, outs, held, sems = rest[:-4], rest[-4:-2], rest[-2], rest[-1]
     count = picker.shape[0]
     splits = sems.shape[2]
     rows = tokens.shape[0] // splits
     copies = []
     for i in range(count):
         for which in range(2):
-            mine, theirs = rest[i // group * 2], rest[i // group * 2 + 1]
-            grad = jnp.concatenate([mine[i % group, which], theirs[i % group, which]], axis=0)
+            grad = jnp.concatenate([value[i, which] for value in parts], axis=0)
             dense = dot(picker[i], grad, 0, 0).astype(BF)
             for r in range(splits):
                 part = pl.ds(r * rows, rows)
@@ -458,8 +512,8 @@
     width = tokens.shape[0]
     out = jax.ShapeDtypeStruct((width, count * H), BF)
     return pl.pallas_call(
-        functools.partial(input_grad_kernel, count // len(parts)),
-        in_specs=[whole()] * (2 + 2 * len(parts)),
+        input_grad_kernel,
+        in_specs=[whole()] * (2 + len(parts)),
         out_specs=(in_hbm(), in_hbm()),
         out_shape=(out, out),
         scratch_shapes=[
@@ -472,7 +526,7 @@
             bytes_accessed=count * 4 * width * H,
             transcendentals=0,
         ),
-    )(picker, tokens, *[value for pair in parts for value in pair])
+    )(picker, tokens, *parts)
 
 
 def add(a, b):
@@ -500,11 +554,11 @@
     return jnp.concatenate(gather_dp_parts(value, count), axis=-2)
 
 
-def exchange_dp(value, count):
+def exchange_dp(value, count, same_order):
     if count == 2:
-        return value, shift(value, "dp", count, 1)
+        return value, shift(value, "dp", count, 1), "add" if same_order else "swap"
     total = gather_dp(scatter_dp(value, count).astype(BF), count)
-    return total, total
+    return total, total, "whole"
 
 
 def body(
@@ -530,6 +584,16 @@
     slots = block // 2 * ranks
     place = jnp.stack([rank, dp, pipe]).astype(jnp.int32)
 
+    near_first = (ranks, dps, pipes) == (4, 2, 2)
+    offset = rank // 2 * 2 if near_first else 0
+    capacity = slots // ranks
+    if near_first:
+        cuts = [(capacity, 2 * capacity), (0, capacity)]
+        token_cuts = [(token_count // 2, token_count), (0, token_count // 2)]
+    else:
+        cuts = [(0, slots // 2)]
+        token_cuts = [(0, token_count)]
+
     paired = ranks & (ranks - 1) == 0
 
     def to_partner(value, s):
@@ -543,30 +607,40 @@
     def source_of(s):
         return rank ^ s if paired else (rank + ranks - s) % ranks
 
-    def place_rows(blocks):
-        rows = jnp.zeros((token_count, blocks[0].shape[1]), BF)
-        for s, value in enumerate(blocks):
-            rows = lax.dynamic_update_slice(rows, value, (source_of(s) * block, 0))
+    def place_rows(rows, blocks):
+        for s, value in blocks:
+            at = (source_of(s) ^ offset) * block
+            rows = lax.dynamic_update_slice(rows, value, (at, 0))
         return rows
 
     def gather_tokens(mine):
-        return place_rows([mine] + [to_partner(mine, s) for s in range(1, ranks)])
-
-    def gather_forwarded(mine):
-        if not paired or ranks != 4:
-            return gather_tokens(mine)
-        far = to_partner(mine, 2)
-        return place_rows([mine, to_partner(mine, 1), far, to_partner(far, 1)])
-
-    def to_owners(product):
-        def block_of(r):
-            return lax.dynamic_slice_in_dim(product, r * block, block, axis=0)
-
-        return [block_of(rank)] + [to_partner(block_of(target_of(s)), s) for s in range(1, ranks)]
-
-    base = gather_tokens(tokens)
+        rows = place_rows(jnp.zeros((token_count, mine.shape[1]), BF), [(0, mine)])
+        near = range(1, 2 if near_first else ranks)
+        near_rows = place_rows(rows, [(s, to_partner(mine, s)) for s in near])
+        rest = range(2, ranks if near_first else 2)
+        return near_rows, place_rows(near_rows, [(s, to_partner(mine, s)) for s in rest])
+
+    def to_owners(product, first, count, low):
+        received = []
+        for s in range(first, first + count):
+            at = (target_of(s) ^ offset) * block - low
+            sent = lax.dynamic_slice_in_dim(product, at, block, axis=0)
+            received.append(to_partner(sent, s) if s else sent)
+        return received
+
+    _, base = gather_tokens(tokens)
     picker, slot_weight, gate_near, up_near = prepare(
-        place, routes.T, gate_weights.T, teacher_gate, teacher_up, ranks, dps, pipes, block, experts
+        place,
+        routes.T,
+        gate_weights.T,
+        teacher_gate,
+        teacher_up,
+        near_first,
+        ranks,
+        dps,
+        pipes,
+        block,
+        experts,
     )
 
     chunks = 2 if teacher_gate.shape[1] % 512 == 0 else 1
@@ -576,51 +650,46 @@
         keep, send = teacher_pre(place, base, gate_near, up_near, i * size, size, dps, pipes)
         halves.append(add(keep, shift(send, "pipe", pipes, 1)))
 
-    group = 2 if experts % 2 == 0 else 1
-    firsts = range(0, experts, group)
-    parts = []
-    last = halves[-1]
-    for first in firsts:
-        keep, send = expert_pre(picker, base, expert_gate, expert_up, last, first, group)
-        last = keep
-        parts.append((keep, shift(send, "pipe", pipes, 1)))
+    outs = expert_pre(picker, base, expert_gate, expert_up, halves[-1], cuts)
+    parts, half = [], halves[-1]
+    for i in range(len(cuts)):
+        half = add_after(outs[2 * i], shift(outs[2 * i + 1], "pipe", pipes, 1), half)
+        parts.append(exchange_dp(half, dps, near_first))
     hiddens = []
     for half in halves:
         total = scatter_dp(half, dps)
         hidden = (jax.nn.silu(total[0]) * total[1]).astype(BF)
-        hidden = jnp.concatenate(gather_dp_parts(hidden, dps), axis=0)
+        hidden = pair(gather_dp_parts(hidden, dps), parts[0][0])
         hiddens.append((hidden, shift(hidden, "pipe", pipes, 1)))
     hidden = join(place, hiddens, dps, pipes)
-    target = to_owners(jnp.dot(hidden, teacher_down, preferred_element_type=F32).astype(BF))
-
-    pre, weighted = [], []
-    for first, (keep, theirs) in zip(firsts, parts):
-        mine, other = exchange_dp(add(keep, theirs), dps)
-        total, part = hidden_act(mine, other, dps == 2, slot_weight, target[-1:], first)
+    product = jnp.dot(hidden, teacher_down, preferred_element_type=F32).astype(BF)
+    target = to_owners(product, 0, ranks, 0)
+
+    pre, dense, student = [], [], []
+    for (mine, other, mode), cut, rows in zip(parts, cuts, token_cuts):
+        total, part = hidden_act(mine, other, mode, slot_weight, [product], cut[0])
         pre.append(total)
-        weighted.append(jnp.concatenate([part, shift(part, "pipe", pipes, 1)], axis=1))
-    weighted = jnp.concatenate(weighted, axis=0)
-
-    dense = spread(picker, weighted)
-    product = jnp.dot(dense, expert_down, preferred_element_type=F32).astype(BF)
-    student = to_owners(product)
-    dense_flipped, base_flipped = flip(dense, base, product)
+        dense.append(spread(picker, part, shift(part, "pipe", pipes, 1), cut, rows))
+        product = jnp.dot(dense[-1], expert_down, preferred_element_type=F32).astype(BF)
+        count = (rows[1] - rows[0]) // block
+        student = to_owners(product, rows[0] // block, count, rows[0]) + student
+    dense_flipped, base_flipped = flip(dense[::-1], base, product)
     student_sum, residual = residual_of(student, target, (base_flipped,))
-    residual = gather_forwarded(residual)
-
-    sums = []
-    last = residual
-    for first in firsts:
-        keep, send = hidden_grad_parts(picker, residual, expert_down, last, first, group)
+
+    residuals = gather_tokens(residual)
+    sums, last = [], residual
+    for rows, cut in zip(residuals[-len(cuts) :], cuts[::-1]):
+        keep, send = hidden_grad_parts(picker, rows, expert_down, last, cut)
         last = keep
         sums.append(add(keep, shift(send, "pipe", pipes, 1)))
-    pairs = [exchange_dp(value, dps) for value in sums]
-    grad_down, done = down_grad(dense_flipped, residual, sums[-1])
-    activations = []
-    for i, first in enumerate(firsts):
-        mine = hidden_grad_act(*pairs[i], dps == 2, pre[i], slot_weight, done, first)
-        activations.append((mine, shift(mine, "pipe", pipes, 1)))
-    grads = input_grads(picker, base_flipped, activations)
+    exchanged = [exchange_dp(value, dps, near_first) for value in sums]
+    grad_down, done = down_grad(dense_flipped, residuals[-1], sums[-1])
+    mine, theirs = [], []
+    for (own, other, mode), total, cut in zip(exchanged, pre[::-1], cuts[::-1]):
+        part = hidden_grad_act(own, other, mode, total, slot_weight, done, cut[0])
+        mine.append(part)
+        theirs.append(shift(part, "pipe", pipes, 1))
+    grads = input_grads(picker, base_flipped, mine + theirs)
     return (student_sum.astype(BF), grads[0], grads[1], grad_down)
 
 

time: 90.4 us -> 89.4 us (0.989)
  waiting for transfers between devices: 24.2 us -> 14 us
  matrix products: 2.24 us -> 7.29 us
  starting transfers between devices: 29.3 us -> 32.4 us
  Pallas kernels: 31.6 us -> 32.7 us
    ppermute x12, waiting for transfers between devices: 15.8 us -> 6.28 us  [to_partner(): return lax.ppermute(value, 'expert', [(i, i ^ s) for i in range(ranks)])]
    dot_general x1, matrix products: 1.12 us -> 4.51 us  [body(): jnp.dot(hidden, teacher_down, preferred_element_type=F32).astype(BF)]
    ppermute x20, starting transfers between devices: 11.6 us -> 13.4 us  [shift(): lax.ppermute(value, axis, [(i, (i + by) % count) for i in range(count)])]
    dot_general x1 -> x2, matrix products: 1.12 us -> 2.78 us  [body(): jnp.dot(dense[-1], expert_down, preferred_element_type=F32).astype(BF)]
    ppermute x12, starting transfers between devices: 17.6 us -> 19.1 us  [to_partner(): return lax.ppermute(value, 'expert', [(i, i ^ s) for i in range(ranks)])]
    pallas_call x12 -> x16, Pallas kernels: 24.2 us -> 25.2 us  [the longest x1 6.5 us: input_grads(): pl.pallas_call(input_grad_kernel, in_specs=[whole()] * (2 + len(parts)),...]
  transfers between devices with their start and end apart: 32 -> 32, of which waited for: 14 -> 10; matrix products, arithmetic and copies ran while one was open for 4% -> 10% of each run, Pallas kernels for 24% -> 27%
where the time goes in v11:
time: 89.4 us; the launch traced here: 89.2 us
  Pallas kernels  32.7 us (37%)
  starting transfers between devices  32.4 us (36%)
  waiting for transfers between devices  14 us (16%)
  matrix products  7.29 us (8%)
  between operations  1.29 us (1%)
  other arithmetic  1.24 us (1%)
    ppermute x12, starting transfers between devices, to_partner(): return lax.ppermute(value, 'expert', [(i, i ^ s) for i in range(ranks)])  19.1 us
    ppermute x20, starting transfers between devices, shift(): lax.ppermute(value, axis, [(i, (i + by) % count) for i in range(count)])  13.4 us
    ppermute x20, waiting for transfers between devices, shift(): lax.ppermute(value, axis, [(i, (i + by) % count) for i in range(count)])  7.74 us
    pallas_call x1, Pallas kernels, input_grads(): pl.pallas_call(input_grad_kernel, in_specs=[whole()] * (2 + len(parts)),...  6.5 us
    ppermute x12, waiting for transfers between devices, to_partner(): return lax.ppermute(value, 'expert', [(i, i ^ s) for i in range(ranks)])  6.28 us
    pallas_call x1, Pallas kernels, expert_pre(): pl.pallas_call(functools.partial(expert_kernel, cuts), in_specs=[whole(),...  5.98 us
    pallas_call x1, Pallas kernels, prepare(): pl.pallas_call(functools.partial(prepare_kernel, near_first, ranks, capac...  5.89 us
    pallas_call x2, Pallas kernels, hidden_grad_parts(): pl.pallas_call(functools.partial(hidden_grad_kernel, cut), in_specs=[whol...  4.97 us
  transfers between devices with their start and end apart: 32, of which 10 were waited for; matrix products, arithmetic and copies ran while one was open for 10% of the time, Pallas kernels for 27%

profile of v11, /device:TPU:0, one launch (start us, length us, event | category | flops | bytes accessed | tf_op | source)
XLA Modules:
  0.0 89.2 jit_solution(4594909319741289748)
XLA Ops:
  0.6 3.1 %collective-permute-start = (bf16[32,1024]{1,0:T(8,128)(2,1)}, bf16[32,1024]{1,0:T(8,128)(2,1)S(1)}, u32[]{:S(2)}, u32[]{:S(2)}) collective-permute-start(bf16[32,1024]{1,0:T(8,128)(2,1)} %param.9), channel_id=1, source_target_pairs={{0,4},{4,0},{8,12},{12,8},{1,5},{5,1},{9,13},{13,9},{2,6},{6,2},{1... | collective-permute-start | bytes 196616 | tf_op jit(solution)/shard_map/ppermute | solution.py:601
  3.7 2.5 %collective-permute-start.2 = (bf16[32,1024]{1,0:T(8,128)(2,1)}, bf16[32,1024]{1,0:T(8,128)(2,1)S(1)}, u32[]{:S(2)}, u32[]{:S(2)}) collective-permute-start(bf16[32,1024]{1,0:T(8,128)(2,1)} %param.9), channel_id=1, source_target_pairs={{0,12},{4,8},{8,4},{12,0},{1,13},{5,9},{9,5},{13,1},{2,14},{6,10},... | collective-permute-start | bytes 196616 | tf_op jit(solution)/shard_map/ppermute | solution.py:601
  6.2 0.1 collective-permute-start.1
  6.3 0.1 pad_add_fusion.place
  6.4 5.9 %shard_map.120 = (bf16[4,64,128]{2,1,0:T(8,128)(2,1)S(1)}, f32[4,64,1]{2,1,0:T(8,128)S(1)}, bf16[1024,3584]{1,0:T(8,128)(2,1)S(1)}, bf16[1024,3584]{1,0:T(8,128)(2,1)S(1)}) custom-call(s32[3]{0:T(128)S(1)} %pad_add_fusion.place, s32[4,128]{1,0:T(4,128)} %bitcast.33, f32[4,128]{1,0:T(4,128)} %bitcast.34, bf16[1024,3584]{1,0:T(8,128)(2,1)} %gate.2, ...), custom_call_target="tpu_custom_call" | custom-call | bytes 14680064 | tf_op jit(solution)/shard_map/pallas_call | solution.py:131
  12.4 0.5 collective-permute-done.1
  12.9 1.7 %shard_map.125 = (bf16[2,64,1792]{2,1,0:T(8,128)(2,1)S(1)}, bf16[2,64,1792]{2,1,0:T(8,128)(2,1)S(1)}) custom-call(s32[3]{0:T(128)S(1)} %pad_add_fusion.place, bf16[128,1024]{1,0:T(8,128)(2,1)S(1)} %constant_dynamic-update-slice_fusion.4.tokens.refs_2_, bf16[1024,3584]{1,0:T(8,128)(2,1)S(1)} %get-tuple-element.33.gate, ...), custom_call_target="tpu_custom_call" | custom-call | flops 939524096 | bytes 7340032 | tf_op jit(solution)/shard_map/pallas_call | solution.py:201
  14.6 0.1 collective-permute-start.8
  14.7 1.7 %shard_map.121 = (bf16[2,64,1792]{2,1,0:T(8,128)(2,1)S(1)}, bf16[2,64,1792]{2,1,0:T(8,128)(2,1)S(1)}) custom-call(s32[3]{0:T(128)S(1)} %pad_add_fusion.place, bf16[128,1024]{1,0:T(8,128)(2,1)S(1)} %constant_dynamic-update-slice_fusion.4.tokens.refs_2_, bf16[1024,3584]{1,0:T(8,128)(2,1)S(1)} %get-tuple-element.33.gate, ...), custom_call_target="tpu_custom_call" | custom-call | flops 939524096 | bytes 7340032 | tf_op jit(solution)/shard_map/pallas_call | solution.py:201
  16.3 0.6 collective-permute-start.3
  16.9 0.1 add_convert_fusion
  17.0 1.6 %collective-permute-start.9 = (bf16[2,32,1792]{2,1,0:T(8,128)(2,1)S(1)}, bf16[2,32,1792]{2,1,0:T(8,128)(2,1)S(1)}, u32[]{:S(2)}, u32[]{:S(2)}) collective-permute-start(bf16[2,32,1792]{2,1,0:T(8,128)(2,1)S(1)} %slice.33), channel_id=1, source_target_pairs={{0,2},{2,0},{1,3},{3,1},{4,6},{6,4},{5,7},{7,5},{8,10},{10,8},{9,1... | collective-permute-start | bytes 688136 | tf_op jit(solution)/shard_map/ppermute | solution.py:16
  18.6 0.1 add_convert_fusion.1.before
  18.7 1.3 %collective-permute-start.12 = (bf16[2,32,1792]{2,1,0:T(8,128)(2,1)S(1)}, bf16[2,32,1792]{2,1,0:T(8,128)(2,1)S(1)}, u32[]{:S(2)}, u32[]{:S(2)}) collective-permute-start(bf16[2,32,1792]{2,1,0:T(8,128)(2,1)S(1)} %slice.37), channel_id=1, source_target_pairs={{0,2},{2,0},{1,3},{3,1},{4,6},{6,4},{5,7},{7,5},{8,10},{10,8},{9,1... | collective-permute-start | bytes 688136 | tf_op jit(solution)/shard_map/ppermute | solution.py:16
  20.1 6.0 %shard_map.122 = (bf16[4,2,16,896]{3,2,1,0:T(8,128)(2,1)S(1)}, bf16[4,2,16,896]{3,2,1,0:T(8,128)(2,1)S(1)}, bf16[4,2,16,896]{3,2,1,0:T(8,128)(2,1)S(1)}, bf16[4,2,16,896]{3,2,1,0:T(8,128)(2,1)S(1)}) custom-call(bf16[4,64,128]{2,1,0:T(8,128)(2,1)S(1)} %get-tuple-element.32.picker, bf16[128,1024]{1,0:T(8,128)(2,1)S(1)} %constant_dynamic-update-slice_fusion.4.tokens.refs_2_, ...), custom_call_target="tpu_custom_call" | custom-call | flops 939524096 | bytes 14680064 | tf_op jit(solution)/shard_map/pallas_call | solution.py:245
  26.1 0.1 collective-permute-start.5
  26.2 0.1 fusion.3.refs_0_
  26.3 0.9 %collective-permute-start.10 = (bf16[32,1792]{1,0:T(8,128)(2,1)S(1)}, bf16[32,1792]{1,0:T(8,128)(2,1)S(1)}, u32[]{:S(2)}, u32[]{:S(2)}) collective-permute-start(bf16[32,1792]{1,0:T(8,128)(2,1)S(1)} %fusion.3.refs_0_), channel_id=1, source_target_pairs={{0,2},{2,0},{1,3},{3,1},{4,6},{6,4},{5,7},{7,5},{8,10},{10,8},{9,1... | collective-permute-start | bytes 344072 | tf_op jit(solution)/shard_map/ppermute | solution.py:16
  27.3 2.3 %collective-permute-done.12 = bf16[2,32,1792]{2,1,0:T(8,128)(2,1)S(1)} collective-permute-done((bf16[2,32,1792]{2,1,0:T(8,128)(2,1)S(1)}, bf16[2,32,1792]{2,1,0:T(8,128)(2,1)S(1)}, u32[]{:S(2)}, u32[]{:S(2)}) %collective-permute-start.12) | collective-permute-done | bytes 229408 | tf_op jit(solution)/shard_map/ppermute | solution.py:16
  29.7 0.1 fusion.1.refs_0_
  29.7 2.3 %collective-permute-start.13 = (bf16[32,1792]{1,0:T(8,128)(2,1)S(1)}, bf16[32,1792]{1,0:T(8,128)(2,1)S(1)}, u32[]{:S(2)}, u32[]{:S(2)}) collective-permute-start(bf16[32,1792]{1,0:T(8,128)(2,1)S(1)} %fusion.1.refs_0_), channel_id=1, source_target_pairs={{0,2},{2,0},{1,3},{3,1},{4,6},{6,4},{5,7},{7,5},{8,10},{10,8},{9,1... | collective-permute-start | bytes 344072 | tf_op jit(solution)/shard_map/ppermute | solution.py:16
  32.1 0.2 collective-permute-done.10.refs_1_
  32.4 0.3 collective-permute-start.11
  32.7 2.1 %collective-permute-done.13.refs_1_ = bf16[32,1792]{1,0:T(8,128)(2,1)S(1)} collective-permute-done((bf16[32,1792]{1,0:T(8,128)(2,1)S(1)}, bf16[32,1792]{1,0:T(8,128)(2,1)S(1)}, u32[]{:S(2)}, u32[]{:S(2)}) %collective-permute-start.13) | collective-permute-done | bytes 114720 | tf_op jit(solution)/shard_map/ppermute | solution.py:16
  34.8 0.1 collective-permute-start.14
  34.9 2.1 %collective-permute-start.7 = (bf16[4,2,16,896]{3,2,1,0:T(8,128)(2,1)S(1)}, bf16[4,2,16,896]{3,2,1,0:T(8,128)(2,1)S(1)}, u32[]{:S(2)}, u32[]{:S(2)}) collective-permute-start(bf16[4,2,16,896]{3,2,1,0:T(8,128)(2,1)S(1)} %shard_map.123.before.refs_2_.mine), channel_id=1, source_target_pairs={{0,2},{2,0},{1,3},{3,1},{4,6},{6,4},{5,7},{7,5},{8,10},{10,8},{9,1... | collective-permute-start | bytes 688136 | tf_op jit(solution)/shard_map/ppermute | solution.py:16
  37.1 0.1 collective-permute-start.6
  37.2 0.6 shard_map.128
  37.8 4.5 %convolution_convert_fusion.rest_0_ = bf16[128,1024]{1,0:T(8,128)(2,1)S(1)} fusion(bf16[128,3584]{1,0:T(8,128)(2,1)S(1)} %shard_map.128, bf16[3584,1024]{1,0:T(8,128)(2,1)} %param.14), kind=kOutput, calls=%fused_computation | convolution fusion | flops 939655168 | bytes 8519680 | tf_op jit(solution)/shard_map/dot_general | solution.py:665
  42.4 1.1 %collective-permute-done.7.other = bf16[4,2,16,896]{3,2,1,0:T(8,128)(2,1)S(1)} collective-permute-done((bf16[4,2,16,896]{3,2,1,0:T(8,128)(2,1)S(1)}, bf16[4,2,16,896]{3,2,1,0:T(8,128)(2,1)S(1)}, u32[]{:S(2)}, u32[]{:S(2)}) %collective-permute-start.7) | collective-permute-done | bytes 229408 | tf_op jit(solution)/shard_map/ppermute | solution.py:16
  43.5 0.1 shard_map.129
  43.6 0.1 collective-permute-start.15
  43.7 2.5 %collective-permute-start.22 = (bf16[32,1024]{1,0:T(8,128)(2,1)S(1)}, bf16[32,1024]{1,0:T(8,128)(2,1)S(1)}, u32[]{:S(2)}, u32[]{:S(2)}) collective-permute-start(bf16[32,1024]{1,0:T(8,128)(2,1)S(1)} %get-tuple-element.60), channel_id=1, source_target_pairs={{0,12},{4,8},{8,4},{12,0},{1,13},{5,9},{9,5},{13,1},{2,14},{6,10},... | collective-permute-start | bytes 196616 | tf_op jit(solution)/shard_map/ppermute | solution.py:601
  46.2 0.3 collective-permute-start.21
  46.6 1.6 %collective-permute-start.20 = (bf16[32,1024]{1,0:T(8,128)(2,1)S(1)}, bf16[32,1024]{1,0:T(8,128)(2,1)S(1)}, u32[]{:S(2)}, u32[]{:S(2)}) collective-permute-start(bf16[32,1024]{1,0:T(8,128)(2,1)S(1)} %get-tuple-element.62), channel_id=1, source_target_pairs={{0,4},{4,0},{8,12},{12,8},{1,5},{5,1},{9,13},{13,9},{2,6},{6,2},{1... | collective-permute-start | bytes 196616 | tf_op jit(solution)/shard_map/ppermute | solution.py:601
  48.2 0.4 shard_map.130.refs_1_
  48.6 1.4 %convolution_convert_fusion.2.rest_0_ = bf16[64,1024]{1,0:T(8,128)(2,1)S(1)} fusion(bf16[64,3584]{1,0:T(8,128)(2,1)S(1)} %shard_map.130.refs_1_, bf16[3584,1024]{1,0:T(8,128)(2,1)S(1)} %bitcast.32), kind=kOutput, calls=%fused_computation.2 | convolution fusion | flops 469827584 | bytes 7929856 | tf_op jit(solution)/shard_map/dot_general | solution.py:673
  50.0 0.1 shard_map.131
  50.1 0.1 collective-permute-start.16
  50.2 2.5 %collective-permute-start.19 = (bf16[32,1024]{1,0:T(8,128)(2,1)S(1)}, bf16[32,1024]{1,0:T(8,128)(2,1)S(1)}, u32[]{:S(2)}, u32[]{:S(2)}) collective-permute-start(bf16[32,1024]{1,0:T(8,128)(2,1)S(1)} %get-tuple-element.64), channel_id=1, source_target_pairs={{0,12},{4,8},{8,4},{12,0},{1,13},{5,9},{9,5},{13,1},{2,14},{6,10},... | collective-permute-start | bytes 196616 | tf_op jit(solution)/shard_map/ppermute | solution.py:601
  52.8 0.2 collective-permute-start.18
  53.0 0.4 shard_map.132.refs_0_
  53.4 1.4 %convolution_convert_fusion.1.refs_3_ = bf16[64,1024]{1,0:T(8,128)(2,1)S(1)} fusion(bf16[64,3584]{1,0:T(8,128)(2,1)S(1)} %shard_map.132.refs_0_, bf16[3584,1024]{1,0:T(8,128)(2,1)S(1)} %bitcast.32), kind=kOutput, calls=%fused_computation.1 | convolution fusion | flops 469827584 | bytes 7929856 | tf_op jit(solution)/shard_map/dot_general | solution.py:673
  54.8 1.8 %collective-permute-start.17 = (bf16[32,1024]{1,0:T(8,128)(2,1)S(1)}, bf16[32,1024]{1,0:T(8,128)(2,1)S(1)}, u32[]{:S(2)}, u32[]{:S(2)}) collective-permute-start(bf16[32,1024]{1,0:T(8,128)(2,1)S(1)} %get-tuple-element.66), channel_id=1, source_target_pairs={{0,4},{4,0},{8,12},{12,8},{1,5},{5,1},{9,13},{13,9},{2,6},{6,2},{1... | collective-permute-start | bytes 196616 | tf_op jit(solution)/shard_map/ppermute | solution.py:601
  56.6 0.4 shard_map.133
  57.0 2.5 %collective-permute-done.18.refs_2_ = bf16[32,1024]{1,0:T(8,128)(2,1)S(1)} collective-permute-done((bf16[32,1024]{1,0:T(8,128)(2,1)S(1)}, bf16[32,1024]{1,0:T(8,128)(2,1)S(1)}, u32[]{:S(2)}, u32[]{:S(2)}) %collective-permute-start.18) | collective-permute-done | bytes 65568 | tf_op jit(solution)/shard_map/ppermute | solution.py:601
  59.5 0.7 collective-permute-done.17.refs_1_
  60.2 0.1 shard_map.134
  60.3 2.4 %collective-permute-start.27 = (bf16[32,1024]{1,0:T(8,128)(2,1)S(1)}, bf16[32,1024]{1,0:T(8,128)(2,1)S(1)}, u32[]{:S(2)}, u32[]{:S(2)}) collective-permute-start(bf16[32,1024]{1,0:T(8,128)(2,1)S(1)} %get-tuple-element.48.before), channel_id=1, source_target_pairs={{0,12},{4,8},{8,4},{12,0},{1,13},{5,9},{9,5},{13,1},{2,14},{6,10},... | collective-permute-start | bytes 196616 | tf_op jit(solution)/shard_map/ppermute | solution.py:601
  62.7 2.0 %collective-permute-start.23 = (bf16[32,1024]{1,0:T(8,128)(2,1)S(1)}, bf16[32,1024]{1,0:T(8,128)(2,1)S(1)}, u32[]{:S(2)}, u32[]{:S(2)}) collective-permute-start(bf16[32,1024]{1,0:T(8,128)(2,1)S(1)} %get-tuple-element.48.before), channel_id=1, source_target_pairs={{0,4},{4,0},{8,12},{12,8},{1,5},{5,1},{9,13},{13,9},{2,6},{6,2},{1... | collective-permute-start | bytes 196616 | tf_op jit(solution)/shard_map/ppermute | solution.py:601
  64.8 2.6 %collective-permute-done.23 = bf16[32,1024]{1,0:T(8,128)(2,1)S(1)} collective-permute-done((bf16[32,1024]{1,0:T(8,128)(2,1)S(1)}, bf16[32,1024]{1,0:T(8,128)(2,1)S(1)}, u32[]{:S(2)}, u32[]{:S(2)}) %collective-permute-start.23) | collective-permute-done | bytes 65568 | tf_op jit(solution)/shard_map/ppermute | solution.py:601
  67.4 2.6 %shard_map.135 = (bf16[4,16,896]{2,1,0:T(8,128)(2,1)S(1)}, bf16[4,16,896]{2,1,0:T(8,128)(2,1)S(1)}) custom-call(bf16[4,64,128]{2,1,0:T(8,128)(2,1)S(1)} %get-tuple-element.32.picker, bf16[128,1024]{1,0:T(8,128)(2,1)S(1)} %constant_dynamic-update-slice_fusion.2.residual, bf16[3584,1024]{1,0:T(8,128)(2,1)S(1)} %bitcast.32, ...), custom_call_target="tpu_custom_call" | custom-call | tf_op jit(solution)/shard_map/pallas_call | solution.py:416
  70.1 2.4 %shard_map.136 = (bf16[4,16,896]{2,1,0:T(8,128)(2,1)S(1)}, bf16[4,16,896]{2,1,0:T(8,128)(2,1)S(1)}) custom-call(bf16[4,64,128]{2,1,0:T(8,128)(2,1)S(1)} %get-tuple-element.32.picker, bf16[128,1024]{1,0:T(8,128)(2,1)S(1)} %constant_dynamic-update-slice_fusion.residual, bf16[3584,1024]{1,0:T(8,128)(2,1)S(1)} %bitcast.32, ...), custom_call_target="tpu_custom_call" | custom-call | tf_op jit(solution)/shard_map/pallas_call | solution.py:416
  72.5 0.5 collective-permute-start.28
  73.0 2.0 %collective-permute-start.25 = (bf16[4,16,896]{2,1,0:T(8,128)(2,1)S(1)}, bf16[4,16,896]{2,1,0:T(8,128)(2,1)S(1)}, u32[]{:S(2)}, u32[]{:S(2)}) collective-permute-start(bf16[4,16,896]{2,1,0:T(8,128)(2,1)S(1)} %add_convert_fusion.3.mine), channel_id=1, source_target_pairs={{0,2},{2,0},{1,3},{3,1},{4,6},{6,4},{5,7},{7,5},{8,10},{10,8},{9,1... | collective-permute-start | bytes 344072 | tf_op jit(solution)/shard_map/ppermute | solution.py:16
  75.1 0.9 %collective-permute-start.29 = (bf16[4,16,896]{2,1,0:T(8,128)(2,1)S(1)}, bf16[4,16,896]{2,1,0:T(8,128)(2,1)S(1)}, u32[]{:S(2)}, u32[]{:S(2)}) collective-permute-start(bf16[4,16,896]{2,1,0:T(8,128)(2,1)S(1)} %add_convert_fusion.2.before.mine), channel_id=1, source_target_pairs={{0,2},{2,0},{1,3},{3,1},{4,6},{6,4},{5,7},{7,5},{8,10},{10,8},{9,1... | collective-permute-start | bytes 344072 | tf_op jit(solution)/shard_map/ppermute | solution.py:16
  76.0 3.4 %shard_map.137 = (bf16[3584,1024]{1,0:T(8,128)(2,1)}, f32[8,128]{1,0:T(8,128)S(1)}) custom-call(bf16[3584,128]{1,0:T(8,128)(2,1)S(1)} %get-tuple-element.52.hidden, bf16[128,1024]{1,0:T(8,128)(2,1)S(1)} %constant_dynamic-update-slice_fusion.residual, bf16[4,16,896]{2,1,0:T(8,128)(2,1)S(1)} %add_convert_fusion.2.before.mine), custom_call_target="tpu_custom_call" | custom-call | flops 939524096 | bytes 7340032 | tf_op jit(solution)/shard_map/pallas_call | solution.py:465
  79.5 0.2 shard_map.138.rest_0_
  79.6 0.1 collective-permute-start.30
  79.8 1.1 %collective-permute-done.29.other = bf16[4,16,896]{2,1,0:T(8,128)(2,1)S(1)} collective-permute-done((bf16[4,16,896]{2,1,0:T(8,128)(2,1)S(1)}, bf16[4,16,896]{2,1,0:T(8,128)(2,1)S(1)}, u32[]{:S(2)}, u32[]{:S(2)}) %collective-permute-start.29) | collective-permute-done | bytes 114720 | tf_op jit(solution)/shard_map/ppermute | solution.py:16
  80.8 0.2 shard_map.139.rest_1_
  81.1 0.6 convert_element_type.81
  81.7 0.8 collective-permute-done.31.rest_3_
  82.6 6.5 %shard_map.140 = (bf16[1024,3584]{1,0:T(8,128)(2,1)}, bf16[1024,3584]{1,0:T(8,128)(2,1)}) custom-call(bf16[4,64,128]{2,1,0:T(8,128)(2,1)S(1)} %get-tuple-element.32.picker, bf16[1024,128]{1,0:T(8,128)(2,1)S(1)} %get-tuple-element.46.refs_8_.tokens, bf16[4,2,16,896]{3,2,1,0:T(8,128)(2,1)S(1)} %shard_map.138.rest_0_, ...), custom_call_target="tpu_custom_call" | custom-call | flops 1879048192 | bytes 14680064 | tf_op jit(solution)/shard_map/pallas_call | solution.py:514
  (56 shorter events, 0.8 us)
Async XLA Ops:
  0.6 11.7 %collective-permute-start = (bf16[32,1024]{1,0:T(8,128)(2,1)}, bf16[32,1024]{1,0:T(8,128)(2,1)S(1)}, u32[]{:S(2)}, u32[]{:S(2)}) collective-permute-start(bf16[32,1024]{1,0:T(8,128)(2,1)} %param.9), channel_id=1, source_target_pairs={{0,4},{4,0},{8,12},{12,8},{1,5},{5,1},{9,13},{13,9},{2,6},{6,2},{1... | collective-permute-start | bytes 196616 | tf_op jit(solution)/shard_map/ppermute | solution.py:601
  3.7 9.2 %collective-permute-start.2 = (bf16[32,1024]{1,0:T(8,128)(2,1)}, bf16[32,1024]{1,0:T(8,128)(2,1)S(1)}, u32[]{:S(2)}, u32[]{:S(2)}) collective-permute-start(bf16[32,1024]{1,0:T(8,128)(2,1)} %param.9), channel_id=1, source_target_pairs={{0,12},{4,8},{8,4},{12,0},{1,13},{5,9},{9,5},{13,1},{2,14},{6,10},... | collective-permute-start | bytes 196616 | tf_op jit(solution)/shard_map/ppermute | solution.py:601
  6.2 6.7 %collective-permute-start.1 = (bf16[32,1024]{1,0:T(8,128)(2,1)}, bf16[32,1024]{1,0:T(8,128)(2,1)S(1)}, u32[]{:S(2)}, u32[]{:S(2)}) collective-permute-start(bf16[32,1024]{1,0:T(8,128)(2,1)} %param.9), channel_id=1, source_target_pairs={{0,8},{4,12},{8,0},{12,4},{1,9},{5,13},{9,1},{13,5},{2,10},{6,14},... | collective-permute-start | bytes 196616 | tf_op jit(solution)/shard_map/ppermute | solution.py:601
  6.4 5.9 %copy-start = (bf16[32,1024]{1,0:T(8,128)(2,1)S(1)}, bf16[32,1024]{1,0:T(8,128)(2,1)}, u32[]{:S(2)}) copy-start(bf16[32,1024]{1,0:T(8,128)(2,1)} %param.9) | copy-start | bytes 196612
  14.6 2.3 %collective-permute-start.8 = (bf16[2,64,1792]{2,1,0:T(8,128)(2,1)S(1)}, bf16[2,64,1792]{2,1,0:T(8,128)(2,1)S(1)}, u32[]{:S(2)}, u32[]{:S(2)}) collective-permute-start(bf16[2,64,1792]{2,1,0:T(8,128)(2,1)S(1)} %get-tuple-element.43), channel_id=1, source_target_pairs={{0,1},{1,0},{2,3},{3,2},{4,5},{5,4},{6,7},{7,6},{8,9},{9,8},{10,11... | collective-permute-start | bytes 1376264 | tf_op jit(solution)/shard_map/ppermute | solution.py:16
  16.3 2.3 %collective-permute-start.3 = (bf16[2,64,1792]{2,1,0:T(8,128)(2,1)S(1)}, bf16[2,64,1792]{2,1,0:T(8,128)(2,1)S(1)}, u32[]{:S(2)}, u32[]{:S(2)}) collective-permute-start(bf16[2,64,1792]{2,1,0:T(8,128)(2,1)S(1)} %get-tuple-element.36), channel_id=1, source_target_pairs={{0,1},{1,0},{2,3},{3,2},{4,5},{5,4},{6,7},{7,6},{8,9},{9,8},{10,11... | collective-permute-start | bytes 1376264 | tf_op jit(solution)/shard_map/ppermute | solution.py:16
  17.0 9.2 %collective-permute-start.9 = (bf16[2,32,1792]{2,1,0:T(8,128)(2,1)S(1)}, bf16[2,32,1792]{2,1,0:T(8,128)(2,1)S(1)}, u32[]{:S(2)}, u32[]{:S(2)}) collective-permute-start(bf16[2,32,1792]{2,1,0:T(8,128)(2,1)S(1)} %slice.33), channel_id=1, source_target_pairs={{0,2},{2,0},{1,3},{3,1},{4,6},{6,4},{5,7},{7,5},{8,10},{10,8},{9,1... | collective-permute-start | bytes 688136 | tf_op jit(solution)/shard_map/ppermute | solution.py:16
  18.7 10.9 %collective-permute-start.12 = (bf16[2,32,1792]{2,1,0:T(8,128)(2,1)S(1)}, bf16[2,32,1792]{2,1,0:T(8,128)(2,1)S(1)}, u32[]{:S(2)}, u32[]{:S(2)}) collective-permute-start(bf16[2,32,1792]{2,1,0:T(8,128)(2,1)S(1)} %slice.37), channel_id=1, source_target_pairs={{0,2},{2,0},{1,3},{3,1},{4,6},{6,4},{5,7},{7,5},{8,10},{10,8},{9,1... | collective-permute-start | bytes 688136 | tf_op jit(solution)/shard_map/ppermute | solution.py:16
  26.1 6.0 %collective-permute-start.5 = (bf16[4,2,16,896]{3,2,1,0:T(8,128)(2,1)S(1)}, bf16[4,2,16,896]{3,2,1,0:T(8,128)(2,1)S(1)}, u32[]{:S(2)}, u32[]{:S(2)}) collective-permute-start(bf16[4,2,16,896]{3,2,1,0:T(8,128)(2,1)S(1)} %get-tuple-element.40), channel_id=1, source_target_pairs={{0,1},{1,0},{2,3},{3,2},{4,5},{5,4},{6,7},{7,6},{8,9},{9,8},{10,11... | collective-permute-start | bytes 688136 | tf_op jit(solution)/shard_map/ppermute | solution.py:16
  26.3 6.0 %collective-permute-start.10 = (bf16[32,1792]{1,0:T(8,128)(2,1)S(1)}, bf16[32,1792]{1,0:T(8,128)(2,1)S(1)}, u32[]{:S(2)}, u32[]{:S(2)}) collective-permute-start(bf16[32,1792]{1,0:T(8,128)(2,1)S(1)} %fusion.3.refs_0_), channel_id=1, source_target_pairs={{0,2},{2,0},{1,3},{3,1},{4,6},{6,4},{5,7},{7,5},{8,10},{10,8},{9,1... | collective-permute-start | bytes 344072 | tf_op jit(solution)/shard_map/ppermute | solution.py:16
  29.7 5.1 %collective-permute-start.13 = (bf16[32,1792]{1,0:T(8,128)(2,1)S(1)}, bf16[32,1792]{1,0:T(8,128)(2,1)S(1)}, u32[]{:S(2)}, u32[]{:S(2)}) collective-permute-start(bf16[32,1792]{1,0:T(8,128)(2,1)S(1)} %fusion.1.refs_0_), channel_id=1, source_target_pairs={{0,2},{2,0},{1,3},{3,1},{4,6},{6,4},{5,7},{7,5},{8,10},{10,8},{9,1... | collective-permute-start | bytes 344072 | tf_op jit(solution)/shard_map/ppermute | solution.py:16
  32.0 5.0 %collective-permute-start.4 = (bf16[4,2,16,896]{3,2,1,0:T(8,128)(2,1)S(1)}, bf16[4,2,16,896]{3,2,1,0:T(8,128)(2,1)S(1)}, u32[]{:S(2)}, u32[]{:S(2)}) collective-permute-start(bf16[4,2,16,896]{3,2,1,0:T(8,128)(2,1)S(1)} %get-tuple-element.38), channel_id=1, source_target_pairs={{0,1},{1,0},{2,3},{3,2},{4,5},{5,4},{6,7},{7,6},{8,9},{9,8},{10,11... | collective-permute-start | bytes 688136 | tf_op jit(solution)/shard_map/ppermute | solution.py:16
  32.4 4.8 %collective-permute-start.11 = (bf16[64,1792]{1,0:T(8,128)(2,1)S(1)}, bf16[64,1792]{1,0:T(8,128)(2,1)S(1)}, u32[]{:S(2)}, u32[]{:S(2)}) collective-permute-start(bf16[64,1792]{1,0:T(8,128)(2,1)S(1)} %shard_map.126.refs_0_), channel_id=1, source_target_pairs={{0,1},{1,0},{2,3},{3,2},{4,5},{5,4},{6,7},{7,6},{8,9},{9,8},{10,11... | collective-permute-start | bytes 688136 | tf_op jit(solution)/shard_map/ppermute | solution.py:16
  34.8 2.4 %collective-permute-start.14 = (bf16[64,1792]{1,0:T(8,128)(2,1)S(1)}, bf16[64,1792]{1,0:T(8,128)(2,1)S(1)}, u32[]{:S(2)}, u32[]{:S(2)}) collective-permute-start(bf16[64,1792]{1,0:T(8,128)(2,1)S(1)} %shard_map.127.refs_2_), channel_id=1, source_target_pairs={{0,1},{1,0},{2,3},{3,2},{4,5},{5,4},{6,7},{7,6},{8,9},{9,8},{10,11... | collective-permute-start | bytes 688136 | tf_op jit(solution)/shard_map/ppermute | solution.py:16
  34.9 8.5 %collective-permute-start.7 = (bf16[4,2,16,896]{3,2,1,0:T(8,128)(2,1)S(1)}, bf16[4,2,16,896]{3,2,1,0:T(8,128)(2,1)S(1)}, u32[]{:S(2)}, u32[]{:S(2)}) collective-permute-start(bf16[4,2,16,896]{3,2,1,0:T(8,128)(2,1)S(1)} %shard_map.123.before.refs_2_.mine), channel_id=1, source_target_pairs={{0,2},{2,0},{1,3},{3,1},{4,6},{6,4},{5,7},{7,5},{8,10},{10,8},{9,1... | collective-permute-start | bytes 688136 | tf_op jit(solution)/shard_map/ppermute | solution.py:16
  37.1 12.9 %collective-permute-start.6 = (bf16[4,2,16,896]{3,2,1,0:T(8,128)(2,1)S(1)}, bf16[4,2,16,896]{3,2,1,0:T(8,128)(2,1)S(1)}, u32[]{:S(2)}, u32[]{:S(2)}) collective-permute-start(bf16[4,2,16,896]{3,2,1,0:T(8,128)(2,1)S(1)} %shard_map.124.mine), channel_id=1, source_target_pairs={{0,2},{2,0},{1,3},{3,1},{4,6},{6,4},{5,7},{7,5},{8,10},{10,8},{9,1... | collective-permute-start | bytes 688136 | tf_op jit(solution)/shard_map/ppermute | solution.py:16
  37.2 11.4 %slice-start = ((s8[7340032]{0:T(1024)(128)(4,1)}), s8[4194304]{0:T(1024)(128)(4,1)S(1)}, s32[]{:S(2)}) async-start(s8[7340032]{0:T(1024)(128)(4,1)} %bitcast.31), calls=%async_computation | async-start | bytes 8388608
  37.8 10.8 %slice-start.1 = ((s8[7340032]{0:T(1024)(128)(4,1)}), s8[3145728]{0:T(1024)(128)(4,1)S(1)}, s32[]{:S(2)}) async-start(s8[7340032]{0:T(1024)(128)(4,1)} %bitcast.31), calls=%async_computation.1 | async-start | bytes 6291456
  43.6 4.6 %collective-permute-start.15 = (bf16[4,16,896]{2,1,0:T(8,128)(2,1)S(1)}, bf16[4,16,896]{2,1,0:T(8,128)(2,1)S(1)}, u32[]{:S(2)}, u32[]{:S(2)}) collective-permute-start(bf16[4,16,896]{2,1,0:T(8,128)(2,1)S(1)} %get-tuple-element.44.mine), channel_id=1, source_target_pairs={{0,1},{1,0},{2,3},{3,2},{4,5},{5,4},{6,7},{7,6},{8,9},{9,8},{10,11... | collective-permute-start | bytes 344072 | tf_op jit(solution)/shard_map/ppermute | solution.py:16
  43.7 11.1 %collective-permute-start.22 = (bf16[32,1024]{1,0:T(8,128)(2,1)S(1)}, bf16[32,1024]{1,0:T(8,128)(2,1)S(1)}, u32[]{:S(2)}, u32[]{:S(2)}) collective-permute-start(bf16[32,1024]{1,0:T(8,128)(2,1)S(1)} %get-tuple-element.60), channel_id=1, source_target_pairs={{0,12},{4,8},{8,4},{12,0},{1,13},{5,9},{9,5},{13,1},{2,14},{6,10},... | collective-permute-start | bytes 196616 | tf_op jit(solution)/shard_map/ppermute | solution.py:601
  46.2 10.8 %collective-permute-start.21 = (bf16[32,1024]{1,0:T(8,128)(2,1)S(1)}, bf16[32,1024]{1,0:T(8,128)(2,1)S(1)}, u32[]{:S(2)}, u32[]{:S(2)}) collective-permute-start(bf16[32,1024]{1,0:T(8,128)(2,1)S(1)} %get-tuple-element.61), channel_id=1, source_target_pairs={{0,8},{4,12},{8,0},{12,4},{1,9},{5,13},{9,1},{13,5},{2,10},{6,14},... | collective-permute-start | bytes 196616 | tf_op jit(solution)/shard_map/ppermute | solution.py:601
  46.6 10.4 %collective-permute-start.20 = (bf16[32,1024]{1,0:T(8,128)(2,1)S(1)}, bf16[32,1024]{1,0:T(8,128)(2,1)S(1)}, u32[]{:S(2)}, u32[]{:S(2)}) collective-permute-start(bf16[32,1024]{1,0:T(8,128)(2,1)S(1)} %get-tuple-element.62), channel_id=1, source_target_pairs={{0,4},{4,0},{8,12},{12,8},{1,5},{5,1},{9,13},{13,9},{2,6},{6,2},{1... | collective-permute-start | bytes 196616 | tf_op jit(solution)/shard_map/ppermute | solution.py:601
  50.1 2.6 %collective-permute-start.16 = (bf16[4,16,896]{2,1,0:T(8,128)(2,1)S(1)}, bf16[4,16,896]{2,1,0:T(8,128)(2,1)S(1)}, u32[]{:S(2)}, u32[]{:S(2)}) collective-permute-start(bf16[4,16,896]{2,1,0:T(8,128)(2,1)S(1)} %get-tuple-element.45.mine), channel_id=1, source_target_pairs={{0,1},{1,0},{2,3},{3,2},{4,5},{5,4},{6,7},{7,6},{8,9},{9,8},{10,11... | collective-permute-start | bytes 344072 | tf_op jit(solution)/shard_map/ppermute | solution.py:16
  50.2 6.8 %collective-permute-start.19 = (bf16[32,1024]{1,0:T(8,128)(2,1)S(1)}, bf16[32,1024]{1,0:T(8,128)(2,1)S(1)}, u32[]{:S(2)}, u32[]{:S(2)}) collective-permute-start(bf16[32,1024]{1,0:T(8,128)(2,1)S(1)} %get-tuple-element.64), channel_id=1, source_target_pairs={{0,12},{4,8},{8,4},{12,0},{1,13},{5,9},{9,5},{13,1},{2,14},{6,10},... | collective-permute-start | bytes 196616 | tf_op jit(solution)/shard_map/ppermute | solution.py:601
  52.8 6.7 %collective-permute-start.18 = (bf16[32,1024]{1,0:T(8,128)(2,1)S(1)}, bf16[32,1024]{1,0:T(8,128)(2,1)S(1)}, u32[]{:S(2)}, u32[]{:S(2)}) collective-permute-start(bf16[32,1024]{1,0:T(8,128)(2,1)S(1)} %get-tuple-element.65), channel_id=1, source_target_pairs={{0,8},{4,12},{8,0},{12,4},{1,9},{5,13},{9,1},{13,5},{2,10},{6,14},... | collective-permute-start | bytes 196616 | tf_op jit(solution)/shard_map/ppermute | solution.py:601
  54.8 5.3 %collective-permute-start.17 = (bf16[32,1024]{1,0:T(8,128)(2,1)S(1)}, bf16[32,1024]{1,0:T(8,128)(2,1)S(1)}, u32[]{:S(2)}, u32[]{:S(2)}) collective-permute-start(bf16[32,1024]{1,0:T(8,128)(2,1)S(1)} %get-tuple-element.66), channel_id=1, source_target_pairs={{0,4},{4,0},{8,12},{12,8},{1,5},{5,1},{9,13},{13,9},{2,6},{6,2},{1... | collective-permute-start | bytes 196616 | tf_op jit(solution)/shard_map/ppermute | solution.py:601
  60.3 9.8 %collective-permute-start.27 = (bf16[32,1024]{1,0:T(8,128)(2,1)S(1)}, bf16[32,1024]{1,0:T(8,128)(2,1)S(1)}, u32[]{:S(2)}, u32[]{:S(2)}) collective-permute-start(bf16[32,1024]{1,0:T(8,128)(2,1)S(1)} %get-tuple-element.48.before), channel_id=1, source_target_pairs={{0,12},{4,8},{8,4},{12,0},{1,13},{5,9},{9,5},{13,1},{2,14},{6,10},... | collective-permute-start | bytes 196616 | tf_op jit(solution)/shard_map/ppermute | solution.py:601
  62.7 7.3 %collective-permute-start.26 = (bf16[32,1024]{1,0:T(8,128)(2,1)S(1)}, bf16[32,1024]{1,0:T(8,128)(2,1)S(1)}, u32[]{:S(2)}, u32[]{:S(2)}) collective-permute-start(bf16[32,1024]{1,0:T(8,128)(2,1)S(1)} %get-tuple-element.48.before), channel_id=1, source_target_pairs={{0,8},{4,12},{8,0},{12,4},{1,9},{5,13},{9,1},{13,5},{2,10},{6,14},... | collective-permute-start | bytes 196616 | tf_op jit(solution)/shard_map/ppermute | solution.py:601
  62.7 4.7 %collective-permute-start.23 = (bf16[32,1024]{1,0:T(8,128)(2,1)S(1)}, bf16[32,1024]{1,0:T(8,128)(2,1)S(1)}, u32[]{:S(2)}, u32[]{:S(2)}) collective-permute-start(bf16[32,1024]{1,0:T(8,128)(2,1)S(1)} %get-tuple-element.48.before), channel_id=1, source_target_pairs={{0,4},{4,0},{8,12},{12,8},{1,5},{5,1},{9,13},{13,9},{2,6},{6,2},{1... | collective-permute-start | bytes 196616 | tf_op jit(solution)/shard_map/ppermute | solution.py:601
  69.9 3.1 %collective-permute-start.24 = (bf16[4,16,896]{2,1,0:T(8,128)(2,1)S(1)}, bf16[4,16,896]{2,1,0:T(8,128)(2,1)S(1)}, u32[]{:S(2)}, u32[]{:S(2)}) collective-permute-start(bf16[4,16,896]{2,1,0:T(8,128)(2,1)S(1)} %get-tuple-element.50), channel_id=1, source_target_pairs={{0,1},{1,0},{2,3},{3,2},{4,5},{5,4},{6,7},{7,6},{8,9},{9,8},{10,11... | collective-permute-start | bytes 344072 | tf_op jit(solution)/shard_map/ppermute | solution.py:16
  72.5 2.6 %collective-permute-start.28 = (bf16[4,16,896]{2,1,0:T(8,128)(2,1)S(1)}, bf16[4,16,896]{2,1,0:T(8,128)(2,1)S(1)}, u32[]{:S(2)}, u32[]{:S(2)}) collective-permute-start(bf16[4,16,896]{2,1,0:T(8,128)(2,1)S(1)} %get-tuple-element.54), channel_id=1, source_target_pairs={{0,1},{1,0},{2,3},{3,2},{4,5},{5,4},{6,7},{7,6},{8,9},{9,8},{10,11... | collective-permute-start | bytes 344072 | tf_op jit(solution)/shard_map/ppermute | solution.py:16
  73.0 6.4 %collective-permute-start.25 = (bf16[4,16,896]{2,1,0:T(8,128)(2,1)S(1)}, bf16[4,16,896]{2,1,0:T(8,128)(2,1)S(1)}, u32[]{:S(2)}, u32[]{:S(2)}) collective-permute-start(bf16[4,16,896]{2,1,0:T(8,128)(2,1)S(1)} %add_convert_fusion.3.mine), channel_id=1, source_target_pairs={{0,2},{2,0},{1,3},{3,1},{4,6},{6,4},{5,7},{7,5},{8,10},{10,8},{9,1... | collective-permute-start | bytes 344072 | tf_op jit(solution)/shard_map/ppermute | solution.py:16
  75.1 5.8 %collective-permute-start.29 = (bf16[4,16,896]{2,1,0:T(8,128)(2,1)S(1)}, bf16[4,16,896]{2,1,0:T(8,128)(2,1)S(1)}, u32[]{:S(2)}, u32[]{:S(2)}) collective-permute-start(bf16[4,16,896]{2,1,0:T(8,128)(2,1)S(1)} %add_convert_fusion.2.before.mine), channel_id=1, source_target_pairs={{0,2},{2,0},{1,3},{3,1},{4,6},{6,4},{5,7},{7,5},{8,10},{10,8},{9,1... | collective-permute-start | bytes 344072 | tf_op jit(solution)/shard_map/ppermute | solution.py:16
  79.6 2.1 %collective-permute-start.30 = (bf16[4,2,16,896]{3,2,1,0:T(8,128)(2,1)S(1)}, bf16[4,2,16,896]{3,2,1,0:T(8,128)(2,1)S(1)}, u32[]{:S(2)}, u32[]{:S(2)}) collective-permute-start(bf16[4,2,16,896]{3,2,1,0:T(8,128)(2,1)S(1)} %shard_map.138.rest_0_), channel_id=1, source_target_pairs={{0,1},{1,0},{2,3},{3,2},{4,5},{5,4},{6,7},{7,6},{8,9},{9,8},{10,11... | collective-permute-start | bytes 688136 | tf_op jit(solution)/shard_map/ppermute | solution.py:16
  81.0 1.6 %collective-permute-start.31 = (bf16[4,2,16,896]{3,2,1,0:T(8,128)(2,1)S(1)}, bf16[4,2,16,896]{3,2,1,0:T(8,128)(2,1)S(1)}, u32[]{:S(2)}, u32[]{:S(2)}) collective-permute-start(bf16[4,2,16,896]{3,2,1,0:T(8,128)(2,1)S(1)} %shard_map.139.rest_1_), channel_id=1, source_target_pairs={{0,1},{1,0},{2,3},{3,2},{4,5},{5,4},{6,7},{7,6},{8,9},{9,8},{10,11... | collective-permute-start | bytes 688136 | tf_op jit(solution)/shard_map/ppermute | solution.py:16

commit v12 on v11

--- a/solution.py
+++ b/solution.py
@@ -213,27 +213,39 @@
 def expert_kernel(cuts, picker, tokens, gate, up, before, *rest):
     outs, held, sems = rest[:-2], rest[-2], rest[-1]
     count, slots = picker.shape[:2]
-    pieces = sems.shape[2]
+    depth, _, pieces = sems.shape
     rows_each = gate.shape[0] // pieces
-    copies = {}
-    for e in range(count):
-        for which, weight in enumerate((gate, up)):
-            for p in range(pieces):
-                part = pl.ds(p * rows_each, rows_each)
-                columns = pl.ds(e * H, H)
-                copies[e, which, p] = pltpu.make_async_copy(
-                    weight.at[part, columns], held.at[e, which, part], sems.at[e, which, p]
+
+    def copies(e, which):
+        weight = (gate, up)[which]
+        found = []
+        for p in range(pieces):
+            part = pl.ds(p * rows_each, rows_each)
+            found.append(
+                pltpu.make_async_copy(
+                    weight.at[part, pl.ds(e * H, H)],
+                    held.at[e % depth, which, part],
+                    sems.at[e % depth, which, p],
                 )
-                copies[e, which, p].start()
+            )
+        return found
+
+    for e in range(min(depth, count)):
+        for which in range(2):
+            for copy in copies(e, which):
+                copy.start()
     for e in range(count):
         rows = dot(picker[e], tokens[...]).astype(BF)
         for which in range(2):
-            for p in range(pieces):
-                copies[e, which, p].wait()
-            product = dot(rows, held[e, which]).astype(BF)
+            for copy in copies(e, which):
+                copy.wait()
+            product = dot(rows, held[e % depth, which]).astype(BF)
             for i, (low, high) in enumerate(cuts):
                 outs[2 * i][e, which] = product[low:high]
                 outs[2 * i + 1][e, which] = product[slots // 2 + low : slots // 2 + high]
+            if e + depth < count:
+                for copy in copies(e + depth, which):
+                    copy.start()
 
 
 def expert_pre(picker, tokens, gate, up, before, cuts):
@@ -248,10 +260,10 @@
         out_specs=tuple(whole() for _ in outs),
         out_shape=tuple(outs),
         scratch_shapes=[
-            pltpu.VMEM((count, 2, width, H), BF),
-            pltpu.SemaphoreType.DMA((count, 2, 4)),
+            pltpu.VMEM((min(count, 2), 2, width, H), BF),
+            pltpu.SemaphoreType.DMA((min(count, 2), 2, 4)),
         ],
-        compiler_params=pltpu.CompilerParams(vmem_limit_bytes=24 * 1024 * 1024),
+        compiler_params=pltpu.CompilerParams(vmem_limit_bytes=12 * 1024 * 1024),
         cost_estimate=pl.CostEstimate(
             flops=count * 4 * slots * width * H,
             bytes_accessed=count * 4 * width * H,
@@ -401,20 +413,20 @@
     )(*dense, tokens, before)
 
 
-def hidden_grad_kernel(cut, picker, residual, down, before, keep, send):
+def hidden_grad_kernel(first, picker, residual, down, before, keep, send):
     rows = keep.shape[1]
-    for e in range(keep.shape[0]):
-        picked = dot(slot_rows(picker[e], *cut), residual[...]).astype(BF)
+    for i in range(keep.shape[0]):
+        e = first + i
+        picked = dot(picker[e], residual[...]).astype(BF)
         product = dot(down[e * H : (e + 1) * H, :], picked, 1, 1).T.astype(BF)
-        keep[e] = product[:rows]
-        send[e] = product[rows:]
-
-
-def hidden_grad_parts(picker, residual, down, before, cut):
-    count = picker.shape[0]
-    part = jax.ShapeDtypeStruct((count, cut[1] - cut[0], H), BF)
-    return pl.pallas_call(
-        functools.partial(hidden_grad_kernel, cut),
+        keep[i] = product[:rows]
+        send[i] = product[rows:]
+
+
+def hidden_grad_parts(picker, residual, down, before, first, count):
+    part = jax.ShapeDtypeStruct((count, picker.shape[1] // 2, H), BF)
+    return pl.pallas_call(
+        functools.partial(hidden_grad_kernel, first),
         in_specs=[whole(), whole(), whole(), anywhere()],
         out_specs=(whole(), whole()),
         out_shape=(part, part),
@@ -422,11 +434,14 @@
     )(picker, residual, down, before)
 
 
-def hidden_grad_act_kernel(mode, low, mine, other, pre, weight, before, out):
+def hidden_grad_act_kernel(mode, first, mine, other, weight, before, *rest):
+    pres, out = rest[:-1], rest[-1]
     count, rows = mine.shape[:2]
     for i in range(count):
-        total = dp_total(mode, mine[i], other[i]) * weight[i, low : low + rows]
-        pre_gate, pre_up = pre[i, 0], pre[i, 1]
+        e = first + i
+        total = dp_total(mode, mine[i], other[i]) * weight[e, :rows]
+        pre_gate = jnp.concatenate([pre[e, 0] for pre in pres], axis=0)
+        pre_up = jnp.concatenate([pre[e, 1] for pre in pres], axis=0)
         sig = jax.nn.sigmoid(pre_gate)
         gate_grad = total * pre_up * sig * (1.0 + pre_gate * (1.0 - sig))
         up_grad = total * pre_gate * sig
@@ -434,15 +449,15 @@
         out[i, 1] = up_grad.astype(BF)
 
 
-def hidden_grad_act(mine, other, mode, pre, weight, before, low):
+def hidden_grad_act(mine, other, mode, pres, weight, before, first):
     count, rows, width = mine.shape
     return pl.pallas_call(
-        functools.partial(hidden_grad_act_kernel, mode, low),
-        in_specs=[whole(), whole(), whole(), whole(), anywhere()],
+        functools.partial(hidden_grad_act_kernel, mode, first),
+        in_specs=[whole(), whole(), whole(), anywhere()] + [whole()] * len(pres),
         out_specs=whole(),
         out_shape=jax.ShapeDtypeStruct((count, 2, rows, width), BF),
         compiler_params=pltpu.CompilerParams(vmem_limit_bytes=8 * 1024 * 1024),
-    )(mine, other, pre, weight, before)
+    )(mine, other, weight, before, *pres)
 
 
 def down_grad_kernel(hidden, residual, before, out, done, held, sems):
@@ -483,15 +498,16 @@
     )(hidden, residual, before)
 
 
-def input_grad_kernel(picker, tokens, *rest):
-    parts, outs, held, sems = rest[:-4], rest[-4:-2], rest[-2], rest[-1]
+def input_grad_kernel(group, picker, tokens, *rest):
+    outs, held, sems = rest[-4:-2], rest[-2], rest[-1]
     count = picker.shape[0]
     splits = sems.shape[2]
     rows = tokens.shape[0] // splits
     copies = []
     for i in range(count):
         for which in range(2):
-            grad = jnp.concatenate([value[i, which] for value in parts], axis=0)
+            mine, theirs = rest[i // group * 2], rest[i // group * 2 + 1]
+            grad = jnp.concatenate([mine[i % group, which], theirs[i % group, which]], axis=0)
             dense = dot(picker[i], grad, 0, 0).astype(BF)
             for r in range(splits):
                 part = pl.ds(r * rows, rows)
@@ -512,8 +528,8 @@
     width = tokens.shape[0]
     out = jax.ShapeDtypeStruct((width, count * H), BF)
     return pl.pallas_call(
-        input_grad_kernel,
-        in_specs=[whole()] * (2 + len(parts)),
+        functools.partial(input_grad_kernel, count // len(parts)),
+        in_specs=[whole()] * (2 + 2 * len(parts)),
         out_specs=(in_hbm(), in_hbm()),
         out_shape=(out, out),
         scratch_shapes=[
@@ -526,7 +542,7 @@
             bytes_accessed=count * 4 * width * H,
             transcendentals=0,
         ),
-    )(picker, tokens, *parts)
+    )(picker, tokens, *[value for pair in parts for value in pair])
 
 
 def add(a, b):
@@ -666,30 +682,33 @@
     target = to_owners(product, 0, ranks, 0)
 
     pre, dense, student = [], [], []
+    wait = [target[1], target[-1]]
     for (mine, other, mode), cut, rows in zip(parts, cuts, token_cuts):
-        total, part = hidden_act(mine, other, mode, slot_weight, [product], cut[0])
+        total, part = hidden_act(mine, other, mode, slot_weight, wait, cut[0])
         pre.append(total)
         dense.append(spread(picker, part, shift(part, "pipe", pipes, 1), cut, rows))
+        wait = dense[-1:]
         product = jnp.dot(dense[-1], expert_down, preferred_element_type=F32).astype(BF)
         count = (rows[1] - rows[0]) // block
         student = to_owners(product, rows[0] // block, count, rows[0]) + student
     dense_flipped, base_flipped = flip(dense[::-1], base, product)
     student_sum, residual = residual_of(student, target, (base_flipped,))
 
-    residuals = gather_tokens(residual)
+    _, residual = gather_tokens(residual)
+    group = 2 if experts % 2 == 0 else 1
+    firsts = range(0, experts, group)
     sums, last = [], residual
-    for rows, cut in zip(residuals[-len(cuts) :], cuts[::-1]):
-        keep, send = hidden_grad_parts(picker, rows, expert_down, last, cut)
+    for first in firsts:
+        keep, send = hidden_grad_parts(picker, residual, expert_down, last, first, group)
         last = keep
         sums.append(add(keep, shift(send, "pipe", pipes, 1)))
     exchanged = [exchange_dp(value, dps, near_first) for value in sums]
-    grad_down, done = down_grad(dense_flipped, residuals[-1], sums[-1])
-    mine, theirs = [], []
-    for (own, other, mode), total, cut in zip(exchanged, pre[::-1], cuts[::-1]):
-        part = hidden_grad_act(own, other, mode, total, slot_weight, done, cut[0])
-        mine.append(part)
-        theirs.append(shift(part, "pipe", pipes, 1))
-    grads = input_grads(picker, base_flipped, mine + theirs)
+    grad_down, done = down_grad(dense_flipped, residual, sums[-1])
+    grads = []
+    for first, (own, other, mode) in zip(firsts, exchanged):
+        part = hidden_grad_act(own, other, mode, pre[::-1], slot_weight, done, first)
+        grads.append((part, shift(part, "pipe", pipes, 1)))
+    grads = input_grads(picker, base_flipped, grads)
     return (student_sum.astype(BF), grads[0], grads[1], grad_down)
 
 

time: 89.4 us -> 93.7 us (1.048)
  waiting for transfers between devices: 14 us -> 19.1 us
  matrix products: 7.29 us -> 10.4 us
  starting transfers between devices: 32.4 us -> 30.1 us
  Pallas kernels: 32.7 us -> 31.2 us
    dot_general x2, matrix products: 2.78 us -> 9.24 us  [body(): jnp.dot(dense[-1], expert_down, preferred_element_type=F32).astype(BF)]
    dot_general x1, matrix products: 4.51 us -> 1.12 us  [body(): jnp.dot(hidden, teacher_down, preferred_element_type=F32).astype(BF)]
    ppermute x12, waiting for transfers between devices: 6.28 us -> 9.38 us  [to_partner(): return lax.ppermute(value, 'expert', [(i, i ^ s) for i in range(ranks)])]
    pallas_call x5, Pallas kernels: 11.8 us -> 9.68 us  [the longest x1 6.5 us: input_grads(): pl.pallas_call(functools.partial(input_grad_kernel, count // len(parts)),...]
    ppermute x20, waiting for transfers between devices: 7.74 us -> 9.74 us  [shift(): lax.ppermute(value, axis, [(i, (i + by) % count) for i in range(count)])]
    ppermute x20, starting transfers between devices: 13.4 us -> 11.9 us  [shift(): lax.ppermute(value, axis, [(i, (i + by) % count) for i in range(count)])]
  transfers between devices with their start and end apart: 32 -> 32, of which waited for: 10 -> 14; matrix products, arithmetic and copies ran while one was open for 10% -> 13% of each run, Pallas kernels for 27% -> 23%
where the time goes in v12:
time: 93.7 us; the launch traced here: 93.5 us
  Pallas kernels  31.2 us (33%)
  starting transfers between devices  30.1 us (32%)
  waiting for transfers between devices  19.1 us (20%)
  matrix products  10.4 us (11%)
  between operations  1.32 us (1%)
  other arithmetic  1.23 us (1%)
    ppermute x12, starting transfers between devices, to_partner(): return lax.ppermute(value, 'expert', [(i, i ^ s) for i in range(ranks)])  18.2 us
    ppermute x20, starting transfers between devices, shift(): lax.ppermute(value, axis, [(i, (i + by) % count) for i in range(count)])  11.9 us
    ppermute x20, waiting for transfers between devices, shift(): lax.ppermute(value, axis, [(i, (i + by) % count) for i in range(count)])  9.74 us
    ppermute x12, waiting for transfers between devices, to_partner(): return lax.ppermute(value, 'expert', [(i, i ^ s) for i in range(ranks)])  9.38 us
    dot_general x2, matrix products, body(): jnp.dot(dense[-1], expert_down, preferred_element_type=F32).astype(BF)  9.24 us
    pallas_call x1, Pallas kernels, expert_pre(): pl.pallas_call(functools.partial(expert_kernel, cuts), in_specs=[whole(),...  6.57 us
    pallas_call x1, Pallas kernels, input_grads(): pl.pallas_call(functools.partial(input_grad_kernel, count // len(parts)),...  6.5 us
    pallas_call x1, Pallas kernels, prepare(): pl.pallas_call(functools.partial(prepare_kernel, near_first, ranks, capac...  5.89 us
  transfers between devices with their start and end apart: 32, of which 14 were waited for; matrix products, arithmetic and copies ran while one was open for 13% of the time, Pallas kernels for 23%

profile of v12, /device:TPU:0, one launch (start us, length us, event | category | flops | bytes accessed | tf_op | source)
XLA Modules:
  0.0 93.5 jit_solution(3335218634445669556)
XLA Ops:
  0.6 3.1 %collective-permute-start = (bf16[32,1024]{1,0:T(8,128)(2,1)}, bf16[32,1024]{1,0:T(8,128)(2,1)S(1)}, u32[]{:S(2)}, u32[]{:S(2)}) collective-permute-start(bf16[32,1024]{1,0:T(8,128)(2,1)} %param.9), channel_id=1, source_target_pairs={{0,4},{4,0},{8,12},{12,8},{1,5},{5,1},{9,13},{13,9},{2,6},{6,2},{1... | collective-permute-start | bytes 196616 | tf_op jit(solution)/shard_map/ppermute | solution.py:617
  3.7 2.5 %collective-permute-start.2 = (bf16[32,1024]{1,0:T(8,128)(2,1)}, bf16[32,1024]{1,0:T(8,128)(2,1)S(1)}, u32[]{:S(2)}, u32[]{:S(2)}) collective-permute-start(bf16[32,1024]{1,0:T(8,128)(2,1)} %param.9), channel_id=1, source_target_pairs={{0,12},{4,8},{8,4},{12,0},{1,13},{5,9},{9,5},{13,1},{2,14},{6,10},... | collective-permute-start | bytes 196616 | tf_op jit(solution)/shard_map/ppermute | solution.py:617
  6.2 0.1 collective-permute-start.1
  6.3 0.1 pad_add_fusion.place
  6.4 5.9 %shard_map.120 = (bf16[4,64,128]{2,1,0:T(8,128)(2,1)S(1)}, f32[4,64,1]{2,1,0:T(8,128)S(1)}, bf16[1024,3584]{1,0:T(8,128)(2,1)S(1)}, bf16[1024,3584]{1,0:T(8,128)(2,1)S(1)}) custom-call(s32[3]{0:T(128)S(1)} %pad_add_fusion.place, s32[4,128]{1,0:T(4,128)} %bitcast.35, f32[4,128]{1,0:T(4,128)} %bitcast.36, bf16[1024,3584]{1,0:T(8,128)(2,1)} %gate.2, ...), custom_call_target="tpu_custom_call" | custom-call | bytes 14680064 | tf_op jit(solution)/shard_map/pallas_call | solution.py:131
  12.4 0.5 collective-permute-done.1
  12.9 1.7 %shard_map.125 = (bf16[2,64,1792]{2,1,0:T(8,128)(2,1)S(1)}, bf16[2,64,1792]{2,1,0:T(8,128)(2,1)S(1)}) custom-call(s32[3]{0:T(128)S(1)} %pad_add_fusion.place, bf16[128,1024]{1,0:T(8,128)(2,1)S(1)} %constant_dynamic-update-slice_fusion.4.tokens.refs_2_, bf16[1024,3584]{1,0:T(8,128)(2,1)S(1)} %get-tuple-element.33.gate, ...), custom_call_target="tpu_custom_call" | custom-call | flops 939524096 | bytes 7340032 | tf_op jit(solution)/shard_map/pallas_call | solution.py:201
  14.7 1.7 %shard_map.121 = (bf16[2,64,1792]{2,1,0:T(8,128)(2,1)S(1)}, bf16[2,64,1792]{2,1,0:T(8,128)(2,1)S(1)}) custom-call(s32[3]{0:T(128)S(1)} %pad_add_fusion.place, bf16[128,1024]{1,0:T(8,128)(2,1)S(1)} %constant_dynamic-update-slice_fusion.4.tokens.refs_2_, bf16[1024,3584]{1,0:T(8,128)(2,1)S(1)} %get-tuple-element.33.gate, ...), custom_call_target="tpu_custom_call" | custom-call | flops 939524096 | bytes 7340032 | tf_op jit(solution)/shard_map/pallas_call | solution.py:201
  16.3 0.6 collective-permute-start.3
  16.9 0.1 add_convert_fusion
  17.0 1.6 %collective-permute-start.9 = (bf16[2,32,1792]{2,1,0:T(8,128)(2,1)S(1)}, bf16[2,32,1792]{2,1,0:T(8,128)(2,1)S(1)}, u32[]{:S(2)}, u32[]{:S(2)}) collective-permute-start(bf16[2,32,1792]{2,1,0:T(8,128)(2,1)S(1)} %slice.33), channel_id=1, source_target_pairs={{0,2},{2,0},{1,3},{3,1},{4,6},{6,4},{5,7},{7,5},{8,10},{10,8},{9,1... | collective-permute-start | bytes 688136 | tf_op jit(solution)/shard_map/ppermute | solution.py:16
  18.6 0.1 add_convert_fusion.1.before
  18.7 1.3 %collective-permute-start.12 = (bf16[2,32,1792]{2,1,0:T(8,128)(2,1)S(1)}, bf16[2,32,1792]{2,1,0:T(8,128)(2,1)S(1)}, u32[]{:S(2)}, u32[]{:S(2)}) collective-permute-start(bf16[2,32,1792]{2,1,0:T(8,128)(2,1)S(1)} %slice.37), channel_id=1, source_target_pairs={{0,2},{2,0},{1,3},{3,1},{4,6},{6,4},{5,7},{7,5},{8,10},{10,8},{9,1... | collective-permute-start | bytes 688136 | tf_op jit(solution)/shard_map/ppermute | solution.py:16
  20.1 6.6 %shard_map.122 = (bf16[4,2,16,896]{3,2,1,0:T(8,128)(2,1)S(1)}, bf16[4,2,16,896]{3,2,1,0:T(8,128)(2,1)S(1)}, bf16[4,2,16,896]{3,2,1,0:T(8,128)(2,1)S(1)}, bf16[4,2,16,896]{3,2,1,0:T(8,128)(2,1)S(1)}) custom-call(bf16[4,64,128]{2,1,0:T(8,128)(2,1)S(1)} %get-tuple-element.32.picker, bf16[128,1024]{1,0:T(8,128)(2,1)S(1)} %constant_dynamic-update-slice_fusion.4.tokens.refs_2_, ...), custom_call_target="tpu_custom_call" | custom-call | flops 939524096 | bytes 14680064 | tf_op jit(solution)/shard_map/pallas_call | solution.py:257
  26.6 0.1 collective-permute-start.5
  26.8 0.1 fusion.3.refs_0_
  26.9 0.8 collective-permute-start.10
  27.7 1.9 %collective-permute-done.12 = bf16[2,32,1792]{2,1,0:T(8,128)(2,1)S(1)} collective-permute-done((bf16[2,32,1792]{2,1,0:T(8,128)(2,1)S(1)}, bf16[2,32,1792]{2,1,0:T(8,128)(2,1)S(1)}, u32[]{:S(2)}, u32[]{:S(2)}) %collective-permute-start.12) | collective-permute-done | bytes 229408 | tf_op jit(solution)/shard_map/ppermute | solution.py:16
  29.6 0.1 fusion.1.refs_0_
  29.7 1.8 %collective-permute-start.13 = (bf16[32,1792]{1,0:T(8,128)(2,1)S(1)}, bf16[32,1792]{1,0:T(8,128)(2,1)S(1)}, u32[]{:S(2)}, u32[]{:S(2)}) collective-permute-start(bf16[32,1792]{1,0:T(8,128)(2,1)S(1)} %fusion.1.refs_0_), channel_id=1, source_target_pairs={{0,2},{2,0},{1,3},{3,1},{4,6},{6,4},{5,7},{7,5},{8,10},{10,8},{9,1... | collective-permute-start | bytes 344072 | tf_op jit(solution)/shard_map/ppermute | solution.py:16
  31.5 1.4 %collective-permute-done.10.refs_1_ = bf16[32,1792]{1,0:T(8,128)(2,1)S(1)} collective-permute-done((bf16[32,1792]{1,0:T(8,128)(2,1)S(1)}, bf16[32,1792]{1,0:T(8,128)(2,1)S(1)}, u32[]{:S(2)}, u32[]{:S(2)}) %collective-permute-start.10) | collective-permute-done | bytes 114720 | tf_op jit(solution)/shard_map/ppermute | solution.py:16
  33.0 1.9 %collective-permute-done.13.refs_1_ = bf16[32,1792]{1,0:T(8,128)(2,1)S(1)} collective-permute-done((bf16[32,1792]{1,0:T(8,128)(2,1)S(1)}, bf16[32,1792]{1,0:T(8,128)(2,1)S(1)}, u32[]{:S(2)}, u32[]{:S(2)}) %collective-permute-start.13) | collective-permute-done | bytes 114720 | tf_op jit(solution)/shard_map/ppermute | solution.py:16
  35.0 1.4 %collective-permute-start.7 = (bf16[4,2,16,896]{3,2,1,0:T(8,128)(2,1)S(1)}, bf16[4,2,16,896]{3,2,1,0:T(8,128)(2,1)S(1)}, u32[]{:S(2)}, u32[]{:S(2)}) collective-permute-start(bf16[4,2,16,896]{3,2,1,0:T(8,128)(2,1)S(1)} %shard_map.123.before.refs_2_.mine), channel_id=1, source_target_pairs={{0,2},{2,0},{1,3},{3,1},{4,6},{6,4},{5,7},{7,5},{8,10},{10,8},{9,1... | collective-permute-start | bytes 688136 | tf_op jit(solution)/shard_map/ppermute | solution.py:16
  36.5 0.8 collective-permute-start.6
  37.3 0.6 shard_map.128
  37.9 1.1 %convolution_convert_fusion = bf16[128,1024]{1,0:T(8,128)(2,1)S(1)} fusion(bf16[128,3584]{1,0:T(8,128)(2,1)S(1)} %shard_map.128, bf16[3584,1024]{1,0:T(8,128)(2,1)S(1)} %bitcast.34), kind=kOutput, calls=%fused_computation | convolution fusion | flops 939655168 | bytes 8519680 | tf_op jit(solution)/shard_map/dot_general | solution.py:681
  39.1 2.5 %collective-permute-start.16 = (bf16[32,1024]{1,0:T(8,128)(2,1)S(1)}, bf16[32,1024]{1,0:T(8,128)(2,1)S(1)}, u32[]{:S(2)}, u32[]{:S(2)}) collective-permute-start(bf16[32,1024]{1,0:T(8,128)(2,1)S(1)} %get-tuple-element.62), channel_id=1, source_target_pairs={{0,12},{4,8},{8,4},{12,0},{1,13},{5,9},{9,5},{13,1},{2,14},{6,10},... | collective-permute-start | bytes 196616 | tf_op jit(solution)/shard_map/ppermute | solution.py:617
  41.6 0.5 collective-permute-start.15
  42.0 1.5 %collective-permute-done.7.other = bf16[4,2,16,896]{3,2,1,0:T(8,128)(2,1)S(1)} collective-permute-done((bf16[4,2,16,896]{3,2,1,0:T(8,128)(2,1)S(1)}, bf16[4,2,16,896]{3,2,1,0:T(8,128)(2,1)S(1)}, u32[]{:S(2)}, u32[]{:S(2)}) %collective-permute-start.7) | collective-permute-done | bytes 229408 | tf_op jit(solution)/shard_map/ppermute | solution.py:16
  43.5 2.1 %collective-permute-done.16.rest_1_.refs_7_ = bf16[32,1024]{1,0:T(8,128)(2,1)S(1)} collective-permute-done((bf16[32,1024]{1,0:T(8,128)(2,1)S(1)}, bf16[32,1024]{1,0:T(8,128)(2,1)S(1)}, u32[]{:S(2)}, u32[]{:S(2)}) %collective-permute-start.16) | collective-permute-done | bytes 65568 | tf_op jit(solution)/shard_map/ppermute | solution.py:617
  45.6 0.7 collective-permute-done.15.rest_0_.refs_5_
  46.3 0.1 shard_map.129
  46.5 0.6 collective-permute-start.22
  47.1 0.7 collective-permute-done.17.theirs
  47.8 0.4 shard_map.130.rest_0_.refs_1_
  48.2 0.1 shard_map.131
  48.3 0.2 collective-permute-start.18
  48.5 4.6 %convolution_convert_fusion.1 = bf16[64,1024]{1,0:T(8,128)(2,1)S(1)} fusion(bf16[64,3584]{1,0:T(8,128)(2,1)S(1)} %shard_map.130.rest_0_.refs_1_, bf16[3584,1024]{1,0:T(8,128)(2,1)} %down.3), kind=kOutput, calls=%fused_computation.1 | convolution fusion | flops 469827584 | bytes 7929856 | tf_op jit(solution)/shard_map/dot_general | solution.py:691
  53.2 2.2 %collective-permute-start.21 = (bf16[32,1024]{1,0:T(8,128)(2,1)S(1)}, bf16[32,1024]{1,0:T(8,128)(2,1)S(1)}, u32[]{:S(2)}, u32[]{:S(2)}) collective-permute-start(bf16[32,1024]{1,0:T(8,128)(2,1)S(1)} %get-tuple-element.64), channel_id=1, source_target_pairs={{0,12},{4,8},{8,4},{12,0},{1,13},{5,9},{9,5},{13,1},{2,14},{6,10},... | collective-permute-start | bytes 196616 | tf_op jit(solution)/shard_map/ppermute | solution.py:617
  55.3 0.5 collective-permute-start.20
  55.8 0.4 shard_map.132.refs_0_
  56.3 4.6 %convolution_convert_fusion.2.refs_3_ = bf16[64,1024]{1,0:T(8,128)(2,1)S(1)} fusion(bf16[64,3584]{1,0:T(8,128)(2,1)S(1)} %shard_map.132.refs_0_, bf16[3584,1024]{1,0:T(8,128)(2,1)} %down.3), kind=kOutput, calls=%fused_computation.2 | convolution fusion | flops 469827584 | bytes 7929856 | tf_op jit(solution)/shard_map/dot_general | solution.py:691
  60.9 1.9 %collective-permute-start.19 = (bf16[32,1024]{1,0:T(8,128)(2,1)S(1)}, bf16[32,1024]{1,0:T(8,128)(2,1)S(1)}, u32[]{:S(2)}, u32[]{:S(2)}) collective-permute-start(bf16[32,1024]{1,0:T(8,128)(2,1)S(1)} %get-tuple-element.66), channel_id=1, source_target_pairs={{0,4},{4,0},{8,12},{12,8},{1,5},{5,1},{9,13},{13,9},{2,6},{6,2},{1... | collective-permute-start | bytes 196616 | tf_op jit(solution)/shard_map/ppermute | solution.py:617
  62.8 0.4 shard_map.133
  63.2 2.1 %collective-permute-done.19.refs_1_ = bf16[32,1024]{1,0:T(8,128)(2,1)S(1)} collective-permute-done((bf16[32,1024]{1,0:T(8,128)(2,1)S(1)}, bf16[32,1024]{1,0:T(8,128)(2,1)S(1)}, u32[]{:S(2)}, u32[]{:S(2)}) %collective-permute-start.19) | collective-permute-done | bytes 65568 | tf_op jit(solution)/shard_map/ppermute | solution.py:617
  65.3 0.1 shard_map.134
  65.3 2.4 %collective-permute-start.25 = (bf16[32,1024]{1,0:T(8,128)(2,1)S(1)}, bf16[32,1024]{1,0:T(8,128)(2,1)S(1)}, u32[]{:S(2)}, u32[]{:S(2)}) collective-permute-start(bf16[32,1024]{1,0:T(8,128)(2,1)S(1)} %get-tuple-element.48), channel_id=1, source_target_pairs={{0,12},{4,8},{8,4},{12,0},{1,13},{5,9},{9,5},{13,1},{2,14},{6,10},... | collective-permute-start | bytes 196616 | tf_op jit(solution)/shard_map/ppermute | solution.py:617
  67.7 0.9 %collective-permute-start.24 = (bf16[32,1024]{1,0:T(8,128)(2,1)S(1)}, bf16[32,1024]{1,0:T(8,128)(2,1)S(1)}, u32[]{:S(2)}, u32[]{:S(2)}) collective-permute-start(bf16[32,1024]{1,0:T(8,128)(2,1)S(1)} %get-tuple-element.48), channel_id=1, source_target_pairs={{0,8},{4,12},{8,0},{12,4},{1,9},{5,13},{9,1},{13,5},{2,10},{6,14},... | collective-permute-start | bytes 196616 | tf_op jit(solution)/shard_map/ppermute | solution.py:617
  68.7 1.1 %collective-permute-start.23 = (bf16[32,1024]{1,0:T(8,128)(2,1)S(1)}, bf16[32,1024]{1,0:T(8,128)(2,1)S(1)}, u32[]{:S(2)}, u32[]{:S(2)}) collective-permute-start(bf16[32,1024]{1,0:T(8,128)(2,1)S(1)} %get-tuple-element.48), channel_id=1, source_target_pairs={{0,4},{4,0},{8,12},{12,8},{1,5},{5,1},{9,13},{13,9},{2,6},{6,2},{1... | collective-permute-start | bytes 196616 | tf_op jit(solution)/shard_map/ppermute | solution.py:617
  69.8 3.1 %collective-permute-done.23 = bf16[32,1024]{1,0:T(8,128)(2,1)S(1)} collective-permute-done((bf16[32,1024]{1,0:T(8,128)(2,1)S(1)}, bf16[32,1024]{1,0:T(8,128)(2,1)S(1)}, u32[]{:S(2)}, u32[]{:S(2)}) %collective-permute-start.23) | collective-permute-done | bytes 65568 | tf_op jit(solution)/shard_map/ppermute | solution.py:617
  73.0 0.9 %collective-permute-done.24 = bf16[32,1024]{1,0:T(8,128)(2,1)S(1)} collective-permute-done((bf16[32,1024]{1,0:T(8,128)(2,1)S(1)}, bf16[32,1024]{1,0:T(8,128)(2,1)S(1)}, u32[]{:S(2)}, u32[]{:S(2)}) %collective-permute-start.24) | collective-permute-done | bytes 65568 | tf_op jit(solution)/shard_map/ppermute | solution.py:617
  74.0 1.5 %shard_map.135 = (bf16[2,32,896]{2,1,0:T(8,128)(2,1)S(1)}, bf16[2,32,896]{2,1,0:T(8,128)(2,1)S(1)}) custom-call(bf16[4,64,128]{2,1,0:T(8,128)(2,1)S(1)} %get-tuple-element.32.picker, bf16[128,1024]{1,0:T(8,128)(2,1)S(1)} %constant_dynamic-update-slice_fusion.residual.before, bf16[3584,1024]{1,0:T(8,128)(2,1)S(1)} %bitcast.32, ...), custom_call_target="tpu_custom_call" | custom-call | tf_op jit(solution)/shard_map/pallas_call | solution.py:428
  75.6 1.3 %shard_map.136 = (bf16[2,32,896]{2,1,0:T(8,128)(2,1)S(1)}, bf16[2,32,896]{2,1,0:T(8,128)(2,1)S(1)}) custom-call(bf16[4,64,128]{2,1,0:T(8,128)(2,1)S(1)} %get-tuple-element.32.picker, bf16[128,1024]{1,0:T(8,128)(2,1)S(1)} %constant_dynamic-update-slice_fusion.residual.before, bf16[3584,1024]{1,0:T(8,128)(2,1)S(1)} %bitcast.32, ...), custom_call_target="tpu_custom_call" | custom-call | tf_op jit(solution)/shard_map/pallas_call | solution.py:428
  77.0 0.6 collective-permute-start.28
  77.6 1.4 %collective-permute-start.27 = (bf16[2,32,896]{2,1,0:T(8,128)(2,1)S(1)}, bf16[2,32,896]{2,1,0:T(8,128)(2,1)S(1)}, u32[]{:S(2)}, u32[]{:S(2)}) collective-permute-start(bf16[2,32,896]{2,1,0:T(8,128)(2,1)S(1)} %add_convert_fusion.3.mine), channel_id=1, source_target_pairs={{0,2},{2,0},{1,3},{3,1},{4,6},{6,4},{5,7},{7,5},{8,10},{10,8},{9,1... | collective-permute-start | bytes 344072 | tf_op jit(solution)/shard_map/ppermute | solution.py:16
  79.0 0.9 %collective-permute-start.30 = (bf16[2,32,896]{2,1,0:T(8,128)(2,1)S(1)}, bf16[2,32,896]{2,1,0:T(8,128)(2,1)S(1)}, u32[]{:S(2)}, u32[]{:S(2)}) collective-permute-start(bf16[2,32,896]{2,1,0:T(8,128)(2,1)S(1)} %add_convert_fusion.2.before.mine), channel_id=1, source_target_pairs={{0,2},{2,0},{1,3},{3,1},{4,6},{6,4},{5,7},{7,5},{8,10},{10,8},{9,1... | collective-permute-start | bytes 344072 | tf_op jit(solution)/shard_map/ppermute | solution.py:16
  79.9 3.4 %shard_map.137 = (bf16[3584,1024]{1,0:T(8,128)(2,1)}, f32[8,128]{1,0:T(8,128)S(1)}) custom-call(bf16[3584,128]{1,0:T(8,128)(2,1)S(1)} %get-tuple-element.51.hidden, bf16[128,1024]{1,0:T(8,128)(2,1)S(1)} %constant_dynamic-update-slice_fusion.residual.before, bf16[2,32,896]{2,1,0:T(8,128)(2,1)S(1)} %add_convert_fusion.2.before.mine), custom_call_target="tpu_custom_call" | custom-call | flops 939524096 | bytes 7340032 | tf_op jit(solution)/shard_map/pallas_call | solution.py:480
  83.3 0.3 collective-permute-done.27.other
  83.6 0.2 shard_map.138.rest_0_
  83.9 1.3 %collective-permute-done.30.other = bf16[2,32,896]{2,1,0:T(8,128)(2,1)S(1)} collective-permute-done((bf16[2,32,896]{2,1,0:T(8,128)(2,1)S(1)}, bf16[2,32,896]{2,1,0:T(8,128)(2,1)S(1)}, u32[]{:S(2)}, u32[]{:S(2)}) %collective-permute-start.30) | collective-permute-done | bytes 114720 | tf_op jit(solution)/shard_map/ppermute | solution.py:16
  85.2 0.2 shard_map.139.rest_2_
  85.4 0.6 convert_element_type.81
  86.0 0.8 collective-permute-done.31.rest_3_
  86.9 6.5 %shard_map.140 = (bf16[1024,3584]{1,0:T(8,128)(2,1)}, bf16[1024,3584]{1,0:T(8,128)(2,1)}) custom-call(bf16[4,64,128]{2,1,0:T(8,128)(2,1)S(1)} %get-tuple-element.32.picker, bf16[1024,128]{1,0:T(8,128)(2,1)S(1)} %get-tuple-element.46.refs_8_.tokens, bf16[2,2,32,896]{3,2,1,0:T(8,128)(2,1)S(1)} %shard_map.138.rest_0_, ...), custom_call_target="tpu_custom_call" | custom-call | flops 1879048192 | bytes 14680064 | tf_op jit(solution)/shard_map/pallas_call | solution.py:530
  (61 shorter events, 1.1 us)
Async XLA Ops:
  0.6 11.7 %collective-permute-start = (bf16[32,1024]{1,0:T(8,128)(2,1)}, bf16[32,1024]{1,0:T(8,128)(2,1)S(1)}, u32[]{:S(2)}, u32[]{:S(2)}) collective-permute-start(bf16[32,1024]{1,0:T(8,128)(2,1)} %param.9), channel_id=1, source_target_pairs={{0,4},{4,0},{8,12},{12,8},{1,5},{5,1},{9,13},{13,9},{2,6},{6,2},{1... | collective-permute-start | bytes 196616 | tf_op jit(solution)/shard_map/ppermute | solution.py:617
  3.7 9.2 %collective-permute-start.2 = (bf16[32,1024]{1,0:T(8,128)(2,1)}, bf16[32,1024]{1,0:T(8,128)(2,1)S(1)}, u32[]{:S(2)}, u32[]{:S(2)}) collective-permute-start(bf16[32,1024]{1,0:T(8,128)(2,1)} %param.9), channel_id=1, source_target_pairs={{0,12},{4,8},{8,4},{12,0},{1,13},{5,9},{9,5},{13,1},{2,14},{6,10},... | collective-permute-start | bytes 196616 | tf_op jit(solution)/shard_map/ppermute | solution.py:617
  6.2 6.7 %collective-permute-start.1 = (bf16[32,1024]{1,0:T(8,128)(2,1)}, bf16[32,1024]{1,0:T(8,128)(2,1)S(1)}, u32[]{:S(2)}, u32[]{:S(2)}) collective-permute-start(bf16[32,1024]{1,0:T(8,128)(2,1)} %param.9), channel_id=1, source_target_pairs={{0,8},{4,12},{8,0},{12,4},{1,9},{5,13},{9,1},{13,5},{2,10},{6,14},... | collective-permute-start | bytes 196616 | tf_op jit(solution)/shard_map/ppermute | solution.py:617
  6.4 5.9 %copy-start = (bf16[32,1024]{1,0:T(8,128)(2,1)S(1)}, bf16[32,1024]{1,0:T(8,128)(2,1)}, u32[]{:S(2)}) copy-start(bf16[32,1024]{1,0:T(8,128)(2,1)} %param.9) | copy-start | bytes 196612
  14.6 2.3 %collective-permute-start.8 = (bf16[2,64,1792]{2,1,0:T(8,128)(2,1)S(1)}, bf16[2,64,1792]{2,1,0:T(8,128)(2,1)S(1)}, u32[]{:S(2)}, u32[]{:S(2)}) collective-permute-start(bf16[2,64,1792]{2,1,0:T(8,128)(2,1)S(1)} %get-tuple-element.43), channel_id=1, source_target_pairs={{0,1},{1,0},{2,3},{3,2},{4,5},{5,4},{6,7},{7,6},{8,9},{9,8},{10,11... | collective-permute-start | bytes 1376264 | tf_op jit(solution)/shard_map/ppermute | solution.py:16
  16.3 2.3 %collective-permute-start.3 = (bf16[2,64,1792]{2,1,0:T(8,128)(2,1)S(1)}, bf16[2,64,1792]{2,1,0:T(8,128)(2,1)S(1)}, u32[]{:S(2)}, u32[]{:S(2)}) collective-permute-start(bf16[2,64,1792]{2,1,0:T(8,128)(2,1)S(1)} %get-tuple-element.36), channel_id=1, source_target_pairs={{0,1},{1,0},{2,3},{3,2},{4,5},{5,4},{6,7},{7,6},{8,9},{9,8},{10,11... | collective-permute-start | bytes 1376264 | tf_op jit(solution)/shard_map/ppermute | solution.py:16
  17.0 9.7 %collective-permute-start.9 = (bf16[2,32,1792]{2,1,0:T(8,128)(2,1)S(1)}, bf16[2,32,1792]{2,1,0:T(8,128)(2,1)S(1)}, u32[]{:S(2)}, u32[]{:S(2)}) collective-permute-start(bf16[2,32,1792]{2,1,0:T(8,128)(2,1)S(1)} %slice.33), channel_id=1, source_target_pairs={{0,2},{2,0},{1,3},{3,1},{4,6},{6,4},{5,7},{7,5},{8,10},{10,8},{9,1... | collective-permute-start | bytes 688136 | tf_op jit(solution)/shard_map/ppermute | solution.py:16
  18.7 10.8 %collective-permute-start.12 = (bf16[2,32,1792]{2,1,0:T(8,128)(2,1)S(1)}, bf16[2,32,1792]{2,1,0:T(8,128)(2,1)S(1)}, u32[]{:S(2)}, u32[]{:S(2)}) collective-permute-start(bf16[2,32,1792]{2,1,0:T(8,128)(2,1)S(1)} %slice.37), channel_id=1, source_target_pairs={{0,2},{2,0},{1,3},{3,1},{4,6},{6,4},{5,7},{7,5},{8,10},{10,8},{9,1... | collective-permute-start | bytes 688136 | tf_op jit(solution)/shard_map/ppermute | solution.py:16
  20.1 17.8 %slice-start.2 = ((s8[7340032]{0:T(1024)(128)(4,1)}), s8[4194304]{0:T(1024)(128)(4,1)S(1)}, s32[]{:S(2)}) async-start(s8[7340032]{0:T(1024)(128)(4,1)} %bitcast.33), calls=%async_computation.2 | async-start | bytes 8388608
  20.1 17.8 %slice-start.3 = ((s8[7340032]{0:T(1024)(128)(4,1)}), s8[3145728]{0:T(1024)(128)(4,1)S(1)}, s32[]{:S(2)}) async-start(s8[7340032]{0:T(1024)(128)(4,1)} %bitcast.33), calls=%async_computation.3 | async-start | bytes 6291456
  26.6 4.8 %collective-permute-start.5 = (bf16[4,2,16,896]{3,2,1,0:T(8,128)(2,1)S(1)}, bf16[4,2,16,896]{3,2,1,0:T(8,128)(2,1)S(1)}, u32[]{:S(2)}, u32[]{:S(2)}) collective-permute-start(bf16[4,2,16,896]{3,2,1,0:T(8,128)(2,1)S(1)} %get-tuple-element.40), channel_id=1, source_target_pairs={{0,1},{1,0},{2,3},{3,2},{4,5},{5,4},{6,7},{7,6},{8,9},{9,8},{10,11... | collective-permute-start | bytes 688136 | tf_op jit(solution)/shard_map/ppermute | solution.py:16
  26.9 6.0 %collective-permute-start.10 = (bf16[32,1792]{1,0:T(8,128)(2,1)S(1)}, bf16[32,1792]{1,0:T(8,128)(2,1)S(1)}, u32[]{:S(2)}, u32[]{:S(2)}) collective-permute-start(bf16[32,1792]{1,0:T(8,128)(2,1)S(1)} %fusion.3.refs_0_), channel_id=1, source_target_pairs={{0,2},{2,0},{1,3},{3,1},{4,6},{6,4},{5,7},{7,5},{8,10},{10,8},{9,1... | collective-permute-start | bytes 344072 | tf_op jit(solution)/shard_map/ppermute | solution.py:16
  29.7 5.2 %collective-permute-start.13 = (bf16[32,1792]{1,0:T(8,128)(2,1)S(1)}, bf16[32,1792]{1,0:T(8,128)(2,1)S(1)}, u32[]{:S(2)}, u32[]{:S(2)}) collective-permute-start(bf16[32,1792]{1,0:T(8,128)(2,1)S(1)} %fusion.1.refs_0_), channel_id=1, source_target_pairs={{0,2},{2,0},{1,3},{3,1},{4,6},{6,4},{5,7},{7,5},{8,10},{10,8},{9,1... | collective-permute-start | bytes 344072 | tf_op jit(solution)/shard_map/ppermute | solution.py:16
  31.4 5.0 %collective-permute-start.4 = (bf16[4,2,16,896]{3,2,1,0:T(8,128)(2,1)S(1)}, bf16[4,2,16,896]{3,2,1,0:T(8,128)(2,1)S(1)}, u32[]{:S(2)}, u32[]{:S(2)}) collective-permute-start(bf16[4,2,16,896]{3,2,1,0:T(8,128)(2,1)S(1)} %get-tuple-element.38), channel_id=1, source_target_pairs={{0,1},{1,0},{2,3},{3,2},{4,5},{5,4},{6,7},{7,6},{8,9},{9,8},{10,11... | collective-permute-start | bytes 688136 | tf_op jit(solution)/shard_map/ppermute | solution.py:16
  33.0 4.3 %collective-permute-start.11 = (bf16[64,1792]{1,0:T(8,128)(2,1)S(1)}, bf16[64,1792]{1,0:T(8,128)(2,1)S(1)}, u32[]{:S(2)}, u32[]{:S(2)}) collective-permute-start(bf16[64,1792]{1,0:T(8,128)(2,1)S(1)} %shard_map.126.refs_0_), channel_id=1, source_target_pairs={{0,1},{1,0},{2,3},{3,2},{4,5},{5,4},{6,7},{7,6},{8,9},{9,8},{10,11... | collective-permute-start | bytes 688136 | tf_op jit(solution)/shard_map/ppermute | solution.py:16
  35.0 2.3 %collective-permute-start.14 = (bf16[64,1792]{1,0:T(8,128)(2,1)S(1)}, bf16[64,1792]{1,0:T(8,128)(2,1)S(1)}, u32[]{:S(2)}, u32[]{:S(2)}) collective-permute-start(bf16[64,1792]{1,0:T(8,128)(2,1)S(1)} %shard_map.127.refs_2_), channel_id=1, source_target_pairs={{0,1},{1,0},{2,3},{3,2},{4,5},{5,4},{6,7},{7,6},{8,9},{9,8},{10,11... | collective-permute-start | bytes 688136 | tf_op jit(solution)/shard_map/ppermute | solution.py:16
  35.0 8.5 %collective-permute-start.7 = (bf16[4,2,16,896]{3,2,1,0:T(8,128)(2,1)S(1)}, bf16[4,2,16,896]{3,2,1,0:T(8,128)(2,1)S(1)}, u32[]{:S(2)}, u32[]{:S(2)}) collective-permute-start(bf16[4,2,16,896]{3,2,1,0:T(8,128)(2,1)S(1)} %shard_map.123.before.refs_2_.mine), channel_id=1, source_target_pairs={{0,2},{2,0},{1,3},{3,1},{4,6},{6,4},{5,7},{7,5},{8,10},{10,8},{9,1... | collective-permute-start | bytes 688136 | tf_op jit(solution)/shard_map/ppermute | solution.py:16
  36.5 11.7 %collective-permute-start.6 = (bf16[4,2,16,896]{3,2,1,0:T(8,128)(2,1)S(1)}, bf16[4,2,16,896]{3,2,1,0:T(8,128)(2,1)S(1)}, u32[]{:S(2)}, u32[]{:S(2)}) collective-permute-start(bf16[4,2,16,896]{3,2,1,0:T(8,128)(2,1)S(1)} %shard_map.124.mine), channel_id=1, source_target_pairs={{0,2},{2,0},{1,3},{3,1},{4,6},{6,4},{5,7},{7,5},{8,10},{10,8},{9,1... | collective-permute-start | bytes 688136 | tf_op jit(solution)/shard_map/ppermute | solution.py:16
  39.1 6.5 %collective-permute-start.16 = (bf16[32,1024]{1,0:T(8,128)(2,1)S(1)}, bf16[32,1024]{1,0:T(8,128)(2,1)S(1)}, u32[]{:S(2)}, u32[]{:S(2)}) collective-permute-start(bf16[32,1024]{1,0:T(8,128)(2,1)S(1)} %get-tuple-element.62), channel_id=1, source_target_pairs={{0,12},{4,8},{8,4},{12,0},{1,13},{5,9},{9,5},{13,1},{2,14},{6,10},... | collective-permute-start | bytes 196616 | tf_op jit(solution)/shard_map/ppermute | solution.py:617
  41.6 4.7 %collective-permute-start.15 = (bf16[32,1024]{1,0:T(8,128)(2,1)S(1)}, bf16[32,1024]{1,0:T(8,128)(2,1)S(1)}, u32[]{:S(2)}, u32[]{:S(2)}) collective-permute-start(bf16[32,1024]{1,0:T(8,128)(2,1)S(1)} %get-tuple-element.63), channel_id=1, source_target_pairs={{0,4},{4,0},{8,12},{12,8},{1,5},{5,1},{9,13},{13,9},{2,6},{6,2},{1... | collective-permute-start | bytes 196616 | tf_op jit(solution)/shard_map/ppermute | solution.py:617
  46.4 1.4 %collective-permute-start.17 = (bf16[4,16,896]{2,1,0:T(8,128)(2,1)S(1)}, bf16[4,16,896]{2,1,0:T(8,128)(2,1)S(1)}, u32[]{:S(2)}, u32[]{:S(2)}) collective-permute-start(bf16[4,16,896]{2,1,0:T(8,128)(2,1)S(1)} %get-tuple-element.44.mine), channel_id=1, source_target_pairs={{0,1},{1,0},{2,3},{3,2},{4,5},{5,4},{6,7},{7,6},{8,9},{9,8},{10,11... | collective-permute-start | bytes 344072 | tf_op jit(solution)/shard_map/ppermute | solution.py:16
  46.5 16.7 %collective-permute-start.22 = (bf16[32,1024]{1,0:T(8,128)(2,1)S(1)}, bf16[32,1024]{1,0:T(8,128)(2,1)S(1)}, u32[]{:S(2)}, u32[]{:S(2)}) collective-permute-start(bf16[32,1024]{1,0:T(8,128)(2,1)S(1)} %get-tuple-element.60), channel_id=1, source_target_pairs={{0,8},{4,12},{8,0},{12,4},{1,9},{5,13},{9,1},{13,5},{2,10},{6,14},... | collective-permute-start | bytes 196616 | tf_op jit(solution)/shard_map/ppermute | solution.py:617
  48.3 7.5 %collective-permute-start.18 = (bf16[4,16,896]{2,1,0:T(8,128)(2,1)S(1)}, bf16[4,16,896]{2,1,0:T(8,128)(2,1)S(1)}, u32[]{:S(2)}, u32[]{:S(2)}) collective-permute-start(bf16[4,16,896]{2,1,0:T(8,128)(2,1)S(1)} %get-tuple-element.45.mine), channel_id=1, source_target_pairs={{0,1},{1,0},{2,3},{3,2},{4,5},{5,4},{6,7},{7,6},{8,9},{9,8},{10,11... | collective-permute-start | bytes 344072 | tf_op jit(solution)/shard_map/ppermute | solution.py:16
  48.5 25.5 %slice-start = ((s8[7340032]{0:T(1024)(128)(4,1)}), s8[4194304]{0:T(1024)(128)(4,1)S(1)}, s32[]{:S(2)}) async-start(s8[7340032]{0:T(1024)(128)(4,1)} %bitcast.31), calls=%async_computation | async-start | bytes 8388608
  53.2 10.0 %collective-permute-start.21 = (bf16[32,1024]{1,0:T(8,128)(2,1)S(1)}, bf16[32,1024]{1,0:T(8,128)(2,1)S(1)}, u32[]{:S(2)}, u32[]{:S(2)}) collective-permute-start(bf16[32,1024]{1,0:T(8,128)(2,1)S(1)} %get-tuple-element.64), channel_id=1, source_target_pairs={{0,12},{4,8},{8,4},{12,0},{1,13},{5,9},{9,5},{13,1},{2,14},{6,10},... | collective-permute-start | bytes 196616 | tf_op jit(solution)/shard_map/ppermute | solution.py:617
  55.3 7.8 %collective-permute-start.20 = (bf16[32,1024]{1,0:T(8,128)(2,1)S(1)}, bf16[32,1024]{1,0:T(8,128)(2,1)S(1)}, u32[]{:S(2)}, u32[]{:S(2)}) collective-permute-start(bf16[32,1024]{1,0:T(8,128)(2,1)S(1)} %get-tuple-element.65), channel_id=1, source_target_pairs={{0,8},{4,12},{8,0},{12,4},{1,9},{5,13},{9,1},{13,5},{2,10},{6,14},... | collective-permute-start | bytes 196616 | tf_op jit(solution)/shard_map/ppermute | solution.py:617
  56.3 17.7 %slice-start.1 = ((s8[7340032]{0:T(1024)(128)(4,1)}), s8[3145728]{0:T(1024)(128)(4,1)S(1)}, s32[]{:S(2)}) async-start(s8[7340032]{0:T(1024)(128)(4,1)} %bitcast.31), calls=%async_computation.1 | async-start | bytes 6291456
  60.9 4.3 %collective-permute-start.19 = (bf16[32,1024]{1,0:T(8,128)(2,1)S(1)}, bf16[32,1024]{1,0:T(8,128)(2,1)S(1)}, u32[]{:S(2)}, u32[]{:S(2)}) collective-permute-start(bf16[32,1024]{1,0:T(8,128)(2,1)S(1)} %get-tuple-element.66), channel_id=1, source_target_pairs={{0,4},{4,0},{8,12},{12,8},{1,5},{5,1},{9,13},{13,9},{2,6},{6,2},{1... | collective-permute-start | bytes 196616 | tf_op jit(solution)/shard_map/ppermute | solution.py:617
  65.3 8.6 %collective-permute-start.25 = (bf16[32,1024]{1,0:T(8,128)(2,1)S(1)}, bf16[32,1024]{1,0:T(8,128)(2,1)S(1)}, u32[]{:S(2)}, u32[]{:S(2)}) collective-permute-start(bf16[32,1024]{1,0:T(8,128)(2,1)S(1)} %get-tuple-element.48), channel_id=1, source_target_pairs={{0,12},{4,8},{8,4},{12,0},{1,13},{5,9},{9,5},{13,1},{2,14},{6,10},... | collective-permute-start | bytes 196616 | tf_op jit(solution)/shard_map/ppermute | solution.py:617
  67.7 6.2 %collective-permute-start.24 = (bf16[32,1024]{1,0:T(8,128)(2,1)S(1)}, bf16[32,1024]{1,0:T(8,128)(2,1)S(1)}, u32[]{:S(2)}, u32[]{:S(2)}) collective-permute-start(bf16[32,1024]{1,0:T(8,128)(2,1)S(1)} %get-tuple-element.48), channel_id=1, source_target_pairs={{0,8},{4,12},{8,0},{12,4},{1,9},{5,13},{9,1},{13,5},{2,10},{6,14},... | collective-permute-start | bytes 196616 | tf_op jit(solution)/shard_map/ppermute | solution.py:617
  68.7 4.3 %collective-permute-start.23 = (bf16[32,1024]{1,0:T(8,128)(2,1)S(1)}, bf16[32,1024]{1,0:T(8,128)(2,1)S(1)}, u32[]{:S(2)}, u32[]{:S(2)}) collective-permute-start(bf16[32,1024]{1,0:T(8,128)(2,1)S(1)} %get-tuple-element.48), channel_id=1, source_target_pairs={{0,4},{4,0},{8,12},{12,8},{1,5},{5,1},{9,13},{13,9},{2,6},{6,2},{1... | collective-permute-start | bytes 196616 | tf_op jit(solution)/shard_map/ppermute | solution.py:617
  75.5 2.0 %collective-permute-start.26 = (bf16[2,32,896]{2,1,0:T(8,128)(2,1)S(1)}, bf16[2,32,896]{2,1,0:T(8,128)(2,1)S(1)}, u32[]{:S(2)}, u32[]{:S(2)}) collective-permute-start(bf16[2,32,896]{2,1,0:T(8,128)(2,1)S(1)} %get-tuple-element.50), channel_id=1, source_target_pairs={{0,1},{1,0},{2,3},{3,2},{4,5},{5,4},{6,7},{7,6},{8,9},{9,8},{10,11... | collective-permute-start | bytes 344072 | tf_op jit(solution)/shard_map/ppermute | solution.py:16
  77.0 2.0 %collective-permute-start.28 = (bf16[2,32,896]{2,1,0:T(8,128)(2,1)S(1)}, bf16[2,32,896]{2,1,0:T(8,128)(2,1)S(1)}, u32[]{:S(2)}, u32[]{:S(2)}) collective-permute-start(bf16[2,32,896]{2,1,0:T(8,128)(2,1)S(1)} %get-tuple-element.53), channel_id=1, source_target_pairs={{0,1},{1,0},{2,3},{3,2},{4,5},{5,4},{6,7},{7,6},{8,9},{9,8},{10,11... | collective-permute-start | bytes 344072 | tf_op jit(solution)/shard_map/ppermute | solution.py:16
  77.6 6.1 %collective-permute-start.27 = (bf16[2,32,896]{2,1,0:T(8,128)(2,1)S(1)}, bf16[2,32,896]{2,1,0:T(8,128)(2,1)S(1)}, u32[]{:S(2)}, u32[]{:S(2)}) collective-permute-start(bf16[2,32,896]{2,1,0:T(8,128)(2,1)S(1)} %add_convert_fusion.3.mine), channel_id=1, source_target_pairs={{0,2},{2,0},{1,3},{3,1},{4,6},{6,4},{5,7},{7,5},{8,10},{10,8},{9,1... | collective-permute-start | bytes 344072 | tf_op jit(solution)/shard_map/ppermute | solution.py:16
  79.0 6.2 %collective-permute-start.30 = (bf16[2,32,896]{2,1,0:T(8,128)(2,1)S(1)}, bf16[2,32,896]{2,1,0:T(8,128)(2,1)S(1)}, u32[]{:S(2)}, u32[]{:S(2)}) collective-permute-start(bf16[2,32,896]{2,1,0:T(8,128)(2,1)S(1)} %add_convert_fusion.2.before.mine), channel_id=1, source_target_pairs={{0,2},{2,0},{1,3},{3,1},{4,6},{6,4},{5,7},{7,5},{8,10},{10,8},{9,1... | collective-permute-start | bytes 344072 | tf_op jit(solution)/shard_map/ppermute | solution.py:16
  83.8 2.2 %collective-permute-start.29 = (bf16[2,2,32,896]{3,2,1,0:T(8,128)(2,1)S(1)}, bf16[2,2,32,896]{3,2,1,0:T(8,128)(2,1)S(1)}, u32[]{:S(2)}, u32[]{:S(2)}) collective-permute-start(bf16[2,2,32,896]{3,2,1,0:T(8,128)(2,1)S(1)} %shard_map.138.rest_0_), channel_id=1, source_target_pairs={{0,1},{1,0},{2,3},{3,2},{4,5},{5,4},{6,7},{7,6},{8,9},{9,8},{10,11... | collective-permute-start | bytes 688136 | tf_op jit(solution)/shard_map/ppermute | solution.py:16
  85.3 1.6 %collective-permute-start.31 = (bf16[2,2,32,896]{3,2,1,0:T(8,128)(2,1)S(1)}, bf16[2,2,32,896]{3,2,1,0:T(8,128)(2,1)S(1)}, u32[]{:S(2)}, u32[]{:S(2)}) collective-permute-start(bf16[2,2,32,896]{3,2,1,0:T(8,128)(2,1)S(1)} %shard_map.139.rest_2_), channel_id=1, source_target_pairs={{0,1},{1,0},{2,3},{3,2},{4,5},{5,4},{6,7},{7,6},{8,9},{9,8},{10,11... | collective-permute-start | bytes 688136 | tf_op jit(solution)/shard_map/ppermute | solution.py:16

commit v13 on v12

--- a/solution.py
+++ b/solution.py
@@ -151,6 +151,47 @@
     )(place, far(routes), far(shares), far(gate), far(up))
 
 
+def load_kernel(source, before, out, sems):
+    for copy in load_start(((source, out),), sems, 8):
+        copy.wait()
+
+
+def load(source, before):
+    return pl.pallas_call(
+        load_kernel,
+        in_specs=[in_hbm(), anywhere()],
+        out_specs=whole(),
+        out_shape=pltpu.VMEM(source.shape, source.dtype),
+        scratch_shapes=[pltpu.SemaphoreType.DMA((1, 8))],
+        compiler_params=pltpu.CompilerParams(vmem_limit_bytes=4 * 1024 * 1024),
+    )(far(source), before)
+
+
+def teacher_act_kernel(count, *refs):
+    out = refs[-1]
+    rows = out.shape[0]
+    totals = []
+    for which in range(2):
+        total = refs[0][which, :rows].astype(F32)
+        for theirs in refs[1:count]:
+            total = total + theirs[which].astype(F32)
+        totals.append(total)
+    gate, up = totals
+    out[...] = (gate * jax.nn.sigmoid(gate) * up).astype(BF)
+
+
+def teacher_act(half, dps, before):
+    pieces = split_rows(half, dps)
+    received = [shift(pieces[r], "dp", dps, r) for r in range(1, dps)]
+    return pl.pallas_call(
+        functools.partial(teacher_act_kernel, dps),
+        in_specs=[whole()] * dps + [anywhere()] * len(before),
+        out_specs=whole(),
+        out_shape=jax.ShapeDtypeStruct((half.shape[1] // dps, half.shape[2]), BF),
+        compiler_params=pltpu.CompilerParams(vmem_limit_bytes=4 * 1024 * 1024),
+    )(half, *received, *before)
+
+
 def residual_kernel(ranks, *refs):
     student = refs[0][...].astype(F32)
     target = refs[ranks][...].astype(F32)
@@ -672,9 +713,12 @@
         half = add_after(outs[2 * i], shift(outs[2 * i + 1], "pipe", pipes, 1), half)
         parts.append(exchange_dp(half, dps, near_first))
     hiddens = []
+    before = []
     for half in halves:
-        total = scatter_dp(half, dps)
-        hidden = (jax.nn.silu(total[0]) * total[1]).astype(BF)
+        hidden = teacher_act(half, dps, before)
+        if not before:
+            expert_near = load(expert_down, hidden)
+            before = [expert_near]
         hidden = pair(gather_dp_parts(hidden, dps), parts[0][0])
         hiddens.append((hidden, shift(hidden, "pipe", pipes, 1)))
     hidden = join(place, hiddens, dps, pipes)
@@ -687,19 +731,19 @@
         total, part = hidden_act(mine, other, mode, slot_weight, wait, cut[0])
         pre.append(total)
         dense.append(spread(picker, part, shift(part, "pipe", pipes, 1), cut, rows))
-        wait = dense[-1:]
-        product = jnp.dot(dense[-1], expert_down, preferred_element_type=F32).astype(BF)
+        product = jnp.dot(dense[-1], expert_near, preferred_element_type=F32).astype(BF)
         count = (rows[1] - rows[0]) // block
         student = to_owners(product, rows[0] // block, count, rows[0]) + student
     dense_flipped, base_flipped = flip(dense[::-1], base, product)
-    student_sum, residual = residual_of(student, target, (base_flipped,))
+    expert_near = load(expert_down, base_flipped)
+    student_sum, residual = residual_of(student, target, (expert_near,))
 
     _, residual = gather_tokens(residual)
     group = 2 if experts % 2 == 0 else 1
     firsts = range(0, experts, group)
     sums, last = [], residual
     for first in firsts:
-        keep, send = hidden_grad_parts(picker, residual, expert_down, last, first, group)
+        keep, send = hidden_grad_parts(picker, residual, expert_near, last, first, group)
         last = keep
         sums.append(add(keep, shift(send, "pipe", pipes, 1)))
     exchanged = [exchange_dp(value, dps, near_first) for value in sums]

time: 93.7 us -> 98.9 us (1.055)
  Pallas kernels: 31.2 us -> 37.4 us
  waiting for transfers between devices: 19.1 us -> 15.9 us
  local copies, waits for them, and re-layouts: 0.25 us -> 3.29 us
    pallas_call x0 -> x4, Pallas kernels: none -> 6.61 us  [the longest x2 6.43 us: load(): pl.pallas_call(load_kernel, in_specs=[in_hbm(), anywhere()], out_specs=wh...]
    unnamed x10 -> x8, local copies, waits for them, and re-layouts: 0.02 us -> 3.06 us
    ppermute x12, waiting for transfers between devices: 9.38 us -> 7.39 us  [to_partner(): return lax.ppermute(value, 'expert', [(i, i ^ s) for i in range(ranks)])]
    ppermute x20, waiting for transfers between devices: 9.74 us -> 8.5 us  [shift(): lax.ppermute(value, axis, [(i, (i + by) % count) for i in range(count)])]
  transfers between devices with their start and end apart: 32 -> 32, of which waited for: 14 -> 11; matrix products, arithmetic and copies ran while one was open for 13% -> 11% of each run, Pallas kernels for 23% -> 28%
where the time goes in v13:
time: 98.9 us; the launch traced here: 98.7 us
  Pallas kernels  37.4 us (38%)
  starting transfers between devices  29.7 us (30%)
  waiting for transfers between devices  15.9 us (16%)
  matrix products  10.1 us (10%)
  local copies, waits for them, and re-layouts  3.29 us (3%)
  between operations  1.33 us (1%)
  other arithmetic  0.99 us (1%)
    ppermute x12, starting transfers between devices, to_partner(): return lax.ppermute(value, 'expert', [(i, i ^ s) for i in range(ranks)])  18.2 us
    ppermute x20, starting transfers between devices, shift(): lax.ppermute(value, axis, [(i, (i + by) % count) for i in range(count)])  11.5 us
    dot_general x2, matrix products, body(): jnp.dot(dense[-1], expert_near, preferred_element_type=F32).astype(BF)  8.94 us
    ppermute x20, waiting for transfers between devices, shift(): lax.ppermute(value, axis, [(i, (i + by) % count) for i in range(count)])  8.5 us
    ppermute x12, waiting for transfers between devices, to_partner(): return lax.ppermute(value, 'expert', [(i, i ^ s) for i in range(ranks)])  7.39 us
    pallas_call x1, Pallas kernels, input_grads(): pl.pallas_call(functools.partial(input_grad_kernel, count // len(parts)),...  6.48 us
    pallas_call x2, Pallas kernels, load(): pl.pallas_call(load_kernel, in_specs=[in_hbm(), anywhere()], out_specs=wh...  6.43 us
    pallas_call x1, Pallas kernels, expert_pre(): pl.pallas_call(functools.partial(expert_kernel, cuts), in_specs=[whole(),...  6.25 us
  transfers between devices with their start and end apart: 32, of which 11 were waited for; matrix products, arithmetic and copies ran while one was open for 11% of the time, Pallas kernels for 28%

profile of v13, /device:TPU:0, one launch (start us, length us, event | category | flops | bytes accessed | tf_op | source)
XLA Modules:
  0.0 98.7 jit_solution(13829566117975854664)
XLA Ops:
  0.6 3.1 %collective-permute-start = (bf16[32,1024]{1,0:T(8,128)(2,1)}, bf16[32,1024]{1,0:T(8,128)(2,1)S(1)}, u32[]{:S(2)}, u32[]{:S(2)}) collective-permute-start(bf16[32,1024]{1,0:T(8,128)(2,1)} %param.9), channel_id=1, source_target_pairs={{0,4},{4,0},{8,12},{12,8},{1,5},{5,1},{9,13},{13,9},{2,6},{6,2},{1... | collective-permute-start | bytes 196616 | tf_op jit(solution)/shard_map/ppermute | solution.py:658
  3.7 2.5 %collective-permute-start.2 = (bf16[32,1024]{1,0:T(8,128)(2,1)}, bf16[32,1024]{1,0:T(8,128)(2,1)S(1)}, u32[]{:S(2)}, u32[]{:S(2)}) collective-permute-start(bf16[32,1024]{1,0:T(8,128)(2,1)} %param.9), channel_id=1, source_target_pairs={{0,12},{4,8},{8,4},{12,0},{1,13},{5,9},{9,5},{13,1},{2,14},{6,10},... | collective-permute-start | bytes 196616 | tf_op jit(solution)/shard_map/ppermute | solution.py:658
  6.2 0.1 collective-permute-start.1
  6.3 0.1 pad_add_fusion.place
  6.4 5.9 %shard_map.120 = (bf16[4,64,128]{2,1,0:T(8,128)(2,1)S(1)}, f32[4,64,1]{2,1,0:T(8,128)S(1)}, bf16[1024,3584]{1,0:T(8,128)(2,1)S(1)}, bf16[1024,3584]{1,0:T(8,128)(2,1)S(1)}) custom-call(s32[3]{0:T(128)S(1)} %pad_add_fusion.place, s32[4,128]{1,0:T(4,128)} %bitcast.13, f32[4,128]{1,0:T(4,128)} %bitcast.14, bf16[1024,3584]{1,0:T(8,128)(2,1)} %gate.2, ...), custom_call_target="tpu_custom_call" | custom-call | bytes 14680064 | tf_op jit(solution)/shard_map/pallas_call | solution.py:131
  12.4 0.5 collective-permute-done.1
  12.9 1.7 %shard_map.125 = (bf16[2,64,1792]{2,1,0:T(8,128)(2,1)S(1)}, bf16[2,64,1792]{2,1,0:T(8,128)(2,1)S(1)}) custom-call(s32[3]{0:T(128)S(1)} %pad_add_fusion.place, bf16[128,1024]{1,0:T(8,128)(2,1)S(1)} %constant_dynamic-update-slice_fusion.4.tokens.refs_2_, bf16[1024,3584]{1,0:T(8,128)(2,1)S(1)} %get-tuple-element.33.gate, ...), custom_call_target="tpu_custom_call" | custom-call | flops 939524096 | bytes 7340032 | tf_op jit(solution)/shard_map/pallas_call | solution.py:242
  14.6 0.1 collective-permute-start.7
  14.7 1.7 %shard_map.121 = (bf16[2,64,1792]{2,1,0:T(8,128)(2,1)S(1)}, bf16[2,64,1792]{2,1,0:T(8,128)(2,1)S(1)}) custom-call(s32[3]{0:T(128)S(1)} %pad_add_fusion.place, bf16[128,1024]{1,0:T(8,128)(2,1)S(1)} %constant_dynamic-update-slice_fusion.4.tokens.refs_2_, bf16[1024,3584]{1,0:T(8,128)(2,1)S(1)} %get-tuple-element.33.gate, ...), custom_call_target="tpu_custom_call" | custom-call | flops 939524096 | bytes 7340032 | tf_op jit(solution)/shard_map/pallas_call | solution.py:242
  16.3 0.6 collective-permute-start.3
  16.9 0.1 add_convert_fusion.refs_0_
  17.0 1.6 %collective-permute-start.8 = (bf16[2,32,1792]{2,1,0:T(8,128)(2,1)S(1)}, bf16[2,32,1792]{2,1,0:T(8,128)(2,1)S(1)}, u32[]{:S(2)}, u32[]{:S(2)}) collective-permute-start(bf16[2,32,1792]{2,1,0:T(8,128)(2,1)S(1)} %slice.8), channel_id=1, source_target_pairs={{0,2},{2,0},{1,3},{3,1},{4,6},{6,4},{5,7},{7,5},{8,10},{10,8},{9,1... | collective-permute-start | bytes 688136 | tf_op jit(solution)/shard_map/ppermute | solution.py:16
  18.6 0.1 add_convert_fusion.1.before.refs_0_
  18.7 1.3 %collective-permute-start.11 = (bf16[2,32,1792]{2,1,0:T(8,128)(2,1)S(1)}, bf16[2,32,1792]{2,1,0:T(8,128)(2,1)S(1)}, u32[]{:S(2)}, u32[]{:S(2)}) collective-permute-start(bf16[2,32,1792]{2,1,0:T(8,128)(2,1)S(1)} %slice.9), channel_id=1, source_target_pairs={{0,2},{2,0},{1,3},{3,1},{4,6},{6,4},{5,7},{7,5},{8,10},{10,8},{9,1... | collective-permute-start | bytes 688136 | tf_op jit(solution)/shard_map/ppermute | solution.py:16
  20.1 6.2 %shard_map.122 = (bf16[4,2,16,896]{3,2,1,0:T(8,128)(2,1)S(1)}, bf16[4,2,16,896]{3,2,1,0:T(8,128)(2,1)S(1)}, bf16[4,2,16,896]{3,2,1,0:T(8,128)(2,1)S(1)}, bf16[4,2,16,896]{3,2,1,0:T(8,128)(2,1)S(1)}) custom-call(bf16[4,64,128]{2,1,0:T(8,128)(2,1)S(1)} %get-tuple-element.32.picker, bf16[128,1024]{1,0:T(8,128)(2,1)S(1)} %constant_dynamic-update-slice_fusion.4.tokens.refs_2_, ...), custom_call_target="tpu_custom_call" | custom-call | flops 939524096 | bytes 14680064 | tf_op jit(solution)/shard_map/pallas_call | solution.py:298
  26.3 0.1 collective-permute-start.5
  26.5 0.1 shard_map.126.refs_0_.before
  26.6 0.8 collective-permute-start.9
  27.3 3.3 %shard_map.128.refs_2_ = bf16[3584,1024]{1,0:T(8,128)(2,1)S(1)} custom-call(bf16[3584,1024]{1,0:T(8,128)(2,1)} %source.3, bf16[32,1792]{1,0:T(8,128)(2,1)S(1)} %shard_map.126.refs_0_.before), custom_call_target="tpu_custom_call" | custom-call | tf_op jit(solution)/shard_map/pallas_call | solution.py:160
  30.6 0.1 shard_map.129.refs_0_
  30.7 3.0 %copy-done = bf16[3584,1024]{1,0:T(8,128)(2,1)} copy-done((bf16[3584,1024]{1,0:T(8,128)(2,1)}, bf16[3584,1024]{1,0:T(8,128)(2,1)S(1)}, u32[]{:S(2)}) %copy-start) | copy-done | bytes 7340056
  33.8 1.2 %collective-permute-start.12 = (bf16[32,1792]{1,0:T(8,128)(2,1)S(1)}, bf16[32,1792]{1,0:T(8,128)(2,1)S(1)}, u32[]{:S(2)}, u32[]{:S(2)}) collective-permute-start(bf16[32,1792]{1,0:T(8,128)(2,1)S(1)} %shard_map.129.refs_0_), channel_id=1, source_target_pairs={{0,2},{2,0},{1,3},{3,1},{4,6},{6,4},{5,7},{7,5},{8,10},{10,8},{9,1... | collective-permute-start | bytes 344072 | tf_op jit(solution)/shard_map/ppermute | solution.py:16
  35.1 0.6 collective-permute-start.10
  35.7 3.6 %collective-permute-done.12.refs_1_ = bf16[32,1792]{1,0:T(8,128)(2,1)S(1)} collective-permute-done((bf16[32,1792]{1,0:T(8,128)(2,1)S(1)}, bf16[32,1792]{1,0:T(8,128)(2,1)S(1)}, u32[]{:S(2)}, u32[]{:S(2)}) %collective-permute-start.12) | collective-permute-done | bytes 114720 | tf_op jit(solution)/shard_map/ppermute | solution.py:16
  39.3 1.1 %collective-permute-start.18 = (bf16[4,2,16,896]{3,2,1,0:T(8,128)(2,1)S(1)}, bf16[4,2,16,896]{3,2,1,0:T(8,128)(2,1)S(1)}, u32[]{:S(2)}, u32[]{:S(2)}) collective-permute-start(bf16[4,2,16,896]{3,2,1,0:T(8,128)(2,1)S(1)} %shard_map.123.before.refs_2_.mine), channel_id=1, source_target_pairs={{0,2},{2,0},{1,3},{3,1},{4,6},{6,4},{5,7},{7,5},{8,10},{10,8},{9,1... | collective-permute-start | bytes 688136 | tf_op jit(solution)/shard_map/ppermute | solution.py:16
  40.4 1.1 %collective-permute-start.6 = (bf16[4,2,16,896]{3,2,1,0:T(8,128)(2,1)S(1)}, bf16[4,2,16,896]{3,2,1,0:T(8,128)(2,1)S(1)}, u32[]{:S(2)}, u32[]{:S(2)}) collective-permute-start(bf16[4,2,16,896]{3,2,1,0:T(8,128)(2,1)S(1)} %shard_map.124.mine), channel_id=1, source_target_pairs={{0,2},{2,0},{1,3},{3,1},{4,6},{6,4},{5,7},{7,5},{8,10},{10,8},{9,1... | collective-permute-start | bytes 688136 | tf_op jit(solution)/shard_map/ppermute | solution.py:16
  41.5 0.6 shard_map.131
  42.2 1.1 %convolution_convert_fusion = bf16[128,1024]{1,0:T(8,128)(2,1)S(1)} fusion(bf16[128,3584]{1,0:T(8,128)(2,1)S(1)} %shard_map.131, bf16[3584,1024]{1,0:T(8,128)(2,1)S(1)} %bitcast.12), kind=kOutput, calls=%fused_computation | convolution fusion | flops 939655168 | bytes 8519680 | tf_op jit(solution)/shard_map/dot_general | solution.py:725
  43.4 2.5 %collective-permute-start.15 = (bf16[32,1024]{1,0:T(8,128)(2,1)S(1)}, bf16[32,1024]{1,0:T(8,128)(2,1)S(1)}, u32[]{:S(2)}, u32[]{:S(2)}) collective-permute-start(bf16[32,1024]{1,0:T(8,128)(2,1)S(1)} %get-tuple-element.62), channel_id=1, source_target_pairs={{0,12},{4,8},{8,4},{12,0},{1,13},{5,9},{9,5},{13,1},{2,14},{6,10},... | collective-permute-start | bytes 196616 | tf_op jit(solution)/shard_map/ppermute | solution.py:658
  45.9 0.5 collective-permute-start.14
  46.3 1.5 %collective-permute-done.18.other = bf16[4,2,16,896]{3,2,1,0:T(8,128)(2,1)S(1)} collective-permute-done((bf16[4,2,16,896]{3,2,1,0:T(8,128)(2,1)S(1)}, bf16[4,2,16,896]{3,2,1,0:T(8,128)(2,1)S(1)}, u32[]{:S(2)}, u32[]{:S(2)}) %collective-permute-start.18) | collective-permute-done | bytes 229408 | tf_op jit(solution)/shard_map/ppermute | solution.py:16
  47.8 2.1 %collective-permute-done.15.rest_1_.refs_7_ = bf16[32,1024]{1,0:T(8,128)(2,1)S(1)} collective-permute-done((bf16[32,1024]{1,0:T(8,128)(2,1)S(1)}, bf16[32,1024]{1,0:T(8,128)(2,1)S(1)}, u32[]{:S(2)}, u32[]{:S(2)}) %collective-permute-start.15) | collective-permute-done | bytes 65568 | tf_op jit(solution)/shard_map/ppermute | solution.py:658
  49.8 0.7 collective-permute-done.14.rest_0_.refs_5_
  50.5 0.1 shard_map.134
  50.8 0.6 collective-permute-start.22
  51.4 0.9 collective-permute-done.6.other
  52.2 0.1 shard_map.132
  52.4 0.4 shard_map.135.refs_1_
  52.9 4.5 %convolution_convert_fusion.1 = bf16[64,1024]{1,0:T(8,128)(2,1)S(1)} fusion(bf16[64,3584]{1,0:T(8,128)(2,1)S(1)} %shard_map.135.refs_1_, bf16[3584,1024]{1,0:T(8,128)(2,1)} %copy-done), kind=kOutput, calls=%fused_computation.1 | convolution fusion | flops 469827584 | bytes 7929856 | tf_op jit(solution)/shard_map/dot_general | solution.py:734
  57.4 2.5 %collective-permute-start.21 = (bf16[32,1024]{1,0:T(8,128)(2,1)S(1)}, bf16[32,1024]{1,0:T(8,128)(2,1)S(1)}, u32[]{:S(2)}, u32[]{:S(2)}) collective-permute-start(bf16[32,1024]{1,0:T(8,128)(2,1)S(1)} %get-tuple-element.64), channel_id=1, source_target_pairs={{0,12},{4,8},{8,4},{12,0},{1,13},{5,9},{9,5},{13,1},{2,14},{6,10},... | collective-permute-start | bytes 196616 | tf_op jit(solution)/shard_map/ppermute | solution.py:658
  59.9 0.3 collective-permute-start.20
  60.2 0.4 shard_map.133.refs_0_
  60.7 4.5 %convolution_convert_fusion.2.refs_3_ = bf16[64,1024]{1,0:T(8,128)(2,1)S(1)} fusion(bf16[64,3584]{1,0:T(8,128)(2,1)S(1)} %shard_map.133.refs_0_, bf16[3584,1024]{1,0:T(8,128)(2,1)} %copy-done), kind=kOutput, calls=%fused_computation.2 | convolution fusion | flops 469827584 | bytes 7929856 | tf_op jit(solution)/shard_map/dot_general | solution.py:734
  65.2 1.7 %collective-permute-start.17 = (bf16[32,1024]{1,0:T(8,128)(2,1)S(1)}, bf16[32,1024]{1,0:T(8,128)(2,1)S(1)}, u32[]{:S(2)}, u32[]{:S(2)}) collective-permute-start(bf16[32,1024]{1,0:T(8,128)(2,1)S(1)} %get-tuple-element.66), channel_id=1, source_target_pairs={{0,4},{4,0},{8,12},{12,8},{1,5},{5,1},{9,13},{13,9},{2,6},{6,2},{1... | collective-permute-start | bytes 196616 | tf_op jit(solution)/shard_map/ppermute | solution.py:658
  66.8 0.4 shard_map.136
  67.2 3.2 %shard_map.137.refs_8_.down = bf16[3584,1024]{1,0:T(8,128)(2,1)S(1)} custom-call(bf16[3584,1024]{1,0:T(8,128)(2,1)} %source.3, bf16[1024,128]{1,0:T(8,128)(2,1)S(1)} %get-tuple-element.46.before.tokens), custom_call_target="tpu_custom_call" | custom-call | tf_op jit(solution)/shard_map/pallas_call | solution.py:160
  70.4 0.1 shard_map.138
  70.5 2.5 %collective-permute-start.25 = (bf16[32,1024]{1,0:T(8,128)(2,1)S(1)}, bf16[32,1024]{1,0:T(8,128)(2,1)S(1)}, u32[]{:S(2)}, u32[]{:S(2)}) collective-permute-start(bf16[32,1024]{1,0:T(8,128)(2,1)S(1)} %get-tuple-element.48), channel_id=1, source_target_pairs={{0,12},{4,8},{8,4},{12,0},{1,13},{5,9},{9,5},{13,1},{2,14},{6,10},... | collective-permute-start | bytes 196616 | tf_op jit(solution)/shard_map/ppermute | solution.py:658
  73.0 1.9 %collective-permute-start.23 = (bf16[32,1024]{1,0:T(8,128)(2,1)S(1)}, bf16[32,1024]{1,0:T(8,128)(2,1)S(1)}, u32[]{:S(2)}, u32[]{:S(2)}) collective-permute-start(bf16[32,1024]{1,0:T(8,128)(2,1)S(1)} %get-tuple-element.48), channel_id=1, source_target_pairs={{0,4},{4,0},{8,12},{12,8},{1,5},{5,1},{9,13},{13,9},{2,6},{6,2},{1... | collective-permute-start | bytes 196616 | tf_op jit(solution)/shard_map/ppermute | solution.py:658
  75.0 2.6 %collective-permute-done.23 = bf16[32,1024]{1,0:T(8,128)(2,1)S(1)} collective-permute-done((bf16[32,1024]{1,0:T(8,128)(2,1)S(1)}, bf16[32,1024]{1,0:T(8,128)(2,1)S(1)}, u32[]{:S(2)}, u32[]{:S(2)}) %collective-permute-start.23) | collective-permute-done | bytes 65568 | tf_op jit(solution)/shard_map/ppermute | solution.py:658
  77.6 1.6 %collective-permute-done.24 = bf16[32,1024]{1,0:T(8,128)(2,1)S(1)} collective-permute-done((bf16[32,1024]{1,0:T(8,128)(2,1)S(1)}, bf16[32,1024]{1,0:T(8,128)(2,1)S(1)}, u32[]{:S(2)}, u32[]{:S(2)}) %collective-permute-start.24) | collective-permute-done | bytes 65568 | tf_op jit(solution)/shard_map/ppermute | solution.py:658
  79.2 1.5 %shard_map.139 = (bf16[2,32,896]{2,1,0:T(8,128)(2,1)S(1)}, bf16[2,32,896]{2,1,0:T(8,128)(2,1)S(1)}) custom-call(bf16[4,64,128]{2,1,0:T(8,128)(2,1)S(1)} %get-tuple-element.32.picker, bf16[128,1024]{1,0:T(8,128)(2,1)S(1)} %constant_dynamic-update-slice_fusion.residual.before, bf16[3584,1024]{1,0:T(8,128)(2,1)S(1)} %shard_map.137.refs_8_.down, ...), custom_call_target="tpu_custom_call" | custom-call | tf_op jit(solution)/shard_map/pallas_call | solution.py:469
  80.8 1.4 %shard_map.140 = (bf16[2,32,896]{2,1,0:T(8,128)(2,1)S(1)}, bf16[2,32,896]{2,1,0:T(8,128)(2,1)S(1)}) custom-call(bf16[4,64,128]{2,1,0:T(8,128)(2,1)S(1)} %get-tuple-element.32.picker, bf16[128,1024]{1,0:T(8,128)(2,1)S(1)} %constant_dynamic-update-slice_fusion.residual.before, bf16[3584,1024]{1,0:T(8,128)(2,1)S(1)} %shard_map.137.refs_8_.down, ...), custom_call_target="tpu_custom_call" | custom-call | tf_op jit(solution)/shard_map/pallas_call | solution.py:469
  82.2 0.6 collective-permute-start.28
  82.8 1.1 %collective-permute-start.27 = (bf16[2,32,896]{2,1,0:T(8,128)(2,1)S(1)}, bf16[2,32,896]{2,1,0:T(8,128)(2,1)S(1)}, u32[]{:S(2)}, u32[]{:S(2)}) collective-permute-start(bf16[2,32,896]{2,1,0:T(8,128)(2,1)S(1)} %add_convert_fusion.3.mine), channel_id=1, source_target_pairs={{0,2},{2,0},{1,3},{3,1},{4,6},{6,4},{5,7},{7,5},{8,10},{10,8},{9,1... | collective-permute-start | bytes 344072 | tf_op jit(solution)/shard_map/ppermute | solution.py:16
  83.8 1.1 %collective-permute-start.30 = (bf16[2,32,896]{2,1,0:T(8,128)(2,1)S(1)}, bf16[2,32,896]{2,1,0:T(8,128)(2,1)S(1)}, u32[]{:S(2)}, u32[]{:S(2)}) collective-permute-start(bf16[2,32,896]{2,1,0:T(8,128)(2,1)S(1)} %add_convert_fusion.2.before.mine), channel_id=1, source_target_pairs={{0,2},{2,0},{1,3},{3,1},{4,6},{6,4},{5,7},{7,5},{8,10},{10,8},{9,1... | collective-permute-start | bytes 344072 | tf_op jit(solution)/shard_map/ppermute | solution.py:16
  84.9 3.4 %shard_map.141 = (bf16[3584,1024]{1,0:T(8,128)(2,1)}, f32[8,128]{1,0:T(8,128)S(1)}) custom-call(bf16[3584,128]{1,0:T(8,128)(2,1)S(1)} %get-tuple-element.51.hidden, bf16[128,1024]{1,0:T(8,128)(2,1)S(1)} %constant_dynamic-update-slice_fusion.residual.before, bf16[2,32,896]{2,1,0:T(8,128)(2,1)S(1)} %add_convert_fusion.2.before.mine), custom_call_target="tpu_custom_call" | custom-call | flops 939524096 | bytes 7340032 | tf_op jit(solution)/shard_map/pallas_call | solution.py:521
  88.4 0.4 collective-permute-done.27.other
  88.8 0.2 shard_map.142.rest_0_
  89.1 1.3 %collective-permute-done.30.other = bf16[2,32,896]{2,1,0:T(8,128)(2,1)S(1)} collective-permute-done((bf16[2,32,896]{2,1,0:T(8,128)(2,1)S(1)}, bf16[2,32,896]{2,1,0:T(8,128)(2,1)S(1)}, u32[]{:S(2)}, u32[]{:S(2)}) %collective-permute-start.30) | collective-permute-done | bytes 114720 | tf_op jit(solution)/shard_map/ppermute | solution.py:16
  90.4 0.2 shard_map.143.rest_2_
  90.6 0.6 convert_element_type.57
  91.2 0.8 collective-permute-done.31.rest_3_
  92.1 6.5 %shard_map.144 = (bf16[1024,3584]{1,0:T(8,128)(2,1)}, bf16[1024,3584]{1,0:T(8,128)(2,1)}) custom-call(bf16[4,64,128]{2,1,0:T(8,128)(2,1)S(1)} %get-tuple-element.32.picker, bf16[1024,128]{1,0:T(8,128)(2,1)S(1)} %get-tuple-element.46.before.tokens, bf16[2,2,32,896]{3,2,1,0:T(8,128)(2,1)S(1)} %shard_map.142.rest_0_, ...), custom_call_target="tpu_custom_call" | custom-call | flops 1879048192 | bytes 14680064 | tf_op jit(solution)/shard_map/pallas_call | solution.py:571
  (58 shorter events, 0.9 us)
Async XLA Ops:
  0.6 11.7 %collective-permute-start = (bf16[32,1024]{1,0:T(8,128)(2,1)}, bf16[32,1024]{1,0:T(8,128)(2,1)S(1)}, u32[]{:S(2)}, u32[]{:S(2)}) collective-permute-start(bf16[32,1024]{1,0:T(8,128)(2,1)} %param.9), channel_id=1, source_target_pairs={{0,4},{4,0},{8,12},{12,8},{1,5},{5,1},{9,13},{13,9},{2,6},{6,2},{1... | collective-permute-start | bytes 196616 | tf_op jit(solution)/shard_map/ppermute | solution.py:658
  3.7 9.2 %collective-permute-start.2 = (bf16[32,1024]{1,0:T(8,128)(2,1)}, bf16[32,1024]{1,0:T(8,128)(2,1)S(1)}, u32[]{:S(2)}, u32[]{:S(2)}) collective-permute-start(bf16[32,1024]{1,0:T(8,128)(2,1)} %param.9), channel_id=1, source_target_pairs={{0,12},{4,8},{8,4},{12,0},{1,13},{5,9},{9,5},{13,1},{2,14},{6,10},... | collective-permute-start | bytes 196616 | tf_op jit(solution)/shard_map/ppermute | solution.py:658
  6.2 6.7 %collective-permute-start.1 = (bf16[32,1024]{1,0:T(8,128)(2,1)}, bf16[32,1024]{1,0:T(8,128)(2,1)S(1)}, u32[]{:S(2)}, u32[]{:S(2)}) collective-permute-start(bf16[32,1024]{1,0:T(8,128)(2,1)} %param.9), channel_id=1, source_target_pairs={{0,8},{4,12},{8,0},{12,4},{1,9},{5,13},{9,1},{13,5},{2,10},{6,14},... | collective-permute-start | bytes 196616 | tf_op jit(solution)/shard_map/ppermute | solution.py:658
  6.4 5.9 %copy-start.1 = (bf16[32,1024]{1,0:T(8,128)(2,1)S(1)}, bf16[32,1024]{1,0:T(8,128)(2,1)}, u32[]{:S(2)}) copy-start(bf16[32,1024]{1,0:T(8,128)(2,1)} %param.9) | copy-start | bytes 196612
  14.6 2.3 %collective-permute-start.7 = (bf16[2,64,1792]{2,1,0:T(8,128)(2,1)S(1)}, bf16[2,64,1792]{2,1,0:T(8,128)(2,1)S(1)}, u32[]{:S(2)}, u32[]{:S(2)}) collective-permute-start(bf16[2,64,1792]{2,1,0:T(8,128)(2,1)S(1)} %get-tuple-element.43), channel_id=1, source_target_pairs={{0,1},{1,0},{2,3},{3,2},{4,5},{5,4},{6,7},{7,6},{8,9},{9,8},{10,11... | collective-permute-start | bytes 1376264 | tf_op jit(solution)/shard_map/ppermute | solution.py:16
  16.3 2.3 %collective-permute-start.3 = (bf16[2,64,1792]{2,1,0:T(8,128)(2,1)S(1)}, bf16[2,64,1792]{2,1,0:T(8,128)(2,1)S(1)}, u32[]{:S(2)}, u32[]{:S(2)}) collective-permute-start(bf16[2,64,1792]{2,1,0:T(8,128)(2,1)S(1)} %get-tuple-element.36), channel_id=1, source_target_pairs={{0,1},{1,0},{2,3},{3,2},{4,5},{5,4},{6,7},{7,6},{8,9},{9,8},{10,11... | collective-permute-start | bytes 1376264 | tf_op jit(solution)/shard_map/ppermute | solution.py:16
  17.0 9.4 %collective-permute-start.8 = (bf16[2,32,1792]{2,1,0:T(8,128)(2,1)S(1)}, bf16[2,32,1792]{2,1,0:T(8,128)(2,1)S(1)}, u32[]{:S(2)}, u32[]{:S(2)}) collective-permute-start(bf16[2,32,1792]{2,1,0:T(8,128)(2,1)S(1)} %slice.8), channel_id=1, source_target_pairs={{0,2},{2,0},{1,3},{3,1},{4,6},{6,4},{5,7},{7,5},{8,10},{10,8},{9,1... | collective-permute-start | bytes 688136 | tf_op jit(solution)/shard_map/ppermute | solution.py:16
  18.7 11.9 %collective-permute-start.11 = (bf16[2,32,1792]{2,1,0:T(8,128)(2,1)S(1)}, bf16[2,32,1792]{2,1,0:T(8,128)(2,1)S(1)}, u32[]{:S(2)}, u32[]{:S(2)}) collective-permute-start(bf16[2,32,1792]{2,1,0:T(8,128)(2,1)S(1)} %slice.9), channel_id=1, source_target_pairs={{0,2},{2,0},{1,3},{3,1},{4,6},{6,4},{5,7},{7,5},{8,10},{10,8},{9,1... | collective-permute-start | bytes 688136 | tf_op jit(solution)/shard_map/ppermute | solution.py:16
  20.1 22.1 %slice-start = ((s8[7340032]{0:T(1024)(128)(4,1)}), s8[4194304]{0:T(1024)(128)(4,1)S(1)}, s32[]{:S(2)}) async-start(s8[7340032]{0:T(1024)(128)(4,1)} %bitcast.11), calls=%async_computation | async-start | bytes 8388608
  26.3 8.7 %collective-permute-start.5 = (bf16[4,2,16,896]{3,2,1,0:T(8,128)(2,1)S(1)}, bf16[4,2,16,896]{3,2,1,0:T(8,128)(2,1)S(1)}, u32[]{:S(2)}, u32[]{:S(2)}) collective-permute-start(bf16[4,2,16,896]{3,2,1,0:T(8,128)(2,1)S(1)} %get-tuple-element.40), channel_id=1, source_target_pairs={{0,1},{1,0},{2,3},{3,2},{4,5},{5,4},{6,7},{7,6},{8,9},{9,8},{10,11... | collective-permute-start | bytes 688136 | tf_op jit(solution)/shard_map/ppermute | solution.py:16
  26.5 15.6 %slice-start.1 = ((s8[7340032]{0:T(1024)(128)(4,1)}), s8[3145728]{0:T(1024)(128)(4,1)S(1)}, s32[]{:S(2)}) async-start(s8[7340032]{0:T(1024)(128)(4,1)} %bitcast.11), calls=%async_computation.1 | async-start | bytes 6291456
  26.6 8.5 %collective-permute-start.9 = (bf16[32,1792]{1,0:T(8,128)(2,1)S(1)}, bf16[32,1792]{1,0:T(8,128)(2,1)S(1)}, u32[]{:S(2)}, u32[]{:S(2)}) collective-permute-start(bf16[32,1792]{1,0:T(8,128)(2,1)S(1)} %shard_map.126.refs_0_.before), channel_id=1, source_target_pairs={{0,2},{2,0},{1,3},{3,1},{4,6},{6,4},{5,7},{7,5},{8,10},{10,8},{9,1... | collective-permute-start | bytes 344072 | tf_op jit(solution)/shard_map/ppermute | solution.py:16
  30.7 3.1 %copy-start = (bf16[3584,1024]{1,0:T(8,128)(2,1)}, bf16[3584,1024]{1,0:T(8,128)(2,1)S(1)}, u32[]{:S(2)}) copy-start(bf16[3584,1024]{1,0:T(8,128)(2,1)S(1)} %shard_map.128.refs_2_) | copy-start | bytes 22020100
  33.8 5.4 %collective-permute-start.12 = (bf16[32,1792]{1,0:T(8,128)(2,1)S(1)}, bf16[32,1792]{1,0:T(8,128)(2,1)S(1)}, u32[]{:S(2)}, u32[]{:S(2)}) collective-permute-start(bf16[32,1792]{1,0:T(8,128)(2,1)S(1)} %shard_map.129.refs_0_), channel_id=1, source_target_pairs={{0,2},{2,0},{1,3},{3,1},{4,6},{6,4},{5,7},{7,5},{8,10},{10,8},{9,1... | collective-permute-start | bytes 344072 | tf_op jit(solution)/shard_map/ppermute | solution.py:16
  35.0 5.4 %collective-permute-start.4 = (bf16[4,2,16,896]{3,2,1,0:T(8,128)(2,1)S(1)}, bf16[4,2,16,896]{3,2,1,0:T(8,128)(2,1)S(1)}, u32[]{:S(2)}, u32[]{:S(2)}) collective-permute-start(bf16[4,2,16,896]{3,2,1,0:T(8,128)(2,1)S(1)} %get-tuple-element.38), channel_id=1, source_target_pairs={{0,1},{1,0},{2,3},{3,2},{4,5},{5,4},{6,7},{7,6},{8,9},{9,8},{10,11... | collective-permute-start | bytes 688136 | tf_op jit(solution)/shard_map/ppermute | solution.py:16
  35.1 6.4 %collective-permute-start.10 = (bf16[64,1792]{1,0:T(8,128)(2,1)S(1)}, bf16[64,1792]{1,0:T(8,128)(2,1)S(1)}, u32[]{:S(2)}, u32[]{:S(2)}) collective-permute-start(bf16[64,1792]{1,0:T(8,128)(2,1)S(1)} %shard_map.127.refs_0_), channel_id=1, source_target_pairs={{0,1},{1,0},{2,3},{3,2},{4,5},{5,4},{6,7},{7,6},{8,9},{9,8},{10,11... | collective-permute-start | bytes 688136 | tf_op jit(solution)/shard_map/ppermute | solution.py:16
  39.2 2.3 %collective-permute-start.13 = (bf16[64,1792]{1,0:T(8,128)(2,1)S(1)}, bf16[64,1792]{1,0:T(8,128)(2,1)S(1)}, u32[]{:S(2)}, u32[]{:S(2)}) collective-permute-start(bf16[64,1792]{1,0:T(8,128)(2,1)S(1)} %shard_map.130.refs_2_), channel_id=1, source_target_pairs={{0,1},{1,0},{2,3},{3,2},{4,5},{5,4},{6,7},{7,6},{8,9},{9,8},{10,11... | collective-permute-start | bytes 688136 | tf_op jit(solution)/shard_map/ppermute | solution.py:16
  39.3 8.5 %collective-permute-start.18 = (bf16[4,2,16,896]{3,2,1,0:T(8,128)(2,1)S(1)}, bf16[4,2,16,896]{3,2,1,0:T(8,128)(2,1)S(1)}, u32[]{:S(2)}, u32[]{:S(2)}) collective-permute-start(bf16[4,2,16,896]{3,2,1,0:T(8,128)(2,1)S(1)} %shard_map.123.before.refs_2_.mine), channel_id=1, source_target_pairs={{0,2},{2,0},{1,3},{3,1},{4,6},{6,4},{5,7},{7,5},{8,10},{10,8},{9,1... | collective-permute-start | bytes 688136 | tf_op jit(solution)/shard_map/ppermute | solution.py:16
  40.4 11.8 %collective-permute-start.6 = (bf16[4,2,16,896]{3,2,1,0:T(8,128)(2,1)S(1)}, bf16[4,2,16,896]{3,2,1,0:T(8,128)(2,1)S(1)}, u32[]{:S(2)}, u32[]{:S(2)}) collective-permute-start(bf16[4,2,16,896]{3,2,1,0:T(8,128)(2,1)S(1)} %shard_map.124.mine), channel_id=1, source_target_pairs={{0,2},{2,0},{1,3},{3,1},{4,6},{6,4},{5,7},{7,5},{8,10},{10,8},{9,1... | collective-permute-start | bytes 688136 | tf_op jit(solution)/shard_map/ppermute | solution.py:16
  43.4 6.5 %collective-permute-start.15 = (bf16[32,1024]{1,0:T(8,128)(2,1)S(1)}, bf16[32,1024]{1,0:T(8,128)(2,1)S(1)}, u32[]{:S(2)}, u32[]{:S(2)}) collective-permute-start(bf16[32,1024]{1,0:T(8,128)(2,1)S(1)} %get-tuple-element.62), channel_id=1, source_target_pairs={{0,12},{4,8},{8,4},{12,0},{1,13},{5,9},{9,5},{13,1},{2,14},{6,10},... | collective-permute-start | bytes 196616 | tf_op jit(solution)/shard_map/ppermute | solution.py:658
  45.9 4.7 %collective-permute-start.14 = (bf16[32,1024]{1,0:T(8,128)(2,1)S(1)}, bf16[32,1024]{1,0:T(8,128)(2,1)S(1)}, u32[]{:S(2)}, u32[]{:S(2)}) collective-permute-start(bf16[32,1024]{1,0:T(8,128)(2,1)S(1)} %get-tuple-element.63), channel_id=1, source_target_pairs={{0,4},{4,0},{8,12},{12,8},{1,5},{5,1},{9,13},{13,9},{2,6},{6,2},{1... | collective-permute-start | bytes 196616 | tf_op jit(solution)/shard_map/ppermute | solution.py:658
  50.6 1.8 %collective-permute-start.19 = (bf16[4,16,896]{2,1,0:T(8,128)(2,1)S(1)}, bf16[4,16,896]{2,1,0:T(8,128)(2,1)S(1)}, u32[]{:S(2)}, u32[]{:S(2)}) collective-permute-start(bf16[4,16,896]{2,1,0:T(8,128)(2,1)S(1)} %get-tuple-element.45.mine), channel_id=1, source_target_pairs={{0,1},{1,0},{2,3},{3,2},{4,5},{5,4},{6,7},{7,6},{8,9},{9,8},{10,11... | collective-permute-start | bytes 344072 | tf_op jit(solution)/shard_map/ppermute | solution.py:16
  50.8 19.6 %collective-permute-start.22 = (bf16[32,1024]{1,0:T(8,128)(2,1)S(1)}, bf16[32,1024]{1,0:T(8,128)(2,1)S(1)}, u32[]{:S(2)}, u32[]{:S(2)}) collective-permute-start(bf16[32,1024]{1,0:T(8,128)(2,1)S(1)} %get-tuple-element.60), channel_id=1, source_target_pairs={{0,8},{4,12},{8,0},{12,4},{1,9},{5,13},{9,1},{13,5},{2,10},{6,14},... | collective-permute-start | bytes 196616 | tf_op jit(solution)/shard_map/ppermute | solution.py:658
  52.3 7.9 %collective-permute-start.16 = (bf16[4,16,896]{2,1,0:T(8,128)(2,1)S(1)}, bf16[4,16,896]{2,1,0:T(8,128)(2,1)S(1)}, u32[]{:S(2)}, u32[]{:S(2)}) collective-permute-start(bf16[4,16,896]{2,1,0:T(8,128)(2,1)S(1)} %get-tuple-element.44.mine), channel_id=1, source_target_pairs={{0,1},{1,0},{2,3},{3,2},{4,5},{5,4},{6,7},{7,6},{8,9},{9,8},{10,11... | collective-permute-start | bytes 344072 | tf_op jit(solution)/shard_map/ppermute | solution.py:16
  57.4 13.0 %collective-permute-start.21 = (bf16[32,1024]{1,0:T(8,128)(2,1)S(1)}, bf16[32,1024]{1,0:T(8,128)(2,1)S(1)}, u32[]{:S(2)}, u32[]{:S(2)}) collective-permute-start(bf16[32,1024]{1,0:T(8,128)(2,1)S(1)} %get-tuple-element.64), channel_id=1, source_target_pairs={{0,12},{4,8},{8,4},{12,0},{1,13},{5,9},{9,5},{13,1},{2,14},{6,10},... | collective-permute-start | bytes 196616 | tf_op jit(solution)/shard_map/ppermute | solution.py:658
  59.9 10.5 %collective-permute-start.20 = (bf16[32,1024]{1,0:T(8,128)(2,1)S(1)}, bf16[32,1024]{1,0:T(8,128)(2,1)S(1)}, u32[]{:S(2)}, u32[]{:S(2)}) collective-permute-start(bf16[32,1024]{1,0:T(8,128)(2,1)S(1)} %get-tuple-element.65), channel_id=1, source_target_pairs={{0,8},{4,12},{8,0},{12,4},{1,9},{5,13},{9,1},{13,5},{2,10},{6,14},... | collective-permute-start | bytes 196616 | tf_op jit(solution)/shard_map/ppermute | solution.py:658
  65.2 5.3 %collective-permute-start.17 = (bf16[32,1024]{1,0:T(8,128)(2,1)S(1)}, bf16[32,1024]{1,0:T(8,128)(2,1)S(1)}, u32[]{:S(2)}, u32[]{:S(2)}) collective-permute-start(bf16[32,1024]{1,0:T(8,128)(2,1)S(1)} %get-tuple-element.66), channel_id=1, source_target_pairs={{0,4},{4,0},{8,12},{12,8},{1,5},{5,1},{9,13},{13,9},{2,6},{6,2},{1... | collective-permute-start | bytes 196616 | tf_op jit(solution)/shard_map/ppermute | solution.py:658
  70.5 8.7 %collective-permute-start.25 = (bf16[32,1024]{1,0:T(8,128)(2,1)S(1)}, bf16[32,1024]{1,0:T(8,128)(2,1)S(1)}, u32[]{:S(2)}, u32[]{:S(2)}) collective-permute-start(bf16[32,1024]{1,0:T(8,128)(2,1)S(1)} %get-tuple-element.48), channel_id=1, source_target_pairs={{0,12},{4,8},{8,4},{12,0},{1,13},{5,9},{9,5},{13,1},{2,14},{6,10},... | collective-permute-start | bytes 196616 | tf_op jit(solution)/shard_map/ppermute | solution.py:658
  73.0 6.1 %collective-permute-start.24 = (bf16[32,1024]{1,0:T(8,128)(2,1)S(1)}, bf16[32,1024]{1,0:T(8,128)(2,1)S(1)}, u32[]{:S(2)}, u32[]{:S(2)}) collective-permute-start(bf16[32,1024]{1,0:T(8,128)(2,1)S(1)} %get-tuple-element.48), channel_id=1, source_target_pairs={{0,8},{4,12},{8,0},{12,4},{1,9},{5,13},{9,1},{13,5},{2,10},{6,14},... | collective-permute-start | bytes 196616 | tf_op jit(solution)/shard_map/ppermute | solution.py:658
  73.0 4.6 %collective-permute-start.23 = (bf16[32,1024]{1,0:T(8,128)(2,1)S(1)}, bf16[32,1024]{1,0:T(8,128)(2,1)S(1)}, u32[]{:S(2)}, u32[]{:S(2)}) collective-permute-start(bf16[32,1024]{1,0:T(8,128)(2,1)S(1)} %get-tuple-element.48), channel_id=1, source_target_pairs={{0,4},{4,0},{8,12},{12,8},{1,5},{5,1},{9,13},{13,9},{2,6},{6,2},{1... | collective-permute-start | bytes 196616 | tf_op jit(solution)/shard_map/ppermute | solution.py:658
  80.7 2.0 %collective-permute-start.26 = (bf16[2,32,896]{2,1,0:T(8,128)(2,1)S(1)}, bf16[2,32,896]{2,1,0:T(8,128)(2,1)S(1)}, u32[]{:S(2)}, u32[]{:S(2)}) collective-permute-start(bf16[2,32,896]{2,1,0:T(8,128)(2,1)S(1)} %get-tuple-element.50), channel_id=1, source_target_pairs={{0,1},{1,0},{2,3},{3,2},{4,5},{5,4},{6,7},{7,6},{8,9},{9,8},{10,11... | collective-permute-start | bytes 344072 | tf_op jit(solution)/shard_map/ppermute | solution.py:16
  82.2 1.6 %collective-permute-start.28 = (bf16[2,32,896]{2,1,0:T(8,128)(2,1)S(1)}, bf16[2,32,896]{2,1,0:T(8,128)(2,1)S(1)}, u32[]{:S(2)}, u32[]{:S(2)}) collective-permute-start(bf16[2,32,896]{2,1,0:T(8,128)(2,1)S(1)} %get-tuple-element.53), channel_id=1, source_target_pairs={{0,1},{1,0},{2,3},{3,2},{4,5},{5,4},{6,7},{7,6},{8,9},{9,8},{10,11... | collective-permute-start | bytes 344072 | tf_op jit(solution)/shard_map/ppermute | solution.py:16
  82.8 6.1 %collective-permute-start.27 = (bf16[2,32,896]{2,1,0:T(8,128)(2,1)S(1)}, bf16[2,32,896]{2,1,0:T(8,128)(2,1)S(1)}, u32[]{:S(2)}, u32[]{:S(2)}) collective-permute-start(bf16[2,32,896]{2,1,0:T(8,128)(2,1)S(1)} %add_convert_fusion.3.mine), channel_id=1, source_target_pairs={{0,2},{2,0},{1,3},{3,1},{4,6},{6,4},{5,7},{7,5},{8,10},{10,8},{9,1... | collective-permute-start | bytes 344072 | tf_op jit(solution)/shard_map/ppermute | solution.py:16
  83.8 6.5 %collective-permute-start.30 = (bf16[2,32,896]{2,1,0:T(8,128)(2,1)S(1)}, bf16[2,32,896]{2,1,0:T(8,128)(2,1)S(1)}, u32[]{:S(2)}, u32[]{:S(2)}) collective-permute-start(bf16[2,32,896]{2,1,0:T(8,128)(2,1)S(1)} %add_convert_fusion.2.before.mine), channel_id=1, source_target_pairs={{0,2},{2,0},{1,3},{3,1},{4,6},{6,4},{5,7},{7,5},{8,10},{10,8},{9,1... | collective-permute-start | bytes 344072 | tf_op jit(solution)/shard_map/ppermute | solution.py:16
  89.0 2.2 %collective-permute-start.29 = (bf16[2,2,32,896]{3,2,1,0:T(8,128)(2,1)S(1)}, bf16[2,2,32,896]{3,2,1,0:T(8,128)(2,1)S(1)}, u32[]{:S(2)}, u32[]{:S(2)}) collective-permute-start(bf16[2,2,32,896]{3,2,1,0:T(8,128)(2,1)S(1)} %shard_map.142.rest_0_), channel_id=1, source_target_pairs={{0,1},{1,0},{2,3},{3,2},{4,5},{5,4},{6,7},{7,6},{8,9},{9,8},{10,11... | collective-permute-start | bytes 688136 | tf_op jit(solution)/shard_map/ppermute | solution.py:16
  90.5 1.6 %collective-permute-start.31 = (bf16[2,2,32,896]{3,2,1,0:T(8,128)(2,1)S(1)}, bf16[2,2,32,896]{3,2,1,0:T(8,128)(2,1)S(1)}, u32[]{:S(2)}, u32[]{:S(2)}) collective-permute-start(bf16[2,2,32,896]{3,2,1,0:T(8,128)(2,1)S(1)} %shard_map.143.rest_2_), channel_id=1, source_target_pairs={{0,1},{1,0},{2,3},{3,2},{4,5},{5,4},{6,7},{7,6},{8,9},{9,8},{10,11... | collective-permute-start | bytes 688136 | tf_op jit(solution)/shard_map/ppermute | solution.py:16

commit v14 on v12

--- a/solution.py
+++ b/solution.py
@@ -151,6 +151,22 @@
     )(place, far(routes), far(shares), far(gate), far(up))
 
 
+def load_kernel(source, before, out, sems):
+    for copy in load_start(((source, out),), sems, 8):
+        copy.wait()
+
+
+def load(source, before):
+    return pl.pallas_call(
+        load_kernel,
+        in_specs=[in_hbm(), anywhere()],
+        out_specs=whole(),
+        out_shape=pltpu.VMEM(source.shape, source.dtype),
+        scratch_shapes=[pltpu.SemaphoreType.DMA((1, 8))],
+        compiler_params=pltpu.CompilerParams(vmem_limit_bytes=4 * 1024 * 1024),
+    )(far(source), before)
+
+
 def residual_kernel(ranks, *refs):
     student = refs[0][...].astype(F32)
     target = refs[ranks][...].astype(F32)
@@ -682,24 +698,25 @@
     target = to_owners(product, 0, ranks, 0)
 
     pre, dense, student = [], [], []
-    wait = [target[1], target[-1]]
+    expert_near = load(expert_down, product)
+    wait = [target[1], target[-1], expert_near]
     for (mine, other, mode), cut, rows in zip(parts, cuts, token_cuts):
         total, part = hidden_act(mine, other, mode, slot_weight, wait, cut[0])
         pre.append(total)
         dense.append(spread(picker, part, shift(part, "pipe", pipes, 1), cut, rows))
-        wait = dense[-1:]
-        product = jnp.dot(dense[-1], expert_down, preferred_element_type=F32).astype(BF)
+        product = jnp.dot(dense[-1], expert_near, preferred_element_type=F32).astype(BF)
         count = (rows[1] - rows[0]) // block
         student = to_owners(product, rows[0] // block, count, rows[0]) + student
     dense_flipped, base_flipped = flip(dense[::-1], base, product)
-    student_sum, residual = residual_of(student, target, (base_flipped,))
+    expert_near = load(expert_down, base_flipped)
+    student_sum, residual = residual_of(student, target, (expert_near,))
 
     _, residual = gather_tokens(residual)
     group = 2 if experts % 2 == 0 else 1
     firsts = range(0, experts, group)
     sums, last = [], residual
     for first in firsts:
-        keep, send = hidden_grad_parts(picker, residual, expert_down, last, first, group)
+        keep, send = hidden_grad_parts(picker, residual, expert_near, last, first, group)
         last = keep
         sums.append(add(keep, shift(send, "pipe", pipes, 1)))
     exchanged = [exchange_dp(value, dps, near_first) for value in sums]

time: 93.7 us -> 95.9 us (1.023)
  local copies, waits for them, and re-layouts: 0.25 us -> 8.62 us
  matrix products: 10.4 us -> 3.89 us
  Pallas kernels: 31.2 us -> 37.3 us
  waiting for transfers between devices: 19.1 us -> 13.4 us
    unnamed x10 -> x12, local copies, waits for them, and re-layouts: 0.02 us -> 8.4 us
    dot_general x2, matrix products: 9.24 us -> 2.77 us  [body(): jnp.dot(dense[-1], expert_near, preferred_element_type=F32).astype(BF)]
    pallas_call x0 -> x2, Pallas kernels: none -> 6.34 us  [load(): pl.pallas_call(load_kernel, in_specs=[in_hbm(), anywhere()], out_specs=wh...]
    ppermute x12, waiting for transfers between devices: 9.38 us -> 5.79 us  [to_partner(): return lax.ppermute(value, 'expert', [(i, i ^ s) for i in range(ranks)])]
    ppermute x20, waiting for transfers between devices: 9.74 us -> 7.62 us  [shift(): lax.ppermute(value, axis, [(i, (i + by) % count) for i in range(count)])]
  transfers between devices with their start and end apart: 32 -> 32, of which waited for: 14 -> 12; matrix products, arithmetic and copies ran while one was open for 13% -> 6% of each run, Pallas kernels for 23% -> 29%
where the time goes in v14:
time: 95.9 us; the launch traced here: 95.7 us
  Pallas kernels  37.3 us (39%)
  starting transfers between devices  30 us (31%)
  waiting for transfers between devices  13.4 us (14%)
  local copies, waits for them, and re-layouts  8.62 us (9%)
  matrix products  3.89 us (4%)
  between operations  1.27 us (1%)
  other arithmetic  1.23 us (1%)
    ppermute x12, starting transfers between devices, to_partner(): return lax.ppermute(value, 'expert', [(i, i ^ s) for i in range(ranks)])  18.2 us
    ppermute x20, starting transfers between devices, shift(): lax.ppermute(value, axis, [(i, (i + by) % count) for i in range(count)])  11.8 us
    unnamed x12, local copies, waits for them, and re-layouts  8.4 us
    ppermute x20, waiting for transfers between devices, shift(): lax.ppermute(value, axis, [(i, (i + by) % count) for i in range(count)])  7.62 us
    pallas_call x1, Pallas kernels, expert_pre(): pl.pallas_call(functools.partial(expert_kernel, cuts), in_specs=[whole(),...  6.57 us
    pallas_call x1, Pallas kernels, input_grads(): pl.pallas_call(functools.partial(input_grad_kernel, count // len(parts)),...  6.48 us
    pallas_call x2, Pallas kernels, load(): pl.pallas_call(load_kernel, in_specs=[in_hbm(), anywhere()], out_specs=wh...  6.34 us
    pallas_call x1, Pallas kernels, prepare(): pl.pallas_call(functools.partial(prepare_kernel, near_first, ranks, capac...  5.89 us
  transfers between devices with their start and end apart: 32, of which 12 were waited for; matrix products, arithmetic and copies ran while one was open for 6% of the time, Pallas kernels for 29%

profile of v14, /device:TPU:0, one launch (start us, length us, event | category | flops | bytes accessed | tf_op | source)
XLA Modules:
  0.0 95.7 jit_solution(11452086333817358293)
XLA Ops:
  0.6 3.1 %collective-permute-start = (bf16[32,1024]{1,0:T(8,128)(2,1)}, bf16[32,1024]{1,0:T(8,128)(2,1)S(1)}, u32[]{:S(2)}, u32[]{:S(2)}) collective-permute-start(bf16[32,1024]{1,0:T(8,128)(2,1)} %param.9), channel_id=1, source_target_pairs={{0,4},{4,0},{8,12},{12,8},{1,5},{5,1},{9,13},{13,9},{2,6},{6,2},{1... | collective-permute-start | bytes 196616 | tf_op jit(solution)/shard_map/ppermute | solution.py:633
  3.7 2.5 %collective-permute-start.2 = (bf16[32,1024]{1,0:T(8,128)(2,1)}, bf16[32,1024]{1,0:T(8,128)(2,1)S(1)}, u32[]{:S(2)}, u32[]{:S(2)}) collective-permute-start(bf16[32,1024]{1,0:T(8,128)(2,1)} %param.9), channel_id=1, source_target_pairs={{0,12},{4,8},{8,4},{12,0},{1,13},{5,9},{9,5},{13,1},{2,14},{6,10},... | collective-permute-start | bytes 196616 | tf_op jit(solution)/shard_map/ppermute | solution.py:633
  6.2 0.1 collective-permute-start.1
  6.3 0.1 pad_add_fusion.place
  6.4 5.9 %shard_map.120 = (bf16[4,64,128]{2,1,0:T(8,128)(2,1)S(1)}, f32[4,64,1]{2,1,0:T(8,128)S(1)}, bf16[1024,3584]{1,0:T(8,128)(2,1)S(1)}, bf16[1024,3584]{1,0:T(8,128)(2,1)S(1)}) custom-call(s32[3]{0:T(128)S(1)} %pad_add_fusion.place, s32[4,128]{1,0:T(4,128)} %bitcast.33, f32[4,128]{1,0:T(4,128)} %bitcast.34, bf16[1024,3584]{1,0:T(8,128)(2,1)} %gate.2, ...), custom_call_target="tpu_custom_call" | custom-call | bytes 14680064 | tf_op jit(solution)/shard_map/pallas_call | solution.py:131
  12.4 0.5 collective-permute-done.1
  12.9 1.7 %shard_map.125 = (bf16[2,64,1792]{2,1,0:T(8,128)(2,1)S(1)}, bf16[2,64,1792]{2,1,0:T(8,128)(2,1)S(1)}) custom-call(s32[3]{0:T(128)S(1)} %pad_add_fusion.place, bf16[128,1024]{1,0:T(8,128)(2,1)S(1)} %constant_dynamic-update-slice_fusion.4.tokens.refs_2_, bf16[1024,3584]{1,0:T(8,128)(2,1)S(1)} %get-tuple-element.33.gate, ...), custom_call_target="tpu_custom_call" | custom-call | flops 939524096 | bytes 7340032 | tf_op jit(solution)/shard_map/pallas_call | solution.py:217
  14.7 1.7 %shard_map.121 = (bf16[2,64,1792]{2,1,0:T(8,128)(2,1)S(1)}, bf16[2,64,1792]{2,1,0:T(8,128)(2,1)S(1)}) custom-call(s32[3]{0:T(128)S(1)} %pad_add_fusion.place, bf16[128,1024]{1,0:T(8,128)(2,1)S(1)} %constant_dynamic-update-slice_fusion.4.tokens.refs_2_, bf16[1024,3584]{1,0:T(8,128)(2,1)S(1)} %get-tuple-element.33.gate, ...), custom_call_target="tpu_custom_call" | custom-call | flops 939524096 | bytes 7340032 | tf_op jit(solution)/shard_map/pallas_call | solution.py:217
  16.3 0.6 collective-permute-start.3
  16.9 0.1 add_convert_fusion
  17.0 1.6 %collective-permute-start.8 = (bf16[2,32,1792]{2,1,0:T(8,128)(2,1)S(1)}, bf16[2,32,1792]{2,1,0:T(8,128)(2,1)S(1)}, u32[]{:S(2)}, u32[]{:S(2)}) collective-permute-start(bf16[2,32,1792]{2,1,0:T(8,128)(2,1)S(1)} %slice.33), channel_id=1, source_target_pairs={{0,2},{2,0},{1,3},{3,1},{4,6},{6,4},{5,7},{7,5},{8,10},{10,8},{9,1... | collective-permute-start | bytes 688136 | tf_op jit(solution)/shard_map/ppermute | solution.py:16
  18.6 0.1 add_convert_fusion.1.before
  18.7 1.3 %collective-permute-start.11 = (bf16[2,32,1792]{2,1,0:T(8,128)(2,1)S(1)}, bf16[2,32,1792]{2,1,0:T(8,128)(2,1)S(1)}, u32[]{:S(2)}, u32[]{:S(2)}) collective-permute-start(bf16[2,32,1792]{2,1,0:T(8,128)(2,1)S(1)} %slice.37), channel_id=1, source_target_pairs={{0,2},{2,0},{1,3},{3,1},{4,6},{6,4},{5,7},{7,5},{8,10},{10,8},{9,1... | collective-permute-start | bytes 688136 | tf_op jit(solution)/shard_map/ppermute | solution.py:16
  20.1 6.6 %shard_map.122 = (bf16[4,2,16,896]{3,2,1,0:T(8,128)(2,1)S(1)}, bf16[4,2,16,896]{3,2,1,0:T(8,128)(2,1)S(1)}, bf16[4,2,16,896]{3,2,1,0:T(8,128)(2,1)S(1)}, bf16[4,2,16,896]{3,2,1,0:T(8,128)(2,1)S(1)}) custom-call(bf16[4,64,128]{2,1,0:T(8,128)(2,1)S(1)} %get-tuple-element.32.picker, bf16[128,1024]{1,0:T(8,128)(2,1)S(1)} %constant_dynamic-update-slice_fusion.4.tokens.refs_2_, ...), custom_call_target="tpu_custom_call" | custom-call | flops 939524096 | bytes 14680064 | tf_op jit(solution)/shard_map/pallas_call | solution.py:273
  26.6 0.1 collective-permute-start.5
  26.9 0.8 collective-permute-start.9
  27.7 1.9 %collective-permute-done.11 = bf16[2,32,1792]{2,1,0:T(8,128)(2,1)S(1)} collective-permute-done((bf16[2,32,1792]{2,1,0:T(8,128)(2,1)S(1)}, bf16[2,32,1792]{2,1,0:T(8,128)(2,1)S(1)}, u32[]{:S(2)}, u32[]{:S(2)}) %collective-permute-start.11) | collective-permute-done | bytes 229408 | tf_op jit(solution)/shard_map/ppermute | solution.py:16
  29.6 0.1 fusion.1.refs_0_
  29.7 1.8 %collective-permute-start.12 = (bf16[32,1792]{1,0:T(8,128)(2,1)S(1)}, bf16[32,1792]{1,0:T(8,128)(2,1)S(1)}, u32[]{:S(2)}, u32[]{:S(2)}) collective-permute-start(bf16[32,1792]{1,0:T(8,128)(2,1)S(1)} %fusion.1.refs_0_), channel_id=1, source_target_pairs={{0,2},{2,0},{1,3},{3,1},{4,6},{6,4},{5,7},{7,5},{8,10},{10,8},{9,1... | collective-permute-start | bytes 344072 | tf_op jit(solution)/shard_map/ppermute | solution.py:16
  31.5 1.4 %collective-permute-done.9.refs_1_ = bf16[32,1792]{1,0:T(8,128)(2,1)S(1)} collective-permute-done((bf16[32,1792]{1,0:T(8,128)(2,1)S(1)}, bf16[32,1792]{1,0:T(8,128)(2,1)S(1)}, u32[]{:S(2)}, u32[]{:S(2)}) %collective-permute-start.9) | collective-permute-done | bytes 114720 | tf_op jit(solution)/shard_map/ppermute | solution.py:16
  33.0 1.9 %collective-permute-done.12.refs_1_ = bf16[32,1792]{1,0:T(8,128)(2,1)S(1)} collective-permute-done((bf16[32,1792]{1,0:T(8,128)(2,1)S(1)}, bf16[32,1792]{1,0:T(8,128)(2,1)S(1)}, u32[]{:S(2)}, u32[]{:S(2)}) %collective-permute-start.12) | collective-permute-done | bytes 114720 | tf_op jit(solution)/shard_map/ppermute | solution.py:16
  35.0 1.4 %collective-permute-start.18 = (bf16[4,2,16,896]{3,2,1,0:T(8,128)(2,1)S(1)}, bf16[4,2,16,896]{3,2,1,0:T(8,128)(2,1)S(1)}, u32[]{:S(2)}, u32[]{:S(2)}) collective-permute-start(bf16[4,2,16,896]{3,2,1,0:T(8,128)(2,1)S(1)} %shard_map.123.before.refs_2_.mine), channel_id=1, source_target_pairs={{0,2},{2,0},{1,3},{3,1},{4,6},{6,4},{5,7},{7,5},{8,10},{10,8},{9,1... | collective-permute-start | bytes 688136 | tf_op jit(solution)/shard_map/ppermute | solution.py:16
  36.5 0.8 collective-permute-start.6
  37.3 0.6 shard_map.128
  37.9 1.1 %convolution_convert_fusion.before = bf16[128,1024]{1,0:T(8,128)(2,1)S(1)} fusion(bf16[128,3584]{1,0:T(8,128)(2,1)S(1)} %shard_map.128, bf16[3584,1024]{1,0:T(8,128)(2,1)S(1)} %bitcast.32), kind=kOutput, calls=%fused_computation | convolution fusion | flops 939655168 | bytes 8519680 | tf_op jit(solution)/shard_map/dot_general | solution.py:697
  39.1 2.5 %collective-permute-start.15 = (bf16[32,1024]{1,0:T(8,128)(2,1)S(1)}, bf16[32,1024]{1,0:T(8,128)(2,1)S(1)}, u32[]{:S(2)}, u32[]{:S(2)}) collective-permute-start(bf16[32,1024]{1,0:T(8,128)(2,1)S(1)} %get-tuple-element.62), channel_id=1, source_target_pairs={{0,12},{4,8},{8,4},{12,0},{1,13},{5,9},{9,5},{13,1},{2,14},{6,10},... | collective-permute-start | bytes 196616 | tf_op jit(solution)/shard_map/ppermute | solution.py:633
  41.6 0.5 collective-permute-start.14
  42.0 3.2 %shard_map.129.rest_2_ = bf16[3584,1024]{1,0:T(8,128)(2,1)S(1)} custom-call(bf16[3584,1024]{1,0:T(8,128)(2,1)} %source.3, bf16[128,1024]{1,0:T(8,128)(2,1)S(1)} %convolution_convert_fusion.before), custom_call_target="tpu_custom_call" | custom-call | tf_op jit(solution)/shard_map/pallas_call | solution.py:160
  45.2 0.3 collective-permute-done.15.rest_1_.refs_7_
  45.6 0.7 collective-permute-done.14.rest_0_.refs_5_
  46.3 0.1 shard_map.132
  46.4 3.0 %copy-done = bf16[3584,1024]{1,0:T(8,128)(2,1)} copy-done((bf16[3584,1024]{1,0:T(8,128)(2,1)}, bf16[3584,1024]{1,0:T(8,128)(2,1)S(1)}, u32[]{:S(2)}) %copy-start) | copy-done | bytes 7340056
  49.4 0.5 collective-permute-start.22
  50.0 3.1 %copy-done.1 = bf16[3584,1024]{1,0:T(8,128)(2,1)S(1)} copy-done((bf16[3584,1024]{1,0:T(8,128)(2,1)S(1)}, bf16[3584,1024]{1,0:T(8,128)(2,1)}, u32[]{:S(2)}) %copy-start.1) | copy-done | bytes 7340056
  53.0 0.1 shard_map.130
  53.1 0.3 collective-permute-start.16
  53.4 0.4 shard_map.133.refs_1_
  53.9 2.3 %copy-done.2 = bf16[3584,1024]{1,0:T(8,128)(2,1)S(1)} copy-done((bf16[3584,1024]{1,0:T(8,128)(2,1)S(1)}, bf16[3584,1024]{1,0:T(8,128)(2,1)}, u32[]{:S(2)}) %copy-start.2) | copy-done | bytes 7340056
  56.1 1.4 %convolution_convert_fusion.1 = bf16[64,1024]{1,0:T(8,128)(2,1)S(1)} fusion(bf16[64,3584]{1,0:T(8,128)(2,1)S(1)} %shard_map.133.refs_1_, bf16[3584,1024]{1,0:T(8,128)(2,1)S(1)} %copy-done.2), kind=kOutput, calls=%fused_computation.1 | convolution fusion | flops 469827584 | bytes 7929856 | tf_op jit(solution)/shard_map/dot_general | solution.py:707
  57.5 2.5 %collective-permute-start.21 = (bf16[32,1024]{1,0:T(8,128)(2,1)S(1)}, bf16[32,1024]{1,0:T(8,128)(2,1)S(1)}, u32[]{:S(2)}, u32[]{:S(2)}) collective-permute-start(bf16[32,1024]{1,0:T(8,128)(2,1)S(1)} %get-tuple-element.64), channel_id=1, source_target_pairs={{0,12},{4,8},{8,4},{12,0},{1,13},{5,9},{9,5},{13,1},{2,14},{6,10},... | collective-permute-start | bytes 196616 | tf_op jit(solution)/shard_map/ppermute | solution.py:633
  60.1 0.8 collective-permute-start.20
  60.9 0.4 shard_map.131.refs_0_
  61.3 1.4 %convolution_convert_fusion.2.refs_3_ = bf16[64,1024]{1,0:T(8,128)(2,1)S(1)} fusion(bf16[64,3584]{1,0:T(8,128)(2,1)S(1)} %shard_map.131.refs_0_, bf16[3584,1024]{1,0:T(8,128)(2,1)S(1)} %copy-done.2), kind=kOutput, calls=%fused_computation.2 | convolution fusion | flops 469827584 | bytes 7929856 | tf_op jit(solution)/shard_map/dot_general | solution.py:707
  62.7 1.2 %collective-permute-start.17 = (bf16[32,1024]{1,0:T(8,128)(2,1)S(1)}, bf16[32,1024]{1,0:T(8,128)(2,1)S(1)}, u32[]{:S(2)}, u32[]{:S(2)}) collective-permute-start(bf16[32,1024]{1,0:T(8,128)(2,1)S(1)} %get-tuple-element.66), channel_id=1, source_target_pairs={{0,4},{4,0},{8,12},{12,8},{1,5},{5,1},{9,13},{13,9},{2,6},{6,2},{1... | collective-permute-start | bytes 196616 | tf_op jit(solution)/shard_map/ppermute | solution.py:633
  63.9 0.4 shard_map.134
  64.3 3.2 %shard_map.135.refs_8_.down = bf16[3584,1024]{1,0:T(8,128)(2,1)S(1)} custom-call(bf16[3584,1024]{1,0:T(8,128)(2,1)} %source.3, bf16[1024,128]{1,0:T(8,128)(2,1)S(1)} %get-tuple-element.46.before.tokens), custom_call_target="tpu_custom_call" | custom-call | tf_op jit(solution)/shard_map/pallas_call | solution.py:160
  67.5 0.4 collective-permute-done.17.refs_1_
  68.0 2.2 %collective-permute-start.25 = (bf16[32,1024]{1,0:T(8,128)(2,1)S(1)}, bf16[32,1024]{1,0:T(8,128)(2,1)S(1)}, u32[]{:S(2)}, u32[]{:S(2)}) collective-permute-start(bf16[32,1024]{1,0:T(8,128)(2,1)S(1)} %get-tuple-element.48), channel_id=1, source_target_pairs={{0,12},{4,8},{8,4},{12,0},{1,13},{5,9},{9,5},{13,1},{2,14},{6,10},... | collective-permute-start | bytes 196616 | tf_op jit(solution)/shard_map/ppermute | solution.py:633
  70.2 2.2 %collective-permute-start.23 = (bf16[32,1024]{1,0:T(8,128)(2,1)S(1)}, bf16[32,1024]{1,0:T(8,128)(2,1)S(1)}, u32[]{:S(2)}, u32[]{:S(2)}) collective-permute-start(bf16[32,1024]{1,0:T(8,128)(2,1)S(1)} %get-tuple-element.48), channel_id=1, source_target_pairs={{0,4},{4,0},{8,12},{12,8},{1,5},{5,1},{9,13},{13,9},{2,6},{6,2},{1... | collective-permute-start | bytes 196616 | tf_op jit(solution)/shard_map/ppermute | solution.py:633
  72.5 2.7 %collective-permute-done.23 = bf16[32,1024]{1,0:T(8,128)(2,1)S(1)} collective-permute-done((bf16[32,1024]{1,0:T(8,128)(2,1)S(1)}, bf16[32,1024]{1,0:T(8,128)(2,1)S(1)}, u32[]{:S(2)}, u32[]{:S(2)}) %collective-permute-start.23) | collective-permute-done | bytes 65568 | tf_op jit(solution)/shard_map/ppermute | solution.py:633
  75.2 1.1 %collective-permute-done.24 = bf16[32,1024]{1,0:T(8,128)(2,1)S(1)} collective-permute-done((bf16[32,1024]{1,0:T(8,128)(2,1)S(1)}, bf16[32,1024]{1,0:T(8,128)(2,1)S(1)}, u32[]{:S(2)}, u32[]{:S(2)}) %collective-permute-start.24) | collective-permute-done | bytes 65568 | tf_op jit(solution)/shard_map/ppermute | solution.py:633
  76.4 1.4 %shard_map.137 = (bf16[2,32,896]{2,1,0:T(8,128)(2,1)S(1)}, bf16[2,32,896]{2,1,0:T(8,128)(2,1)S(1)}) custom-call(bf16[4,64,128]{2,1,0:T(8,128)(2,1)S(1)} %get-tuple-element.32.picker, bf16[128,1024]{1,0:T(8,128)(2,1)S(1)} %constant_dynamic-update-slice_fusion.residual.before, bf16[3584,1024]{1,0:T(8,128)(2,1)S(1)} %shard_map.135.refs_8_.down, ...), custom_call_target="tpu_custom_call" | custom-call | tf_op jit(solution)/shard_map/pallas_call | solution.py:444
  77.8 1.4 %shard_map.138 = (bf16[2,32,896]{2,1,0:T(8,128)(2,1)S(1)}, bf16[2,32,896]{2,1,0:T(8,128)(2,1)S(1)}) custom-call(bf16[4,64,128]{2,1,0:T(8,128)(2,1)S(1)} %get-tuple-element.32.picker, bf16[128,1024]{1,0:T(8,128)(2,1)S(1)} %constant_dynamic-update-slice_fusion.residual.before, bf16[3584,1024]{1,0:T(8,128)(2,1)S(1)} %shard_map.135.refs_8_.down, ...), custom_call_target="tpu_custom_call" | custom-call | tf_op jit(solution)/shard_map/pallas_call | solution.py:444
  79.2 0.6 collective-permute-start.28
  79.8 1.4 %collective-permute-start.27 = (bf16[2,32,896]{2,1,0:T(8,128)(2,1)S(1)}, bf16[2,32,896]{2,1,0:T(8,128)(2,1)S(1)}, u32[]{:S(2)}, u32[]{:S(2)}) collective-permute-start(bf16[2,32,896]{2,1,0:T(8,128)(2,1)S(1)} %add_convert_fusion.3.mine), channel_id=1, source_target_pairs={{0,2},{2,0},{1,3},{3,1},{4,6},{6,4},{5,7},{7,5},{8,10},{10,8},{9,1... | collective-permute-start | bytes 344072 | tf_op jit(solution)/shard_map/ppermute | solution.py:16
  81.2 0.9 collective-permute-start.30
  82.1 3.4 %shard_map.139 = (bf16[3584,1024]{1,0:T(8,128)(2,1)}, f32[8,128]{1,0:T(8,128)S(1)}) custom-call(bf16[3584,128]{1,0:T(8,128)(2,1)S(1)} %get-tuple-element.51.hidden, bf16[128,1024]{1,0:T(8,128)(2,1)S(1)} %constant_dynamic-update-slice_fusion.residual.before, bf16[2,32,896]{2,1,0:T(8,128)(2,1)S(1)} %add_convert_fusion.2.before.mine), custom_call_target="tpu_custom_call" | custom-call | flops 939524096 | bytes 7340032 | tf_op jit(solution)/shard_map/pallas_call | solution.py:496
  85.6 0.3 collective-permute-done.27.other
  85.9 0.2 shard_map.140.rest_0_
  86.1 1.3 %collective-permute-done.30.other = bf16[2,32,896]{2,1,0:T(8,128)(2,1)S(1)} collective-permute-done((bf16[2,32,896]{2,1,0:T(8,128)(2,1)S(1)}, bf16[2,32,896]{2,1,0:T(8,128)(2,1)S(1)}, u32[]{:S(2)}, u32[]{:S(2)}) %collective-permute-start.30) | collective-permute-done | bytes 114720 | tf_op jit(solution)/shard_map/ppermute | solution.py:16
  87.4 0.2 shard_map.141.rest_2_
  87.6 0.6 convert_element_type.81
  88.3 0.8 collective-permute-done.31.rest_3_
  89.1 6.5 %shard_map.142 = (bf16[1024,3584]{1,0:T(8,128)(2,1)}, bf16[1024,3584]{1,0:T(8,128)(2,1)}) custom-call(bf16[4,64,128]{2,1,0:T(8,128)(2,1)S(1)} %get-tuple-element.32.picker, bf16[1024,128]{1,0:T(8,128)(2,1)S(1)} %get-tuple-element.46.before.tokens, bf16[2,2,32,896]{3,2,1,0:T(8,128)(2,1)S(1)} %shard_map.140.rest_0_, ...), custom_call_target="tpu_custom_call" | custom-call | flops 1879048192 | bytes 14680064 | tf_op jit(solution)/shard_map/pallas_call | solution.py:546
  (64 shorter events, 1.2 us)
Async XLA Ops:
  0.6 11.7 %collective-permute-start = (bf16[32,1024]{1,0:T(8,128)(2,1)}, bf16[32,1024]{1,0:T(8,128)(2,1)S(1)}, u32[]{:S(2)}, u32[]{:S(2)}) collective-permute-start(bf16[32,1024]{1,0:T(8,128)(2,1)} %param.9), channel_id=1, source_target_pairs={{0,4},{4,0},{8,12},{12,8},{1,5},{5,1},{9,13},{13,9},{2,6},{6,2},{1... | collective-permute-start | bytes 196616 | tf_op jit(solution)/shard_map/ppermute | solution.py:633
  3.7 9.2 %collective-permute-start.2 = (bf16[32,1024]{1,0:T(8,128)(2,1)}, bf16[32,1024]{1,0:T(8,128)(2,1)S(1)}, u32[]{:S(2)}, u32[]{:S(2)}) collective-permute-start(bf16[32,1024]{1,0:T(8,128)(2,1)} %param.9), channel_id=1, source_target_pairs={{0,12},{4,8},{8,4},{12,0},{1,13},{5,9},{9,5},{13,1},{2,14},{6,10},... | collective-permute-start | bytes 196616 | tf_op jit(solution)/shard_map/ppermute | solution.py:633
  6.2 6.7 %collective-permute-start.1 = (bf16[32,1024]{1,0:T(8,128)(2,1)}, bf16[32,1024]{1,0:T(8,128)(2,1)S(1)}, u32[]{:S(2)}, u32[]{:S(2)}) collective-permute-start(bf16[32,1024]{1,0:T(8,128)(2,1)} %param.9), channel_id=1, source_target_pairs={{0,8},{4,12},{8,0},{12,4},{1,9},{5,13},{9,1},{13,5},{2,10},{6,14},... | collective-permute-start | bytes 196616 | tf_op jit(solution)/shard_map/ppermute | solution.py:633
  6.4 5.9 %copy-start.3 = (bf16[32,1024]{1,0:T(8,128)(2,1)S(1)}, bf16[32,1024]{1,0:T(8,128)(2,1)}, u32[]{:S(2)}) copy-start(bf16[32,1024]{1,0:T(8,128)(2,1)} %param.9) | copy-start | bytes 196612
  14.6 2.3 %collective-permute-start.7 = (bf16[2,64,1792]{2,1,0:T(8,128)(2,1)S(1)}, bf16[2,64,1792]{2,1,0:T(8,128)(2,1)S(1)}, u32[]{:S(2)}, u32[]{:S(2)}) collective-permute-start(bf16[2,64,1792]{2,1,0:T(8,128)(2,1)S(1)} %get-tuple-element.43), channel_id=1, source_target_pairs={{0,1},{1,0},{2,3},{3,2},{4,5},{5,4},{6,7},{7,6},{8,9},{9,8},{10,11... | collective-permute-start | bytes 1376264 | tf_op jit(solution)/shard_map/ppermute | solution.py:16
  16.3 2.3 %collective-permute-start.3 = (bf16[2,64,1792]{2,1,0:T(8,128)(2,1)S(1)}, bf16[2,64,1792]{2,1,0:T(8,128)(2,1)S(1)}, u32[]{:S(2)}, u32[]{:S(2)}) collective-permute-start(bf16[2,64,1792]{2,1,0:T(8,128)(2,1)S(1)} %get-tuple-element.36), channel_id=1, source_target_pairs={{0,1},{1,0},{2,3},{3,2},{4,5},{5,4},{6,7},{7,6},{8,9},{9,8},{10,11... | collective-permute-start | bytes 1376264 | tf_op jit(solution)/shard_map/ppermute | solution.py:16
  17.0 9.7 %collective-permute-start.8 = (bf16[2,32,1792]{2,1,0:T(8,128)(2,1)S(1)}, bf16[2,32,1792]{2,1,0:T(8,128)(2,1)S(1)}, u32[]{:S(2)}, u32[]{:S(2)}) collective-permute-start(bf16[2,32,1792]{2,1,0:T(8,128)(2,1)S(1)} %slice.33), channel_id=1, source_target_pairs={{0,2},{2,0},{1,3},{3,1},{4,6},{6,4},{5,7},{7,5},{8,10},{10,8},{9,1... | collective-permute-start | bytes 688136 | tf_op jit(solution)/shard_map/ppermute | solution.py:16
  18.7 10.8 %collective-permute-start.11 = (bf16[2,32,1792]{2,1,0:T(8,128)(2,1)S(1)}, bf16[2,32,1792]{2,1,0:T(8,128)(2,1)S(1)}, u32[]{:S(2)}, u32[]{:S(2)}) collective-permute-start(bf16[2,32,1792]{2,1,0:T(8,128)(2,1)S(1)} %slice.37), channel_id=1, source_target_pairs={{0,2},{2,0},{1,3},{3,1},{4,6},{6,4},{5,7},{7,5},{8,10},{10,8},{9,1... | collective-permute-start | bytes 688136 | tf_op jit(solution)/shard_map/ppermute | solution.py:16
  20.1 17.8 %slice-start = ((s8[7340032]{0:T(1024)(128)(4,1)}), s8[4194304]{0:T(1024)(128)(4,1)S(1)}, s32[]{:S(2)}) async-start(s8[7340032]{0:T(1024)(128)(4,1)} %bitcast.31), calls=%async_computation | async-start | bytes 8388608
  20.1 17.8 %slice-start.1 = ((s8[7340032]{0:T(1024)(128)(4,1)}), s8[3145728]{0:T(1024)(128)(4,1)S(1)}, s32[]{:S(2)}) async-start(s8[7340032]{0:T(1024)(128)(4,1)} %bitcast.31), calls=%async_computation.1 | async-start | bytes 6291456
  26.6 4.8 %collective-permute-start.5 = (bf16[4,2,16,896]{3,2,1,0:T(8,128)(2,1)S(1)}, bf16[4,2,16,896]{3,2,1,0:T(8,128)(2,1)S(1)}, u32[]{:S(2)}, u32[]{:S(2)}) collective-permute-start(bf16[4,2,16,896]{3,2,1,0:T(8,128)(2,1)S(1)} %get-tuple-element.40), channel_id=1, source_target_pairs={{0,1},{1,0},{2,3},{3,2},{4,5},{5,4},{6,7},{7,6},{8,9},{9,8},{10,11... | collective-permute-start | bytes 688136 | tf_op jit(solution)/shard_map/ppermute | solution.py:16
  26.9 6.0 %collective-permute-start.9 = (bf16[32,1792]{1,0:T(8,128)(2,1)S(1)}, bf16[32,1792]{1,0:T(8,128)(2,1)S(1)}, u32[]{:S(2)}, u32[]{:S(2)}) collective-permute-start(bf16[32,1792]{1,0:T(8,128)(2,1)S(1)} %fusion.3.refs_0_), channel_id=1, source_target_pairs={{0,2},{2,0},{1,3},{3,1},{4,6},{6,4},{5,7},{7,5},{8,10},{10,8},{9,1... | collective-permute-start | bytes 344072 | tf_op jit(solution)/shard_map/ppermute | solution.py:16
  29.7 5.2 %collective-permute-start.12 = (bf16[32,1792]{1,0:T(8,128)(2,1)S(1)}, bf16[32,1792]{1,0:T(8,128)(2,1)S(1)}, u32[]{:S(2)}, u32[]{:S(2)}) collective-permute-start(bf16[32,1792]{1,0:T(8,128)(2,1)S(1)} %fusion.1.refs_0_), channel_id=1, source_target_pairs={{0,2},{2,0},{1,3},{3,1},{4,6},{6,4},{5,7},{7,5},{8,10},{10,8},{9,1... | collective-permute-start | bytes 344072 | tf_op jit(solution)/shard_map/ppermute | solution.py:16
  31.4 5.0 %collective-permute-start.4 = (bf16[4,2,16,896]{3,2,1,0:T(8,128)(2,1)S(1)}, bf16[4,2,16,896]{3,2,1,0:T(8,128)(2,1)S(1)}, u32[]{:S(2)}, u32[]{:S(2)}) collective-permute-start(bf16[4,2,16,896]{3,2,1,0:T(8,128)(2,1)S(1)} %get-tuple-element.38), channel_id=1, source_target_pairs={{0,1},{1,0},{2,3},{3,2},{4,5},{5,4},{6,7},{7,6},{8,9},{9,8},{10,11... | collective-permute-start | bytes 688136 | tf_op jit(solution)/shard_map/ppermute | solution.py:16
  33.0 4.3 %collective-permute-start.10 = (bf16[64,1792]{1,0:T(8,128)(2,1)S(1)}, bf16[64,1792]{1,0:T(8,128)(2,1)S(1)}, u32[]{:S(2)}, u32[]{:S(2)}) collective-permute-start(bf16[64,1792]{1,0:T(8,128)(2,1)S(1)} %shard_map.126.refs_0_), channel_id=1, source_target_pairs={{0,1},{1,0},{2,3},{3,2},{4,5},{5,4},{6,7},{7,6},{8,9},{9,8},{10,11... | collective-permute-start | bytes 688136 | tf_op jit(solution)/shard_map/ppermute | solution.py:16
  35.0 2.3 %collective-permute-start.13 = (bf16[64,1792]{1,0:T(8,128)(2,1)S(1)}, bf16[64,1792]{1,0:T(8,128)(2,1)S(1)}, u32[]{:S(2)}, u32[]{:S(2)}) collective-permute-start(bf16[64,1792]{1,0:T(8,128)(2,1)S(1)} %shard_map.127.refs_2_), channel_id=1, source_target_pairs={{0,1},{1,0},{2,3},{3,2},{4,5},{5,4},{6,7},{7,6},{8,9},{9,8},{10,11... | collective-permute-start | bytes 688136 | tf_op jit(solution)/shard_map/ppermute | solution.py:16
  35.0 10.2 %collective-permute-start.18 = (bf16[4,2,16,896]{3,2,1,0:T(8,128)(2,1)S(1)}, bf16[4,2,16,896]{3,2,1,0:T(8,128)(2,1)S(1)}, u32[]{:S(2)}, u32[]{:S(2)}) collective-permute-start(bf16[4,2,16,896]{3,2,1,0:T(8,128)(2,1)S(1)} %shard_map.123.before.refs_2_.mine), channel_id=1, source_target_pairs={{0,2},{2,0},{1,3},{3,1},{4,6},{6,4},{5,7},{7,5},{8,10},{10,8},{9,1... | collective-permute-start | bytes 688136 | tf_op jit(solution)/shard_map/ppermute | solution.py:16
  36.5 13.5 %collective-permute-start.6 = (bf16[4,2,16,896]{3,2,1,0:T(8,128)(2,1)S(1)}, bf16[4,2,16,896]{3,2,1,0:T(8,128)(2,1)S(1)}, u32[]{:S(2)}, u32[]{:S(2)}) collective-permute-start(bf16[4,2,16,896]{3,2,1,0:T(8,128)(2,1)S(1)} %shard_map.124.mine), channel_id=1, source_target_pairs={{0,2},{2,0},{1,3},{3,1},{4,6},{6,4},{5,7},{7,5},{8,10},{10,8},{9,1... | collective-permute-start | bytes 688136 | tf_op jit(solution)/shard_map/ppermute | solution.py:16
  39.1 6.5 %collective-permute-start.15 = (bf16[32,1024]{1,0:T(8,128)(2,1)S(1)}, bf16[32,1024]{1,0:T(8,128)(2,1)S(1)}, u32[]{:S(2)}, u32[]{:S(2)}) collective-permute-start(bf16[32,1024]{1,0:T(8,128)(2,1)S(1)} %get-tuple-element.62), channel_id=1, source_target_pairs={{0,12},{4,8},{8,4},{12,0},{1,13},{5,9},{9,5},{13,1},{2,14},{6,10},... | collective-permute-start | bytes 196616 | tf_op jit(solution)/shard_map/ppermute | solution.py:633
  41.6 4.7 %collective-permute-start.14 = (bf16[32,1024]{1,0:T(8,128)(2,1)S(1)}, bf16[32,1024]{1,0:T(8,128)(2,1)S(1)}, u32[]{:S(2)}, u32[]{:S(2)}) collective-permute-start(bf16[32,1024]{1,0:T(8,128)(2,1)S(1)} %get-tuple-element.63), channel_id=1, source_target_pairs={{0,4},{4,0},{8,12},{12,8},{1,5},{5,1},{9,13},{13,9},{2,6},{6,2},{1... | collective-permute-start | bytes 196616 | tf_op jit(solution)/shard_map/ppermute | solution.py:633
  46.4 3.1 %copy-start = (bf16[3584,1024]{1,0:T(8,128)(2,1)}, bf16[3584,1024]{1,0:T(8,128)(2,1)S(1)}, u32[]{:S(2)}) copy-start(bf16[3584,1024]{1,0:T(8,128)(2,1)S(1)} %shard_map.129.rest_2_) | copy-start | bytes 22020100
  49.4 4.0 %collective-permute-start.19 = (bf16[4,16,896]{2,1,0:T(8,128)(2,1)S(1)}, bf16[4,16,896]{2,1,0:T(8,128)(2,1)S(1)}, u32[]{:S(2)}, u32[]{:S(2)}) collective-permute-start(bf16[4,16,896]{2,1,0:T(8,128)(2,1)S(1)} %get-tuple-element.45.mine), channel_id=1, source_target_pairs={{0,1},{1,0},{2,3},{3,2},{4,5},{5,4},{6,7},{7,6},{8,9},{9,8},{10,11... | collective-permute-start | bytes 344072 | tf_op jit(solution)/shard_map/ppermute | solution.py:16
  49.4 18.1 %collective-permute-start.22 = (bf16[32,1024]{1,0:T(8,128)(2,1)S(1)}, bf16[32,1024]{1,0:T(8,128)(2,1)S(1)}, u32[]{:S(2)}, u32[]{:S(2)}) collective-permute-start(bf16[32,1024]{1,0:T(8,128)(2,1)S(1)} %get-tuple-element.60), channel_id=1, source_target_pairs={{0,8},{4,12},{8,0},{12,4},{1,9},{5,13},{9,1},{13,5},{2,10},{6,14},... | collective-permute-start | bytes 196616 | tf_op jit(solution)/shard_map/ppermute | solution.py:633
  50.0 3.1 %copy-start.1 = (bf16[3584,1024]{1,0:T(8,128)(2,1)S(1)}, bf16[3584,1024]{1,0:T(8,128)(2,1)}, u32[]{:S(2)}) copy-start(bf16[3584,1024]{1,0:T(8,128)(2,1)} %copy-done) | copy-start | bytes 22020100
  53.0 3.1 %copy-start.2 = (bf16[3584,1024]{1,0:T(8,128)(2,1)S(1)}, bf16[3584,1024]{1,0:T(8,128)(2,1)}, u32[]{:S(2)}) copy-start(bf16[3584,1024]{1,0:T(8,128)(2,1)} %copy-done) | copy-start | bytes 22020100
  53.1 7.7 %collective-permute-start.16 = (bf16[4,16,896]{2,1,0:T(8,128)(2,1)S(1)}, bf16[4,16,896]{2,1,0:T(8,128)(2,1)S(1)}, u32[]{:S(2)}, u32[]{:S(2)}) collective-permute-start(bf16[4,16,896]{2,1,0:T(8,128)(2,1)S(1)} %get-tuple-element.44.mine), channel_id=1, source_target_pairs={{0,1},{1,0},{2,3},{3,2},{4,5},{5,4},{6,7},{7,6},{8,9},{9,8},{10,11... | collective-permute-start | bytes 344072 | tf_op jit(solution)/shard_map/ppermute | solution.py:16
  57.5 9.9 %collective-permute-start.21 = (bf16[32,1024]{1,0:T(8,128)(2,1)S(1)}, bf16[32,1024]{1,0:T(8,128)(2,1)S(1)}, u32[]{:S(2)}, u32[]{:S(2)}) collective-permute-start(bf16[32,1024]{1,0:T(8,128)(2,1)S(1)} %get-tuple-element.64), channel_id=1, source_target_pairs={{0,12},{4,8},{8,4},{12,0},{1,13},{5,9},{9,5},{13,1},{2,14},{6,10},... | collective-permute-start | bytes 196616 | tf_op jit(solution)/shard_map/ppermute | solution.py:633
  60.1 7.4 %collective-permute-start.20 = (bf16[32,1024]{1,0:T(8,128)(2,1)S(1)}, bf16[32,1024]{1,0:T(8,128)(2,1)S(1)}, u32[]{:S(2)}, u32[]{:S(2)}) collective-permute-start(bf16[32,1024]{1,0:T(8,128)(2,1)S(1)} %get-tuple-element.65), channel_id=1, source_target_pairs={{0,8},{4,12},{8,0},{12,4},{1,9},{5,13},{9,1},{13,5},{2,10},{6,14},... | collective-permute-start | bytes 196616 | tf_op jit(solution)/shard_map/ppermute | solution.py:633
  62.7 5.2 %collective-permute-start.17 = (bf16[32,1024]{1,0:T(8,128)(2,1)S(1)}, bf16[32,1024]{1,0:T(8,128)(2,1)S(1)}, u32[]{:S(2)}, u32[]{:S(2)}) collective-permute-start(bf16[32,1024]{1,0:T(8,128)(2,1)S(1)} %get-tuple-element.66), channel_id=1, source_target_pairs={{0,4},{4,0},{8,12},{12,8},{1,5},{5,1},{9,13},{13,9},{2,6},{6,2},{1... | collective-permute-start | bytes 196616 | tf_op jit(solution)/shard_map/ppermute | solution.py:633
  68.0 8.4 %collective-permute-start.25 = (bf16[32,1024]{1,0:T(8,128)(2,1)S(1)}, bf16[32,1024]{1,0:T(8,128)(2,1)S(1)}, u32[]{:S(2)}, u32[]{:S(2)}) collective-permute-start(bf16[32,1024]{1,0:T(8,128)(2,1)S(1)} %get-tuple-element.48), channel_id=1, source_target_pairs={{0,12},{4,8},{8,4},{12,0},{1,13},{5,9},{9,5},{13,1},{2,14},{6,10},... | collective-permute-start | bytes 196616 | tf_op jit(solution)/shard_map/ppermute | solution.py:633
  70.2 6.1 %collective-permute-start.24 = (bf16[32,1024]{1,0:T(8,128)(2,1)S(1)}, bf16[32,1024]{1,0:T(8,128)(2,1)S(1)}, u32[]{:S(2)}, u32[]{:S(2)}) collective-permute-start(bf16[32,1024]{1,0:T(8,128)(2,1)S(1)} %get-tuple-element.48), channel_id=1, source_target_pairs={{0,8},{4,12},{8,0},{12,4},{1,9},{5,13},{9,1},{13,5},{2,10},{6,14},... | collective-permute-start | bytes 196616 | tf_op jit(solution)/shard_map/ppermute | solution.py:633
  70.2 5.0 %collective-permute-start.23 = (bf16[32,1024]{1,0:T(8,128)(2,1)S(1)}, bf16[32,1024]{1,0:T(8,128)(2,1)S(1)}, u32[]{:S(2)}, u32[]{:S(2)}) collective-permute-start(bf16[32,1024]{1,0:T(8,128)(2,1)S(1)} %get-tuple-element.48), channel_id=1, source_target_pairs={{0,4},{4,0},{8,12},{12,8},{1,5},{5,1},{9,13},{13,9},{2,6},{6,2},{1... | collective-permute-start | bytes 196616 | tf_op jit(solution)/shard_map/ppermute | solution.py:633
  77.8 2.0 %collective-permute-start.26 = (bf16[2,32,896]{2,1,0:T(8,128)(2,1)S(1)}, bf16[2,32,896]{2,1,0:T(8,128)(2,1)S(1)}, u32[]{:S(2)}, u32[]{:S(2)}) collective-permute-start(bf16[2,32,896]{2,1,0:T(8,128)(2,1)S(1)} %get-tuple-element.50), channel_id=1, source_target_pairs={{0,1},{1,0},{2,3},{3,2},{4,5},{5,4},{6,7},{7,6},{8,9},{9,8},{10,11... | collective-permute-start | bytes 344072 | tf_op jit(solution)/shard_map/ppermute | solution.py:16
  79.2 2.0 %collective-permute-start.28 = (bf16[2,32,896]{2,1,0:T(8,128)(2,1)S(1)}, bf16[2,32,896]{2,1,0:T(8,128)(2,1)S(1)}, u32[]{:S(2)}, u32[]{:S(2)}) collective-permute-start(bf16[2,32,896]{2,1,0:T(8,128)(2,1)S(1)} %get-tuple-element.53), channel_id=1, source_target_pairs={{0,1},{1,0},{2,3},{3,2},{4,5},{5,4},{6,7},{7,6},{8,9},{9,8},{10,11... | collective-permute-start | bytes 344072 | tf_op jit(solution)/shard_map/ppermute | solution.py:16
  79.8 6.1 %collective-permute-start.27 = (bf16[2,32,896]{2,1,0:T(8,128)(2,1)S(1)}, bf16[2,32,896]{2,1,0:T(8,128)(2,1)S(1)}, u32[]{:S(2)}, u32[]{:S(2)}) collective-permute-start(bf16[2,32,896]{2,1,0:T(8,128)(2,1)S(1)} %add_convert_fusion.3.mine), channel_id=1, source_target_pairs={{0,2},{2,0},{1,3},{3,1},{4,6},{6,4},{5,7},{7,5},{8,10},{10,8},{9,1... | collective-permute-start | bytes 344072 | tf_op jit(solution)/shard_map/ppermute | solution.py:16
  81.2 6.2 %collective-permute-start.30 = (bf16[2,32,896]{2,1,0:T(8,128)(2,1)S(1)}, bf16[2,32,896]{2,1,0:T(8,128)(2,1)S(1)}, u32[]{:S(2)}, u32[]{:S(2)}) collective-permute-start(bf16[2,32,896]{2,1,0:T(8,128)(2,1)S(1)} %add_convert_fusion.2.before.mine), channel_id=1, source_target_pairs={{0,2},{2,0},{1,3},{3,1},{4,6},{6,4},{5,7},{7,5},{8,10},{10,8},{9,1... | collective-permute-start | bytes 344072 | tf_op jit(solution)/shard_map/ppermute | solution.py:16
  86.0 2.2 %collective-permute-start.29 = (bf16[2,2,32,896]{3,2,1,0:T(8,128)(2,1)S(1)}, bf16[2,2,32,896]{3,2,1,0:T(8,128)(2,1)S(1)}, u32[]{:S(2)}, u32[]{:S(2)}) collective-permute-start(bf16[2,2,32,896]{3,2,1,0:T(8,128)(2,1)S(1)} %shard_map.140.rest_0_), channel_id=1, source_target_pairs={{0,1},{1,0},{2,3},{3,2},{4,5},{5,4},{6,7},{7,6},{8,9},{9,8},{10,11... | collective-permute-start | bytes 688136 | tf_op jit(solution)/shard_map/ppermute | solution.py:16
  87.5 1.6 %collective-permute-start.31 = (bf16[2,2,32,896]{3,2,1,0:T(8,128)(2,1)S(1)}, bf16[2,2,32,896]{3,2,1,0:T(8,128)(2,1)S(1)}, u32[]{:S(2)}, u32[]{:S(2)}) collective-permute-start(bf16[2,2,32,896]{3,2,1,0:T(8,128)(2,1)S(1)} %shard_map.141.rest_2_), channel_id=1, source_target_pairs={{0,1},{1,0},{2,3},{3,2},{4,5},{5,4},{6,7},{7,6},{8,9},{9,8},{10,11... | collective-permute-start | bytes 688136 | tf_op jit(solution)/shard_map/ppermute | solution.py:16

commit v15 on v12

--- a/solution.py
+++ b/solution.py
@@ -144,7 +144,7 @@
             pltpu.SemaphoreType.DMA((2, 8)),
             pltpu.SemaphoreType.DMA((2,)),
         ],
-        compiler_params=pltpu.CompilerParams(vmem_limit_bytes=8 * 1024 * 1024),
+        compiler_params=pltpu.CompilerParams(vmem_limit_bytes=3 * 1024 * 1024),
         cost_estimate=pl.CostEstimate(
             flops=0, bytes_accessed=4 * gate.size, transcendentals=0
         ),
@@ -169,7 +169,7 @@
         in_specs=[whole()] * (2 * ranks) + [anywhere()] * len(before),
         out_specs=(whole(), whole()),
         out_shape=(jax.ShapeDtypeStruct(shape, F32), jax.ShapeDtypeStruct(shape, BF)),
-        compiler_params=pltpu.CompilerParams(vmem_limit_bytes=4 * 1024 * 1024),
+        compiler_params=pltpu.CompilerParams(vmem_limit_bytes=2 * 1024 * 1024),
     )(*student, *target, *before)
 
 
@@ -203,7 +203,7 @@
         in_specs=[scalars(), whole(), whole(), whole()],
         out_specs=(whole(), whole()),
         out_shape=(half, half),
-        compiler_params=pltpu.CompilerParams(vmem_limit_bytes=8 * 1024 * 1024),
+        compiler_params=pltpu.CompilerParams(vmem_limit_bytes=4 * 1024 * 1024),
         cost_estimate=pl.CostEstimate(
             flops=4 * token_count * width * size, bytes_accessed=4 * width * size, transcendentals=0
         ),
@@ -263,7 +263,7 @@
             pltpu.VMEM((min(count, 2), 2, width, H), BF),
             pltpu.SemaphoreType.DMA((min(count, 2), 2, 4)),
         ],
-        compiler_params=pltpu.CompilerParams(vmem_limit_bytes=12 * 1024 * 1024),
+        compiler_params=pltpu.CompilerParams(vmem_limit_bytes=10 * 1024 * 1024),
         cost_estimate=pl.CostEstimate(
             flops=count * 4 * slots * width * H,
             bytes_accessed=count * 4 * width * H,
@@ -282,7 +282,7 @@
         in_specs=[whole(), whole(), anywhere()],
         out_specs=whole(),
         out_shape=jax.ShapeDtypeStruct(a.shape, BF),
-        compiler_params=pltpu.CompilerParams(vmem_limit_bytes=4 * 1024 * 1024),
+        compiler_params=pltpu.CompilerParams(vmem_limit_bytes=2 * 1024 * 1024),
     )(a, b, before)
 
 
@@ -318,7 +318,7 @@
             jax.ShapeDtypeStruct(mine.shape, F32),
             jax.ShapeDtypeStruct((count, rows, width), BF),
         ),
-        compiler_params=pltpu.CompilerParams(vmem_limit_bytes=8 * 1024 * 1024),
+        compiler_params=pltpu.CompilerParams(vmem_limit_bytes=2 * 1024 * 1024),
     )(mine, other, weight, *before)
 
 
@@ -336,7 +336,7 @@
         in_specs=[whole()] * len(values) + [anywhere()],
         out_specs=whole(),
         out_shape=jax.ShapeDtypeStruct((rows * len(values), width), BF),
-        compiler_params=pltpu.CompilerParams(vmem_limit_bytes=4 * 1024 * 1024),
+        compiler_params=pltpu.CompilerParams(vmem_limit_bytes=2 * 1024 * 1024),
     )(*values, before)
 
 
@@ -365,7 +365,7 @@
         in_specs=[scalars()] + [whole()] * len(flat),
         out_specs=whole(),
         out_shape=jax.ShapeDtypeStruct((rows, width), BF),
-        compiler_params=pltpu.CompilerParams(vmem_limit_bytes=8 * 1024 * 1024),
+        compiler_params=pltpu.CompilerParams(vmem_limit_bytes=2 * 1024 * 1024),
     )(place, *flat)
 
 
@@ -388,7 +388,7 @@
         in_specs=[whole()] * 3,
         out_specs=whole(),
         out_shape=jax.ShapeDtypeStruct((tokens[1] - tokens[0], count * H), BF),
-        compiler_params=pltpu.CompilerParams(vmem_limit_bytes=8 * 1024 * 1024),
+        compiler_params=pltpu.CompilerParams(vmem_limit_bytes=3 * 1024 * 1024),
     )(picker, mine, theirs)
 
 
@@ -409,7 +409,7 @@
             jax.ShapeDtypeStruct((dense[0].shape[1], tokens.shape[0]), BF),
             jax.ShapeDtypeStruct(tokens.shape[::-1], BF),
         ),
-        compiler_params=pltpu.CompilerParams(vmem_limit_bytes=16 * 1024 * 1024),
+        compiler_params=pltpu.CompilerParams(vmem_limit_bytes=6 * 1024 * 1024),
     )(*dense, tokens, before)
 
 
@@ -430,7 +430,7 @@
         in_specs=[whole(), whole(), whole(), anywhere()],
         out_specs=(whole(), whole()),
         out_shape=(part, part),
-        compiler_params=pltpu.CompilerParams(vmem_limit_bytes=8 * 1024 * 1024),
+        compiler_params=pltpu.CompilerParams(vmem_limit_bytes=3 * 1024 * 1024),
     )(picker, residual, down, before)
 
 
@@ -456,7 +456,7 @@
         in_specs=[whole(), whole(), whole(), anywhere()] + [whole()] * len(pres),
         out_specs=whole(),
         out_shape=jax.ShapeDtypeStruct((count, 2, rows, width), BF),
-        compiler_params=pltpu.CompilerParams(vmem_limit_bytes=8 * 1024 * 1024),
+        compiler_params=pltpu.CompilerParams(vmem_limit_bytes=2 * 1024 * 1024),
     )(mine, other, weight, before, *pres)
 
 
@@ -489,7 +489,7 @@
             pltpu.VMEM((rows, width), BF),
             pltpu.SemaphoreType.DMA((rows // (H // 2),)),
         ],
-        compiler_params=pltpu.CompilerParams(vmem_limit_bytes=16 * 1024 * 1024),
+        compiler_params=pltpu.CompilerParams(vmem_limit_bytes=10 * 1024 * 1024),
         cost_estimate=pl.CostEstimate(
             flops=2 * rows * width * token_count,
             bytes_accessed=2 * rows * width,
@@ -536,7 +536,7 @@
             pltpu.VMEM((count, 2, width, H), BF),
             pltpu.SemaphoreType.DMA((count, 2, 2)),
         ],
-        compiler_params=pltpu.CompilerParams(vmem_limit_bytes=24 * 1024 * 1024),
+        compiler_params=pltpu.CompilerParams(vmem_limit_bytes=18 * 1024 * 1024),
         cost_estimate=pl.CostEstimate(
             flops=count * 4 * token_count * width * H,
             bytes_accessed=count * 4 * width * H,

time: 93.7 us -> 93.7 us (level)
  no operation moved by 1% of the time
where the time goes in v15:
time: 93.7 us; the launch traced here: 93.5 us
  Pallas kernels  31.1 us (33%)
  starting transfers between devices  30.1 us (32%)
  waiting for transfers between devices  19.1 us (20%)
  matrix products  10.4 us (11%)
  between operations  1.32 us (1%)
  other arithmetic  1.23 us (1%)
    ppermute x12, starting transfers between devices, to_partner(): return lax.ppermute(value, 'expert', [(i, i ^ s) for i in range(ranks)])  18.2 us
    ppermute x20, starting transfers between devices, shift(): lax.ppermute(value, axis, [(i, (i + by) % count) for i in range(count)])  11.8 us
    ppermute x20, waiting for transfers between devices, shift(): lax.ppermute(value, axis, [(i, (i + by) % count) for i in range(count)])  9.76 us
    ppermute x12, waiting for transfers between devices, to_partner(): return lax.ppermute(value, 'expert', [(i, i ^ s) for i in range(ranks)])  9.38 us
    dot_general x2, matrix products, body(): jnp.dot(dense[-1], expert_down, preferred_element_type=F32).astype(BF)  9.24 us
    pallas_call x1, Pallas kernels, expert_pre(): pl.pallas_call(functools.partial(expert_kernel, cuts), in_specs=[whole(),...  6.57 us
    pallas_call x1, Pallas kernels, input_grads(): pl.pallas_call(functools.partial(input_grad_kernel, count // len(parts)),...  6.49 us
    pallas_call x1, Pallas kernels, prepare(): pl.pallas_call(functools.partial(prepare_kernel, near_first, ranks, capac...  5.89 us
  transfers between devices with their start and end apart: 32, of which 14 were waited for; matrix products, arithmetic and copies ran while one was open for 13% of the time, Pallas kernels for 23%

profile of v15, /device:TPU:0, one launch (start us, length us, event | category | flops | bytes accessed | tf_op | source)
XLA Modules:
  0.0 93.5 jit_solution(2371135099304311213)
XLA Ops:
  0.6 3.1 %collective-permute-start = (bf16[32,1024]{1,0:T(8,128)(2,1)}, bf16[32,1024]{1,0:T(8,128)(2,1)S(1)}, u32[]{:S(2)}, u32[]{:S(2)}) collective-permute-start(bf16[32,1024]{1,0:T(8,128)(2,1)} %param.9), channel_id=1, source_target_pairs={{0,4},{4,0},{8,12},{12,8},{1,5},{5,1},{9,13},{13,9},{2,6},{6,2},{1... | collective-permute-start | bytes 196616 | tf_op jit(solution)/shard_map/ppermute | solution.py:617
  3.7 2.5 %collective-permute-start.2 = (bf16[32,1024]{1,0:T(8,128)(2,1)}, bf16[32,1024]{1,0:T(8,128)(2,1)S(1)}, u32[]{:S(2)}, u32[]{:S(2)}) collective-permute-start(bf16[32,1024]{1,0:T(8,128)(2,1)} %param.9), channel_id=1, source_target_pairs={{0,12},{4,8},{8,4},{12,0},{1,13},{5,9},{9,5},{13,1},{2,14},{6,10},... | collective-permute-start | bytes 196616 | tf_op jit(solution)/shard_map/ppermute | solution.py:617
  6.2 0.1 collective-permute-start.1
  6.3 0.1 pad_add_fusion.place
  6.4 5.9 %shard_map.120 = (bf16[4,64,128]{2,1,0:T(8,128)(2,1)S(1)}, f32[4,64,1]{2,1,0:T(8,128)S(1)}, bf16[1024,3584]{1,0:T(8,128)(2,1)S(1)}, bf16[1024,3584]{1,0:T(8,128)(2,1)S(1)}) custom-call(s32[3]{0:T(128)S(1)} %pad_add_fusion.place, s32[4,128]{1,0:T(4,128)} %bitcast.35, f32[4,128]{1,0:T(4,128)} %bitcast.36, bf16[1024,3584]{1,0:T(8,128)(2,1)} %gate.2, ...), custom_call_target="tpu_custom_call" | custom-call | bytes 14680064 | tf_op jit(solution)/shard_map/pallas_call | solution.py:131
  12.4 0.5 collective-permute-done.1
  12.9 1.7 %shard_map.125 = (bf16[2,64,1792]{2,1,0:T(8,128)(2,1)S(1)}, bf16[2,64,1792]{2,1,0:T(8,128)(2,1)S(1)}) custom-call(s32[3]{0:T(128)S(1)} %pad_add_fusion.place, bf16[128,1024]{1,0:T(8,128)(2,1)S(1)} %constant_dynamic-update-slice_fusion.4.tokens.refs_2_, bf16[1024,3584]{1,0:T(8,128)(2,1)S(1)} %get-tuple-element.33.gate, ...), custom_call_target="tpu_custom_call" | custom-call | flops 939524096 | bytes 7340032 | tf_op jit(solution)/shard_map/pallas_call | solution.py:201
  14.7 1.7 %shard_map.121 = (bf16[2,64,1792]{2,1,0:T(8,128)(2,1)S(1)}, bf16[2,64,1792]{2,1,0:T(8,128)(2,1)S(1)}) custom-call(s32[3]{0:T(128)S(1)} %pad_add_fusion.place, bf16[128,1024]{1,0:T(8,128)(2,1)S(1)} %constant_dynamic-update-slice_fusion.4.tokens.refs_2_, bf16[1024,3584]{1,0:T(8,128)(2,1)S(1)} %get-tuple-element.33.gate, ...), custom_call_target="tpu_custom_call" | custom-call | flops 939524096 | bytes 7340032 | tf_op jit(solution)/shard_map/pallas_call | solution.py:201
  16.3 0.6 collective-permute-start.3
  16.9 0.1 add_convert_fusion
  17.0 1.6 %collective-permute-start.9 = (bf16[2,32,1792]{2,1,0:T(8,128)(2,1)S(1)}, bf16[2,32,1792]{2,1,0:T(8,128)(2,1)S(1)}, u32[]{:S(2)}, u32[]{:S(2)}) collective-permute-start(bf16[2,32,1792]{2,1,0:T(8,128)(2,1)S(1)} %slice.33), channel_id=1, source_target_pairs={{0,2},{2,0},{1,3},{3,1},{4,6},{6,4},{5,7},{7,5},{8,10},{10,8},{9,1... | collective-permute-start | bytes 688136 | tf_op jit(solution)/shard_map/ppermute | solution.py:16
  18.6 0.1 add_convert_fusion.1.before
  18.7 1.3 %collective-permute-start.12 = (bf16[2,32,1792]{2,1,0:T(8,128)(2,1)S(1)}, bf16[2,32,1792]{2,1,0:T(8,128)(2,1)S(1)}, u32[]{:S(2)}, u32[]{:S(2)}) collective-permute-start(bf16[2,32,1792]{2,1,0:T(8,128)(2,1)S(1)} %slice.37), channel_id=1, source_target_pairs={{0,2},{2,0},{1,3},{3,1},{4,6},{6,4},{5,7},{7,5},{8,10},{10,8},{9,1... | collective-permute-start | bytes 688136 | tf_op jit(solution)/shard_map/ppermute | solution.py:16
  20.1 6.6 %shard_map.122 = (bf16[4,2,16,896]{3,2,1,0:T(8,128)(2,1)S(1)}, bf16[4,2,16,896]{3,2,1,0:T(8,128)(2,1)S(1)}, bf16[4,2,16,896]{3,2,1,0:T(8,128)(2,1)S(1)}, bf16[4,2,16,896]{3,2,1,0:T(8,128)(2,1)S(1)}) custom-call(bf16[4,64,128]{2,1,0:T(8,128)(2,1)S(1)} %get-tuple-element.32.picker, bf16[128,1024]{1,0:T(8,128)(2,1)S(1)} %constant_dynamic-update-slice_fusion.4.tokens.refs_2_, ...), custom_call_target="tpu_custom_call" | custom-call | flops 939524096 | bytes 14680064 | tf_op jit(solution)/shard_map/pallas_call | solution.py:257
  26.6 0.1 collective-permute-start.5
  26.8 0.1 fusion.3.refs_0_
  26.9 0.8 collective-permute-start.10
  27.7 1.9 %collective-permute-done.12 = bf16[2,32,1792]{2,1,0:T(8,128)(2,1)S(1)} collective-permute-done((bf16[2,32,1792]{2,1,0:T(8,128)(2,1)S(1)}, bf16[2,32,1792]{2,1,0:T(8,128)(2,1)S(1)}, u32[]{:S(2)}, u32[]{:S(2)}) %collective-permute-start.12) | collective-permute-done | bytes 229408 | tf_op jit(solution)/shard_map/ppermute | solution.py:16
  29.6 0.1 fusion.1.refs_0_
  29.7 1.8 %collective-permute-start.13 = (bf16[32,1792]{1,0:T(8,128)(2,1)S(1)}, bf16[32,1792]{1,0:T(8,128)(2,1)S(1)}, u32[]{:S(2)}, u32[]{:S(2)}) collective-permute-start(bf16[32,1792]{1,0:T(8,128)(2,1)S(1)} %fusion.1.refs_0_), channel_id=1, source_target_pairs={{0,2},{2,0},{1,3},{3,1},{4,6},{6,4},{5,7},{7,5},{8,10},{10,8},{9,1... | collective-permute-start | bytes 344072 | tf_op jit(solution)/shard_map/ppermute | solution.py:16
  31.5 1.4 %collective-permute-done.10.refs_1_ = bf16[32,1792]{1,0:T(8,128)(2,1)S(1)} collective-permute-done((bf16[32,1792]{1,0:T(8,128)(2,1)S(1)}, bf16[32,1792]{1,0:T(8,128)(2,1)S(1)}, u32[]{:S(2)}, u32[]{:S(2)}) %collective-permute-start.10) | collective-permute-done | bytes 114720 | tf_op jit(solution)/shard_map/ppermute | solution.py:16
  33.0 1.9 %collective-permute-done.13.refs_1_ = bf16[32,1792]{1,0:T(8,128)(2,1)S(1)} collective-permute-done((bf16[32,1792]{1,0:T(8,128)(2,1)S(1)}, bf16[32,1792]{1,0:T(8,128)(2,1)S(1)}, u32[]{:S(2)}, u32[]{:S(2)}) %collective-permute-start.13) | collective-permute-done | bytes 114720 | tf_op jit(solution)/shard_map/ppermute | solution.py:16
  35.0 1.4 %collective-permute-start.7 = (bf16[4,2,16,896]{3,2,1,0:T(8,128)(2,1)S(1)}, bf16[4,2,16,896]{3,2,1,0:T(8,128)(2,1)S(1)}, u32[]{:S(2)}, u32[]{:S(2)}) collective-permute-start(bf16[4,2,16,896]{3,2,1,0:T(8,128)(2,1)S(1)} %shard_map.123.before.refs_2_.mine), channel_id=1, source_target_pairs={{0,2},{2,0},{1,3},{3,1},{4,6},{6,4},{5,7},{7,5},{8,10},{10,8},{9,1... | collective-permute-start | bytes 688136 | tf_op jit(solution)/shard_map/ppermute | solution.py:16
  36.5 0.8 collective-permute-start.6
  37.3 0.6 shard_map.128
  37.9 1.1 %convolution_convert_fusion = bf16[128,1024]{1,0:T(8,128)(2,1)S(1)} fusion(bf16[128,3584]{1,0:T(8,128)(2,1)S(1)} %shard_map.128, bf16[3584,1024]{1,0:T(8,128)(2,1)S(1)} %bitcast.34), kind=kOutput, calls=%fused_computation | convolution fusion | flops 939655168 | bytes 8519680 | tf_op jit(solution)/shard_map/dot_general | solution.py:681
  39.1 2.5 %collective-permute-start.16 = (bf16[32,1024]{1,0:T(8,128)(2,1)S(1)}, bf16[32,1024]{1,0:T(8,128)(2,1)S(1)}, u32[]{:S(2)}, u32[]{:S(2)}) collective-permute-start(bf16[32,1024]{1,0:T(8,128)(2,1)S(1)} %get-tuple-element.62), channel_id=1, source_target_pairs={{0,12},{4,8},{8,4},{12,0},{1,13},{5,9},{9,5},{13,1},{2,14},{6,10},... | collective-permute-start | bytes 196616 | tf_op jit(solution)/shard_map/ppermute | solution.py:617
  41.6 0.5 collective-permute-start.15
  42.0 1.5 %collective-permute-done.7.other = bf16[4,2,16,896]{3,2,1,0:T(8,128)(2,1)S(1)} collective-permute-done((bf16[4,2,16,896]{3,2,1,0:T(8,128)(2,1)S(1)}, bf16[4,2,16,896]{3,2,1,0:T(8,128)(2,1)S(1)}, u32[]{:S(2)}, u32[]{:S(2)}) %collective-permute-start.7) | collective-permute-done | bytes 229408 | tf_op jit(solution)/shard_map/ppermute | solution.py:16
  43.5 2.1 %collective-permute-done.16.rest_1_.refs_7_ = bf16[32,1024]{1,0:T(8,128)(2,1)S(1)} collective-permute-done((bf16[32,1024]{1,0:T(8,128)(2,1)S(1)}, bf16[32,1024]{1,0:T(8,128)(2,1)S(1)}, u32[]{:S(2)}, u32[]{:S(2)}) %collective-permute-start.16) | collective-permute-done | bytes 65568 | tf_op jit(solution)/shard_map/ppermute | solution.py:617
  45.6 0.7 collective-permute-done.15.rest_0_.refs_5_
  46.3 0.1 shard_map.129
  46.5 0.6 collective-permute-start.22
  47.1 0.7 collective-permute-done.17.theirs
  47.8 0.4 shard_map.130.rest_0_.refs_1_
  48.2 0.1 shard_map.131
  48.3 0.2 collective-permute-start.18
  48.5 4.6 %convolution_convert_fusion.1 = bf16[64,1024]{1,0:T(8,128)(2,1)S(1)} fusion(bf16[64,3584]{1,0:T(8,128)(2,1)S(1)} %shard_map.130.rest_0_.refs_1_, bf16[3584,1024]{1,0:T(8,128)(2,1)} %down.3), kind=kOutput, calls=%fused_computation.1 | convolution fusion | flops 469827584 | bytes 7929856 | tf_op jit(solution)/shard_map/dot_general | solution.py:691
  53.2 2.2 %collective-permute-start.21 = (bf16[32,1024]{1,0:T(8,128)(2,1)S(1)}, bf16[32,1024]{1,0:T(8,128)(2,1)S(1)}, u32[]{:S(2)}, u32[]{:S(2)}) collective-permute-start(bf16[32,1024]{1,0:T(8,128)(2,1)S(1)} %get-tuple-element.64), channel_id=1, source_target_pairs={{0,12},{4,8},{8,4},{12,0},{1,13},{5,9},{9,5},{13,1},{2,14},{6,10},... | collective-permute-start | bytes 196616 | tf_op jit(solution)/shard_map/ppermute | solution.py:617
  55.3 0.5 collective-permute-start.20
  55.8 0.4 shard_map.132.refs_0_
  56.3 4.6 %convolution_convert_fusion.2.refs_3_ = bf16[64,1024]{1,0:T(8,128)(2,1)S(1)} fusion(bf16[64,3584]{1,0:T(8,128)(2,1)S(1)} %shard_map.132.refs_0_, bf16[3584,1024]{1,0:T(8,128)(2,1)} %down.3), kind=kOutput, calls=%fused_computation.2 | convolution fusion | flops 469827584 | bytes 7929856 | tf_op jit(solution)/shard_map/dot_general | solution.py:691
  60.9 1.9 %collective-permute-start.19 = (bf16[32,1024]{1,0:T(8,128)(2,1)S(1)}, bf16[32,1024]{1,0:T(8,128)(2,1)S(1)}, u32[]{:S(2)}, u32[]{:S(2)}) collective-permute-start(bf16[32,1024]{1,0:T(8,128)(2,1)S(1)} %get-tuple-element.66), channel_id=1, source_target_pairs={{0,4},{4,0},{8,12},{12,8},{1,5},{5,1},{9,13},{13,9},{2,6},{6,2},{1... | collective-permute-start | bytes 196616 | tf_op jit(solution)/shard_map/ppermute | solution.py:617
  62.8 0.4 shard_map.133
  63.2 2.1 %collective-permute-done.19.refs_1_ = bf16[32,1024]{1,0:T(8,128)(2,1)S(1)} collective-permute-done((bf16[32,1024]{1,0:T(8,128)(2,1)S(1)}, bf16[32,1024]{1,0:T(8,128)(2,1)S(1)}, u32[]{:S(2)}, u32[]{:S(2)}) %collective-permute-start.19) | collective-permute-done | bytes 65568 | tf_op jit(solution)/shard_map/ppermute | solution.py:617
  65.3 0.1 shard_map.134
  65.3 2.4 %collective-permute-start.25 = (bf16[32,1024]{1,0:T(8,128)(2,1)S(1)}, bf16[32,1024]{1,0:T(8,128)(2,1)S(1)}, u32[]{:S(2)}, u32[]{:S(2)}) collective-permute-start(bf16[32,1024]{1,0:T(8,128)(2,1)S(1)} %get-tuple-element.48), channel_id=1, source_target_pairs={{0,12},{4,8},{8,4},{12,0},{1,13},{5,9},{9,5},{13,1},{2,14},{6,10},... | collective-permute-start | bytes 196616 | tf_op jit(solution)/shard_map/ppermute | solution.py:617
  67.7 0.9 %collective-permute-start.24 = (bf16[32,1024]{1,0:T(8,128)(2,1)S(1)}, bf16[32,1024]{1,0:T(8,128)(2,1)S(1)}, u32[]{:S(2)}, u32[]{:S(2)}) collective-permute-start(bf16[32,1024]{1,0:T(8,128)(2,1)S(1)} %get-tuple-element.48), channel_id=1, source_target_pairs={{0,8},{4,12},{8,0},{12,4},{1,9},{5,13},{9,1},{13,5},{2,10},{6,14},... | collective-permute-start | bytes 196616 | tf_op jit(solution)/shard_map/ppermute | solution.py:617
  68.7 1.1 %collective-permute-start.23 = (bf16[32,1024]{1,0:T(8,128)(2,1)S(1)}, bf16[32,1024]{1,0:T(8,128)(2,1)S(1)}, u32[]{:S(2)}, u32[]{:S(2)}) collective-permute-start(bf16[32,1024]{1,0:T(8,128)(2,1)S(1)} %get-tuple-element.48), channel_id=1, source_target_pairs={{0,4},{4,0},{8,12},{12,8},{1,5},{5,1},{9,13},{13,9},{2,6},{6,2},{1... | collective-permute-start | bytes 196616 | tf_op jit(solution)/shard_map/ppermute | solution.py:617
  69.8 3.1 %collective-permute-done.23 = bf16[32,1024]{1,0:T(8,128)(2,1)S(1)} collective-permute-done((bf16[32,1024]{1,0:T(8,128)(2,1)S(1)}, bf16[32,1024]{1,0:T(8,128)(2,1)S(1)}, u32[]{:S(2)}, u32[]{:S(2)}) %collective-permute-start.23) | collective-permute-done | bytes 65568 | tf_op jit(solution)/shard_map/ppermute | solution.py:617
  73.0 0.9 %collective-permute-done.24 = bf16[32,1024]{1,0:T(8,128)(2,1)S(1)} collective-permute-done((bf16[32,1024]{1,0:T(8,128)(2,1)S(1)}, bf16[32,1024]{1,0:T(8,128)(2,1)S(1)}, u32[]{:S(2)}, u32[]{:S(2)}) %collective-permute-start.24) | collective-permute-done | bytes 65568 | tf_op jit(solution)/shard_map/ppermute | solution.py:617
  74.0 1.5 %shard_map.135 = (bf16[2,32,896]{2,1,0:T(8,128)(2,1)S(1)}, bf16[2,32,896]{2,1,0:T(8,128)(2,1)S(1)}) custom-call(bf16[4,64,128]{2,1,0:T(8,128)(2,1)S(1)} %get-tuple-element.32.picker, bf16[128,1024]{1,0:T(8,128)(2,1)S(1)} %constant_dynamic-update-slice_fusion.residual.before, bf16[3584,1024]{1,0:T(8,128)(2,1)S(1)} %bitcast.32, ...), custom_call_target="tpu_custom_call" | custom-call | tf_op jit(solution)/shard_map/pallas_call | solution.py:428
  75.6 1.3 %shard_map.136 = (bf16[2,32,896]{2,1,0:T(8,128)(2,1)S(1)}, bf16[2,32,896]{2,1,0:T(8,128)(2,1)S(1)}) custom-call(bf16[4,64,128]{2,1,0:T(8,128)(2,1)S(1)} %get-tuple-element.32.picker, bf16[128,1024]{1,0:T(8,128)(2,1)S(1)} %constant_dynamic-update-slice_fusion.residual.before, bf16[3584,1024]{1,0:T(8,128)(2,1)S(1)} %bitcast.32, ...), custom_call_target="tpu_custom_call" | custom-call | tf_op jit(solution)/shard_map/pallas_call | solution.py:428
  77.0 0.6 collective-permute-start.28
  77.6 1.4 %collective-permute-start.27 = (bf16[2,32,896]{2,1,0:T(8,128)(2,1)S(1)}, bf16[2,32,896]{2,1,0:T(8,128)(2,1)S(1)}, u32[]{:S(2)}, u32[]{:S(2)}) collective-permute-start(bf16[2,32,896]{2,1,0:T(8,128)(2,1)S(1)} %add_convert_fusion.3.mine), channel_id=1, source_target_pairs={{0,2},{2,0},{1,3},{3,1},{4,6},{6,4},{5,7},{7,5},{8,10},{10,8},{9,1... | collective-permute-start | bytes 344072 | tf_op jit(solution)/shard_map/ppermute | solution.py:16
  79.0 0.9 %collective-permute-start.30 = (bf16[2,32,896]{2,1,0:T(8,128)(2,1)S(1)}, bf16[2,32,896]{2,1,0:T(8,128)(2,1)S(1)}, u32[]{:S(2)}, u32[]{:S(2)}) collective-permute-start(bf16[2,32,896]{2,1,0:T(8,128)(2,1)S(1)} %add_convert_fusion.2.before.mine), channel_id=1, source_target_pairs={{0,2},{2,0},{1,3},{3,1},{4,6},{6,4},{5,7},{7,5},{8,10},{10,8},{9,1... | collective-permute-start | bytes 344072 | tf_op jit(solution)/shard_map/ppermute | solution.py:16
  79.9 3.4 %shard_map.137 = (bf16[3584,1024]{1,0:T(8,128)(2,1)}, f32[8,128]{1,0:T(8,128)S(1)}) custom-call(bf16[3584,128]{1,0:T(8,128)(2,1)S(1)} %get-tuple-element.51.hidden, bf16[128,1024]{1,0:T(8,128)(2,1)S(1)} %constant_dynamic-update-slice_fusion.residual.before, bf16[2,32,896]{2,1,0:T(8,128)(2,1)S(1)} %add_convert_fusion.2.before.mine), custom_call_target="tpu_custom_call" | custom-call | flops 939524096 | bytes 7340032 | tf_op jit(solution)/shard_map/pallas_call | solution.py:480
  83.3 0.3 collective-permute-done.27.other
  83.6 0.2 shard_map.138.rest_0_
  83.9 1.3 %collective-permute-done.30.other = bf16[2,32,896]{2,1,0:T(8,128)(2,1)S(1)} collective-permute-done((bf16[2,32,896]{2,1,0:T(8,128)(2,1)S(1)}, bf16[2,32,896]{2,1,0:T(8,128)(2,1)S(1)}, u32[]{:S(2)}, u32[]{:S(2)}) %collective-permute-start.30) | collective-permute-done | bytes 114720 | tf_op jit(solution)/shard_map/ppermute | solution.py:16
  85.2 0.2 shard_map.139.rest_2_
  85.4 0.6 convert_element_type.81
  86.0 0.8 collective-permute-done.31.rest_3_
  86.9 6.5 %shard_map.140 = (bf16[1024,3584]{1,0:T(8,128)(2,1)}, bf16[1024,3584]{1,0:T(8,128)(2,1)}) custom-call(bf16[4,64,128]{2,1,0:T(8,128)(2,1)S(1)} %get-tuple-element.32.picker, bf16[1024,128]{1,0:T(8,128)(2,1)S(1)} %get-tuple-element.46.refs_8_.tokens, bf16[2,2,32,896]{3,2,1,0:T(8,128)(2,1)S(1)} %shard_map.138.rest_0_, ...), custom_call_target="tpu_custom_call" | custom-call | flops 1879048192 | bytes 14680064 | tf_op jit(solution)/shard_map/pallas_call | solution.py:530
  (61 shorter events, 1.1 us)
Async XLA Ops:
  0.6 11.7 %collective-permute-start = (bf16[32,1024]{1,0:T(8,128)(2,1)}, bf16[32,1024]{1,0:T(8,128)(2,1)S(1)}, u32[]{:S(2)}, u32[]{:S(2)}) collective-permute-start(bf16[32,1024]{1,0:T(8,128)(2,1)} %param.9), channel_id=1, source_target_pairs={{0,4},{4,0},{8,12},{12,8},{1,5},{5,1},{9,13},{13,9},{2,6},{6,2},{1... | collective-permute-start | bytes 196616 | tf_op jit(solution)/shard_map/ppermute | solution.py:617
  3.7 9.2 %collective-permute-start.2 = (bf16[32,1024]{1,0:T(8,128)(2,1)}, bf16[32,1024]{1,0:T(8,128)(2,1)S(1)}, u32[]{:S(2)}, u32[]{:S(2)}) collective-permute-start(bf16[32,1024]{1,0:T(8,128)(2,1)} %param.9), channel_id=1, source_target_pairs={{0,12},{4,8},{8,4},{12,0},{1,13},{5,9},{9,5},{13,1},{2,14},{6,10},... | collective-permute-start | bytes 196616 | tf_op jit(solution)/shard_map/ppermute | solution.py:617
  6.2 6.7 %collective-permute-start.1 = (bf16[32,1024]{1,0:T(8,128)(2,1)}, bf16[32,1024]{1,0:T(8,128)(2,1)S(1)}, u32[]{:S(2)}, u32[]{:S(2)}) collective-permute-start(bf16[32,1024]{1,0:T(8,128)(2,1)} %param.9), channel_id=1, source_target_pairs={{0,8},{4,12},{8,0},{12,4},{1,9},{5,13},{9,1},{13,5},{2,10},{6,14},... | collective-permute-start | bytes 196616 | tf_op jit(solution)/shard_map/ppermute | solution.py:617
  6.4 5.9 %copy-start = (bf16[32,1024]{1,0:T(8,128)(2,1)S(1)}, bf16[32,1024]{1,0:T(8,128)(2,1)}, u32[]{:S(2)}) copy-start(bf16[32,1024]{1,0:T(8,128)(2,1)} %param.9) | copy-start | bytes 196612
  14.6 2.3 %collective-permute-start.8 = (bf16[2,64,1792]{2,1,0:T(8,128)(2,1)S(1)}, bf16[2,64,1792]{2,1,0:T(8,128)(2,1)S(1)}, u32[]{:S(2)}, u32[]{:S(2)}) collective-permute-start(bf16[2,64,1792]{2,1,0:T(8,128)(2,1)S(1)} %get-tuple-element.43), channel_id=1, source_target_pairs={{0,1},{1,0},{2,3},{3,2},{4,5},{5,4},{6,7},{7,6},{8,9},{9,8},{10,11... | collective-permute-start | bytes 1376264 | tf_op jit(solution)/shard_map/ppermute | solution.py:16
  16.3 2.3 %collective-permute-start.3 = (bf16[2,64,1792]{2,1,0:T(8,128)(2,1)S(1)}, bf16[2,64,1792]{2,1,0:T(8,128)(2,1)S(1)}, u32[]{:S(2)}, u32[]{:S(2)}) collective-permute-start(bf16[2,64,1792]{2,1,0:T(8,128)(2,1)S(1)} %get-tuple-element.36), channel_id=1, source_target_pairs={{0,1},{1,0},{2,3},{3,2},{4,5},{5,4},{6,7},{7,6},{8,9},{9,8},{10,11... | collective-permute-start | bytes 1376264 | tf_op jit(solution)/shard_map/ppermute | solution.py:16
  17.0 9.7 %collective-permute-start.9 = (bf16[2,32,1792]{2,1,0:T(8,128)(2,1)S(1)}, bf16[2,32,1792]{2,1,0:T(8,128)(2,1)S(1)}, u32[]{:S(2)}, u32[]{:S(2)}) collective-permute-start(bf16[2,32,1792]{2,1,0:T(8,128)(2,1)S(1)} %slice.33), channel_id=1, source_target_pairs={{0,2},{2,0},{1,3},{3,1},{4,6},{6,4},{5,7},{7,5},{8,10},{10,8},{9,1... | collective-permute-start | bytes 688136 | tf_op jit(solution)/shard_map/ppermute | solution.py:16
  18.7 10.8 %collective-permute-start.12 = (bf16[2,32,1792]{2,1,0:T(8,128)(2,1)S(1)}, bf16[2,32,1792]{2,1,0:T(8,128)(2,1)S(1)}, u32[]{:S(2)}, u32[]{:S(2)}) collective-permute-start(bf16[2,32,1792]{2,1,0:T(8,128)(2,1)S(1)} %slice.37), channel_id=1, source_target_pairs={{0,2},{2,0},{1,3},{3,1},{4,6},{6,4},{5,7},{7,5},{8,10},{10,8},{9,1... | collective-permute-start | bytes 688136 | tf_op jit(solution)/shard_map/ppermute | solution.py:16
  20.1 17.8 %slice-start.2 = ((s8[7340032]{0:T(1024)(128)(4,1)}), s8[4194304]{0:T(1024)(128)(4,1)S(1)}, s32[]{:S(2)}) async-start(s8[7340032]{0:T(1024)(128)(4,1)} %bitcast.33), calls=%async_computation.2 | async-start | bytes 8388608
  20.1 17.8 %slice-start.3 = ((s8[7340032]{0:T(1024)(128)(4,1)}), s8[3145728]{0:T(1024)(128)(4,1)S(1)}, s32[]{:S(2)}) async-start(s8[7340032]{0:T(1024)(128)(4,1)} %bitcast.33), calls=%async_computation.3 | async-start | bytes 6291456
  26.6 4.8 %collective-permute-start.5 = (bf16[4,2,16,896]{3,2,1,0:T(8,128)(2,1)S(1)}, bf16[4,2,16,896]{3,2,1,0:T(8,128)(2,1)S(1)}, u32[]{:S(2)}, u32[]{:S(2)}) collective-permute-start(bf16[4,2,16,896]{3,2,1,0:T(8,128)(2,1)S(1)} %get-tuple-element.40), channel_id=1, source_target_pairs={{0,1},{1,0},{2,3},{3,2},{4,5},{5,4},{6,7},{7,6},{8,9},{9,8},{10,11... | collective-permute-start | bytes 688136 | tf_op jit(solution)/shard_map/ppermute | solution.py:16
  26.9 6.0 %collective-permute-start.10 = (bf16[32,1792]{1,0:T(8,128)(2,1)S(1)}, bf16[32,1792]{1,0:T(8,128)(2,1)S(1)}, u32[]{:S(2)}, u32[]{:S(2)}) collective-permute-start(bf16[32,1792]{1,0:T(8,128)(2,1)S(1)} %fusion.3.refs_0_), channel_id=1, source_target_pairs={{0,2},{2,0},{1,3},{3,1},{4,6},{6,4},{5,7},{7,5},{8,10},{10,8},{9,1... | collective-permute-start | bytes 344072 | tf_op jit(solution)/shard_map/ppermute | solution.py:16
  29.7 5.2 %collective-permute-start.13 = (bf16[32,1792]{1,0:T(8,128)(2,1)S(1)}, bf16[32,1792]{1,0:T(8,128)(2,1)S(1)}, u32[]{:S(2)}, u32[]{:S(2)}) collective-permute-start(bf16[32,1792]{1,0:T(8,128)(2,1)S(1)} %fusion.1.refs_0_), channel_id=1, source_target_pairs={{0,2},{2,0},{1,3},{3,1},{4,6},{6,4},{5,7},{7,5},{8,10},{10,8},{9,1... | collective-permute-start | bytes 344072 | tf_op jit(solution)/shard_map/ppermute | solution.py:16
  31.4 5.0 %collective-permute-start.4 = (bf16[4,2,16,896]{3,2,1,0:T(8,128)(2,1)S(1)}, bf16[4,2,16,896]{3,2,1,0:T(8,128)(2,1)S(1)}, u32[]{:S(2)}, u32[]{:S(2)}) collective-permute-start(bf16[4,2,16,896]{3,2,1,0:T(8,128)(2,1)S(1)} %get-tuple-element.38), channel_id=1, source_target_pairs={{0,1},{1,0},{2,3},{3,2},{4,5},{5,4},{6,7},{7,6},{8,9},{9,8},{10,11... | collective-permute-start | bytes 688136 | tf_op jit(solution)/shard_map/ppermute | solution.py:16
  33.0 4.3 %collective-permute-start.11 = (bf16[64,1792]{1,0:T(8,128)(2,1)S(1)}, bf16[64,1792]{1,0:T(8,128)(2,1)S(1)}, u32[]{:S(2)}, u32[]{:S(2)}) collective-permute-start(bf16[64,1792]{1,0:T(8,128)(2,1)S(1)} %shard_map.126.refs_0_), channel_id=1, source_target_pairs={{0,1},{1,0},{2,3},{3,2},{4,5},{5,4},{6,7},{7,6},{8,9},{9,8},{10,11... | collective-permute-start | bytes 688136 | tf_op jit(solution)/shard_map/ppermute | solution.py:16
  35.0 2.3 %collective-permute-start.14 = (bf16[64,1792]{1,0:T(8,128)(2,1)S(1)}, bf16[64,1792]{1,0:T(8,128)(2,1)S(1)}, u32[]{:S(2)}, u32[]{:S(2)}) collective-permute-start(bf16[64,1792]{1,0:T(8,128)(2,1)S(1)} %shard_map.127.refs_2_), channel_id=1, source_target_pairs={{0,1},{1,0},{2,3},{3,2},{4,5},{5,4},{6,7},{7,6},{8,9},{9,8},{10,11... | collective-permute-start | bytes 688136 | tf_op jit(solution)/shard_map/ppermute | solution.py:16
  35.0 8.5 %collective-permute-start.7 = (bf16[4,2,16,896]{3,2,1,0:T(8,128)(2,1)S(1)}, bf16[4,2,16,896]{3,2,1,0:T(8,128)(2,1)S(1)}, u32[]{:S(2)}, u32[]{:S(2)}) collective-permute-start(bf16[4,2,16,896]{3,2,1,0:T(8,128)(2,1)S(1)} %shard_map.123.before.refs_2_.mine), channel_id=1, source_target_pairs={{0,2},{2,0},{1,3},{3,1},{4,6},{6,4},{5,7},{7,5},{8,10},{10,8},{9,1... | collective-permute-start | bytes 688136 | tf_op jit(solution)/shard_map/ppermute | solution.py:16
  36.5 11.7 %collective-permute-start.6 = (bf16[4,2,16,896]{3,2,1,0:T(8,128)(2,1)S(1)}, bf16[4,2,16,896]{3,2,1,0:T(8,128)(2,1)S(1)}, u32[]{:S(2)}, u32[]{:S(2)}) collective-permute-start(bf16[4,2,16,896]{3,2,1,0:T(8,128)(2,1)S(1)} %shard_map.124.mine), channel_id=1, source_target_pairs={{0,2},{2,0},{1,3},{3,1},{4,6},{6,4},{5,7},{7,5},{8,10},{10,8},{9,1... | collective-permute-start | bytes 688136 | tf_op jit(solution)/shard_map/ppermute | solution.py:16
  39.1 6.5 %collective-permute-start.16 = (bf16[32,1024]{1,0:T(8,128)(2,1)S(1)}, bf16[32,1024]{1,0:T(8,128)(2,1)S(1)}, u32[]{:S(2)}, u32[]{:S(2)}) collective-permute-start(bf16[32,1024]{1,0:T(8,128)(2,1)S(1)} %get-tuple-element.62), channel_id=1, source_target_pairs={{0,12},{4,8},{8,4},{12,0},{1,13},{5,9},{9,5},{13,1},{2,14},{6,10},... | collective-permute-start | bytes 196616 | tf_op jit(solution)/shard_map/ppermute | solution.py:617
  41.6 4.7 %collective-permute-start.15 = (bf16[32,1024]{1,0:T(8,128)(2,1)S(1)}, bf16[32,1024]{1,0:T(8,128)(2,1)S(1)}, u32[]{:S(2)}, u32[]{:S(2)}) collective-permute-start(bf16[32,1024]{1,0:T(8,128)(2,1)S(1)} %get-tuple-element.63), channel_id=1, source_target_pairs={{0,4},{4,0},{8,12},{12,8},{1,5},{5,1},{9,13},{13,9},{2,6},{6,2},{1... | collective-permute-start | bytes 196616 | tf_op jit(solution)/shard_map/ppermute | solution.py:617
  46.4 1.4 %collective-permute-start.17 = (bf16[4,16,896]{2,1,0:T(8,128)(2,1)S(1)}, bf16[4,16,896]{2,1,0:T(8,128)(2,1)S(1)}, u32[]{:S(2)}, u32[]{:S(2)}) collective-permute-start(bf16[4,16,896]{2,1,0:T(8,128)(2,1)S(1)} %get-tuple-element.44.mine), channel_id=1, source_target_pairs={{0,1},{1,0},{2,3},{3,2},{4,5},{5,4},{6,7},{7,6},{8,9},{9,8},{10,11... | collective-permute-start | bytes 344072 | tf_op jit(solution)/shard_map/ppermute | solution.py:16
  46.5 16.7 %collective-permute-start.22 = (bf16[32,1024]{1,0:T(8,128)(2,1)S(1)}, bf16[32,1024]{1,0:T(8,128)(2,1)S(1)}, u32[]{:S(2)}, u32[]{:S(2)}) collective-permute-start(bf16[32,1024]{1,0:T(8,128)(2,1)S(1)} %get-tuple-element.60), channel_id=1, source_target_pairs={{0,8},{4,12},{8,0},{12,4},{1,9},{5,13},{9,1},{13,5},{2,10},{6,14},... | collective-permute-start | bytes 196616 | tf_op jit(solution)/shard_map/ppermute | solution.py:617
  48.3 7.5 %collective-permute-start.18 = (bf16[4,16,896]{2,1,0:T(8,128)(2,1)S(1)}, bf16[4,16,896]{2,1,0:T(8,128)(2,1)S(1)}, u32[]{:S(2)}, u32[]{:S(2)}) collective-permute-start(bf16[4,16,896]{2,1,0:T(8,128)(2,1)S(1)} %get-tuple-element.45.mine), channel_id=1, source_target_pairs={{0,1},{1,0},{2,3},{3,2},{4,5},{5,4},{6,7},{7,6},{8,9},{9,8},{10,11... | collective-permute-start | bytes 344072 | tf_op jit(solution)/shard_map/ppermute | solution.py:16
  48.5 25.5 %slice-start = ((s8[7340032]{0:T(1024)(128)(4,1)}), s8[4194304]{0:T(1024)(128)(4,1)S(1)}, s32[]{:S(2)}) async-start(s8[7340032]{0:T(1024)(128)(4,1)} %bitcast.31), calls=%async_computation | async-start | bytes 8388608
  53.2 10.0 %collective-permute-start.21 = (bf16[32,1024]{1,0:T(8,128)(2,1)S(1)}, bf16[32,1024]{1,0:T(8,128)(2,1)S(1)}, u32[]{:S(2)}, u32[]{:S(2)}) collective-permute-start(bf16[32,1024]{1,0:T(8,128)(2,1)S(1)} %get-tuple-element.64), channel_id=1, source_target_pairs={{0,12},{4,8},{8,4},{12,0},{1,13},{5,9},{9,5},{13,1},{2,14},{6,10},... | collective-permute-start | bytes 196616 | tf_op jit(solution)/shard_map/ppermute | solution.py:617
  55.3 7.8 %collective-permute-start.20 = (bf16[32,1024]{1,0:T(8,128)(2,1)S(1)}, bf16[32,1024]{1,0:T(8,128)(2,1)S(1)}, u32[]{:S(2)}, u32[]{:S(2)}) collective-permute-start(bf16[32,1024]{1,0:T(8,128)(2,1)S(1)} %get-tuple-element.65), channel_id=1, source_target_pairs={{0,8},{4,12},{8,0},{12,4},{1,9},{5,13},{9,1},{13,5},{2,10},{6,14},... | collective-permute-start | bytes 196616 | tf_op jit(solution)/shard_map/ppermute | solution.py:617
  56.3 17.7 %slice-start.1 = ((s8[7340032]{0:T(1024)(128)(4,1)}), s8[3145728]{0:T(1024)(128)(4,1)S(1)}, s32[]{:S(2)}) async-start(s8[7340032]{0:T(1024)(128)(4,1)} %bitcast.31), calls=%async_computation.1 | async-start | bytes 6291456
  60.9 4.3 %collective-permute-start.19 = (bf16[32,1024]{1,0:T(8,128)(2,1)S(1)}, bf16[32,1024]{1,0:T(8,128)(2,1)S(1)}, u32[]{:S(2)}, u32[]{:S(2)}) collective-permute-start(bf16[32,1024]{1,0:T(8,128)(2,1)S(1)} %get-tuple-element.66), channel_id=1, source_target_pairs={{0,4},{4,0},{8,12},{12,8},{1,5},{5,1},{9,13},{13,9},{2,6},{6,2},{1... | collective-permute-start | bytes 196616 | tf_op jit(solution)/shard_map/ppermute | solution.py:617
  65.3 8.6 %collective-permute-start.25 = (bf16[32,1024]{1,0:T(8,128)(2,1)S(1)}, bf16[32,1024]{1,0:T(8,128)(2,1)S(1)}, u32[]{:S(2)}, u32[]{:S(2)}) collective-permute-start(bf16[32,1024]{1,0:T(8,128)(2,1)S(1)} %get-tuple-element.48), channel_id=1, source_target_pairs={{0,12},{4,8},{8,4},{12,0},{1,13},{5,9},{9,5},{13,1},{2,14},{6,10},... | collective-permute-start | bytes 196616 | tf_op jit(solution)/shard_map/ppermute | solution.py:617
  67.7 6.2 %collective-permute-start.24 = (bf16[32,1024]{1,0:T(8,128)(2,1)S(1)}, bf16[32,1024]{1,0:T(8,128)(2,1)S(1)}, u32[]{:S(2)}, u32[]{:S(2)}) collective-permute-start(bf16[32,1024]{1,0:T(8,128)(2,1)S(1)} %get-tuple-element.48), channel_id=1, source_target_pairs={{0,8},{4,12},{8,0},{12,4},{1,9},{5,13},{9,1},{13,5},{2,10},{6,14},... | collective-permute-start | bytes 196616 | tf_op jit(solution)/shard_map/ppermute | solution.py:617
  68.7 4.3 %collective-permute-start.23 = (bf16[32,1024]{1,0:T(8,128)(2,1)S(1)}, bf16[32,1024]{1,0:T(8,128)(2,1)S(1)}, u32[]{:S(2)}, u32[]{:S(2)}) collective-permute-start(bf16[32,1024]{1,0:T(8,128)(2,1)S(1)} %get-tuple-element.48), channel_id=1, source_target_pairs={{0,4},{4,0},{8,12},{12,8},{1,5},{5,1},{9,13},{13,9},{2,6},{6,2},{1... | collective-permute-start | bytes 196616 | tf_op jit(solution)/shard_map/ppermute | solution.py:617
  75.5 2.0 %collective-permute-start.26 = (bf16[2,32,896]{2,1,0:T(8,128)(2,1)S(1)}, bf16[2,32,896]{2,1,0:T(8,128)(2,1)S(1)}, u32[]{:S(2)}, u32[]{:S(2)}) collective-permute-start(bf16[2,32,896]{2,1,0:T(8,128)(2,1)S(1)} %get-tuple-element.50), channel_id=1, source_target_pairs={{0,1},{1,0},{2,3},{3,2},{4,5},{5,4},{6,7},{7,6},{8,9},{9,8},{10,11... | collective-permute-start | bytes 344072 | tf_op jit(solution)/shard_map/ppermute | solution.py:16
  77.0 2.0 %collective-permute-start.28 = (bf16[2,32,896]{2,1,0:T(8,128)(2,1)S(1)}, bf16[2,32,896]{2,1,0:T(8,128)(2,1)S(1)}, u32[]{:S(2)}, u32[]{:S(2)}) collective-permute-start(bf16[2,32,896]{2,1,0:T(8,128)(2,1)S(1)} %get-tuple-element.53), channel_id=1, source_target_pairs={{0,1},{1,0},{2,3},{3,2},{4,5},{5,4},{6,7},{7,6},{8,9},{9,8},{10,11... | collective-permute-start | bytes 344072 | tf_op jit(solution)/shard_map/ppermute | solution.py:16
  77.6 6.1 %collective-permute-start.27 = (bf16[2,32,896]{2,1,0:T(8,128)(2,1)S(1)}, bf16[2,32,896]{2,1,0:T(8,128)(2,1)S(1)}, u32[]{:S(2)}, u32[]{:S(2)}) collective-permute-start(bf16[2,32,896]{2,1,0:T(8,128)(2,1)S(1)} %add_convert_fusion.3.mine), channel_id=1, source_target_pairs={{0,2},{2,0},{1,3},{3,1},{4,6},{6,4},{5,7},{7,5},{8,10},{10,8},{9,1... | collective-permute-start | bytes 344072 | tf_op jit(solution)/shard_map/ppermute | solution.py:16
  79.0 6.2 %collective-permute-start.30 = (bf16[2,32,896]{2,1,0:T(8,128)(2,1)S(1)}, bf16[2,32,896]{2,1,0:T(8,128)(2,1)S(1)}, u32[]{:S(2)}, u32[]{:S(2)}) collective-permute-start(bf16[2,32,896]{2,1,0:T(8,128)(2,1)S(1)} %add_convert_fusion.2.before.mine), channel_id=1, source_target_pairs={{0,2},{2,0},{1,3},{3,1},{4,6},{6,4},{5,7},{7,5},{8,10},{10,8},{9,1... | collective-permute-start | bytes 344072 | tf_op jit(solution)/shard_map/ppermute | solution.py:16
  83.8 2.2 %collective-permute-start.29 = (bf16[2,2,32,896]{3,2,1,0:T(8,128)(2,1)S(1)}, bf16[2,2,32,896]{3,2,1,0:T(8,128)(2,1)S(1)}, u32[]{:S(2)}, u32[]{:S(2)}) collective-permute-start(bf16[2,2,32,896]{3,2,1,0:T(8,128)(2,1)S(1)} %shard_map.138.rest_0_), channel_id=1, source_target_pairs={{0,1},{1,0},{2,3},{3,2},{4,5},{5,4},{6,7},{7,6},{8,9},{9,8},{10,11... | collective-permute-start | bytes 688136 | tf_op jit(solution)/shard_map/ppermute | solution.py:16
  85.3 1.6 %collective-permute-start.31 = (bf16[2,2,32,896]{3,2,1,0:T(8,128)(2,1)S(1)}, bf16[2,2,32,896]{3,2,1,0:T(8,128)(2,1)S(1)}, u32[]{:S(2)}, u32[]{:S(2)}) collective-permute-start(bf16[2,2,32,896]{3,2,1,0:T(8,128)(2,1)S(1)} %shard_map.139.rest_2_), channel_id=1, source_target_pairs={{0,1},{1,0},{2,3},{3,2},{4,5},{5,4},{6,7},{7,6},{8,9},{9,8},{10,11... | collective-permute-start | bytes 688136 | tf_op jit(solution)/shard_map/ppermute | solution.py:16

commit v16 on v12

--- a/solution.py
+++ b/solution.py
@@ -213,39 +213,27 @@
 def expert_kernel(cuts, picker, tokens, gate, up, before, *rest):
     outs, held, sems = rest[:-2], rest[-2], rest[-1]
     count, slots = picker.shape[:2]
-    depth, _, pieces = sems.shape
+    pieces = sems.shape[2]
     rows_each = gate.shape[0] // pieces
-
-    def copies(e, which):
-        weight = (gate, up)[which]
-        found = []
-        for p in range(pieces):
-            part = pl.ds(p * rows_each, rows_each)
-            found.append(
-                pltpu.make_async_copy(
-                    weight.at[part, pl.ds(e * H, H)],
-                    held.at[e % depth, which, part],
-                    sems.at[e % depth, which, p],
+    copies = {}
+    for e in range(count):
+        for which, weight in enumerate((gate, up)):
+            for p in range(pieces):
+                part = pl.ds(p * rows_each, rows_each)
+                columns = pl.ds(e * H, H)
+                copies[e, which, p] = pltpu.make_async_copy(
+                    weight.at[part, columns], held.at[e, which, part], sems.at[e, which, p]
                 )
-            )
-        return found
-
-    for e in range(min(depth, count)):
-        for which in range(2):
-            for copy in copies(e, which):
-                copy.start()
+                copies[e, which, p].start()
     for e in range(count):
         rows = dot(picker[e], tokens[...]).astype(BF)
         for which in range(2):
-            for copy in copies(e, which):
-                copy.wait()
-            product = dot(rows, held[e % depth, which]).astype(BF)
+            for p in range(pieces):
+                copies[e, which, p].wait()
+            product = dot(rows, held[e, which]).astype(BF)
             for i, (low, high) in enumerate(cuts):
                 outs[2 * i][e, which] = product[low:high]
                 outs[2 * i + 1][e, which] = product[slots // 2 + low : slots // 2 + high]
-            if e + depth < count:
-                for copy in copies(e + depth, which):
-                    copy.start()
 
 
 def expert_pre(picker, tokens, gate, up, before, cuts):
@@ -260,10 +248,10 @@
         out_specs=tuple(whole() for _ in outs),
         out_shape=tuple(outs),
         scratch_shapes=[
-            pltpu.VMEM((min(count, 2), 2, width, H), BF),
-            pltpu.SemaphoreType.DMA((min(count, 2), 2, 4)),
+            pltpu.VMEM((count, 2, width, H), BF),
+            pltpu.SemaphoreType.DMA((count, 2, 4)),
         ],
-        compiler_params=pltpu.CompilerParams(vmem_limit_bytes=12 * 1024 * 1024),
+        compiler_params=pltpu.CompilerParams(vmem_limit_bytes=24 * 1024 * 1024),
         cost_estimate=pl.CostEstimate(
             flops=count * 4 * slots * width * H,
             bytes_accessed=count * 4 * width * H,
@@ -682,12 +670,10 @@
     target = to_owners(product, 0, ranks, 0)
 
     pre, dense, student = [], [], []
-    wait = [target[1], target[-1]]
     for (mine, other, mode), cut, rows in zip(parts, cuts, token_cuts):
-        total, part = hidden_act(mine, other, mode, slot_weight, wait, cut[0])
+        total, part = hidden_act(mine, other, mode, slot_weight, [product], cut[0])
         pre.append(total)
         dense.append(spread(picker, part, shift(part, "pipe", pipes, 1), cut, rows))
-        wait = dense[-1:]
         product = jnp.dot(dense[-1], expert_down, preferred_element_type=F32).astype(BF)
         count = (rows[1] - rows[0]) // block
         student = to_owners(product, rows[0] // block, count, rows[0]) + student

time: 93.7 us -> 88.9 us (0.949)
  waiting for transfers between devices: 19.1 us -> 15.6 us
  matrix products: 10.4 us -> 7.29 us
  starting transfers between devices: 30.1 us -> 32.5 us
    dot_general x2, matrix products: 9.24 us -> 2.78 us  [body(): jnp.dot(dense[-1], expert_down, preferred_element_type=F32).astype(BF)]
    dot_general x1, matrix products: 1.12 us -> 4.51 us  [body(): jnp.dot(hidden, teacher_down, preferred_element_type=F32).astype(BF)]
    ppermute x20, waiting for transfers between devices: 9.74 us -> 7.73 us  [shift(): lax.ppermute(value, axis, [(i, (i + by) % count) for i in range(count)])]
    ppermute x12, waiting for transfers between devices: 9.38 us -> 7.83 us  [to_partner(): return lax.ppermute(value, 'expert', [(i, i ^ s) for i in range(ranks)])]
    ppermute x20, starting transfers between devices: 11.9 us -> 13.4 us  [shift(): lax.ppermute(value, axis, [(i, (i + by) % count) for i in range(count)])]
  transfers between devices with their start and end apart: 32 -> 32, of which waited for: 14 -> 11; matrix products, arithmetic and copies ran while one was open for 13% -> 10% of each run, Pallas kernels for 23% -> 23%
where the time goes in v16:
time: 88.9 us; the launch traced here: 88.7 us
  starting transfers between devices  32.5 us (37%)
  Pallas kernels  30.6 us (34%)
  waiting for transfers between devices  15.6 us (18%)
  matrix products  7.29 us (8%)
  between operations  1.29 us (1%)
  other arithmetic  1.24 us (1%)
    ppermute x12, starting transfers between devices, to_partner(): return lax.ppermute(value, 'expert', [(i, i ^ s) for i in range(ranks)])  19.1 us
    ppermute x20, starting transfers between devices, shift(): lax.ppermute(value, axis, [(i, (i + by) % count) for i in range(count)])  13.4 us
    ppermute x12, waiting for transfers between devices, to_partner(): return lax.ppermute(value, 'expert', [(i, i ^ s) for i in range(ranks)])  7.83 us
    ppermute x20, waiting for transfers between devices, shift(): lax.ppermute(value, axis, [(i, (i + by) % count) for i in range(count)])  7.73 us
    pallas_call x1, Pallas kernels, input_grads(): pl.pallas_call(functools.partial(input_grad_kernel, count // len(parts)),...  6.5 us
    pallas_call x1, Pallas kernels, expert_pre(): pl.pallas_call(functools.partial(expert_kernel, cuts), in_specs=[whole(),...  5.98 us
    pallas_call x1, Pallas kernels, prepare(): pl.pallas_call(functools.partial(prepare_kernel, near_first, ranks, capac...  5.89 us
    dot_general x1, matrix products, body(): jnp.dot(hidden, teacher_down, preferred_element_type=F32).astype(BF)  4.51 us
  transfers between devices with their start and end apart: 32, of which 11 were waited for; matrix products, arithmetic and copies ran while one was open for 10% of the time, Pallas kernels for 23%

profile of v16, /device:TPU:0, one launch (start us, length us, event | category | flops | bytes accessed | tf_op | source)
XLA Modules:
  0.0 88.7 jit_solution(10967759997567666853)
XLA Ops:
  0.6 3.1 %collective-permute-start = (bf16[32,1024]{1,0:T(8,128)(2,1)}, bf16[32,1024]{1,0:T(8,128)(2,1)S(1)}, u32[]{:S(2)}, u32[]{:S(2)}) collective-permute-start(bf16[32,1024]{1,0:T(8,128)(2,1)} %param.9), channel_id=1, source_target_pairs={{0,4},{4,0},{8,12},{12,8},{1,5},{5,1},{9,13},{13,9},{2,6},{6,2},{1... | collective-permute-start | bytes 196616 | tf_op jit(solution)/shard_map/ppermute | solution.py:605
  3.7 2.5 %collective-permute-start.2 = (bf16[32,1024]{1,0:T(8,128)(2,1)}, bf16[32,1024]{1,0:T(8,128)(2,1)S(1)}, u32[]{:S(2)}, u32[]{:S(2)}) collective-permute-start(bf16[32,1024]{1,0:T(8,128)(2,1)} %param.9), channel_id=1, source_target_pairs={{0,12},{4,8},{8,4},{12,0},{1,13},{5,9},{9,5},{13,1},{2,14},{6,10},... | collective-permute-start | bytes 196616 | tf_op jit(solution)/shard_map/ppermute | solution.py:605
  6.2 0.1 collective-permute-start.1
  6.3 0.1 pad_add_fusion.place
  6.4 5.9 %shard_map.120 = (bf16[4,64,128]{2,1,0:T(8,128)(2,1)S(1)}, f32[4,64,1]{2,1,0:T(8,128)S(1)}, bf16[1024,3584]{1,0:T(8,128)(2,1)S(1)}, bf16[1024,3584]{1,0:T(8,128)(2,1)S(1)}) custom-call(s32[3]{0:T(128)S(1)} %pad_add_fusion.place, s32[4,128]{1,0:T(4,128)} %bitcast.33, f32[4,128]{1,0:T(4,128)} %bitcast.34, bf16[1024,3584]{1,0:T(8,128)(2,1)} %gate.2, ...), custom_call_target="tpu_custom_call" | custom-call | bytes 14680064 | tf_op jit(solution)/shard_map/pallas_call | solution.py:131
  12.4 0.5 collective-permute-done.1
  12.9 1.7 %shard_map.125 = (bf16[2,64,1792]{2,1,0:T(8,128)(2,1)S(1)}, bf16[2,64,1792]{2,1,0:T(8,128)(2,1)S(1)}) custom-call(s32[3]{0:T(128)S(1)} %pad_add_fusion.place, bf16[128,1024]{1,0:T(8,128)(2,1)S(1)} %constant_dynamic-update-slice_fusion.4.tokens.refs_2_, bf16[1024,3584]{1,0:T(8,128)(2,1)S(1)} %get-tuple-element.33.gate, ...), custom_call_target="tpu_custom_call" | custom-call | flops 939524096 | bytes 7340032 | tf_op jit(solution)/shard_map/pallas_call | solution.py:201
  14.6 0.1 collective-permute-start.8
  14.7 1.7 %shard_map.121 = (bf16[2,64,1792]{2,1,0:T(8,128)(2,1)S(1)}, bf16[2,64,1792]{2,1,0:T(8,128)(2,1)S(1)}) custom-call(s32[3]{0:T(128)S(1)} %pad_add_fusion.place, bf16[128,1024]{1,0:T(8,128)(2,1)S(1)} %constant_dynamic-update-slice_fusion.4.tokens.refs_2_, bf16[1024,3584]{1,0:T(8,128)(2,1)S(1)} %get-tuple-element.33.gate, ...), custom_call_target="tpu_custom_call" | custom-call | flops 939524096 | bytes 7340032 | tf_op jit(solution)/shard_map/pallas_call | solution.py:201
  16.3 0.6 collective-permute-start.3
  16.9 0.1 add_convert_fusion
  17.0 1.6 %collective-permute-start.9 = (bf16[2,32,1792]{2,1,0:T(8,128)(2,1)S(1)}, bf16[2,32,1792]{2,1,0:T(8,128)(2,1)S(1)}, u32[]{:S(2)}, u32[]{:S(2)}) collective-permute-start(bf16[2,32,1792]{2,1,0:T(8,128)(2,1)S(1)} %slice.33), channel_id=1, source_target_pairs={{0,2},{2,0},{1,3},{3,1},{4,6},{6,4},{5,7},{7,5},{8,10},{10,8},{9,1... | collective-permute-start | bytes 688136 | tf_op jit(solution)/shard_map/ppermute | solution.py:16
  18.6 0.1 add_convert_fusion.1.before
  18.7 1.3 %collective-permute-start.12 = (bf16[2,32,1792]{2,1,0:T(8,128)(2,1)S(1)}, bf16[2,32,1792]{2,1,0:T(8,128)(2,1)S(1)}, u32[]{:S(2)}, u32[]{:S(2)}) collective-permute-start(bf16[2,32,1792]{2,1,0:T(8,128)(2,1)S(1)} %slice.37), channel_id=1, source_target_pairs={{0,2},{2,0},{1,3},{3,1},{4,6},{6,4},{5,7},{7,5},{8,10},{10,8},{9,1... | collective-permute-start | bytes 688136 | tf_op jit(solution)/shard_map/ppermute | solution.py:16
  20.1 6.0 %shard_map.122 = (bf16[4,2,16,896]{3,2,1,0:T(8,128)(2,1)S(1)}, bf16[4,2,16,896]{3,2,1,0:T(8,128)(2,1)S(1)}, bf16[4,2,16,896]{3,2,1,0:T(8,128)(2,1)S(1)}, bf16[4,2,16,896]{3,2,1,0:T(8,128)(2,1)S(1)}) custom-call(bf16[4,64,128]{2,1,0:T(8,128)(2,1)S(1)} %get-tuple-element.32.picker, bf16[128,1024]{1,0:T(8,128)(2,1)S(1)} %constant_dynamic-update-slice_fusion.4.tokens.refs_2_, ...), custom_call_target="tpu_custom_call" | custom-call | flops 939524096 | bytes 14680064 | tf_op jit(solution)/shard_map/pallas_call | solution.py:245
  26.1 0.1 collective-permute-start.5
  26.2 0.1 fusion.3.refs_0_
  26.3 0.9 %collective-permute-start.10 = (bf16[32,1792]{1,0:T(8,128)(2,1)S(1)}, bf16[32,1792]{1,0:T(8,128)(2,1)S(1)}, u32[]{:S(2)}, u32[]{:S(2)}) collective-permute-start(bf16[32,1792]{1,0:T(8,128)(2,1)S(1)} %fusion.3.refs_0_), channel_id=1, source_target_pairs={{0,2},{2,0},{1,3},{3,1},{4,6},{6,4},{5,7},{7,5},{8,10},{10,8},{9,1... | collective-permute-start | bytes 344072 | tf_op jit(solution)/shard_map/ppermute | solution.py:16
  27.3 2.3 %collective-permute-done.12 = bf16[2,32,1792]{2,1,0:T(8,128)(2,1)S(1)} collective-permute-done((bf16[2,32,1792]{2,1,0:T(8,128)(2,1)S(1)}, bf16[2,32,1792]{2,1,0:T(8,128)(2,1)S(1)}, u32[]{:S(2)}, u32[]{:S(2)}) %collective-permute-start.12) | collective-permute-done | bytes 229408 | tf_op jit(solution)/shard_map/ppermute | solution.py:16
  29.7 0.1 fusion.1.refs_0_
  29.7 2.3 %collective-permute-start.13 = (bf16[32,1792]{1,0:T(8,128)(2,1)S(1)}, bf16[32,1792]{1,0:T(8,128)(2,1)S(1)}, u32[]{:S(2)}, u32[]{:S(2)}) collective-permute-start(bf16[32,1792]{1,0:T(8,128)(2,1)S(1)} %fusion.1.refs_0_), channel_id=1, source_target_pairs={{0,2},{2,0},{1,3},{3,1},{4,6},{6,4},{5,7},{7,5},{8,10},{10,8},{9,1... | collective-permute-start | bytes 344072 | tf_op jit(solution)/shard_map/ppermute | solution.py:16
  32.1 0.2 collective-permute-done.10.refs_1_
  32.4 0.3 collective-permute-start.11
  32.7 2.1 %collective-permute-done.13.refs_1_ = bf16[32,1792]{1,0:T(8,128)(2,1)S(1)} collective-permute-done((bf16[32,1792]{1,0:T(8,128)(2,1)S(1)}, bf16[32,1792]{1,0:T(8,128)(2,1)S(1)}, u32[]{:S(2)}, u32[]{:S(2)}) %collective-permute-start.13) | collective-permute-done | bytes 114720 | tf_op jit(solution)/shard_map/ppermute | solution.py:16
  34.9 2.1 %collective-permute-start.7 = (bf16[4,2,16,896]{3,2,1,0:T(8,128)(2,1)S(1)}, bf16[4,2,16,896]{3,2,1,0:T(8,128)(2,1)S(1)}, u32[]{:S(2)}, u32[]{:S(2)}) collective-permute-start(bf16[4,2,16,896]{3,2,1,0:T(8,128)(2,1)S(1)} %shard_map.123.before.refs_2_.mine), channel_id=1, source_target_pairs={{0,2},{2,0},{1,3},{3,1},{4,6},{6,4},{5,7},{7,5},{8,10},{10,8},{9,1... | collective-permute-start | bytes 688136 | tf_op jit(solution)/shard_map/ppermute | solution.py:16
  37.1 0.1 collective-permute-start.6
  37.2 0.6 shard_map.128
  37.8 4.5 %convolution_convert_fusion.rest_0_ = bf16[128,1024]{1,0:T(8,128)(2,1)S(1)} fusion(bf16[128,3584]{1,0:T(8,128)(2,1)S(1)} %shard_map.128, bf16[3584,1024]{1,0:T(8,128)(2,1)} %param.14), kind=kOutput, calls=%fused_computation | convolution fusion | flops 939655168 | bytes 8519680 | tf_op jit(solution)/shard_map/dot_general | solution.py:669
  42.4 1.1 %collective-permute-done.7.other = bf16[4,2,16,896]{3,2,1,0:T(8,128)(2,1)S(1)} collective-permute-done((bf16[4,2,16,896]{3,2,1,0:T(8,128)(2,1)S(1)}, bf16[4,2,16,896]{3,2,1,0:T(8,128)(2,1)S(1)}, u32[]{:S(2)}, u32[]{:S(2)}) %collective-permute-start.7) | collective-permute-done | bytes 229408 | tf_op jit(solution)/shard_map/ppermute | solution.py:16
  43.5 0.1 shard_map.129
  43.6 0.1 collective-permute-start.15
  43.7 2.5 %collective-permute-start.22 = (bf16[32,1024]{1,0:T(8,128)(2,1)S(1)}, bf16[32,1024]{1,0:T(8,128)(2,1)S(1)}, u32[]{:S(2)}, u32[]{:S(2)}) collective-permute-start(bf16[32,1024]{1,0:T(8,128)(2,1)S(1)} %get-tuple-element.60), channel_id=1, source_target_pairs={{0,12},{4,8},{8,4},{12,0},{1,13},{5,9},{9,5},{13,1},{2,14},{6,10},... | collective-permute-start | bytes 196616 | tf_op jit(solution)/shard_map/ppermute | solution.py:605
  46.2 0.3 collective-permute-start.21
  46.6 1.6 %collective-permute-start.20 = (bf16[32,1024]{1,0:T(8,128)(2,1)S(1)}, bf16[32,1024]{1,0:T(8,128)(2,1)S(1)}, u32[]{:S(2)}, u32[]{:S(2)}) collective-permute-start(bf16[32,1024]{1,0:T(8,128)(2,1)S(1)} %get-tuple-element.62), channel_id=1, source_target_pairs={{0,4},{4,0},{8,12},{12,8},{1,5},{5,1},{9,13},{13,9},{2,6},{6,2},{1... | collective-permute-start | bytes 196616 | tf_op jit(solution)/shard_map/ppermute | solution.py:605
  48.2 0.4 shard_map.130.refs_1_
  48.6 1.4 %convolution_convert_fusion.2.rest_0_ = bf16[64,1024]{1,0:T(8,128)(2,1)S(1)} fusion(bf16[64,3584]{1,0:T(8,128)(2,1)S(1)} %shard_map.130.refs_1_, bf16[3584,1024]{1,0:T(8,128)(2,1)S(1)} %bitcast.32), kind=kOutput, calls=%fused_computation.2 | convolution fusion | flops 469827584 | bytes 7929856 | tf_op jit(solution)/shard_map/dot_general | solution.py:677
  50.0 0.1 shard_map.131
  50.1 0.1 collective-permute-start.16
  50.2 2.5 %collective-permute-start.19 = (bf16[32,1024]{1,0:T(8,128)(2,1)S(1)}, bf16[32,1024]{1,0:T(8,128)(2,1)S(1)}, u32[]{:S(2)}, u32[]{:S(2)}) collective-permute-start(bf16[32,1024]{1,0:T(8,128)(2,1)S(1)} %get-tuple-element.64), channel_id=1, source_target_pairs={{0,12},{4,8},{8,4},{12,0},{1,13},{5,9},{9,5},{13,1},{2,14},{6,10},... | collective-permute-start | bytes 196616 | tf_op jit(solution)/shard_map/ppermute | solution.py:605
  52.8 0.2 collective-permute-start.18
  53.0 0.4 shard_map.132.refs_0_
  53.4 1.4 %convolution_convert_fusion.1.refs_3_ = bf16[64,1024]{1,0:T(8,128)(2,1)S(1)} fusion(bf16[64,3584]{1,0:T(8,128)(2,1)S(1)} %shard_map.132.refs_0_, bf16[3584,1024]{1,0:T(8,128)(2,1)S(1)} %bitcast.32), kind=kOutput, calls=%fused_computation.1 | convolution fusion | flops 469827584 | bytes 7929856 | tf_op jit(solution)/shard_map/dot_general | solution.py:677
  54.8 1.8 %collective-permute-start.17 = (bf16[32,1024]{1,0:T(8,128)(2,1)S(1)}, bf16[32,1024]{1,0:T(8,128)(2,1)S(1)}, u32[]{:S(2)}, u32[]{:S(2)}) collective-permute-start(bf16[32,1024]{1,0:T(8,128)(2,1)S(1)} %get-tuple-element.66), channel_id=1, source_target_pairs={{0,4},{4,0},{8,12},{12,8},{1,5},{5,1},{9,13},{13,9},{2,6},{6,2},{1... | collective-permute-start | bytes 196616 | tf_op jit(solution)/shard_map/ppermute | solution.py:605
  56.6 0.4 shard_map.133
  57.0 2.5 %collective-permute-done.18.refs_2_ = bf16[32,1024]{1,0:T(8,128)(2,1)S(1)} collective-permute-done((bf16[32,1024]{1,0:T(8,128)(2,1)S(1)}, bf16[32,1024]{1,0:T(8,128)(2,1)S(1)}, u32[]{:S(2)}, u32[]{:S(2)}) %collective-permute-start.18) | collective-permute-done | bytes 65568 | tf_op jit(solution)/shard_map/ppermute | solution.py:605
  59.5 0.7 collective-permute-done.17.refs_1_
  60.2 0.1 shard_map.134
  60.3 2.4 %collective-permute-start.25 = (bf16[32,1024]{1,0:T(8,128)(2,1)S(1)}, bf16[32,1024]{1,0:T(8,128)(2,1)S(1)}, u32[]{:S(2)}, u32[]{:S(2)}) collective-permute-start(bf16[32,1024]{1,0:T(8,128)(2,1)S(1)} %get-tuple-element.48), channel_id=1, source_target_pairs={{0,12},{4,8},{8,4},{12,0},{1,13},{5,9},{9,5},{13,1},{2,14},{6,10},... | collective-permute-start | bytes 196616 | tf_op jit(solution)/shard_map/ppermute | solution.py:605
  62.7 2.0 %collective-permute-start.23 = (bf16[32,1024]{1,0:T(8,128)(2,1)S(1)}, bf16[32,1024]{1,0:T(8,128)(2,1)S(1)}, u32[]{:S(2)}, u32[]{:S(2)}) collective-permute-start(bf16[32,1024]{1,0:T(8,128)(2,1)S(1)} %get-tuple-element.48), channel_id=1, source_target_pairs={{0,4},{4,0},{8,12},{12,8},{1,5},{5,1},{9,13},{13,9},{2,6},{6,2},{1... | collective-permute-start | bytes 196616 | tf_op jit(solution)/shard_map/ppermute | solution.py:605
  64.8 2.6 %collective-permute-done.23 = bf16[32,1024]{1,0:T(8,128)(2,1)S(1)} collective-permute-done((bf16[32,1024]{1,0:T(8,128)(2,1)S(1)}, bf16[32,1024]{1,0:T(8,128)(2,1)S(1)}, u32[]{:S(2)}, u32[]{:S(2)}) %collective-permute-start.23) | collective-permute-done | bytes 65568 | tf_op jit(solution)/shard_map/ppermute | solution.py:605
  67.4 1.6 %collective-permute-done.24 = bf16[32,1024]{1,0:T(8,128)(2,1)S(1)} collective-permute-done((bf16[32,1024]{1,0:T(8,128)(2,1)S(1)}, bf16[32,1024]{1,0:T(8,128)(2,1)S(1)}, u32[]{:S(2)}, u32[]{:S(2)}) %collective-permute-start.24) | collective-permute-done | bytes 65568 | tf_op jit(solution)/shard_map/ppermute | solution.py:605
  69.0 1.5 %shard_map.135 = (bf16[2,32,896]{2,1,0:T(8,128)(2,1)S(1)}, bf16[2,32,896]{2,1,0:T(8,128)(2,1)S(1)}) custom-call(bf16[4,64,128]{2,1,0:T(8,128)(2,1)S(1)} %get-tuple-element.32.picker, bf16[128,1024]{1,0:T(8,128)(2,1)S(1)} %constant_dynamic-update-slice_fusion.residual.before, bf16[3584,1024]{1,0:T(8,128)(2,1)S(1)} %bitcast.32, ...), custom_call_target="tpu_custom_call" | custom-call | tf_op jit(solution)/shard_map/pallas_call | solution.py:416
  70.6 1.3 %shard_map.136 = (bf16[2,32,896]{2,1,0:T(8,128)(2,1)S(1)}, bf16[2,32,896]{2,1,0:T(8,128)(2,1)S(1)}) custom-call(bf16[4,64,128]{2,1,0:T(8,128)(2,1)S(1)} %get-tuple-element.32.picker, bf16[128,1024]{1,0:T(8,128)(2,1)S(1)} %constant_dynamic-update-slice_fusion.residual.before, bf16[3584,1024]{1,0:T(8,128)(2,1)S(1)} %bitcast.32, ...), custom_call_target="tpu_custom_call" | custom-call | tf_op jit(solution)/shard_map/pallas_call | solution.py:416
  71.9 0.6 collective-permute-start.28
  72.5 2.0 %collective-permute-start.27 = (bf16[2,32,896]{2,1,0:T(8,128)(2,1)S(1)}, bf16[2,32,896]{2,1,0:T(8,128)(2,1)S(1)}, u32[]{:S(2)}, u32[]{:S(2)}) collective-permute-start(bf16[2,32,896]{2,1,0:T(8,128)(2,1)S(1)} %add_convert_fusion.3.mine), channel_id=1, source_target_pairs={{0,2},{2,0},{1,3},{3,1},{4,6},{6,4},{5,7},{7,5},{8,10},{10,8},{9,1... | collective-permute-start | bytes 344072 | tf_op jit(solution)/shard_map/ppermute | solution.py:16
  74.6 0.9 %collective-permute-start.30 = (bf16[2,32,896]{2,1,0:T(8,128)(2,1)S(1)}, bf16[2,32,896]{2,1,0:T(8,128)(2,1)S(1)}, u32[]{:S(2)}, u32[]{:S(2)}) collective-permute-start(bf16[2,32,896]{2,1,0:T(8,128)(2,1)S(1)} %add_convert_fusion.2.before.mine), channel_id=1, source_target_pairs={{0,2},{2,0},{1,3},{3,1},{4,6},{6,4},{5,7},{7,5},{8,10},{10,8},{9,1... | collective-permute-start | bytes 344072 | tf_op jit(solution)/shard_map/ppermute | solution.py:16
  75.5 3.4 %shard_map.137 = (bf16[3584,1024]{1,0:T(8,128)(2,1)}, f32[8,128]{1,0:T(8,128)S(1)}) custom-call(bf16[3584,128]{1,0:T(8,128)(2,1)S(1)} %get-tuple-element.51.hidden, bf16[128,1024]{1,0:T(8,128)(2,1)S(1)} %constant_dynamic-update-slice_fusion.residual.before, bf16[2,32,896]{2,1,0:T(8,128)(2,1)S(1)} %add_convert_fusion.2.before.mine), custom_call_target="tpu_custom_call" | custom-call | flops 939524096 | bytes 7340032 | tf_op jit(solution)/shard_map/pallas_call | solution.py:468
  79.0 0.2 shard_map.138.rest_0_
  79.1 0.1 collective-permute-start.29
  79.3 1.1 %collective-permute-done.30.other = bf16[2,32,896]{2,1,0:T(8,128)(2,1)S(1)} collective-permute-done((bf16[2,32,896]{2,1,0:T(8,128)(2,1)S(1)}, bf16[2,32,896]{2,1,0:T(8,128)(2,1)S(1)}, u32[]{:S(2)}, u32[]{:S(2)}) %collective-permute-start.30) | collective-permute-done | bytes 114720 | tf_op jit(solution)/shard_map/ppermute | solution.py:16
  80.3 0.2 shard_map.139.rest_2_
  80.6 0.6 convert_element_type.81
  81.2 0.8 collective-permute-done.31.rest_3_
  82.1 6.5 %shard_map.140 = (bf16[1024,3584]{1,0:T(8,128)(2,1)}, bf16[1024,3584]{1,0:T(8,128)(2,1)}) custom-call(bf16[4,64,128]{2,1,0:T(8,128)(2,1)S(1)} %get-tuple-element.32.picker, bf16[1024,128]{1,0:T(8,128)(2,1)S(1)} %get-tuple-element.46.refs_8_.tokens, bf16[2,2,32,896]{3,2,1,0:T(8,128)(2,1)S(1)} %shard_map.138.rest_0_, ...), custom_call_target="tpu_custom_call" | custom-call | flops 1879048192 | bytes 14680064 | tf_op jit(solution)/shard_map/pallas_call | solution.py:518
  (56 shorter events, 0.9 us)
Async XLA Ops:
  0.6 11.7 %collective-permute-start = (bf16[32,1024]{1,0:T(8,128)(2,1)}, bf16[32,1024]{1,0:T(8,128)(2,1)S(1)}, u32[]{:S(2)}, u32[]{:S(2)}) collective-permute-start(bf16[32,1024]{1,0:T(8,128)(2,1)} %param.9), channel_id=1, source_target_pairs={{0,4},{4,0},{8,12},{12,8},{1,5},{5,1},{9,13},{13,9},{2,6},{6,2},{1... | collective-permute-start | bytes 196616 | tf_op jit(solution)/shard_map/ppermute | solution.py:605
  3.7 9.2 %collective-permute-start.2 = (bf16[32,1024]{1,0:T(8,128)(2,1)}, bf16[32,1024]{1,0:T(8,128)(2,1)S(1)}, u32[]{:S(2)}, u32[]{:S(2)}) collective-permute-start(bf16[32,1024]{1,0:T(8,128)(2,1)} %param.9), channel_id=1, source_target_pairs={{0,12},{4,8},{8,4},{12,0},{1,13},{5,9},{9,5},{13,1},{2,14},{6,10},... | collective-permute-start | bytes 196616 | tf_op jit(solution)/shard_map/ppermute | solution.py:605
  6.2 6.7 %collective-permute-start.1 = (bf16[32,1024]{1,0:T(8,128)(2,1)}, bf16[32,1024]{1,0:T(8,128)(2,1)S(1)}, u32[]{:S(2)}, u32[]{:S(2)}) collective-permute-start(bf16[32,1024]{1,0:T(8,128)(2,1)} %param.9), channel_id=1, source_target_pairs={{0,8},{4,12},{8,0},{12,4},{1,9},{5,13},{9,1},{13,5},{2,10},{6,14},... | collective-permute-start | bytes 196616 | tf_op jit(solution)/shard_map/ppermute | solution.py:605
  6.4 5.9 %copy-start = (bf16[32,1024]{1,0:T(8,128)(2,1)S(1)}, bf16[32,1024]{1,0:T(8,128)(2,1)}, u32[]{:S(2)}) copy-start(bf16[32,1024]{1,0:T(8,128)(2,1)} %param.9) | copy-start | bytes 196612
  14.6 2.3 %collective-permute-start.8 = (bf16[2,64,1792]{2,1,0:T(8,128)(2,1)S(1)}, bf16[2,64,1792]{2,1,0:T(8,128)(2,1)S(1)}, u32[]{:S(2)}, u32[]{:S(2)}) collective-permute-start(bf16[2,64,1792]{2,1,0:T(8,128)(2,1)S(1)} %get-tuple-element.43), channel_id=1, source_target_pairs={{0,1},{1,0},{2,3},{3,2},{4,5},{5,4},{6,7},{7,6},{8,9},{9,8},{10,11... | collective-permute-start | bytes 1376264 | tf_op jit(solution)/shard_map/ppermute | solution.py:16
  16.3 2.3 %collective-permute-start.3 = (bf16[2,64,1792]{2,1,0:T(8,128)(2,1)S(1)}, bf16[2,64,1792]{2,1,0:T(8,128)(2,1)S(1)}, u32[]{:S(2)}, u32[]{:S(2)}) collective-permute-start(bf16[2,64,1792]{2,1,0:T(8,128)(2,1)S(1)} %get-tuple-element.36), channel_id=1, source_target_pairs={{0,1},{1,0},{2,3},{3,2},{4,5},{5,4},{6,7},{7,6},{8,9},{9,8},{10,11... | collective-permute-start | bytes 1376264 | tf_op jit(solution)/shard_map/ppermute | solution.py:16
  17.0 9.2 %collective-permute-start.9 = (bf16[2,32,1792]{2,1,0:T(8,128)(2,1)S(1)}, bf16[2,32,1792]{2,1,0:T(8,128)(2,1)S(1)}, u32[]{:S(2)}, u32[]{:S(2)}) collective-permute-start(bf16[2,32,1792]{2,1,0:T(8,128)(2,1)S(1)} %slice.33), channel_id=1, source_target_pairs={{0,2},{2,0},{1,3},{3,1},{4,6},{6,4},{5,7},{7,5},{8,10},{10,8},{9,1... | collective-permute-start | bytes 688136 | tf_op jit(solution)/shard_map/ppermute | solution.py:16
  18.7 10.9 %collective-permute-start.12 = (bf16[2,32,1792]{2,1,0:T(8,128)(2,1)S(1)}, bf16[2,32,1792]{2,1,0:T(8,128)(2,1)S(1)}, u32[]{:S(2)}, u32[]{:S(2)}) collective-permute-start(bf16[2,32,1792]{2,1,0:T(8,128)(2,1)S(1)} %slice.37), channel_id=1, source_target_pairs={{0,2},{2,0},{1,3},{3,1},{4,6},{6,4},{5,7},{7,5},{8,10},{10,8},{9,1... | collective-permute-start | bytes 688136 | tf_op jit(solution)/shard_map/ppermute | solution.py:16
  26.1 6.0 %collective-permute-start.5 = (bf16[4,2,16,896]{3,2,1,0:T(8,128)(2,1)S(1)}, bf16[4,2,16,896]{3,2,1,0:T(8,128)(2,1)S(1)}, u32[]{:S(2)}, u32[]{:S(2)}) collective-permute-start(bf16[4,2,16,896]{3,2,1,0:T(8,128)(2,1)S(1)} %get-tuple-element.40), channel_id=1, source_target_pairs={{0,1},{1,0},{2,3},{3,2},{4,5},{5,4},{6,7},{7,6},{8,9},{9,8},{10,11... | collective-permute-start | bytes 688136 | tf_op jit(solution)/shard_map/ppermute | solution.py:16
  26.3 6.0 %collective-permute-start.10 = (bf16[32,1792]{1,0:T(8,128)(2,1)S(1)}, bf16[32,1792]{1,0:T(8,128)(2,1)S(1)}, u32[]{:S(2)}, u32[]{:S(2)}) collective-permute-start(bf16[32,1792]{1,0:T(8,128)(2,1)S(1)} %fusion.3.refs_0_), channel_id=1, source_target_pairs={{0,2},{2,0},{1,3},{3,1},{4,6},{6,4},{5,7},{7,5},{8,10},{10,8},{9,1... | collective-permute-start | bytes 344072 | tf_op jit(solution)/shard_map/ppermute | solution.py:16
  29.7 5.1 %collective-permute-start.13 = (bf16[32,1792]{1,0:T(8,128)(2,1)S(1)}, bf16[32,1792]{1,0:T(8,128)(2,1)S(1)}, u32[]{:S(2)}, u32[]{:S(2)}) collective-permute-start(bf16[32,1792]{1,0:T(8,128)(2,1)S(1)} %fusion.1.refs_0_), channel_id=1, source_target_pairs={{0,2},{2,0},{1,3},{3,1},{4,6},{6,4},{5,7},{7,5},{8,10},{10,8},{9,1... | collective-permute-start | bytes 344072 | tf_op jit(solution)/shard_map/ppermute | solution.py:16
  32.0 5.0 %collective-permute-start.4 = (bf16[4,2,16,896]{3,2,1,0:T(8,128)(2,1)S(1)}, bf16[4,2,16,896]{3,2,1,0:T(8,128)(2,1)S(1)}, u32[]{:S(2)}, u32[]{:S(2)}) collective-permute-start(bf16[4,2,16,896]{3,2,1,0:T(8,128)(2,1)S(1)} %get-tuple-element.38), channel_id=1, source_target_pairs={{0,1},{1,0},{2,3},{3,2},{4,5},{5,4},{6,7},{7,6},{8,9},{9,8},{10,11... | collective-permute-start | bytes 688136 | tf_op jit(solution)/shard_map/ppermute | solution.py:16
  32.4 4.8 %collective-permute-start.11 = (bf16[64,1792]{1,0:T(8,128)(2,1)S(1)}, bf16[64,1792]{1,0:T(8,128)(2,1)S(1)}, u32[]{:S(2)}, u32[]{:S(2)}) collective-permute-start(bf16[64,1792]{1,0:T(8,128)(2,1)S(1)} %shard_map.126.refs_0_), channel_id=1, source_target_pairs={{0,1},{1,0},{2,3},{3,2},{4,5},{5,4},{6,7},{7,6},{8,9},{9,8},{10,11... | collective-permute-start | bytes 688136 | tf_op jit(solution)/shard_map/ppermute | solution.py:16
  34.8 2.4 %collective-permute-start.14 = (bf16[64,1792]{1,0:T(8,128)(2,1)S(1)}, bf16[64,1792]{1,0:T(8,128)(2,1)S(1)}, u32[]{:S(2)}, u32[]{:S(2)}) collective-permute-start(bf16[64,1792]{1,0:T(8,128)(2,1)S(1)} %shard_map.127.refs_2_), channel_id=1, source_target_pairs={{0,1},{1,0},{2,3},{3,2},{4,5},{5,4},{6,7},{7,6},{8,9},{9,8},{10,11... | collective-permute-start | bytes 688136 | tf_op jit(solution)/shard_map/ppermute | solution.py:16
  34.9 8.5 %collective-permute-start.7 = (bf16[4,2,16,896]{3,2,1,0:T(8,128)(2,1)S(1)}, bf16[4,2,16,896]{3,2,1,0:T(8,128)(2,1)S(1)}, u32[]{:S(2)}, u32[]{:S(2)}) collective-permute-start(bf16[4,2,16,896]{3,2,1,0:T(8,128)(2,1)S(1)} %shard_map.123.before.refs_2_.mine), channel_id=1, source_target_pairs={{0,2},{2,0},{1,3},{3,1},{4,6},{6,4},{5,7},{7,5},{8,10},{10,8},{9,1... | collective-permute-start | bytes 688136 | tf_op jit(solution)/shard_map/ppermute | solution.py:16
  37.1 12.9 %collective-permute-start.6 = (bf16[4,2,16,896]{3,2,1,0:T(8,128)(2,1)S(1)}, bf16[4,2,16,896]{3,2,1,0:T(8,128)(2,1)S(1)}, u32[]{:S(2)}, u32[]{:S(2)}) collective-permute-start(bf16[4,2,16,896]{3,2,1,0:T(8,128)(2,1)S(1)} %shard_map.124.mine), channel_id=1, source_target_pairs={{0,2},{2,0},{1,3},{3,1},{4,6},{6,4},{5,7},{7,5},{8,10},{10,8},{9,1... | collective-permute-start | bytes 688136 | tf_op jit(solution)/shard_map/ppermute | solution.py:16
  37.2 11.4 %slice-start = ((s8[7340032]{0:T(1024)(128)(4,1)}), s8[4194304]{0:T(1024)(128)(4,1)S(1)}, s32[]{:S(2)}) async-start(s8[7340032]{0:T(1024)(128)(4,1)} %bitcast.31), calls=%async_computation | async-start | bytes 8388608
  37.8 10.8 %slice-start.1 = ((s8[7340032]{0:T(1024)(128)(4,1)}), s8[3145728]{0:T(1024)(128)(4,1)S(1)}, s32[]{:S(2)}) async-start(s8[7340032]{0:T(1024)(128)(4,1)} %bitcast.31), calls=%async_computation.1 | async-start | bytes 6291456
  43.6 4.6 %collective-permute-start.15 = (bf16[4,16,896]{2,1,0:T(8,128)(2,1)S(1)}, bf16[4,16,896]{2,1,0:T(8,128)(2,1)S(1)}, u32[]{:S(2)}, u32[]{:S(2)}) collective-permute-start(bf16[4,16,896]{2,1,0:T(8,128)(2,1)S(1)} %get-tuple-element.44.mine), channel_id=1, source_target_pairs={{0,1},{1,0},{2,3},{3,2},{4,5},{5,4},{6,7},{7,6},{8,9},{9,8},{10,11... | collective-permute-start | bytes 344072 | tf_op jit(solution)/shard_map/ppermute | solution.py:16
  43.7 11.1 %collective-permute-start.22 = (bf16[32,1024]{1,0:T(8,128)(2,1)S(1)}, bf16[32,1024]{1,0:T(8,128)(2,1)S(1)}, u32[]{:S(2)}, u32[]{:S(2)}) collective-permute-start(bf16[32,1024]{1,0:T(8,128)(2,1)S(1)} %get-tuple-element.60), channel_id=1, source_target_pairs={{0,12},{4,8},{8,4},{12,0},{1,13},{5,9},{9,5},{13,1},{2,14},{6,10},... | collective-permute-start | bytes 196616 | tf_op jit(solution)/shard_map/ppermute | solution.py:605
  46.2 10.8 %collective-permute-start.21 = (bf16[32,1024]{1,0:T(8,128)(2,1)S(1)}, bf16[32,1024]{1,0:T(8,128)(2,1)S(1)}, u32[]{:S(2)}, u32[]{:S(2)}) collective-permute-start(bf16[32,1024]{1,0:T(8,128)(2,1)S(1)} %get-tuple-element.61), channel_id=1, source_target_pairs={{0,8},{4,12},{8,0},{12,4},{1,9},{5,13},{9,1},{13,5},{2,10},{6,14},... | collective-permute-start | bytes 196616 | tf_op jit(solution)/shard_map/ppermute | solution.py:605
  46.6 10.4 %collective-permute-start.20 = (bf16[32,1024]{1,0:T(8,128)(2,1)S(1)}, bf16[32,1024]{1,0:T(8,128)(2,1)S(1)}, u32[]{:S(2)}, u32[]{:S(2)}) collective-permute-start(bf16[32,1024]{1,0:T(8,128)(2,1)S(1)} %get-tuple-element.62), channel_id=1, source_target_pairs={{0,4},{4,0},{8,12},{12,8},{1,5},{5,1},{9,13},{13,9},{2,6},{6,2},{1... | collective-permute-start | bytes 196616 | tf_op jit(solution)/shard_map/ppermute | solution.py:605
  50.1 2.6 %collective-permute-start.16 = (bf16[4,16,896]{2,1,0:T(8,128)(2,1)S(1)}, bf16[4,16,896]{2,1,0:T(8,128)(2,1)S(1)}, u32[]{:S(2)}, u32[]{:S(2)}) collective-permute-start(bf16[4,16,896]{2,1,0:T(8,128)(2,1)S(1)} %get-tuple-element.45.mine), channel_id=1, source_target_pairs={{0,1},{1,0},{2,3},{3,2},{4,5},{5,4},{6,7},{7,6},{8,9},{9,8},{10,11... | collective-permute-start | bytes 344072 | tf_op jit(solution)/shard_map/ppermute | solution.py:16
  50.2 6.8 %collective-permute-start.19 = (bf16[32,1024]{1,0:T(8,128)(2,1)S(1)}, bf16[32,1024]{1,0:T(8,128)(2,1)S(1)}, u32[]{:S(2)}, u32[]{:S(2)}) collective-permute-start(bf16[32,1024]{1,0:T(8,128)(2,1)S(1)} %get-tuple-element.64), channel_id=1, source_target_pairs={{0,12},{4,8},{8,4},{12,0},{1,13},{5,9},{9,5},{13,1},{2,14},{6,10},... | collective-permute-start | bytes 196616 | tf_op jit(solution)/shard_map/ppermute | solution.py:605
  52.8 6.7 %collective-permute-start.18 = (bf16[32,1024]{1,0:T(8,128)(2,1)S(1)}, bf16[32,1024]{1,0:T(8,128)(2,1)S(1)}, u32[]{:S(2)}, u32[]{:S(2)}) collective-permute-start(bf16[32,1024]{1,0:T(8,128)(2,1)S(1)} %get-tuple-element.65), channel_id=1, source_target_pairs={{0,8},{4,12},{8,0},{12,4},{1,9},{5,13},{9,1},{13,5},{2,10},{6,14},... | collective-permute-start | bytes 196616 | tf_op jit(solution)/shard_map/ppermute | solution.py:605
  54.8 5.3 %collective-permute-start.17 = (bf16[32,1024]{1,0:T(8,128)(2,1)S(1)}, bf16[32,1024]{1,0:T(8,128)(2,1)S(1)}, u32[]{:S(2)}, u32[]{:S(2)}) collective-permute-start(bf16[32,1024]{1,0:T(8,128)(2,1)S(1)} %get-tuple-element.66), channel_id=1, source_target_pairs={{0,4},{4,0},{8,12},{12,8},{1,5},{5,1},{9,13},{13,9},{2,6},{6,2},{1... | collective-permute-start | bytes 196616 | tf_op jit(solution)/shard_map/ppermute | solution.py:605
  60.3 8.7 %collective-permute-start.25 = (bf16[32,1024]{1,0:T(8,128)(2,1)S(1)}, bf16[32,1024]{1,0:T(8,128)(2,1)S(1)}, u32[]{:S(2)}, u32[]{:S(2)}) collective-permute-start(bf16[32,1024]{1,0:T(8,128)(2,1)S(1)} %get-tuple-element.48), channel_id=1, source_target_pairs={{0,12},{4,8},{8,4},{12,0},{1,13},{5,9},{9,5},{13,1},{2,14},{6,10},... | collective-permute-start | bytes 196616 | tf_op jit(solution)/shard_map/ppermute | solution.py:605
  62.7 6.2 %collective-permute-start.24 = (bf16[32,1024]{1,0:T(8,128)(2,1)S(1)}, bf16[32,1024]{1,0:T(8,128)(2,1)S(1)}, u32[]{:S(2)}, u32[]{:S(2)}) collective-permute-start(bf16[32,1024]{1,0:T(8,128)(2,1)S(1)} %get-tuple-element.48), channel_id=1, source_target_pairs={{0,8},{4,12},{8,0},{12,4},{1,9},{5,13},{9,1},{13,5},{2,10},{6,14},... | collective-permute-start | bytes 196616 | tf_op jit(solution)/shard_map/ppermute | solution.py:605
  62.7 4.7 %collective-permute-start.23 = (bf16[32,1024]{1,0:T(8,128)(2,1)S(1)}, bf16[32,1024]{1,0:T(8,128)(2,1)S(1)}, u32[]{:S(2)}, u32[]{:S(2)}) collective-permute-start(bf16[32,1024]{1,0:T(8,128)(2,1)S(1)} %get-tuple-element.48), channel_id=1, source_target_pairs={{0,4},{4,0},{8,12},{12,8},{1,5},{5,1},{9,13},{13,9},{2,6},{6,2},{1... | collective-permute-start | bytes 196616 | tf_op jit(solution)/shard_map/ppermute | solution.py:605
  70.5 2.0 %collective-permute-start.26 = (bf16[2,32,896]{2,1,0:T(8,128)(2,1)S(1)}, bf16[2,32,896]{2,1,0:T(8,128)(2,1)S(1)}, u32[]{:S(2)}, u32[]{:S(2)}) collective-permute-start(bf16[2,32,896]{2,1,0:T(8,128)(2,1)S(1)} %get-tuple-element.50), channel_id=1, source_target_pairs={{0,1},{1,0},{2,3},{3,2},{4,5},{5,4},{6,7},{7,6},{8,9},{9,8},{10,11... | collective-permute-start | bytes 344072 | tf_op jit(solution)/shard_map/ppermute | solution.py:16
  71.9 2.6 %collective-permute-start.28 = (bf16[2,32,896]{2,1,0:T(8,128)(2,1)S(1)}, bf16[2,32,896]{2,1,0:T(8,128)(2,1)S(1)}, u32[]{:S(2)}, u32[]{:S(2)}) collective-permute-start(bf16[2,32,896]{2,1,0:T(8,128)(2,1)S(1)} %get-tuple-element.53), channel_id=1, source_target_pairs={{0,1},{1,0},{2,3},{3,2},{4,5},{5,4},{6,7},{7,6},{8,9},{9,8},{10,11... | collective-permute-start | bytes 344072 | tf_op jit(solution)/shard_map/ppermute | solution.py:16
  72.5 6.4 %collective-permute-start.27 = (bf16[2,32,896]{2,1,0:T(8,128)(2,1)S(1)}, bf16[2,32,896]{2,1,0:T(8,128)(2,1)S(1)}, u32[]{:S(2)}, u32[]{:S(2)}) collective-permute-start(bf16[2,32,896]{2,1,0:T(8,128)(2,1)S(1)} %add_convert_fusion.3.mine), channel_id=1, source_target_pairs={{0,2},{2,0},{1,3},{3,1},{4,6},{6,4},{5,7},{7,5},{8,10},{10,8},{9,1... | collective-permute-start | bytes 344072 | tf_op jit(solution)/shard_map/ppermute | solution.py:16
  74.6 5.8 %collective-permute-start.30 = (bf16[2,32,896]{2,1,0:T(8,128)(2,1)S(1)}, bf16[2,32,896]{2,1,0:T(8,128)(2,1)S(1)}, u32[]{:S(2)}, u32[]{:S(2)}) collective-permute-start(bf16[2,32,896]{2,1,0:T(8,128)(2,1)S(1)} %add_convert_fusion.2.before.mine), channel_id=1, source_target_pairs={{0,2},{2,0},{1,3},{3,1},{4,6},{6,4},{5,7},{7,5},{8,10},{10,8},{9,1... | collective-permute-start | bytes 344072 | tf_op jit(solution)/shard_map/ppermute | solution.py:16
  79.1 2.1 %collective-permute-start.29 = (bf16[2,2,32,896]{3,2,1,0:T(8,128)(2,1)S(1)}, bf16[2,2,32,896]{3,2,1,0:T(8,128)(2,1)S(1)}, u32[]{:S(2)}, u32[]{:S(2)}) collective-permute-start(bf16[2,2,32,896]{3,2,1,0:T(8,128)(2,1)S(1)} %shard_map.138.rest_0_), channel_id=1, source_target_pairs={{0,1},{1,0},{2,3},{3,2},{4,5},{5,4},{6,7},{7,6},{8,9},{9,8},{10,11... | collective-permute-start | bytes 688136 | tf_op jit(solution)/shard_map/ppermute | solution.py:16
  80.5 1.6 %collective-permute-start.31 = (bf16[2,2,32,896]{3,2,1,0:T(8,128)(2,1)S(1)}, bf16[2,2,32,896]{3,2,1,0:T(8,128)(2,1)S(1)}, u32[]{:S(2)}, u32[]{:S(2)}) collective-permute-start(bf16[2,2,32,896]{3,2,1,0:T(8,128)(2,1)S(1)} %shard_map.139.rest_2_), channel_id=1, source_target_pairs={{0,1},{1,0},{2,3},{3,2},{4,5},{5,4},{6,7},{7,6},{8,9},{9,8},{10,11... | collective-permute-start | bytes 688136 | tf_op jit(solution)/shard_map/ppermute | solution.py:16

commit v17 on v12

--- a/solution.py
+++ b/solution.py
@@ -366,6 +366,7 @@
         out_specs=whole(),
         out_shape=jax.ShapeDtypeStruct((rows, width), BF),
         compiler_params=pltpu.CompilerParams(vmem_limit_bytes=8 * 1024 * 1024),
+        cost_estimate=pl.CostEstimate(flops=0, bytes_accessed=16 * 2**20, transcendentals=0),
     )(place, *flat)
 
 

time: 93.7 us -> 93.7 us (level)
  no operation moved by 1% of the time
where the time goes in v17:
time: 93.7 us; the launch traced here: 93.5 us
  Pallas kernels  31.2 us (33%)
  starting transfers between devices  30.1 us (32%)
  waiting for transfers between devices  19.1 us (20%)
  matrix products  10.4 us (11%)
  between operations  1.32 us (1%)
  other arithmetic  1.23 us (1%)
    ppermute x12, starting transfers between devices, to_partner(): return lax.ppermute(value, 'expert', [(i, i ^ s) for i in range(ranks)])  18.2 us
    ppermute x20, starting transfers between devices, shift(): lax.ppermute(value, axis, [(i, (i + by) % count) for i in range(count)])  11.9 us
    ppermute x20, waiting for transfers between devices, shift(): lax.ppermute(value, axis, [(i, (i + by) % count) for i in range(count)])  9.74 us
    ppermute x12, waiting for transfers between devices, to_partner(): return lax.ppermute(value, 'expert', [(i, i ^ s) for i in range(ranks)])  9.38 us
    dot_general x2, matrix products, body(): jnp.dot(dense[-1], expert_down, preferred_element_type=F32).astype(BF)  9.24 us
    pallas_call x1, Pallas kernels, expert_pre(): pl.pallas_call(functools.partial(expert_kernel, cuts), in_specs=[whole(),...  6.57 us
    pallas_call x1, Pallas kernels, input_grads(): pl.pallas_call(functools.partial(input_grad_kernel, count // len(parts)),...  6.5 us
    pallas_call x1, Pallas kernels, prepare(): pl.pallas_call(functools.partial(prepare_kernel, near_first, ranks, capac...  5.89 us
  transfers between devices with their start and end apart: 32, of which 14 were waited for; matrix products, arithmetic and copies ran while one was open for 13% of the time, Pallas kernels for 23%

profile of v17, /device:TPU:0, one launch (start us, length us, event | category | flops | bytes accessed | tf_op | source)
XLA Modules:
  0.0 93.5 jit_solution(3335218634445669556)
XLA Ops:
  0.6 3.1 %collective-permute-start = (bf16[32,1024]{1,0:T(8,128)(2,1)}, bf16[32,1024]{1,0:T(8,128)(2,1)S(1)}, u32[]{:S(2)}, u32[]{:S(2)}) collective-permute-start(bf16[32,1024]{1,0:T(8,128)(2,1)} %param.9), channel_id=1, source_target_pairs={{0,4},{4,0},{8,12},{12,8},{1,5},{5,1},{9,13},{13,9},{2,6},{6,2},{1... | collective-permute-start | bytes 196616 | tf_op jit(solution)/shard_map/ppermute | solution.py:618
  3.7 2.5 %collective-permute-start.2 = (bf16[32,1024]{1,0:T(8,128)(2,1)}, bf16[32,1024]{1,0:T(8,128)(2,1)S(1)}, u32[]{:S(2)}, u32[]{:S(2)}) collective-permute-start(bf16[32,1024]{1,0:T(8,128)(2,1)} %param.9), channel_id=1, source_target_pairs={{0,12},{4,8},{8,4},{12,0},{1,13},{5,9},{9,5},{13,1},{2,14},{6,10},... | collective-permute-start | bytes 196616 | tf_op jit(solution)/shard_map/ppermute | solution.py:618
  6.2 0.1 collective-permute-start.1
  6.3 0.1 pad_add_fusion.place
  6.4 5.9 %shard_map.120 = (bf16[4,64,128]{2,1,0:T(8,128)(2,1)S(1)}, f32[4,64,1]{2,1,0:T(8,128)S(1)}, bf16[1024,3584]{1,0:T(8,128)(2,1)S(1)}, bf16[1024,3584]{1,0:T(8,128)(2,1)S(1)}) custom-call(s32[3]{0:T(128)S(1)} %pad_add_fusion.place, s32[4,128]{1,0:T(4,128)} %bitcast.35, f32[4,128]{1,0:T(4,128)} %bitcast.36, bf16[1024,3584]{1,0:T(8,128)(2,1)} %gate.2, ...), custom_call_target="tpu_custom_call" | custom-call | bytes 14680064 | tf_op jit(solution)/shard_map/pallas_call | solution.py:131
  12.4 0.5 collective-permute-done.1
  12.9 1.7 %shard_map.125 = (bf16[2,64,1792]{2,1,0:T(8,128)(2,1)S(1)}, bf16[2,64,1792]{2,1,0:T(8,128)(2,1)S(1)}) custom-call(s32[3]{0:T(128)S(1)} %pad_add_fusion.place, bf16[128,1024]{1,0:T(8,128)(2,1)S(1)} %constant_dynamic-update-slice_fusion.4.tokens.refs_2_, bf16[1024,3584]{1,0:T(8,128)(2,1)S(1)} %get-tuple-element.33.gate, ...), custom_call_target="tpu_custom_call" | custom-call | flops 939524096 | bytes 7340032 | tf_op jit(solution)/shard_map/pallas_call | solution.py:201
  14.7 1.7 %shard_map.121 = (bf16[2,64,1792]{2,1,0:T(8,128)(2,1)S(1)}, bf16[2,64,1792]{2,1,0:T(8,128)(2,1)S(1)}) custom-call(s32[3]{0:T(128)S(1)} %pad_add_fusion.place, bf16[128,1024]{1,0:T(8,128)(2,1)S(1)} %constant_dynamic-update-slice_fusion.4.tokens.refs_2_, bf16[1024,3584]{1,0:T(8,128)(2,1)S(1)} %get-tuple-element.33.gate, ...), custom_call_target="tpu_custom_call" | custom-call | flops 939524096 | bytes 7340032 | tf_op jit(solution)/shard_map/pallas_call | solution.py:201
  16.3 0.6 collective-permute-start.3
  16.9 0.1 add_convert_fusion
  17.0 1.6 %collective-permute-start.9 = (bf16[2,32,1792]{2,1,0:T(8,128)(2,1)S(1)}, bf16[2,32,1792]{2,1,0:T(8,128)(2,1)S(1)}, u32[]{:S(2)}, u32[]{:S(2)}) collective-permute-start(bf16[2,32,1792]{2,1,0:T(8,128)(2,1)S(1)} %slice.33), channel_id=1, source_target_pairs={{0,2},{2,0},{1,3},{3,1},{4,6},{6,4},{5,7},{7,5},{8,10},{10,8},{9,1... | collective-permute-start | bytes 688136 | tf_op jit(solution)/shard_map/ppermute | solution.py:16
  18.6 0.1 add_convert_fusion.1.before
  18.7 1.3 %collective-permute-start.12 = (bf16[2,32,1792]{2,1,0:T(8,128)(2,1)S(1)}, bf16[2,32,1792]{2,1,0:T(8,128)(2,1)S(1)}, u32[]{:S(2)}, u32[]{:S(2)}) collective-permute-start(bf16[2,32,1792]{2,1,0:T(8,128)(2,1)S(1)} %slice.37), channel_id=1, source_target_pairs={{0,2},{2,0},{1,3},{3,1},{4,6},{6,4},{5,7},{7,5},{8,10},{10,8},{9,1... | collective-permute-start | bytes 688136 | tf_op jit(solution)/shard_map/ppermute | solution.py:16
  20.1 6.6 %shard_map.122 = (bf16[4,2,16,896]{3,2,1,0:T(8,128)(2,1)S(1)}, bf16[4,2,16,896]{3,2,1,0:T(8,128)(2,1)S(1)}, bf16[4,2,16,896]{3,2,1,0:T(8,128)(2,1)S(1)}, bf16[4,2,16,896]{3,2,1,0:T(8,128)(2,1)S(1)}) custom-call(bf16[4,64,128]{2,1,0:T(8,128)(2,1)S(1)} %get-tuple-element.32.picker, bf16[128,1024]{1,0:T(8,128)(2,1)S(1)} %constant_dynamic-update-slice_fusion.4.tokens.refs_2_, ...), custom_call_target="tpu_custom_call" | custom-call | flops 939524096 | bytes 14680064 | tf_op jit(solution)/shard_map/pallas_call | solution.py:257
  26.6 0.1 collective-permute-start.5
  26.8 0.1 fusion.3.refs_0_
  26.9 0.8 collective-permute-start.10
  27.7 1.9 %collective-permute-done.12 = bf16[2,32,1792]{2,1,0:T(8,128)(2,1)S(1)} collective-permute-done((bf16[2,32,1792]{2,1,0:T(8,128)(2,1)S(1)}, bf16[2,32,1792]{2,1,0:T(8,128)(2,1)S(1)}, u32[]{:S(2)}, u32[]{:S(2)}) %collective-permute-start.12) | collective-permute-done | bytes 229408 | tf_op jit(solution)/shard_map/ppermute | solution.py:16
  29.6 0.1 fusion.1.refs_0_
  29.7 1.8 %collective-permute-start.13 = (bf16[32,1792]{1,0:T(8,128)(2,1)S(1)}, bf16[32,1792]{1,0:T(8,128)(2,1)S(1)}, u32[]{:S(2)}, u32[]{:S(2)}) collective-permute-start(bf16[32,1792]{1,0:T(8,128)(2,1)S(1)} %fusion.1.refs_0_), channel_id=1, source_target_pairs={{0,2},{2,0},{1,3},{3,1},{4,6},{6,4},{5,7},{7,5},{8,10},{10,8},{9,1... | collective-permute-start | bytes 344072 | tf_op jit(solution)/shard_map/ppermute | solution.py:16
  31.5 1.4 %collective-permute-done.10.refs_1_ = bf16[32,1792]{1,0:T(8,128)(2,1)S(1)} collective-permute-done((bf16[32,1792]{1,0:T(8,128)(2,1)S(1)}, bf16[32,1792]{1,0:T(8,128)(2,1)S(1)}, u32[]{:S(2)}, u32[]{:S(2)}) %collective-permute-start.10) | collective-permute-done | bytes 114720 | tf_op jit(solution)/shard_map/ppermute | solution.py:16
  33.0 1.9 %collective-permute-done.13.refs_1_ = bf16[32,1792]{1,0:T(8,128)(2,1)S(1)} collective-permute-done((bf16[32,1792]{1,0:T(8,128)(2,1)S(1)}, bf16[32,1792]{1,0:T(8,128)(2,1)S(1)}, u32[]{:S(2)}, u32[]{:S(2)}) %collective-permute-start.13) | collective-permute-done | bytes 114720 | tf_op jit(solution)/shard_map/ppermute | solution.py:16
  35.0 1.4 %collective-permute-start.7 = (bf16[4,2,16,896]{3,2,1,0:T(8,128)(2,1)S(1)}, bf16[4,2,16,896]{3,2,1,0:T(8,128)(2,1)S(1)}, u32[]{:S(2)}, u32[]{:S(2)}) collective-permute-start(bf16[4,2,16,896]{3,2,1,0:T(8,128)(2,1)S(1)} %shard_map.123.before.refs_2_.mine), channel_id=1, source_target_pairs={{0,2},{2,0},{1,3},{3,1},{4,6},{6,4},{5,7},{7,5},{8,10},{10,8},{9,1... | collective-permute-start | bytes 688136 | tf_op jit(solution)/shard_map/ppermute | solution.py:16
  36.5 0.8 collective-permute-start.6
  37.3 0.6 shard_map.128
  37.9 1.1 %convolution_convert_fusion = bf16[128,1024]{1,0:T(8,128)(2,1)S(1)} fusion(bf16[128,3584]{1,0:T(8,128)(2,1)S(1)} %shard_map.128, bf16[3584,1024]{1,0:T(8,128)(2,1)S(1)} %bitcast.34), kind=kOutput, calls=%fused_computation | convolution fusion | flops 939655168 | bytes 8519680 | tf_op jit(solution)/shard_map/dot_general | solution.py:682
  39.1 2.5 %collective-permute-start.16 = (bf16[32,1024]{1,0:T(8,128)(2,1)S(1)}, bf16[32,1024]{1,0:T(8,128)(2,1)S(1)}, u32[]{:S(2)}, u32[]{:S(2)}) collective-permute-start(bf16[32,1024]{1,0:T(8,128)(2,1)S(1)} %get-tuple-element.62), channel_id=1, source_target_pairs={{0,12},{4,8},{8,4},{12,0},{1,13},{5,9},{9,5},{13,1},{2,14},{6,10},... | collective-permute-start | bytes 196616 | tf_op jit(solution)/shard_map/ppermute | solution.py:618
  41.6 0.5 collective-permute-start.15
  42.0 1.5 %collective-permute-done.7.other = bf16[4,2,16,896]{3,2,1,0:T(8,128)(2,1)S(1)} collective-permute-done((bf16[4,2,16,896]{3,2,1,0:T(8,128)(2,1)S(1)}, bf16[4,2,16,896]{3,2,1,0:T(8,128)(2,1)S(1)}, u32[]{:S(2)}, u32[]{:S(2)}) %collective-permute-start.7) | collective-permute-done | bytes 229408 | tf_op jit(solution)/shard_map/ppermute | solution.py:16
  43.5 2.1 %collective-permute-done.16.rest_1_.refs_7_ = bf16[32,1024]{1,0:T(8,128)(2,1)S(1)} collective-permute-done((bf16[32,1024]{1,0:T(8,128)(2,1)S(1)}, bf16[32,1024]{1,0:T(8,128)(2,1)S(1)}, u32[]{:S(2)}, u32[]{:S(2)}) %collective-permute-start.16) | collective-permute-done | bytes 65568 | tf_op jit(solution)/shard_map/ppermute | solution.py:618
  45.6 0.7 collective-permute-done.15.rest_0_.refs_5_
  46.3 0.1 shard_map.129
  46.5 0.6 collective-permute-start.22
  47.1 0.7 collective-permute-done.17.theirs
  47.8 0.4 shard_map.130.rest_0_.refs_1_
  48.2 0.1 shard_map.131
  48.3 0.2 collective-permute-start.18
  48.5 4.6 %convolution_convert_fusion.1 = bf16[64,1024]{1,0:T(8,128)(2,1)S(1)} fusion(bf16[64,3584]{1,0:T(8,128)(2,1)S(1)} %shard_map.130.rest_0_.refs_1_, bf16[3584,1024]{1,0:T(8,128)(2,1)} %down.3), kind=kOutput, calls=%fused_computation.1 | convolution fusion | flops 469827584 | bytes 7929856 | tf_op jit(solution)/shard_map/dot_general | solution.py:692
  53.2 2.2 %collective-permute-start.21 = (bf16[32,1024]{1,0:T(8,128)(2,1)S(1)}, bf16[32,1024]{1,0:T(8,128)(2,1)S(1)}, u32[]{:S(2)}, u32[]{:S(2)}) collective-permute-start(bf16[32,1024]{1,0:T(8,128)(2,1)S(1)} %get-tuple-element.64), channel_id=1, source_target_pairs={{0,12},{4,8},{8,4},{12,0},{1,13},{5,9},{9,5},{13,1},{2,14},{6,10},... | collective-permute-start | bytes 196616 | tf_op jit(solution)/shard_map/ppermute | solution.py:618
  55.3 0.5 collective-permute-start.20
  55.8 0.4 shard_map.132.refs_0_
  56.3 4.6 %convolution_convert_fusion.2.refs_3_ = bf16[64,1024]{1,0:T(8,128)(2,1)S(1)} fusion(bf16[64,3584]{1,0:T(8,128)(2,1)S(1)} %shard_map.132.refs_0_, bf16[3584,1024]{1,0:T(8,128)(2,1)} %down.3), kind=kOutput, calls=%fused_computation.2 | convolution fusion | flops 469827584 | bytes 7929856 | tf_op jit(solution)/shard_map/dot_general | solution.py:692
  60.9 1.9 %collective-permute-start.19 = (bf16[32,1024]{1,0:T(8,128)(2,1)S(1)}, bf16[32,1024]{1,0:T(8,128)(2,1)S(1)}, u32[]{:S(2)}, u32[]{:S(2)}) collective-permute-start(bf16[32,1024]{1,0:T(8,128)(2,1)S(1)} %get-tuple-element.66), channel_id=1, source_target_pairs={{0,4},{4,0},{8,12},{12,8},{1,5},{5,1},{9,13},{13,9},{2,6},{6,2},{1... | collective-permute-start | bytes 196616 | tf_op jit(solution)/shard_map/ppermute | solution.py:618
  62.8 0.4 shard_map.133
  63.2 2.1 %collective-permute-done.19.refs_1_ = bf16[32,1024]{1,0:T(8,128)(2,1)S(1)} collective-permute-done((bf16[32,1024]{1,0:T(8,128)(2,1)S(1)}, bf16[32,1024]{1,0:T(8,128)(2,1)S(1)}, u32[]{:S(2)}, u32[]{:S(2)}) %collective-permute-start.19) | collective-permute-done | bytes 65568 | tf_op jit(solution)/shard_map/ppermute | solution.py:618
  65.3 0.1 shard_map.134
  65.3 2.4 %collective-permute-start.25 = (bf16[32,1024]{1,0:T(8,128)(2,1)S(1)}, bf16[32,1024]{1,0:T(8,128)(2,1)S(1)}, u32[]{:S(2)}, u32[]{:S(2)}) collective-permute-start(bf16[32,1024]{1,0:T(8,128)(2,1)S(1)} %get-tuple-element.48), channel_id=1, source_target_pairs={{0,12},{4,8},{8,4},{12,0},{1,13},{5,9},{9,5},{13,1},{2,14},{6,10},... | collective-permute-start | bytes 196616 | tf_op jit(solution)/shard_map/ppermute | solution.py:618
  67.7 0.9 %collective-permute-start.24 = (bf16[32,1024]{1,0:T(8,128)(2,1)S(1)}, bf16[32,1024]{1,0:T(8,128)(2,1)S(1)}, u32[]{:S(2)}, u32[]{:S(2)}) collective-permute-start(bf16[32,1024]{1,0:T(8,128)(2,1)S(1)} %get-tuple-element.48), channel_id=1, source_target_pairs={{0,8},{4,12},{8,0},{12,4},{1,9},{5,13},{9,1},{13,5},{2,10},{6,14},... | collective-permute-start | bytes 196616 | tf_op jit(solution)/shard_map/ppermute | solution.py:618
  68.7 1.1 %collective-permute-start.23 = (bf16[32,1024]{1,0:T(8,128)(2,1)S(1)}, bf16[32,1024]{1,0:T(8,128)(2,1)S(1)}, u32[]{:S(2)}, u32[]{:S(2)}) collective-permute-start(bf16[32,1024]{1,0:T(8,128)(2,1)S(1)} %get-tuple-element.48), channel_id=1, source_target_pairs={{0,4},{4,0},{8,12},{12,8},{1,5},{5,1},{9,13},{13,9},{2,6},{6,2},{1... | collective-permute-start | bytes 196616 | tf_op jit(solution)/shard_map/ppermute | solution.py:618
  69.8 3.1 %collective-permute-done.23 = bf16[32,1024]{1,0:T(8,128)(2,1)S(1)} collective-permute-done((bf16[32,1024]{1,0:T(8,128)(2,1)S(1)}, bf16[32,1024]{1,0:T(8,128)(2,1)S(1)}, u32[]{:S(2)}, u32[]{:S(2)}) %collective-permute-start.23) | collective-permute-done | bytes 65568 | tf_op jit(solution)/shard_map/ppermute | solution.py:618
  73.0 0.9 %collective-permute-done.24 = bf16[32,1024]{1,0:T(8,128)(2,1)S(1)} collective-permute-done((bf16[32,1024]{1,0:T(8,128)(2,1)S(1)}, bf16[32,1024]{1,0:T(8,128)(2,1)S(1)}, u32[]{:S(2)}, u32[]{:S(2)}) %collective-permute-start.24) | collective-permute-done | bytes 65568 | tf_op jit(solution)/shard_map/ppermute | solution.py:618
  74.0 1.5 %shard_map.135 = (bf16[2,32,896]{2,1,0:T(8,128)(2,1)S(1)}, bf16[2,32,896]{2,1,0:T(8,128)(2,1)S(1)}) custom-call(bf16[4,64,128]{2,1,0:T(8,128)(2,1)S(1)} %get-tuple-element.32.picker, bf16[128,1024]{1,0:T(8,128)(2,1)S(1)} %constant_dynamic-update-slice_fusion.residual.before, bf16[3584,1024]{1,0:T(8,128)(2,1)S(1)} %bitcast.32, ...), custom_call_target="tpu_custom_call" | custom-call | tf_op jit(solution)/shard_map/pallas_call | solution.py:429
  75.6 1.3 %shard_map.136 = (bf16[2,32,896]{2,1,0:T(8,128)(2,1)S(1)}, bf16[2,32,896]{2,1,0:T(8,128)(2,1)S(1)}) custom-call(bf16[4,64,128]{2,1,0:T(8,128)(2,1)S(1)} %get-tuple-element.32.picker, bf16[128,1024]{1,0:T(8,128)(2,1)S(1)} %constant_dynamic-update-slice_fusion.residual.before, bf16[3584,1024]{1,0:T(8,128)(2,1)S(1)} %bitcast.32, ...), custom_call_target="tpu_custom_call" | custom-call | tf_op jit(solution)/shard_map/pallas_call | solution.py:429
  77.0 0.6 collective-permute-start.28
  77.6 1.4 %collective-permute-start.27 = (bf16[2,32,896]{2,1,0:T(8,128)(2,1)S(1)}, bf16[2,32,896]{2,1,0:T(8,128)(2,1)S(1)}, u32[]{:S(2)}, u32[]{:S(2)}) collective-permute-start(bf16[2,32,896]{2,1,0:T(8,128)(2,1)S(1)} %add_convert_fusion.3.mine), channel_id=1, source_target_pairs={{0,2},{2,0},{1,3},{3,1},{4,6},{6,4},{5,7},{7,5},{8,10},{10,8},{9,1... | collective-permute-start | bytes 344072 | tf_op jit(solution)/shard_map/ppermute | solution.py:16
  79.0 0.9 %collective-permute-start.30 = (bf16[2,32,896]{2,1,0:T(8,128)(2,1)S(1)}, bf16[2,32,896]{2,1,0:T(8,128)(2,1)S(1)}, u32[]{:S(2)}, u32[]{:S(2)}) collective-permute-start(bf16[2,32,896]{2,1,0:T(8,128)(2,1)S(1)} %add_convert_fusion.2.before.mine), channel_id=1, source_target_pairs={{0,2},{2,0},{1,3},{3,1},{4,6},{6,4},{5,7},{7,5},{8,10},{10,8},{9,1... | collective-permute-start | bytes 344072 | tf_op jit(solution)/shard_map/ppermute | solution.py:16
  79.9 3.4 %shard_map.137 = (bf16[3584,1024]{1,0:T(8,128)(2,1)}, f32[8,128]{1,0:T(8,128)S(1)}) custom-call(bf16[3584,128]{1,0:T(8,128)(2,1)S(1)} %get-tuple-element.51.hidden, bf16[128,1024]{1,0:T(8,128)(2,1)S(1)} %constant_dynamic-update-slice_fusion.residual.before, bf16[2,32,896]{2,1,0:T(8,128)(2,1)S(1)} %add_convert_fusion.2.before.mine), custom_call_target="tpu_custom_call" | custom-call | flops 939524096 | bytes 7340032 | tf_op jit(solution)/shard_map/pallas_call | solution.py:481
  83.3 0.3 collective-permute-done.27.other
  83.6 0.2 shard_map.138.rest_0_
  83.9 1.3 %collective-permute-done.30.other = bf16[2,32,896]{2,1,0:T(8,128)(2,1)S(1)} collective-permute-done((bf16[2,32,896]{2,1,0:T(8,128)(2,1)S(1)}, bf16[2,32,896]{2,1,0:T(8,128)(2,1)S(1)}, u32[]{:S(2)}, u32[]{:S(2)}) %collective-permute-start.30) | collective-permute-done | bytes 114720 | tf_op jit(solution)/shard_map/ppermute | solution.py:16
  85.2 0.2 shard_map.139.rest_2_
  85.4 0.6 convert_element_type.81
  86.0 0.8 collective-permute-done.31.rest_3_
  86.9 6.5 %shard_map.140 = (bf16[1024,3584]{1,0:T(8,128)(2,1)}, bf16[1024,3584]{1,0:T(8,128)(2,1)}) custom-call(bf16[4,64,128]{2,1,0:T(8,128)(2,1)S(1)} %get-tuple-element.32.picker, bf16[1024,128]{1,0:T(8,128)(2,1)S(1)} %get-tuple-element.46.refs_8_.tokens, bf16[2,2,32,896]{3,2,1,0:T(8,128)(2,1)S(1)} %shard_map.138.rest_0_, ...), custom_call_target="tpu_custom_call" | custom-call | flops 1879048192 | bytes 14680064 | tf_op jit(solution)/shard_map/pallas_call | solution.py:531
  (61 shorter events, 1.1 us)
Async XLA Ops:
  0.6 11.7 %collective-permute-start = (bf16[32,1024]{1,0:T(8,128)(2,1)}, bf16[32,1024]{1,0:T(8,128)(2,1)S(1)}, u32[]{:S(2)}, u32[]{:S(2)}) collective-permute-start(bf16[32,1024]{1,0:T(8,128)(2,1)} %param.9), channel_id=1, source_target_pairs={{0,4},{4,0},{8,12},{12,8},{1,5},{5,1},{9,13},{13,9},{2,6},{6,2},{1... | collective-permute-start | bytes 196616 | tf_op jit(solution)/shard_map/ppermute | solution.py:618
  3.7 9.2 %collective-permute-start.2 = (bf16[32,1024]{1,0:T(8,128)(2,1)}, bf16[32,1024]{1,0:T(8,128)(2,1)S(1)}, u32[]{:S(2)}, u32[]{:S(2)}) collective-permute-start(bf16[32,1024]{1,0:T(8,128)(2,1)} %param.9), channel_id=1, source_target_pairs={{0,12},{4,8},{8,4},{12,0},{1,13},{5,9},{9,5},{13,1},{2,14},{6,10},... | collective-permute-start | bytes 196616 | tf_op jit(solution)/shard_map/ppermute | solution.py:618
  6.2 6.7 %collective-permute-start.1 = (bf16[32,1024]{1,0:T(8,128)(2,1)}, bf16[32,1024]{1,0:T(8,128)(2,1)S(1)}, u32[]{:S(2)}, u32[]{:S(2)}) collective-permute-start(bf16[32,1024]{1,0:T(8,128)(2,1)} %param.9), channel_id=1, source_target_pairs={{0,8},{4,12},{8,0},{12,4},{1,9},{5,13},{9,1},{13,5},{2,10},{6,14},... | collective-permute-start | bytes 196616 | tf_op jit(solution)/shard_map/ppermute | solution.py:618
  6.4 5.9 %copy-start = (bf16[32,1024]{1,0:T(8,128)(2,1)S(1)}, bf16[32,1024]{1,0:T(8,128)(2,1)}, u32[]{:S(2)}) copy-start(bf16[32,1024]{1,0:T(8,128)(2,1)} %param.9) | copy-start | bytes 196612
  14.6 2.3 %collective-permute-start.8 = (bf16[2,64,1792]{2,1,0:T(8,128)(2,1)S(1)}, bf16[2,64,1792]{2,1,0:T(8,128)(2,1)S(1)}, u32[]{:S(2)}, u32[]{:S(2)}) collective-permute-start(bf16[2,64,1792]{2,1,0:T(8,128)(2,1)S(1)} %get-tuple-element.43), channel_id=1, source_target_pairs={{0,1},{1,0},{2,3},{3,2},{4,5},{5,4},{6,7},{7,6},{8,9},{9,8},{10,11... | collective-permute-start | bytes 1376264 | tf_op jit(solution)/shard_map/ppermute | solution.py:16
  16.3 2.3 %collective-permute-start.3 = (bf16[2,64,1792]{2,1,0:T(8,128)(2,1)S(1)}, bf16[2,64,1792]{2,1,0:T(8,128)(2,1)S(1)}, u32[]{:S(2)}, u32[]{:S(2)}) collective-permute-start(bf16[2,64,1792]{2,1,0:T(8,128)(2,1)S(1)} %get-tuple-element.36), channel_id=1, source_target_pairs={{0,1},{1,0},{2,3},{3,2},{4,5},{5,4},{6,7},{7,6},{8,9},{9,8},{10,11... | collective-permute-start | bytes 1376264 | tf_op jit(solution)/shard_map/ppermute | solution.py:16
  17.0 9.7 %collective-permute-start.9 = (bf16[2,32,1792]{2,1,0:T(8,128)(2,1)S(1)}, bf16[2,32,1792]{2,1,0:T(8,128)(2,1)S(1)}, u32[]{:S(2)}, u32[]{:S(2)}) collective-permute-start(bf16[2,32,1792]{2,1,0:T(8,128)(2,1)S(1)} %slice.33), channel_id=1, source_target_pairs={{0,2},{2,0},{1,3},{3,1},{4,6},{6,4},{5,7},{7,5},{8,10},{10,8},{9,1... | collective-permute-start | bytes 688136 | tf_op jit(solution)/shard_map/ppermute | solution.py:16
  18.7 10.8 %collective-permute-start.12 = (bf16[2,32,1792]{2,1,0:T(8,128)(2,1)S(1)}, bf16[2,32,1792]{2,1,0:T(8,128)(2,1)S(1)}, u32[]{:S(2)}, u32[]{:S(2)}) collective-permute-start(bf16[2,32,1792]{2,1,0:T(8,128)(2,1)S(1)} %slice.37), channel_id=1, source_target_pairs={{0,2},{2,0},{1,3},{3,1},{4,6},{6,4},{5,7},{7,5},{8,10},{10,8},{9,1... | collective-permute-start | bytes 688136 | tf_op jit(solution)/shard_map/ppermute | solution.py:16
  20.1 17.8 %slice-start.2 = ((s8[7340032]{0:T(1024)(128)(4,1)}), s8[4194304]{0:T(1024)(128)(4,1)S(1)}, s32[]{:S(2)}) async-start(s8[7340032]{0:T(1024)(128)(4,1)} %bitcast.33), calls=%async_computation.2 | async-start | bytes 8388608
  20.1 17.8 %slice-start.3 = ((s8[7340032]{0:T(1024)(128)(4,1)}), s8[3145728]{0:T(1024)(128)(4,1)S(1)}, s32[]{:S(2)}) async-start(s8[7340032]{0:T(1024)(128)(4,1)} %bitcast.33), calls=%async_computation.3 | async-start | bytes 6291456
  26.6 4.8 %collective-permute-start.5 = (bf16[4,2,16,896]{3,2,1,0:T(8,128)(2,1)S(1)}, bf16[4,2,16,896]{3,2,1,0:T(8,128)(2,1)S(1)}, u32[]{:S(2)}, u32[]{:S(2)}) collective-permute-start(bf16[4,2,16,896]{3,2,1,0:T(8,128)(2,1)S(1)} %get-tuple-element.40), channel_id=1, source_target_pairs={{0,1},{1,0},{2,3},{3,2},{4,5},{5,4},{6,7},{7,6},{8,9},{9,8},{10,11... | collective-permute-start | bytes 688136 | tf_op jit(solution)/shard_map/ppermute | solution.py:16
  26.9 6.0 %collective-permute-start.10 = (bf16[32,1792]{1,0:T(8,128)(2,1)S(1)}, bf16[32,1792]{1,0:T(8,128)(2,1)S(1)}, u32[]{:S(2)}, u32[]{:S(2)}) collective-permute-start(bf16[32,1792]{1,0:T(8,128)(2,1)S(1)} %fusion.3.refs_0_), channel_id=1, source_target_pairs={{0,2},{2,0},{1,3},{3,1},{4,6},{6,4},{5,7},{7,5},{8,10},{10,8},{9,1... | collective-permute-start | bytes 344072 | tf_op jit(solution)/shard_map/ppermute | solution.py:16
  29.7 5.2 %collective-permute-start.13 = (bf16[32,1792]{1,0:T(8,128)(2,1)S(1)}, bf16[32,1792]{1,0:T(8,128)(2,1)S(1)}, u32[]{:S(2)}, u32[]{:S(2)}) collective-permute-start(bf16[32,1792]{1,0:T(8,128)(2,1)S(1)} %fusion.1.refs_0_), channel_id=1, source_target_pairs={{0,2},{2,0},{1,3},{3,1},{4,6},{6,4},{5,7},{7,5},{8,10},{10,8},{9,1... | collective-permute-start | bytes 344072 | tf_op jit(solution)/shard_map/ppermute | solution.py:16
  31.4 5.0 %collective-permute-start.4 = (bf16[4,2,16,896]{3,2,1,0:T(8,128)(2,1)S(1)}, bf16[4,2,16,896]{3,2,1,0:T(8,128)(2,1)S(1)}, u32[]{:S(2)}, u32[]{:S(2)}) collective-permute-start(bf16[4,2,16,896]{3,2,1,0:T(8,128)(2,1)S(1)} %get-tuple-element.38), channel_id=1, source_target_pairs={{0,1},{1,0},{2,3},{3,2},{4,5},{5,4},{6,7},{7,6},{8,9},{9,8},{10,11... | collective-permute-start | bytes 688136 | tf_op jit(solution)/shard_map/ppermute | solution.py:16
  33.0 4.3 %collective-permute-start.11 = (bf16[64,1792]{1,0:T(8,128)(2,1)S(1)}, bf16[64,1792]{1,0:T(8,128)(2,1)S(1)}, u32[]{:S(2)}, u32[]{:S(2)}) collective-permute-start(bf16[64,1792]{1,0:T(8,128)(2,1)S(1)} %shard_map.126.refs_0_), channel_id=1, source_target_pairs={{0,1},{1,0},{2,3},{3,2},{4,5},{5,4},{6,7},{7,6},{8,9},{9,8},{10,11... | collective-permute-start | bytes 688136 | tf_op jit(solution)/shard_map/ppermute | solution.py:16
  35.0 2.3 %collective-permute-start.14 = (bf16[64,1792]{1,0:T(8,128)(2,1)S(1)}, bf16[64,1792]{1,0:T(8,128)(2,1)S(1)}, u32[]{:S(2)}, u32[]{:S(2)}) collective-permute-start(bf16[64,1792]{1,0:T(8,128)(2,1)S(1)} %shard_map.127.refs_2_), channel_id=1, source_target_pairs={{0,1},{1,0},{2,3},{3,2},{4,5},{5,4},{6,7},{7,6},{8,9},{9,8},{10,11... | collective-permute-start | bytes 688136 | tf_op jit(solution)/shard_map/ppermute | solution.py:16
  35.0 8.5 %collective-permute-start.7 = (bf16[4,2,16,896]{3,2,1,0:T(8,128)(2,1)S(1)}, bf16[4,2,16,896]{3,2,1,0:T(8,128)(2,1)S(1)}, u32[]{:S(2)}, u32[]{:S(2)}) collective-permute-start(bf16[4,2,16,896]{3,2,1,0:T(8,128)(2,1)S(1)} %shard_map.123.before.refs_2_.mine), channel_id=1, source_target_pairs={{0,2},{2,0},{1,3},{3,1},{4,6},{6,4},{5,7},{7,5},{8,10},{10,8},{9,1... | collective-permute-start | bytes 688136 | tf_op jit(solution)/shard_map/ppermute | solution.py:16
  36.5 11.7 %collective-permute-start.6 = (bf16[4,2,16,896]{3,2,1,0:T(8,128)(2,1)S(1)}, bf16[4,2,16,896]{3,2,1,0:T(8,128)(2,1)S(1)}, u32[]{:S(2)}, u32[]{:S(2)}) collective-permute-start(bf16[4,2,16,896]{3,2,1,0:T(8,128)(2,1)S(1)} %shard_map.124.mine), channel_id=1, source_target_pairs={{0,2},{2,0},{1,3},{3,1},{4,6},{6,4},{5,7},{7,5},{8,10},{10,8},{9,1... | collective-permute-start | bytes 688136 | tf_op jit(solution)/shard_map/ppermute | solution.py:16
  39.1 6.5 %collective-permute-start.16 = (bf16[32,1024]{1,0:T(8,128)(2,1)S(1)}, bf16[32,1024]{1,0:T(8,128)(2,1)S(1)}, u32[]{:S(2)}, u32[]{:S(2)}) collective-permute-start(bf16[32,1024]{1,0:T(8,128)(2,1)S(1)} %get-tuple-element.62), channel_id=1, source_target_pairs={{0,12},{4,8},{8,4},{12,0},{1,13},{5,9},{9,5},{13,1},{2,14},{6,10},... | collective-permute-start | bytes 196616 | tf_op jit(solution)/shard_map/ppermute | solution.py:618
  41.6 4.7 %collective-permute-start.15 = (bf16[32,1024]{1,0:T(8,128)(2,1)S(1)}, bf16[32,1024]{1,0:T(8,128)(2,1)S(1)}, u32[]{:S(2)}, u32[]{:S(2)}) collective-permute-start(bf16[32,1024]{1,0:T(8,128)(2,1)S(1)} %get-tuple-element.63), channel_id=1, source_target_pairs={{0,4},{4,0},{8,12},{12,8},{1,5},{5,1},{9,13},{13,9},{2,6},{6,2},{1... | collective-permute-start | bytes 196616 | tf_op jit(solution)/shard_map/ppermute | solution.py:618
  46.4 1.4 %collective-permute-start.17 = (bf16[4,16,896]{2,1,0:T(8,128)(2,1)S(1)}, bf16[4,16,896]{2,1,0:T(8,128)(2,1)S(1)}, u32[]{:S(2)}, u32[]{:S(2)}) collective-permute-start(bf16[4,16,896]{2,1,0:T(8,128)(2,1)S(1)} %get-tuple-element.44.mine), channel_id=1, source_target_pairs={{0,1},{1,0},{2,3},{3,2},{4,5},{5,4},{6,7},{7,6},{8,9},{9,8},{10,11... | collective-permute-start | bytes 344072 | tf_op jit(solution)/shard_map/ppermute | solution.py:16
  46.5 16.7 %collective-permute-start.22 = (bf16[32,1024]{1,0:T(8,128)(2,1)S(1)}, bf16[32,1024]{1,0:T(8,128)(2,1)S(1)}, u32[]{:S(2)}, u32[]{:S(2)}) collective-permute-start(bf16[32,1024]{1,0:T(8,128)(2,1)S(1)} %get-tuple-element.60), channel_id=1, source_target_pairs={{0,8},{4,12},{8,0},{12,4},{1,9},{5,13},{9,1},{13,5},{2,10},{6,14},... | collective-permute-start | bytes 196616 | tf_op jit(solution)/shard_map/ppermute | solution.py:618
  48.3 7.5 %collective-permute-start.18 = (bf16[4,16,896]{2,1,0:T(8,128)(2,1)S(1)}, bf16[4,16,896]{2,1,0:T(8,128)(2,1)S(1)}, u32[]{:S(2)}, u32[]{:S(2)}) collective-permute-start(bf16[4,16,896]{2,1,0:T(8,128)(2,1)S(1)} %get-tuple-element.45.mine), channel_id=1, source_target_pairs={{0,1},{1,0},{2,3},{3,2},{4,5},{5,4},{6,7},{7,6},{8,9},{9,8},{10,11... | collective-permute-start | bytes 344072 | tf_op jit(solution)/shard_map/ppermute | solution.py:16
  48.5 25.5 %slice-start = ((s8[7340032]{0:T(1024)(128)(4,1)}), s8[4194304]{0:T(1024)(128)(4,1)S(1)}, s32[]{:S(2)}) async-start(s8[7340032]{0:T(1024)(128)(4,1)} %bitcast.31), calls=%async_computation | async-start | bytes 8388608
  53.2 10.0 %collective-permute-start.21 = (bf16[32,1024]{1,0:T(8,128)(2,1)S(1)}, bf16[32,1024]{1,0:T(8,128)(2,1)S(1)}, u32[]{:S(2)}, u32[]{:S(2)}) collective-permute-start(bf16[32,1024]{1,0:T(8,128)(2,1)S(1)} %get-tuple-element.64), channel_id=1, source_target_pairs={{0,12},{4,8},{8,4},{12,0},{1,13},{5,9},{9,5},{13,1},{2,14},{6,10},... | collective-permute-start | bytes 196616 | tf_op jit(solution)/shard_map/ppermute | solution.py:618
  55.3 7.8 %collective-permute-start.20 = (bf16[32,1024]{1,0:T(8,128)(2,1)S(1)}, bf16[32,1024]{1,0:T(8,128)(2,1)S(1)}, u32[]{:S(2)}, u32[]{:S(2)}) collective-permute-start(bf16[32,1024]{1,0:T(8,128)(2,1)S(1)} %get-tuple-element.65), channel_id=1, source_target_pairs={{0,8},{4,12},{8,0},{12,4},{1,9},{5,13},{9,1},{13,5},{2,10},{6,14},... | collective-permute-start | bytes 196616 | tf_op jit(solution)/shard_map/ppermute | solution.py:618
  56.3 17.7 %slice-start.1 = ((s8[7340032]{0:T(1024)(128)(4,1)}), s8[3145728]{0:T(1024)(128)(4,1)S(1)}, s32[]{:S(2)}) async-start(s8[7340032]{0:T(1024)(128)(4,1)} %bitcast.31), calls=%async_computation.1 | async-start | bytes 6291456
  60.9 4.3 %collective-permute-start.19 = (bf16[32,1024]{1,0:T(8,128)(2,1)S(1)}, bf16[32,1024]{1,0:T(8,128)(2,1)S(1)}, u32[]{:S(2)}, u32[]{:S(2)}) collective-permute-start(bf16[32,1024]{1,0:T(8,128)(2,1)S(1)} %get-tuple-element.66), channel_id=1, source_target_pairs={{0,4},{4,0},{8,12},{12,8},{1,5},{5,1},{9,13},{13,9},{2,6},{6,2},{1... | collective-permute-start | bytes 196616 | tf_op jit(solution)/shard_map/ppermute | solution.py:618
  65.3 8.6 %collective-permute-start.25 = (bf16[32,1024]{1,0:T(8,128)(2,1)S(1)}, bf16[32,1024]{1,0:T(8,128)(2,1)S(1)}, u32[]{:S(2)}, u32[]{:S(2)}) collective-permute-start(bf16[32,1024]{1,0:T(8,128)(2,1)S(1)} %get-tuple-element.48), channel_id=1, source_target_pairs={{0,12},{4,8},{8,4},{12,0},{1,13},{5,9},{9,5},{13,1},{2,14},{6,10},... | collective-permute-start | bytes 196616 | tf_op jit(solution)/shard_map/ppermute | solution.py:618
  67.7 6.2 %collective-permute-start.24 = (bf16[32,1024]{1,0:T(8,128)(2,1)S(1)}, bf16[32,1024]{1,0:T(8,128)(2,1)S(1)}, u32[]{:S(2)}, u32[]{:S(2)}) collective-permute-start(bf16[32,1024]{1,0:T(8,128)(2,1)S(1)} %get-tuple-element.48), channel_id=1, source_target_pairs={{0,8},{4,12},{8,0},{12,4},{1,9},{5,13},{9,1},{13,5},{2,10},{6,14},... | collective-permute-start | bytes 196616 | tf_op jit(solution)/shard_map/ppermute | solution.py:618
  68.7 4.3 %collective-permute-start.23 = (bf16[32,1024]{1,0:T(8,128)(2,1)S(1)}, bf16[32,1024]{1,0:T(8,128)(2,1)S(1)}, u32[]{:S(2)}, u32[]{:S(2)}) collective-permute-start(bf16[32,1024]{1,0:T(8,128)(2,1)S(1)} %get-tuple-element.48), channel_id=1, source_target_pairs={{0,4},{4,0},{8,12},{12,8},{1,5},{5,1},{9,13},{13,9},{2,6},{6,2},{1... | collective-permute-start | bytes 196616 | tf_op jit(solution)/shard_map/ppermute | solution.py:618
  75.5 2.0 %collective-permute-start.26 = (bf16[2,32,896]{2,1,0:T(8,128)(2,1)S(1)}, bf16[2,32,896]{2,1,0:T(8,128)(2,1)S(1)}, u32[]{:S(2)}, u32[]{:S(2)}) collective-permute-start(bf16[2,32,896]{2,1,0:T(8,128)(2,1)S(1)} %get-tuple-element.50), channel_id=1, source_target_pairs={{0,1},{1,0},{2,3},{3,2},{4,5},{5,4},{6,7},{7,6},{8,9},{9,8},{10,11... | collective-permute-start | bytes 344072 | tf_op jit(solution)/shard_map/ppermute | solution.py:16
  77.0 2.0 %collective-permute-start.28 = (bf16[2,32,896]{2,1,0:T(8,128)(2,1)S(1)}, bf16[2,32,896]{2,1,0:T(8,128)(2,1)S(1)}, u32[]{:S(2)}, u32[]{:S(2)}) collective-permute-start(bf16[2,32,896]{2,1,0:T(8,128)(2,1)S(1)} %get-tuple-element.53), channel_id=1, source_target_pairs={{0,1},{1,0},{2,3},{3,2},{4,5},{5,4},{6,7},{7,6},{8,9},{9,8},{10,11... | collective-permute-start | bytes 344072 | tf_op jit(solution)/shard_map/ppermute | solution.py:16
  77.6 6.1 %collective-permute-start.27 = (bf16[2,32,896]{2,1,0:T(8,128)(2,1)S(1)}, bf16[2,32,896]{2,1,0:T(8,128)(2,1)S(1)}, u32[]{:S(2)}, u32[]{:S(2)}) collective-permute-start(bf16[2,32,896]{2,1,0:T(8,128)(2,1)S(1)} %add_convert_fusion.3.mine), channel_id=1, source_target_pairs={{0,2},{2,0},{1,3},{3,1},{4,6},{6,4},{5,7},{7,5},{8,10},{10,8},{9,1... | collective-permute-start | bytes 344072 | tf_op jit(solution)/shard_map/ppermute | solution.py:16
  79.0 6.2 %collective-permute-start.30 = (bf16[2,32,896]{2,1,0:T(8,128)(2,1)S(1)}, bf16[2,32,896]{2,1,0:T(8,128)(2,1)S(1)}, u32[]{:S(2)}, u32[]{:S(2)}) collective-permute-start(bf16[2,32,896]{2,1,0:T(8,128)(2,1)S(1)} %add_convert_fusion.2.before.mine), channel_id=1, source_target_pairs={{0,2},{2,0},{1,3},{3,1},{4,6},{6,4},{5,7},{7,5},{8,10},{10,8},{9,1... | collective-permute-start | bytes 344072 | tf_op jit(solution)/shard_map/ppermute | solution.py:16
  83.8 2.2 %collective-permute-start.29 = (bf16[2,2,32,896]{3,2,1,0:T(8,128)(2,1)S(1)}, bf16[2,2,32,896]{3,2,1,0:T(8,128)(2,1)S(1)}, u32[]{:S(2)}, u32[]{:S(2)}) collective-permute-start(bf16[2,2,32,896]{3,2,1,0:T(8,128)(2,1)S(1)} %shard_map.138.rest_0_), channel_id=1, source_target_pairs={{0,1},{1,0},{2,3},{3,2},{4,5},{5,4},{6,7},{7,6},{8,9},{9,8},{10,11... | collective-permute-start | bytes 688136 | tf_op jit(solution)/shard_map/ppermute | solution.py:16
  85.3 1.6 %collective-permute-start.31 = (bf16[2,2,32,896]{3,2,1,0:T(8,128)(2,1)S(1)}, bf16[2,2,32,896]{3,2,1,0:T(8,128)(2,1)S(1)}, u32[]{:S(2)}, u32[]{:S(2)}) collective-permute-start(bf16[2,2,32,896]{3,2,1,0:T(8,128)(2,1)S(1)} %shard_map.139.rest_2_), channel_id=1, source_target_pairs={{0,1},{1,0},{2,3},{3,2},{4,5},{5,4},{6,7},{7,6},{8,9},{9,8},{10,11... | collective-permute-start | bytes 688136 | tf_op jit(solution)/shard_map/ppermute | solution.py:16
